TPU v7x, 32 devices: a whole 2x2x4 slice. The times are simulated.
32 devices in a mesh: grp: 2 (over x), tile: 16 (over z, y, core).
Axes of the slice: x: 2, y: 2, z: 4, core: 2. Of those that a mesh axis runs over, the one named last changes fastest.
Arguments:
- visibility: bfloat16 [32, 16, 2, 256, 256], P('tile', 'grp'), parts along dimension 1, may hold values from -12 to 12
- station_beam: bfloat16 [16, 2, 512, 2048], P('grp', None, 'tile'), parts along dimension 0, may hold values from -4.1875 to 4.1875
- antenna_uvw: float32 [16, 3, 2048], P('grp'), parts along dimension 0, may hold values from -40 to 40
- source_dirs: float32 [2, 4096], P(None, 'tile'), may hold values from -0.4 to 0.4
- source_flux: bfloat16 [8192], P(('grp', 'tile')), parts along dimension 0, may hold values from 0.0029907227 to 0.029907227
- visible_list: int32 [8, 512], P(None, 'tile'), may hold values from 0 to 255
- antenna_flags: int32 [16, 2048], P('grp'), parts along dimension 0, may hold values 0 or 1
Outputs:
- residual: bfloat16 [32, 16, 2, 256, 256], P('tile', 'grp'), parts along dimension 1
- flux_grad: float32 [16, 512], P('grp', 'tile'), parts along dimension 0
There are 2 independent parts, one for each index of `grp`. A program takes and returns all parts, laid end to end along the dimension named above; an argument that names none is the same for every part. Nothing has to cross between parts.
Inputs may be any that keep to these rules, and one draw needn't show every extreme that they name: `visible_list`: entry k of a slot names pool source 256 * (k // 32) + value, a source of its own group. `antenna_flags`: 1 marks a flagged antenna.
All inputs are finite; a program needn't handle non-finite values.
Results may differ from a plain program's by a relative error of at most 0.0034.
Values may be sent and summed in bfloat16 or wider, within the bound.
No kernel may reach another device: no remote copies, remote signals or barrier semaphores. Data moves between devices by JAX's collectives and lax.ppermute only.
A program may use at most 192 MiB of HBM per device.

v0:
```python
import math

import jax
import jax.numpy as jnp
import numpy as np
from jax import lax
from jax.sharding import PartitionSpec as P

BLOCKS = 8


two_pi = 2.0 * math.pi


def unit_table(block_count):
    first_list = []
    second_list = []
    diag_list = []
    for row_block in range(block_count):
        for col_block in range(row_block + 1, block_count):
            first_list.append(row_block)
            second_list.append(col_block)
            diag_list.append(0)
    for pair_index in range(block_count // 2):
        first_list.append(2 * pair_index)
        second_list.append(2 * pair_index + 1)
        diag_list.append(1)
    return (
        np.array(first_list, np.int32),
        np.array(second_list, np.int32),
        np.array(diag_list, np.int32),
    )


def build_factors(station_beam, antenna_uvw, source_dirs, source_flux, visible_list):
    pool_size = source_dirs.shape[1]
    chosen = visible_list[:, :, None] == jnp.arange(pool_size, dtype=jnp.int32)[None, None, :]
    coord_east = jnp.sum(jnp.where(chosen, source_dirs[0][None, None, :], 0.0), axis=2)
    coord_north = jnp.sum(jnp.where(chosen, source_dirs[1][None, None, :], 0.0), axis=2)
    brightness = jnp.sum(
        jnp.where(chosen, source_flux.astype(jnp.float32)[None, None, :], 0.0), axis=2
    ).astype(jnp.bfloat16)
    depth_term = jnp.sqrt(1.0 - coord_east * coord_east - coord_north * coord_north) - 1.0
    delay_sum = (
        antenna_uvw[:, 0, None, :] * coord_east[:, :, None]
        + antenna_uvw[:, 1, None, :] * coord_north[:, :, None]
        + antenna_uvw[:, 2, None, :] * depth_term[:, :, None]
    )
    phases = two_pi * delay_sum
    cosine = jnp.cos(phases)
    sine = jnp.sin(phases)
    beam_f = station_beam.astype(jnp.float32)
    real_part = beam_f[:, 0] * cosine + beam_f[:, 1] * sine
    imag_part = beam_f[:, 1] * cosine - beam_f[:, 0] * sine
    return (jnp.stack([real_part, imag_part], 1).astype(jnp.bfloat16), brightness)


def predict(rows_f, cols_f, brightness):
    scaled = (rows_f.astype(jnp.float32) * brightness.astype(jnp.float32)[:, None, :, None]).astype(
        jnp.bfloat16
    )
    turned = jnp.stack([scaled[:, 1], -scaled[:, 0]], 1)
    stacked = jnp.stack([scaled, turned], 1)
    return jnp.einsum("tdckr,tckq->tdrq", stacked, cols_f, preferred_element_type=jnp.float32)


def pull_back(resid, rows_f, cols_f):
    rstack = jnp.stack(
        [jnp.stack([resid[:, 0], -resid[:, 1]], 1), jnp.stack([resid[:, 1], resid[:, 0]], 1)], 1
    )
    pulled = jnp.einsum("tdcrq,tckq->tdkr", rstack, cols_f, preferred_element_type=jnp.float32)
    return jnp.sum(rows_f.astype(jnp.float32) * pulled, axis=(1, 3))


def unit_work(block_one, block_two, diag_tile, bright_all, vis_unit, keep_one, keep_two):
    span = vis_unit.shape[3]
    local_ids = jnp.arange(span, dtype=jnp.int32)
    upper_part = local_ids[:, None] < local_ids[None, :]
    lower_part = local_ids[:, None] > local_ids[None, :]
    cols_one = jnp.where(diag_tile, block_one, block_two)
    first_pred = predict(block_one, cols_one, bright_all)
    pred_shape = first_pred.shape
    second_pred = lax.cond(
        diag_tile,
        lambda: predict(block_two, block_two, bright_all),
        lambda: jnp.zeros(pred_shape, jnp.float32),
    )
    first_mask = jnp.logical_or(jnp.logical_not(diag_tile), upper_part)
    predicted = jnp.where(first_mask[None, None], first_pred, jnp.swapaxes(second_pred, 2, 3))
    upper_f = upper_part.astype(jnp.float32)
    lower_f = lower_part.astype(jnp.float32)
    off_weight = keep_one[:, :, None] * keep_two[:, None, :]
    diag_weight = (
        upper_f[None] * keep_one[:, :, None] * keep_one[:, None, :]
        + lower_f[None] * keep_two[:, :, None] * keep_two[:, None, :]
    )
    weights = jnp.where(diag_tile, diag_weight, off_weight)
    residual = (weights[:, None] * (vis_unit.astype(jnp.float32) - predicted)).astype(jnp.bfloat16)
    zero_res = jnp.zeros_like(residual)
    first_res = jnp.where(first_mask[None, None], residual, zero_res)
    partial_value = pull_back(first_res, block_one, cols_one)
    second_sel = jnp.logical_and(diag_tile, lower_part)
    grad_shape = partial_value.shape
    second_part = lax.cond(
        diag_tile,
        lambda: pull_back(
            jnp.swapaxes(jnp.where(second_sel[None, None], residual, zero_res), 2, 3),
            block_two,
            block_two,
        ),
        lambda: jnp.zeros(grad_shape, jnp.float32),
    )
    return (residual, partial_value + second_part)


def per_device(
    visibility, station_beam, antenna_uvw, source_dirs, source_flux, visible_list, antenna_flags
):
    tile_count = lax.axis_size("tile")
    units_dev = visibility.shape[0]
    span = visibility.shape[4]
    slot_count = station_beam.shape[0]
    per_group = station_beam.shape[2]
    antennas = station_beam.shape[3]
    tile_index = lax.axis_index("tile")
    first_tab, second_tab, diag_tab = unit_table(BLOCKS)
    first_arr = jnp.asarray(first_tab)
    second_arr = jnp.asarray(second_tab)
    diag_arr = jnp.asarray(diag_tab)
    keep_all = 1.0 - antenna_flags.astype(jnp.float32)
    owned, brightness = build_factors(
        station_beam, antenna_uvw, source_dirs, source_flux, visible_list
    )
    gathered, bright_all = (
        lax.all_gather(owned, "tile", axis=2, tiled=True),
        lax.all_gather(brightness, "tile", axis=1, tiled=True),
    )
    residuals = []
    partial_total = jnp.zeros((slot_count, per_group * tile_count), jnp.float32)
    for unit_slot in range(units_dev):
        unit_id = tile_index * units_dev + unit_slot
        start_one = (first_arr[unit_id] * span).astype(jnp.int32)
        start_two = (second_arr[unit_id] * span).astype(jnp.int32)
        diag_tile = diag_arr[unit_id] == 1
        block_one = lax.dynamic_slice_in_dim(gathered, start_one, span, 3)
        block_two = lax.dynamic_slice_in_dim(gathered, start_two, span, 3)
        keep_one = lax.dynamic_slice_in_dim(keep_all, start_one, span, 1)
        keep_two = lax.dynamic_slice_in_dim(keep_all, start_two, span, 1)
        residual, partial_value = unit_work(
            block_one, block_two, diag_tile, bright_all, visibility[unit_slot], keep_one, keep_two
        )
        residuals.append(residual)
        partial_total = partial_total + partial_value
    summed = lax.psum_scatter(partial_total, "tile", scatter_dimension=1, tiled=True)
    flux_grad = summed * (-1.0 / (8.0 * antennas))
    return (jnp.stack(residuals, 0), flux_grad)


def solution(mesh):
    return jax.shard_map(
        per_device,
        mesh=mesh,
        in_specs=(
            P("tile", "grp", None, None, None),
            P("grp", None, "tile", None),
            P("grp", None, None),
            P(None, "tile"),
            P(("grp", "tile")),
            P(None, "tile"),
            P("grp", None),
        ),
        out_specs=(P("tile", "grp", None, None, None), P("grp", "tile")),
        check_vma=False,
    )
```

profile of v0, /device:TPU:0, one launch (start us, length us, event | category | flops | bytes accessed | tf_op | source)
XLA Modules:
  0.0 425.4 jit_solution(3471020011920112316)
XLA Ops:
  7.2 0.8 fusion.93
  8.0 0.7 convert_element_type.108
  8.6 0.9 slice_bitcast_fusion.2
  9.6 2.1 convert_element_type.106
  11.7 0.3 select_reduce_fusion
  12.0 8.9 %add_convert_fusion = (bf16[8,1,32,2048]{3,2,1,0:T(8,128)(2,1)S(1)}, bf16[8,1,32,2048]{3,2,1,0:T(8,128)(2,1)S(1)}) fusion(f32[8,2,32,2048]{3,2,1,0:T(8,128)S(1)} %convert_element_type.106, f32[8,32]{1,0:T(8,128)S(1)} %sqrt_add_fusion, f32[8,2048]{1,0:T(8,128)S(1)} %get-tuple-element.134, f32[8,32]{1,0:T(8,128)S(1)} %get-tuple-element.95, ...), kind=kLoop, calls=%fused_computation.93 | loop fusion | flops 7340032 | bytes 6491136 | tf_op jit(solution)/shard_map/convert.2
  20.9 0.2 pad_maximum_fusion.4
  21.2 2.5 copy.115
  23.8 0.7 fusion.94
  27.0 0.7 fusion.96
  29.1 23.6 %all-gather = bf16[16,32,8]{1,2,0:T(8,128)(2,1)S(1)} all-gather(bf16[1,32,8]{1,2,0:T(8,128)(2,1)S(1)} %bitcast.185), channel_id=1, replica_groups=mesh['grp'=2,'tile'=16] {'tile'}, dimensions={0}, use_global_device_ids=true | all-gather | bytes 8704 | tf_op jit(solution)/shard_map/all_gather | solution.py:136
  53.2 2.7 multiply_select_fusion.1
  55.8 138.9 %all-gather.3.cloned.1.call-done = bf16[8,2,512,2048]{3,0,1,2:T(8,128)(2,1)} async-done(((bf16[8,2,32,2048]{3,0,1,2:T(8,128)(2,1)}), bf16[8,2,512,2048]{3,0,1,2:T(8,128)(2,1)}) %all-gather.3.cloned.1.call-update) | async-done | bytes 33554448 | tf_op jit(solution)/shard_map/all_gather | solution.py:135
  194.7 12.4 %constant_dynamic-slice_fusion.5 = (bf16[8,2,512,256]{3,0,1,2:T(8,128)(2,1)}, bf16[8,2,512,256]{3,0,1,2:T(8,128)(2,1)}, bf16[8,2,512,256]{3,0,1,2:T(8,128)(2,1)}, bf16[8,2,512,256]{3,0,1,2:T(8,128)(2,1)}) fusion(bf16[8,2,512,2048]{3,0,1,2:T(8,128)(2,1)} %all-gather.3.cloned.1.call-done, s32[]{:T(128)S(6)} %select_n.94, s32[]{:T(128)S(6)} %select_n.105, ...), kind=kLoop, calls=%fused_computation.123 | loop fusion | bytes 33554448 | tf_op jit(solution)/shard_map/dynamic_slice | solution.py:145
  207.1 7.6 %copy.167 = bf16[8,2,512,256]{2,3,1,0:T(8,128)(2,1)} copy(bf16[8,2,512,256]{3,0,1,2:T(8,128)(2,1)} %get-tuple-element.111) | data formatting | bytes 8388608
  214.7 7.6 %copy.169 = bf16[8,2,512,256]{2,3,1,0:T(8,128)(2,1)} copy(bf16[8,2,512,256]{3,0,1,2:T(8,128)(2,1)} %get-tuple-element.112) | data formatting | bytes 8388608
  222.3 7.5 %fusion.44 = (bf16[8,2,512,256]{2,3,1,0:T(8,128)(2,1)S(1)}, bf16[8,2,512,256]{2,3,1,0:T(8,128)(2,1)}) fusion(bf16[8,2,512,256]{2,3,1,0:T(8,128)(2,1)} %copy.167, f32[8,512]{1,0:T(8,128)S(1)} %bitcast_convert_fusion, bf16[8,2,512,256]{2,3,1,0:T(8,128)(2,1)} %copy.169), kind=kLoop, calls=%fused_computation.50 | loop fusion | flops 12582912 | bytes 16793600 | tf_op jit(solution)/shard_map/convert_element_type | solution.py:59
  229.8 1.9 fusion.91
  231.7 0.8 copy-done.9
  232.4 7.6 %copy.168 = bf16[8,2,512,256]{2,3,1,0:T(8,128)(2,1)} copy(bf16[8,2,512,256]{3,0,1,2:T(8,128)(2,1)} %get-tuple-element.113) | data formatting | bytes 8388608
  240.1 2.5 conditional.4
  240.1 2.5 broadcast.220
  242.5 5.4 %copy.121 = f32[8,2,256,256]{2,3,1,0:T(8,128)} copy(f32[8,2,256,256]{3,2,1,0:T(8,128)} %get-tuple-element.156) | data formatting | bytes 8388608 | tf_op jit(solution)/shard_map/cond | solution.py:83
  248.0 4.3 %maximum_bitcast_fusion.6 = bf16[8,1,2,512,256]{3,4,2,1,0:T(8,128)(2,1)} fusion(bf16[8,1,512,256]{2,3,1,0:T(8,128)(2,1)} %get-tuple-element.118, bf16[8,1,512,256]{2,3,1,0:T(8,128)(2,1)S(1)} %get-tuple-element.117), kind=kLoop, calls=%fused_computation.61 | loop fusion | flops 2097152 | bytes 8388608 | tf_op jit(solution)/shard_map/stack | solution.py:63
  252.3 1.3 copy-done.6
  253.6 8.4 %broadcast_select_fusion.3 = (bf16[8,2,256,256]{3,2,1,0:T(8,128)(2,1)S(1)}, bf16[8,2,256,256]{3,2,1,0:T(8,128)(2,1)}) fusion(pred[256,256]{1,0:T(8,128)(4,1)S(1)} %fusion.85, f32[8,2,256,256]{2,3,1,0:T(8,128)} %copy.121, bf16[8,2,512,256]{2,3,1,0:T(8,128)(2,1)S(1)} %copy-done.6, bf16[8,2,512,256]{2,3,1,0:T(8,128)(2,1)S(1)} %copy-done, pred[]{:T(512)} %bitcast.28, ...), kind=kOutput, calls=%fused_computation.99 | convolution fusion | flops 2160066560 | bytes 29425664 | tf_op jit(solution)/shard_map/tdckr,tckq->tdrq/dot_general | solution.py:64
  262.0 1.8 slice_negate_fusion.7
  263.7 1.6 copy-done.7
  265.3 1.6 fusion.92
  266.9 7.5 %copy.170 = bf16[8,2,512,256]{2,3,1,0:T(8,128)(2,1)} copy(bf16[8,2,512,256]{3,0,1,2:T(8,128)(2,1)} %get-tuple-element.114) | data formatting | bytes 8388608
  274.4 2.5 conditional.5
  274.4 2.5 broadcast.221
  276.9 5.3 %copy.126 = f32[8,2,256,256]{2,3,1,0:T(8,128)} copy(f32[8,2,256,256]{3,2,1,0:T(8,128)} %get-tuple-element.157) | data formatting | bytes 8388608 | tf_op jit(solution)/shard_map/cond | solution.py:83
  282.2 4.3 %maximum_bitcast_fusion.7 = bf16[8,1,2,512,256]{3,4,2,0,1:T(8,128)(2,1)} fusion(bf16[8,1,512,256]{2,3,1,0:T(8,128)(2,1)} %get-tuple-element.120, bf16[8,1,512,256]{2,3,1,0:T(8,128)(2,1)S(1)} %get-tuple-element.119), kind=kLoop, calls=%fused_computation.62 | loop fusion | flops 2097152 | bytes 8388608 | tf_op jit(solution)/shard_map/stack | solution.py:63
  286.5 1.3 copy-done.8
  287.8 8.8 %broadcast_select_fusion.2 = (bf16[8,2,256,256]{3,2,1,0:T(8,128)(2,1)S(1)}, bf16[8,2,256,256]{3,2,1,0:T(8,128)(2,1)}) fusion(pred[256,256]{1,0:T(8,128)(4,1)S(1)} %fusion.84, f32[8,2,256,256]{2,3,1,0:T(8,128)} %copy.126, bf16[8,2,512,256]{2,3,1,0:T(8,128)(2,1)S(1)} %copy-done.4, bf16[8,2,512,256]{2,3,1,0:T(8,128)(2,1)} %copy.170, pred[]{:T(512)} %bitcast.48, ...), kind=kOutput, calls=%fused_computation.98 | convolution fusion | flops 2160066560 | bytes 29425664 | tf_op jit(solution)/shard_map/tdckr,tckq->tdrq/dot_general | solution.py:64
  296.6 1.8 slice_negate_fusion.6
  298.4 1.2 copy-done.10
  299.6 4.5 %maximum_bitcast_fusion.8 = (bf16[8,1,2,256,256]{4,3,2,0,1:T(8,128)(2,1)}, bf16[8,1,2,256,256]{4,3,2,0,1:T(8,128)(2,1)}) fusion(bf16[8,1,256,256]{3,2,1,0:T(8,128)(2,1)S(1)} %copy-done.10, bf16[8,1,256,256]{3,2,1,0:T(8,128)(2,1)} %get-tuple-element.123, bf16[8,1,256,256]{3,2,1,0:T(8,128)(2,1)} %get-tuple-element.122), kind=kLoop, calls=%fused_computation.87 | loop fusion | flops 2097152 | bytes 7340032 | tf_op jit(solution)/shard_map/stack | solution.py:68
  304.2 6.4 %fusion.45 = f32[8,512]{1,0:T(8,128)S(1)} fusion(bf16[8,2,512,256]{2,3,1,0:T(8,128)(2,1)} %copy.167, bf16[8,2,512,256]{2,3,1,0:T(8,128)(2,1)S(1)} %copy-done.1, pred[]{:T(512)} %bitcast.28, bf16[8,1,2,256,256]{4,3,2,0,1:T(8,128)(2,1)} %get-tuple-element.128, bf16[8,1,2,256,256]{4,3,2,0,1:T(8,128)(2,1)} %get-tuple-element.127), kind=kOutput, calls=%fused_computation.51 | convolution fusion | flops 2157965312 | bytes 12599297 | tf_op jit(solution)/shard_map/tdcrq,tckq->tdkr/dot_general | solution.py:71
  310.7 4.1 maximum_bitcast_fusion.10
  314.8 6.4 %fusion.47 = f32[8,512]{1,0:T(8,128)S(1)} fusion(bf16[8,2,512,256]{2,3,1,0:T(8,128)(2,1)S(1)} %copy-done.5, bf16[8,2,512,256]{2,3,1,0:T(8,128)(2,1)} %copy.170, pred[]{:T(512)} %bitcast.48, bf16[8,1,2,256,256]{4,3,2,0,1:T(8,128)(2,1)} %get-tuple-element.130, bf16[8,1,2,256,256]{4,3,2,0,1:T(8,128)(2,1)} %get-tuple-element.129), kind=kOutput, calls=%fused_computation.53 | convolution fusion | flops 2157965312 | bytes 12599297 | tf_op jit(solution)/shard_map/tdcrq,tckq->tdkr/dot_general | solution.py:71
  321.2 0.3 conditional.7
  321.5 0.9 copy.165
  322.4 4.6 %pad_maximum_fusion.1 = bf16[2,8,2,256,256]{4,3,2,1,0:T(8,128)(2,1)} fusion(bf16[1,8,2,256,256]{4,3,2,1,0:T(8,128)(2,1)} %bitcast.180, bf16[1,8,2,256,256]{4,3,2,1,0:T(8,128)(2,1)} %bitcast.179), kind=kLoop, calls=%fused_computation.63 | loop fusion | flops 2097152 | bytes 8388608 | tf_op jit(solution)/shard_map/stack | solution.py:156
  327.0 90.1 %reduce-scatter.4.cloned.1.call-done = f32[32,8]{1,0:T(8,128)} async-done(((f32[512,8]{1,0:T(8,128)}), f32[32,8]{1,0:T(8,128)}) %reduce-scatter.4.cloned.1.call-update) | async-done | bytes 1040
  417.1 0.8 copy.166
  417.9 0.6 broadcast_multiply_fusion
  (47 shorter events, 0.6 us)
Async XLA Ops:
  7.2 4.5 %copy-start.15 = (s32[8,32]{1,0:T(8,128)S(1)}, s32[8,32]{1,0:T(8,128)}, u32[]{:S(2)}) copy-start(s32[8,32]{1,0:T(8,128)} %param.23) | copy-start | bytes 3076
  7.2 187.5 %all-gather.3.cloned.1.call-start = ((), (), s32[]{:S(2)}) async-start(), calls=%async_computation.1 | async-start | bytes 35651584 | tf_op jit(solution)/shard_map/all_gather | solution.py:135
  21.1 2.6 copy-start.17
  21.2 2.6 copy-start.18
  21.2 5.9 %copy-start.16 = (s32[32]{0:T(128)S(1)}, s32[32]{0:T(128)}, u32[]{:S(2)}) copy-start(s32[32]{0:T(128)} %constant.62.clone) | copy-start | bytes 388
  21.2 31.8 %copy-start.14 = (s32[8,2048]{1,0:T(8,128)S(1)}, s32[8,2048]{1,0:T(8,128)}, u32[]{:S(2)}) copy-start(s32[8,2048]{1,0:T(8,128)} %param.24) | copy-start | bytes 196612
  23.7 393.5 %reduce-scatter.4.cloned.1.call-start = ((), (), s32[]{:S(2)}) async-start(), calls=%async_computation.2 | async-start | bytes 278528
  229.8 2.7 copy-start.9
  248.0 4.3 %copy-start = (bf16[8,2,512,256]{2,3,1,0:T(8,128)(2,1)S(1)}, bf16[8,2,512,256]{2,3,1,0:T(8,128)(2,1)}, u32[]{:S(2)}) copy-start(bf16[8,2,512,256]{2,3,1,0:T(8,128)(2,1)} %copy.168) | copy-start | bytes 12582916
  248.0 5.6 %copy-start.6 = (bf16[8,2,512,256]{2,3,1,0:T(8,128)(2,1)S(1)}, bf16[8,2,512,256]{2,3,1,0:T(8,128)(2,1)}, u32[]{:S(2)}) copy-start(bf16[8,2,512,256]{2,3,1,0:T(8,128)(2,1)} %copy.167) | copy-start | bytes 12582916
  262.0 3.3 copy-start.7
  282.2 4.3 %copy-start.4 = (bf16[8,2,512,256]{2,3,1,0:T(8,128)(2,1)S(1)}, bf16[8,2,512,256]{2,3,1,0:T(8,128)(2,1)}, u32[]{:S(2)}) copy-start(bf16[8,2,512,256]{2,3,1,0:T(8,128)(2,1)} %copy.169) | copy-start | bytes 12582916
  282.2 5.6 %copy-start.8 = (bf16[8,2,512,256]{2,3,1,0:T(8,128)(2,1)S(1)}, bf16[8,2,512,256]{2,3,1,0:T(8,128)(2,1)}, u32[]{:S(2)}) copy-start(bf16[8,2,512,256]{2,3,1,0:T(8,128)(2,1)} %get-tuple-element.141) | copy-start | bytes 12582916
  298.4 1.2 copy-start.10
  298.4 5.8 %copy-start.1 = (bf16[8,2,512,256]{2,3,1,0:T(8,128)(2,1)S(1)}, bf16[8,2,512,256]{2,3,1,0:T(8,128)(2,1)}, u32[]{:S(2)}) copy-start(bf16[8,2,512,256]{2,3,1,0:T(8,128)(2,1)} %copy.168) | copy-start | bytes 12582916
  304.2 6.5 %copy-start.11 = (bf16[8,1,256,256]{3,2,1,0:T(8,128)(2,1)S(1)}, bf16[8,1,256,256]{3,2,1,0:T(8,128)(2,1)}, u32[]{:S(2)}) copy-start(bf16[8,1,256,256]{3,2,1,0:T(8,128)(2,1)} %get-tuple-element.124) | copy-start | bytes 3145732
  304.2 6.5 %copy-start.12 = (bf16[8,1,256,256]{3,2,1,0:T(8,128)(2,1)S(1)}, bf16[8,1,256,256]{3,2,1,0:T(8,128)(2,1)}, u32[]{:S(2)}) copy-start(bf16[8,1,256,256]{3,2,1,0:T(8,128)(2,1)} %get-tuple-element.125) | copy-start | bytes 3145732
  310.6 4.2 copy-start.5
Sparse Core Ops, SparseCore 0:
  23.8 170.8 all-gather.2
  322.5 94.5 reduce-scatter.3
where the time goes:
time: 427 us; the launch traced here: 425 us
  waiting for transfers between devices  229 us (54%)
  local copies, waits for them, and re-layouts  72.1 us (17%)
  other arithmetic  52 us (12%)
  matrix products  30 us (7%)
  blocking collectives  23.6 us (6%)
  between operations  18.3 us (4%)
    all_gather x1, waiting for transfers between devices, per_device(): lax.all_gather(owned, 'tile', axis=2, tiled=True)  139 us
    unnamed x3, waiting for transfers between devices  90.2 us
    unnamed x39, local copies, waits for them, and re-layouts  38.4 us
    all_gather x1, blocking collectives, per_device(): lax.all_gather(brightness, 'tile', axis=1, tiled=True)  23.6 us
    dot_general x2, matrix products, predict(): jnp.einsum('tdckr,tckq->tdrq', stacked, cols_f, preferred_element_type=jn...  17.1 us
    dot_general x2, matrix products, pull_back(): jnp.einsum('tdcrq,tckq->tdkr', rstack, cols_f, preferred_element_type=jnp...  12.9 us
    dynamic_slice x1, local copies, waits for them, and re-layouts, per_device(): block_one = lax.dynamic_slice_in_dim(gathered, start_one, span, 3)  12.4 us
    cond x2, local copies, waits for them, and re-layouts, unit_work(): lax.cond(diag_tile, lambda: predict(block_two, block_two, bright_all), la...  10.8 us
  transfers between devices with their start and end apart: 2, of which 2 were waited for; matrix products, arithmetic and copies ran while one was open for 2% of the time, Pallas kernels for 0%

commit v1 on v0

v1 whole, which is shorter than its diff:
```python
import functools
import math

import jax
import jax.numpy as jnp
import numpy as np
from jax import lax
from jax.experimental import pallas as pl
from jax.experimental.pallas import tpu as pltpu
from jax.sharding import PartitionSpec as P

BLOCKS = 8
CHUNKS = 4


def unit_table(block_count):
    first_list = []
    second_list = []
    diag_list = []
    for row_block in range(block_count):
        for col_block in range(row_block + 1, block_count):
            first_list.append(row_block)
            second_list.append(col_block)
            diag_list.append(0)
    for pair_index in range(block_count // 2):
        first_list.append(2 * pair_index)
        second_list.append(2 * pair_index + 1)
        diag_list.append(1)
    return np.stack([first_list, second_list, diag_list], 1).astype(np.int32)


def turn_polynomials():
    nodes = 0.125 + 0.125 * np.cos(np.pi * (np.arange(64) + 0.5) / 64)
    root = np.sqrt(nodes)
    fit = np.polynomial.Polynomial.fit
    sine = fit(nodes, np.sin(2 * np.pi * root) / root, 7, domain=[0, 0.25]).convert()
    cosine = fit(nodes, np.cos(2 * np.pi * root), 8, domain=[0, 0.25]).convert()
    return [float(c) for c in sine.coef], [float(c) for c in cosine.coef]


def horner(coefs, x):
    total = coefs[-1]
    for coef in coefs[-2::-1]:
        total = total * x + coef
    return total


def build_kernel(first_slot, beam_ref, uvw_ref, dirs_ref, list_ref, out_ref):
    slot = first_slot + pl.program_id(0)
    pool = dirs_ref.shape[1]
    slots = list_ref.shape[1]
    picked = lax.broadcasted_iota(jnp.int32, list_ref.shape, 1) == slot
    chosen_id = jnp.sum(jnp.where(picked, list_ref[...], 0), axis=1, keepdims=True)
    chosen = chosen_id == lax.broadcasted_iota(jnp.int32, (list_ref.shape[0], pool), 1)
    east = jnp.sum(jnp.where(chosen, dirs_ref[0:1, :], 0.0), axis=1, keepdims=True)
    north = jnp.sum(jnp.where(chosen, dirs_ref[1:2, :], 0.0), axis=1, keepdims=True)
    depth = jnp.sqrt(1.0 - east * east - north * north) - 1.0
    sin_coefs, cos_coefs = turn_polynomials()
    width = 512
    for start in range(0, beam_ref.shape[3], width):
        cols = pl.ds(start, width)
        delay = (
            uvw_ref[0, 0:1, cols] * east
            + uvw_ref[0, 1:2, cols] * north
            + uvw_ref[0, 2:3, cols] * depth
        )
        turn = delay - jnp.floor(delay + 0.5)
        square = turn * turn
        sine = horner(sin_coefs, square) * turn
        cosine = horner(cos_coefs, square)
        real = beam_ref[0, 0, :, cols].astype(jnp.float32)
        imag = beam_ref[0, 1, :, cols].astype(jnp.float32)
        out_ref[0, 0, :, cols] = (real * cosine + imag * sine).astype(jnp.bfloat16)
        out_ref[0, 1, :, cols] = (imag * cosine - real * sine).astype(jnp.bfloat16)


def build_factors(first_slot, slot_count, station_beam, antenna_uvw, source_dirs, list_cols):
    _, _, per_group, antennas = station_beam.shape
    return pl.pallas_call(
        functools.partial(build_kernel, first_slot),
        grid=(slot_count,),
        in_specs=[
            pl.BlockSpec((1, 2, per_group, antennas), lambda t: (first_slot + t, 0, 0, 0)),
            pl.BlockSpec((1, 3, antennas), lambda t: (first_slot + t, 0, 0)),
            pl.BlockSpec(source_dirs.shape, lambda t: (0, 0)),
            pl.BlockSpec(list_cols.shape, lambda t: (0, 0)),
        ],
        out_specs=pl.BlockSpec((1, 2, per_group, antennas), lambda t: (t, 0, 0, 0)),
        out_shape=jax.ShapeDtypeStruct((slot_count, 2, per_group, antennas), jnp.bfloat16),
        compiler_params=pltpu.CompilerParams(vmem_limit_bytes=32 * 1024 * 1024),
        name="build_factors",
    )(station_beam, antenna_uvw, source_dirs, list_cols)


def flat(parts, real, imag):
    groups, per_group, span = real.shape
    return jnp.stack([real, imag], 1).reshape(groups * 2 * per_group, span)


def unit_kernel(first_slot, tab_ref, one_ref, two_ref, vis_ref, keep_one_ref, keep_two_ref, bright_ref, *rest):
    res_ref, grad_ref, total_ref = rest[-3:]
    unit = pl.program_id(1)
    slot = first_slot + pl.program_id(0)
    groups, _, _, per_group, span = one_ref.shape
    rows = groups * 2 * per_group

    def dot(a, b):
        return lax.dot_general(a, b, (((1,), (0,)), ((), ())), preferred_element_type=jnp.float32)

    bright = jnp.broadcast_to(bright_ref[pl.ds(slot, 1), :], (128, groups * per_group)).T
    bright = jnp.concatenate([bright] * (span // 128), 1).reshape(groups, 1, per_group, span)

    def scaled_of(factors):
        return (factors.astype(jnp.float32) * bright).astype(jnp.bfloat16)

    def turned_of(factors):
        return jnp.stack([factors[:, 1], -factors[:, 0]], 1)

    def flat_of(factors):
        return factors.reshape(rows, span)

    def outer(a, b):
        row_ids = lax.broadcasted_iota(jnp.int32, a.shape, 0)
        a = jnp.where(row_ids == slot, a, 0.0)
        return lax.dot_general(a, b, (((0,), (0,)), ((), ())), preferred_element_type=jnp.float32)

    def pull(factors, res_re, res_im):
        flat_f = flat_of(factors)
        with_re = dot(flat_f, res_re).reshape(groups, 2, per_group, span)
        with_im = dot(flat_f, res_im).reshape(groups, 2, per_group, span)
        return with_re, with_im

    def add_grad(value):
        value = value.reshape(groups * per_group, span)
        folded = value[:, :128]
        for start in range(128, span, 128):
            folded = folded + value[:, start : start + 128]

        @pl.when(unit == 0)
        def _():
            total_ref[...] = folded

        @pl.when(unit > 0)
        def _():
            total_ref[...] += folded

    vis_re = vis_ref[0, 0, 0].astype(jnp.float32)
    vis_im = vis_ref[0, 0, 1].astype(jnp.float32)

    @pl.when(tab_ref[unit, 2] == 0)
    def _():
        one = one_ref[:, 0]
        two = two_ref[:, 0]
        lhs = flat_of(scaled_of(one)).T
        pred_re = dot(lhs, flat_of(two))
        pred_im = -dot(lhs, flat_of(turned_of(two)))
        weights = outer(keep_one_ref[...], keep_two_ref[...])
        res_re = (weights * (vis_re - pred_re)).astype(jnp.bfloat16)
        res_im = (weights * (vis_im - pred_im)).astype(jnp.bfloat16)
        res_ref[0, 0, 0] = res_re
        res_ref[0, 0, 1] = res_im
        with_re, with_im = pull(one, res_re, res_im)
        sum_re = with_re[:, 0] + with_im[:, 1]
        sum_im = with_im[:, 0] - with_re[:, 1]
        add_grad(sum_re * two[:, 0].astype(jnp.float32) - sum_im * two[:, 1].astype(jnp.float32))

    @pl.when(tab_ref[unit, 2] == 1)
    def _():
        one = one_ref[:, 0]
        two = two_ref[:, 0]
        row_ids = lax.broadcasted_iota(jnp.int32, (span, span), 0)
        col_ids = lax.broadcasted_iota(jnp.int32, (span, span), 1)
        upper = row_ids < col_ids
        lower = row_ids > col_ids
        lhs = flat_of(scaled_of(one)).T
        first_re = dot(lhs, flat_of(one))
        first_im = -dot(lhs, flat_of(turned_of(one)))
        scaled = scaled_of(two)
        lhs = flat_of(two).T
        second_re = dot(lhs, flat_of(scaled))
        second_im = dot(lhs, flat_of(turned_of(scaled)))
        keep_one = keep_one_ref[...]
        keep_two = keep_two_ref[...]
        weights = jnp.where(upper, outer(keep_one, keep_one), 0.0) + jnp.where(
            lower, outer(keep_two, keep_two), 0.0
        )
        res_re = (weights * (vis_re - jnp.where(upper, first_re, second_re))).astype(jnp.bfloat16)
        res_im = (weights * (vis_im - jnp.where(upper, first_im, second_im))).astype(jnp.bfloat16)
        res_ref[0, 0, 0] = res_re
        res_ref[0, 0, 1] = res_im
        none = jnp.zeros_like(res_re)
        with_re, with_im = pull(one, jnp.where(upper, res_re, none), jnp.where(upper, res_im, none))
        sum_re = with_re[:, 0] + with_im[:, 1]
        sum_im = with_im[:, 0] - with_re[:, 1]
        value = sum_re * one[:, 0].astype(jnp.float32) - sum_im * one[:, 1].astype(jnp.float32)
        with_re, with_im = pull(two, jnp.where(lower, res_re, none), jnp.where(lower, res_im, none))
        sum_re = with_re[:, 0] - with_im[:, 1]
        sum_im = with_im[:, 0] + with_re[:, 1]
        value += sum_re * two[:, 0].astype(jnp.float32) + sum_im * two[:, 1].astype(jnp.float32)
        add_grad(value)

    @pl.when(unit == pl.num_programs(1) - 1)
    def _():
        grad_ref[0] = jnp.sum(total_ref[...].T, axis=0, keepdims=True)


def unit_work(first_slot, slot_count, table, gathered, visibility, keep, bright, residual):
    units_dev, slots, _, span, _ = visibility.shape
    groups, _, _, per_group, _ = gathered.shape
    in_specs = [
        pl.BlockSpec((groups, 1, 2, per_group, span), lambda t, u, tab: (0, t, 0, 0, tab[u, 0])),
        pl.BlockSpec((groups, 1, 2, per_group, span), lambda t, u, tab: (0, t, 0, 0, tab[u, 1])),
        pl.BlockSpec((1, 1, 2, span, span), lambda t, u, tab: (u, first_slot + t, 0, 0, 0)),
        pl.BlockSpec((slots, span), lambda t, u, tab: (0, tab[u, 0])),
        pl.BlockSpec((slots, span), lambda t, u, tab: (0, tab[u, 1])),
        pl.BlockSpec(bright.shape, lambda t, u, tab: (0, 0)),
    ]
    operands = [table, gathered, gathered, visibility, keep, keep, bright]
    aliases = {}
    if residual is not None:
        in_specs.append(pl.BlockSpec(memory_space=pl.ANY))
        operands.append(residual)
        aliases = {7: 0}
    flops = 16 * slot_count * units_dev * groups * per_group * span * span
    return pl.pallas_call(
        functools.partial(unit_kernel, first_slot),
        grid_spec=pltpu.PrefetchScalarGridSpec(
            num_scalar_prefetch=1,
            grid=(slot_count, units_dev),
            in_specs=in_specs,
            out_specs=[
                pl.BlockSpec((1, 1, 2, span, span), lambda t, u, tab: (u, first_slot + t, 0, 0, 0)),
                pl.BlockSpec((1, 1, groups * per_group), lambda t, u, tab: (t, 0, 0)),
            ],
            scratch_shapes=[pltpu.VMEM((groups * per_group, 128), jnp.float32)],
        ),
        out_shape=[
            jax.ShapeDtypeStruct(visibility.shape, jnp.bfloat16),
            jax.ShapeDtypeStruct((slot_count, 1, groups * per_group), jnp.float32),
        ],
        input_output_aliases=aliases,
        compiler_params=pltpu.CompilerParams(vmem_limit_bytes=48 * 1024 * 1024),
        cost_estimate=pl.CostEstimate(flops=flops, bytes_accessed=flops // 128, transcendentals=0),
        name="unit_work",
    )(*operands)


def per_device(
    visibility, station_beam, antenna_uvw, source_dirs, source_flux, visible_list, antenna_flags
):
    units_dev = visibility.shape[0]
    slot_count, _, per_group, antennas = station_beam.shape
    chunk = slot_count // CHUNKS
    tile_index = lax.axis_index("tile")
    table = lax.dynamic_slice_in_dim(
        jnp.asarray(unit_table(BLOCKS)), tile_index * units_dev, units_dev, 0
    )
    list_cols = visible_list.T
    gathered = []
    for first_slot in range(0, slot_count, chunk):
        owned = build_factors(first_slot, chunk, station_beam, antenna_uvw, source_dirs, list_cols)
        gathered.append(lax.all_gather(owned, "tile", axis=0))
    chosen = visible_list[:, :, None] == jnp.arange(source_flux.shape[0], dtype=jnp.int32)
    brightness = jnp.sum(jnp.where(chosen, source_flux.astype(jnp.float32), 0.0), axis=2)
    bright_all = lax.all_gather(brightness, "tile", axis=1, tiled=True)
    keep = 1.0 - antenna_flags.astype(jnp.float32)
    residual = None
    grads = []
    for index, first_slot in enumerate(range(0, slot_count, chunk)):
        residual, grad = unit_work(
            first_slot, chunk, table, gathered[index], visibility, keep, bright_all, residual
        )
        grads.append(grad)
    partial_total = jnp.concatenate(grads, 0)[:, 0]
    summed = lax.psum_scatter(partial_total, "tile", scatter_dimension=1, tiled=True)
    flux_grad = summed * (-1.0 / (8.0 * antennas))
    return (residual, flux_grad)


def solution(mesh):
    return jax.shard_map(
        per_device,
        mesh=mesh,
        in_specs=(
            P("tile", "grp", None, None, None),
            P("grp", None, "tile", None),
            P("grp", None, None),
            P(None, "tile"),
            P(("grp", "tile")),
            P(None, "tile"),
            P("grp", None),
        ),
        out_specs=(P("tile", "grp", None, None, None), P("grp", "tile")),
        check_vma=False,
    )
```

time: 427 us -> 393 us (0.920)
  waiting for transfers between devices: 229 us -> 298 us
  local copies, waits for them, and re-layouts: 72.1 us -> 16 us
  other arithmetic: 52 us -> 0.81 us
  Pallas kernels: 0 us -> 38.8 us
  matrix products: 30 us -> 0 us
  between operations: 18.3 us -> 13.9 us
    all_gather x1 -> x4, waiting for transfers between devices: 139 us -> 243 us  [per_device(): gathered.append(lax.all_gather(owned, 'tile', axis=0))]
    pallas_call x0 -> x8, Pallas kernels: none -> 38.8 us  [the longest x4 30.8 us: unit_work(): pl.pallas_call(functools.partial(unit_kernel, first_slot), grid_spec=pltp...]
    unnamed x3 -> x6, waiting for transfers between devices: 90.2 us -> 55.9 us
    another operation x7 -> x0, other arithmetic: 31 us -> none
    dot_general x4 -> x0, matrix products: 30 us -> none  [the longest x2 17.1 us: predict(): jnp.einsum('tdckr,tckq->tdrq', stacked, cols_f, preferred_element_type=jn...]
    unnamed x39 -> x29, local copies, waits for them, and re-layouts: 38.4 us -> 15.3 us
    dynamic_slice x4 -> x1, local copies, waits for them, and re-layouts: 13.8 us -> 0.7 us  [per_device(): lax.dynamic_slice_in_dim(jnp.asarray(unit_table(BLOCKS)), tile_index * un...]
    cond x2 -> x0, local copies, waits for them, and re-layouts: 10.8 us -> none  [unit_work(): lax.cond(diag_tile, lambda: predict(block_two, block_two, bright_all), la...]
  transfers between devices with their start and end apart: 2 -> 5, of which waited for: 2 -> 5; matrix products, arithmetic and copies ran while one was open for 2% -> 0% of each run, Pallas kernels for 0% -> 7%
where the time goes in v1:
time: 393 us; the launch traced here: 392 us
  waiting for transfers between devices  298 us (76%)
  Pallas kernels  38.8 us (10%)
  blocking collectives  23.9 us (6%)
  local copies, waits for them, and re-layouts  16 us (4%)
  between operations  13.9 us (4%)
    all_gather x4, waiting for transfers between devices, per_device(): gathered.append(lax.all_gather(owned, 'tile', axis=0))  243 us
    unnamed x6, waiting for transfers between devices  55.9 us
    pallas_call x4, Pallas kernels, unit_work(): pl.pallas_call(functools.partial(unit_kernel, first_slot), grid_spec=pltp...  30.8 us
    all_gather x1, blocking collectives, per_device(): bright_all = lax.all_gather(brightness, 'tile', axis=1, tiled=True)  23.9 us
    unnamed x29, local copies, waits for them, and re-layouts  15.3 us
    pallas_call x4, Pallas kernels, build_factors(): pl.pallas_call(functools.partial(build_kernel, first_slot), grid=(slot_co...  8 us
  transfers between devices with their start and end apart: 5, of which 5 were waited for; matrix products, arithmetic and copies ran while one was open for 0% of the time, Pallas kernels for 7%

profile of v1, /device:TPU:0, one launch (start us, length us, event | category | flops | bytes accessed | tf_op | source)
XLA Modules:
  0.0 392.0 jit_solution(1287410708848417455)
XLA Ops:
  7.2 0.0 copy-start.8
  7.2 0.0 all-gather.16.cloned.1.call-start
  7.2 0.8 copy.24
  8.0 1.1 copy.25.uvw_ref
  9.1 0.0 copy-start.4
  9.1 1.6 copy-done.4
  10.6 0.0 copy-start.6
  10.6 0.7 copy-done.6
  11.3 2.0 build_factors.7
  13.3 0.0 all-gather.16.cloned.1.call-update
  13.3 0.0 all-gather.14.cloned.1.call-start
  13.4 0.0 copy-done.5
  13.4 0.0 copy-start.7
  13.4 0.7 copy-done.7
  14.1 2.0 build_factors.6
  16.1 0.0 all-gather.14.cloned.1.call-update
  16.1 0.0 all-gather.12.cloned.1.call-start
  16.1 0.0 copy-done.8
  16.2 2.0 build_factors.5
  18.2 0.0 all-gather.12.cloned.1.call-update
  18.2 0.0 all-gather.10.cloned.1.call-start
  18.2 2.0 build_factors.4
  20.3 0.0 all-gather.10.cloned.1.call-update
  20.3 0.0 reduce-scatter.4.cloned.1.call-start
  20.3 0.0 copy-done.11
  20.4 0.0 copy-done.10
  20.4 0.2 select_reduce_fusion
  20.6 23.9 %all-gather.4 = f32[16,32,8]{1,2,0:T(8,128)S(1)} all-gather(f32[1,32,8]{1,2,0:T(8,128)S(1)} %bitcast.33), channel_id=1, replica_groups=mesh['grp'=2,'tile'=16] {'tile'}, dimensions={0}, use_global_device_ids=true | all-gather | bytes 17408 | tf_op jit(solution)/shard_map/all_gather | solution.py:265
  44.4 0.1 reshape.10
  44.5 0.7 constant_dynamic-slice_fusion.tab_ref
  45.2 0.0 copy-done.9
  45.2 46.1 %all-gather.16.cloned.1.call-done = bf16[32,2,32,2048]{3,2,1,0:T(8,128)(2,1)} async-done(((bf16[2,2,32,2048]{3,2,1,0:T(8,128)(2,1)}), bf16[32,2,32,2048]{3,2,1,0:T(8,128)(2,1)}) %all-gather.16.cloned.1.call-update) | async-done | bytes 8388624 | tf_op jit(solution)/shard_map/all_gather | solution.py:262
  91.4 2.2 copy-done
  93.6 7.7 %unit_work.4 = (bf16[2,8,2,256,256]{4,3,2,1,0:T(8,128)(2,1)}, f32[2,1,512]{2,1,0:T(1,128)S(1)}) custom-call(s32[2,3]{1,0:T(2,128)S(1)} %constant_dynamic-slice_fusion.tab_ref, bf16[16,2,2,32,2048]{4,3,2,1,0:T(8,128)(2,1)} %bitcast.23, bf16[16,2,2,32,2048]{4,3,2,1,0:T(8,128)(2,1)} %bitcast.24, bf16[2,8,2,256,256]{4,3,2,1,0:T(8,128)(2,1)S(1)} %copy-done, ...), custom_call_target="tpu_custom_call" | custom-call | flops 2147483648 | bytes 16777216 | tf_op jit(solution)/shard_map/unit_work/pallas_call | solution.py:225
  101.2 65.5 %all-gather.14.cloned.1.call-done = bf16[32,2,32,2048]{3,2,1,0:T(8,128)(2,1)} async-done(((bf16[2,2,32,2048]{3,2,1,0:T(8,128)(2,1)}), bf16[32,2,32,2048]{3,2,1,0:T(8,128)(2,1)}) %all-gather.14.cloned.1.call-update) | async-done | bytes 8388624 | tf_op jit(solution)/shard_map/all_gather | solution.py:262
  166.7 2.2 copy-done.1
  168.9 7.7 %unit_work.5 = (bf16[2,8,2,256,256]{4,3,2,1,0:T(8,128)(2,1)}, f32[2,1,512]{2,1,0:T(1,128)S(1)}) custom-call(s32[2,3]{1,0:T(2,128)S(1)} %constant_dynamic-slice_fusion.tab_ref, bf16[16,2,2,32,2048]{4,3,2,1,0:T(8,128)(2,1)} %bitcast.25, bf16[16,2,2,32,2048]{4,3,2,1,0:T(8,128)(2,1)} %bitcast.26, ...), custom_call_target="tpu_custom_call", output_to_operand_aliasing={{0}: (7, {})} | custom-call | flops 2147483648 | bytes 16777216 | tf_op jit(solution)/shard_map/unit_work/pallas_call | solution.py:225
  176.6 65.5 %all-gather.12.cloned.1.call-done = bf16[32,2,32,2048]{3,2,1,0:T(8,128)(2,1)} async-done(((bf16[2,2,32,2048]{3,2,1,0:T(8,128)(2,1)}), bf16[32,2,32,2048]{3,2,1,0:T(8,128)(2,1)}) %all-gather.12.cloned.1.call-update) | async-done | bytes 8388624 | tf_op jit(solution)/shard_map/all_gather | solution.py:262
  242.1 2.2 copy-done.2
  244.3 7.7 %unit_work.6 = (bf16[2,8,2,256,256]{4,3,2,1,0:T(8,128)(2,1)}, f32[2,1,512]{2,1,0:T(1,128)S(1)}) custom-call(s32[2,3]{1,0:T(2,128)S(1)} %constant_dynamic-slice_fusion.tab_ref, bf16[16,2,2,32,2048]{4,3,2,1,0:T(8,128)(2,1)} %bitcast.27, bf16[16,2,2,32,2048]{4,3,2,1,0:T(8,128)(2,1)} %bitcast.28, ...), custom_call_target="tpu_custom_call", output_to_operand_aliasing={{0}: (7, {})} | custom-call | flops 2147483648 | bytes 16777216 | tf_op jit(solution)/shard_map/unit_work/pallas_call | solution.py:225
  252.0 65.5 %all-gather.10.cloned.1.call-done = bf16[32,2,32,2048]{3,2,1,0:T(8,128)(2,1)} async-done(((bf16[2,2,32,2048]{3,2,1,0:T(8,128)(2,1)}), bf16[32,2,32,2048]{3,2,1,0:T(8,128)(2,1)}) %all-gather.10.cloned.1.call-update) | async-done | bytes 8388624 | tf_op jit(solution)/shard_map/all_gather | solution.py:262
  317.4 2.2 copy-done.3
  319.6 7.7 %unit_work.7 = (bf16[2,8,2,256,256]{4,3,2,1,0:T(8,128)(2,1)}, f32[2,1,512]{2,1,0:T(1,128)S(1)}) custom-call(s32[2,3]{1,0:T(2,128)S(1)} %constant_dynamic-slice_fusion.tab_ref, bf16[16,2,2,32,2048]{4,3,2,1,0:T(8,128)(2,1)} %bitcast.29, bf16[16,2,2,32,2048]{4,3,2,1,0:T(8,128)(2,1)} %bitcast.30, ...), custom_call_target="tpu_custom_call", output_to_operand_aliasing={{0}: (7, {})} | custom-call | flops 2147483648 | bytes 16777216 | tf_op jit(solution)/shard_map/unit_work/pallas_call | solution.py:225
  327.3 0.8 copy.32
  328.2 0.0 reduce-scatter.4.cloned.1.call-update
  328.2 55.9 %reduce-scatter.4.cloned.1.call-done = f32[32,8]{1,0:T(8,128)} async-done(((f32[512,8]{1,0:T(8,128)}), f32[32,8]{1,0:T(8,128)}) %reduce-scatter.4.cloned.1.call-update) | async-done | bytes 1040
  384.0 0.8 copy.31
  384.8 0.6 broadcast_multiply_fusion
  (12 shorter events, 0.1 us)
Async XLA Ops:
  7.2 9.0 %copy-start.8 = (f32[2,256]{1,0:T(2,128)S(1)}, f32[2,256]{1,0:T(2,128)}, u32[]{:S(2)}) copy-start(f32[2,256]{1,0:T(2,128)} %dirs_ref.7) | copy-start | bytes 6148
  7.2 84.2 %all-gather.16.cloned.1.call-start = ((), (), s32[]{:S(2)}) async-start(), calls=%async_computation.4 | async-start | bytes 8912896 | tf_op jit(solution)/shard_map/all_gather | solution.py:262
  9.1 1.6 copy-start.4
  10.6 0.7 copy-start.6
  11.3 2.1 copy-start.5
  13.3 153.4 %all-gather.14.cloned.1.call-start = ((), (), s32[]{:S(2)}) async-start(), calls=%async_computation.3 | async-start | bytes 8912896 | tf_op jit(solution)/shard_map/all_gather | solution.py:262
  13.4 0.7 copy-start.7
  16.1 4.3 %copy-start.11 = (bf16[256]{0:T(256)(128)(2,1)S(1)}, bf16[256]{0:T(256)(128)(2,1)}, u32[]{:S(2)}) copy-start(bf16[256]{0:T(256)(128)(2,1)} %param.12) | copy-start | bytes 1540
  16.1 4.3 %copy-start.10 = (s32[8,32]{1,0:T(8,128)S(1)}, s32[8,32]{1,0:T(8,128)}, u32[]{:S(2)}) copy-start(s32[8,32]{1,0:T(8,128)} %param.13) | copy-start | bytes 3076
  16.1 29.1 %copy-start.9 = (s32[8,2048]{1,0:T(8,128)S(1)}, s32[8,2048]{1,0:T(8,128)}, u32[]{:S(2)}) copy-start(s32[8,2048]{1,0:T(8,128)} %param.14) | copy-start | bytes 196612
  16.1 226.0 %all-gather.12.cloned.1.call-start = ((), (), s32[]{:S(2)}) async-start(), calls=%async_computation.2 | async-start | bytes 8912896 | tf_op jit(solution)/shard_map/all_gather | solution.py:262
  18.2 299.2 %all-gather.10.cloned.1.call-start = ((), (), s32[]{:S(2)}) async-start(), calls=%async_computation.1 | async-start | bytes 8912896 | tf_op jit(solution)/shard_map/all_gather | solution.py:262
  20.3 363.8 %reduce-scatter.4.cloned.1.call-start = ((), (), s32[]{:S(2)}) async-start(), calls=%async_computation.5 | async-start | bytes 278528
  91.4 2.2 copy-start
  166.7 2.2 copy-start.1
  242.1 2.2 copy-start.2
  317.4 2.2 copy-start.3
Sparse Core Ops, SparseCore 0:
  13.5 77.8 all-gather.15
  93.5 73.1 all-gather.13
  168.9 73.1 all-gather.11
  244.1 73.2 all-gather.9
  328.3 55.6 reduce-scatter.3

commit v2 on v1

v2 whole, which is shorter than its diff:
```python
import functools
import math

import jax
import jax.numpy as jnp
import numpy as np
from jax import lax
from jax.experimental import pallas as pl
from jax.experimental.pallas import tpu as pltpu
from jax.sharding import PartitionSpec as P


def unit_table(block_count):
    first_list = []
    second_list = []
    diag_list = []
    for row_block in range(block_count):
        for col_block in range(row_block + 1, block_count):
            first_list.append(row_block)
            second_list.append(col_block)
            diag_list.append(0)
    for pair_index in range(block_count // 2):
        first_list.append(2 * pair_index)
        second_list.append(2 * pair_index + 1)
        diag_list.append(1)
    return np.stack([first_list, second_list, diag_list], 1).astype(np.int32)


def turn_polynomials():
    nodes = 0.125 + 0.125 * np.cos(np.pi * (np.arange(64) + 0.5) / 64)
    root = np.sqrt(nodes)
    fit = np.polynomial.Polynomial.fit
    sine = fit(nodes, np.sin(2 * np.pi * root) / root, 7, domain=[0, 0.25]).convert()
    cosine = fit(nodes, np.cos(2 * np.pi * root), 8, domain=[0, 0.25]).convert()
    return [float(c) for c in sine.coef], [float(c) for c in cosine.coef]


def horner(coefs, x):
    total = coefs[-1]
    for coef in coefs[-2::-1]:
        total = total * x + coef
    return total


def build_kernel(chunk, parts, picks_ref, *refs):
    sets, refs = refs[: 4 * parts], refs[4 * parts :]
    uvw_ref, out_ref, pick_ref = refs
    first, count, with_bright = chunk
    per_group, span = out_ref.shape[2:]
    blocks = uvw_ref.shape[2] // span
    places = pick_ref.shape[0] // (2 * count)
    sin_coefs, cos_coefs = turn_polynomials()
    for part in range(parts):
        beam_ref, dirs_ref, flux_ref, list_ref = sets[4 * part : 4 * part + 4]
        pool = dirs_ref.shape[1]
        slots = list_ref.shape[1]
        pool_ids = lax.broadcasted_iota(jnp.int32, (per_group, pool), 1)
        lanes = lax.broadcasted_iota(jnp.int32, (per_group, span), 1)
        if with_bright:
            bright = jnp.zeros((per_group, span), jnp.float32)
            for slot in range(slots):
                chosen = list_ref[:, slot : slot + 1] == pool_ids
                flux = jnp.sum(jnp.where(chosen, flux_ref[...], 0.0), axis=1, keepdims=True)
                bright = jnp.where(lanes == slot, flux, bright)
            out_ref[part, 2 * count * blocks] = bright.astype(jnp.bfloat16)
        for index in range(count):
            slot = first + index
            chosen = list_ref[:, slot : slot + 1] == pool_ids
            east = jnp.sum(jnp.where(chosen, dirs_ref[0:1, :], 0.0), axis=1, keepdims=True)
            north = jnp.sum(jnp.where(chosen, dirs_ref[1:2, :], 0.0), axis=1, keepdims=True)
            depth = jnp.sqrt(1.0 - east * east - north * north) - 1.0
            for block in range(blocks):
                cols = pl.ds(block * span, span)
                delay = (
                    uvw_ref[slot, 0:1, cols] * east
                    + uvw_ref[slot, 1:2, cols] * north
                    + uvw_ref[slot, 2:3, cols] * depth
                )
                turn = delay - jnp.floor(delay + 0.5)
                square = turn * turn
                sine = horner(sin_coefs, square) * turn
                cosine = horner(cos_coefs, square)
                real = beam_ref[index, 0, :, cols].astype(jnp.float32)
                imag = beam_ref[index, 1, :, cols].astype(jnp.float32)
                row = 2 * index * blocks + block
                out_ref[part, row] = (real * cosine + imag * sine).astype(jnp.bfloat16)
                out_ref[part, row + blocks] = (imag * cosine - real * sine).astype(jnp.bfloat16)
    copy_blocks(out_ref.at[0], pick_ref, 0, count, blocks, places, lambda place: picks_ref[place])
    if with_bright:
        pick_ref[2 * count * places] = out_ref[0, 2 * count * blocks]


def copy_blocks(source, target, start, count, blocks, places, block_at):
    for place in range(places):
        block = block_at(place)
        for row in range(2 * count):
            target[start + row * places + place] = source[row * blocks + block]


def chunk_rows(chunk, places):
    return 2 * chunk[1] * places + chunk[2]


def build_factors(chunk, span, sets, antenna_uvw, picks):
    first, count, _ = chunk
    _, _, per_group, antennas = sets[0][0].shape
    blocks = antennas // span
    whole = pl.BlockSpec(memory_space=pltpu.VMEM)
    assert first % count == 0
    in_specs = [pl.BlockSpec(memory_space=pltpu.SMEM)]
    operands = [picks]
    for beam, *small in sets:
        in_specs.append(
            pl.BlockSpec((count, 2, per_group, antennas), lambda t: (first // count, 0, 0, 0))
        )
        in_specs += [pl.BlockSpec(array.shape, lambda t: (0, 0)) for array in small]
        operands += [beam, *small]
    in_specs.append(pl.BlockSpec(antenna_uvw.shape, lambda t: (0, 0, 0)))
    out_shapes = [
        (len(sets), chunk_rows(chunk, blocks), per_group, span),
        (chunk_rows(chunk, picks.shape[0]), per_group, span),
    ]
    return pl.pallas_call(
        functools.partial(build_kernel, chunk, len(sets)),
        grid=(1,),
        in_specs=in_specs,
        out_specs=[
            pl.BlockSpec(out_shapes[0], lambda t: (0, 0, 0, 0)),
            pl.BlockSpec(out_shapes[1], lambda t: (0, 0, 0)),
        ],
        out_shape=[jax.ShapeDtypeStruct(shape, jnp.bfloat16) for shape in out_shapes],
        compiler_params=pltpu.CompilerParams(vmem_limit_bytes=40 * 1024 * 1024),
        name="build_factors",
    )(*operands, antenna_uvw)


def pick_side_kernel(items, blocks, tab_ref, *refs):
    out_ref = refs[-1]
    start = 0
    for ref, (chunk, lead) in zip(refs, items):
        source = ref if lead is None else ref.at[lead]
        copy_blocks(
            source, out_ref, start, chunk[1], blocks, SIDE_PLACES, lambda n: tab_ref[SIDE_ROW, n]
        )
        start += chunk_rows(chunk, SIDE_PLACES)
        if chunk[2]:
            out_ref[start - 1] = source[2 * chunk[1] * blocks]


def pick_core_kernel(chunk, starts, blocks, tab_ref, chip, near, far, *refs):
    sides, (send_out, mine_out) = refs[:-2], refs[-2:]
    columns = [chip.at[0], near.at[0], near.at[1], far]
    count = chunk[1]
    for out_ref, row in ((send_out, SEND_ROW), (mine_out, MINE_ROW)):
        for lead, source in enumerate(columns):
            copy_blocks(
                source, out_ref.at[lead], 0, count, blocks, CORE_PLACES, lambda n: tab_ref[row, n]
            )
            if chunk[2]:
                out_ref[lead, 2 * count * CORE_PLACES] = source[2 * count * blocks]
        for lead, (source, start) in enumerate(zip(sides, starts)):
            copy_blocks(
                source,
                out_ref.at[len(columns) + lead],
                0,
                count,
                SIDE_PLACES,
                CORE_PLACES,
                lambda n: start + tab_ref[row + 1, n],
            )
            if chunk[2]:
                bright = source[start + 2 * count * SIDE_PLACES]
                out_ref[len(columns) + lead, 2 * count * CORE_PLACES] = bright


def pick_blocks(kernel, out_shapes, table, *arrays):
    whole = pl.BlockSpec(memory_space=pltpu.VMEM)
    return pl.pallas_call(
        kernel,
        in_specs=[pl.BlockSpec(memory_space=pltpu.SMEM)] + [whole] * len(arrays),
        out_specs=[whole] * len(out_shapes),
        out_shape=[jax.ShapeDtypeStruct(shape, jnp.bfloat16) for shape in out_shapes],
        compiler_params=pltpu.CompilerParams(vmem_limit_bytes=40 * 1024 * 1024),
        name="pick_blocks",
    )(table, *arrays)


def unit_kernel(chunk, layers, guest, tab_ref, *refs):
    factors, refs = refs[: 4 * layers], refs[4 * layers :]
    brights, refs = refs[:layers], refs[layers:]
    vis_ref, keep_one_ref, keep_two_ref = refs[:3]
    guest_ref = refs[3] if guest else None
    out_refs = refs[-4 if guest else -3 :]
    res_ref, grad_ref, total_ref = out_refs[0], out_refs[-2], out_refs[-1]
    unit = pl.program_id(1)
    slot = chunk[0] + pl.program_id(0)
    per_group, span = factors[0].shape[2:]

    def joined(which):
        parts = [ref[:, 0] for ref in factors[which * layers : (which + 1) * layers]]
        return jnp.concatenate(parts, 0).reshape(-1, span)

    def dot(a, b):
        return lax.dot_general(a, b, (((1,), (0,)), ((), ())), preferred_element_type=jnp.float32)

    def scaled_of(re, im):
        lanes = lax.broadcasted_iota(jnp.int32, (re.shape[0], brights[0].shape[3]), 1)
        rows = jnp.concatenate([ref[:, 0] for ref in brights], 0).reshape(lanes.shape)
        column = jnp.where(lanes == slot, rows.astype(jnp.float32), 0.0)
        column = jnp.sum(column, axis=1, keepdims=True)
        return (
            (re.astype(jnp.float32) * column).astype(jnp.bfloat16),
            (im.astype(jnp.float32) * column).astype(jnp.bfloat16),
        )

    def outer(a, b):
        row_ids = lax.broadcasted_iota(jnp.int32, a.shape, 0)
        a = jnp.where(row_ids == slot, a, 0.0)
        return lax.dot_general(a, b, (((0,), (0,)), ((), ())), preferred_element_type=jnp.float32)

    def cross(a_re, a_im, b_re, b_im):
        lhs = jnp.concatenate([a_re, a_im], 0).T
        rhs = jnp.concatenate(
            [jnp.concatenate([b_re, -b_im], 1), jnp.concatenate([b_im, b_re], 1)], 0
        )
        both = dot(lhs, rhs)
        return both[:, :span], both[:, span:]

    def pull(re, im, res_re, res_im, sign):
        lhs = jnp.concatenate([re, im], 1)
        rhs = jnp.concatenate(
            [
                jnp.concatenate([res_re, res_im], 1),
                jnp.concatenate([res_im, -res_re] if sign == 1 else [-res_im, res_re], 1),
            ],
            0,
        )
        both = dot(lhs, rhs)
        return both[:, :span], both[:, span:]

    def add_grad(value):
        folded = value[:, :128]
        for start in range(128, span, 128):
            folded = folded + value[:, start : start + 128]
        total_ref[...] += folded

    def put(res_re, res_im):
        if guest:

            @pl.when(unit < 2)
            def _():
                res_ref[0, 0, 0] = res_re
                res_ref[0, 0, 1] = res_im

            @pl.when(unit == 2)
            def _():
                out_refs[1][0, 0] = res_re
                out_refs[1][0, 1] = res_im
        else:
            res_ref[0, 0, 0] = res_re
            res_ref[0, 0, 1] = res_im

    def vis(part):
        if guest:
            return jnp.where(unit == 2, guest_ref[0, part], vis_ref[0, 0, part]).astype(jnp.float32)
        return vis_ref[0, 0, part].astype(jnp.float32)

    @pl.when(unit == 0)
    def _():
        total_ref[...] = jnp.zeros_like(total_ref)

    @pl.when(tab_ref[unit, 2] == 0)
    def _():
        one_re, one_im, two_re, two_im = [joined(n) for n in range(4)]
        pred_re, pred_im = cross(*scaled_of(one_re, one_im), two_re, two_im)
        weights = outer(keep_one_ref[...], keep_two_ref[...])
        res_re = (weights * (vis(0) - pred_re)).astype(jnp.bfloat16)
        res_im = (weights * (vis(1) - pred_im)).astype(jnp.bfloat16)
        put(res_re, res_im)
        sum_re, sum_im = pull(one_re, one_im, res_re, res_im, 1)
        add_grad(sum_re * two_re.astype(jnp.float32) - sum_im * two_im.astype(jnp.float32))

    @pl.when(tab_ref[unit, 2] == 1)
    def _():
        one_re, one_im, two_re, two_im = [joined(n) for n in range(4)]
        row_ids = lax.broadcasted_iota(jnp.int32, (span, span), 0)
        col_ids = lax.broadcasted_iota(jnp.int32, (span, span), 1)
        upper = row_ids < col_ids
        lower = row_ids > col_ids
        first_re, first_im = cross(*scaled_of(one_re, one_im), one_re, one_im)
        second_re, second_im = cross(two_re, two_im, *scaled_of(two_re, two_im))
        keep_one = keep_one_ref[...]
        keep_two = keep_two_ref[...]
        weights = jnp.where(upper, outer(keep_one, keep_one), 0.0) + jnp.where(
            lower, outer(keep_two, keep_two), 0.0
        )
        res_re = (weights * (vis(0) - jnp.where(upper, first_re, second_re))).astype(jnp.bfloat16)
        res_im = (weights * (vis(1) - jnp.where(upper, first_im, -second_im))).astype(jnp.bfloat16)
        put(res_re, res_im)
        none = jnp.zeros_like(res_re)
        sum_re, sum_im = pull(
            one_re, one_im, jnp.where(upper, res_re, none), jnp.where(upper, res_im, none), 1
        )
        add_grad(sum_re * one_re.astype(jnp.float32) - sum_im * one_im.astype(jnp.float32))
        sum_re, sum_im = pull(
            two_re, two_im, jnp.where(lower, res_re, none), jnp.where(lower, res_im, none), -1
        )
        add_grad(sum_re * two_re.astype(jnp.float32) + sum_im * two_im.astype(jnp.float32))

    @pl.when(unit == pl.num_programs(1) - 1)
    def _():
        grad_ref[0] = jnp.sum(total_ref[...].T, axis=0, keepdims=True)


def unit_work(chunk, table, factors, places, bright, visibility, keep, guest, residual):
    first, count, _ = chunk
    units_dev, slots, _, span, _ = visibility.shape
    steps = table.shape[0]
    per_group = factors[0].shape[2]
    groups = sum(array.shape[0] for array in factors)
    in_specs = []
    for column in (3, 4):
        for part in (0, 1):
            for array in factors:
                in_specs.append(
                    pl.BlockSpec(
                        (array.shape[0], 1, per_group, span),
                        lambda t, u, tab, column=column, part=part: (
                            0,
                            (2 * t + part) * places + tab[u, column],
                            0,
                            0,
                        ),
                    )
                )
    for array in bright:
        in_specs.append(
            pl.BlockSpec(
                (array.shape[0], 1, per_group, 128),
                lambda t, u, tab, row=array.shape[1] - 1: (0, row, 0, 0),
            )
        )
    vis_spec = pl.BlockSpec(
        (1, 1, 2, span, span),
        lambda t, u, tab: (jnp.minimum(u, units_dev - 1), first + t, 0, 0, 0),
    )
    in_specs += [
        vis_spec,
        pl.BlockSpec((slots, span), lambda t, u, tab: (0, tab[u, 0])),
        pl.BlockSpec((slots, span), lambda t, u, tab: (0, tab[u, 1])),
    ]
    operands = [table, *factors * 4, *bright, visibility, keep, keep]
    out_specs = [vis_spec]
    out_shapes = [jax.ShapeDtypeStruct(visibility.shape, jnp.bfloat16)]
    if guest is not None:
        in_specs.append(
            pl.BlockSpec((1, 2, span, span), lambda t, u, tab: (first + t, 0, 0, 0))
        )
        operands.append(guest)
        out_specs.append(pl.BlockSpec((1, 2, span, span), lambda t, u, tab: (t, 0, 0, 0)))
        out_shapes.append(jax.ShapeDtypeStruct((count, 2, span, span), jnp.bfloat16))
    out_specs.append(pl.BlockSpec((1, 1, groups * per_group), lambda t, u, tab: (t, 0, 0)))
    out_shapes.append(jax.ShapeDtypeStruct((count, 1, groups * per_group), jnp.float32))
    aliases = {}
    if residual is not None:
        in_specs.append(pl.BlockSpec(memory_space=pl.ANY))
        aliases = {len(operands): 0}
        operands.append(residual)
    flops = 16 * count * units_dev * groups * per_group * span * span
    return pl.pallas_call(
        functools.partial(unit_kernel, chunk, len(factors), guest is not None),
        grid_spec=pltpu.PrefetchScalarGridSpec(
            num_scalar_prefetch=1,
            grid=(count, steps),
            in_specs=in_specs,
            out_specs=out_specs,
            scratch_shapes=[pltpu.VMEM((groups * per_group, 128), jnp.float32)],
        ),
        out_shape=out_shapes,
        input_output_aliases=aliases,
        compiler_params=pltpu.CompilerParams(vmem_limit_bytes=48 * 1024 * 1024),
        cost_estimate=pl.CostEstimate(flops=flops, bytes_accessed=flops // 128, transcendentals=0),
        name="unit_work",
    )(*operands)


def return_kernel(moves, tab_ref, *refs):
    arrays, res_ref, sem = refs[: len(moves)], refs[-2], refs[-1]

    @pl.when(tab_ref[0] >= 0)
    def _():
        for array, (first, count) in zip(arrays, moves):
            copy = pltpu.make_async_copy(
                array, res_ref.at[tab_ref[0], pl.ds(first, count)], sem.at[0]
            )
            copy.start()
            copy.wait()


def put_returned(chunks, place, returned, residual):
    moves = [chunk[:2] for chunk in chunks]
    anywhere = pl.BlockSpec(memory_space=pl.ANY)
    return pl.pallas_call(
        functools.partial(return_kernel, moves),
        in_specs=[pl.BlockSpec(memory_space=pltpu.SMEM)] + [anywhere] * (len(moves) + 1),
        out_specs=anywhere,
        out_shape=jax.ShapeDtypeStruct(residual.shape, residual.dtype),
        scratch_shapes=[pltpu.SemaphoreType.DMA((1,))],
        input_output_aliases={len(moves) + 1: 0},
        name="put_returned",
    )(place, *returned, residual)


SIDE_ROW = 0
SEND_ROW = 1
MINE_ROW = 3
SIDE_PLACES = 6
CORE_PLACES = 4


class Routes:
    def __init__(self, planes, chips, cores, units):
        ring = [0] + list(range(1, planes, 2)) + list(range(planes - 2, 0, -2))
        count = planes * chips * cores
        units_dev = units.shape[0] // count

        def tile_of(plane, chip, core):
            return (plane * chips + chip) * cores + core

        places = [(t // (chips * cores), t // cores % chips, t % cores) for t in range(count)]

        def along(plane, step):
            return ring[(ring.index(plane) + step) % planes]

        self.near = [(t, tile_of(along(z, 1 - 2 * c), y, c)) for t, (z, y, c) in enumerate(places)]
        self.near_back = [(b, a) for a, b in self.near]
        self.near_cross = [
            (t, tile_of(along(z, 2 * c - 1), y, 1 - c)) for t, (z, y, c) in enumerate(places)
        ]
        self.far = [(t, tile_of(along(z, 2), y, c)) for t, (z, y, c) in enumerate(places)]
        self.side = [(t, tile_of(z, 1 - y, c)) for t, (z, y, c) in enumerate(places)]
        self.core = [(t, tile_of(z, y, 1 - c)) for t, (z, y, c) in enumerate(places)]
        work = [list(range(t * units_dev, (t + 1) * units_dev)) for t in range(count)]
        self.move = (14, 1, 10)
        home, index, host = self.move
        moved = work[home][index]
        work[home][index] = None
        work[host].append(moved)
        need = []
        for t in range(count):
            need.append(sorted({b for u in work[t] if u is not None for b in units[u, :2].tolist()}))
        chip_need = []
        for z, y, _ in places:
            chip_need.append(
                sorted({b for core in range(cores) for b in need[tile_of(z, y, core)]})
            )
        assert max(len(n) for n in need) <= CORE_PLACES
        assert max(len(n) for n in chip_need) <= SIDE_PLACES

        def padded(values, length=8):
            return (values + values[:1] * length)[:length]

        self.table = np.zeros((count, 5, 8), np.int32)
        self.units = np.zeros((count, units_dev + 1, 5), np.int32)
        self.returns = np.full((count, 1), -1, np.int32)
        self.returns[home] = index
        for t in range(count):
            self.table[t, SIDE_ROW] = padded(chip_need[self.side[t][1]])
            for row, other in ((SEND_ROW, self.core[t][1]), (MINE_ROW, t)):
                blocks = padded(need[other])
                self.table[t, row] = blocks
                self.table[t, row + 1] = [chip_need[t].index(b) for b in blocks]
            rows = work[t] + [None] * (units_dev + 1 - len(work[t]))
            held = [u for u in rows if u is not None]
            for step, u in enumerate(rows):
                known = u if u is not None else held[0 if step == 0 else -1]
                one, two, kind = units[known]
                kind = 2 if u is None else kind
                self.units[t, step] = [one, two, kind, need[t].index(one), need[t].index(two)]


def ship(value, pairs):
    return lax.ppermute(value, "tile", pairs)


def in_order(values, *earlier):
    earlier = tuple(value for value in earlier if value is not None)
    return lax.optimization_barrier(values + earlier)[: len(values)]


def collect(routes, value):
    count = value.shape[0]
    value = value[: count // 2] + ship(value[count // 2 :], routes.core)
    value = value[: count // 4] + ship(value[count // 4 :], routes.side)
    return (value[0] + ship(value[3], routes.far)) + (
        ship(value[1], routes.near_back) + ship(value[2], routes.near_cross)
    )


def plain_program(
    visibility, beam, antenna_uvw, source_dirs, flux, list_cols, keep
):
    units_dev, slots, _, span, _ = visibility.shape
    _, _, per_group, antennas = beam.shape
    blocks = antennas // span
    tile_index = lax.axis_index("tile")
    units = unit_table(blocks)
    unit_tab = lax.dynamic_slice_in_dim(
        jnp.asarray(np.concatenate([units, units[:, :2]], 1)), tile_index * units_dev, units_dev, 0
    )
    picks = jnp.zeros((1,), jnp.int32)
    residual = bright = None
    grads = []
    for slot in range(slots):
        chunk = (slot, 1, int(slot == 0))
        owned, _ = build_factors(
            chunk, span, [(beam, source_dirs, flux, list_cols)], antenna_uvw, picks
        )
        factors = lax.all_gather(owned[0], "tile", axis=0)
        bright = factors if bright is None else bright
        residual, grad = unit_work(
            chunk, unit_tab, [factors], blocks, [bright], visibility, keep, None, residual
        )
        grads.append(grad)
    partial = jnp.concatenate(grads, 0)[:, 0]
    return residual, lax.psum_scatter(partial, "tile", scatter_dimension=1, tiled=True)


CHUNK_SLOTS = (1, 1, 2, 2, 1, 1)


def ring_program(routes, visibility, beam, antenna_uvw, source_dirs, flux, list_cols, keep):
    units_dev, slots, _, span, _ = visibility.shape
    _, _, per_group, antennas = beam.shape
    blocks = antennas // span
    tile_index = lax.axis_index("tile")

    def mine_of(rows):
        return lax.dynamic_index_in_dim(jnp.asarray(rows), tile_index, 0, keepdims=False)

    table = mine_of(routes.table)
    unit_tab = mine_of(routes.units)
    returns = mine_of(routes.returns)
    side_picks = table[SIDE_ROW, :SIDE_PLACES]
    home, home_unit, host = routes.move

    chunks = []
    for count in CHUNK_SLOTS:
        first = sum(chunk[1] for chunk in chunks)
        chunks.append((first, count, int(first == 0)))
    last = len(chunks)

    small = jnp.concatenate(
        [source_dirs, flux, list_cols.T.reshape(1, -1).astype(jnp.float32)], 0
    )
    other_beam = ship(beam, routes.core)
    small = ship(small, routes.core)
    sets = [
        (beam, source_dirs, flux, list_cols),
        (
            other_beam,
            small[:2],
            small[2:3],
            small[3].reshape(slots, per_group).T.astype(jnp.int32),
        ),
    ]
    guest = None

    chip, owned_side, near, far, sides, mine, other, sent, grads, back = ({} for _ in range(10))
    side_at = {}
    residual = None

    def build(c):
        chip[c], owned_side[c] = build_factors(chunks[c], span, sets, antenna_uvw, side_picks)

    def side_message(stage):
        items, arrays, keys = [], [], []
        own = [0, 1] if stage == 0 else [stage + 1]
        for c in own:
            if c < last:
                keys.append(("own", c))
                items.append((chunks[c], 0))
                arrays.append(chip[c])
        c = stage - 1
        if 0 <= c < last:
            for lead in (0, 1):
                keys.append(("near", c, lead))
                items.append((chunks[c], lead))
                arrays.append(near[c])
        c = stage - 2
        if 0 <= c < last:
            keys.append(("far", c))
            items.append((chunks[c], None))
            arrays.append(far[c])
        rows = [chunk_rows(chunk, SIDE_PLACES) for chunk, _ in items]
        (message,) = pick_blocks(
            functools.partial(pick_side_kernel, items, blocks),
            [(sum(rows), per_group, span)],
            table,
            *arrays,
        )
        (message,) = in_order((message,), grads.get(stage - 5))
        sides[stage] = ship(message, routes.side)
        for n, key in enumerate(keys):
            side_at[key] = (stage, sum(rows[:n]))

    def core_message(c):
        keys = [("own", c), ("near", c, 0), ("near", c, 1), ("far", c)]
        rows = chunk_rows(chunks[c], CORE_PLACES)
        send, mine[c] = pick_blocks(
            functools.partial(pick_core_kernel, chunks[c], [side_at[k][1] for k in keys], blocks),
            [(8, rows, per_group, span)] * 2,
            table,
            chip[c],
            near[c],
            far[c],
            *[sides[side_at[k][0]] for k in keys],
        )
        (sent[c],) = in_order((send,), grads.get(c - 2))
        other[c] = ship(sent[c], routes.core)

    build(0)
    build(1)
    for stage in range(last + 5):
        if stage < last:
            (chip[stage],) = in_order(
                (chip[stage],), near.get(stage - 2), sent.get(stage - 4), grads.get(stage - 6)
            )
            near[stage] = ship(chip[stage], routes.near)
        if stage == 0:
            guest = ship(visibility[home_unit], [(home, host)])
        c = stage - 1
        if 0 <= c < last:
            far[c] = ship(near[c][0], routes.near)
        if stage + 2 < last:
            build(stage + 2)
        if stage < last + 2:
            side_message(stage)
        c = stage - 3
        if 0 <= c < last:
            core_message(c)
        c = stage - 4
        if 0 <= c < last:
            residual, guest_res, grads[c] = unit_work(
                chunks[c],
                unit_tab,
                [mine[c], other[c]],
                CORE_PLACES,
                [mine[0], other[0]],
                visibility,
                keep,
                guest,
                residual,
            )
            back[c] = ship(guest_res, [(host, home)])
    residual = put_returned(chunks, returns, [back[c] for c in range(last)], residual)
    partial = jnp.concatenate([grads[c] for c in range(last)], 0)
    partial = jnp.swapaxes(partial.reshape(slots, -1, per_group), 0, 1)
    return residual, collect(routes, partial)


def per_device(
    visibility, station_beam, antenna_uvw, source_dirs, source_flux, visible_list, antenna_flags
):
    span = visibility.shape[4]
    antennas = station_beam.shape[3]
    list_cols = visible_list.T
    flux = source_flux.astype(jnp.float32)[None]
    keep = 1.0 - antenna_flags.astype(jnp.float32)
    arguments = (visibility, station_beam, antenna_uvw, source_dirs, flux, list_cols, keep)
    if lax.axis_size("tile") == 16:
        routes = Routes(4, 2, 2, unit_table(antennas // span))
        residual, summed = ring_program(routes, *arguments)
    else:
        residual, summed = plain_program(*arguments)
    return (residual, summed * (-1.0 / (8.0 * antennas)))


def solution(mesh):
    return jax.shard_map(
        per_device,
        mesh=mesh,
        in_specs=(
            P("tile", "grp", None, None, None),
            P("grp", None, "tile", None),
            P("grp", None, None),
            P(None, "tile"),
            P(("grp", "tile")),
            P(None, "tile"),
            P("grp", None),
        ),
        out_specs=(P("tile", "grp", None, None, None), P("grp", "tile")),
        check_vma=False,
    )
```

time: 393 us -> 360 us (0.916)
  the two profiles are of different devices: /device:TPU:0 before, /device:TPU:28 now
where the time goes in v2:
time: 360 us; the launch traced here: 359 us
  waiting for transfers between devices  158 us (44%)
  Pallas kernels  141 us (39%)
  starting transfers between devices  42.6 us (12%)
  local copies, waits for them, and re-layouts  14 us (4%)
    ppermute x40, waiting for transfers between devices, ship(): return lax.ppermute(value, 'tile', pairs)  158 us
    pallas_call x1, Pallas kernels, put_returned(): pl.pallas_call(functools.partial(return_kernel, moves), in_specs=[pl.Bloc...  70.7 us
    ppermute x40, starting transfers between devices, ship(): return lax.ppermute(value, 'tile', pairs)  42.6 us
    pallas_call x6, Pallas kernels, unit_work(): pl.pallas_call(functools.partial(unit_kernel, chunk, len(factors), guest...  39.3 us
    pallas_call x6, Pallas kernels, build_factors(): pl.pallas_call(functools.partial(build_kernel, chunk, len(sets)), grid=(1...  16.7 us
    pallas_call x14, Pallas kernels, pick_blocks(): pl.pallas_call(kernel, in_specs=[pl.BlockSpec(memory_space=pltpu.SMEM)] +...  14.3 us
    unnamed x75, local copies, waits for them, and re-layouts  9.31 us
  transfers between devices with their start and end apart: 40, of which 22 were waited for; matrix products, arithmetic and copies ran while one was open for 3% of the time, Pallas kernels for 17%

profile of v2, /device:TPU:28, one launch (start us, length us, event | category | flops | bytes accessed | tf_op | source)
XLA Modules:
  0.0 359.4 jit_solution(13696180209475090920)
XLA Ops:
  6.1 1.6 copy-done
  8.3 3.4 build_factors.6
  12.2 2.3 build_factors.7
  14.8 3.2 build_factors.8
  18.0 10.1 %collective-permute-done.2.refs_1_.refs_2_.near = bf16[2,17,32,256]{3,2,1,0:T(8,128)(2,1)S(1)} collective-permute-done((bf16[2,17,32,256]{3,2,1,0:T(8,128)(2,1)S(1)}, bf16[2,17,32,256]{3,2,1,0:T(8,128)(2,1)S(1)}, u32[]{:S(2)}, u32[]{:S(2)}) %collective-permute-start.2) | collective-permute-done | bytes 557088 | tf_op jit(solution)/shard_map/ppermute | solution.py:483
  28.2 1.8 collective-permute-start.3
  29.9 9.5 %collective-permute-done.6.refs_1_.refs_2_.near = bf16[2,16,32,256]{3,2,1,0:T(8,128)(2,1)S(1)} collective-permute-done((bf16[2,16,32,256]{3,2,1,0:T(8,128)(2,1)S(1)}, bf16[2,16,32,256]{3,2,1,0:T(8,128)(2,1)S(1)}, u32[]{:S(2)}, u32[]{:S(2)}) %collective-permute-start.6) | collective-permute-done | bytes 524320 | tf_op jit(solution)/shard_map/ppermute | solution.py:483
  40.7 3.2 build_factors.9
  45.8 22.0 %collective-permute-done.3.refs_3_.far = bf16[17,32,256]{2,1,0:T(8,128)(2,1)S(1)} collective-permute-done((bf16[17,32,256]{2,1,0:T(8,128)(2,1)S(1)}, bf16[17,32,256]{2,1,0:T(8,128)(2,1)S(1)}, u32[]{:S(2)}, u32[]{:S(2)}) %collective-permute-start.3) | collective-permute-done | bytes 278560 | tf_op jit(solution)/shard_map/ppermute | solution.py:483
  69.0 4.4 %collective-permute-done.11.refs_3_.far = bf16[16,32,256]{2,1,0:T(8,128)(2,1)S(1)} collective-permute-done((bf16[16,32,256]{2,1,0:T(8,128)(2,1)S(1)}, bf16[16,32,256]{2,1,0:T(8,128)(2,1)S(1)}, u32[]{:S(2)}, u32[]{:S(2)}) %collective-permute-start.11) | collective-permute-done | bytes 262176 | tf_op jit(solution)/shard_map/ppermute | solution.py:483
  73.9 1.5 slice_bitcast_fusion
  75.5 1.6 collective-permute-start.9
  77.0 2.3 build_factors.10
  79.3 1.7 pick_blocks.18
  81.8 7.2 %collective-permute-done.5.refs_1_.refs_2_.refs_0_ = bf16[50,32,256]{2,1,0:T(8,128)(2,1)S(1)} collective-permute-done((bf16[50,32,256]{2,1,0:T(8,128)(2,1)S(1)}, bf16[50,32,256]{2,1,0:T(8,128)(2,1)S(1)}, u32[]{:S(2)}, u32[]{:S(2)}) %collective-permute-start.5) | collective-permute-done | bytes 819232 | tf_op jit(solution)/shard_map/ppermute | solution.py:483
  89.0 21.4 %collective-permute-done.7.refs_3_.refs_1_.refs_2_.refs_0_ = bf16[61,32,256]{2,1,0:T(8,128)(2,1)S(1)} collective-permute-done((bf16[61,32,256]{2,1,0:T(8,128)(2,1)S(1)}, bf16[61,32,256]{2,1,0:T(8,128)(2,1)S(1)}, u32[]{:S(2)}, u32[]{:S(2)}) %collective-permute-start.7) | collective-permute-done | bytes 999456 | tf_op jit(solution)/shard_map/ppermute | solution.py:483
  111.4 2.3 build_factors.11
  113.7 17.9 %collective-permute-done.16.refs_3_.far = bf16[32,32,256]{2,1,0:T(8,128)(2,1)S(1)} collective-permute-done((bf16[32,32,256]{2,1,0:T(8,128)(2,1)S(1)}, bf16[32,32,256]{2,1,0:T(8,128)(2,1)S(1)}, u32[]{:S(2)}, u32[]{:S(2)}) %collective-permute-start.16) | collective-permute-done | bytes 524320 | tf_op jit(solution)/shard_map/ppermute | solution.py:483
  131.6 1.8 pick_blocks.20
  133.5 2.2 collective-permute-done.13.refs_3_.refs_1_.refs_2_.refs_0_
  136.9 5.6 %collective-permute-done.21.refs_2_.far = bf16[32,32,256]{2,1,0:T(8,128)(2,1)S(1)} collective-permute-done((bf16[32,32,256]{2,1,0:T(8,128)(2,1)S(1)}, bf16[32,32,256]{2,1,0:T(8,128)(2,1)S(1)}, u32[]{:S(2)}, u32[]{:S(2)}) %collective-permute-start.21) | collective-permute-done | bytes 524320 | tf_op jit(solution)/shard_map/ppermute | solution.py:483
  143.3 4.9 %collective-permute-done.22.refs_0_.refs_1_.near = bf16[2,16,32,256]{3,2,1,0:T(8,128)(2,1)S(1)} collective-permute-done((bf16[2,16,32,256]{3,2,1,0:T(8,128)(2,1)S(1)}, bf16[2,16,32,256]{3,2,1,0:T(8,128)(2,1)S(1)}, u32[]{:S(2)}, u32[]{:S(2)}) %collective-permute-start.22) | collective-permute-done | bytes 524320 | tf_op jit(solution)/shard_map/ppermute | solution.py:483
  148.1 1.5 pick_blocks.22
  149.7 5.3 %unit_work.6 = (bf16[2,8,2,256,256]{4,3,2,1,0:T(8,128)(2,1)}, bf16[1,2,256,256]{3,2,1,0:T(8,128)(2,1)S(1)}, f32[1,1,512]{2,1,0:T(1,128)S(1)}) custom-call(s32[3,5]{1,0:T(4,128)S(1)} %dynamic-slice_bitcast_fusion.1.tab_ref, bf16[8,9,32,256]{3,2,1,0:T(8,128)(2,1)S(1)} %get-tuple-element.53.refs_0_.refs_2_.refs_4_.refs_6_.refs_8_, ...), custom_call_target="tpu_custom_call" | custom-call | flops 1073741824 | bytes 8388608 | tf_op jit(solution)/shard_map/unit_work/pallas_call | solution.py:370
  156.1 9.5 %collective-permute-done.18.refs_3_.refs_1_.refs_2_.refs_0_ = bf16[84,32,256]{2,1,0:T(8,128)(2,1)S(1)} collective-permute-done((bf16[84,32,256]{2,1,0:T(8,128)(2,1)}, bf16[84,32,256]{2,1,0:T(8,128)(2,1)S(1)}, u32[]{:S(2)}, u32[]{:S(2)}) %collective-permute-start.18) | collective-permute-done | bytes 1376288 | tf_op jit(solution)/shard_map/ppermute | solution.py:483
  167.9 2.2 pick_blocks.21
  170.1 7.3 %collective-permute-done.23.refs_3_.refs_1_.refs_2_ = bf16[48,32,256]{2,1,0:T(8,128)(2,1)S(1)} collective-permute-done((bf16[48,32,256]{2,1,0:T(8,128)(2,1)}, bf16[48,32,256]{2,1,0:T(8,128)(2,1)S(1)}, u32[]{:S(2)}, u32[]{:S(2)}) %collective-permute-start.23) | collective-permute-done | bytes 786464 | tf_op jit(solution)/shard_map/ppermute | solution.py:483
  178.3 1.4 copy-done.21
  179.7 5.2 %unit_work.7 = (bf16[2,8,2,256,256]{4,3,2,1,0:T(8,128)(2,1)}, bf16[1,2,256,256]{3,2,1,0:T(8,128)(2,1)S(1)}, f32[1,1,512]{2,1,0:T(1,128)S(1)}) custom-call(s32[3,5]{1,0:T(4,128)S(1)} %dynamic-slice_bitcast_fusion.1.tab_ref, bf16[8,8,32,256]{3,2,1,0:T(8,128)(2,1)S(1)} %get-tuple-element.58.refs_0_.refs_2_.refs_4_.refs_6_, ...), custom_call_target="tpu_custom_call", output_to_operand_aliasing={{0}: (15, {})} | custom-call | flops 1073741824 | bytes 8388608 | tf_op jit(solution)/shard_map/unit_work/pallas_call | solution.py:370
  184.9 4.8 %collective-permute-start.27 = (bf16[2,16,32,256]{3,2,1,0:T(8,128)(2,1)S(1)}, bf16[2,16,32,256]{3,2,1,0:T(8,128)(2,1)S(1)}, u32[]{:S(2)}, u32[]{:S(2)}) collective-permute-start(bf16[2,16,32,256]{3,2,1,0:T(8,128)(2,1)S(1)} %copy-done.12), channel_id=1, source_target_pairs={{0,4},{1,9},{2,6},{3,11},{4,12},{5,1},{6,14},{7,3},{8,0},{9,13},{1... | collective-permute-start | bytes 1572872 | tf_op jit(solution)/shard_map/ppermute | solution.py:483
  189.8 11.6 %collective-permute-done.27.refs_0_.refs_1_.near = bf16[2,16,32,256]{3,2,1,0:T(8,128)(2,1)S(1)} collective-permute-done((bf16[2,16,32,256]{3,2,1,0:T(8,128)(2,1)S(1)}, bf16[2,16,32,256]{3,2,1,0:T(8,128)(2,1)S(1)}, u32[]{:S(2)}, u32[]{:S(2)}) %collective-permute-start.27) | collective-permute-done | bytes 524320 | tf_op jit(solution)/shard_map/ppermute | solution.py:483
  201.4 2.8 collective-permute-start.31
  205.1 1.7 collective-permute-start.28
  206.8 4.7 %collective-permute-done.31.refs_0_.far = bf16[16,32,256]{2,1,0:T(8,128)(2,1)S(1)} collective-permute-done((bf16[16,32,256]{2,1,0:T(8,128)(2,1)S(1)}, bf16[16,32,256]{2,1,0:T(8,128)(2,1)S(1)}, u32[]{:S(2)}, u32[]{:S(2)}) %collective-permute-start.31) | collective-permute-done | bytes 262176 | tf_op jit(solution)/shard_map/ppermute | solution.py:483
  212.2 9.2 %unit_work.8 = (bf16[2,8,2,256,256]{4,3,2,1,0:T(8,128)(2,1)}, bf16[2,2,256,256]{3,2,1,0:T(8,128)(2,1)S(1)}, f32[2,1,512]{2,1,0:T(1,128)S(1)}) custom-call(s32[3,5]{1,0:T(4,128)S(1)} %dynamic-slice_bitcast_fusion.1.tab_ref, bf16[8,16,32,256]{3,2,1,0:T(8,128)(2,1)S(1)} %get-tuple-element.64.refs_0_.refs_2_.refs_4_.refs_6_, ...), custom_call_target="tpu_custom_call", output_to_operand_aliasing={{0}: (15, {})} | custom-call | flops 2147483648 | bytes 16777216 | tf_op jit(solution)/shard_map/unit_work/pallas_call | solution.py:370
  223.3 2.2 collective-permute-start.29
  225.6 1.5 collective-permute-done.32.refs_3_
  227.9 9.2 %unit_work.9 = (bf16[2,8,2,256,256]{4,3,2,1,0:T(8,128)(2,1)}, bf16[2,2,256,256]{3,2,1,0:T(8,128)(2,1)S(1)}, f32[2,1,512]{2,1,0:T(1,128)S(1)}) custom-call(s32[3,5]{1,0:T(4,128)S(1)} %dynamic-slice_bitcast_fusion.1.tab_ref, bf16[8,16,32,256]{3,2,1,0:T(8,128)(2,1)S(1)} %get-tuple-element.72.refs_0_.refs_2_.refs_4_.refs_6_, ...), custom_call_target="tpu_custom_call", output_to_operand_aliasing={{0}: (15, {})} | custom-call | flops 2147483648 | bytes 16777216 | tf_op jit(solution)/shard_map/unit_work/pallas_call | solution.py:370
  237.1 5.1 %collective-permute-start.33 = (bf16[8,8,32,256]{3,2,1,0:T(8,128)(2,1)S(1)}, bf16[8,8,32,256]{3,2,1,0:T(8,128)(2,1)S(1)}, u32[]{:S(2)}, u32[]{:S(2)}) collective-permute-start(bf16[8,8,32,256]{3,2,1,0:T(8,128)(2,1)S(1)} %get-tuple-element.90), channel_id=1, source_target_pairs={{0,1},{1,0},{2,3},{3,2},{4,5},{5,4},{6,7},{7,6},{8,9},{9,8},{10,11... | collective-permute-start | bytes 3145736 | tf_op jit(solution)/shard_map/ppermute | solution.py:483
  242.2 5.2 %unit_work.10 = (bf16[2,8,2,256,256]{4,3,2,1,0:T(8,128)(2,1)}, bf16[1,2,256,256]{3,2,1,0:T(8,128)(2,1)S(1)}, f32[1,1,512]{2,1,0:T(1,128)S(1)}) custom-call(s32[3,5]{1,0:T(4,128)S(1)} %dynamic-slice_bitcast_fusion.1.tab_ref, bf16[8,8,32,256]{3,2,1,0:T(8,128)(2,1)S(1)} %get-tuple-element.80.refs_0_.refs_2_.refs_4_.refs_6_, ...), custom_call_target="tpu_custom_call", output_to_operand_aliasing={{0}: (15, {})} | custom-call | flops 1073741824 | bytes 8388608 | tf_op jit(solution)/shard_map/unit_work/pallas_call | solution.py:370
  247.4 5.2 %unit_work.11 = (bf16[2,8,2,256,256]{4,3,2,1,0:T(8,128)(2,1)}, bf16[1,2,256,256]{3,2,1,0:T(8,128)(2,1)S(1)}, f32[1,1,512]{2,1,0:T(1,128)S(1)}) custom-call(s32[3,5]{1,0:T(4,128)S(1)} %dynamic-slice_bitcast_fusion.1.tab_ref, bf16[8,8,32,256]{3,2,1,0:T(8,128)(2,1)S(1)} %get-tuple-element.87.refs_0_.refs_2_.refs_4_.refs_6_, ...), custom_call_target="tpu_custom_call", output_to_operand_aliasing={{0}: (15, {})} | custom-call | flops 1073741824 | bytes 8388608 | tf_op jit(solution)/shard_map/unit_work/pallas_call | solution.py:370
  252.8 2.8 collective-permute-start.35
  260.5 4.7 %collective-permute-start.38 = (f32[8,32]{1,0:T(8,128)S(1)}, f32[8,32]{1,0:T(8,128)S(1)}, u32[]{:S(2)}, u32[]{:S(2)}) collective-permute-start(f32[8,32]{1,0:T(8,128)S(1)} %get-tuple-element.97), channel_id=1, source_target_pairs={{4,0},{9,1},{6,2},{11,3},{12,4},{1,5},{14,6},{3,7},{0,8},{13,9},{2... | collective-permute-start | bytes 3080 | tf_op jit(solution)/shard_map/ppermute | solution.py:483
  267.3 9.5 %collective-permute-done.38 = f32[8,32]{1,0:T(8,128)S(1)} collective-permute-done((f32[8,32]{1,0:T(8,128)S(1)}, f32[8,32]{1,0:T(8,128)S(1)}, u32[]{:S(2)}, u32[]{:S(2)}) %collective-permute-start.38) | collective-permute-done | bytes 1056 | tf_op jit(solution)/shard_map/ppermute | solution.py:483
  278.1 1.3 collective-permute-start.34
  281.2 3.8 %collective-permute-done.30.refs_4_ = bf16[1,2,256,256]{3,2,1,0:T(8,128)(2,1)S(1)} collective-permute-done((bf16[1,2,256,256]{3,2,1,0:T(8,128)(2,1)S(1)}, bf16[1,2,256,256]{3,2,1,0:T(8,128)(2,1)S(1)}, u32[]{:S(2)}, u32[]{:S(2)}) %collective-permute-start.30) | collective-permute-done | bytes 262176 | tf_op jit(solution)/shard_map/ppermute | solution.py:483
  285.0 2.8 collective-permute-done.34.refs_5_
  288.6 70.7 %put_returned.1 = bf16[2,8,2,256,256]{4,3,2,1,0:T(8,128)(2,1)} custom-call(s32[1]{0:T(128)} %bitcast.tab_ref, bf16[1,2,256,256]{3,2,1,0:T(8,128)(2,1)} %copy-done.29, bf16[1,2,256,256]{3,2,1,0:T(8,128)(2,1)} %copy-done.30, bf16[2,2,256,256]{3,2,1,0:T(8,128)(2,1)} %copy-done.27, bf16[2,2,256,256]{3,2,1,0:T(8,128)(2,1)} %copy-done.28, ...), custom_call_target="tpu_custom_call", output_to_operand_aliasing={{}: (7, {})} | custom-call | tf_op jit(solution)/shard_map/put_returned/pallas_call | solution.py:403
  (165 shorter events, 35.0 us)
Async XLA Ops:
  0.6 5.4 %collective-permute-start = (bf16[8,2,32,2048]{3,2,1,0:T(8,128)(2,1)}, bf16[8,2,32,2048]{3,2,1,0:T(8,128)(2,1)S(1)}, u32[]{:S(2)}, u32[]{:S(2)}) collective-permute-start(bf16[8,2,32,2048]{3,2,1,0:T(8,128)(2,1)} %refs_0_.11), channel_id=1, source_target_pairs={{0,1},{1,0},{2,3},{3,2},{4,5},{5,4},{6,7},{7,6},{8,9},{9,8},{10,11... | collective-permute-start | bytes 6291464 | tf_op jit(solution)/shard_map/ppermute | solution.py:483
  2.8 3.0 collective-permute-start.1
  11.7 16.4 %collective-permute-start.2 = (bf16[2,17,32,256]{3,2,1,0:T(8,128)(2,1)S(1)}, bf16[2,17,32,256]{3,2,1,0:T(8,128)(2,1)S(1)}, u32[]{:S(2)}, u32[]{:S(2)}) collective-permute-start(bf16[2,17,32,256]{3,2,1,0:T(8,128)(2,1)S(1)} %get-tuple-element.49.refs_0_.chip), channel_id=1, source_target_pairs={{0,4},{1,9},{2,6},{3,11},{4,12},{5,1},{6,14},{7,3},{8,0},{9,13},{1... | collective-permute-start | bytes 1671176 | tf_op jit(solution)/shard_map/ppermute | solution.py:483
  14.5 24.9 %collective-permute-start.6 = (bf16[2,16,32,256]{3,2,1,0:T(8,128)(2,1)S(1)}, bf16[2,16,32,256]{3,2,1,0:T(8,128)(2,1)S(1)}, u32[]{:S(2)}, u32[]{:S(2)}) collective-permute-start(bf16[2,16,32,256]{3,2,1,0:T(8,128)(2,1)S(1)} %get-tuple-element.50.refs_1_.chip), channel_id=1, source_target_pairs={{0,4},{1,9},{2,6},{3,11},{4,12},{5,1},{6,14},{7,3},{8,0},{9,13},{1... | collective-permute-start | bytes 1572872 | tf_op jit(solution)/shard_map/ppermute | solution.py:483
  18.0 27.1 %copy-start.7 = (bf16[2,32,32,256]{3,2,1,0:T(8,128)(2,1)}, bf16[2,32,32,256]{3,2,1,0:T(8,128)(2,1)S(1)}, u32[]{:S(2)}) copy-start(bf16[2,32,32,256]{3,2,1,0:T(8,128)(2,1)S(1)} %get-tuple-element.57.refs_0_.chip) | copy-start | bytes 3145732
  18.0 22.6 %copy-start.1 = (bf16[8,2,32,2048]{3,2,1,0:T(8,128)(2,1)S(1)}, bf16[8,2,32,2048]{3,2,1,0:T(8,128)(2,1)}, u32[]{:S(2)}) copy-start(bf16[8,2,32,2048]{3,2,1,0:T(8,128)(2,1)} %refs_0_.11) | copy-start | bytes 6291460
  28.1 47.3 %collective-permute-start.12 = (bf16[2,32,32,256]{3,2,1,0:T(8,128)(2,1)S(1)}, bf16[2,32,32,256]{3,2,1,0:T(8,128)(2,1)S(1)}, u32[]{:S(2)}, u32[]{:S(2)}) collective-permute-start(bf16[2,32,32,256]{3,2,1,0:T(8,128)(2,1)S(1)} %get-tuple-element.57.refs_0_.chip), channel_id=1, source_target_pairs={{0,4},{1,9},{2,6},{3,11},{4,12},{5,1},{6,14},{7,3},{8,0},{9,13},{1... | collective-permute-start | bytes 3145736 | tf_op jit(solution)/shard_map/ppermute | solution.py:483
  28.2 39.6 %collective-permute-start.3 = (bf16[17,32,256]{2,1,0:T(8,128)(2,1)S(1)}, bf16[17,32,256]{2,1,0:T(8,128)(2,1)S(1)}, u32[]{:S(2)}, u32[]{:S(2)}) collective-permute-start(bf16[17,32,256]{2,1,0:T(8,128)(2,1)S(1)} %slice_bitcast_fusion.3), channel_id=1, source_target_pairs={{0,4},{1,9},{2,6},{3,11},{4,12},{5,1},{6,14},{7,3},{8,0},{9,13},{1... | collective-permute-start | bytes 835592 | tf_op jit(solution)/shard_map/ppermute | solution.py:483
  39.4 34.0 %collective-permute-start.11 = (bf16[16,32,256]{2,1,0:T(8,128)(2,1)S(1)}, bf16[16,32,256]{2,1,0:T(8,128)(2,1)S(1)}, u32[]{:S(2)}, u32[]{:S(2)}) collective-permute-start(bf16[16,32,256]{2,1,0:T(8,128)(2,1)S(1)} %slice_bitcast_fusion.6), channel_id=1, source_target_pairs={{0,4},{1,9},{2,6},{3,11},{4,12},{5,1},{6,14},{7,3},{8,0},{9,13},{1... | collective-permute-start | bytes 786440 | tf_op jit(solution)/shard_map/ppermute | solution.py:483
  40.1 40.9 %collective-permute-start.4 = (bf16[25,32,256]{2,1,0:T(8,128)(2,1)S(1)}, bf16[25,32,256]{2,1,0:T(8,128)(2,1)S(1)}, u32[]{:S(2)}, u32[]{:S(2)}) collective-permute-start(bf16[25,32,256]{2,1,0:T(8,128)(2,1)S(1)} %pick_blocks.14), channel_id=1, source_target_pairs={{0,2},{1,3},{2,0},{3,1},{4,6},{5,7},{6,4},{7,5},{8,10},{9,11},{10,... | collective-permute-start | bytes 1228808 | tf_op jit(solution)/shard_map/ppermute | solution.py:483
  43.9 25.1 %copy-start.9 = (bf16[2,32,32,256]{3,2,1,0:T(8,128)(2,1)}, bf16[2,32,32,256]{3,2,1,0:T(8,128)(2,1)S(1)}, u32[]{:S(2)}) copy-start(bf16[2,32,32,256]{3,2,1,0:T(8,128)(2,1)S(1)} %get-tuple-element.63.refs_0_.chip) | copy-start | bytes 3145732
  43.9 67.3 %collective-permute-start.17 = (bf16[2,32,32,256]{3,2,1,0:T(8,128)(2,1)S(1)}, bf16[2,32,32,256]{3,2,1,0:T(8,128)(2,1)S(1)}, u32[]{:S(2)}, u32[]{:S(2)}) collective-permute-start(bf16[2,32,32,256]{3,2,1,0:T(8,128)(2,1)S(1)} %get-tuple-element.63.refs_0_.chip), channel_id=1, source_target_pairs={{0,4},{1,9},{2,6},{3,11},{4,12},{5,1},{6,14},{7,3},{8,0},{9,13},{1... | collective-permute-start | bytes 3145736 | tf_op jit(solution)/shard_map/ppermute | solution.py:483
  45.1 28.8 %copy-start.26 = (bf16[2,8,2,256,256]{4,3,2,1,0:T(8,128)(2,1)S(1)}, bf16[2,8,2,256,256]{4,3,2,1,0:T(8,128)(2,1)}, u32[]{:S(2)}) copy-start(bf16[2,8,2,256,256]{4,3,2,1,0:T(8,128)(2,1)} %refs_10_.11) | copy-start | bytes 12582916
  67.8 21.2 %collective-permute-start.5 = (bf16[50,32,256]{2,1,0:T(8,128)(2,1)S(1)}, bf16[50,32,256]{2,1,0:T(8,128)(2,1)S(1)}, u32[]{:S(2)}, u32[]{:S(2)}) collective-permute-start(bf16[50,32,256]{2,1,0:T(8,128)(2,1)S(1)} %pick_blocks.15), channel_id=1, source_target_pairs={{0,2},{1,3},{2,0},{3,1},{4,6},{5,7},{6,4},{7,5},{8,10},{9,11},{10,... | collective-permute-start | bytes 2457608 | tf_op jit(solution)/shard_map/ppermute | solution.py:483
  73.4 37.0 %collective-permute-start.7 = (bf16[61,32,256]{2,1,0:T(8,128)(2,1)S(1)}, bf16[61,32,256]{2,1,0:T(8,128)(2,1)S(1)}, u32[]{:S(2)}, u32[]{:S(2)}) collective-permute-start(bf16[61,32,256]{2,1,0:T(8,128)(2,1)S(1)} %pick_blocks.16), channel_id=1, source_target_pairs={{0,2},{1,3},{2,0},{3,1},{4,6},{5,7},{6,4},{7,5},{8,10},{9,11},{10,... | collective-permute-start | bytes 2998280 | tf_op jit(solution)/shard_map/ppermute | solution.py:483
  75.5 74.2 %collective-permute-start.9 = (bf16[8,2,256,256]{3,2,1,0:T(8,128)(2,1)}, bf16[8,2,256,256]{3,2,1,0:T(8,128)(2,1)S(1)}, u32[]{:S(2)}, u32[]{:S(2)}) collective-permute-start(bf16[8,2,256,256]{3,2,1,0:T(8,128)(2,1)} %slice_bitcast_fusion), channel_id=1, source_target_pairs={{14,10},{30,26}} | collective-permute-start | bytes 6291464 | tf_op jit(solution)/shard_map/ppermute | solution.py:483
  79.3 56.4 %copy-start.17 = (bf16[2,16,32,256]{3,2,1,0:T(8,128)(2,1)}, bf16[2,16,32,256]{3,2,1,0:T(8,128)(2,1)S(1)}, u32[]{:S(2)}) copy-start(bf16[2,16,32,256]{3,2,1,0:T(8,128)(2,1)S(1)} %get-tuple-element.70.refs_0_.chip) | copy-start | bytes 1572868
  81.0 54.7 %collective-permute-start.13 = (bf16[72,32,256]{2,1,0:T(8,128)(2,1)}, bf16[72,32,256]{2,1,0:T(8,128)(2,1)S(1)}, u32[]{:S(2)}, u32[]{:S(2)}) collective-permute-start(bf16[72,32,256]{2,1,0:T(8,128)(2,1)} %pick_blocks.18), channel_id=1, source_target_pairs={{0,2},{1,3},{2,0},{3,1},{4,6},{5,7},{6,4},{7,5},{8,10},{9,11},{10,... | collective-permute-start | bytes 3538952 | tf_op jit(solution)/shard_map/ppermute | solution.py:483
  81.8 29.6 %copy-start.20 = (f32[2,256]{1,0:T(2,128)S(1)}, f32[2,256]{1,0:T(2,128)}, u32[]{:S(2)}) copy-start(f32[2,256]{1,0:T(2,128)} %refs_1_.11) | copy-start | bytes 6148
  89.0 22.2 %copy-start.5 = (bf16[50,32,256]{2,1,0:T(8,128)(2,1)}, bf16[50,32,256]{2,1,0:T(8,128)(2,1)S(1)}, u32[]{:S(2)}) copy-start(bf16[50,32,256]{2,1,0:T(8,128)(2,1)S(1)} %collective-permute-done.5.refs_1_.refs_2_.refs_0_) | copy-start | bytes 2457604
  89.0 42.6 %collective-permute-start.16 = (bf16[32,32,256]{2,1,0:T(8,128)(2,1)S(1)}, bf16[32,32,256]{2,1,0:T(8,128)(2,1)S(1)}, u32[]{:S(2)}, u32[]{:S(2)}) collective-permute-start(bf16[32,32,256]{2,1,0:T(8,128)(2,1)S(1)} %slice_bitcast_fusion.2), channel_id=1, source_target_pairs={{0,4},{1,9},{2,6},{3,11},{4,12},{5,1},{6,14},{7,3},{8,0},{9,13},{1... | collective-permute-start | bytes 1572872 | tf_op jit(solution)/shard_map/ppermute | solution.py:483
  111.2 38.5 %collective-permute-start.8 = (bf16[8,9,32,256]{3,2,1,0:T(8,128)(2,1)S(1)}, bf16[8,9,32,256]{3,2,1,0:T(8,128)(2,1)S(1)}, u32[]{:S(2)}, u32[]{:S(2)}) collective-permute-start(bf16[8,9,32,256]{3,2,1,0:T(8,128)(2,1)S(1)} %get-tuple-element.54), channel_id=1, source_target_pairs={{0,1},{1,0},{2,3},{3,2},{4,5},{5,4},{6,7},{7,6},{8,9},{9,8},{10,11... | collective-permute-start | bytes 3538952 | tf_op jit(solution)/shard_map/ppermute | solution.py:483
  111.3 31.2 %collective-permute-start.21 = (bf16[32,32,256]{2,1,0:T(8,128)(2,1)S(1)}, bf16[32,32,256]{2,1,0:T(8,128)(2,1)S(1)}, u32[]{:S(2)}, u32[]{:S(2)}) collective-permute-start(bf16[32,32,256]{2,1,0:T(8,128)(2,1)S(1)} %slice_bitcast_fusion.1), channel_id=1, source_target_pairs={{0,4},{1,9},{2,6},{3,11},{4,12},{5,1},{6,14},{7,3},{8,0},{9,13},{1... | collective-permute-start | bytes 1572872 | tf_op jit(solution)/shard_map/ppermute | solution.py:483
  133.4 32.2 %collective-permute-start.18 = (bf16[84,32,256]{2,1,0:T(8,128)(2,1)}, bf16[84,32,256]{2,1,0:T(8,128)(2,1)S(1)}, u32[]{:S(2)}, u32[]{:S(2)}) collective-permute-start(bf16[84,32,256]{2,1,0:T(8,128)(2,1)} %pick_blocks.20), channel_id=1, source_target_pairs={{0,2},{1,3},{2,0},{3,1},{4,6},{5,7},{6,4},{7,5},{8,10},{9,11},{10,... | collective-permute-start | bytes 4128776 | tf_op jit(solution)/shard_map/ppermute | solution.py:483
  135.7 12.4 %collective-permute-start.22 = (bf16[2,16,32,256]{3,2,1,0:T(8,128)(2,1)S(1)}, bf16[2,16,32,256]{3,2,1,0:T(8,128)(2,1)S(1)}, u32[]{:S(2)}, u32[]{:S(2)}) collective-permute-start(bf16[2,16,32,256]{3,2,1,0:T(8,128)(2,1)S(1)} %get-tuple-element.70.refs_0_.chip), channel_id=1, source_target_pairs={{0,4},{1,9},{2,6},{3,11},{4,12},{5,1},{6,14},{7,3},{8,0},{9,13},{1... | collective-permute-start | bytes 1572872 | tf_op jit(solution)/shard_map/ppermute | solution.py:483
  142.5 37.2 %collective-permute-start.14 = (bf16[8,8,32,256]{3,2,1,0:T(8,128)(2,1)S(1)}, bf16[8,8,32,256]{3,2,1,0:T(8,128)(2,1)S(1)}, u32[]{:S(2)}, u32[]{:S(2)}) collective-permute-start(bf16[8,8,32,256]{3,2,1,0:T(8,128)(2,1)S(1)} %get-tuple-element.59), channel_id=1, source_target_pairs={{0,1},{1,0},{2,3},{3,2},{4,5},{5,4},{6,7},{7,6},{8,9},{9,8},{10,11... | collective-permute-start | bytes 3145736 | tf_op jit(solution)/shard_map/ppermute | solution.py:483
  155.7 21.7 %collective-permute-start.23 = (bf16[48,32,256]{2,1,0:T(8,128)(2,1)}, bf16[48,32,256]{2,1,0:T(8,128)(2,1)S(1)}, u32[]{:S(2)}, u32[]{:S(2)}) collective-permute-start(bf16[48,32,256]{2,1,0:T(8,128)(2,1)} %pick_blocks.22), channel_id=1, source_target_pairs={{0,2},{1,3},{2,0},{3,1},{4,6},{5,7},{6,4},{7,5},{8,10},{9,11},{10,... | collective-permute-start | bytes 2359304 | tf_op jit(solution)/shard_map/ppermute | solution.py:483
  170.1 42.1 %collective-permute-start.19 = (bf16[8,16,32,256]{3,2,1,0:T(8,128)(2,1)}, bf16[8,16,32,256]{3,2,1,0:T(8,128)(2,1)}, u32[]{:S(2)}, u32[]{:S(2)}) collective-permute-start(bf16[8,16,32,256]{3,2,1,0:T(8,128)(2,1)} %get-tuple-element.67), channel_id=1, source_target_pairs={{0,1},{1,0},{2,3},{3,2},{4,5},{5,4},{6,7},{7,6},{8,9},{9,8},{10,11... | collective-permute-start | bytes 6291464 | tf_op jit(solution)/shard_map/ppermute | solution.py:483
  184.9 43.0 %collective-permute-start.24 = (bf16[8,16,32,256]{3,2,1,0:T(8,128)(2,1)}, bf16[8,16,32,256]{3,2,1,0:T(8,128)(2,1)}, u32[]{:S(2)}, u32[]{:S(2)}) collective-permute-start(bf16[8,16,32,256]{3,2,1,0:T(8,128)(2,1)} %copy-done.21), channel_id=1, source_target_pairs={{0,1},{1,0},{2,3},{3,2},{4,5},{5,4},{6,7},{7,6},{8,9},{9,8},{10,11... | collective-permute-start | bytes 6291464 | tf_op jit(solution)/shard_map/ppermute | solution.py:483
  184.9 16.5 %collective-permute-start.27 = (bf16[2,16,32,256]{3,2,1,0:T(8,128)(2,1)S(1)}, bf16[2,16,32,256]{3,2,1,0:T(8,128)(2,1)S(1)}, u32[]{:S(2)}, u32[]{:S(2)}) collective-permute-start(bf16[2,16,32,256]{3,2,1,0:T(8,128)(2,1)S(1)} %copy-done.12), channel_id=1, source_target_pairs={{0,4},{1,9},{2,6},{3,11},{4,12},{5,1},{6,14},{7,3},{8,0},{9,13},{1... | collective-permute-start | bytes 1572872 | tf_op jit(solution)/shard_map/ppermute | solution.py:483
  189.7 14.7 %collective-permute-start.26 = (bf16[16,32,256]{2,1,0:T(8,128)(2,1)S(1)}, bf16[16,32,256]{2,1,0:T(8,128)(2,1)S(1)}, u32[]{:S(2)}, u32[]{:S(2)}) collective-permute-start(bf16[16,32,256]{2,1,0:T(8,128)(2,1)S(1)} %slice_bitcast_fusion.5), channel_id=1, source_target_pairs={{0,4},{1,9},{2,6},{3,11},{4,12},{5,1},{6,14},{7,3},{8,0},{9,13},{1... | collective-permute-start | bytes 786440 | tf_op jit(solution)/shard_map/ppermute | solution.py:483
  201.4 10.1 %collective-permute-start.31 = (bf16[16,32,256]{2,1,0:T(8,128)(2,1)S(1)}, bf16[16,32,256]{2,1,0:T(8,128)(2,1)S(1)}, u32[]{:S(2)}, u32[]{:S(2)}) collective-permute-start(bf16[16,32,256]{2,1,0:T(8,128)(2,1)S(1)} %slice_bitcast_fusion.4), channel_id=1, source_target_pairs={{0,4},{1,9},{2,6},{3,11},{4,12},{5,1},{6,14},{7,3},{8,0},{9,13},{1... | collective-permute-start | bytes 786440 | tf_op jit(solution)/shard_map/ppermute | solution.py:483
  205.1 17.5 %collective-permute-start.28 = (bf16[36,32,256]{2,1,0:T(8,128)(2,1)S(1)}, bf16[36,32,256]{2,1,0:T(8,128)(2,1)S(1)}, u32[]{:S(2)}, u32[]{:S(2)}) collective-permute-start(bf16[36,32,256]{2,1,0:T(8,128)(2,1)S(1)} %pick_blocks.24), channel_id=1, source_target_pairs={{0,2},{1,3},{2,0},{3,1},{4,6},{5,7},{6,4},{7,5},{8,10},{9,11},{10,... | collective-permute-start | bytes 1769480 | tf_op jit(solution)/shard_map/ppermute | solution.py:483
  221.4 5.7 %collective-permute-start.32 = (bf16[12,32,256]{2,1,0:T(8,128)(2,1)S(1)}, bf16[12,32,256]{2,1,0:T(8,128)(2,1)S(1)}, u32[]{:S(2)}, u32[]{:S(2)}) collective-permute-start(bf16[12,32,256]{2,1,0:T(8,128)(2,1)S(1)} %pick_blocks.26), channel_id=1, source_target_pairs={{0,2},{1,3},{2,0},{3,1},{4,6},{5,7},{6,4},{7,5},{8,10},{9,11},{10,... | collective-permute-start | bytes 589832 | tf_op jit(solution)/shard_map/ppermute | solution.py:483
  223.3 18.8 %collective-permute-start.29 = (bf16[8,8,32,256]{3,2,1,0:T(8,128)(2,1)S(1)}, bf16[8,8,32,256]{3,2,1,0:T(8,128)(2,1)S(1)}, u32[]{:S(2)}, u32[]{:S(2)}) collective-permute-start(bf16[8,8,32,256]{3,2,1,0:T(8,128)(2,1)S(1)} %get-tuple-element.83), channel_id=1, source_target_pairs={{0,1},{1,0},{2,3},{3,2},{4,5},{5,4},{6,7},{7,6},{8,9},{9,8},{10,11... | collective-permute-start | bytes 3145736 | tf_op jit(solution)/shard_map/ppermute | solution.py:483
  237.1 10.3 %collective-permute-start.33 = (bf16[8,8,32,256]{3,2,1,0:T(8,128)(2,1)S(1)}, bf16[8,8,32,256]{3,2,1,0:T(8,128)(2,1)S(1)}, u32[]{:S(2)}, u32[]{:S(2)}) collective-permute-start(bf16[8,8,32,256]{3,2,1,0:T(8,128)(2,1)S(1)} %get-tuple-element.90), channel_id=1, source_target_pairs={{0,1},{1,0},{2,3},{3,2},{4,5},{5,4},{6,7},{7,6},{8,9},{9,8},{10,11... | collective-permute-start | bytes 3145736 | tf_op jit(solution)/shard_map/ppermute | solution.py:483
  252.8 3.6 %collective-permute-start.35 = (f32[8,8,32]{2,1,0:T(8,128)S(1)}, f32[8,8,32]{2,1,0:T(8,128)S(1)}, u32[]{:S(2)}, u32[]{:S(2)}) collective-permute-start(f32[8,8,32]{2,1,0:T(8,128)S(1)} %slice.86), channel_id=1, source_target_pairs={{0,1},{1,0},{2,3},{3,2},{4,5},{5,4},{6,7},{7,6},{8,9},{9,8},{10,11... | collective-permute-start | bytes 24584 | tf_op jit(solution)/shard_map/ppermute | solution.py:483
  256.4 4.0 %collective-permute-start.36 = (f32[4,8,32]{2,1,0:T(8,128)S(1)}, f32[4,8,32]{2,1,0:T(8,128)S(1)}, u32[]{:S(2)}, u32[]{:S(2)}) collective-permute-start(f32[4,8,32]{2,1,0:T(8,128)S(1)} %slice.88), channel_id=1, source_target_pairs={{0,2},{1,3},{2,0},{3,1},{4,6},{5,7},{6,4},{7,5},{8,10},{9,11},{10,... | collective-permute-start | bytes 12296 | tf_op jit(solution)/shard_map/ppermute | solution.py:483
  256.5 8.9 %collective-permute-start.10 = (bf16[1,2,256,256]{3,2,1,0:T(8,128)(2,1)S(1)}, bf16[1,2,256,256]{3,2,1,0:T(8,128)(2,1)S(1)}, u32[]{:S(2)}, u32[]{:S(2)}) collective-permute-start(bf16[1,2,256,256]{3,2,1,0:T(8,128)(2,1)S(1)} %copy-done.25), channel_id=1, source_target_pairs={{10,14},{26,30}} | collective-permute-start | bytes 786440 | tf_op jit(solution)/shard_map/ppermute | solution.py:483
  257.8 23.4 %collective-permute-start.20 = (bf16[2,2,256,256]{3,2,1,0:T(8,128)(2,1)S(1)}, bf16[2,2,256,256]{3,2,1,0:T(8,128)(2,1)S(1)}, u32[]{:S(2)}, u32[]{:S(2)}) collective-permute-start(bf16[2,2,256,256]{3,2,1,0:T(8,128)(2,1)S(1)} %get-tuple-element.69), channel_id=1, source_target_pairs={{10,14},{26,30}} | collective-permute-start | bytes 1572872 | tf_op jit(solution)/shard_map/ppermute | solution.py:483
  259.1 22.1 %collective-permute-start.25 = (bf16[2,2,256,256]{3,2,1,0:T(8,128)(2,1)S(1)}, bf16[2,2,256,256]{3,2,1,0:T(8,128)(2,1)S(1)}, u32[]{:S(2)}, u32[]{:S(2)}) collective-permute-start(bf16[2,2,256,256]{3,2,1,0:T(8,128)(2,1)S(1)} %get-tuple-element.77), channel_id=1, source_target_pairs={{10,14},{26,30}} | collective-permute-start | bytes 1572872 | tf_op jit(solution)/shard_map/ppermute | solution.py:483
  260.4 5.6 %collective-permute-start.37 = (f32[8,32]{1,0:T(8,128)S(1)}, f32[8,32]{1,0:T(8,128)S(1)}, u32[]{:S(2)}, u32[]{:S(2)}) collective-permute-start(f32[8,32]{1,0:T(8,128)S(1)} %get-tuple-element.98), channel_id=1, source_target_pairs={{0,12},{1,13},{2,14},{3,15},{4,8},{5,9},{6,10},{7,11},{8,4},{9,5},... | collective-permute-start | bytes 3080 | tf_op jit(solution)/shard_map/ppermute | solution.py:483
  260.5 16.3 %collective-permute-start.38 = (f32[8,32]{1,0:T(8,128)S(1)}, f32[8,32]{1,0:T(8,128)S(1)}, u32[]{:S(2)}, u32[]{:S(2)}) collective-permute-start(f32[8,32]{1,0:T(8,128)S(1)} %get-tuple-element.97), channel_id=1, source_target_pairs={{4,0},{9,1},{6,2},{11,3},{12,4},{1,5},{14,6},{3,7},{0,8},{13,9},{2... | collective-permute-start | bytes 3080 | tf_op jit(solution)/shard_map/ppermute | solution.py:483
  265.4 23.1 %copy-start.29 = (bf16[1,2,256,256]{3,2,1,0:T(8,128)(2,1)}, bf16[1,2,256,256]{3,2,1,0:T(8,128)(2,1)S(1)}, u32[]{:S(2)}) copy-start(bf16[1,2,256,256]{3,2,1,0:T(8,128)(2,1)S(1)} %collective-permute-done.10.refs_0_) | copy-start | bytes 786436
  265.4 12.7 %collective-permute-start.39 = (f32[8,32]{1,0:T(8,128)S(1)}, f32[8,32]{1,0:T(8,128)S(1)}, u32[]{:S(2)}, u32[]{:S(2)}) collective-permute-start(f32[8,32]{1,0:T(8,128)S(1)} %get-tuple-element.96), channel_id=1, source_target_pairs={{0,9},{1,4},{2,11},{3,6},{4,1},{5,12},{6,3},{7,14},{8,13},{9,0},{1... | collective-permute-start | bytes 3080 | tf_op jit(solution)/shard_map/ppermute | solution.py:483
  266.0 15.2 %collective-permute-start.15 = (bf16[1,2,256,256]{3,2,1,0:T(8,128)(2,1)S(1)}, bf16[1,2,256,256]{3,2,1,0:T(8,128)(2,1)S(1)}, u32[]{:S(2)}, u32[]{:S(2)}) collective-permute-start(bf16[1,2,256,256]{3,2,1,0:T(8,128)(2,1)S(1)} %copy-done.23), channel_id=1, source_target_pairs={{10,14},{26,30}} | collective-permute-start | bytes 786440 | tf_op jit(solution)/shard_map/ppermute | solution.py:483
  276.8 8.3 %collective-permute-start.30 = (bf16[1,2,256,256]{3,2,1,0:T(8,128)(2,1)S(1)}, bf16[1,2,256,256]{3,2,1,0:T(8,128)(2,1)S(1)}, u32[]{:S(2)}, u32[]{:S(2)}) collective-permute-start(bf16[1,2,256,256]{3,2,1,0:T(8,128)(2,1)S(1)} %get-tuple-element.85), channel_id=1, source_target_pairs={{10,14},{26,30}} | collective-permute-start | bytes 786440 | tf_op jit(solution)/shard_map/ppermute | solution.py:483
  278.1 9.8 %collective-permute-start.34 = (bf16[1,2,256,256]{3,2,1,0:T(8,128)(2,1)S(1)}, bf16[1,2,256,256]{3,2,1,0:T(8,128)(2,1)S(1)}, u32[]{:S(2)}, u32[]{:S(2)}) collective-permute-start(bf16[1,2,256,256]{3,2,1,0:T(8,128)(2,1)S(1)} %get-tuple-element.92), channel_id=1, source_target_pairs={{10,14},{26,30}} | collective-permute-start | bytes 786440 | tf_op jit(solution)/shard_map/ppermute | solution.py:483
  (26 other events, 215.2 us)

commit v3 on v0

v3 whole, which is shorter than its diff:
```python
import functools
import itertools

import jax
import jax.numpy as jnp
import numpy as np
from jax import lax
from jax.experimental import pallas as pl
from jax.experimental.pallas import tpu as pltpu
from jax.sharding import PartitionSpec as P


def unit_table(block_count):
    first_list = []
    second_list = []
    diag_list = []
    for row_block in range(block_count):
        for col_block in range(row_block + 1, block_count):
            first_list.append(row_block)
            second_list.append(col_block)
            diag_list.append(0)
    for pair_index in range(block_count // 2):
        first_list.append(2 * pair_index)
        second_list.append(2 * pair_index + 1)
        diag_list.append(1)
    return np.stack([first_list, second_list, diag_list], 1).astype(np.int32)


def turn_polynomials():
    nodes = 0.125 + 0.125 * np.cos(np.pi * (np.arange(64) + 0.5) / 64)
    root = np.sqrt(nodes)
    fit = np.polynomial.Polynomial.fit
    sine = fit(nodes, np.sin(2 * np.pi * root) / root, 7, domain=[0, 0.25]).convert()
    cosine = fit(nodes, np.cos(2 * np.pi * root), 8, domain=[0, 0.25]).convert()
    return [float(c) for c in sine.coef], [float(c) for c in cosine.coef]


def horner(coefs, x):
    total = coefs[-1]
    for coef in coefs[-2::-1]:
        total = total * x + coef
    return total


def build_kernel(sets, slot_ids, pieces, place_ref, *refs):
    beams, smalls, refs = refs[:sets], refs[sets : 2 * sets], refs[2 * sets :]
    uvw_ref, outs, bright_ref = refs[0], refs[1 : 1 + len(pieces)], refs[-1]
    per_group = outs[0].shape[2] // sets
    span = outs[0].shape[3]
    width = smalls[0].shape[1]
    lanes = lax.broadcasted_iota(jnp.int32, (per_group, width), 1)
    rows = lax.broadcasted_iota(jnp.int32, (per_group, width), 0)
    bright_lanes = lax.broadcasted_iota(jnp.int32, (per_group, 128), 1)
    sin_coefs, cos_coefs = turn_polynomials()
    brights = []
    for part, small in enumerate(smalls):
        group = pl.ds(part * per_group, per_group)

        def pick(chosen, row):
            return jnp.sum(jnp.where(chosen, small[row : row + 1, :], 0.0), axis=1, keepdims=True)

        def chosen_at(index):
            listed = pick(lanes == (place_ref[0] + index) * per_group + rows, 3)
            return listed.astype(jnp.int32) == lanes

        bright = jnp.zeros((per_group, 128), jnp.float32)
        for index in range(slot_ids[1]):
            bright = jnp.where(bright_lanes == index, pick(chosen_at(index), 2), bright)
        brights.append(bright)
        chosen = chosen_at(slot_ids[0])
        east = pick(chosen, 0)
        north = pick(chosen, 1)
        depth = jnp.sqrt(1.0 - east * east - north * north) - 1.0
        for out_ref, piece in zip(outs, pieces):
            for place, block in enumerate(piece):
                cols = pl.ds(block * span, span)
                delay = (
                    uvw_ref[0, 0:1, cols] * east
                    + uvw_ref[0, 1:2, cols] * north
                    + uvw_ref[0, 2:3, cols] * depth
                )
                turn = delay - jnp.floor(delay + 0.5)
                square = turn * turn
                sine = horner(sin_coefs, square) * turn
                cosine = horner(cos_coefs, square)
                real = beams[part][0, 0, :, cols].astype(jnp.float32)
                imag = beams[part][0, 1, :, cols].astype(jnp.float32)
                out_ref[0, place, group] = (real * cosine + imag * sine).astype(jnp.bfloat16)
                out_ref[1, place, group] = (imag * cosine - real * sine).astype(jnp.bfloat16)
    missing = -len(brights) * per_group % 128
    if missing:
        brights.append(jnp.zeros((missing, 128), jnp.float32))
    turned = jnp.concatenate(brights, 0).T
    bright_ref[...] = turned[: bright_ref.shape[0], : bright_ref.shape[1]]


def build_factors(slot_ids, place, beam, other_beams, antenna_uvw, smalls, pieces, span):
    _, _, per_group, antennas = beam.shape
    sets = 1 + len(other_beams)
    index = slot_ids[0]
    whole = pl.BlockSpec(memory_space=pltpu.VMEM)
    shapes = [(2, len(piece), sets * per_group, span) for piece in pieces]
    return pl.pallas_call(
        functools.partial(build_kernel, sets, slot_ids, pieces),
        grid_spec=pltpu.PrefetchScalarGridSpec(
            num_scalar_prefetch=1,
            grid=(1,),
            in_specs=[
                pl.BlockSpec((1, 2, per_group, antennas), lambda n, at: (at[0] + index, 0, 0, 0)),
                *[whole] * (len(other_beams) + sets),
                pl.BlockSpec((1, 3, antennas), lambda n, at: (at[0] + index, 0, 0)),
            ],
            out_specs=[whole] * (len(pieces) + 1),
        ),
        out_shape=[jax.ShapeDtypeStruct(shape, jnp.bfloat16) for shape in shapes]
        + [jax.ShapeDtypeStruct((8, sets * per_group), jnp.float32)],
        compiler_params=pltpu.CompilerParams(vmem_limit_bytes=40 * 1024 * 1024),
        name="build_factors",
    )(place, beam, *other_beams, *smalls, antenna_uvw)


KIND, ONE, TWO, ONE_AT, TWO_AT, OUT_ROWS, VIS_AT = 0, 1, 2, 3, 5, 7, 9
COLUMNS = 11


def unit_kernel(index, pieces, outs, aliased, tab_ref, place_ref, *refs):
    arrays = []
    for both, single in pieces:
        entries = [(ref.at[0], ref.at[1]) for ref in refs[:both]]
        if single:
            entries.append((refs[both], refs[both + 1]))
        arrays.append(entries)
        refs = refs[both + 2 * single :]
    vis_ref, keep_one_ref, keep_two_ref, bright_ref = refs[:4]
    refs = refs[4 + aliased :]
    out_refs, grad_ref = refs[:outs], refs[outs]
    total_ref, column_ref, one_ref, two_ref = refs[outs + 1 :]
    step = pl.program_id(0)
    slot = place_ref[0] + index
    sources, span = one_ref.shape[1:]

    def load(target, at):
        for n, entries in enumerate(arrays):

            @pl.when(tab_ref[step, at] == n)
            def _(entries=entries):
                place = tab_ref[step, at + 1]
                start = 0
                for entry in entries:
                    count = entry[0].shape[1]
                    for part in (0, 1):
                        target[part, pl.ds(start, count)] = entry[part][place]
                    start += count

    def dot(a, b):
        return lax.dot_general(a, b, (((1,), (0,)), ((), ())), preferred_element_type=jnp.float32)

    def scaled_of(re, im):
        column = jnp.concatenate([column_ref[...]] * (span // 128), 1)
        return (
            (re.astype(jnp.float32) * column).astype(jnp.bfloat16),
            (im.astype(jnp.float32) * column).astype(jnp.bfloat16),
        )

    def outer(a, b):
        row_ids = lax.broadcasted_iota(jnp.int32, a.shape, 0)
        a = jnp.where(row_ids == slot, a, 0.0)
        return lax.dot_general(a, b, (((0,), (0,)), ((), ())), preferred_element_type=jnp.float32)

    def cross(a_re, a_im, b_re, b_im):
        lhs = jnp.concatenate([a_re, a_im], 0).T
        rhs = jnp.concatenate(
            [jnp.concatenate([b_re, -b_im], 1), jnp.concatenate([b_im, b_re], 1)], 0
        )
        both = dot(lhs, rhs)
        return both[:, :span], both[:, span:]

    def pull(re, im, res_re, res_im, sign):
        lhs = jnp.concatenate([re, im], 1)
        rhs = jnp.concatenate(
            [
                jnp.concatenate([res_re, res_im], 1),
                jnp.concatenate([res_im, -res_re] if sign == 1 else [-res_im, res_re], 1),
            ],
            0,
        )
        both = dot(lhs, rhs)
        return both[:, :span], both[:, span:]

    def add_grad(value):
        folded = value[:, :128]
        for start in range(128, span, 128):
            folded = folded + value[:, start : start + 128]
        total_ref[...] += folded

    def put(res_re, res_im):
        for out_ref in out_refs:
            out_ref[0, 0] = res_re
            out_ref[0, 1] = res_im

    @pl.when(step == 0)
    def _():
        total_ref[...] = jnp.zeros_like(total_ref)
        for start in range(0, sources, 128):
            row = bright_ref[pl.ds(index, 1), pl.ds(start, 128)]
            column_ref[pl.ds(start, 128)] = jnp.broadcast_to(row, (128, 128)).T

    @pl.when(tab_ref[step, KIND] != 2)
    def _():
        load(one_ref, ONE_AT)
        load(two_ref, TWO_AT)

    @pl.when(tab_ref[step, KIND] == 0)
    def _():
        one_re, one_im, two_re, two_im = one_ref[0], one_ref[1], two_ref[0], two_ref[1]
        pred_re, pred_im = cross(*scaled_of(one_re, one_im), two_re, two_im)
        weights = outer(keep_one_ref[...], keep_two_ref[...])
        res_re = (weights * (vis_ref[0, 0, 0, 0].astype(jnp.float32) - pred_re)).astype(jnp.bfloat16)
        res_im = (weights * (vis_ref[0, 0, 0, 1].astype(jnp.float32) - pred_im)).astype(jnp.bfloat16)
        put(res_re, res_im)
        sum_re, sum_im = pull(one_re, one_im, res_re, res_im, 1)
        add_grad(sum_re * two_re.astype(jnp.float32) - sum_im * two_im.astype(jnp.float32))

    @pl.when(tab_ref[step, KIND] == 1)
    def _():
        one_re, one_im, two_re, two_im = one_ref[0], one_ref[1], two_ref[0], two_ref[1]
        row_ids = lax.broadcasted_iota(jnp.int32, (span, span), 0)
        col_ids = lax.broadcasted_iota(jnp.int32, (span, span), 1)
        upper = row_ids < col_ids
        lower = row_ids > col_ids
        first_re, first_im = cross(*scaled_of(one_re, one_im), one_re, one_im)
        second_re, second_im = cross(two_re, two_im, *scaled_of(two_re, two_im))
        keep_one = keep_one_ref[...]
        keep_two = keep_two_ref[...]
        weights = jnp.where(upper, outer(keep_one, keep_one), 0.0) + jnp.where(
            lower, outer(keep_two, keep_two), 0.0
        )
        vis_re = vis_ref[0, 0, 0, 0].astype(jnp.float32)
        vis_im = vis_ref[0, 0, 0, 1].astype(jnp.float32)
        res_re = (weights * (vis_re - jnp.where(upper, first_re, second_re))).astype(jnp.bfloat16)
        res_im = (weights * (vis_im - jnp.where(upper, first_im, -second_im))).astype(jnp.bfloat16)
        put(res_re, res_im)
        none = jnp.zeros_like(res_re)
        sum_re, sum_im = pull(
            one_re, one_im, jnp.where(upper, res_re, none), jnp.where(upper, res_im, none), 1
        )
        add_grad(sum_re * one_re.astype(jnp.float32) - sum_im * one_im.astype(jnp.float32))
        sum_re, sum_im = pull(
            two_re, two_im, jnp.where(lower, res_re, none), jnp.where(lower, res_im, none), -1
        )
        add_grad(sum_re * two_re.astype(jnp.float32) + sum_im * two_im.astype(jnp.float32))

    @pl.when(step == pl.num_programs(0) - 1)
    def _():
        grad_ref[...] = jnp.sum(total_ref[...].T, axis=0, keepdims=True)


def unit_work(index, table, place, pieces, vis, keep, bright, outs):
    span = vis.shape[5]
    slots = keep.shape[0]
    sources = sum(array.shape[-2] for array in pieces[0][0]) + (
        pieces[0][1][0].shape[-2] if pieces[0][1] else 0
    )
    whole = pl.BlockSpec(memory_space=pltpu.VMEM)
    arrays = [array for both, single in pieces for array in (*both, *single)]
    in_specs = [whole] * len(arrays) + [
        pl.BlockSpec(
            (1, 1, 1, 2, span, span),
            lambda u, tab, at: (tab[u, VIS_AT], tab[u, VIS_AT + 1], index, 0, 0, 0),
        ),
        pl.BlockSpec((slots, span), lambda u, tab, at: (0, tab[u, ONE])),
        pl.BlockSpec((slots, span), lambda u, tab, at: (0, tab[u, TWO])),
        whole,
    ]
    operands = [table, place, *arrays, vis, keep, keep, bright]
    aliases = {}
    out_specs, out_shapes = [], []
    for n, out in enumerate(outs):
        rows = out
        if not isinstance(out, int):
            rows = out.shape[0]
            aliases[len(operands)] = n
            operands.append(out)
            in_specs.append(pl.BlockSpec(memory_space=pl.ANY))
        out_specs.append(
            pl.BlockSpec((1, 2, span, span), lambda u, tab, at, n=n: (tab[u, OUT_ROWS + n], 0, 0, 0))
        )
        out_shapes.append(jax.ShapeDtypeStruct((rows, 2, span, span), jnp.bfloat16))
    out_specs.append(pl.BlockSpec((1, sources), lambda u, tab, at: (0, 0)))
    out_shapes.append(jax.ShapeDtypeStruct((1, sources), jnp.float32))
    steps = table.shape[0]
    flops = 16 * steps * sources * span * span
    kinds = [(len(both), int(bool(single))) for both, single in pieces]
    return pl.pallas_call(
        functools.partial(unit_kernel, index, kinds, len(outs), len(aliases)),
        grid_spec=pltpu.PrefetchScalarGridSpec(
            num_scalar_prefetch=2,
            grid=(steps,),
            in_specs=in_specs,
            out_specs=out_specs,
            scratch_shapes=[
                pltpu.VMEM((sources, 128), jnp.float32),
                pltpu.VMEM((sources, 128), jnp.float32),
                pltpu.VMEM((2, sources, span), jnp.bfloat16),
                pltpu.VMEM((2, sources, span), jnp.bfloat16),
            ],
        ),
        out_shape=out_shapes,
        input_output_aliases=aliases,
        compiler_params=pltpu.CompilerParams(vmem_limit_bytes=48 * 1024 * 1024),
        cost_estimate=pl.CostEstimate(flops=flops, bytes_accessed=flops // 128, transcendentals=0),
        name="unit_work",
    )(*operands)


def put_kernel(sources, tab_ref, *refs):
    out_ref = refs[-1]
    for step, (which, row) in enumerate(sources):

        @pl.when(pl.program_id(0) == step)
        def _(which=which, row=row):
            out_ref[0, 0] = refs[which][...] if row is None else refs[which][row]


def put_residuals(sources, arrays, targets, shape, residual):
    span = shape[-1]
    whole = pl.BlockSpec(memory_space=pltpu.VMEM)
    operands = [targets, *arrays]
    in_specs = [whole] * len(arrays)
    aliases = {}
    if residual is not None:
        aliases = {len(operands): 0}
        operands.append(residual)
        in_specs.append(pl.BlockSpec(memory_space=pl.ANY))
    return pl.pallas_call(
        functools.partial(put_kernel, sources),
        grid_spec=pltpu.PrefetchScalarGridSpec(
            num_scalar_prefetch=1,
            grid=(len(sources),),
            in_specs=in_specs,
            out_specs=pl.BlockSpec(
                (1, 1, 2, span, span), lambda n, tab: (tab[n, 0], tab[n, 1], 0, 0, 0)
            ),
        ),
        out_shape=jax.ShapeDtypeStruct(shape, jnp.bfloat16),
        input_output_aliases=aliases,
        compiler_params=pltpu.CompilerParams(vmem_limit_bytes=32 * 1024 * 1024),
        name="put_residuals",
    )(*operands)


class Routes:
    def __init__(self, planes, width, units):
        count = planes * width
        blocks = int(units[:, :2].max()) + 1
        self.width = width
        self.units_dev = units_dev = units.shape[0] // count
        ring = [0] + list(range(1, planes, 2)) + list(range(planes - 2, 0, -2))

        def along(step):
            at = {plane: ring[(n + step) % planes] for n, plane in enumerate(ring)}
            return [(t, at[t // width] * width + t % width) for t in range(count)]

        self.onward = along(1)
        self.backward = along(-1)
        self.opposite = along(2)
        self.partner = [[(t, t ^ m) for t in range(count)] for m in range(width)]

        touched = [set(units[u, :2].tolist()) for u in range(units.shape[0])]
        home = [list(range(t * units_dev, (t + 1) * units_dev)) for t in range(count)]
        of_plane = [range(z * width * units_dev, (z + 1) * width * units_dev) for z in range(planes)]

        def most(wanted):
            return max(sum(bool(wanted(touched[u])) for u in plane) for plane in of_plane)

        def stuck(block):
            return sum(all(block in touched[u] for u in mine) for mine in home)

        end = min(range(blocks), key=lambda b: (stuck(b), most(lambda t: b in t)))
        rest = [b for b in range(blocks) if b != end]
        start = min(
            itertools.combinations(rest, blocks // 2),
            key=lambda c: most(lambda t: end not in t and not t <= set(c)),
        )
        self.pieces = [list(start), [b for b in rest if b not in start], [end]]
        events = []
        for blocks_of in touched:
            events.append(max(n for n, piece in enumerate(self.pieces) if blocks_of & set(piece)))
        order = [sorted(mine, key=lambda u: events[u]) for mine in home]
        self.full = [list(range(blocks))]

        def rows_of(t, pieces, wanted, row_of, trash):
            rows = []
            for m in range(width):
                for phase, u in enumerate(order[t ^ m]):
                    if not wanted(u):
                        continue
                    one, two, kind = units[u].tolist()
                    at = [
                        (n, piece.index(b))
                        for b in (one, two)
                        for n, piece in enumerate(pieces)
                        if b in piece
                    ]
                    rows.append(
                        [kind, one, two, *at[0], *at[1], *row_of(m, phase), m, u % units_dev]
                    )
            return rows

        def table_of(pieces, wanted, row_of, trash):
            tables = [rows_of(t, pieces, wanted, row_of, trash) for t in range(count)]
            steps = max(len(rows) for rows in tables)
            for rows in tables:
                while len(rows) < steps:
                    rows.append([2] + (rows[-1][1:] if rows else [0] * (COLUMNS - 1)))
                    rows[-1][OUT_ROWS : OUT_ROWS + 2] = [trash, trash]
            return np.array(tables, np.int32)

        self.first_table = table_of(
            self.full, lambda u: True, lambda m, phase: (m * units_dev + phase, 0), 0
        )
        self.tables = [
            table_of(
                self.pieces,
                lambda u, n=n: events[u] == n,
                lambda m, phase: (m, width) if phase == 0 else (width, m + width * (phase - 1)),
                width,
            )
            for n in range(len(self.pieces))
        ]
        assert units_dev == 2
        assert all(events[order[t][0]] < len(self.pieces) - 1 for t in range(count))
        self.unit_of = np.array([[u % units_dev for u in order[t]] for t in range(count)], np.int32)


def ship(value, pairs):
    return lax.ppermute(value, "tile", pairs)


def in_order(value, *earlier):
    return lax.optimization_barrier((value, *earlier))[0]


def packed_small(source_dirs, source_flux, visible_list):
    listed = visible_list.astype(jnp.float32).reshape(1, -1)
    rows = [source_dirs, source_flux.astype(jnp.float32)[None], listed]
    width = max(row.shape[1] for row in rows)
    return jnp.concatenate([jnp.pad(row, ((0, 0), (0, width - row.shape[1]))) for row in rows], 0)


def plain_program(visibility, beam, antenna_uvw, small, keep):
    units_dev, slots, _, span, _ = visibility.shape
    blocks = beam.shape[3] // span
    tile_index = lax.axis_index("tile")
    units = unit_table(blocks)
    own_rows = np.tile(np.arange(units_dev), units.shape[0] // units_dev)
    none = np.zeros_like(own_rows)
    table = np.stack(
        [units[:, 2], units[:, 0], units[:, 1], none, units[:, 0], none, units[:, 1]]
        + [own_rows, none, none, own_rows],
        1,
    )
    table = lax.dynamic_slice_in_dim(
        jnp.asarray(table.astype(np.int32)), tile_index * units_dev, units_dev, 0
    )
    place = jnp.zeros((1,), jnp.int32)
    bright = None
    residuals, grads = [], []
    for slot in range(slots):
        owned, shine = build_factors(
            (slot, slots), place, beam, [], antenna_uvw, [small], [list(range(blocks))], span
        )
        factors = lax.all_gather(owned, "tile", axis=2, tiled=True)
        if bright is None:
            bright = lax.all_gather(shine, "tile", axis=1, tiled=True)
        residual, grad = unit_work(
            slot, table, place, [([factors], [])], visibility[None], keep, bright, [units_dev]
        )
        residuals.append(residual)
        grads.append(grad)
    summed = lax.psum_scatter(jnp.concatenate(grads, 0), "tile", scatter_dimension=1, tiled=True)
    return jnp.stack(residuals, 1), summed


def plane_program(routes, visibility, beam, antenna_uvw, small, keep):
    units_dev, slots, _, span, _ = visibility.shape
    width = routes.width
    share = slots // width
    tile_index = lax.axis_index("tile")
    mine = tile_index % width
    others = range(1, width)

    def mine_of(rows):
        return lax.dynamic_index_in_dim(jnp.asarray(rows), tile_index, 0, keepdims=False)

    def slots_of(m):
        return jnp.bitwise_xor(mine, m) * share

    place = slots_of(0).astype(jnp.int32).reshape(1)

    smalls = [small] + [ship(small, routes.partner[m]) for m in others]

    def beams_of(index):
        return [
            lax.dynamic_slice_in_dim(beam, slots_of(m) + index, 1, 0)
            for m in others
        ]

    beams = [ship(part, routes.partner[m]) for m, part in zip(others, beams_of(0))]
    (first, bright) = build_factors(
        (0, share), place, beam, beams, antenna_uvw, smalls, routes.full, span
    )

    def near(piece):
        return [ship(piece, routes.onward), ship(piece, routes.backward)]

    def far(piece, sides):
        halves = [ship(sides[0][0], routes.onward), ship(sides[1][1], routes.backward)]
        return ([piece, *sides], halves)

    sides_first = near(first)

    link = first
    later_beams = []
    for m, part in zip(others, beams_of(1)):
        later_beams.append(ship(in_order(part, link), routes.partner[m]))
    link = later_beams[-1]
    *later, _ = build_factors(
        (1, share), place, beam, later_beams, antenna_uvw, smalls, routes.pieces, span
    )
    brights = [
        bright,
        ship(bright, routes.onward),
        ship(bright, routes.backward),
        ship(bright, routes.opposite),
    ]
    vis = []
    for m in range(width):
        part = lax.dynamic_slice_in_dim(visibility, slots_of(m), share, 1)
        if m:
            part = ship(in_order(part, link), routes.partner[m])
            link = part
        vis.append(part)
    vis = jnp.stack(vis, 0)
    bright = jnp.concatenate(brights, 1)

    held = []
    sides = sides_first
    ready = [far(first, sides_first)]
    for n, piece in enumerate(later):
        if n == len(later) - 1:
            first_res, first_grad = unit_work(
                0,
                mine_of(routes.first_table),
                place,
                [ready[0]],
                vis,
                keep,
                bright,
                [width * units_dev],
            )
            piece = in_order(piece, first_grad)
        piece = in_order(piece, *sides)
        sides = near(piece)
        held.append((piece, sides))
        ready.append(far(piece, sides))

    residual = None
    unit_of = mine_of(routes.unit_of)

    def targets_of(pairs, index):
        return jnp.stack(
            [jnp.stack([unit_of[phase], slots_of(m).astype(jnp.int32) + index]) for m, phase in pairs]
        ).astype(jnp.int32)

    returned = []
    for m in others:
        rows = first_res[m * units_dev : (m + 1) * units_dev]
        returned.append(ship(in_order(rows, link), routes.partner[m]))
        link = returned[-1]
    pairs = [(m, phase) for m in range(width) for phase in range(units_dev)]
    residual = put_residuals(
        [(m, phase) for m, phase in pairs],
        [first_res, *returned],
        targets_of(pairs, 0),
        visibility.shape,
        None,
    )

    grads = []
    outs = [width + 1, width + 1]
    for n in range(len(later)):
        last = n == len(later) - 1
        if last:
            outs = outs[1:]
        table = mine_of(routes.tables[n])
        if last:
            table = jnp.concatenate(
                [table[:, :OUT_ROWS], table[:, OUT_ROWS + 1 :][:, :1], table[:, OUT_ROWS + 1 :]], 1
            )
        *outs, grad = unit_work(1, table, place, ready[1 : n + 2], vis, keep, bright, outs)
        grads.append(grad)
        if n >= len(later) - 2:
            back = [ship(outs[0][m], routes.partner[m]) for m in others]
            phase = 1 if last else 0
            pairs = [(m, phase) for m in range(width)]
            residual = put_residuals(
                [(0, 0)] + [(m, None) for m in others],
                [outs[0], *back],
                targets_of(pairs, 1),
                visibility.shape,
                residual,
            )

    partial = jnp.concatenate([first_grad, sum(grads[1:], grads[0])], 0)
    group = partial.shape[1] // 4
    parts = [partial[:, n * group : (n + 1) * group] for n in range(4)]
    plane_sum = (parts[0] + ship(parts[3], routes.opposite)) + (
        ship(parts[1], routes.backward) + ship(parts[2], routes.onward)
    )
    per_group = group // width
    own = [plane_sum[:, m * per_group : (m + 1) * per_group] for m in range(width)]
    own = jnp.stack([own[0]] + [ship(own[m], routes.partner[m]) for m in others], 0)
    ids = jnp.arange(width, dtype=jnp.int32)
    here = jnp.bitwise_xor(ids[:, None], mine) == ids[None, :]
    summed = jnp.sum(jnp.where(here[:, :, None, None], own[None], 0.0), axis=1)
    return residual, summed.reshape(slots, per_group)


def per_device(
    visibility, station_beam, antenna_uvw, source_dirs, source_flux, visible_list, antenna_flags
):
    span = visibility.shape[4]
    antennas = station_beam.shape[3]
    small = packed_small(source_dirs, source_flux, visible_list)
    keep = 1.0 - antenna_flags.astype(jnp.float32)
    arguments = (visibility, station_beam, antenna_uvw, small, keep)
    if lax.axis_size("tile") == 16:
        routes = Routes(4, 4, unit_table(antennas // span))
        residual, summed = plane_program(routes, *arguments)
    else:
        residual, summed = plain_program(*arguments)
    return (residual, summed * (-1.0 / (8.0 * antennas)))


def solution(mesh):
    return jax.shard_map(
        per_device,
        mesh=mesh,
        in_specs=(
            P("tile", "grp", None, None, None),
            P("grp", None, "tile", None),
            P("grp", None, None),
            P(None, "tile"),
            P(("grp", "tile")),
            P(None, "tile"),
            P("grp", None),
        ),
        out_specs=(P("tile", "grp", None, None, None), P("grp", "tile")),
        check_vma=False,
    )
```

time: 427 us -> 271 us (0.63)
  waiting for transfers between devices: 229 us -> 121 us
  starting transfers between devices: 0.08 us -> 66.8 us
  local copies, waits for them, and re-layouts: 72.1 us -> 19.2 us
  Pallas kernels: 0 us -> 41.8 us
  other arithmetic: 52 us -> 16.5 us
  matrix products: 30 us -> 0 us
  blocking collectives: 23.6 us -> 0 us
  between operations: 18.3 us -> 0.93 us
    all_gather x1 -> x0, waiting for transfers between devices: 139 us -> none  [per_device(): lax.all_gather(owned, 'tile', axis=2, tiled=True)]
    ppermute x0 -> x46, waiting for transfers between devices: none -> 121 us  [ship(): return lax.ppermute(value, 'tile', pairs)]
    unnamed x3 -> x0, waiting for transfers between devices: 90.2 us -> none
    ppermute x0 -> x46, starting transfers between devices: none -> 66.8 us  [ship(): return lax.ppermute(value, 'tile', pairs)]
    pallas_call x0 -> x9, Pallas kernels: none -> 41.8 us  [the longest x4 27.8 us: unit_work(): pl.pallas_call(functools.partial(unit_kernel, index, kinds, len(outs), le...]
    unnamed x39 -> x28, local copies, waits for them, and re-layouts: 38.4 us -> 5.11 us
    dot_general x4 -> x0, matrix products: 30 us -> none  [the longest x2 17.1 us: predict(): jnp.einsum('tdckr,tckq->tdrq', stacked, cols_f, preferred_element_type=jn...]
    all_gather x1 -> x0, blocking collectives: 23.6 us -> none  [per_device(): lax.all_gather(brightness, 'tile', axis=1, tiled=True)]
  transfers between devices with their start and end apart: 2 -> 46, of which waited for: 2 -> 13; matrix products, arithmetic and copies ran while one was open for 2% -> 11% of each run, Pallas kernels for 0% -> 14%
where the time goes in v3:
time: 271 us; the launch traced here: 266 us
  waiting for transfers between devices  121 us (45%)
  starting transfers between devices  66.8 us (25%)
  Pallas kernels  41.8 us (15%)
  local copies, waits for them, and re-layouts  19.2 us (7%)
  other arithmetic  16.5 us (6%)
    ppermute x46, waiting for transfers between devices, ship(): return lax.ppermute(value, 'tile', pairs)  121 us
    ppermute x46, starting transfers between devices, ship(): return lax.ppermute(value, 'tile', pairs)  66.8 us
    pallas_call x4, Pallas kernels, unit_work(): pl.pallas_call(functools.partial(unit_kernel, index, kinds, len(outs), le...  27.8 us
    another operation x12, other arithmetic, targets_of(): jnp.stack([jnp.stack([unit_of[phase], slots_of(m).astype(jnp.int32) + ind...  9.55 us
    pallas_call x3, Pallas kernels, put_residuals(): pl.pallas_call(functools.partial(put_kernel, sources), grid_spec=pltpu.Pr...  7.98 us
    pallas_call x2, Pallas kernels, build_factors(): pl.pallas_call(functools.partial(build_kernel, sets, slot_ids, pieces), g...  6.01 us
  transfers between devices with their start and end apart: 46, of which 13 were waited for; matrix products, arithmetic and copies ran while one was open for 11% of the time, Pallas kernels for 14%

profile of v3, /device:TPU:0, one launch (start us, length us, event | category | flops | bytes accessed | tf_op | source)
XLA Modules:
  0.0 265.9 jit_solution(17638655447476133721)
XLA Ops:
  3.4 2.6 collective-permute-start.4
  5.9 2.4 constant_dynamic-slice_fusion.4
  8.8 1.4 collective-permute-start.2
  14.4 1.3 add_bitcast_fusion.8
  18.4 4.0 %collective-permute-done.5.refs_7_ = f32[4,256]{1,0:T(4,128)S(1)} collective-permute-done((f32[4,256]{1,0:T(4,128)S(1)}, f32[4,256]{1,0:T(4,128)S(1)}, u32[]{:S(2)}, u32[]{:S(2)}) %collective-permute-start.5) | collective-permute-done | bytes 4128 | tf_op jit(solution)/shard_map/ppermute | solution.py:437
  22.4 3.0 %build_factors.2 = (bf16[2,8,128,256]{3,2,1,0:T(8,128)(2,1)}, f32[8,128]{1,0:T(8,128)S(1)}) custom-call(s32[1]{0:T(128)} %bitcast.10.place_ref, bf16[8,2,32,2048]{3,2,1,0:T(8,128)(2,1)S(1)} %copy-done.2, bf16[1,2,32,2048]{3,2,1,0:T(8,128)(2,1)S(1)} %collective-permute-done.refs_1_, bf16[1,2,32,2048]{3,2,1,0:T(8,128)(2,1)S(1)} %collective-permute-done.1.refs_2_, ...), custom_call_target="tpu_custom_call" | custom-call | tf_op jit(solution)/shard_map/build_factors/pallas_call | solution.py:103
  26.3 4.0 %dynamic-slice_bitcast_fusion = (bf16[1,2,2,2,256,256]{5,4,3,2,1,0:T(8,128)(2,1)}, bf16[2,2,2,256,256]{4,3,2,1,0:T(8,128)(2,1)S(1)}, bf16[2,2,2,256,256]{4,3,2,1,0:T(8,128)(2,1)}, bf16[2,2,2,256,256]{4,3,2,1,0:T(8,128)(2,1)}) fusion(bf16[2,8,2,256,256]{4,3,2,1,0:T(8,128)(2,1)} %param.12, s32[]{:T(128)S(6)} %select_n.55, s32[]{:T(128)S(6)} %select_n.50, ...), kind=kLoop, calls=%fused_computation.1 | loop fusion | bytes 8388624 | tf_op jit(solution)/shard_map/stack | solution.py:544
  30.3 3.1 %collective-permute-done.8.refs_3_ = bf16[1,2,32,2048]{3,2,1,0:T(8,128)(2,1)S(1)} collective-permute-done((bf16[1,2,32,2048]{3,2,1,0:T(8,128)(2,1)S(1)}, bf16[1,2,32,2048]{3,2,1,0:T(8,128)(2,1)S(1)}, u32[]{:S(2)}, u32[]{:S(2)}) %collective-permute-start.8) | collective-permute-done | bytes 262176 | tf_op jit(solution)/shard_map/ppermute | solution.py:437
  35.9 1.7 collective-permute-start.9
  37.6 1.3 collective-permute-start.10
  39.9 1.3 add_bitcast_fusion.10
  41.9 1.4 collective-permute-start.24
  43.3 1.2 add_bitcast_fusion.12
  44.6 1.5 collective-permute-start.25
  46.1 37.3 %collective-permute-done.24 = f32[8,128]{1,0:T(8,128)S(1)} collective-permute-done((f32[8,128]{1,0:T(8,128)S(1)}, f32[8,128]{1,0:T(8,128)S(1)}, u32[]{:S(2)}, u32[]{:S(2)}) %collective-permute-start.24) | collective-permute-done | bytes 4128 | tf_op jit(solution)/shard_map/ppermute | solution.py:437
  83.3 1.8 add_bitcast_fusion.14
  86.3 5.4 %collective-permute-start.26 = (f32[8,128]{1,0:T(8,128)S(1)}, f32[8,128]{1,0:T(8,128)S(1)}, u32[]{:S(2)}, u32[]{:S(2)}) collective-permute-start(f32[8,128]{1,0:T(8,128)S(1)} %get-tuple-element.42), channel_id=1, source_target_pairs={{0,12},{1,13},{2,14},{3,15},{4,8},{5,9},{6,10},{7,11},{8,4},{9,5},... | collective-permute-start | bytes 12296 | tf_op jit(solution)/shard_map/ppermute | solution.py:437
  91.7 3.0 %collective-permute-done.7.refs_2_ = bf16[1,2,32,2048]{3,2,1,0:T(8,128)(2,1)S(1)} collective-permute-done((bf16[1,2,32,2048]{3,2,1,0:T(8,128)(2,1)}, bf16[1,2,32,2048]{3,2,1,0:T(8,128)(2,1)S(1)}, u32[]{:S(2)}, u32[]{:S(2)}) %collective-permute-start.7) | collective-permute-done | bytes 262176 | tf_op jit(solution)/shard_map/ppermute | solution.py:437
  95.7 3.0 %build_factors.3 = (bf16[2,4,128,256]{3,2,1,0:T(8,128)(2,1)S(1)}, bf16[2,3,128,256]{3,2,1,0:T(8,128)(2,1)S(1)}, bf16[2,1,128,256]{3,2,1,0:T(8,128)(2,1)S(1)}, f32[8,128]{1,0:T(8,128)}) custom-call(s32[1]{0:T(128)} %bitcast.10.place_ref, bf16[8,2,32,2048]{3,2,1,0:T(8,128)(2,1)S(1)} %copy-done.2, bf16[1,2,32,2048]{3,2,1,0:T(8,128)(2,1)} %collective-permute-done.6.refs_1_, ...), custom_call_target="tpu_custom_call" | custom-call | tf_op jit(solution)/shard_map/build_factors/pallas_call | solution.py:103
  98.8 2.7 %collective-permute-start.11 = (bf16[2,4,128,256]{3,2,1,0:T(8,128)(2,1)S(1)}, bf16[2,4,128,256]{3,2,1,0:T(8,128)(2,1)S(1)}, u32[]{:S(2)}, u32[]{:S(2)}) collective-permute-start(bf16[2,4,128,256]{3,2,1,0:T(8,128)(2,1)S(1)} %get-tuple-element.35.refs_0_), channel_id=1, source_target_pairs={{0,4},{1,5},{2,6},{3,7},{4,12},{5,13},{6,14},{7,15},{8,0},{9,1},{1... | collective-permute-start | bytes 1572872 | tf_op jit(solution)/shard_map/ppermute | solution.py:437
  102.3 2.6 collective-permute-start.19
  106.5 8.6 %collective-permute-done.11.refs_1_ = bf16[2,4,128,256]{3,2,1,0:T(8,128)(2,1)S(1)} collective-permute-done((bf16[2,4,128,256]{3,2,1,0:T(8,128)(2,1)S(1)}, bf16[2,4,128,256]{3,2,1,0:T(8,128)(2,1)S(1)}, u32[]{:S(2)}, u32[]{:S(2)}) %collective-permute-start.11) | collective-permute-done | bytes 524320 | tf_op jit(solution)/shard_map/ppermute | solution.py:437
  115.1 13.2 %collective-permute-done.12.refs_2_ = bf16[2,4,128,256]{3,2,1,0:T(8,128)(2,1)S(1)} collective-permute-done((bf16[2,4,128,256]{3,2,1,0:T(8,128)(2,1)S(1)}, bf16[2,4,128,256]{3,2,1,0:T(8,128)(2,1)S(1)}, u32[]{:S(2)}, u32[]{:S(2)}) %collective-permute-start.12) | collective-permute-done | bytes 524320 | tf_op jit(solution)/shard_map/ppermute | solution.py:437
  128.8 2.4 collective-permute-start.16
  131.3 25.1 %collective-permute-done.15.refs_6_ = bf16[2,3,128,256]{3,2,1,0:T(8,128)(2,1)S(1)} collective-permute-done((bf16[2,3,128,256]{3,2,1,0:T(8,128)(2,1)S(1)}, bf16[2,3,128,256]{3,2,1,0:T(8,128)(2,1)S(1)}, u32[]{:S(2)}, u32[]{:S(2)}) %collective-permute-start.15) | collective-permute-done | bytes 393248 | tf_op jit(solution)/shard_map/ppermute | solution.py:437
  156.4 10.2 %collective-permute-start.13 = (bf16[4,128,256]{2,1,0:T(8,128)(2,1)S(1)}, bf16[4,128,256]{2,1,0:T(8,128)(2,1)S(1)}, u32[]{:S(2)}, u32[]{:S(2)}) collective-permute-start(bf16[4,128,256]{2,1,0:T(8,128)(2,1)S(1)} %slice_bitcast_fusion.3), channel_id=1, source_target_pairs={{0,4},{1,5},{2,6},{3,7},{4,12},{5,13},{6,14},{7,15},{8,0},{9,1},{1... | collective-permute-start | bytes 786440 | tf_op jit(solution)/shard_map/ppermute | solution.py:437
  166.7 3.4 %collective-permute-start.17 = (bf16[3,128,256]{2,1,0:T(8,128)(2,1)S(1)}, bf16[3,128,256]{2,1,0:T(8,128)(2,1)S(1)}, u32[]{:S(2)}, u32[]{:S(2)}) collective-permute-start(bf16[3,128,256]{2,1,0:T(8,128)(2,1)S(1)} %slice_bitcast_fusion.11), channel_id=1, source_target_pairs={{0,4},{1,5},{2,6},{3,7},{4,12},{5,13},{6,14},{7,15},{8,0},{9,1},{1... | collective-permute-start | bytes 589832 | tf_op jit(solution)/shard_map/ppermute | solution.py:437
  170.1 3.3 %pad_maximum_fusion.refs_5_.refs_10_.refs_15_ = bf16[4,2,2,2,256,256]{5,4,3,2,1,0:T(8,128)(2,1)} fusion(bf16[1,2,2,2,256,256]{5,4,3,2,1,0:T(8,128)(2,1)S(1)} %bitcast.92, bf16[1,2,2,2,256,256]{5,4,3,2,1,0:T(8,128)(2,1)} %bitcast.21, bf16[1,2,2,2,256,256]{5,4,3,2,1,0:T(8,128)(2,1)S(1)} %bitcast.91, bf16[1,2,2,2,256,256]{5,4,3,2,1,0:T(8,128)(2,1)S(1)} %copy-done.6), kind=kLoop, calls=%fused_computation | loop fusion | flops 6291456 | bytes 8388608 | tf_op jit(solution)/shard_map/stack | solution.py:544
  173.5 12.0 %unit_work.4 = (bf16[8,2,256,256]{3,2,1,0:T(8,128)(2,1)}, f32[1,512]{1,0:T(1,128)S(1)}) custom-call(s32[8,11]{1,0:T(8,128)S(1)} %dynamic-slice_bitcast_fusion.2.tab_ref, s32[1]{0:T(128)} %bitcast.10.place_ref, bf16[2,8,128,256]{3,2,1,0:T(8,128)(2,1)} %get-tuple-element.30.refs_0_, bf16[2,8,128,256]{3,2,1,0:T(8,128)(2,1)S(1)} %collective-permute-done.9.refs_1_, ...), custom_call_target="tpu_custom_call" | custom-call | flops 4294967296 | bytes 33554432 | tf_op jit(solution)/shard_map/unit_work/pallas_call | solution.py:294
  185.5 2.9 %collective-permute-start.27 = (bf16[2,1,128,256]{3,2,1,0:T(8,128)(2,1)S(1)}, bf16[2,1,128,256]{3,2,1,0:T(8,128)(2,1)S(1)}, u32[]{:S(2)}, u32[]{:S(2)}) collective-permute-start(bf16[2,1,128,256]{3,2,1,0:T(8,128)(2,1)S(1)} %get-tuple-element.45.refs_10_), channel_id=1, source_target_pairs={{0,4},{1,5},{2,6},{3,7},{4,12},{5,13},{6,14},{7,15},{8,0},{9,1},{1... | collective-permute-start | bytes 393224 | tf_op jit(solution)/shard_map/ppermute | solution.py:437
  188.4 1.5 fusion.6
  190.2 6.1 %unit_work.5 = (bf16[5,2,256,256]{3,2,1,0:T(8,128)(2,1)S(1)}, bf16[5,2,256,256]{3,2,1,0:T(8,128)(2,1)S(1)}, f32[1,512]{1,0:T(1,128)S(1)}) custom-call(s32[4,11]{1,0:T(4,128)S(1)} %fusion.1.tab_ref, s32[1]{0:T(128)} %bitcast.10.place_ref, bf16[2,4,128,256]{3,2,1,0:T(8,128)(2,1)S(1)} %get-tuple-element.35.refs_0_, ...), custom_call_target="tpu_custom_call" | custom-call | flops 2147483648 | bytes 16777216 | tf_op jit(solution)/shard_map/unit_work/pallas_call | solution.py:294
  197.4 2.4 collective-permute-start.29
  200.4 6.5 %unit_work.6 = (bf16[5,2,256,256]{3,2,1,0:T(8,128)(2,1)S(1)}, bf16[5,2,256,256]{3,2,1,0:T(8,128)(2,1)}, f32[1,512]{1,0:T(1,128)S(1)}) custom-call(s32[5,11]{1,0:T(8,128)S(1)} %dynamic-slice_bitcast_fusion.1.tab_ref, s32[1]{0:T(128)} %bitcast.10.place_ref, ...), custom_call_target="tpu_custom_call", output_to_operand_aliasing={{0}: (16, {}), {1}: (17, {})} | custom-call | flops 2684354560 | bytes 20971520 | tf_op jit(solution)/shard_map/unit_work/pallas_call | solution.py:294
  207.0 1.3 copy-done.1
  208.3 3.1 %unit_work.7 = (bf16[5,2,256,256]{3,2,1,0:T(8,128)(2,1)S(1)}, f32[1,512]{1,0:T(1,128)S(1)}) custom-call(s32[3,11]{1,0:T(4,128)S(1)} %pad_add_fusion.1.tab_ref, s32[1]{0:T(128)} %bitcast.10.place_ref, bf16[2,4,128,256]{3,2,1,0:T(8,128)(2,1)S(1)} %get-tuple-element.35.refs_0_, ...), custom_call_target="tpu_custom_call", output_to_operand_aliasing={{0}: (21, {})} | custom-call | flops 1610612736 | bytes 12582912 | tf_op jit(solution)/shard_map/unit_work/pallas_call | solution.py:294
  212.0 5.5 %collective-permute-start.41 = (f32[2,128]{1,0:T(2,128)S(1)}, f32[2,128]{1,0:T(2,128)S(1)}, u32[]{:S(2)}, u32[]{:S(2)}) collective-permute-start(f32[2,128]{1,0:T(2,128)S(1)} %get-tuple-element.79), channel_id=1, source_target_pairs={{0,8},{1,9},{2,10},{3,11},{4,0},{5,1},{6,2},{7,3},{8,12},{9,13},{1... | collective-permute-start | bytes 3080 | tf_op jit(solution)/shard_map/ppermute | solution.py:437
  217.6 6.1 %collective-permute-start.40 = (f32[2,128]{1,0:T(2,128)S(1)}, f32[2,128]{1,0:T(2,128)S(1)}, u32[]{:S(2)}, u32[]{:S(2)}) collective-permute-start(f32[2,128]{1,0:T(2,128)S(1)} %get-tuple-element.77), channel_id=1, source_target_pairs={{0,12},{1,13},{2,14},{3,15},{4,8},{5,9},{6,10},{7,11},{8,4},{9,5},... | collective-permute-start | bytes 3080 | tf_op jit(solution)/shard_map/ppermute | solution.py:437
  223.9 1.4 collective-permute-done.40
  225.6 1.5 collective-permute-start.45
  227.2 1.6 collective-permute-start.44
  228.8 10.7 %collective-permute-done.45 = f32[2,32]{1,0:T(2,128)S(1)} collective-permute-done((f32[2,32]{1,0:T(2,128)S(1)}, f32[2,32]{1,0:T(2,128)S(1)}, u32[]{:S(2)}, u32[]{:S(2)}) %collective-permute-start.45) | collective-permute-done | bytes 288 | tf_op jit(solution)/shard_map/ppermute | solution.py:437
  243.8 3.7 %put_residuals.3.refs_4_ = bf16[2,8,2,256,256]{4,3,2,1,0:T(8,128)(2,1)} custom-call(s32[8,2]{1,0:T(8,128)S(1)} %stack.211.tab_ref, bf16[8,2,256,256]{3,2,1,0:T(8,128)(2,1)S(1)} %copy-done.3, bf16[2,2,256,256]{3,2,1,0:T(8,128)(2,1)S(1)} %collective-permute-done.37.refs_1_, bf16[2,2,256,256]{3,2,1,0:T(8,128)(2,1)S(1)} %collective-permute-done.38.refs_2_, ...), custom_call_target="tpu_custom_call" | custom-call | tf_op jit(solution)/shard_map/put_residuals/pallas_call | solution.py:335
  248.7 4.1 %collective-permute-done.36.refs_3_ = bf16[2,256,256]{2,1,0:T(8,128)(2,1)S(1)} collective-permute-done((bf16[2,256,256]{2,1,0:T(8,128)(2,1)S(1)}, bf16[2,256,256]{2,1,0:T(8,128)(2,1)S(1)}, u32[]{:S(2)}, u32[]{:S(2)}) %collective-permute-start.36) | collective-permute-done | bytes 262176 | tf_op jit(solution)/shard_map/ppermute | solution.py:437
  252.8 2.1 put_residuals.4.refs_4_
  255.0 5.0 %collective-permute-done.32.refs_2_ = bf16[2,256,256]{2,1,0:T(8,128)(2,1)S(1)} collective-permute-done((bf16[2,256,256]{2,1,0:T(8,128)(2,1)S(1)}, bf16[2,256,256]{2,1,0:T(8,128)(2,1)S(1)}, u32[]{:S(2)}, u32[]{:S(2)}) %collective-permute-start.32) | collective-permute-done | bytes 262176 | tf_op jit(solution)/shard_map/ppermute | solution.py:437
  259.9 3.9 %collective-permute-done.33.refs_3_ = bf16[2,256,256]{2,1,0:T(8,128)(2,1)S(1)} collective-permute-done((bf16[2,256,256]{2,1,0:T(8,128)(2,1)S(1)}, bf16[2,256,256]{2,1,0:T(8,128)(2,1)S(1)}, u32[]{:S(2)}, u32[]{:S(2)}) %collective-permute-start.33) | collective-permute-done | bytes 262176 | tf_op jit(solution)/shard_map/ppermute | solution.py:437
  263.8 2.1 put_residuals.5
  (133 shorter events, 29.3 us)
Async XLA Ops:
  2.9 13.4 %collective-permute-start.3 = (f32[4,256]{1,0:T(4,128)S(1)}, f32[4,256]{1,0:T(4,128)S(1)}, u32[]{:S(2)}, u32[]{:S(2)}) collective-permute-start(f32[4,256]{1,0:T(4,128)S(1)} %pad_maximum_fusion.1.refs_4_), channel_id=1, source_target_pairs={{0,1},{1,0},{2,3},{3,2},{4,5},{5,4},{6,7},{7,6},{8,9},{9,8},{10,11... | collective-permute-start | bytes 12296 | tf_op jit(solution)/shard_map/ppermute | solution.py:437
  3.4 15.0 %collective-permute-start.4 = (f32[4,256]{1,0:T(4,128)S(1)}, f32[4,256]{1,0:T(4,128)S(1)}, u32[]{:S(2)}, u32[]{:S(2)}) collective-permute-start(f32[4,256]{1,0:T(4,128)S(1)} %pad_maximum_fusion.1.refs_4_), channel_id=1, source_target_pairs={{0,2},{1,3},{2,0},{3,1},{4,6},{5,7},{6,4},{7,5},{8,10},{9,11},{10,... | collective-permute-start | bytes 12296 | tf_op jit(solution)/shard_map/ppermute | solution.py:437
  8.4 14.1 %collective-permute-start = (bf16[1,2,32,2048]{3,2,1,0:T(8,128)(2,1)}, bf16[1,2,32,2048]{3,2,1,0:T(8,128)(2,1)S(1)}, u32[]{:S(2)}, u32[]{:S(2)}) collective-permute-start(bf16[1,2,32,2048]{3,2,1,0:T(8,128)(2,1)} %get-tuple-element.69), channel_id=1, source_target_pairs={{0,1},{1,0},{2,3},{3,2},{4,5},{5,4},{6,7},{7,6},{8,9},{9,8},{10,11... | collective-permute-start | bytes 786440 | tf_op jit(solution)/shard_map/ppermute | solution.py:437
  8.5 13.9 %collective-permute-start.1 = (bf16[1,2,32,2048]{3,2,1,0:T(8,128)(2,1)}, bf16[1,2,32,2048]{3,2,1,0:T(8,128)(2,1)S(1)}, u32[]{:S(2)}, u32[]{:S(2)}) collective-permute-start(bf16[1,2,32,2048]{3,2,1,0:T(8,128)(2,1)} %get-tuple-element.68), channel_id=1, source_target_pairs={{0,2},{1,3},{2,0},{3,1},{4,6},{5,7},{6,4},{7,5},{8,10},{9,11},{10,... | collective-permute-start | bytes 786440 | tf_op jit(solution)/shard_map/ppermute | solution.py:437
  8.8 13.6 %collective-permute-start.2 = (bf16[1,2,32,2048]{3,2,1,0:T(8,128)(2,1)}, bf16[1,2,32,2048]{3,2,1,0:T(8,128)(2,1)S(1)}, u32[]{:S(2)}, u32[]{:S(2)}) collective-permute-start(bf16[1,2,32,2048]{3,2,1,0:T(8,128)(2,1)} %get-tuple-element.67), channel_id=1, source_target_pairs={{0,3},{1,2},{2,1},{3,0},{4,7},{5,6},{6,5},{7,4},{8,11},{9,10},{10,... | collective-permute-start | bytes 786440 | tf_op jit(solution)/shard_map/ppermute | solution.py:437
  16.3 6.1 %collective-permute-start.5 = (f32[4,256]{1,0:T(4,128)S(1)}, f32[4,256]{1,0:T(4,128)S(1)}, u32[]{:S(2)}, u32[]{:S(2)}) collective-permute-start(f32[4,256]{1,0:T(4,128)S(1)} %pad_maximum_fusion.1.refs_4_), channel_id=1, source_target_pairs={{0,3},{1,2},{2,1},{3,0},{4,7},{5,6},{6,5},{7,4},{8,11},{9,10},{10,... | collective-permute-start | bytes 12296 | tf_op jit(solution)/shard_map/ppermute | solution.py:437
  25.4 8.1 %collective-permute-start.8 = (bf16[1,2,32,2048]{3,2,1,0:T(8,128)(2,1)S(1)}, bf16[1,2,32,2048]{3,2,1,0:T(8,128)(2,1)S(1)}, u32[]{:S(2)}, u32[]{:S(2)}) collective-permute-start(bf16[1,2,32,2048]{3,2,1,0:T(8,128)(2,1)S(1)} %get-tuple-element.33), channel_id=1, source_target_pairs={{0,3},{1,2},{2,1},{3,0},{4,7},{5,6},{6,5},{7,4},{8,11},{9,10},{10,... | collective-permute-start | bytes 786440 | tf_op jit(solution)/shard_map/ppermute | solution.py:437
  34.2 5.4 %collective-permute-start.21 = (bf16[2,2,2,256,256]{4,3,2,1,0:T(8,128)(2,1)S(1)}, bf16[2,2,2,256,256]{4,3,2,1,0:T(8,128)(2,1)S(1)}, u32[]{:S(2)}, u32[]{:S(2)}) collective-permute-start(bf16[2,2,2,256,256]{4,3,2,1,0:T(8,128)(2,1)S(1)} %get-tuple-element.39), channel_id=1, source_target_pairs={{0,1},{1,0},{2,3},{3,2},{4,5},{5,4},{6,7},{7,6},{8,9},{9,8},{10,11... | collective-permute-start | bytes 3145736 | tf_op jit(solution)/shard_map/ppermute | solution.py:437
  35.9 62.8 %collective-permute-start.9 = (bf16[2,8,128,256]{3,2,1,0:T(8,128)(2,1)}, bf16[2,8,128,256]{3,2,1,0:T(8,128)(2,1)S(1)}, u32[]{:S(2)}, u32[]{:S(2)}) collective-permute-start(bf16[2,8,128,256]{3,2,1,0:T(8,128)(2,1)} %get-tuple-element.30.refs_0_), channel_id=1, source_target_pairs={{0,4},{1,5},{2,6},{3,7},{4,12},{5,13},{6,14},{7,15},{8,0},{9,1},{1... | collective-permute-start | bytes 3145736 | tf_op jit(solution)/shard_map/ppermute | solution.py:437
  37.6 61.2 %collective-permute-start.10 = (bf16[2,8,128,256]{3,2,1,0:T(8,128)(2,1)}, bf16[2,8,128,256]{3,2,1,0:T(8,128)(2,1)}, u32[]{:S(2)}, u32[]{:S(2)}) collective-permute-start(bf16[2,8,128,256]{3,2,1,0:T(8,128)(2,1)} %get-tuple-element.30.refs_0_), channel_id=1, source_target_pairs={{0,8},{1,9},{2,10},{3,11},{4,0},{5,1},{6,2},{7,3},{8,12},{9,13},{1... | collective-permute-start | bytes 3145736 | tf_op jit(solution)/shard_map/ppermute | solution.py:437
  39.6 65.3 %collective-permute-start.22 = (bf16[2,2,2,256,256]{4,3,2,1,0:T(8,128)(2,1)}, bf16[2,2,2,256,256]{4,3,2,1,0:T(8,128)(2,1)}, u32[]{:S(2)}, u32[]{:S(2)}) collective-permute-start(bf16[2,2,2,256,256]{4,3,2,1,0:T(8,128)(2,1)} %get-tuple-element.40), channel_id=1, source_target_pairs={{0,2},{1,3},{2,0},{3,1},{4,6},{5,7},{6,4},{7,5},{8,10},{9,11},{10,... | collective-permute-start | bytes 3145736 | tf_op jit(solution)/shard_map/ppermute | solution.py:437
  41.9 41.4 %collective-permute-start.24 = (f32[8,128]{1,0:T(8,128)S(1)}, f32[8,128]{1,0:T(8,128)S(1)}, u32[]{:S(2)}, u32[]{:S(2)}) collective-permute-start(f32[8,128]{1,0:T(8,128)S(1)} %get-tuple-element.42), channel_id=1, source_target_pairs={{0,4},{1,5},{2,6},{3,7},{4,12},{5,13},{6,14},{7,15},{8,0},{9,1},{1... | collective-permute-start | bytes 12296 | tf_op jit(solution)/shard_map/ppermute | solution.py:437
  44.6 41.2 %collective-permute-start.25 = (f32[8,128]{1,0:T(8,128)S(1)}, f32[8,128]{1,0:T(8,128)S(1)}, u32[]{:S(2)}, u32[]{:S(2)}) collective-permute-start(f32[8,128]{1,0:T(8,128)S(1)} %get-tuple-element.42), channel_id=1, source_target_pairs={{0,8},{1,9},{2,10},{3,11},{4,0},{5,1},{6,2},{7,3},{8,12},{9,13},{1... | collective-permute-start | bytes 12296 | tf_op jit(solution)/shard_map/ppermute | solution.py:437
  83.3 3.0 %collective-permute-start.6 = (bf16[1,2,32,2048]{3,2,1,0:T(8,128)(2,1)}, bf16[1,2,32,2048]{3,2,1,0:T(8,128)(2,1)}, u32[]{:S(2)}, u32[]{:S(2)}) collective-permute-start(bf16[1,2,32,2048]{3,2,1,0:T(8,128)(2,1)} %get-tuple-element.31), channel_id=1, source_target_pairs={{0,1},{1,0},{2,3},{3,2},{4,5},{5,4},{6,7},{7,6},{8,9},{9,8},{10,11... | collective-permute-start | bytes 786440 | tf_op jit(solution)/shard_map/ppermute | solution.py:437
  85.8 9.0 %collective-permute-start.7 = (bf16[1,2,32,2048]{3,2,1,0:T(8,128)(2,1)}, bf16[1,2,32,2048]{3,2,1,0:T(8,128)(2,1)S(1)}, u32[]{:S(2)}, u32[]{:S(2)}) collective-permute-start(bf16[1,2,32,2048]{3,2,1,0:T(8,128)(2,1)} %get-tuple-element.32), channel_id=1, source_target_pairs={{0,2},{1,3},{2,0},{3,1},{4,6},{5,7},{6,4},{7,5},{8,10},{9,11},{10,... | collective-permute-start | bytes 786440 | tf_op jit(solution)/shard_map/ppermute | solution.py:437
  86.3 16.0 %collective-permute-start.26 = (f32[8,128]{1,0:T(8,128)S(1)}, f32[8,128]{1,0:T(8,128)S(1)}, u32[]{:S(2)}, u32[]{:S(2)}) collective-permute-start(f32[8,128]{1,0:T(8,128)S(1)} %get-tuple-element.42), channel_id=1, source_target_pairs={{0,12},{1,13},{2,14},{3,15},{4,8},{5,9},{6,10},{7,11},{8,4},{9,5},... | collective-permute-start | bytes 12296 | tf_op jit(solution)/shard_map/ppermute | solution.py:437
  95.7 74.4 %copy-start.6 = (bf16[1,2,2,2,256,256]{5,4,3,2,1,0:T(8,128)(2,1)S(1)}, bf16[1,2,2,2,256,256]{5,4,3,2,1,0:T(8,128)(2,1)}, u32[]{:S(2)}) copy-start(bf16[1,2,2,2,256,256]{5,4,3,2,1,0:T(8,128)(2,1)} %get-tuple-element.58) | copy-start | bytes 3145732
  95.7 74.4 %copy-start.9 = (bf16[2,2,2,256,256]{4,3,2,1,0:T(8,128)(2,1)S(1)}, bf16[2,2,2,256,256]{4,3,2,1,0:T(8,128)(2,1)}, u32[]{:S(2)}) copy-start(bf16[2,2,2,256,256]{4,3,2,1,0:T(8,128)(2,1)} %copy-done.8) | copy-start | bytes 3145732
  98.8 16.3 %collective-permute-start.11 = (bf16[2,4,128,256]{3,2,1,0:T(8,128)(2,1)S(1)}, bf16[2,4,128,256]{3,2,1,0:T(8,128)(2,1)S(1)}, u32[]{:S(2)}, u32[]{:S(2)}) collective-permute-start(bf16[2,4,128,256]{3,2,1,0:T(8,128)(2,1)S(1)} %get-tuple-element.35.refs_0_), channel_id=1, source_target_pairs={{0,4},{1,5},{2,6},{3,7},{4,12},{5,13},{6,14},{7,15},{8,0},{9,1},{1... | collective-permute-start | bytes 1572872 | tf_op jit(solution)/shard_map/ppermute | solution.py:437
  101.5 26.9 %collective-permute-start.12 = (bf16[2,4,128,256]{3,2,1,0:T(8,128)(2,1)S(1)}, bf16[2,4,128,256]{3,2,1,0:T(8,128)(2,1)S(1)}, u32[]{:S(2)}, u32[]{:S(2)}) collective-permute-start(bf16[2,4,128,256]{3,2,1,0:T(8,128)(2,1)S(1)} %get-tuple-element.35.refs_0_), channel_id=1, source_target_pairs={{0,8},{1,9},{2,10},{3,11},{4,0},{5,1},{6,2},{7,3},{8,12},{9,13},{1... | collective-permute-start | bytes 1572872 | tf_op jit(solution)/shard_map/ppermute | solution.py:437
  102.3 71.1 %collective-permute-start.19 = (bf16[8,128,256]{2,1,0:T(8,128)(2,1)S(1)}, bf16[8,128,256]{2,1,0:T(8,128)(2,1)S(1)}, u32[]{:S(2)}, u32[]{:S(2)}) collective-permute-start(bf16[8,128,256]{2,1,0:T(8,128)(2,1)S(1)} %slice_bitcast_fusion.1), channel_id=1, source_target_pairs={{0,4},{1,5},{2,6},{3,7},{4,12},{5,13},{6,14},{7,15},{8,0},{9,1},{1... | collective-permute-start | bytes 1572872 | tf_op jit(solution)/shard_map/ppermute | solution.py:437
  104.9 61.8 %collective-permute-start.23 = (bf16[2,2,2,256,256]{4,3,2,1,0:T(8,128)(2,1)S(1)}, bf16[2,2,2,256,256]{4,3,2,1,0:T(8,128)(2,1)S(1)}, u32[]{:S(2)}, u32[]{:S(2)}) collective-permute-start(bf16[2,2,2,256,256]{4,3,2,1,0:T(8,128)(2,1)S(1)} %copy-done.7), channel_id=1, source_target_pairs={{0,3},{1,2},{2,1},{3,0},{4,7},{5,6},{6,5},{7,4},{8,11},{9,10},{10,... | collective-permute-start | bytes 3145736 | tf_op jit(solution)/shard_map/ppermute | solution.py:437
  106.0 67.5 %collective-permute-start.20 = (bf16[8,128,256]{2,1,0:T(8,128)(2,1)S(1)}, bf16[8,128,256]{2,1,0:T(8,128)(2,1)S(1)}, u32[]{:S(2)}, u32[]{:S(2)}) collective-permute-start(bf16[8,128,256]{2,1,0:T(8,128)(2,1)S(1)} %slice_bitcast_fusion), channel_id=1, source_target_pairs={{0,8},{1,9},{2,10},{3,11},{4,0},{5,1},{6,2},{7,3},{8,12},{9,13},{1... | collective-permute-start | bytes 1572872 | tf_op jit(solution)/shard_map/ppermute | solution.py:437
  128.3 28.0 %collective-permute-start.15 = (bf16[2,3,128,256]{3,2,1,0:T(8,128)(2,1)S(1)}, bf16[2,3,128,256]{3,2,1,0:T(8,128)(2,1)S(1)}, u32[]{:S(2)}, u32[]{:S(2)}) collective-permute-start(bf16[2,3,128,256]{3,2,1,0:T(8,128)(2,1)S(1)} %get-tuple-element.37.refs_5_), channel_id=1, source_target_pairs={{0,4},{1,5},{2,6},{3,7},{4,12},{5,13},{6,14},{7,15},{8,0},{9,1},{1... | collective-permute-start | bytes 1179656 | tf_op jit(solution)/shard_map/ppermute | solution.py:437
  128.8 37.7 %collective-permute-start.16 = (bf16[2,3,128,256]{3,2,1,0:T(8,128)(2,1)S(1)}, bf16[2,3,128,256]{3,2,1,0:T(8,128)(2,1)S(1)}, u32[]{:S(2)}, u32[]{:S(2)}) collective-permute-start(bf16[2,3,128,256]{3,2,1,0:T(8,128)(2,1)S(1)} %get-tuple-element.37.refs_5_), channel_id=1, source_target_pairs={{0,8},{1,9},{2,10},{3,11},{4,0},{5,1},{6,2},{7,3},{8,12},{9,13},{1... | collective-permute-start | bytes 1179656 | tf_op jit(solution)/shard_map/ppermute | solution.py:437
  156.4 33.5 %collective-permute-start.13 = (bf16[4,128,256]{2,1,0:T(8,128)(2,1)S(1)}, bf16[4,128,256]{2,1,0:T(8,128)(2,1)S(1)}, u32[]{:S(2)}, u32[]{:S(2)}) collective-permute-start(bf16[4,128,256]{2,1,0:T(8,128)(2,1)S(1)} %slice_bitcast_fusion.3), channel_id=1, source_target_pairs={{0,4},{1,5},{2,6},{3,7},{4,12},{5,13},{6,14},{7,15},{8,0},{9,1},{1... | collective-permute-start | bytes 786440 | tf_op jit(solution)/shard_map/ppermute | solution.py:437
  166.6 23.5 %collective-permute-start.14 = (bf16[4,128,256]{2,1,0:T(8,128)(2,1)S(1)}, bf16[4,128,256]{2,1,0:T(8,128)(2,1)S(1)}, u32[]{:S(2)}, u32[]{:S(2)}) collective-permute-start(bf16[4,128,256]{2,1,0:T(8,128)(2,1)S(1)} %slice_bitcast_fusion.2), channel_id=1, source_target_pairs={{0,8},{1,9},{2,10},{3,11},{4,0},{5,1},{6,2},{7,3},{8,12},{9,13},{1... | collective-permute-start | bytes 786440 | tf_op jit(solution)/shard_map/ppermute | solution.py:437
  166.7 33.7 %collective-permute-start.17 = (bf16[3,128,256]{2,1,0:T(8,128)(2,1)S(1)}, bf16[3,128,256]{2,1,0:T(8,128)(2,1)S(1)}, u32[]{:S(2)}, u32[]{:S(2)}) collective-permute-start(bf16[3,128,256]{2,1,0:T(8,128)(2,1)S(1)} %slice_bitcast_fusion.11), channel_id=1, source_target_pairs={{0,4},{1,5},{2,6},{3,7},{4,12},{5,13},{6,14},{7,15},{8,0},{9,1},{1... | collective-permute-start | bytes 589832 | tf_op jit(solution)/shard_map/ppermute | solution.py:437
  173.4 27.0 %collective-permute-start.18 = (bf16[3,128,256]{2,1,0:T(8,128)(2,1)S(1)}, bf16[3,128,256]{2,1,0:T(8,128)(2,1)S(1)}, u32[]{:S(2)}, u32[]{:S(2)}) collective-permute-start(bf16[3,128,256]{2,1,0:T(8,128)(2,1)S(1)} %slice_bitcast_fusion.10), channel_id=1, source_target_pairs={{0,8},{1,9},{2,10},{3,11},{4,0},{5,1},{6,2},{7,3},{8,12},{9,13},{1... | collective-permute-start | bytes 589832 | tf_op jit(solution)/shard_map/ppermute | solution.py:437
  185.5 11.9 %collective-permute-start.27 = (bf16[2,1,128,256]{3,2,1,0:T(8,128)(2,1)S(1)}, bf16[2,1,128,256]{3,2,1,0:T(8,128)(2,1)S(1)}, u32[]{:S(2)}, u32[]{:S(2)}) collective-permute-start(bf16[2,1,128,256]{3,2,1,0:T(8,128)(2,1)S(1)} %get-tuple-element.45.refs_10_), channel_id=1, source_target_pairs={{0,4},{1,5},{2,6},{3,7},{4,12},{5,13},{6,14},{7,15},{8,0},{9,1},{1... | collective-permute-start | bytes 393224 | tf_op jit(solution)/shard_map/ppermute | solution.py:437
  189.9 9.9 %collective-permute-start.28 = (bf16[2,1,128,256]{3,2,1,0:T(8,128)(2,1)S(1)}, bf16[2,1,128,256]{3,2,1,0:T(8,128)(2,1)S(1)}, u32[]{:S(2)}, u32[]{:S(2)}) collective-permute-start(bf16[2,1,128,256]{3,2,1,0:T(8,128)(2,1)S(1)} %get-tuple-element.45.refs_10_), channel_id=1, source_target_pairs={{0,8},{1,9},{2,10},{3,11},{4,0},{5,1},{6,2},{7,3},{8,12},{9,13},{1... | collective-permute-start | bytes 393224 | tf_op jit(solution)/shard_map/ppermute | solution.py:437
  190.1 21.3 %collective-permute-start.37 = (bf16[2,2,256,256]{3,2,1,0:T(8,128)(2,1)S(1)}, bf16[2,2,256,256]{3,2,1,0:T(8,128)(2,1)S(1)}, u32[]{:S(2)}, u32[]{:S(2)}) collective-permute-start(bf16[2,2,256,256]{3,2,1,0:T(8,128)(2,1)S(1)} %get-tuple-element.52), channel_id=1, source_target_pairs={{0,1},{1,0},{2,3},{3,2},{4,5},{5,4},{6,7},{7,6},{8,9},{9,8},{10,11... | collective-permute-start | bytes 1572872 | tf_op jit(solution)/shard_map/ppermute | solution.py:437
  197.4 9.6 %collective-permute-start.29 = (bf16[1,128,256]{2,1,0:T(8,128)(2,1)S(1)}, bf16[1,128,256]{2,1,0:T(8,128)(2,1)S(1)}, u32[]{:S(2)}, u32[]{:S(2)}) collective-permute-start(bf16[1,128,256]{2,1,0:T(8,128)(2,1)S(1)} %slice_bitcast_fusion.13), channel_id=1, source_target_pairs={{0,4},{1,5},{2,6},{3,7},{4,12},{5,13},{6,14},{7,15},{8,0},{9,1},{1... | collective-permute-start | bytes 196616 | tf_op jit(solution)/shard_map/ppermute | solution.py:437
  199.8 7.2 %collective-permute-start.30 = (bf16[1,128,256]{2,1,0:T(8,128)(2,1)S(1)}, bf16[1,128,256]{2,1,0:T(8,128)(2,1)S(1)}, u32[]{:S(2)}, u32[]{:S(2)}) collective-permute-start(bf16[1,128,256]{2,1,0:T(8,128)(2,1)S(1)} %slice_bitcast_fusion.12), channel_id=1, source_target_pairs={{0,8},{1,9},{2,10},{3,11},{4,0},{5,1},{6,2},{7,3},{8,12},{9,13},{1... | collective-permute-start | bytes 196616 | tf_op jit(solution)/shard_map/ppermute | solution.py:437
  211.4 13.9 %collective-permute-start.38 = (bf16[2,2,256,256]{3,2,1,0:T(8,128)(2,1)S(1)}, bf16[2,2,256,256]{3,2,1,0:T(8,128)(2,1)S(1)}, u32[]{:S(2)}, u32[]{:S(2)}) collective-permute-start(bf16[2,2,256,256]{3,2,1,0:T(8,128)(2,1)S(1)} %get-tuple-element.53), channel_id=1, source_target_pairs={{0,2},{1,3},{2,0},{3,1},{4,6},{5,7},{6,4},{7,5},{8,10},{9,11},{10,... | collective-permute-start | bytes 1572872 | tf_op jit(solution)/shard_map/ppermute | solution.py:437
  212.0 11.8 %collective-permute-start.41 = (f32[2,128]{1,0:T(2,128)S(1)}, f32[2,128]{1,0:T(2,128)S(1)}, u32[]{:S(2)}, u32[]{:S(2)}) collective-permute-start(f32[2,128]{1,0:T(2,128)S(1)} %get-tuple-element.79), channel_id=1, source_target_pairs={{0,8},{1,9},{2,10},{3,11},{4,0},{5,1},{6,2},{7,3},{8,12},{9,13},{1... | collective-permute-start | bytes 3080 | tf_op jit(solution)/shard_map/ppermute | solution.py:437
  217.5 6.4 %collective-permute-start.42 = (f32[2,128]{1,0:T(2,128)S(1)}, f32[2,128]{1,0:T(2,128)S(1)}, u32[]{:S(2)}, u32[]{:S(2)}) collective-permute-start(f32[2,128]{1,0:T(2,128)S(1)} %get-tuple-element.78), channel_id=1, source_target_pairs={{0,4},{1,5},{2,6},{3,7},{4,12},{5,13},{6,14},{7,15},{8,0},{9,1},{1... | collective-permute-start | bytes 3080 | tf_op jit(solution)/shard_map/ppermute | solution.py:437
  217.6 7.7 %collective-permute-start.40 = (f32[2,128]{1,0:T(2,128)S(1)}, f32[2,128]{1,0:T(2,128)S(1)}, u32[]{:S(2)}, u32[]{:S(2)}) collective-permute-start(f32[2,128]{1,0:T(2,128)S(1)} %get-tuple-element.77), channel_id=1, source_target_pairs={{0,12},{1,13},{2,14},{3,15},{4,8},{5,9},{6,10},{7,11},{8,4},{9,5},... | collective-permute-start | bytes 3080 | tf_op jit(solution)/shard_map/ppermute | solution.py:437
  223.8 17.9 %collective-permute-start.34 = (bf16[2,256,256]{2,1,0:T(8,128)(2,1)S(1)}, bf16[2,256,256]{2,1,0:T(8,128)(2,1)S(1)}, u32[]{:S(2)}, u32[]{:S(2)}) collective-permute-start(bf16[2,256,256]{2,1,0:T(8,128)(2,1)S(1)} %get-tuple-element.73), channel_id=1, source_target_pairs={{0,1},{1,0},{2,3},{3,2},{4,5},{5,4},{6,7},{7,6},{8,9},{9,8},{10,11... | collective-permute-start | bytes 786440 | tf_op jit(solution)/shard_map/ppermute | solution.py:437
  225.3 17.4 %collective-permute-start.39 = (bf16[2,2,256,256]{3,2,1,0:T(8,128)(2,1)S(1)}, bf16[2,2,256,256]{3,2,1,0:T(8,128)(2,1)S(1)}, u32[]{:S(2)}, u32[]{:S(2)}) collective-permute-start(bf16[2,2,256,256]{3,2,1,0:T(8,128)(2,1)S(1)} %get-tuple-element.54), channel_id=1, source_target_pairs={{0,3},{1,2},{2,1},{3,0},{4,7},{5,6},{6,5},{7,4},{8,11},{9,10},{10,... | collective-permute-start | bytes 1572872 | tf_op jit(solution)/shard_map/ppermute | solution.py:437
  225.6 13.9 %collective-permute-start.45 = (f32[2,32]{1,0:T(2,128)S(1)}, f32[2,32]{1,0:T(2,128)S(1)}, u32[]{:S(2)}, u32[]{:S(2)}) collective-permute-start(f32[2,32]{1,0:T(2,128)S(1)} %get-tuple-element.81), channel_id=1, source_target_pairs={{0,3},{1,2},{2,1},{3,0},{4,7},{5,6},{6,5},{7,4},{8,11},{9,10},{10,... | collective-permute-start | bytes 776 | tf_op jit(solution)/shard_map/ppermute | solution.py:437
  227.2 13.2 %collective-permute-start.44 = (f32[2,32]{1,0:T(2,128)S(1)}, f32[2,32]{1,0:T(2,128)S(1)}, u32[]{:S(2)}, u32[]{:S(2)}) collective-permute-start(f32[2,32]{1,0:T(2,128)S(1)} %get-tuple-element.82), channel_id=1, source_target_pairs={{0,2},{1,3},{2,0},{3,1},{4,6},{5,7},{6,4},{7,5},{8,10},{9,11},{10,... | collective-permute-start | bytes 776 | tf_op jit(solution)/shard_map/ppermute | solution.py:437
  228.8 12.2 %collective-permute-start.43 = (f32[2,32]{1,0:T(2,128)S(1)}, f32[2,32]{1,0:T(2,128)S(1)}, u32[]{:S(2)}, u32[]{:S(2)}) collective-permute-start(f32[2,32]{1,0:T(2,128)S(1)} %get-tuple-element.83), channel_id=1, source_target_pairs={{0,1},{1,0},{2,3},{3,2},{4,5},{5,4},{6,7},{7,6},{8,9},{9,8},{10,11... | collective-permute-start | bytes 776 | tf_op jit(solution)/shard_map/ppermute | solution.py:437
  239.5 9.2 %collective-permute-start.35 = (bf16[2,256,256]{2,1,0:T(8,128)(2,1)S(1)}, bf16[2,256,256]{2,1,0:T(8,128)(2,1)S(1)}, u32[]{:S(2)}, u32[]{:S(2)}) collective-permute-start(bf16[2,256,256]{2,1,0:T(8,128)(2,1)S(1)} %get-tuple-element.72), channel_id=1, source_target_pairs={{0,2},{1,3},{2,0},{3,1},{4,6},{5,7},{6,4},{7,5},{8,10},{9,11},{10,... | collective-permute-start | bytes 786440 | tf_op jit(solution)/shard_map/ppermute | solution.py:437
  240.4 12.4 %collective-permute-start.36 = (bf16[2,256,256]{2,1,0:T(8,128)(2,1)S(1)}, bf16[2,256,256]{2,1,0:T(8,128)(2,1)S(1)}, u32[]{:S(2)}, u32[]{:S(2)}) collective-permute-start(bf16[2,256,256]{2,1,0:T(8,128)(2,1)S(1)} %get-tuple-element.71), channel_id=1, source_target_pairs={{0,3},{1,2},{2,1},{3,0},{4,7},{5,6},{6,5},{7,4},{8,11},{9,10},{10,... | collective-permute-start | bytes 786440 | tf_op jit(solution)/shard_map/ppermute | solution.py:437
  241.0 14.0 %collective-permute-start.31 = (bf16[2,256,256]{2,1,0:T(8,128)(2,1)S(1)}, bf16[2,256,256]{2,1,0:T(8,128)(2,1)S(1)}, u32[]{:S(2)}, u32[]{:S(2)}) collective-permute-start(bf16[2,256,256]{2,1,0:T(8,128)(2,1)S(1)} %get-tuple-element.76), channel_id=1, source_target_pairs={{0,1},{1,0},{2,3},{3,2},{4,5},{5,4},{6,7},{7,6},{8,9},{9,8},{10,11... | collective-permute-start | bytes 786440 | tf_op jit(solution)/shard_map/ppermute | solution.py:437
  241.7 18.2 %collective-permute-start.32 = (bf16[2,256,256]{2,1,0:T(8,128)(2,1)S(1)}, bf16[2,256,256]{2,1,0:T(8,128)(2,1)S(1)}, u32[]{:S(2)}, u32[]{:S(2)}) collective-permute-start(bf16[2,256,256]{2,1,0:T(8,128)(2,1)S(1)} %get-tuple-element.75), channel_id=1, source_target_pairs={{0,2},{1,3},{2,0},{3,1},{4,6},{5,7},{6,4},{7,5},{8,10},{9,11},{10,... | collective-permute-start | bytes 786440 | tf_op jit(solution)/shard_map/ppermute | solution.py:437
  242.7 21.1 %collective-permute-start.33 = (bf16[2,256,256]{2,1,0:T(8,128)(2,1)S(1)}, bf16[2,256,256]{2,1,0:T(8,128)(2,1)S(1)}, u32[]{:S(2)}, u32[]{:S(2)}) collective-permute-start(bf16[2,256,256]{2,1,0:T(8,128)(2,1)S(1)} %get-tuple-element.74), channel_id=1, source_target_pairs={{0,3},{1,2},{2,1},{3,0},{4,7},{5,6},{6,5},{7,4},{8,11},{9,10},{10,... | collective-permute-start | bytes 786440 | tf_op jit(solution)/shard_map/ppermute | solution.py:437
  (10 other events, 160.5 us)

commit v4 on v3

--- a/solution.py
+++ b/solution.py
@@ -42,8 +42,9 @@
     return total
 
 
-def build_kernel(sets, slot_ids, pieces, place_ref, *refs):
-    beams, smalls, refs = refs[:sets], refs[sets : 2 * sets], refs[2 * sets :]
+def build_kernel(sets, small_count, slot_ids, pieces, tab_ref, *refs):
+    beams, smalls, refs = refs[:sets], refs[sets : sets + small_count], refs[sets + small_count :]
+    beams = (None,) * (small_count - sets) + beams
     uvw_ref, outs, bright_ref = refs[0], refs[1 : 1 + len(pieces)], refs[-1]
     per_group = outs[0].shape[2] // sets
     span = outs[0].shape[3]
@@ -54,19 +55,21 @@
     sin_coefs, cos_coefs = turn_polynomials()
     brights = []
     for part, small in enumerate(smalls):
-        group = pl.ds(part * per_group, per_group)
 
         def pick(chosen, row):
             return jnp.sum(jnp.where(chosen, small[row : row + 1, :], 0.0), axis=1, keepdims=True)
 
         def chosen_at(index):
-            listed = pick(lanes == (place_ref[0] + index) * per_group + rows, 3)
+            listed = pick(lanes == (tab_ref[0] + index) * per_group + rows, 3)
             return listed.astype(jnp.int32) == lanes
 
         bright = jnp.zeros((per_group, 128), jnp.float32)
         for index in range(slot_ids[1]):
             bright = jnp.where(bright_lanes == index, pick(chosen_at(index), 2), bright)
         brights.append(bright)
+        if beams[part] is None:
+            continue
+        group = pl.ds((part - small_count + sets) * per_group, per_group)
         chosen = chosen_at(slot_ids[0])
         east = pick(chosen, 0)
         north = pick(chosen, 1)
@@ -94,63 +97,104 @@
     bright_ref[...] = turned[: bright_ref.shape[0], : bright_ref.shape[1]]
 
 
-def build_factors(slot_ids, place, beam, other_beams, antenna_uvw, smalls, pieces, span):
-    _, _, per_group, antennas = beam.shape
-    sets = 1 + len(other_beams)
+def build_factors(slot_ids, table, beam, other_beams, antenna_uvw, smalls, pieces, span):
+    _, _, per_group, antennas = (other_beams or [beam])[0].shape
+    sets = (beam is not None) + len(other_beams)
     index = slot_ids[0]
     whole = pl.BlockSpec(memory_space=pltpu.VMEM)
     shapes = [(2, len(piece), sets * per_group, span) for piece in pieces]
+    own = []
+    if beam is not None:
+        own.append(
+            pl.BlockSpec((1, 2, per_group, antennas), lambda n, tab: (tab[0] + index, 0, 0, 0))
+        )
     return pl.pallas_call(
-        functools.partial(build_kernel, sets, slot_ids, pieces),
+        functools.partial(build_kernel, sets, len(smalls), slot_ids, pieces),
         grid_spec=pltpu.PrefetchScalarGridSpec(
             num_scalar_prefetch=1,
             grid=(1,),
             in_specs=[
-                pl.BlockSpec((1, 2, per_group, antennas), lambda n, at: (at[0] + index, 0, 0, 0)),
-                *[whole] * (len(other_beams) + sets),
-                pl.BlockSpec((1, 3, antennas), lambda n, at: (at[0] + index, 0, 0)),
+                *own,
+                *[whole] * (len(other_beams) + len(smalls)),
+                pl.BlockSpec((1, 3, antennas), lambda n, tab: (tab[0] + index, 0, 0)),
             ],
             out_specs=[whole] * (len(pieces) + 1),
         ),
         out_shape=[jax.ShapeDtypeStruct(shape, jnp.bfloat16) for shape in shapes]
-        + [jax.ShapeDtypeStruct((8, sets * per_group), jnp.float32)],
+        + [jax.ShapeDtypeStruct((8, len(smalls) * per_group), jnp.float32)],
         compiler_params=pltpu.CompilerParams(vmem_limit_bytes=40 * 1024 * 1024),
         name="build_factors",
-    )(place, beam, *other_beams, *smalls, antenna_uvw)
+    )(table, *([beam] if own else []), *other_beams, *smalls, antenna_uvw)
+
+
+def slice_kernel(count, tab_ref, *refs):
+    for source, target in zip(refs[:count], refs[count:]):
+        target[...] = source[...]
+
+
+def slices_for(array, axis, size, starts, table):
+    lead = axis > 0
+    shape = array.shape[:axis] + (size,) + array.shape[axis + 1 :]
+    block = (1,) + shape[1:] if lead else shape
+    rest = (0,) * (array.ndim - axis - 1)
+    return pl.pallas_call(
+        functools.partial(slice_kernel, len(starts)),
+        grid_spec=pltpu.PrefetchScalarGridSpec(
+            num_scalar_prefetch=1,
+            grid=(shape[0] if lead else 1,),
+            in_specs=[
+                pl.BlockSpec(
+                    block,
+                    lambda n, tab, start=start, shift=shift: (
+                        *((n,) if lead else ()),
+                        tab[start] // size + shift,
+                        *rest,
+                    ),
+                )
+                for start, shift in starts
+            ],
+            out_specs=[
+                pl.BlockSpec(block, lambda n, tab: (n,) + (0,) * (array.ndim - 1)) for _ in starts
+            ],
+        ),
+        out_shape=[jax.ShapeDtypeStruct(shape, array.dtype) for _ in starts],
+        name="slices_for",
+    )(table, *[array] * len(starts))
 
 
 KIND, ONE, TWO, ONE_AT, TWO_AT, OUT_ROWS, VIS_AT = 0, 1, 2, 3, 5, 7, 9
 COLUMNS = 11
 
 
-def unit_kernel(index, pieces, outs, aliased, tab_ref, place_ref, *refs):
+def unit_kernel(index, offset, pieces, outs, aliased, tab_ref, *refs):
     arrays = []
-    for both, single in pieces:
-        entries = [(ref.at[0], ref.at[1]) for ref in refs[:both]]
-        if single:
-            entries.append((refs[both], refs[both + 1]))
-        arrays.append(entries)
-        refs = refs[both + 2 * single :]
+    for entries in pieces:
+        found = []
+        for count, start in entries:
+            parts = (refs[0].at[0], refs[0].at[1]) if count == 1 else refs[:2]
+            found.append((parts, start))
+            refs = refs[count:]
+        arrays.append(found)
     vis_ref, keep_one_ref, keep_two_ref, bright_ref = refs[:4]
     refs = refs[4 + aliased :]
     out_refs, grad_ref = refs[:outs], refs[outs]
     total_ref, column_ref, one_ref, two_ref = refs[outs + 1 :]
     step = pl.program_id(0)
-    slot = place_ref[0] + index
+    slot = tab_ref[0] + index
     sources, span = one_ref.shape[1:]
 
+    def entry(column):
+        return tab_ref[offset + step * COLUMNS + column]
+
     def load(target, at):
-        for n, entries in enumerate(arrays):
-
-            @pl.when(tab_ref[step, at] == n)
-            def _(entries=entries):
-                place = tab_ref[step, at + 1]
-                start = 0
-                for entry in entries:
-                    count = entry[0].shape[1]
+        for n, found in enumerate(arrays):
+
+            @pl.when(entry(at) == n)
+            def _(found=found):
+                place = entry(at + 1)
+                for parts, start in found:
                     for part in (0, 1):
-                        target[part, pl.ds(start, count)] = entry[part][place]
-                    start += count
+                        target[part, pl.ds(start, parts[0].shape[1])] = parts[part][place]
 
     def dot(a, b):
         return lax.dot_general(a, b, (((1,), (0,)), ((), ())), preferred_element_type=jnp.float32)
@@ -205,12 +249,12 @@
             row = bright_ref[pl.ds(index, 1), pl.ds(start, 128)]
             column_ref[pl.ds(start, 128)] = jnp.broadcast_to(row, (128, 128)).T
 
-    @pl.when(tab_ref[step, KIND] != 2)
+    @pl.when(entry(KIND) != 2)
     def _():
         load(one_ref, ONE_AT)
         load(two_ref, TWO_AT)
 
-    @pl.when(tab_ref[step, KIND] == 0)
+    @pl.when(entry(KIND) == 0)
     def _():
         one_re, one_im, two_re, two_im = one_ref[0], one_ref[1], two_ref[0], two_ref[1]
         pred_re, pred_im = cross(*scaled_of(one_re, one_im), two_re, two_im)
@@ -221,7 +265,7 @@
         sum_re, sum_im = pull(one_re, one_im, res_re, res_im, 1)
         add_grad(sum_re * two_re.astype(jnp.float32) - sum_im * two_im.astype(jnp.float32))
 
-    @pl.when(tab_ref[step, KIND] == 1)
+    @pl.when(entry(KIND) == 1)
     def _():
         one_re, one_im, two_re, two_im = one_ref[0], one_ref[1], two_ref[0], two_ref[1]
         row_ids = lax.broadcasted_iota(jnp.int32, (span, span), 0)
@@ -255,47 +299,52 @@
         grad_ref[...] = jnp.sum(total_ref[...].T, axis=0, keepdims=True)
 
 
-def unit_work(index, table, place, pieces, vis, keep, bright, outs):
+def unit_work(index, steps, table, pieces, vis, keep, bright, outs):
     span = vis.shape[5]
     slots = keep.shape[0]
-    sources = sum(array.shape[-2] for array in pieces[0][0]) + (
-        pieces[0][1][0].shape[-2] if pieces[0][1] else 0
-    )
+    sources = sum(arrays[0].shape[-2] for arrays, _ in pieces[0])
+    offset, count = steps
     whole = pl.BlockSpec(memory_space=pltpu.VMEM)
-    arrays = [array for both, single in pieces for array in (*both, *single)]
+    arrays = [array for piece in pieces for entry, _ in piece for array in entry]
+
+    def at(tab, step, column):
+        return tab[offset + step * COLUMNS + column]
+
     in_specs = [whole] * len(arrays) + [
         pl.BlockSpec(
             (1, 1, 1, 2, span, span),
-            lambda u, tab, at: (tab[u, VIS_AT], tab[u, VIS_AT + 1], index, 0, 0, 0),
+            lambda u, tab: (at(tab, u, VIS_AT), at(tab, u, VIS_AT + 1), index, 0, 0, 0),
         ),
-        pl.BlockSpec((slots, span), lambda u, tab, at: (0, tab[u, ONE])),
-        pl.BlockSpec((slots, span), lambda u, tab, at: (0, tab[u, TWO])),
+        pl.BlockSpec((slots, span), lambda u, tab: (0, at(tab, u, ONE))),
+        pl.BlockSpec((slots, span), lambda u, tab: (0, at(tab, u, TWO))),
         whole,
     ]
-    operands = [table, place, *arrays, vis, keep, keep, bright]
+    operands = [table, *arrays, vis, keep, keep, bright]
     aliases = {}
     out_specs, out_shapes = [], []
-    for n, out in enumerate(outs):
+    for which, out in outs:
         rows = out
         if not isinstance(out, int):
             rows = out.shape[0]
-            aliases[len(operands)] = n
+            aliases[len(operands)] = len(out_specs)
             operands.append(out)
             in_specs.append(pl.BlockSpec(memory_space=pl.ANY))
         out_specs.append(
-            pl.BlockSpec((1, 2, span, span), lambda u, tab, at, n=n: (tab[u, OUT_ROWS + n], 0, 0, 0))
+            pl.BlockSpec(
+                (1, 2, span, span),
+                lambda u, tab, which=which: (at(tab, u, OUT_ROWS + which), 0, 0, 0),
+            )
         )
         out_shapes.append(jax.ShapeDtypeStruct((rows, 2, span, span), jnp.bfloat16))
-    out_specs.append(pl.BlockSpec((1, sources), lambda u, tab, at: (0, 0)))
+    out_specs.append(pl.BlockSpec((1, sources), lambda u, tab: (0, 0)))
     out_shapes.append(jax.ShapeDtypeStruct((1, sources), jnp.float32))
-    steps = table.shape[0]
-    flops = 16 * steps * sources * span * span
-    kinds = [(len(both), int(bool(single))) for both, single in pieces]
+    flops = 16 * count * sources * span * span
+    kinds = [[(len(entry), start) for entry, start in piece] for piece in pieces]
     return pl.pallas_call(
-        functools.partial(unit_kernel, index, kinds, len(outs), len(aliases)),
+        functools.partial(unit_kernel, index, offset, kinds, len(outs), len(aliases)),
         grid_spec=pltpu.PrefetchScalarGridSpec(
-            num_scalar_prefetch=2,
-            grid=(steps,),
+            num_scalar_prefetch=1,
+            grid=(count,),
             in_specs=in_specs,
             out_specs=out_specs,
             scratch_shapes=[
@@ -322,10 +371,10 @@
             out_ref[0, 0] = refs[which][...] if row is None else refs[which][row]
 
 
-def put_residuals(sources, arrays, targets, shape, residual):
+def put_residuals(sources, arrays, offset, table, shape, residual):
     span = shape[-1]
     whole = pl.BlockSpec(memory_space=pltpu.VMEM)
-    operands = [targets, *arrays]
+    operands = [table, *arrays]
     in_specs = [whole] * len(arrays)
     aliases = {}
     if residual is not None:
@@ -339,7 +388,8 @@
             grid=(len(sources),),
             in_specs=in_specs,
             out_specs=pl.BlockSpec(
-                (1, 1, 2, span, span), lambda n, tab: (tab[n, 0], tab[n, 1], 0, 0, 0)
+                (1, 1, 2, span, span),
+                lambda n, tab: (tab[offset + 2 * n], tab[offset + 2 * n + 1], 0, 0, 0),
             ),
         ),
         out_shape=jax.ShapeDtypeStruct(shape, jnp.bfloat16),
@@ -350,7 +400,7 @@
 
 
 class Routes:
-    def __init__(self, planes, width, units):
+    def __init__(self, planes, width, units, share):
         count = planes * width
         blocks = int(units[:, :2].max()) + 1
         self.width = width
@@ -416,10 +466,10 @@
                     rows[-1][OUT_ROWS : OUT_ROWS + 2] = [trash, trash]
             return np.array(tables, np.int32)
 
-        self.first_table = table_of(
+        first_table = table_of(
             self.full, lambda u: True, lambda m, phase: (m * units_dev + phase, 0), 0
         )
-        self.tables = [
+        tables = [
             table_of(
                 self.pieces,
                 lambda u, n=n: events[u] == n,
@@ -430,7 +480,23 @@
         ]
         assert units_dev == 2
         assert all(events[order[t][0]] < len(self.pieces) - 1 for t in range(count))
-        self.unit_of = np.array([[u % units_dev for u in order[t]] for t in range(count)], np.int32)
+
+        def targets(phases, index):
+            rows = np.zeros((count, width, len(phases), 2), np.int32)
+            for t in range(count):
+                for m in range(width):
+                    for n, phase in enumerate(phases):
+                        rows[t, m, n] = order[t][phase] % units_dev, (t % width ^ m) * share + index
+            return rows
+
+        starts = np.array([[(t % width ^ m) * share for m in range(width)] for t in range(count)])
+        parts = [starts, first_table, *tables, targets([0, 1], 0), targets([0], 1), targets([1], 1)]
+        parts = [part.reshape(count, -1).astype(np.int32) for part in parts]
+        ends = np.cumsum([part.shape[1] for part in parts]).tolist()
+        self.table = np.concatenate(parts, 1)
+        self.first_steps = (ends[0], first_table.shape[1])
+        self.steps = [(ends[1 + n], table.shape[1]) for n, table in enumerate(tables)]
+        self.targets = ends[1 + len(tables) : 4 + len(tables)]
 
 
 def ship(value, pairs):
@@ -460,21 +526,27 @@
         + [own_rows, none, none, own_rows],
         1,
     )
-    table = lax.dynamic_slice_in_dim(
-        jnp.asarray(table.astype(np.int32)), tile_index * units_dev, units_dev, 0
-    )
-    place = jnp.zeros((1,), jnp.int32)
+    table = table.astype(np.int32).reshape(-1, units_dev * COLUMNS)
+    table = np.pad(table, ((0, 0), (1, 0)))
+    table = lax.dynamic_index_in_dim(jnp.asarray(table), tile_index, 0, keepdims=False)
     bright = None
     residuals, grads = [], []
     for slot in range(slots):
         owned, shine = build_factors(
-            (slot, slots), place, beam, [], antenna_uvw, [small], [list(range(blocks))], span
+            (slot, slots), table, beam, [], antenna_uvw, [small], [list(range(blocks))], span
         )
         factors = lax.all_gather(owned, "tile", axis=2, tiled=True)
         if bright is None:
             bright = lax.all_gather(shine, "tile", axis=1, tiled=True)
         residual, grad = unit_work(
-            slot, table, place, [([factors], [])], visibility[None], keep, bright, [units_dev]
+            slot,
+            (1, units_dev),
+            table,
+            [[((factors,), 0)]],
+            visibility[None],
+            keep,
+            bright,
+            [(0, units_dev)],
         )
         residuals.append(residual)
         grads.append(grad)
@@ -489,136 +561,109 @@
     tile_index = lax.axis_index("tile")
     mine = tile_index % width
     others = range(1, width)
-
-    def mine_of(rows):
-        return lax.dynamic_index_in_dim(jnp.asarray(rows), tile_index, 0, keepdims=False)
-
-    def slots_of(m):
-        return jnp.bitwise_xor(mine, m) * share
-
-    place = slots_of(0).astype(jnp.int32).reshape(1)
-
-    smalls = [small] + [ship(small, routes.partner[m]) for m in others]
-
-    def beams_of(index):
-        return [
-            lax.dynamic_slice_in_dim(beam, slots_of(m) + index, 1, 0)
-            for m in others
-        ]
-
-    beams = [ship(part, routes.partner[m]) for m, part in zip(others, beams_of(0))]
-    (first, bright) = build_factors(
-        (0, share), place, beam, beams, antenna_uvw, smalls, routes.full, span
-    )
+    table = lax.dynamic_index_in_dim(jnp.asarray(routes.table), tile_index, 0, keepdims=False)
 
     def near(piece):
         return [ship(piece, routes.onward), ship(piece, routes.backward)]
 
-    def far(piece, sides):
-        halves = [ship(sides[0][0], routes.onward), ship(sides[1][1], routes.backward)]
-        return ([piece, *sides], halves)
-
-    sides_first = near(first)
-
-    link = first
-    later_beams = []
-    for m, part in zip(others, beams_of(1)):
-        later_beams.append(ship(in_order(part, link), routes.partner[m]))
-    link = later_beams[-1]
-    *later, _ = build_factors(
-        (1, share), place, beam, later_beams, antenna_uvw, smalls, routes.pieces, span
+    def far(sides):
+        return ship(sides[0][0], routes.onward), ship(sides[1][1], routes.backward)
+
+    def entries(piece, sides, halves, first=0):
+        found = [(piece,), (sides[0],), (sides[1],), halves]
+        return [(arrays, n * group + first) for n, arrays in enumerate(found)]
+
+    per_group = beam.shape[2]
+    group = width * per_group
+
+    smalls = [small] + [ship(small, routes.partner[m]) for m in others]
+    beams = slices_for(beam, 0, 1, [(m, 0) for m in others], table)
+    beams = [ship(part, routes.partner[m]) for m, part in zip(others, beams)]
+    first_a, _ = build_factors(
+        (0, share), table, beam, [], antenna_uvw, [small], routes.full, span
     )
-    brights = [
+    sides_a = near(first_a)
+    first_b, bright = build_factors(
+        (0, share), table, None, beams, antenna_uvw, smalls, routes.full, span
+    )
+    bright = [
         bright,
         ship(bright, routes.onward),
         ship(bright, routes.backward),
         ship(bright, routes.opposite),
     ]
-    vis = []
-    for m in range(width):
-        part = lax.dynamic_slice_in_dim(visibility, slots_of(m), share, 1)
-        if m:
-            part = ship(in_order(part, link), routes.partner[m])
-            link = part
-        vis.append(part)
+    bright = jnp.concatenate(bright, 1)
+    sides_b = near(first_b)
+    far_a = far(sides_a)
+
+    waiting = in_order(beam, *sides_a)
+    later_beams = slices_for(waiting, 0, 1, [(m, 1) for m in others], table)
+    later_beams = [ship(part, routes.partner[m]) for m, part in zip(others, later_beams)]
+    later = build_factors(
+        (1, share), table, beam, later_beams, antenna_uvw, smalls, routes.pieces, span
+    )[:-1]
+    vis = list(
+        slices_for(
+            in_order(visibility, *later_beams), 1, share, [(m, 0) for m in range(width)], table
+        )
+    )
+    link = later[0]
+    for m in others:
+        vis[m] = link = ship(in_order(vis[m], link), routes.partner[m])
     vis = jnp.stack(vis, 0)
-    bright = jnp.concatenate(brights, 1)
-
-    held = []
-    sides = sides_first
-    ready = [far(first, sides_first)]
-    for n, piece in enumerate(later):
-        if n == len(later) - 1:
-            first_res, first_grad = unit_work(
-                0,
-                mine_of(routes.first_table),
-                place,
-                [ready[0]],
-                vis,
-                keep,
-                bright,
-                [width * units_dev],
-            )
-            piece = in_order(piece, first_grad)
-        piece = in_order(piece, *sides)
+
+    far_b = far(sides_b)
+    pieces = [entries(first_a, sides_a, far_a) + entries(first_b, sides_b, far_b, per_group)]
+    before = [tuple(sides_b), far_b]
+    ready = []
+    for piece in later:
+        piece = in_order(piece, *before[0])
+        before = before[1:]
         sides = near(piece)
-        held.append((piece, sides))
-        ready.append(far(piece, sides))
-
-    residual = None
-    unit_of = mine_of(routes.unit_of)
-
-    def targets_of(pairs, index):
-        return jnp.stack(
-            [jnp.stack([unit_of[phase], slots_of(m).astype(jnp.int32) + index]) for m, phase in pairs]
-        ).astype(jnp.int32)
-
+        halves = far(sides)
+        before.append(halves)
+        ready.append(entries(piece, sides, halves))
+
+    first_res, first_grad = unit_work(
+        0, routes.first_steps, table, pieces, vis, keep, bright, [(0, width * units_dev)]
+    )
     returned = []
     for m in others:
         rows = first_res[m * units_dev : (m + 1) * units_dev]
-        returned.append(ship(in_order(rows, link), routes.partner[m]))
-        link = returned[-1]
+        returned.append(ship(rows, routes.partner[m]))
     pairs = [(m, phase) for m in range(width) for phase in range(units_dev)]
     residual = put_residuals(
-        [(m, phase) for m, phase in pairs],
-        [first_res, *returned],
-        targets_of(pairs, 0),
-        visibility.shape,
-        None,
+        pairs, [first_res, *returned], routes.targets[0], table, visibility.shape, None
     )
 
     grads = []
-    outs = [width + 1, width + 1]
-    for n in range(len(later)):
-        last = n == len(later) - 1
+    outs = [(0, width + 1), (1, width + 1)]
+    waits = [returned[:1], returned[1:], [residual]]
+    for n, wait in enumerate(waits):
+        last = n == len(waits) - 1
         if last:
             outs = outs[1:]
-        table = mine_of(routes.tables[n])
-        if last:
-            table = jnp.concatenate(
-                [table[:, :OUT_ROWS], table[:, OUT_ROWS + 1 :][:, :1], table[:, OUT_ROWS + 1 :]], 1
-            )
-        *outs, grad = unit_work(1, table, place, ready[1 : n + 2], vis, keep, bright, outs)
+        *found, grad = unit_work(
+            1, routes.steps[n], in_order(table, *wait), ready[: n + 1], vis, keep, bright, outs
+        )
+        outs = [(which, out) for (which, _), out in zip(outs, found)]
         grads.append(grad)
-        if n >= len(later) - 2:
-            back = [ship(outs[0][m], routes.partner[m]) for m in others]
-            phase = 1 if last else 0
-            pairs = [(m, phase) for m in range(width)]
+        if n >= len(waits) - 2:
+            back = [ship(found[0][m], routes.partner[m]) for m in others]
             residual = put_residuals(
                 [(0, 0)] + [(m, None) for m in others],
-                [outs[0], *back],
-                targets_of(pairs, 1),
+                [found[0], *back],
+                routes.targets[2 if last else 1],
+                table,
                 visibility.shape,
                 residual,
             )
 
     partial = jnp.concatenate([first_grad, sum(grads[1:], grads[0])], 0)
-    group = partial.shape[1] // 4
     parts = [partial[:, n * group : (n + 1) * group] for n in range(4)]
     plane_sum = (parts[0] + ship(parts[3], routes.opposite)) + (
         ship(parts[1], routes.backward) + ship(parts[2], routes.onward)
     )
-    per_group = group // width
     own = [plane_sum[:, m * per_group : (m + 1) * per_group] for m in range(width)]
     own = jnp.stack([own[0]] + [ship(own[m], routes.partner[m]) for m in others], 0)
     ids = jnp.arange(width, dtype=jnp.int32)
@@ -636,7 +681,7 @@
     keep = 1.0 - antenna_flags.astype(jnp.float32)
     arguments = (visibility, station_beam, antenna_uvw, small, keep)
     if lax.axis_size("tile") == 16:
-        routes = Routes(4, 4, unit_table(antennas // span))
+        routes = Routes(4, 4, unit_table(antennas // span), visibility.shape[1] // 4)
         residual, summed = plane_program(routes, *arguments)
     else:
         residual, summed = plain_program(*arguments)

time: 271 us -> 277 us (1.022); the launches traced: 266 us -> 276 us
  waiting for transfers between devices: 121 us -> 155 us
  starting transfers between devices: 66.8 us -> 51 us
  other arithmetic: 16.5 us -> 6.23 us
  Pallas kernels: 41.8 us -> 51.2 us
  local copies, waits for them, and re-layouts: 19.2 us -> 12.2 us
    ppermute x46 -> x50, waiting for transfers between devices: 121 us -> 155 us  [ship(): return lax.ppermute(value, 'tile', pairs)]
    ppermute x46 -> x50, starting transfers between devices: 66.8 us -> 51 us  [ship(): return lax.ppermute(value, 'tile', pairs)]
    another operation x12 -> x0, other arithmetic: 9.55 us -> none  [targets_of(): jnp.stack([jnp.stack([unit_of[phase], slots_of(m).astype(jnp.int32) + ind...]
    pallas_call x6 -> x10, Pallas kernels: 33.8 us -> 43.3 us  [the longest x4 26.9 us: unit_work(): pl.pallas_call(functools.partial(unit_kernel, index, offset, kinds, len(o...]
    another operation x2 -> x0, local copies, waits for them, and re-layouts: 4.61 us -> none  [the longest x1 3.96 us: plane_program(): vis = jnp.stack(vis, 0)]
    unnamed x28 -> x60, local copies, waits for them, and re-layouts: 5.11 us -> 9.59 us
  transfers between devices with their start and end apart: 46 -> 50, of which waited for: 13 -> 20; matrix products, arithmetic and copies ran while one was open for 11% -> 2% of each run, Pallas kernels for 14% -> 14%
where the time goes in v4:
time: 277 us; the launch traced here: 276 us
  waiting for transfers between devices  155 us (56%)
  Pallas kernels  51.2 us (18%)
  starting transfers between devices  51 us (18%)
  local copies, waits for them, and re-layouts  12.2 us (4%)
  other arithmetic  6.23 us (2%)
    ppermute x50, waiting for transfers between devices, ship(): return lax.ppermute(value, 'tile', pairs)  155 us
    ppermute x50, starting transfers between devices, ship(): return lax.ppermute(value, 'tile', pairs)  51 us
    pallas_call x4, Pallas kernels, unit_work(): pl.pallas_call(functools.partial(unit_kernel, index, offset, kinds, len(o...  26.9 us
    pallas_call x3, Pallas kernels, slices_for(): pl.pallas_call(functools.partial(slice_kernel, len(starts)), grid_spec=pl...  9.94 us
    unnamed x60, local copies, waits for them, and re-layouts  9.59 us
    pallas_call x3, Pallas kernels, put_residuals(): pl.pallas_call(functools.partial(put_kernel, sources), grid_spec=pltpu.Pr...  7.9 us
    pallas_call x3, Pallas kernels, build_factors(): pl.pallas_call(functools.partial(build_kernel, sets, len(smalls), slot_id...  6.4 us
  transfers between devices with their start and end apart: 50, of which 20 were waited for; matrix products, arithmetic and copies ran while one was open for 2% of the time, Pallas kernels for 14%

profile of v4, /device:TPU:0, one launch (start us, length us, event | category | flops | bytes accessed | tf_op | source)
XLA Modules:
  0.0 276.4 jit_solution(7567568359270008552)
XLA Ops:
  4.5 1.6 copy-done
  6.1 1.7 build_factors.3
  7.9 4.0 %collective-permute-start.1 = (bf16[2,8,32,256]{3,2,1,0:T(8,128)(2,1)S(1)}, bf16[2,8,32,256]{3,2,1,0:T(8,128)(2,1)S(1)}, u32[]{:S(2)}, u32[]{:S(2)}) collective-permute-start(bf16[2,8,32,256]{3,2,1,0:T(8,128)(2,1)S(1)} %get-tuple-element.39.refs_0_), channel_id=1, source_target_pairs={{0,8},{1,9},{2,10},{3,11},{4,0},{5,1},{6,2},{7,3},{8,12},{9,13},{1... | collective-permute-start | bytes 786440 | tf_op jit(solution)/shard_map/ppermute | solution.py:503
  12.6 6.0 %collective-permute-done.1.refs_2_ = bf16[2,8,32,256]{3,2,1,0:T(8,128)(2,1)S(1)} collective-permute-done((bf16[2,8,32,256]{3,2,1,0:T(8,128)(2,1)S(1)}, bf16[2,8,32,256]{3,2,1,0:T(8,128)(2,1)S(1)}, u32[]{:S(2)}, u32[]{:S(2)}) %collective-permute-start.1) | collective-permute-done | bytes 262176 | tf_op jit(solution)/shard_map/ppermute | solution.py:503
  18.7 6.2 %collective-permute-done.refs_1_ = bf16[2,8,32,256]{3,2,1,0:T(8,128)(2,1)S(1)} collective-permute-done((bf16[2,8,32,256]{3,2,1,0:T(8,128)(2,1)S(1)}, bf16[2,8,32,256]{3,2,1,0:T(8,128)(2,1)S(1)}, u32[]{:S(2)}, u32[]{:S(2)}) %collective-permute-start) | collective-permute-done | bytes 262176 | tf_op jit(solution)/shard_map/ppermute | solution.py:503
  24.9 2.7 slices_for.4
  27.6 1.5 collective-permute-start.15
  29.5 1.4 collective-permute-start.9
  31.4 5.5 %collective-permute-done.15.refs_2_ = bf16[1,2,32,2048]{3,2,1,0:T(8,128)(2,1)S(1)} collective-permute-done((bf16[1,2,32,2048]{3,2,1,0:T(8,128)(2,1)}, bf16[1,2,32,2048]{3,2,1,0:T(8,128)(2,1)S(1)}, u32[]{:S(2)}, u32[]{:S(2)}) %collective-permute-start.15) | collective-permute-done | bytes 262176 | tf_op jit(solution)/shard_map/ppermute | solution.py:503
  37.0 4.8 %collective-permute-done.16.refs_3_ = bf16[1,2,32,2048]{3,2,1,0:T(8,128)(2,1)S(1)} collective-permute-done((bf16[1,2,32,2048]{3,2,1,0:T(8,128)(2,1)}, bf16[1,2,32,2048]{3,2,1,0:T(8,128)(2,1)S(1)}, u32[]{:S(2)}, u32[]{:S(2)}) %collective-permute-start.16) | collective-permute-done | bytes 262176 | tf_op jit(solution)/shard_map/ppermute | solution.py:503
  41.7 4.5 %slices_for.5 = (bf16[2,2,2,256,256]{4,3,2,1,0:T(8,128)(2,1)}, bf16[2,2,2,256,256]{4,3,2,1,0:T(8,128)(2,1)}, bf16[2,2,2,256,256]{4,3,2,1,0:T(8,128)(2,1)}, bf16[2,2,2,256,256]{4,3,2,1,0:T(8,128)(2,1)}) custom-call(s32[256]{0:T(256)} %bitcast.46, bf16[2,8,2,256,256]{4,3,2,1,0:T(8,128)(2,1)} %refs_3_, bf16[2,8,2,256,256]{4,3,2,1,0:T(8,128)(2,1)} %refs_3_, ...), custom_call_target="tpu_custom_call" | custom-call | tf_op jit(solution)/shard_map/slices_for/pallas_call | solution.py:140
  50.7 2.5 build_factors.5
  54.3 2.7 slices_for.3
  57.3 1.5 collective-permute-start.5
  58.9 7.6 %collective-permute-done.5.refs_1_ = bf16[1,2,32,2048]{3,2,1,0:T(8,128)(2,1)S(1)} collective-permute-done((bf16[1,2,32,2048]{3,2,1,0:T(8,128)(2,1)}, bf16[1,2,32,2048]{3,2,1,0:T(8,128)(2,1)S(1)}, u32[]{:S(2)}, u32[]{:S(2)}) %collective-permute-start.5) | collective-permute-done | bytes 262176 | tf_op jit(solution)/shard_map/ppermute | solution.py:503
  66.6 4.5 %collective-permute-done.6.refs_2_ = bf16[1,2,32,2048]{3,2,1,0:T(8,128)(2,1)S(1)} collective-permute-done((bf16[1,2,32,2048]{3,2,1,0:T(8,128)(2,1)}, bf16[1,2,32,2048]{3,2,1,0:T(8,128)(2,1)S(1)}, u32[]{:S(2)}, u32[]{:S(2)}) %collective-permute-start.6) | collective-permute-done | bytes 262176 | tf_op jit(solution)/shard_map/ppermute | solution.py:503
  71.1 2.1 build_factors.4
  75.3 1.6 collective-permute-start.18
  76.9 16.3 %collective-permute-done.11.refs_7_ = bf16[2,8,96,256]{3,2,1,0:T(8,128)(2,1)S(1)} collective-permute-done((bf16[2,8,96,256]{3,2,1,0:T(8,128)(2,1)S(1)}, bf16[2,8,96,256]{3,2,1,0:T(8,128)(2,1)S(1)}, u32[]{:S(2)}, u32[]{:S(2)}) %collective-permute-start.11) | collective-permute-done | bytes 786464 | tf_op jit(solution)/shard_map/ppermute | solution.py:503
  93.2 2.0 collective-permute-start.13
  95.2 16.3 %collective-permute-done.10.refs_6_ = bf16[2,8,96,256]{3,2,1,0:T(8,128)(2,1)S(1)} collective-permute-done((bf16[2,8,96,256]{3,2,1,0:T(8,128)(2,1)S(1)}, bf16[2,8,96,256]{3,2,1,0:T(8,128)(2,1)S(1)}, u32[]{:S(2)}, u32[]{:S(2)}) %collective-permute-start.10) | collective-permute-done | bytes 786464 | tf_op jit(solution)/shard_map/ppermute | solution.py:503
  111.6 2.9 %collective-permute-start.27 = (bf16[2,4,128,256]{3,2,1,0:T(8,128)(2,1)S(1)}, bf16[2,4,128,256]{3,2,1,0:T(8,128)(2,1)S(1)}, u32[]{:S(2)}, u32[]{:S(2)}) collective-permute-start(bf16[2,4,128,256]{3,2,1,0:T(8,128)(2,1)S(1)} %get-tuple-element.60.refs_0_), channel_id=1, source_target_pairs={{0,8},{1,9},{2,10},{3,11},{4,0},{5,1},{6,2},{7,3},{8,12},{9,13},{1... | collective-permute-start | bytes 1572872 | tf_op jit(solution)/shard_map/ppermute | solution.py:503
  115.2 4.8 %collective-permute-done.13.refs_9_ = bf16[8,96,256]{2,1,0:T(8,128)(2,1)S(1)} collective-permute-done((bf16[8,96,256]{2,1,0:T(8,128)(2,1)S(1)}, bf16[8,96,256]{2,1,0:T(8,128)(2,1)S(1)}, u32[]{:S(2)}, u32[]{:S(2)}) %collective-permute-start.13) | collective-permute-done | bytes 393248 | tf_op jit(solution)/shard_map/ppermute | solution.py:503
  120.5 8.1 %collective-permute-done.12.refs_8_ = bf16[8,96,256]{2,1,0:T(8,128)(2,1)S(1)} collective-permute-done((bf16[8,96,256]{2,1,0:T(8,128)(2,1)S(1)}, bf16[8,96,256]{2,1,0:T(8,128)(2,1)S(1)}, u32[]{:S(2)}, u32[]{:S(2)}) %collective-permute-start.12) | collective-permute-done | bytes 393248 | tf_op jit(solution)/shard_map/ppermute | solution.py:503
  128.5 11.1 %collective-permute-done.27.refs_2_ = bf16[2,4,128,256]{3,2,1,0:T(8,128)(2,1)S(1)} collective-permute-done((bf16[2,4,128,256]{3,2,1,0:T(8,128)(2,1)S(1)}, bf16[2,4,128,256]{3,2,1,0:T(8,128)(2,1)S(1)}, u32[]{:S(2)}, u32[]{:S(2)}) %collective-permute-start.27) | collective-permute-done | bytes 524320 | tf_op jit(solution)/shard_map/ppermute | solution.py:503
  140.2 10.8 %collective-permute-done.26.refs_1_ = bf16[2,4,128,256]{3,2,1,0:T(8,128)(2,1)S(1)} collective-permute-done((bf16[2,4,128,256]{3,2,1,0:T(8,128)(2,1)S(1)}, bf16[2,4,128,256]{3,2,1,0:T(8,128)(2,1)S(1)}, u32[]{:S(2)}, u32[]{:S(2)}) %collective-permute-start.26) | collective-permute-done | bytes 524320 | tf_op jit(solution)/shard_map/ppermute | solution.py:503
  151.5 1.5 collective-permute-start.28
  154.4 16.1 %collective-permute-done.22 = f32[8,128]{1,0:T(8,128)S(1)} collective-permute-done((f32[8,128]{1,0:T(8,128)S(1)}, f32[8,128]{1,0:T(8,128)S(1)}, u32[]{:S(2)}, u32[]{:S(2)}) %collective-permute-start.22) | collective-permute-done | bytes 4128 | tf_op jit(solution)/shard_map/ppermute | solution.py:503
  170.9 1.6 collective-permute-start.2
  174.0 1.5 collective-permute-start.35
  176.1 3.4 %pad_maximum_fusion.refs_10_.refs_5_.refs_15_ = bf16[4,2,2,2,256,256]{5,4,3,2,1,0:T(8,128)(2,1)} fusion(bf16[1,2,2,2,256,256]{5,4,3,2,1,0:T(8,128)(2,1)S(1)} %bitcast.59, bf16[1,2,2,2,256,256]{5,4,3,2,1,0:T(8,128)(2,1)S(1)} %bitcast.58, bf16[1,2,2,2,256,256]{5,4,3,2,1,0:T(8,128)(2,1)} %bitcast.7, bf16[1,2,2,2,256,256]{5,4,3,2,1,0:T(8,128)(2,1)S(1)} %bitcast.57), kind=kLoop, calls=%fused_computation | loop fusion | flops 6291456 | bytes 8388608 | tf_op jit(solution)/shard_map/stack | solution.py:613
  179.5 11.2 %unit_work.4 = (bf16[8,2,256,256]{3,2,1,0:T(8,128)(2,1)}, f32[1,512]{1,0:T(1,128)S(1)}) custom-call(s32[256]{0:T(256)S(1)} %bitcast.50, bf16[2,8,32,256]{3,2,1,0:T(8,128)(2,1)S(1)} %copy-done.25, bf16[2,8,32,256]{3,2,1,0:T(8,128)(2,1)S(1)} %copy-done.17, bf16[2,8,32,256]{3,2,1,0:T(8,128)(2,1)S(1)} %copy-done.15, ...), custom_call_target="tpu_custom_call" | custom-call | flops 4294967296 | bytes 33554432 | tf_op jit(solution)/shard_map/unit_work/pallas_call | solution.py:343
  190.7 1.5 fusion.4
  194.2 2.4 collective-permute-start.33
  196.7 9.8 %collective-permute-done.25.refs_3_ = bf16[2,2,256,256]{3,2,1,0:T(8,128)(2,1)S(1)} collective-permute-done((bf16[2,2,256,256]{3,2,1,0:T(8,128)(2,1)S(1)}, bf16[2,2,256,256]{3,2,1,0:T(8,128)(2,1)S(1)}, u32[]{:S(2)}, u32[]{:S(2)}) %collective-permute-start.25) | collective-permute-done | bytes 524320 | tf_op jit(solution)/shard_map/ppermute | solution.py:503
  206.4 2.3 collective-permute-start.37
  208.8 9.0 %collective-permute-done.24.refs_2_ = bf16[2,2,256,256]{3,2,1,0:T(8,128)(2,1)S(1)} collective-permute-done((bf16[2,2,256,256]{3,2,1,0:T(8,128)(2,1)S(1)}, bf16[2,2,256,256]{3,2,1,0:T(8,128)(2,1)S(1)}, u32[]{:S(2)}, u32[]{:S(2)}) %collective-permute-start.24) | collective-permute-done | bytes 524320 | tf_op jit(solution)/shard_map/ppermute | solution.py:503
  219.1 6.1 %unit_work.5 = (bf16[5,2,256,256]{3,2,1,0:T(8,128)(2,1)S(1)}, bf16[5,2,256,256]{3,2,1,0:T(8,128)(2,1)S(1)}, f32[1,512]{1,0:T(1,128)S(1)}) custom-call(s32[256]{0:T(256)S(1)} %bitcast.51, bf16[2,4,128,256]{3,2,1,0:T(8,128)(2,1)S(1)} %get-tuple-element.60.refs_0_, bf16[2,4,128,256]{3,2,1,0:T(8,128)(2,1)S(1)} %collective-permute-done.26.refs_1_, ...), custom_call_target="tpu_custom_call" | custom-call | flops 2147483648 | bytes 16777216 | tf_op jit(solution)/shard_map/unit_work/pallas_call | solution.py:343
  226.3 6.6 %unit_work.6 = (bf16[5,2,256,256]{3,2,1,0:T(8,128)(2,1)S(1)}, bf16[5,2,256,256]{3,2,1,0:T(8,128)(2,1)}, f32[1,512]{1,0:T(1,128)S(1)}) custom-call(s32[256]{0:T(256)S(1)} %bitcast.52, bf16[2,4,128,256]{3,2,1,0:T(8,128)(2,1)S(1)} %get-tuple-element.60.refs_0_, ...), custom_call_target="tpu_custom_call", output_to_operand_aliasing={{0}: (15, {}), {1}: (16, {})} | custom-call | flops 2684354560 | bytes 20971520 | tf_op jit(solution)/shard_map/unit_work/pallas_call | solution.py:343
  232.9 3.6 %put_residuals.3.refs_4_ = bf16[2,8,2,256,256]{4,3,2,1,0:T(8,128)(2,1)} custom-call(s32[256]{0:T(256)S(1)} %bitcast.53, bf16[8,2,256,256]{3,2,1,0:T(8,128)(2,1)S(1)} %copy-done.4, bf16[2,2,256,256]{3,2,1,0:T(8,128)(2,1)S(1)} %collective-permute-done.23.refs_1_, bf16[2,2,256,256]{3,2,1,0:T(8,128)(2,1)S(1)} %collective-permute-done.24.refs_2_, ...), custom_call_target="tpu_custom_call" | custom-call | tf_op jit(solution)/shard_map/put_residuals/pallas_call | solution.py:384
  236.5 3.0 %unit_work.7 = (bf16[5,2,256,256]{3,2,1,0:T(8,128)(2,1)S(1)}, f32[1,512]{1,0:T(1,128)S(1)}) custom-call(s32[256]{0:T(256)S(1)} %bitcast.54, bf16[2,4,128,256]{3,2,1,0:T(8,128)(2,1)S(1)} %get-tuple-element.60.refs_0_, bf16[2,4,128,256]{3,2,1,0:T(8,128)(2,1)S(1)} %collective-permute-done.26.refs_1_, ...), custom_call_target="tpu_custom_call", output_to_operand_aliasing={{0}: (20, {})} | custom-call | flops 1610612736 | bytes 12582912 | tf_op jit(solution)/shard_map/unit_work/pallas_call | solution.py:343
  239.6 5.0 %collective-permute-start.44 = (f32[2,128]{1,0:T(2,128)S(1)}, f32[2,128]{1,0:T(2,128)S(1)}, u32[]{:S(2)}, u32[]{:S(2)}) collective-permute-start(f32[2,128]{1,0:T(2,128)S(1)} %get-tuple-element.85), channel_id=1, source_target_pairs={{0,12},{1,13},{2,14},{3,15},{4,8},{5,9},{6,10},{7,11},{8,4},{9,5},... | collective-permute-start | bytes 3080 | tf_op jit(solution)/shard_map/ppermute | solution.py:503
  244.6 2.9 %collective-permute-start.45 = (f32[2,128]{1,0:T(2,128)S(1)}, f32[2,128]{1,0:T(2,128)S(1)}, u32[]{:S(2)}, u32[]{:S(2)}) collective-permute-start(f32[2,128]{1,0:T(2,128)S(1)} %get-tuple-element.87), channel_id=1, source_target_pairs={{0,8},{1,9},{2,10},{3,11},{4,0},{5,1},{6,2},{7,3},{8,12},{9,13},{1... | collective-permute-start | bytes 3080 | tf_op jit(solution)/shard_map/ppermute | solution.py:503
  251.8 4.5 %collective-permute-done.49 = f32[2,32]{1,0:T(2,128)S(1)} collective-permute-done((f32[2,32]{1,0:T(2,128)S(1)}, f32[2,32]{1,0:T(2,128)S(1)}, u32[]{:S(2)}, u32[]{:S(2)}) %collective-permute-start.49) | collective-permute-done | bytes 288 | tf_op jit(solution)/shard_map/ppermute | solution.py:503
  257.2 3.6 %collective-permute-done.48 = f32[2,32]{1,0:T(2,128)S(1)} collective-permute-done((f32[2,32]{1,0:T(2,128)S(1)}, f32[2,32]{1,0:T(2,128)S(1)}, u32[]{:S(2)}, u32[]{:S(2)}) %collective-permute-start.48) | collective-permute-done | bytes 288 | tf_op jit(solution)/shard_map/ppermute | solution.py:503
  263.7 8.4 %collective-permute-done.42.refs_2_ = bf16[2,256,256]{2,1,0:T(8,128)(2,1)S(1)} collective-permute-done((bf16[2,256,256]{2,1,0:T(8,128)(2,1)S(1)}, bf16[2,256,256]{2,1,0:T(8,128)(2,1)S(1)}, u32[]{:S(2)}, u32[]{:S(2)}) %collective-permute-start.42) | collective-permute-done | bytes 262176 | tf_op jit(solution)/shard_map/ppermute | solution.py:503
  272.1 2.1 put_residuals.4.refs_4_
  274.2 2.1 put_residuals.5
  (156 shorter events, 32.2 us)
Async XLA Ops:
  7.9 10.8 %collective-permute-start.1 = (bf16[2,8,32,256]{3,2,1,0:T(8,128)(2,1)S(1)}, bf16[2,8,32,256]{3,2,1,0:T(8,128)(2,1)S(1)}, u32[]{:S(2)}, u32[]{:S(2)}) collective-permute-start(bf16[2,8,32,256]{3,2,1,0:T(8,128)(2,1)S(1)} %get-tuple-element.39.refs_0_), channel_id=1, source_target_pairs={{0,8},{1,9},{2,10},{3,11},{4,0},{5,1},{6,2},{7,3},{8,12},{9,13},{1... | collective-permute-start | bytes 786440 | tf_op jit(solution)/shard_map/ppermute | solution.py:503
  11.9 13.0 %collective-permute-start = (bf16[2,8,32,256]{3,2,1,0:T(8,128)(2,1)S(1)}, bf16[2,8,32,256]{3,2,1,0:T(8,128)(2,1)S(1)}, u32[]{:S(2)}, u32[]{:S(2)}) collective-permute-start(bf16[2,8,32,256]{3,2,1,0:T(8,128)(2,1)S(1)} %get-tuple-element.39.refs_0_), channel_id=1, source_target_pairs={{0,4},{1,5},{2,6},{3,7},{4,12},{5,13},{6,14},{7,15},{8,0},{9,1},{1... | collective-permute-start | bytes 786440 | tf_op jit(solution)/shard_map/ppermute | solution.py:503
  27.6 9.3 %collective-permute-start.15 = (bf16[1,2,32,2048]{3,2,1,0:T(8,128)(2,1)}, bf16[1,2,32,2048]{3,2,1,0:T(8,128)(2,1)S(1)}, u32[]{:S(2)}, u32[]{:S(2)}) collective-permute-start(bf16[1,2,32,2048]{3,2,1,0:T(8,128)(2,1)} %get-tuple-element.46), channel_id=1, source_target_pairs={{0,2},{1,3},{2,0},{3,1},{4,6},{5,7},{6,4},{7,5},{8,10},{9,11},{10,... | collective-permute-start | bytes 786440 | tf_op jit(solution)/shard_map/ppermute | solution.py:503
  29.2 12.6 %collective-permute-start.16 = (bf16[1,2,32,2048]{3,2,1,0:T(8,128)(2,1)}, bf16[1,2,32,2048]{3,2,1,0:T(8,128)(2,1)S(1)}, u32[]{:S(2)}, u32[]{:S(2)}) collective-permute-start(bf16[1,2,32,2048]{3,2,1,0:T(8,128)(2,1)} %get-tuple-element.47), channel_id=1, source_target_pairs={{0,3},{1,2},{2,1},{3,0},{4,7},{5,6},{6,5},{7,4},{8,11},{9,10},{10,... | collective-permute-start | bytes 786440 | tf_op jit(solution)/shard_map/ppermute | solution.py:503
  29.5 16.8 %collective-permute-start.9 = (f32[4,256]{1,0:T(4,128)S(1)}, f32[4,256]{1,0:T(4,128)S(1)}, u32[]{:S(2)}, u32[]{:S(2)}) collective-permute-start(f32[4,256]{1,0:T(4,128)S(1)} %pad_maximum_fusion.1.refs_1_.refs_3_.refs_4_), channel_id=1, source_target_pairs={{0,3},{1,2},{2,1},{3,0},{4,7},{5,6},{6,5},{7,4},{8,11},{9,10},{10,... | collective-permute-start | bytes 12296 | tf_op jit(solution)/shard_map/ppermute | solution.py:503
  30.9 15.4 %collective-permute-start.8 = (f32[4,256]{1,0:T(4,128)S(1)}, f32[4,256]{1,0:T(4,128)S(1)}, u32[]{:S(2)}, u32[]{:S(2)}) collective-permute-start(f32[4,256]{1,0:T(4,128)S(1)} %pad_maximum_fusion.1.refs_1_.refs_3_.refs_4_), channel_id=1, source_target_pairs={{0,2},{1,3},{2,0},{3,1},{4,6},{5,7},{6,4},{7,5},{8,10},{9,11},{10,... | collective-permute-start | bytes 12296 | tf_op jit(solution)/shard_map/ppermute | solution.py:503
  31.4 15.4 %collective-permute-start.7 = (f32[4,256]{1,0:T(4,128)S(1)}, f32[4,256]{1,0:T(4,128)S(1)}, u32[]{:S(2)}, u32[]{:S(2)}) collective-permute-start(f32[4,256]{1,0:T(4,128)S(1)} %pad_maximum_fusion.1.refs_1_.refs_3_.refs_4_), channel_id=1, source_target_pairs={{0,1},{1,0},{2,3},{3,2},{4,5},{5,4},{6,7},{7,6},{8,9},{9,8},{10,11... | collective-permute-start | bytes 12296 | tf_op jit(solution)/shard_map/ppermute | solution.py:503
  53.9 21.3 %collective-permute-start.17 = (bf16[2,2,2,256,256]{4,3,2,1,0:T(8,128)(2,1)}, bf16[2,2,2,256,256]{4,3,2,1,0:T(8,128)(2,1)}, u32[]{:S(2)}, u32[]{:S(2)}) collective-permute-start(bf16[2,2,2,256,256]{4,3,2,1,0:T(8,128)(2,1)} %get-tuple-element.52), channel_id=1, source_target_pairs={{0,1},{1,0},{2,3},{3,2},{4,5},{5,4},{6,7},{7,6},{8,9},{9,8},{10,11... | collective-permute-start | bytes 3145736 | tf_op jit(solution)/shard_map/ppermute | solution.py:503
  57.3 9.3 %collective-permute-start.5 = (bf16[1,2,32,2048]{3,2,1,0:T(8,128)(2,1)}, bf16[1,2,32,2048]{3,2,1,0:T(8,128)(2,1)S(1)}, u32[]{:S(2)}, u32[]{:S(2)}) collective-permute-start(bf16[1,2,32,2048]{3,2,1,0:T(8,128)(2,1)} %get-tuple-element.41), channel_id=1, source_target_pairs={{0,2},{1,3},{2,0},{3,1},{4,6},{5,7},{6,4},{7,5},{8,10},{9,11},{10,... | collective-permute-start | bytes 786440 | tf_op jit(solution)/shard_map/ppermute | solution.py:503
  58.8 12.3 %collective-permute-start.6 = (bf16[1,2,32,2048]{3,2,1,0:T(8,128)(2,1)}, bf16[1,2,32,2048]{3,2,1,0:T(8,128)(2,1)S(1)}, u32[]{:S(2)}, u32[]{:S(2)}) collective-permute-start(bf16[1,2,32,2048]{3,2,1,0:T(8,128)(2,1)} %get-tuple-element.42), channel_id=1, source_target_pairs={{0,3},{1,2},{2,1},{3,0},{4,7},{5,6},{6,5},{7,4},{8,11},{9,10},{10,... | collective-permute-start | bytes 786440 | tf_op jit(solution)/shard_map/ppermute | solution.py:503
  73.2 20.0 %collective-permute-start.11 = (bf16[2,8,96,256]{3,2,1,0:T(8,128)(2,1)S(1)}, bf16[2,8,96,256]{3,2,1,0:T(8,128)(2,1)S(1)}, u32[]{:S(2)}, u32[]{:S(2)}) collective-permute-start(bf16[2,8,96,256]{3,2,1,0:T(8,128)(2,1)S(1)} %get-tuple-element.43.refs_5_), channel_id=1, source_target_pairs={{0,8},{1,9},{2,10},{3,11},{4,0},{5,1},{6,2},{7,3},{8,12},{9,13},{1... | collective-permute-start | bytes 2359304 | tf_op jit(solution)/shard_map/ppermute | solution.py:503
  73.8 37.7 %collective-permute-start.10 = (bf16[2,8,96,256]{3,2,1,0:T(8,128)(2,1)S(1)}, bf16[2,8,96,256]{3,2,1,0:T(8,128)(2,1)S(1)}, u32[]{:S(2)}, u32[]{:S(2)}) collective-permute-start(bf16[2,8,96,256]{3,2,1,0:T(8,128)(2,1)S(1)} %get-tuple-element.43.refs_5_), channel_id=1, source_target_pairs={{0,4},{1,5},{2,6},{3,7},{4,12},{5,13},{6,14},{7,15},{8,0},{9,1},{1... | collective-permute-start | bytes 2359304 | tf_op jit(solution)/shard_map/ppermute | solution.py:503
  75.3 39.4 %collective-permute-start.18 = (bf16[2,2,2,256,256]{4,3,2,1,0:T(8,128)(2,1)}, bf16[2,2,2,256,256]{4,3,2,1,0:T(8,128)(2,1)S(1)}, u32[]{:S(2)}, u32[]{:S(2)}) collective-permute-start(bf16[2,2,2,256,256]{4,3,2,1,0:T(8,128)(2,1)} %get-tuple-element.54), channel_id=1, source_target_pairs={{0,2},{1,3},{2,0},{3,1},{4,6},{5,7},{6,4},{7,5},{8,10},{9,11},{10,... | collective-permute-start | bytes 3145736 | tf_op jit(solution)/shard_map/ppermute | solution.py:503
  93.2 26.8 %collective-permute-start.13 = (bf16[8,96,256]{2,1,0:T(8,128)(2,1)S(1)}, bf16[8,96,256]{2,1,0:T(8,128)(2,1)S(1)}, u32[]{:S(2)}, u32[]{:S(2)}) collective-permute-start(bf16[8,96,256]{2,1,0:T(8,128)(2,1)S(1)} %slice_bitcast_fusion), channel_id=1, source_target_pairs={{0,8},{1,9},{2,10},{3,11},{4,0},{5,1},{6,2},{7,3},{8,12},{9,13},{1... | collective-permute-start | bytes 1179656 | tf_op jit(solution)/shard_map/ppermute | solution.py:503
  111.6 17.0 %collective-permute-start.12 = (bf16[8,96,256]{2,1,0:T(8,128)(2,1)S(1)}, bf16[8,96,256]{2,1,0:T(8,128)(2,1)S(1)}, u32[]{:S(2)}, u32[]{:S(2)}) collective-permute-start(bf16[8,96,256]{2,1,0:T(8,128)(2,1)S(1)} %slice_bitcast_fusion.1), channel_id=1, source_target_pairs={{0,4},{1,5},{2,6},{3,7},{4,12},{5,13},{6,14},{7,15},{8,0},{9,1},{1... | collective-permute-start | bytes 1179656 | tf_op jit(solution)/shard_map/ppermute | solution.py:503
  111.6 28.0 %collective-permute-start.27 = (bf16[2,4,128,256]{3,2,1,0:T(8,128)(2,1)S(1)}, bf16[2,4,128,256]{3,2,1,0:T(8,128)(2,1)S(1)}, u32[]{:S(2)}, u32[]{:S(2)}) collective-permute-start(bf16[2,4,128,256]{3,2,1,0:T(8,128)(2,1)S(1)} %get-tuple-element.60.refs_0_), channel_id=1, source_target_pairs={{0,8},{1,9},{2,10},{3,11},{4,0},{5,1},{6,2},{7,3},{8,12},{9,13},{1... | collective-permute-start | bytes 1572872 | tf_op jit(solution)/shard_map/ppermute | solution.py:503
  114.6 36.4 %collective-permute-start.26 = (bf16[2,4,128,256]{3,2,1,0:T(8,128)(2,1)S(1)}, bf16[2,4,128,256]{3,2,1,0:T(8,128)(2,1)S(1)}, u32[]{:S(2)}, u32[]{:S(2)}) collective-permute-start(bf16[2,4,128,256]{3,2,1,0:T(8,128)(2,1)S(1)} %get-tuple-element.60.refs_0_), channel_id=1, source_target_pairs={{0,4},{1,5},{2,6},{3,7},{4,12},{5,13},{6,14},{7,15},{8,0},{9,1},{1... | collective-permute-start | bytes 1572872 | tf_op jit(solution)/shard_map/ppermute | solution.py:503
  114.7 60.8 %collective-permute-start.19 = (bf16[2,2,2,256,256]{4,3,2,1,0:T(8,128)(2,1)}, bf16[2,2,2,256,256]{4,3,2,1,0:T(8,128)(2,1)S(1)}, u32[]{:S(2)}, u32[]{:S(2)}) collective-permute-start(bf16[2,2,2,256,256]{4,3,2,1,0:T(8,128)(2,1)} %get-tuple-element.56), channel_id=1, source_target_pairs={{0,3},{1,2},{2,1},{3,0},{4,7},{5,6},{6,5},{7,4},{8,11},{9,10},{10,... | collective-permute-start | bytes 3145736 | tf_op jit(solution)/shard_map/ppermute | solution.py:503
  120.1 33.0 %collective-permute-start.21 = (f32[8,128]{1,0:T(8,128)S(1)}, f32[8,128]{1,0:T(8,128)S(1)}, u32[]{:S(2)}, u32[]{:S(2)}) collective-permute-start(f32[8,128]{1,0:T(8,128)S(1)} %get-tuple-element.57), channel_id=1, source_target_pairs={{0,8},{1,9},{2,10},{3,11},{4,0},{5,1},{6,2},{7,3},{8,12},{9,13},{1... | collective-permute-start | bytes 12296 | tf_op jit(solution)/shard_map/ppermute | solution.py:503
  128.5 23.0 %collective-permute-start.20 = (f32[8,128]{1,0:T(8,128)S(1)}, f32[8,128]{1,0:T(8,128)S(1)}, u32[]{:S(2)}, u32[]{:S(2)}) collective-permute-start(f32[8,128]{1,0:T(8,128)S(1)} %get-tuple-element.57), channel_id=1, source_target_pairs={{0,4},{1,5},{2,6},{3,7},{4,12},{5,13},{6,14},{7,15},{8,0},{9,1},{1... | collective-permute-start | bytes 12296 | tf_op jit(solution)/shard_map/ppermute | solution.py:503
  139.6 34.3 %collective-permute-start.31 = (bf16[2,3,128,256]{3,2,1,0:T(8,128)(2,1)S(1)}, bf16[2,3,128,256]{3,2,1,0:T(8,128)(2,1)S(1)}, u32[]{:S(2)}, u32[]{:S(2)}) collective-permute-start(bf16[2,3,128,256]{3,2,1,0:T(8,128)(2,1)S(1)} %get-tuple-element.62.refs_5_), channel_id=1, source_target_pairs={{0,8},{1,9},{2,10},{3,11},{4,0},{5,1},{6,2},{7,3},{8,12},{9,13},{1... | collective-permute-start | bytes 1179656 | tf_op jit(solution)/shard_map/ppermute | solution.py:503
  150.9 20.0 %collective-permute-start.29 = (bf16[4,128,256]{2,1,0:T(8,128)(2,1)S(1)}, bf16[4,128,256]{2,1,0:T(8,128)(2,1)S(1)}, u32[]{:S(2)}, u32[]{:S(2)}) collective-permute-start(bf16[4,128,256]{2,1,0:T(8,128)(2,1)S(1)} %slice_bitcast_fusion.2), channel_id=1, source_target_pairs={{0,8},{1,9},{2,10},{3,11},{4,0},{5,1},{6,2},{7,3},{8,12},{9,13},{1... | collective-permute-start | bytes 786440 | tf_op jit(solution)/shard_map/ppermute | solution.py:503
  151.5 21.0 %collective-permute-start.28 = (bf16[4,128,256]{2,1,0:T(8,128)(2,1)S(1)}, bf16[4,128,256]{2,1,0:T(8,128)(2,1)S(1)}, u32[]{:S(2)}, u32[]{:S(2)}) collective-permute-start(bf16[4,128,256]{2,1,0:T(8,128)(2,1)S(1)} %slice_bitcast_fusion.3), channel_id=1, source_target_pairs={{0,4},{1,5},{2,6},{3,7},{4,12},{5,13},{6,14},{7,15},{8,0},{9,1},{1... | collective-permute-start | bytes 786440 | tf_op jit(solution)/shard_map/ppermute | solution.py:503
  153.1 17.4 %collective-permute-start.22 = (f32[8,128]{1,0:T(8,128)S(1)}, f32[8,128]{1,0:T(8,128)S(1)}, u32[]{:S(2)}, u32[]{:S(2)}) collective-permute-start(f32[8,128]{1,0:T(8,128)S(1)} %get-tuple-element.57), channel_id=1, source_target_pairs={{0,12},{1,13},{2,14},{3,15},{4,8},{5,9},{6,10},{7,11},{8,4},{9,5},... | collective-permute-start | bytes 12296 | tf_op jit(solution)/shard_map/ppermute | solution.py:503
  170.5 9.0 %collective-permute-start.3 = (bf16[8,32,256]{2,1,0:T(8,128)(2,1)S(1)}, bf16[8,32,256]{2,1,0:T(8,128)(2,1)S(1)}, u32[]{:S(2)}, u32[]{:S(2)}) collective-permute-start(bf16[8,32,256]{2,1,0:T(8,128)(2,1)S(1)} %slice_bitcast_fusion.12), channel_id=1, source_target_pairs={{0,8},{1,9},{2,10},{3,11},{4,0},{5,1},{6,2},{7,3},{8,12},{9,13},{1... | collective-permute-start | bytes 393224 | tf_op jit(solution)/shard_map/ppermute | solution.py:503
  170.9 8.6 %collective-permute-start.2 = (bf16[8,32,256]{2,1,0:T(8,128)(2,1)S(1)}, bf16[8,32,256]{2,1,0:T(8,128)(2,1)S(1)}, u32[]{:S(2)}, u32[]{:S(2)}) collective-permute-start(bf16[8,32,256]{2,1,0:T(8,128)(2,1)S(1)} %slice_bitcast_fusion.13), channel_id=1, source_target_pairs={{0,4},{1,5},{2,6},{3,7},{4,12},{5,13},{6,14},{7,15},{8,0},{9,1},{1... | collective-permute-start | bytes 393224 | tf_op jit(solution)/shard_map/ppermute | solution.py:503
  172.5 21.4 %collective-permute-start.30 = (bf16[2,3,128,256]{3,2,1,0:T(8,128)(2,1)S(1)}, bf16[2,3,128,256]{3,2,1,0:T(8,128)(2,1)S(1)}, u32[]{:S(2)}, u32[]{:S(2)}) collective-permute-start(bf16[2,3,128,256]{3,2,1,0:T(8,128)(2,1)S(1)} %get-tuple-element.62.refs_5_), channel_id=1, source_target_pairs={{0,4},{1,5},{2,6},{3,7},{4,12},{5,13},{6,14},{7,15},{8,0},{9,1},{1... | collective-permute-start | bytes 1179656 | tf_op jit(solution)/shard_map/ppermute | solution.py:503
  174.0 20.2 %collective-permute-start.35 = (bf16[2,1,128,256]{3,2,1,0:T(8,128)(2,1)S(1)}, bf16[2,1,128,256]{3,2,1,0:T(8,128)(2,1)S(1)}, u32[]{:S(2)}, u32[]{:S(2)}) collective-permute-start(bf16[2,1,128,256]{3,2,1,0:T(8,128)(2,1)S(1)} %copy-done.13), channel_id=1, source_target_pairs={{0,8},{1,9},{2,10},{3,11},{4,0},{5,1},{6,2},{7,3},{8,12},{9,13},{1... | collective-permute-start | bytes 393224 | tf_op jit(solution)/shard_map/ppermute | solution.py:503
  175.5 21.1 %collective-permute-start.34 = (bf16[2,1,128,256]{3,2,1,0:T(8,128)(2,1)S(1)}, bf16[2,1,128,256]{3,2,1,0:T(8,128)(2,1)S(1)}, u32[]{:S(2)}, u32[]{:S(2)}) collective-permute-start(bf16[2,1,128,256]{3,2,1,0:T(8,128)(2,1)S(1)} %copy-done.13), channel_id=1, source_target_pairs={{0,4},{1,5},{2,6},{3,7},{4,12},{5,13},{6,14},{7,15},{8,0},{9,1},{1... | collective-permute-start | bytes 393224 | tf_op jit(solution)/shard_map/ppermute | solution.py:503
  192.2 14.2 %collective-permute-start.25 = (bf16[2,2,256,256]{3,2,1,0:T(8,128)(2,1)S(1)}, bf16[2,2,256,256]{3,2,1,0:T(8,128)(2,1)S(1)}, u32[]{:S(2)}, u32[]{:S(2)}) collective-permute-start(bf16[2,2,256,256]{3,2,1,0:T(8,128)(2,1)S(1)} %get-tuple-element.76), channel_id=1, source_target_pairs={{0,3},{1,2},{2,1},{3,0},{4,7},{5,6},{6,5},{7,4},{8,11},{9,10},{10,... | collective-permute-start | bytes 1572872 | tf_op jit(solution)/shard_map/ppermute | solution.py:503
  193.3 24.5 %collective-permute-start.24 = (bf16[2,2,256,256]{3,2,1,0:T(8,128)(2,1)S(1)}, bf16[2,2,256,256]{3,2,1,0:T(8,128)(2,1)S(1)}, u32[]{:S(2)}, u32[]{:S(2)}) collective-permute-start(bf16[2,2,256,256]{3,2,1,0:T(8,128)(2,1)S(1)} %get-tuple-element.77), channel_id=1, source_target_pairs={{0,2},{1,3},{2,0},{3,1},{4,6},{5,7},{6,4},{7,5},{8,10},{9,11},{10,... | collective-permute-start | bytes 1572872 | tf_op jit(solution)/shard_map/ppermute | solution.py:503
  193.9 25.2 %collective-permute-start.23 = (bf16[2,2,256,256]{3,2,1,0:T(8,128)(2,1)S(1)}, bf16[2,2,256,256]{3,2,1,0:T(8,128)(2,1)S(1)}, u32[]{:S(2)}, u32[]{:S(2)}) collective-permute-start(bf16[2,2,256,256]{3,2,1,0:T(8,128)(2,1)S(1)} %get-tuple-element.78), channel_id=1, source_target_pairs={{0,1},{1,0},{2,3},{3,2},{4,5},{5,4},{6,7},{7,6},{8,9},{9,8},{10,11... | collective-permute-start | bytes 1572872 | tf_op jit(solution)/shard_map/ppermute | solution.py:503
  194.2 32.1 %collective-permute-start.33 = (bf16[3,128,256]{2,1,0:T(8,128)(2,1)S(1)}, bf16[3,128,256]{2,1,0:T(8,128)(2,1)S(1)}, u32[]{:S(2)}, u32[]{:S(2)}) collective-permute-start(bf16[3,128,256]{2,1,0:T(8,128)(2,1)S(1)} %slice_bitcast_fusion.10), channel_id=1, source_target_pairs={{0,8},{1,9},{2,10},{3,11},{4,0},{5,1},{6,2},{7,3},{8,12},{9,13},{1... | collective-permute-start | bytes 589832 | tf_op jit(solution)/shard_map/ppermute | solution.py:503
  196.6 29.7 %collective-permute-start.32 = (bf16[3,128,256]{2,1,0:T(8,128)(2,1)S(1)}, bf16[3,128,256]{2,1,0:T(8,128)(2,1)S(1)}, u32[]{:S(2)}, u32[]{:S(2)}) collective-permute-start(bf16[3,128,256]{2,1,0:T(8,128)(2,1)S(1)} %slice_bitcast_fusion.11), channel_id=1, source_target_pairs={{0,4},{1,5},{2,6},{3,7},{4,12},{5,13},{6,14},{7,15},{8,0},{9,1},{1... | collective-permute-start | bytes 589832 | tf_op jit(solution)/shard_map/ppermute | solution.py:503
  206.4 30.1 %collective-permute-start.37 = (bf16[1,128,256]{2,1,0:T(8,128)(2,1)S(1)}, bf16[1,128,256]{2,1,0:T(8,128)(2,1)S(1)}, u32[]{:S(2)}, u32[]{:S(2)}) collective-permute-start(bf16[1,128,256]{2,1,0:T(8,128)(2,1)S(1)} %slice_bitcast_fusion.14), channel_id=1, source_target_pairs={{0,8},{1,9},{2,10},{3,11},{4,0},{5,1},{6,2},{7,3},{8,12},{9,13},{1... | collective-permute-start | bytes 196616 | tf_op jit(solution)/shard_map/ppermute | solution.py:503
  217.7 18.8 %collective-permute-start.36 = (bf16[1,128,256]{2,1,0:T(8,128)(2,1)S(1)}, bf16[1,128,256]{2,1,0:T(8,128)(2,1)S(1)}, u32[]{:S(2)}, u32[]{:S(2)}) collective-permute-start(bf16[1,128,256]{2,1,0:T(8,128)(2,1)S(1)} %slice_bitcast_fusion.15), channel_id=1, source_target_pairs={{0,4},{1,5},{2,6},{3,7},{4,12},{5,13},{6,14},{7,15},{8,0},{9,1},{1... | collective-permute-start | bytes 196616 | tf_op jit(solution)/shard_map/ppermute | solution.py:503
  239.6 8.2 %collective-permute-start.44 = (f32[2,128]{1,0:T(2,128)S(1)}, f32[2,128]{1,0:T(2,128)S(1)}, u32[]{:S(2)}, u32[]{:S(2)}) collective-permute-start(f32[2,128]{1,0:T(2,128)S(1)} %get-tuple-element.85), channel_id=1, source_target_pairs={{0,12},{1,13},{2,14},{3,15},{4,8},{5,9},{6,10},{7,11},{8,4},{9,5},... | collective-permute-start | bytes 3080 | tf_op jit(solution)/shard_map/ppermute | solution.py:503
  244.6 4.5 %collective-permute-start.46 = (f32[2,128]{1,0:T(2,128)S(1)}, f32[2,128]{1,0:T(2,128)S(1)}, u32[]{:S(2)}, u32[]{:S(2)}) collective-permute-start(f32[2,128]{1,0:T(2,128)S(1)} %get-tuple-element.86), channel_id=1, source_target_pairs={{0,4},{1,5},{2,6},{3,7},{4,12},{5,13},{6,14},{7,15},{8,0},{9,1},{1... | collective-permute-start | bytes 3080 | tf_op jit(solution)/shard_map/ppermute | solution.py:503
  244.6 4.5 %collective-permute-start.45 = (f32[2,128]{1,0:T(2,128)S(1)}, f32[2,128]{1,0:T(2,128)S(1)}, u32[]{:S(2)}, u32[]{:S(2)}) collective-permute-start(f32[2,128]{1,0:T(2,128)S(1)} %get-tuple-element.87), channel_id=1, source_target_pairs={{0,8},{1,9},{2,10},{3,11},{4,0},{5,1},{6,2},{7,3},{8,12},{9,13},{1... | collective-permute-start | bytes 3080 | tf_op jit(solution)/shard_map/ppermute | solution.py:503
  247.7 15.3 %collective-permute-start.43 = (bf16[2,256,256]{2,1,0:T(8,128)(2,1)S(1)}, bf16[2,256,256]{2,1,0:T(8,128)(2,1)S(1)}, u32[]{:S(2)}, u32[]{:S(2)}) collective-permute-start(bf16[2,256,256]{2,1,0:T(8,128)(2,1)S(1)} %get-tuple-element.79), channel_id=1, source_target_pairs={{0,3},{1,2},{2,1},{3,0},{4,7},{5,6},{6,5},{7,4},{8,11},{9,10},{10,... | collective-permute-start | bytes 786440 | tf_op jit(solution)/shard_map/ppermute | solution.py:503
  249.2 7.1 %collective-permute-start.49 = (f32[2,32]{1,0:T(2,128)S(1)}, f32[2,32]{1,0:T(2,128)S(1)}, u32[]{:S(2)}, u32[]{:S(2)}) collective-permute-start(f32[2,32]{1,0:T(2,128)S(1)} %get-tuple-element.89), channel_id=1, source_target_pairs={{0,3},{1,2},{2,1},{3,0},{4,7},{5,6},{6,5},{7,4},{8,11},{9,10},{10,... | collective-permute-start | bytes 776 | tf_op jit(solution)/shard_map/ppermute | solution.py:503
  249.6 24.7 %collective-permute-start.40 = (bf16[2,256,256]{2,1,0:T(8,128)(2,1)S(1)}, bf16[2,256,256]{2,1,0:T(8,128)(2,1)S(1)}, u32[]{:S(2)}, u32[]{:S(2)}) collective-permute-start(bf16[2,256,256]{2,1,0:T(8,128)(2,1)S(1)} %get-tuple-element.82), channel_id=1, source_target_pairs={{0,3},{1,2},{2,1},{3,0},{4,7},{5,6},{6,5},{7,4},{8,11},{9,10},{10,... | collective-permute-start | bytes 786440 | tf_op jit(solution)/shard_map/ppermute | solution.py:503
  250.9 9.9 %collective-permute-start.48 = (f32[2,32]{1,0:T(2,128)S(1)}, f32[2,32]{1,0:T(2,128)S(1)}, u32[]{:S(2)}, u32[]{:S(2)}) collective-permute-start(f32[2,32]{1,0:T(2,128)S(1)} %get-tuple-element.90), channel_id=1, source_target_pairs={{0,2},{1,3},{2,0},{3,1},{4,6},{5,7},{6,4},{7,5},{8,10},{9,11},{10,... | collective-permute-start | bytes 776 | tf_op jit(solution)/shard_map/ppermute | solution.py:503
  251.8 10.3 %collective-permute-start.47 = (f32[2,32]{1,0:T(2,128)S(1)}, f32[2,32]{1,0:T(2,128)S(1)}, u32[]{:S(2)}, u32[]{:S(2)}) collective-permute-start(f32[2,32]{1,0:T(2,128)S(1)} %get-tuple-element.91), channel_id=1, source_target_pairs={{0,1},{1,0},{2,3},{3,2},{4,5},{5,4},{6,7},{7,6},{8,9},{9,8},{10,11... | collective-permute-start | bytes 776 | tf_op jit(solution)/shard_map/ppermute | solution.py:503
  256.3 17.9 %collective-permute-start.39 = (bf16[2,256,256]{2,1,0:T(8,128)(2,1)S(1)}, bf16[2,256,256]{2,1,0:T(8,128)(2,1)S(1)}, u32[]{:S(2)}, u32[]{:S(2)}) collective-permute-start(bf16[2,256,256]{2,1,0:T(8,128)(2,1)S(1)} %get-tuple-element.83), channel_id=1, source_target_pairs={{0,2},{1,3},{2,0},{3,1},{4,6},{5,7},{6,4},{7,5},{8,10},{9,11},{10,... | collective-permute-start | bytes 786440 | tf_op jit(solution)/shard_map/ppermute | solution.py:503
  260.9 13.4 %collective-permute-start.38 = (bf16[2,256,256]{2,1,0:T(8,128)(2,1)S(1)}, bf16[2,256,256]{2,1,0:T(8,128)(2,1)S(1)}, u32[]{:S(2)}, u32[]{:S(2)}) collective-permute-start(bf16[2,256,256]{2,1,0:T(8,128)(2,1)S(1)} %get-tuple-element.84), channel_id=1, source_target_pairs={{0,1},{1,0},{2,3},{3,2},{4,5},{5,4},{6,7},{7,6},{8,9},{9,8},{10,11... | collective-permute-start | bytes 786440 | tf_op jit(solution)/shard_map/ppermute | solution.py:503
  262.0 10.1 %collective-permute-start.42 = (bf16[2,256,256]{2,1,0:T(8,128)(2,1)S(1)}, bf16[2,256,256]{2,1,0:T(8,128)(2,1)S(1)}, u32[]{:S(2)}, u32[]{:S(2)}) collective-permute-start(bf16[2,256,256]{2,1,0:T(8,128)(2,1)S(1)} %get-tuple-element.80), channel_id=1, source_target_pairs={{0,2},{1,3},{2,0},{3,1},{4,6},{5,7},{6,4},{7,5},{8,10},{9,11},{10,... | collective-permute-start | bytes 786440 | tf_op jit(solution)/shard_map/ppermute | solution.py:503
  263.0 9.1 %collective-permute-start.41 = (bf16[2,256,256]{2,1,0:T(8,128)(2,1)S(1)}, bf16[2,256,256]{2,1,0:T(8,128)(2,1)S(1)}, u32[]{:S(2)}, u32[]{:S(2)}) collective-permute-start(bf16[2,256,256]{2,1,0:T(8,128)(2,1)S(1)} %get-tuple-element.81), channel_id=1, source_target_pairs={{0,1},{1,0},{2,3},{3,2},{4,5},{5,4},{6,7},{7,6},{8,9},{9,8},{10,11... | collective-permute-start | bytes 786440 | tf_op jit(solution)/shard_map/ppermute | solution.py:503
  (30 other events, 555.9 us)

commit v5 on v4

v5 whole, which is shorter than its diff:
```python
import functools
import itertools

import jax
import jax.numpy as jnp
import numpy as np
from jax import lax
from jax.experimental import pallas as pl
from jax.experimental.pallas import tpu as pltpu
from jax.sharding import PartitionSpec as P


def unit_table(block_count):
    first_list = []
    second_list = []
    diag_list = []
    for row_block in range(block_count):
        for col_block in range(row_block + 1, block_count):
            first_list.append(row_block)
            second_list.append(col_block)
            diag_list.append(0)
    for pair_index in range(block_count // 2):
        first_list.append(2 * pair_index)
        second_list.append(2 * pair_index + 1)
        diag_list.append(1)
    return np.stack([first_list, second_list, diag_list], 1).astype(np.int32)


def turn_polynomials():
    nodes = 0.125 + 0.125 * np.cos(np.pi * (np.arange(64) + 0.5) / 64)
    root = np.sqrt(nodes)
    fit = np.polynomial.Polynomial.fit
    sine = fit(nodes, np.sin(2 * np.pi * root) / root, 7, domain=[0, 0.25]).convert()
    cosine = fit(nodes, np.cos(2 * np.pi * root), 8, domain=[0, 0.25]).convert()
    return [float(c) for c in sine.coef], [float(c) for c in cosine.coef]


def horner(coefs, x):
    total = coefs[-1]
    for coef in coefs[-2::-1]:
        total = total * x + coef
    return total


def build_kernel(sets, slot_ids, pieces, bright_rows, width, tab_ref, *refs):
    uvw_ref, outs = refs[-1 - len(pieces)], refs[-len(pieces) :]
    per_group = sets[0][0]
    span = outs[0].shape[2]
    count = len(sets) * per_group
    sin_coefs, cos_coefs = turn_polynomials()
    brights = []
    for part, (_, beam_at, small_at) in enumerate(sets):
        beam_ref = refs[beam_at]
        if beam_ref.shape[0] == 1:
            beam = [beam_ref.at[0, 0], beam_ref.at[0, 1]]
        else:
            beam = [beam_ref.at[pl.ds(n * per_group, per_group)] for n in (0, 1)]
        small_ref = refs[small_at]
        if small_ref.dtype == jnp.float32:
            small = small_ref[...]
        else:
            small = unsplit(small_ref, 2 * per_group, width)
        lanes = lax.broadcasted_iota(jnp.int32, (per_group, width), 1)
        rows = lax.broadcasted_iota(jnp.int32, (per_group, width), 0)

        def pick(chosen, row):
            return jnp.sum(jnp.where(chosen, small[row : row + 1, :], 0.0), axis=1, keepdims=True)

        def chosen_at(index):
            listed = pick(lanes == (tab_ref[0] + index) * per_group + rows, 3)
            return listed.astype(jnp.int32) == lanes

        group = part * per_group
        if bright_rows:
            columns = lax.broadcasted_iota(jnp.int32, (per_group, span), 1)
            numbers = lax.broadcasted_iota(jnp.int32, (per_group, span), 0) + group
            for index in range(slot_ids[1]):
                flux = pick(chosen_at(index), 2)
                line = jnp.sum(jnp.where(columns == numbers, flux, 0.0), axis=0, keepdims=True)
                if part == 0:
                    brights.append(line)
                else:
                    brights[index] += line
        chosen = chosen_at(slot_ids[0])
        east = pick(chosen, 0)
        north = pick(chosen, 1)
        depth = jnp.sqrt(1.0 - east * east - north * north) - 1.0
        for out_ref, piece in zip(outs, pieces):
            for place, block in enumerate(piece):
                cols = pl.ds(block * span, span)
                delay = (
                    uvw_ref[0, 0:1, cols] * east
                    + uvw_ref[0, 1:2, cols] * north
                    + uvw_ref[0, 2:3, cols] * depth
                )
                turn = delay - jnp.floor(delay + 0.5)
                square = turn * turn
                sine = horner(sin_coefs, square) * turn
                cosine = horner(cos_coefs, square)
                real = beam[0][:, cols].astype(jnp.float32)
                imag = beam[1][:, cols].astype(jnp.float32)
                at = pl.ds(place * count + group, per_group)
                out_ref[0, at] = (real * cosine + imag * sine).astype(jnp.bfloat16)
                out_ref[1, at] = (imag * cosine - real * sine).astype(jnp.bfloat16)
    if bright_rows:
        padding = jnp.zeros((bright_rows - len(brights), span), jnp.float32)
        block = jnp.concatenate(brights + [padding], 0).astype(jnp.bfloat16)
        for part in (0, 1):
            outs[0][part, pl.ds(len(pieces[0]) * count, bright_rows)] = block


def unsplit(message_ref, start, width):
    terms = [message_ref[pl.ds(start, 16), pl.ds(n * width, width)].astype(jnp.float32) for n in range(3)]
    return (terms[0] + terms[1]) + terms[2]


BRIGHT_ROWS = 16


def build_factors(
    slot_ids, table, beam, messages, antenna_uvw, smalls, pieces, span, bright_rows, small_width
):
    slots, _, antennas = antenna_uvw.shape
    per_group = slot_ids[2]
    index = slot_ids[0]
    whole = pl.BlockSpec(memory_space=pltpu.VMEM)
    operands, in_specs, sets = [], [], []
    if beam is not None:
        operands.append(beam)
        in_specs.append(
            pl.BlockSpec((1, 2, per_group, antennas), lambda n, tab: (tab[0] + index, 0, 0, 0))
        )
    operands += messages
    beams = len(operands)
    for n, small in enumerate(smalls):
        at = next((k for k, known in enumerate(operands) if known is small), len(operands))
        if at == len(operands):
            operands.append(small)
        sets.append((per_group, n, at))
    in_specs += [whole] * (len(operands) - len(in_specs))
    in_specs.append(pl.BlockSpec((1, 3, antennas), lambda n, tab: (tab[0] + index, 0, 0)))
    count = beams * per_group
    shapes = [
        (2, len(piece) * count + (0 if n else bright_rows), span) for n, piece in enumerate(pieces)
    ]
    return pl.pallas_call(
        functools.partial(build_kernel, sets, slot_ids, pieces, bright_rows, small_width),
        grid_spec=pltpu.PrefetchScalarGridSpec(
            num_scalar_prefetch=1,
            grid=(1,),
            in_specs=in_specs,
            out_specs=[whole] * len(pieces),
        ),
        out_shape=[jax.ShapeDtypeStruct(shape, jnp.bfloat16) for shape in shapes],
        compiler_params=pltpu.CompilerParams(vmem_limit_bytes=40 * 1024 * 1024),
        cost_estimate=LITTLE,
        name="build_factors",
    )(table, *operands, antenna_uvw)


LITTLE = pl.CostEstimate(flops=1, bytes_accessed=1, transcendentals=0)


def message_kernel(per_group, tab_ref, *refs):
    outs = [ref for ref in refs if ref.dtype == jnp.bfloat16 and len(ref.shape) == 2]
    small_ref = refs[len(outs)] if len(refs) > 2 * len(outs) else None
    for beam_ref, out_ref in zip(refs, outs):
        for part in (0, 1):
            out_ref[pl.ds(part * per_group, per_group)] = beam_ref[0, part]
        if small_ref is not None:
            count, width = small_ref.shape
            rest = jnp.concatenate([small_ref[...], jnp.zeros((16 - count, width), jnp.float32)], 0)
            out_ref[pl.ds(2 * per_group, 16)] = jnp.zeros((16, out_ref.shape[1]), jnp.bfloat16)
            for n in range(3):
                term = rest.astype(jnp.bfloat16)
                out_ref[pl.ds(2 * per_group, 16), pl.ds(n * width, width)] = term
                rest = rest - term.astype(jnp.float32)


def messages_for(beam, index, others, small, table):
    _, _, per_group, antennas = beam.shape
    rows = 2 * per_group + (0 if small is None else 16)
    whole = pl.BlockSpec(memory_space=pltpu.VMEM)
    return pl.pallas_call(
        functools.partial(message_kernel, per_group),
        grid_spec=pltpu.PrefetchScalarGridSpec(
            num_scalar_prefetch=1,
            grid=(1,),
            in_specs=[
                pl.BlockSpec(
                    (1, 2, per_group, antennas), lambda n, tab, m=m: (tab[m] + index, 0, 0, 0)
                )
                for m in others
            ]
            + ([] if small is None else [whole]),
            out_specs=[whole for _ in others],
        ),
        out_shape=[jax.ShapeDtypeStruct((rows, antennas), jnp.bfloat16) for _ in others],
        cost_estimate=LITTLE,
        name="messages_for",
    )(table, *[beam] * len(others), *([] if small is None else [small]))


def slice_kernel(count, tab_ref, *refs):
    for source, target in zip(refs[:count], refs[count:]):
        target[...] = source[...]


def slices_for(array, axis, size, starts, table):
    lead = axis > 0
    shape = array.shape[:axis] + (size,) + array.shape[axis + 1 :]
    block = (1,) + shape[1:] if lead else shape
    rest = (0,) * (array.ndim - axis - 1)
    return pl.pallas_call(
        functools.partial(slice_kernel, len(starts)),
        grid_spec=pltpu.PrefetchScalarGridSpec(
            num_scalar_prefetch=1,
            grid=(shape[0] if lead else 1,),
            in_specs=[
                pl.BlockSpec(
                    block,
                    lambda n, tab, start=start, shift=shift: (
                        *((n,) if lead else ()),
                        tab[start] // size + shift,
                        *rest,
                    ),
                )
                for start, shift in starts
            ],
            out_specs=[
                pl.BlockSpec(block, lambda n, tab: (n,) + (0,) * (array.ndim - 1)) for _ in starts
            ],
        ),
        out_shape=[jax.ShapeDtypeStruct(shape, array.dtype) for _ in starts],
        cost_estimate=LITTLE,
        name="slices_for",
    )(table, *[array] * len(starts))


KIND, ONE, TWO, ONE_AT, TWO_AT, OUT_ROW, VIS_AT = 0, 1, 2, 3, 5, 7, 8
COLUMNS = 10


def unit_kernel(index, offset, pieces, bright_at, outs, aliased, tab_ref, *refs):
    arrays = []
    for entries in pieces:
        found = []
        for count, start, number in entries:
            parts = (refs[0].at[0], refs[0].at[1]) if count == 1 else refs[:2]
            found.append((parts, start, number))
            refs = refs[count:]
        arrays.append(found)
    vis_ref, keep_one_ref, keep_two_ref = refs[:3]
    refs = refs[3:]
    columns_ref = None
    if bright_at is None:
        columns_ref, refs = refs[0], refs[1:]
    refs = refs[aliased:]
    out_refs, grad_ref = refs[:outs], refs[outs]
    refs = refs[outs + 1 :]
    if bright_at is not None:
        columns_ref, refs = refs[0], refs[1:]
    total_ref, one_ref, two_ref = refs
    step = pl.program_id(0)
    slot = tab_ref[0] + index
    sources, span = one_ref.shape[1:]

    def entry(column):
        return tab_ref[offset + step * COLUMNS + column]

    def load(target, at):
        for n, found in enumerate(arrays):

            @pl.when(entry(at) == n)
            def _(found=found):
                place = entry(at + 1)
                for parts, start, number in found:
                    rows = pl.ds(pl.multiple_of(place * number, number), number)
                    for part in (0, 1):
                        target[part, pl.ds(start, number)] = parts[part][rows]

    if bright_at is not None:

        @pl.when(step == 0)
        def _():
            for parts, start, number in arrays[0]:
                lines = parts[0][pl.ds(bright_at * number, BRIGHT_ROWS)].astype(jnp.float32)
                lanes = lax.broadcasted_iota(jnp.int32, (number, span), 1)
                rows = lax.broadcasted_iota(jnp.int32, (number, span), 0)
                for n in range(columns_ref.shape[0]):
                    line = jnp.where(lanes == rows, lines[n : n + 1, :], 0.0)
                    column = jnp.sum(line, axis=1, keepdims=True)
                    columns_ref[n, pl.ds(start, number)] = jnp.broadcast_to(column, (number, 128))

    def dot(a, b):
        return lax.dot_general(a, b, (((1,), (0,)), ((), ())), preferred_element_type=jnp.float32)

    def scaled_of(re, im):
        column = jnp.concatenate([columns_ref[index]] * (span // 128), 1)
        return (
            (re.astype(jnp.float32) * column).astype(jnp.bfloat16),
            (im.astype(jnp.float32) * column).astype(jnp.bfloat16),
        )

    def outer(a, b):
        row_ids = lax.broadcasted_iota(jnp.int32, a.shape, 0)
        a = jnp.where(row_ids == slot, a, 0.0)
        return lax.dot_general(a, b, (((0,), (0,)), ((), ())), preferred_element_type=jnp.float32)

    def cross(a_re, a_im, b_re, b_im):
        lhs = jnp.concatenate([a_re, a_im], 0).T
        rhs = jnp.concatenate(
            [jnp.concatenate([b_re, -b_im], 1), jnp.concatenate([b_im, b_re], 1)], 0
        )
        both = dot(lhs, rhs)
        return both[:, :span], both[:, span:]

    def pull(re, im, res_re, res_im, sign):
        lhs = jnp.concatenate([re, im], 1)
        rhs = jnp.concatenate(
            [
                jnp.concatenate([res_re, res_im], 1),
                jnp.concatenate([res_im, -res_re] if sign == 1 else [-res_im, res_re], 1),
            ],
            0,
        )
        both = dot(lhs, rhs)
        return both[:, :span], both[:, span:]

    def add_grad(value):
        folded = value[:, :128]
        for start in range(128, span, 128):
            folded = folded + value[:, start : start + 128]
        total_ref[...] += folded

    def put(res_re, res_im):
        for out_ref in out_refs:
            out_ref[0, 0] = res_re
            out_ref[0, 1] = res_im

    @pl.when(step == 0)
    def _():
        total_ref[...] = jnp.zeros_like(total_ref)

    @pl.when(entry(KIND) != 2)
    def _():
        load(one_ref, ONE_AT)
        load(two_ref, TWO_AT)

    @pl.when(entry(KIND) == 0)
    def _():
        one_re, one_im, two_re, two_im = one_ref[0], one_ref[1], two_ref[0], two_ref[1]
        pred_re, pred_im = cross(*scaled_of(one_re, one_im), two_re, two_im)
        weights = outer(keep_one_ref[...], keep_two_ref[...])
        res_re = (weights * (vis_ref[0, 0, 0, 0].astype(jnp.float32) - pred_re)).astype(jnp.bfloat16)
        res_im = (weights * (vis_ref[0, 0, 0, 1].astype(jnp.float32) - pred_im)).astype(jnp.bfloat16)
        put(res_re, res_im)
        sum_re, sum_im = pull(one_re, one_im, res_re, res_im, 1)
        add_grad(sum_re * two_re.astype(jnp.float32) - sum_im * two_im.astype(jnp.float32))

    @pl.when(entry(KIND) == 1)
    def _():
        one_re, one_im, two_re, two_im = one_ref[0], one_ref[1], two_ref[0], two_ref[1]
        row_ids = lax.broadcasted_iota(jnp.int32, (span, span), 0)
        col_ids = lax.broadcasted_iota(jnp.int32, (span, span), 1)
        upper = row_ids < col_ids
        lower = row_ids > col_ids
        first_re, first_im = cross(*scaled_of(one_re, one_im), one_re, one_im)
        second_re, second_im = cross(two_re, two_im, *scaled_of(two_re, two_im))
        keep_one = keep_one_ref[...]
        keep_two = keep_two_ref[...]
        weights = jnp.where(upper, outer(keep_one, keep_one), 0.0) + jnp.where(
            lower, outer(keep_two, keep_two), 0.0
        )
        vis_re = vis_ref[0, 0, 0, 0].astype(jnp.float32)
        vis_im = vis_ref[0, 0, 0, 1].astype(jnp.float32)
        res_re = (weights * (vis_re - jnp.where(upper, first_re, second_re))).astype(jnp.bfloat16)
        res_im = (weights * (vis_im - jnp.where(upper, first_im, -second_im))).astype(jnp.bfloat16)
        put(res_re, res_im)
        none = jnp.zeros_like(res_re)
        sum_re, sum_im = pull(
            one_re, one_im, jnp.where(upper, res_re, none), jnp.where(upper, res_im, none), 1
        )
        add_grad(sum_re * one_re.astype(jnp.float32) - sum_im * one_im.astype(jnp.float32))
        sum_re, sum_im = pull(
            two_re, two_im, jnp.where(lower, res_re, none), jnp.where(lower, res_im, none), -1
        )
        add_grad(sum_re * two_re.astype(jnp.float32) + sum_im * two_im.astype(jnp.float32))

    @pl.when(step == pl.num_programs(0) - 1)
    def _():
        grad_ref[...] = jnp.sum(total_ref[...].T, axis=0, keepdims=True)


def unit_work(index, steps, table, pieces, vis, keep, bright, outs):
    span = vis.shape[5]
    slots = keep.shape[0]
    sources = sum(number for _, _, number in pieces[0])
    offset, count = steps
    whole = pl.BlockSpec(memory_space=pltpu.VMEM)
    arrays = [array for piece in pieces for entry, _, _ in piece for array in entry]

    def at(tab, step, column):
        return tab[offset + step * COLUMNS + column]

    in_specs = [whole] * len(arrays) + [
        pl.BlockSpec(
            (1, 1, 1, 2, span, span),
            lambda u, tab: (at(tab, u, VIS_AT), at(tab, u, VIS_AT + 1), index, 0, 0, 0),
        ),
        pl.BlockSpec((slots, span), lambda u, tab: (0, at(tab, u, ONE))),
        pl.BlockSpec((slots, span), lambda u, tab: (0, at(tab, u, TWO))),
    ]
    operands = [table, *arrays, vis, keep, keep]
    bright_at = None
    if isinstance(bright, int):
        first = pieces[0][0]
        bright_at = (first[0][0].shape[1] - BRIGHT_ROWS) // first[2]
    else:
        in_specs.append(whole)
        operands.append(bright)
    aliases = {}
    out_specs, out_shapes = [], []
    for out in outs:
        rows = out
        if not isinstance(out, int):
            rows = out.shape[0]
            aliases[len(operands)] = len(out_specs)
            operands.append(out)
            in_specs.append(pl.BlockSpec(memory_space=pl.ANY))
        out_specs.append(
            pl.BlockSpec((1, 2, span, span), lambda u, tab: (at(tab, u, OUT_ROW), 0, 0, 0))
        )
        out_shapes.append(jax.ShapeDtypeStruct((rows, 2, span, span), jnp.bfloat16))
    out_specs.append(pl.BlockSpec((1, sources), lambda u, tab: (0, 0)))
    out_shapes.append(jax.ShapeDtypeStruct((1, sources), jnp.float32))
    if bright_at is not None:
        out_specs.append(pl.BlockSpec((bright, sources, 128), lambda u, tab: (0, 0, 0)))
        out_shapes.append(jax.ShapeDtypeStruct((bright, sources, 128), jnp.float32))
    kinds = [[(len(entry), start, number) for entry, start, number in piece] for piece in pieces]
    return pl.pallas_call(
        functools.partial(unit_kernel, index, offset, kinds, bright_at, len(outs), len(aliases)),
        grid_spec=pltpu.PrefetchScalarGridSpec(
            num_scalar_prefetch=1,
            grid=(count,),
            in_specs=in_specs,
            out_specs=out_specs,
            scratch_shapes=[
                pltpu.VMEM((sources, 128), jnp.float32),
                pltpu.VMEM((2, sources, span), jnp.bfloat16),
                pltpu.VMEM((2, sources, span), jnp.bfloat16),
            ],
        ),
        out_shape=out_shapes,
        input_output_aliases=aliases,
        compiler_params=pltpu.CompilerParams(vmem_limit_bytes=48 * 1024 * 1024),
        cost_estimate=LITTLE,
        name="unit_work",
    )(*operands)


def put_kernel(sources, tab_ref, *refs):
    out_ref = refs[-1]
    for step, (which, row) in enumerate(sources):

        @pl.when(pl.program_id(0) == step)
        def _(which=which, row=row):
            out_ref[0, 0] = refs[which][...] if row is None else refs[which][row]


def put_residuals(sources, arrays, offset, table, shape, residual):
    span = shape[-1]
    whole = pl.BlockSpec(memory_space=pltpu.VMEM)
    operands = [table, *arrays]
    in_specs = [whole] * len(arrays)
    aliases = {}
    if residual is not None:
        aliases = {len(operands): 0}
        operands.append(residual)
        in_specs.append(pl.BlockSpec(memory_space=pl.ANY))
    return pl.pallas_call(
        functools.partial(put_kernel, sources),
        grid_spec=pltpu.PrefetchScalarGridSpec(
            num_scalar_prefetch=1,
            grid=(len(sources),),
            in_specs=in_specs,
            out_specs=pl.BlockSpec(
                (1, 1, 2, span, span),
                lambda n, tab: (tab[offset + 2 * n], tab[offset + 2 * n + 1], 0, 0, 0),
            ),
        ),
        out_shape=jax.ShapeDtypeStruct(shape, jnp.bfloat16),
        input_output_aliases=aliases,
        compiler_params=pltpu.CompilerParams(vmem_limit_bytes=32 * 1024 * 1024),
        cost_estimate=LITTLE,
        name="put_residuals",
    )(*operands)


class Routes:
    def __init__(self, planes, width, units, share):
        count = planes * width
        blocks = int(units[:, :2].max()) + 1
        self.width = width
        self.units_dev = units_dev = units.shape[0] // count
        ring = [0] + list(range(1, planes, 2)) + list(range(planes - 2, 0, -2))

        def along(step):
            at = {plane: ring[(n + step) % planes] for n, plane in enumerate(ring)}
            return [(t, at[t // width] * width + t % width) for t in range(count)]

        self.onward = along(1)
        self.backward = along(-1)
        self.opposite = along(2)
        self.partner = [[(t, t ^ m) for t in range(count)] for m in range(width)]

        touched = [set(units[u, :2].tolist()) for u in range(units.shape[0])]
        home = [list(range(t * units_dev, (t + 1) * units_dev)) for t in range(count)]
        of_plane = [range(z * width * units_dev, (z + 1) * width * units_dev) for z in range(planes)]

        def most(wanted):
            return max(sum(bool(wanted(touched[u])) for u in plane) for plane in of_plane)

        def stuck(block):
            return sum(all(block in touched[u] for u in mine) for mine in home)

        end = min(range(blocks), key=lambda b: most(lambda t: b in t))
        rest = [b for b in range(blocks) if b != end]
        start = min(
            itertools.combinations(rest, blocks * FIRST_PART // 8),
            key=lambda c: most(lambda t: end not in t and not t <= set(c)),
        )
        self.pieces = [list(start), [b for b in rest if b not in start], [end]]
        self.full = [list(range(blocks))]
        events = []
        for blocks_of in touched:
            events.append(max(n for n, piece in enumerate(self.pieces) if blocks_of & set(piece)))

        def rows_of(t, pieces, wanted):
            rows = []
            for m in range(width):
                for n, u in enumerate(home[t ^ m]):
                    if not wanted(u):
                        continue
                    one, two, kind = units[u].tolist()
                    at = [
                        (k, piece.index(b))
                        for b in (one, two)
                        for k, piece in enumerate(pieces)
                        if b in piece
                    ]
                    rows.append([kind, one, two, *at[0], *at[1], m * units_dev + n, m, n])
            return rows

        def table_of(pieces, wanted):
            tables = [rows_of(t, pieces, wanted) for t in range(count)]
            steps = max(len(rows) for rows in tables)
            for rows in tables:
                while len(rows) < steps:
                    rows.append([2] + (rows[-1][1:] if rows else [0] * (COLUMNS - 1)))
                    rows[-1][OUT_ROW] = width * units_dev
            return np.array(tables, np.int32)

        first_table = table_of(self.full, lambda u: True)
        tables = [
            table_of(self.pieces, lambda u, n=n: events[u] == n) for n in range(len(self.pieces))
        ]

        def targets(index):
            rows = np.zeros((count, width, units_dev, 2), np.int32)
            for t in range(count):
                for m in range(width):
                    for n in range(units_dev):
                        rows[t, m, n] = n, (t % width ^ m) * share + index
            return rows

        starts = np.array([[(t % width ^ m) * share for m in range(width)] for t in range(count)])
        parts = [starts, first_table, *tables, *[targets(n) for n in range(share)]]
        parts = [part.reshape(count, -1).astype(np.int32) for part in parts]
        ends = np.cumsum([part.shape[1] for part in parts]).tolist()
        self.table = np.concatenate(parts, 1)
        self.first_steps = (ends[0], first_table.shape[1])
        self.steps = [(ends[1 + n], table.shape[1]) for n, table in enumerate(tables)]
        self.targets = ends[1 + len(tables) :]


FIRST_PART = 4


def packed_small(source_dirs, source_flux, visible_list):
    listed = visible_list.astype(jnp.float32).reshape(1, -1)
    rows = [source_dirs, source_flux.astype(jnp.float32)[None], listed]
    width = max(row.shape[1] for row in rows)
    rows = [jnp.pad(row, ((0, 0), (0, width - row.shape[1]))) for row in rows]
    return jnp.concatenate(rows, 0)


def plain_program(visibility, beam, antenna_uvw, small, keep):
    units_dev, slots, _, span, _ = visibility.shape
    _, _, per_group, antennas = beam.shape
    blocks = antennas // span
    tile_index = lax.axis_index("tile")
    units = unit_table(blocks)
    own_rows = np.tile(np.arange(units_dev), units.shape[0] // units_dev)
    none = np.zeros_like(own_rows)
    table = np.stack(
        [units[:, 2], units[:, 0], units[:, 1], none, units[:, 0], none, units[:, 1]]
        + [own_rows, none, own_rows],
        1,
    )
    table = table.astype(np.int32).reshape(-1, units_dev * COLUMNS)
    table = np.pad(table, ((0, 0), (1, 0)))
    table = lax.dynamic_index_in_dim(jnp.asarray(table), tile_index, 0, keepdims=False)
    columns = None
    residuals, grads = [], []
    for slot in range(slots):
        (owned,) = build_factors(
            (slot, slots, per_group),
            table,
            beam,
            [],
            antenna_uvw,
            [small],
            [list(range(blocks))],
            span,
            0 if slot else BRIGHT_ROWS,
            small.shape[1],
        )
        everyone = lax.all_gather(owned, "tile", axis=0)
        rows = blocks * per_group
        if columns is None:
            bright = everyone[:, 0, rows : rows + slots, :per_group].astype(jnp.float32)
            bright = jnp.swapaxes(bright, 0, 1).reshape(slots, -1, 1)
            columns = jnp.broadcast_to(bright, bright.shape[:2] + (128,))
        factors = everyone[:, :, :rows].reshape(-1, 2, blocks, per_group, span)
        number = factors.shape[0] * per_group
        factors = factors.transpose(1, 2, 0, 3, 4).reshape(2, blocks * number, span)
        residual, grad = unit_work(
            slot,
            (1, units_dev),
            table,
            [[((factors,), 0, number)]],
            visibility[None],
            keep,
            columns,
            [units_dev],
        )
        residuals.append(residual)
        grads.append(grad)
    summed = lax.psum_scatter(jnp.concatenate(grads, 0), "tile", scatter_dimension=1, tiled=True)
    return jnp.stack(residuals, 1), summed


GATES = {
    "own": (),
}


def plane_program(routes, visibility, beam, antenna_uvw, small, keep):
    units_dev, slots, _, span, _ = visibility.shape
    per_group = beam.shape[2]
    width = routes.width
    share = slots // width
    group = width * per_group
    tile_index = lax.axis_index("tile")
    mine = tile_index % width
    others = range(1, width)
    table = lax.dynamic_index_in_dim(jnp.asarray(routes.table), tile_index, 0, keepdims=False)
    done = {}

    def gated(name, value):
        earlier = [done[gate] for gate in GATES.get(name, ())]
        return lax.optimization_barrier((value, *earlier))[0] if earlier else value

    def send(name, value, pairs):
        done[name] = lax.ppermute(gated(name, value), "tile", pairs)
        return done[name]

    def near(name, piece):
        return [
            send(name + " onward", piece, routes.onward),
            send(name + " backward", piece, routes.backward),
        ]

    def far(name, sides):
        return [
            send(name + " onward", sides[0][0], routes.onward),
            send(name + " backward", sides[1][1], routes.backward),
        ]

    def entries(piece, sides, halves, first, number):
        found = [(piece,), (sides[0],), (sides[1],), tuple(halves)]
        return [(arrays, n * group + first, number) for n, arrays in enumerate(found)]

    def sent_home(name, results):
        parts = [results[m * units_dev : (m + 1) * units_dev] for m in others]
        return [send(f"{name} {m}", part, routes.partner[m]) for m, part in zip(others, parts)]

    first_slot = (0, share, per_group)
    (own,) = build_factors(
        first_slot,
        gated("own", table),
        beam,
        [],
        antenna_uvw,
        [small],
        routes.full,
        span,
        BRIGHT_ROWS,
        small.shape[1],
    )
    done["own"] = own
    own_sides = near("own near", own)
    messages = messages_for(beam, 0, others, small, gated("beams", table))
    messages = [send(f"beams {m}", messages[m - 1], routes.partner[m]) for m in others]
    own_far = far("own far", own_sides)
    (rest,) = build_factors(
        first_slot,
        gated("rest", table),
        None,
        messages,
        antenna_uvw,
        messages,
        routes.full,
        span,
        BRIGHT_ROWS,
        small.shape[1],
    )
    done["rest"] = rest
    rest_sides = near("rest near", rest)

    later = messages_for(beam, 1, others, None, gated("later beams", table))
    later = [send(f"later beams {m}", later[m - 1], routes.partner[m]) for m in others]
    vis = slices_for(
        visibility, 1, share, [(m, 0) for m in range(width)], gated("vis", table)
    )
    vis = [vis[0]] + [send(f"vis {m}", vis[m], routes.partner[m]) for m in others]
    later_pieces = build_factors(
        (1, share, per_group),
        gated("later", table),
        beam,
        later,
        antenna_uvw,
        [small, *messages],
        routes.pieces,
        span,
        0,
        small.shape[1],
    )
    rest_far = far("rest far", rest_sides)
    near_0 = near("piece 0 near", later_pieces[0])
    near_1 = near("piece 1 near", later_pieces[1])
    far_0 = far("piece 0 far", near_0)

    vis = jnp.stack(vis, 0)
    pieces = entries(own, own_sides, own_far, 0, per_group)
    pieces += entries(rest, rest_sides, rest_far, per_group, group - per_group)
    results, grad, columns = unit_work(
        0,
        routes.first_steps,
        gated("work", table),
        [pieces],
        vis,
        keep,
        share,
        [width * units_dev],
    )
    done["work"] = grad
    grads = [grad]
    home = sent_home("home", results)
    far_1 = far("piece 1 far", near_1)
    near_2 = near("piece 2 near", later_pieces[2])
    far_2 = far("piece 2 far", near_2)
    ready = [
        entries(piece, sides, halves, 0, group)
        for piece, sides, halves in zip(
            later_pieces, (near_0, near_1, near_2), (far_0, far_1, far_2)
        )
    ]
    pairs = [(m, n) for m in range(width) for n in range(units_dev)]
    residual = put_residuals(
        pairs, [results, *home], routes.targets[0], gated("put", table), visibility.shape, None
    )
    done["put"] = residual

    results = width * units_dev + 1
    for n, steps in enumerate(routes.steps):
        results, grad = unit_work(
            1,
            steps,
            gated(f"work {n}", table),
            ready[: n + 1],
            vis,
            keep,
            columns,
            [results],
        )
        done[f"work {n}"] = grad
        grads.append(grad)
    returned = sent_home("later home", results)

    partial = jnp.concatenate([grads[0], sum(grads[2:], grads[1])], 0)
    parts = [partial[:, n * group : (n + 1) * group] for n in range(4)]
    plane_sum = (parts[0] + send("sum opposite", parts[3], routes.opposite)) + (
        send("sum backward", parts[1], routes.backward)
        + send("sum onward", parts[2], routes.onward)
    )
    sums = [plane_sum[:, m * per_group : (m + 1) * per_group] for m in range(width)]
    sums = [sums[0]] + [send(f"sum {m}", sums[m], routes.partner[m]) for m in others]
    sums = jnp.stack(sums, 0)
    ids = jnp.arange(width, dtype=jnp.int32)
    here = jnp.bitwise_xor(ids[:, None], mine) == ids[None, :]
    summed = jnp.sum(jnp.where(here[:, :, None, None], sums[None], 0.0), axis=1)
    summed = summed.reshape(slots, per_group)

    residual = put_residuals(
        pairs,
        [results, *returned],
        routes.targets[1],
        gated("later put", table),
        visibility.shape,
        residual,
    )
    return residual, summed


def per_device(
    visibility, station_beam, antenna_uvw, source_dirs, source_flux, visible_list, antenna_flags
):
    span = visibility.shape[4]
    antennas = station_beam.shape[3]
    small = packed_small(source_dirs, source_flux, visible_list)
    keep = 1.0 - antenna_flags.astype(jnp.float32)
    arguments = (visibility, station_beam, antenna_uvw, small, keep)
    if lax.axis_size("tile") == 16:
        routes = Routes(4, 4, unit_table(antennas // span), visibility.shape[1] // 4)
        residual, summed = plane_program(routes, *arguments)
    else:
        residual, summed = plain_program(*arguments)
    return (residual, summed * (-1.0 / (8.0 * antennas)))


def solution(mesh):
    return jax.shard_map(
        per_device,
        mesh=mesh,
        in_specs=(
            P("tile", "grp", None, None, None),
            P("grp", None, "tile", None),
            P("grp", None, None),
            P(None, "tile"),
            P(("grp", "tile")),
            P(None, "tile"),
            P("grp", None),
        ),
        out_specs=(P("tile", "grp", None, None, None), P("grp", "tile")),
        check_vma=False,
    )
```

time: 277 us -> 274 us (0.989)
  starting transfers between devices: 51 us -> 42.4 us
  waiting for transfers between devices: 155 us -> 162 us
    ppermute x50 -> x41, starting transfers between devices: 51 us -> 42.4 us  [send(): done[name] = lax.ppermute(gated(name, value), 'tile', pairs)]
    pallas_call x7 -> x9, Pallas kernels: 33.3 us -> 40.7 us  [the longest x4 27.6 us: unit_work(): pl.pallas_call(functools.partial(unit_kernel, index, offset, kinds, brigh...]
    ppermute x50 -> x41, waiting for transfers between devices: 155 us -> 162 us  [send(): done[name] = lax.ppermute(gated(name, value), 'tile', pairs)]
    pallas_call x3 -> x1, Pallas kernels: 9.94 us -> 4.55 us  [slices_for(): pl.pallas_call(functools.partial(slice_kernel, len(starts)), grid_spec=pl...]
    unnamed x60 -> x41, local copies, waits for them, and re-layouts: 9.59 us -> 7.39 us
    pallas_call x3 -> x2, Pallas kernels: 7.9 us -> 7.27 us  [put_residuals(): pl.pallas_call(functools.partial(put_kernel, sources), grid_spec=pltpu.Pr...]
  transfers between devices with their start and end apart: 50 -> 41, of which waited for: 20 -> 12; matrix products, arithmetic and copies ran while one was open for 2% -> 2% of each run, Pallas kernels for 14% -> 15%
where the time goes in v5:
time: 274 us; the launch traced here: 273 us
  waiting for transfers between devices  162 us (59%)
  Pallas kernels  52.5 us (19%)
  starting transfers between devices  42.4 us (15%)
  local copies, waits for them, and re-layouts  10.4 us (4%)
  other arithmetic  5.12 us (2%)
    ppermute x41, waiting for transfers between devices, send(): done[name] = lax.ppermute(gated(name, value), 'tile', pairs)  162 us
    ppermute x41, starting transfers between devices, send(): done[name] = lax.ppermute(gated(name, value), 'tile', pairs)  42.4 us
    pallas_call x4, Pallas kernels, unit_work(): pl.pallas_call(functools.partial(unit_kernel, index, offset, kinds, brigh...  27.6 us
    pallas_call x3, Pallas kernels, build_factors(): pl.pallas_call(functools.partial(build_kernel, sets, slot_ids, pieces, br...  7.62 us
    unnamed x41, local copies, waits for them, and re-layouts  7.39 us
    pallas_call x2, Pallas kernels, put_residuals(): pl.pallas_call(functools.partial(put_kernel, sources), grid_spec=pltpu.Pr...  7.27 us
    pallas_call x2, Pallas kernels, messages_for(): pl.pallas_call(functools.partial(message_kernel, per_group), grid_spec=pl...  5.5 us
  transfers between devices with their start and end apart: 41, of which 12 were waited for; matrix products, arithmetic and copies ran while one was open for 2% of the time, Pallas kernels for 15%

profile of v5, /device:TPU:0, one launch (start us, length us, event | category | flops | bytes accessed | tf_op | source)
XLA Modules:
  0.0 273.2 jit_solution(17599826124687329596)
XLA Ops:
  2.1 1.1 copy.16.refs_8_.refs_2_.refs_3_
  4.5 1.6 copy-done
  6.1 1.9 build_factors.4.refs_0_
  8.0 3.0 %collective-permute-start.21 = (bf16[2,272,256]{2,1,0:T(8,128)(2,1)}, bf16[2,272,256]{2,1,0:T(8,128)(2,1)S(1)}, u32[]{:S(2)}, u32[]{:S(2)}) collective-permute-start(bf16[2,272,256]{2,1,0:T(8,128)(2,1)} %build_factors.4.refs_0_), channel_id=1, source_target_pairs={{0,4},{1,5},{2,6},{3,7},{4,12},{5,13},{6,14},{7,15},{8,0},{9,1},{1... | collective-permute-start | bytes 835592 | tf_op jit(solution)/shard_map/ppermute | solution.py:676
  11.0 2.7 messages_for.2
  13.7 1.6 collective-permute-start.1
  15.3 1.3 collective-permute-start.22
  16.7 2.8 %messages_for.3 = (bf16[80,2048]{1,0:T(8,128)(2,1)}, bf16[80,2048]{1,0:T(8,128)(2,1)}, bf16[80,2048]{1,0:T(8,128)(2,1)}) custom-call(s32[226]{0:T(256)} %bitcast.34, bf16[8,2,32,2048]{3,2,1,0:T(8,128)(2,1)} %refs_0_.9, bf16[8,2,32,2048]{3,2,1,0:T(8,128)(2,1)} %refs_0_.9, bf16[8,2,32,2048]{3,2,1,0:T(8,128)(2,1)} %refs_0_.9, f32[4,256]{1,0:T(4,128)} %copy-done.13), custom_call_target="tpu_custom_call" | custom-call | flops 1 | bytes 1 | tf_op jit(solution)/shard_map/messages_for/pallas_call | solution.py:184
  20.4 2.3 collective-permute-done.1.refs_2_
  25.2 4.5 %slices_for.1 = (bf16[2,2,2,256,256]{4,3,2,1,0:T(8,128)(2,1)}, bf16[2,2,2,256,256]{4,3,2,1,0:T(8,128)(2,1)}, bf16[2,2,2,256,256]{4,3,2,1,0:T(8,128)(2,1)}, bf16[2,2,2,256,256]{4,3,2,1,0:T(8,128)(2,1)}) custom-call(s32[226]{0:T(256)} %bitcast.35, bf16[2,8,2,256,256]{4,3,2,1,0:T(8,128)(2,1)} %refs_3_.2, bf16[2,8,2,256,256]{4,3,2,1,0:T(8,128)(2,1)} %refs_3_.2, ...), custom_call_target="tpu_custom_call" | custom-call | flops 1 | bytes 1 | tf_op jit(solution)/shard_map/slices_for/pallas_call | solution.py:214
  30.6 12.2 %collective-permute-done.2.refs_3_ = bf16[64,2048]{1,0:T(8,128)(2,1)} collective-permute-done((bf16[64,2048]{1,0:T(8,128)(2,1)}, bf16[64,2048]{1,0:T(8,128)(2,1)}, u32[]{:S(2)}, u32[]{:S(2)}) %collective-permute-start.2) | collective-permute-done | bytes 262176 | tf_op jit(solution)/shard_map/ppermute | solution.py:676
  42.9 1.7 collective-permute-start.23
  44.6 0.9 copy-done.8
  45.5 0.9 copy-done.10
  46.5 3.7 %build_factors.3 = (bf16[2,512,256]{2,1,0:T(8,128)(2,1)S(1)}, bf16[2,384,256]{2,1,0:T(8,128)(2,1)S(1)}, bf16[2,128,256]{2,1,0:T(8,128)(2,1)S(1)}) custom-call(s32[226]{0:T(256)S(1)} %bitcast.36, bf16[8,2,32,2048]{3,2,1,0:T(8,128)(2,1)S(1)} %copy-done.1, bf16[64,2048]{1,0:T(8,128)(2,1)S(1)} %copy-done.8, bf16[64,2048]{1,0:T(8,128)(2,1)S(1)} %copy-done.10, ...), custom_call_target="tpu_custom_call" | custom-call | flops 1 | bytes 1 | tf_op jit(solution)/shard_map/build_factors/pallas_call | solution.py:146
  50.2 2.5 collective-permute-start.14
  52.8 0.9 slice_bitcast_fusion.6
  54.2 2.1 build_factors.5.refs_5_
  56.2 1.6 collective-permute-start.25
  59.1 2.6 collective-permute-start.24
  61.8 1.1 collective-permute-start.11
  62.9 36.5 %collective-permute-done.24.refs_4_ = bf16[272,256]{1,0:T(8,128)(2,1)S(1)} collective-permute-done((bf16[272,256]{1,0:T(8,128)(2,1)S(1)}, bf16[272,256]{1,0:T(8,128)(2,1)S(1)}, u32[]{:S(2)}, u32[]{:S(2)}) %collective-permute-start.24) | collective-permute-done | bytes 139296 | tf_op jit(solution)/shard_map/ppermute | solution.py:676
  100.0 25.2 %collective-permute-done.10.refs_6_ = bf16[2,384,256]{2,1,0:T(8,128)(2,1)S(1)} collective-permute-done((bf16[2,384,256]{2,1,0:T(8,128)(2,1)S(1)}, bf16[2,384,256]{2,1,0:T(8,128)(2,1)S(1)}, u32[]{:S(2)}, u32[]{:S(2)}) %collective-permute-start.10) | collective-permute-done | bytes 393248 | tf_op jit(solution)/shard_map/ppermute | solution.py:676
  125.3 1.3 collective-permute-start.18
  126.8 23.9 %collective-permute-done.26.refs_7_ = bf16[2,784,256]{2,1,0:T(8,128)(2,1)S(1)} collective-permute-done((bf16[2,784,256]{2,1,0:T(8,128)(2,1)S(1)}, bf16[2,784,256]{2,1,0:T(8,128)(2,1)S(1)}, u32[]{:S(2)}, u32[]{:S(2)}) %collective-permute-start.26) | collective-permute-done | bytes 802848 | tf_op jit(solution)/shard_map/ppermute | solution.py:676
  150.8 16.8 %collective-permute-done.7.refs_2_ = bf16[2,512,256]{2,1,0:T(8,128)(2,1)S(1)} collective-permute-done((bf16[2,512,256]{2,1,0:T(8,128)(2,1)S(1)}, bf16[2,512,256]{2,1,0:T(8,128)(2,1)S(1)}, u32[]{:S(2)}, u32[]{:S(2)}) %collective-permute-start.7) | collective-permute-done | bytes 524320 | tf_op jit(solution)/shard_map/ppermute | solution.py:676
  167.6 2.9 %collective-permute-start.28 = (bf16[784,256]{1,0:T(8,128)(2,1)S(1)}, bf16[784,256]{1,0:T(8,128)(2,1)S(1)}, u32[]{:S(2)}, u32[]{:S(2)}) collective-permute-start(bf16[784,256]{1,0:T(8,128)(2,1)S(1)} %slice_bitcast_fusion), channel_id=1, source_target_pairs={{0,8},{1,9},{2,10},{3,11},{4,0},{5,1},{6,2},{7,3},{8,12},{9,13},{1... | collective-permute-start | bytes 1204232 | tf_op jit(solution)/shard_map/ppermute | solution.py:676
  170.6 2.9 %collective-permute-start.13 = (bf16[384,256]{1,0:T(8,128)(2,1)S(1)}, bf16[384,256]{1,0:T(8,128)(2,1)S(1)}, u32[]{:S(2)}, u32[]{:S(2)}) collective-permute-start(bf16[384,256]{1,0:T(8,128)(2,1)S(1)} %slice_bitcast_fusion.4), channel_id=1, source_target_pairs={{0,8},{1,9},{2,10},{3,11},{4,0},{5,1},{6,2},{7,3},{8,12},{9,13},{1... | collective-permute-start | bytes 589832 | tf_op jit(solution)/shard_map/ppermute | solution.py:676
  173.6 2.3 pad_maximum_fusion.refs_10_.refs_5_.refs_15_
  175.9 8.8 %collective-permute-done.27.refs_8_ = bf16[784,256]{1,0:T(8,128)(2,1)S(1)} collective-permute-done((bf16[784,256]{1,0:T(8,128)(2,1)S(1)}, bf16[784,256]{1,0:T(8,128)(2,1)S(1)}, u32[]{:S(2)}, u32[]{:S(2)}) %collective-permute-start.27) | collective-permute-done | bytes 401440 | tf_op jit(solution)/shard_map/ppermute | solution.py:676
  184.7 2.9 %collective-permute-start.17 = (bf16[128,256]{1,0:T(8,128)(2,1)S(1)}, bf16[128,256]{1,0:T(8,128)(2,1)S(1)}, u32[]{:S(2)}, u32[]{:S(2)}) collective-permute-start(bf16[128,256]{1,0:T(8,128)(2,1)S(1)} %slice_bitcast_fusion.8), channel_id=1, source_target_pairs={{0,8},{1,9},{2,10},{3,11},{4,0},{5,1},{6,2},{7,3},{8,12},{9,13},{1... | collective-permute-start | bytes 196616 | tf_op jit(solution)/shard_map/ppermute | solution.py:676
  187.7 11.6 %unit_work.4 = (bf16[8,2,256,256]{3,2,1,0:T(8,128)(2,1)}, f32[1,512]{1,0:T(1,128)S(1)}, f32[2,512,128]{2,1,0:T(8,128)S(1)}) custom-call(s32[226]{0:T(256)S(1)} %bitcast.38, bf16[2,272,256]{2,1,0:T(8,128)(2,1)} %build_factors.4.refs_0_, bf16[2,272,256]{2,1,0:T(8,128)(2,1)S(1)} %copy-done.6, bf16[2,272,256]{2,1,0:T(8,128)(2,1)} %collective-permute-done.22.refs_2_, ...), custom_call_target="tpu_custom_call" | custom-call | flops 1 | bytes 1 | tf_op jit(solution)/shard_map/unit_work/pallas_call | solution.py:441
  199.2 4.9 %unit_work.5 = (bf16[9,2,256,256]{3,2,1,0:T(8,128)(2,1)S(1)}, f32[1,512]{1,0:T(1,128)S(1)}) custom-call(s32[226]{0:T(256)S(1)} %bitcast.39, bf16[2,512,256]{2,1,0:T(8,128)(2,1)S(1)} %get-tuple-element.30.refs_0_, bf16[2,512,256]{2,1,0:T(8,128)(2,1)S(1)} %collective-permute-done.6.refs_1_, bf16[2,512,256]{2,1,0:T(8,128)(2,1)S(1)} %collective-permute-done.7.refs_2_, ...), custom_call_target="tpu_custom_call" | custom-call | flops 1 | bytes 1 | tf_op jit(solution)/shard_map/unit_work/pallas_call | solution.py:441
  204.2 1.4 copy-done.2
  205.6 6.4 %unit_work.6 = (bf16[9,2,256,256]{3,2,1,0:T(8,128)(2,1)}, f32[1,512]{1,0:T(1,128)S(1)}) custom-call(s32[226]{0:T(256)S(1)} %bitcast.40, bf16[2,512,256]{2,1,0:T(8,128)(2,1)S(1)} %get-tuple-element.30.refs_0_, bf16[2,512,256]{2,1,0:T(8,128)(2,1)S(1)} %collective-permute-done.6.refs_1_, ...), custom_call_target="tpu_custom_call", output_to_operand_aliasing={{0}: (15, {})} | custom-call | flops 1 | bytes 1 | tf_op jit(solution)/shard_map/unit_work/pallas_call | solution.py:441
  212.0 4.7 %unit_work.7 = (bf16[9,2,256,256]{3,2,1,0:T(8,128)(2,1)}, f32[1,512]{1,0:T(1,128)S(1)}) custom-call(s32[226]{0:T(256)S(1)} %bitcast.41, bf16[2,512,256]{2,1,0:T(8,128)(2,1)S(1)} %get-tuple-element.30.refs_0_, bf16[2,512,256]{2,1,0:T(8,128)(2,1)S(1)} %collective-permute-done.6.refs_1_, ...), custom_call_target="tpu_custom_call", output_to_operand_aliasing={{0}: (20, {})} | custom-call | flops 1 | bytes 1 | tf_op jit(solution)/shard_map/unit_work/pallas_call | solution.py:441
  216.7 3.0 %collective-permute-start.35 = (f32[2,128]{1,0:T(2,128)S(1)}, f32[2,128]{1,0:T(2,128)S(1)}, u32[]{:S(2)}, u32[]{:S(2)}) collective-permute-start(f32[2,128]{1,0:T(2,128)S(1)} %get-tuple-element.52), channel_id=1, source_target_pairs={{0,12},{1,13},{2,14},{3,15},{4,8},{5,9},{6,10},{7,11},{8,4},{9,5},... | collective-permute-start | bytes 3080 | tf_op jit(solution)/shard_map/ppermute | solution.py:676
  219.7 2.0 collective-permute-start.37
  222.0 1.8 collective-permute-start.33
  224.4 1.8 collective-permute-start.39
  226.4 1.6 collective-permute-start.34
  227.9 8.9 %collective-permute-done.39 = f32[2,32]{1,0:T(2,128)S(1)} collective-permute-done((f32[2,32]{1,0:T(2,128)S(1)}, f32[2,32]{1,0:T(2,128)S(1)}, u32[]{:S(2)}, u32[]{:S(2)}) %collective-permute-start.39) | collective-permute-done | bytes 288 | tf_op jit(solution)/shard_map/ppermute | solution.py:676
  236.8 1.7 collective-permute-start.30
  239.5 7.8 %collective-permute-done.34.refs_3_ = bf16[2,2,256,256]{3,2,1,0:T(8,128)(2,1)S(1)} collective-permute-done((bf16[2,2,256,256]{3,2,1,0:T(8,128)(2,1)S(1)}, bf16[2,2,256,256]{3,2,1,0:T(8,128)(2,1)S(1)}, u32[]{:S(2)}, u32[]{:S(2)}) %collective-permute-start.34) | collective-permute-done | bytes 524320 | tf_op jit(solution)/shard_map/ppermute | solution.py:676
  247.2 3.6 %put_residuals.2.refs_4_ = bf16[2,8,2,256,256]{4,3,2,1,0:T(8,128)(2,1)} custom-call(s32[226]{0:T(256)S(1)} %bitcast.42, bf16[8,2,256,256]{3,2,1,0:T(8,128)(2,1)S(1)} %copy-done.4, bf16[2,2,256,256]{3,2,1,0:T(8,128)(2,1)S(1)} %collective-permute-done.32.refs_1_, bf16[2,2,256,256]{3,2,1,0:T(8,128)(2,1)S(1)} %collective-permute-done.33.refs_2_, ...), custom_call_target="tpu_custom_call" | custom-call | flops 1 | bytes 1 | tf_op jit(solution)/shard_map/put_residuals/pallas_call | solution.py:481
  250.9 8.4 %collective-permute-done.30.refs_2_ = bf16[2,2,256,256]{3,2,1,0:T(8,128)(2,1)S(1)} collective-permute-done((bf16[2,2,256,256]{3,2,1,0:T(8,128)(2,1)S(1)}, bf16[2,2,256,256]{3,2,1,0:T(8,128)(2,1)S(1)}, u32[]{:S(2)}, u32[]{:S(2)}) %collective-permute-start.30) | collective-permute-done | bytes 524320 | tf_op jit(solution)/shard_map/ppermute | solution.py:676
  259.3 10.3 %collective-permute-done.31.refs_3_ = bf16[2,2,256,256]{3,2,1,0:T(8,128)(2,1)S(1)} collective-permute-done((bf16[2,2,256,256]{3,2,1,0:T(8,128)(2,1)S(1)}, bf16[2,2,256,256]{3,2,1,0:T(8,128)(2,1)S(1)}, u32[]{:S(2)}, u32[]{:S(2)}) %collective-permute-start.31) | collective-permute-done | bytes 524320 | tf_op jit(solution)/shard_map/ppermute | solution.py:676
  269.6 3.6 %put_residuals.3 = bf16[2,8,2,256,256]{4,3,2,1,0:T(8,128)(2,1)} custom-call(s32[226]{0:T(256)S(1)} %bitcast.43, bf16[9,2,256,256]{3,2,1,0:T(8,128)(2,1)S(1)} %copy-done.3, bf16[2,2,256,256]{3,2,1,0:T(8,128)(2,1)S(1)} %collective-permute-done.29.refs_1_, bf16[2,2,256,256]{3,2,1,0:T(8,128)(2,1)S(1)} %collective-permute-done.30.refs_2_, ...), custom_call_target="tpu_custom_call", output_to_operand_aliasing={{}: (5, {})} | custom-call | flops 1 | bytes 1 | tf_op jit(solution)/shard_map/put_residuals/pallas_call | solution.py:481
  (116 shorter events, 11.9 us)
Async XLA Ops:
  8.0 16.2 %collective-permute-start.21 = (bf16[2,272,256]{2,1,0:T(8,128)(2,1)}, bf16[2,272,256]{2,1,0:T(8,128)(2,1)S(1)}, u32[]{:S(2)}, u32[]{:S(2)}) collective-permute-start(bf16[2,272,256]{2,1,0:T(8,128)(2,1)} %build_factors.4.refs_0_), channel_id=1, source_target_pairs={{0,4},{1,5},{2,6},{3,7},{4,12},{5,13},{6,14},{7,15},{8,0},{9,1},{1... | collective-permute-start | bytes 835592 | tf_op jit(solution)/shard_map/ppermute | solution.py:676
  13.7 5.7 %collective-permute-start = (bf16[64,2048]{1,0:T(8,128)(2,1)}, bf16[64,2048]{1,0:T(8,128)(2,1)S(1)}, u32[]{:S(2)}, u32[]{:S(2)}) collective-permute-start(bf16[64,2048]{1,0:T(8,128)(2,1)} %get-tuple-element.24), channel_id=1, source_target_pairs={{0,1},{1,0},{2,3},{3,2},{4,5},{5,4},{6,7},{7,6},{8,9},{9,8},{10,11... | collective-permute-start | bytes 786440 | tf_op jit(solution)/shard_map/ppermute | solution.py:676
  13.7 8.9 %collective-permute-start.1 = (bf16[64,2048]{1,0:T(8,128)(2,1)}, bf16[64,2048]{1,0:T(8,128)(2,1)S(1)}, u32[]{:S(2)}, u32[]{:S(2)}) collective-permute-start(bf16[64,2048]{1,0:T(8,128)(2,1)} %get-tuple-element.25), channel_id=1, source_target_pairs={{0,2},{1,3},{2,0},{3,1},{4,6},{5,7},{6,4},{7,5},{8,10},{9,11},{10,... | collective-permute-start | bytes 786440 | tf_op jit(solution)/shard_map/ppermute | solution.py:676
  15.3 37.4 %collective-permute-start.22 = (bf16[2,272,256]{2,1,0:T(8,128)(2,1)}, bf16[2,272,256]{2,1,0:T(8,128)(2,1)}, u32[]{:S(2)}, u32[]{:S(2)}) collective-permute-start(bf16[2,272,256]{2,1,0:T(8,128)(2,1)} %build_factors.4.refs_0_), channel_id=1, source_target_pairs={{0,8},{1,9},{2,10},{3,11},{4,0},{5,1},{6,2},{7,3},{8,12},{9,13},{1... | collective-permute-start | bytes 835592 | tf_op jit(solution)/shard_map/ppermute | solution.py:676
  19.5 25.1 %collective-permute-start.3 = (bf16[80,2048]{1,0:T(8,128)(2,1)}, bf16[80,2048]{1,0:T(8,128)(2,1)S(1)}, u32[]{:S(2)}, u32[]{:S(2)}) collective-permute-start(bf16[80,2048]{1,0:T(8,128)(2,1)} %get-tuple-element.27), channel_id=1, source_target_pairs={{0,1},{1,0},{2,3},{3,2},{4,5},{5,4},{6,7},{7,6},{8,9},{9,8},{10,11... | collective-permute-start | bytes 983048 | tf_op jit(solution)/shard_map/ppermute | solution.py:676
  20.2 24.4 %collective-permute-start.4 = (bf16[80,2048]{1,0:T(8,128)(2,1)}, bf16[80,2048]{1,0:T(8,128)(2,1)S(1)}, u32[]{:S(2)}, u32[]{:S(2)}) collective-permute-start(bf16[80,2048]{1,0:T(8,128)(2,1)} %get-tuple-element.28), channel_id=1, source_target_pairs={{0,2},{1,3},{2,0},{3,1},{4,6},{5,7},{6,4},{7,5},{8,10},{9,11},{10,... | collective-permute-start | bytes 983048 | tf_op jit(solution)/shard_map/ppermute | solution.py:676
  23.4 21.2 %collective-permute-start.5 = (bf16[80,2048]{1,0:T(8,128)(2,1)}, bf16[80,2048]{1,0:T(8,128)(2,1)S(1)}, u32[]{:S(2)}, u32[]{:S(2)}) collective-permute-start(bf16[80,2048]{1,0:T(8,128)(2,1)} %get-tuple-element.29), channel_id=1, source_target_pairs={{0,3},{1,2},{2,1},{3,0},{4,7},{5,6},{6,5},{7,4},{8,11},{9,10},{10,... | collective-permute-start | bytes 983048 | tf_op jit(solution)/shard_map/ppermute | solution.py:676
  24.2 18.6 %collective-permute-start.2 = (bf16[64,2048]{1,0:T(8,128)(2,1)}, bf16[64,2048]{1,0:T(8,128)(2,1)}, u32[]{:S(2)}, u32[]{:S(2)}) collective-permute-start(bf16[64,2048]{1,0:T(8,128)(2,1)} %get-tuple-element.26), channel_id=1, source_target_pairs={{0,3},{1,2},{2,1},{3,0},{4,7},{5,6},{6,5},{7,4},{8,11},{9,10},{10,... | collective-permute-start | bytes 786440 | tf_op jit(solution)/shard_map/ppermute | solution.py:676
  25.1 19.4 %copy-start.1 = (bf16[8,2,32,2048]{3,2,1,0:T(8,128)(2,1)S(1)}, bf16[8,2,32,2048]{3,2,1,0:T(8,128)(2,1)}, u32[]{:S(2)}) copy-start(bf16[8,2,32,2048]{3,2,1,0:T(8,128)(2,1)} %refs_0_.9) | copy-start | bytes 6291460
  25.1 19.4 %copy-start.12 = (s32[1,226]{1,0:T(1,128)S(1)}, s32[1,226]{1,0:T(1,128)}, u32[]{:S(2)}) copy-start(s32[1,226]{1,0:T(1,128)} %copy-done.11) | copy-start | bytes 2716
  25.1 19.4 %copy-start.14 = (f32[4,256]{1,0:T(4,128)S(1)}, f32[4,256]{1,0:T(4,128)}, u32[]{:S(2)}) copy-start(f32[4,256]{1,0:T(4,128)} %copy-done.13) | copy-start | bytes 12292
  42.9 16.3 %collective-permute-start.23 = (bf16[272,256]{1,0:T(8,128)(2,1)S(1)}, bf16[272,256]{1,0:T(8,128)(2,1)S(1)}, u32[]{:S(2)}, u32[]{:S(2)}) collective-permute-start(bf16[272,256]{1,0:T(8,128)(2,1)S(1)} %slice_bitcast_fusion.7), channel_id=1, source_target_pairs={{0,4},{1,5},{2,6},{3,7},{4,12},{5,13},{6,14},{7,15},{8,0},{9,1},{1... | collective-permute-start | bytes 417800 | tf_op jit(solution)/shard_map/ppermute | solution.py:676
  46.5 52.9 %copy-start.19 = (bf16[2,2,2,256,256]{4,3,2,1,0:T(8,128)(2,1)S(1)}, bf16[2,2,2,256,256]{4,3,2,1,0:T(8,128)(2,1)}, u32[]{:S(2)}) copy-start(bf16[2,2,2,256,256]{4,3,2,1,0:T(8,128)(2,1)} %get-tuple-element.35) | copy-start | bytes 3145732
  46.5 78.7 %copy-start.18 = (bf16[2,2,2,256,256]{4,3,2,1,0:T(8,128)(2,1)S(1)}, bf16[2,2,2,256,256]{4,3,2,1,0:T(8,128)(2,1)}, u32[]{:S(2)}) copy-start(bf16[2,2,2,256,256]{4,3,2,1,0:T(8,128)(2,1)} %get-tuple-element.36) | copy-start | bytes 3145732
  46.5 78.8 %copy-start.17 = (bf16[2,2,2,256,256]{4,3,2,1,0:T(8,128)(2,1)S(1)}, bf16[2,2,2,256,256]{4,3,2,1,0:T(8,128)(2,1)}, u32[]{:S(2)}) copy-start(bf16[2,2,2,256,256]{4,3,2,1,0:T(8,128)(2,1)} %get-tuple-element.34) | copy-start | bytes 3145732
  46.5 127.1 %copy-start.15 = (bf16[2,2,2,256,256]{4,3,2,1,0:T(8,128)(2,1)S(1)}, bf16[2,2,2,256,256]{4,3,2,1,0:T(8,128)(2,1)}, u32[]{:S(2)}) copy-start(bf16[2,2,2,256,256]{4,3,2,1,0:T(8,128)(2,1)} %get-tuple-element.33) | copy-start | bytes 3145732
  50.2 8.6 %collective-permute-start.14 = (bf16[2,128,256]{2,1,0:T(8,128)(2,1)S(1)}, bf16[2,128,256]{2,1,0:T(8,128)(2,1)S(1)}, u32[]{:S(2)}, u32[]{:S(2)}) collective-permute-start(bf16[2,128,256]{2,1,0:T(8,128)(2,1)S(1)} %get-tuple-element.32.refs_10_), channel_id=1, source_target_pairs={{0,4},{1,5},{2,6},{3,7},{4,12},{5,13},{6,14},{7,15},{8,0},{9,1},{1... | collective-permute-start | bytes 393224 | tf_op jit(solution)/shard_map/ppermute | solution.py:676
  53.7 8.1 %collective-permute-start.15 = (bf16[2,128,256]{2,1,0:T(8,128)(2,1)S(1)}, bf16[2,128,256]{2,1,0:T(8,128)(2,1)S(1)}, u32[]{:S(2)}, u32[]{:S(2)}) collective-permute-start(bf16[2,128,256]{2,1,0:T(8,128)(2,1)S(1)} %get-tuple-element.32.refs_10_), channel_id=1, source_target_pairs={{0,8},{1,9},{2,10},{3,11},{4,0},{5,1},{6,2},{7,3},{8,12},{9,13},{1... | collective-permute-start | bytes 393224 | tf_op jit(solution)/shard_map/ppermute | solution.py:676
  56.2 70.5 %collective-permute-start.25 = (bf16[2,784,256]{2,1,0:T(8,128)(2,1)S(1)}, bf16[2,784,256]{2,1,0:T(8,128)(2,1)S(1)}, u32[]{:S(2)}, u32[]{:S(2)}) collective-permute-start(bf16[2,784,256]{2,1,0:T(8,128)(2,1)S(1)} %build_factors.5.refs_5_), channel_id=1, source_target_pairs={{0,4},{1,5},{2,6},{3,7},{4,12},{5,13},{6,14},{7,15},{8,0},{9,1},{1... | collective-permute-start | bytes 2408456 | tf_op jit(solution)/shard_map/ppermute | solution.py:676
  57.9 67.4 %collective-permute-start.6 = (bf16[2,512,256]{2,1,0:T(8,128)(2,1)S(1)}, bf16[2,512,256]{2,1,0:T(8,128)(2,1)S(1)}, u32[]{:S(2)}, u32[]{:S(2)}) collective-permute-start(bf16[2,512,256]{2,1,0:T(8,128)(2,1)S(1)} %get-tuple-element.30.refs_0_), channel_id=1, source_target_pairs={{0,4},{1,5},{2,6},{3,7},{4,12},{5,13},{6,14},{7,15},{8,0},{9,1},{1... | collective-permute-start | bytes 1572872 | tf_op jit(solution)/shard_map/ppermute | solution.py:676
  58.8 66.4 %collective-permute-start.10 = (bf16[2,384,256]{2,1,0:T(8,128)(2,1)S(1)}, bf16[2,384,256]{2,1,0:T(8,128)(2,1)S(1)}, u32[]{:S(2)}, u32[]{:S(2)}) collective-permute-start(bf16[2,384,256]{2,1,0:T(8,128)(2,1)S(1)} %get-tuple-element.31.refs_5_), channel_id=1, source_target_pairs={{0,4},{1,5},{2,6},{3,7},{4,12},{5,13},{6,14},{7,15},{8,0},{9,1},{1... | collective-permute-start | bytes 1179656 | tf_op jit(solution)/shard_map/ppermute | solution.py:676
  59.1 40.3 %collective-permute-start.24 = (bf16[272,256]{1,0:T(8,128)(2,1)S(1)}, bf16[272,256]{1,0:T(8,128)(2,1)S(1)}, u32[]{:S(2)}, u32[]{:S(2)}) collective-permute-start(bf16[272,256]{1,0:T(8,128)(2,1)S(1)} %slice_bitcast_fusion.6), channel_id=1, source_target_pairs={{0,8},{1,9},{2,10},{3,11},{4,0},{5,1},{6,2},{7,3},{8,12},{9,13},{1... | collective-permute-start | bytes 417800 | tf_op jit(solution)/shard_map/ppermute | solution.py:676
  61.8 63.4 %collective-permute-start.11 = (bf16[2,384,256]{2,1,0:T(8,128)(2,1)S(1)}, bf16[2,384,256]{2,1,0:T(8,128)(2,1)S(1)}, u32[]{:S(2)}, u32[]{:S(2)}) collective-permute-start(bf16[2,384,256]{2,1,0:T(8,128)(2,1)S(1)} %get-tuple-element.31.refs_5_), channel_id=1, source_target_pairs={{0,8},{1,9},{2,10},{3,11},{4,0},{5,1},{6,2},{7,3},{8,12},{9,13},{1... | collective-permute-start | bytes 1179656 | tf_op jit(solution)/shard_map/ppermute | solution.py:676
  99.4 68.2 %collective-permute-start.19 = (bf16[2,2,2,256,256]{4,3,2,1,0:T(8,128)(2,1)S(1)}, bf16[2,2,2,256,256]{4,3,2,1,0:T(8,128)(2,1)S(1)}, u32[]{:S(2)}, u32[]{:S(2)}) collective-permute-start(bf16[2,2,2,256,256]{4,3,2,1,0:T(8,128)(2,1)S(1)} %copy-done.19), channel_id=1, source_target_pairs={{0,2},{1,3},{2,0},{3,1},{4,6},{5,7},{6,4},{7,5},{8,10},{9,11},{10,... | collective-permute-start | bytes 3145736 | tf_op jit(solution)/shard_map/ppermute | solution.py:676
  125.2 25.6 %collective-permute-start.26 = (bf16[2,784,256]{2,1,0:T(8,128)(2,1)S(1)}, bf16[2,784,256]{2,1,0:T(8,128)(2,1)S(1)}, u32[]{:S(2)}, u32[]{:S(2)}) collective-permute-start(bf16[2,784,256]{2,1,0:T(8,128)(2,1)S(1)} %build_factors.5.refs_5_), channel_id=1, source_target_pairs={{0,8},{1,9},{2,10},{3,11},{4,0},{5,1},{6,2},{7,3},{8,12},{9,13},{1... | collective-permute-start | bytes 2408456 | tf_op jit(solution)/shard_map/ppermute | solution.py:676
  125.2 45.3 %collective-permute-start.20 = (bf16[2,2,2,256,256]{4,3,2,1,0:T(8,128)(2,1)S(1)}, bf16[2,2,2,256,256]{4,3,2,1,0:T(8,128)(2,1)S(1)}, u32[]{:S(2)}, u32[]{:S(2)}) collective-permute-start(bf16[2,2,2,256,256]{4,3,2,1,0:T(8,128)(2,1)S(1)} %copy-done.18), channel_id=1, source_target_pairs={{0,3},{1,2},{2,1},{3,0},{4,7},{5,6},{6,5},{7,4},{8,11},{9,10},{10,... | collective-permute-start | bytes 3145736 | tf_op jit(solution)/shard_map/ppermute | solution.py:676
  125.3 45.3 %collective-permute-start.18 = (bf16[2,2,2,256,256]{4,3,2,1,0:T(8,128)(2,1)S(1)}, bf16[2,2,2,256,256]{4,3,2,1,0:T(8,128)(2,1)S(1)}, u32[]{:S(2)}, u32[]{:S(2)}) collective-permute-start(bf16[2,2,2,256,256]{4,3,2,1,0:T(8,128)(2,1)S(1)} %copy-done.17), channel_id=1, source_target_pairs={{0,1},{1,0},{2,3},{3,2},{4,5},{5,4},{6,7},{7,6},{8,9},{9,8},{10,11... | collective-permute-start | bytes 3145736 | tf_op jit(solution)/shard_map/ppermute | solution.py:676
  126.7 40.9 %collective-permute-start.7 = (bf16[2,512,256]{2,1,0:T(8,128)(2,1)S(1)}, bf16[2,512,256]{2,1,0:T(8,128)(2,1)S(1)}, u32[]{:S(2)}, u32[]{:S(2)}) collective-permute-start(bf16[2,512,256]{2,1,0:T(8,128)(2,1)S(1)} %get-tuple-element.30.refs_0_), channel_id=1, source_target_pairs={{0,8},{1,9},{2,10},{3,11},{4,0},{5,1},{6,2},{7,3},{8,12},{9,13},{1... | collective-permute-start | bytes 1572872 | tf_op jit(solution)/shard_map/ppermute | solution.py:676
  150.8 22.8 %collective-permute-start.8 = (bf16[512,256]{1,0:T(8,128)(2,1)S(1)}, bf16[512,256]{1,0:T(8,128)(2,1)S(1)}, u32[]{:S(2)}, u32[]{:S(2)}) collective-permute-start(bf16[512,256]{1,0:T(8,128)(2,1)S(1)} %slice_bitcast_fusion.3), channel_id=1, source_target_pairs={{0,4},{1,5},{2,6},{3,7},{4,12},{5,13},{6,14},{7,15},{8,0},{9,1},{1... | collective-permute-start | bytes 786440 | tf_op jit(solution)/shard_map/ppermute | solution.py:676
  167.6 17.1 %collective-permute-start.27 = (bf16[784,256]{1,0:T(8,128)(2,1)S(1)}, bf16[784,256]{1,0:T(8,128)(2,1)S(1)}, u32[]{:S(2)}, u32[]{:S(2)}) collective-permute-start(bf16[784,256]{1,0:T(8,128)(2,1)S(1)} %slice_bitcast_fusion.1), channel_id=1, source_target_pairs={{0,4},{1,5},{2,6},{3,7},{4,12},{5,13},{6,14},{7,15},{8,0},{9,1},{1... | collective-permute-start | bytes 1204232 | tf_op jit(solution)/shard_map/ppermute | solution.py:676
  167.6 17.1 %collective-permute-start.28 = (bf16[784,256]{1,0:T(8,128)(2,1)S(1)}, bf16[784,256]{1,0:T(8,128)(2,1)S(1)}, u32[]{:S(2)}, u32[]{:S(2)}) collective-permute-start(bf16[784,256]{1,0:T(8,128)(2,1)S(1)} %slice_bitcast_fusion), channel_id=1, source_target_pairs={{0,8},{1,9},{2,10},{3,11},{4,0},{5,1},{6,2},{7,3},{8,12},{9,13},{1... | collective-permute-start | bytes 1204232 | tf_op jit(solution)/shard_map/ppermute | solution.py:676
  170.6 35.0 %collective-permute-start.12 = (bf16[384,256]{1,0:T(8,128)(2,1)S(1)}, bf16[384,256]{1,0:T(8,128)(2,1)S(1)}, u32[]{:S(2)}, u32[]{:S(2)}) collective-permute-start(bf16[384,256]{1,0:T(8,128)(2,1)S(1)} %slice_bitcast_fusion.5), channel_id=1, source_target_pairs={{0,4},{1,5},{2,6},{3,7},{4,12},{5,13},{6,14},{7,15},{8,0},{9,1},{1... | collective-permute-start | bytes 589832 | tf_op jit(solution)/shard_map/ppermute | solution.py:676
  170.6 34.9 %collective-permute-start.13 = (bf16[384,256]{1,0:T(8,128)(2,1)S(1)}, bf16[384,256]{1,0:T(8,128)(2,1)S(1)}, u32[]{:S(2)}, u32[]{:S(2)}) collective-permute-start(bf16[384,256]{1,0:T(8,128)(2,1)S(1)} %slice_bitcast_fusion.4), channel_id=1, source_target_pairs={{0,8},{1,9},{2,10},{3,11},{4,0},{5,1},{6,2},{7,3},{8,12},{9,13},{1... | collective-permute-start | bytes 589832 | tf_op jit(solution)/shard_map/ppermute | solution.py:676
  173.6 25.7 %collective-permute-start.9 = (bf16[512,256]{1,0:T(8,128)(2,1)S(1)}, bf16[512,256]{1,0:T(8,128)(2,1)S(1)}, u32[]{:S(2)}, u32[]{:S(2)}) collective-permute-start(bf16[512,256]{1,0:T(8,128)(2,1)S(1)} %slice_bitcast_fusion.2), channel_id=1, source_target_pairs={{0,8},{1,9},{2,10},{3,11},{4,0},{5,1},{6,2},{7,3},{8,12},{9,13},{1... | collective-permute-start | bytes 786440 | tf_op jit(solution)/shard_map/ppermute | solution.py:676
  184.7 27.3 %collective-permute-start.16 = (bf16[128,256]{1,0:T(8,128)(2,1)S(1)}, bf16[128,256]{1,0:T(8,128)(2,1)S(1)}, u32[]{:S(2)}, u32[]{:S(2)}) collective-permute-start(bf16[128,256]{1,0:T(8,128)(2,1)S(1)} %slice_bitcast_fusion.9), channel_id=1, source_target_pairs={{0,4},{1,5},{2,6},{3,7},{4,12},{5,13},{6,14},{7,15},{8,0},{9,1},{1... | collective-permute-start | bytes 196616 | tf_op jit(solution)/shard_map/ppermute | solution.py:676
  184.7 27.3 %collective-permute-start.17 = (bf16[128,256]{1,0:T(8,128)(2,1)S(1)}, bf16[128,256]{1,0:T(8,128)(2,1)S(1)}, u32[]{:S(2)}, u32[]{:S(2)}) collective-permute-start(bf16[128,256]{1,0:T(8,128)(2,1)S(1)} %slice_bitcast_fusion.8), channel_id=1, source_target_pairs={{0,8},{1,9},{2,10},{3,11},{4,0},{5,1},{6,2},{7,3},{8,12},{9,13},{1... | collective-permute-start | bytes 196616 | tf_op jit(solution)/shard_map/ppermute | solution.py:676
  216.7 7.0 %collective-permute-start.35 = (f32[2,128]{1,0:T(2,128)S(1)}, f32[2,128]{1,0:T(2,128)S(1)}, u32[]{:S(2)}, u32[]{:S(2)}) collective-permute-start(f32[2,128]{1,0:T(2,128)S(1)} %get-tuple-element.52), channel_id=1, source_target_pairs={{0,12},{1,13},{2,14},{3,15},{4,8},{5,9},{6,10},{7,11},{8,4},{9,5},... | collective-permute-start | bytes 3080 | tf_op jit(solution)/shard_map/ppermute | solution.py:676
  219.7 4.0 %collective-permute-start.36 = (f32[2,128]{1,0:T(2,128)S(1)}, f32[2,128]{1,0:T(2,128)S(1)}, u32[]{:S(2)}, u32[]{:S(2)}) collective-permute-start(f32[2,128]{1,0:T(2,128)S(1)} %get-tuple-element.54), channel_id=1, source_target_pairs={{0,8},{1,9},{2,10},{3,11},{4,0},{5,1},{6,2},{7,3},{8,12},{9,13},{1... | collective-permute-start | bytes 3080 | tf_op jit(solution)/shard_map/ppermute | solution.py:676
  219.7 4.5 %collective-permute-start.37 = (f32[2,128]{1,0:T(2,128)S(1)}, f32[2,128]{1,0:T(2,128)S(1)}, u32[]{:S(2)}, u32[]{:S(2)}) collective-permute-start(f32[2,128]{1,0:T(2,128)S(1)} %get-tuple-element.53), channel_id=1, source_target_pairs={{0,4},{1,5},{2,6},{3,7},{4,12},{5,13},{6,14},{7,15},{8,0},{9,1},{1... | collective-permute-start | bytes 3080 | tf_op jit(solution)/shard_map/ppermute | solution.py:676
  221.9 16.6 %collective-permute-start.32 = (bf16[2,2,256,256]{3,2,1,0:T(8,128)(2,1)S(1)}, bf16[2,2,256,256]{3,2,1,0:T(8,128)(2,1)S(1)}, u32[]{:S(2)}, u32[]{:S(2)}) collective-permute-start(bf16[2,2,256,256]{3,2,1,0:T(8,128)(2,1)S(1)} %get-tuple-element.51), channel_id=1, source_target_pairs={{0,1},{1,0},{2,3},{3,2},{4,5},{5,4},{6,7},{7,6},{8,9},{9,8},{10,11... | collective-permute-start | bytes 1572872 | tf_op jit(solution)/shard_map/ppermute | solution.py:676
  222.0 17.5 %collective-permute-start.33 = (bf16[2,2,256,256]{3,2,1,0:T(8,128)(2,1)S(1)}, bf16[2,2,256,256]{3,2,1,0:T(8,128)(2,1)S(1)}, u32[]{:S(2)}, u32[]{:S(2)}) collective-permute-start(bf16[2,2,256,256]{3,2,1,0:T(8,128)(2,1)S(1)} %get-tuple-element.50), channel_id=1, source_target_pairs={{0,2},{1,3},{2,0},{3,1},{4,6},{5,7},{6,4},{7,5},{8,10},{9,11},{10,... | collective-permute-start | bytes 1572872 | tf_op jit(solution)/shard_map/ppermute | solution.py:676
  224.3 2.1 collective-permute-start.38
  224.4 12.4 %collective-permute-start.39 = (f32[2,32]{1,0:T(2,128)S(1)}, f32[2,32]{1,0:T(2,128)S(1)}, u32[]{:S(2)}, u32[]{:S(2)}) collective-permute-start(f32[2,32]{1,0:T(2,128)S(1)} %get-tuple-element.57), channel_id=1, source_target_pairs={{0,2},{1,3},{2,0},{3,1},{4,6},{5,7},{6,4},{7,5},{8,10},{9,11},{10,... | collective-permute-start | bytes 776 | tf_op jit(solution)/shard_map/ppermute | solution.py:676
  226.2 10.6 %collective-permute-start.40 = (f32[2,32]{1,0:T(2,128)S(1)}, f32[2,32]{1,0:T(2,128)S(1)}, u32[]{:S(2)}, u32[]{:S(2)}) collective-permute-start(f32[2,32]{1,0:T(2,128)S(1)} %get-tuple-element.56), channel_id=1, source_target_pairs={{0,3},{1,2},{2,1},{3,0},{4,7},{5,6},{6,5},{7,4},{8,11},{9,10},{10,... | collective-permute-start | bytes 776 | tf_op jit(solution)/shard_map/ppermute | solution.py:676
  226.4 20.9 %collective-permute-start.34 = (bf16[2,2,256,256]{3,2,1,0:T(8,128)(2,1)S(1)}, bf16[2,2,256,256]{3,2,1,0:T(8,128)(2,1)S(1)}, u32[]{:S(2)}, u32[]{:S(2)}) collective-permute-start(bf16[2,2,256,256]{3,2,1,0:T(8,128)(2,1)S(1)} %get-tuple-element.49), channel_id=1, source_target_pairs={{0,3},{1,2},{2,1},{3,0},{4,7},{5,6},{6,5},{7,4},{8,11},{9,10},{10,... | collective-permute-start | bytes 1572872 | tf_op jit(solution)/shard_map/ppermute | solution.py:676
  236.8 14.1 %collective-permute-start.29 = (bf16[2,2,256,256]{3,2,1,0:T(8,128)(2,1)S(1)}, bf16[2,2,256,256]{3,2,1,0:T(8,128)(2,1)S(1)}, u32[]{:S(2)}, u32[]{:S(2)}) collective-permute-start(bf16[2,2,256,256]{3,2,1,0:T(8,128)(2,1)S(1)} %get-tuple-element.48), channel_id=1, source_target_pairs={{0,1},{1,0},{2,3},{3,2},{4,5},{5,4},{6,7},{7,6},{8,9},{9,8},{10,11... | collective-permute-start | bytes 1572872 | tf_op jit(solution)/shard_map/ppermute | solution.py:676
  236.8 22.4 %collective-permute-start.30 = (bf16[2,2,256,256]{3,2,1,0:T(8,128)(2,1)S(1)}, bf16[2,2,256,256]{3,2,1,0:T(8,128)(2,1)S(1)}, u32[]{:S(2)}, u32[]{:S(2)}) collective-permute-start(bf16[2,2,256,256]{3,2,1,0:T(8,128)(2,1)S(1)} %get-tuple-element.47), channel_id=1, source_target_pairs={{0,2},{1,3},{2,0},{3,1},{4,6},{5,7},{6,4},{7,5},{8,10},{9,11},{10,... | collective-permute-start | bytes 1572872 | tf_op jit(solution)/shard_map/ppermute | solution.py:676
  238.5 31.1 %collective-permute-start.31 = (bf16[2,2,256,256]{3,2,1,0:T(8,128)(2,1)S(1)}, bf16[2,2,256,256]{3,2,1,0:T(8,128)(2,1)S(1)}, u32[]{:S(2)}, u32[]{:S(2)}) collective-permute-start(bf16[2,2,256,256]{3,2,1,0:T(8,128)(2,1)S(1)} %get-tuple-element.46), channel_id=1, source_target_pairs={{0,3},{1,2},{2,1},{3,0},{4,7},{5,6},{6,5},{7,4},{8,11},{9,10},{10,... | collective-permute-start | bytes 1572872 | tf_op jit(solution)/shard_map/ppermute | solution.py:676
  (13 other events, 66.4 us)

commit v6 on v5

--- a/solution.py
+++ b/solution.py
@@ -1,5 +1,4 @@
 import functools
-import itertools
 
 import jax
 import jax.numpy as jnp
@@ -237,11 +236,11 @@
     )(table, *[array] * len(starts))
 
 
-KIND, ONE, TWO, ONE_AT, TWO_AT, OUT_ROW, VIS_AT = 0, 1, 2, 3, 5, 7, 8
-COLUMNS = 10
-
-
-def unit_kernel(index, offset, pieces, bright_at, outs, aliased, tab_ref, *refs):
+KIND, ONE, TWO, ONE_AT, TWO_AT = 0, 1, 2, 3, 5
+COLUMNS = 7
+
+
+def unit_kernel(index, offset, pieces, bright_at, homes, tab_ref, *refs):
     arrays = []
     for entries in pieces:
         found = []
@@ -250,17 +249,16 @@
             found.append((parts, start, number))
             refs = refs[count:]
         arrays.append(found)
-    vis_ref, keep_one_ref, keep_two_ref = refs[:3]
-    refs = refs[3:]
+    vis_refs, (keep_one_ref, keep_two_ref) = refs[:homes], refs[homes : homes + 2]
+    refs = refs[homes + 2 :]
     columns_ref = None
     if bright_at is None:
         columns_ref, refs = refs[0], refs[1:]
-    refs = refs[aliased:]
-    out_refs, grad_ref = refs[:outs], refs[outs]
-    refs = refs[outs + 1 :]
+    out_refs, grad_ref = refs[:homes], refs[homes]
+    refs = refs[homes + 1 :]
     if bright_at is not None:
         columns_ref, refs = refs[0], refs[1:]
-    total_ref, one_ref, two_ref = refs
+    total_ref, one_ref, two_ref, vis_ref = refs
     step = pl.program_id(0)
     slot = tab_ref[0] + index
     sources, span = one_ref.shape[1:]
@@ -333,27 +331,35 @@
             folded = folded + value[:, start : start + 128]
         total_ref[...] += folded
 
+    each = pl.num_programs(0) // homes
+
     def put(res_re, res_im):
-        for out_ref in out_refs:
-            out_ref[0, 0] = res_re
-            out_ref[0, 1] = res_im
+        for home, out_ref in enumerate(out_refs):
+
+            @pl.when(step // each == home)
+            def _(out_ref=out_ref):
+                out_ref[0, 0] = res_re
+                out_ref[0, 1] = res_im
 
     @pl.when(step == 0)
     def _():
         total_ref[...] = jnp.zeros_like(total_ref)
 
-    @pl.when(entry(KIND) != 2)
-    def _():
-        load(one_ref, ONE_AT)
-        load(two_ref, TWO_AT)
+    load(one_ref, ONE_AT)
+    load(two_ref, TWO_AT)
+    for home, home_ref in enumerate(vis_refs):
+
+        @pl.when(step // each == home)
+        def _(home_ref=home_ref):
+            vis_ref[...] = home_ref[0, 0]
 
     @pl.when(entry(KIND) == 0)
     def _():
         one_re, one_im, two_re, two_im = one_ref[0], one_ref[1], two_ref[0], two_ref[1]
         pred_re, pred_im = cross(*scaled_of(one_re, one_im), two_re, two_im)
         weights = outer(keep_one_ref[...], keep_two_ref[...])
-        res_re = (weights * (vis_ref[0, 0, 0, 0].astype(jnp.float32) - pred_re)).astype(jnp.bfloat16)
-        res_im = (weights * (vis_ref[0, 0, 0, 1].astype(jnp.float32) - pred_im)).astype(jnp.bfloat16)
+        res_re = (weights * (vis_ref[0].astype(jnp.float32) - pred_re)).astype(jnp.bfloat16)
+        res_im = (weights * (vis_ref[1].astype(jnp.float32) - pred_im)).astype(jnp.bfloat16)
         put(res_re, res_im)
         sum_re, sum_im = pull(one_re, one_im, res_re, res_im, 1)
         add_grad(sum_re * two_re.astype(jnp.float32) - sum_im * two_im.astype(jnp.float32))
@@ -372,8 +378,8 @@
         weights = jnp.where(upper, outer(keep_one, keep_one), 0.0) + jnp.where(
             lower, outer(keep_two, keep_two), 0.0
         )
-        vis_re = vis_ref[0, 0, 0, 0].astype(jnp.float32)
-        vis_im = vis_ref[0, 0, 0, 1].astype(jnp.float32)
+        vis_re = vis_ref[0].astype(jnp.float32)
+        vis_im = vis_ref[1].astype(jnp.float32)
         res_re = (weights * (vis_re - jnp.where(upper, first_re, second_re))).astype(jnp.bfloat16)
         res_im = (weights * (vis_im - jnp.where(upper, first_im, -second_im))).astype(jnp.bfloat16)
         put(res_re, res_im)
@@ -392,26 +398,37 @@
         grad_ref[...] = jnp.sum(total_ref[...].T, axis=0, keepdims=True)
 
 
-def unit_work(index, steps, table, pieces, vis, keep, bright, outs):
-    span = vis.shape[5]
+def unit_work(index, offset, table, pieces, vis, keep, bright):
+    units_dev, _, _, span, _ = vis[0].shape
     slots = keep.shape[0]
     sources = sum(number for _, _, number in pieces[0])
-    offset, count = steps
+    count = units_dev * len(vis)
     whole = pl.BlockSpec(memory_space=pltpu.VMEM)
     arrays = [array for piece in pieces for entry, _, _ in piece for array in entry]
 
     def at(tab, step, column):
         return tab[offset + step * COLUMNS + column]
 
-    in_specs = [whole] * len(arrays) + [
-        pl.BlockSpec(
-            (1, 1, 1, 2, span, span),
-            lambda u, tab: (at(tab, u, VIS_AT), at(tab, u, VIS_AT + 1), index, 0, 0, 0),
-        ),
+    def unit(step, home):
+        return jnp.clip(step - home * units_dev, 0, units_dev - 1)
+
+    in_specs = [whole] * len(arrays)
+    for home, array in enumerate(vis):
+        if array.shape[1] == slots:
+            slot = lambda tab: tab[0] + index
+        else:
+            slot = lambda tab: index
+        in_specs.append(
+            pl.BlockSpec(
+                (1, 1, 2, span, span),
+                lambda u, tab, home=home, slot=slot: (unit(u, home), slot(tab), 0, 0, 0),
+            )
+        )
+    in_specs += [
         pl.BlockSpec((slots, span), lambda u, tab: (0, at(tab, u, ONE))),
         pl.BlockSpec((slots, span), lambda u, tab: (0, at(tab, u, TWO))),
     ]
-    operands = [table, *arrays, vis, keep, keep]
+    operands = [table, *arrays, *vis, keep, keep]
     bright_at = None
     if isinstance(bright, int):
         first = pieces[0][0]
@@ -419,19 +436,11 @@
     else:
         in_specs.append(whole)
         operands.append(bright)
-    aliases = {}
-    out_specs, out_shapes = [], []
-    for out in outs:
-        rows = out
-        if not isinstance(out, int):
-            rows = out.shape[0]
-            aliases[len(operands)] = len(out_specs)
-            operands.append(out)
-            in_specs.append(pl.BlockSpec(memory_space=pl.ANY))
-        out_specs.append(
-            pl.BlockSpec((1, 2, span, span), lambda u, tab: (at(tab, u, OUT_ROW), 0, 0, 0))
-        )
-        out_shapes.append(jax.ShapeDtypeStruct((rows, 2, span, span), jnp.bfloat16))
+    out_specs = [
+        pl.BlockSpec((1, 2, span, span), lambda u, tab, home=home: (unit(u, home), 0, 0, 0))
+        for home in range(len(vis))
+    ]
+    out_shapes = [jax.ShapeDtypeStruct((units_dev, 2, span, span), jnp.bfloat16) for _ in vis]
     out_specs.append(pl.BlockSpec((1, sources), lambda u, tab: (0, 0)))
     out_shapes.append(jax.ShapeDtypeStruct((1, sources), jnp.float32))
     if bright_at is not None:
@@ -439,7 +448,7 @@
         out_shapes.append(jax.ShapeDtypeStruct((bright, sources, 128), jnp.float32))
     kinds = [[(len(entry), start, number) for entry, start, number in piece] for piece in pieces]
     return pl.pallas_call(
-        functools.partial(unit_kernel, index, offset, kinds, bright_at, len(outs), len(aliases)),
+        functools.partial(unit_kernel, index, offset, kinds, bright_at, len(vis)),
         grid_spec=pltpu.PrefetchScalarGridSpec(
             num_scalar_prefetch=1,
             grid=(count,),
@@ -449,10 +458,10 @@
                 pltpu.VMEM((sources, 128), jnp.float32),
                 pltpu.VMEM((2, sources, span), jnp.bfloat16),
                 pltpu.VMEM((2, sources, span), jnp.bfloat16),
+                pltpu.VMEM((2, span, span), jnp.bfloat16),
             ],
         ),
         out_shape=out_shapes,
-        input_output_aliases=aliases,
         compiler_params=pltpu.CompilerParams(vmem_limit_bytes=48 * 1024 * 1024),
         cost_estimate=LITTLE,
         name="unit_work",
@@ -514,77 +523,44 @@
         self.opposite = along(2)
         self.partner = [[(t, t ^ m) for t in range(count)] for m in range(width)]
 
-        touched = [set(units[u, :2].tolist()) for u in range(units.shape[0])]
-        home = [list(range(t * units_dev, (t + 1) * units_dev)) for t in range(count)]
-        of_plane = [range(z * width * units_dev, (z + 1) * width * units_dev) for z in range(planes)]
-
-        def most(wanted):
-            return max(sum(bool(wanted(touched[u])) for u in plane) for plane in of_plane)
-
-        def stuck(block):
-            return sum(all(block in touched[u] for u in mine) for mine in home)
-
-        end = min(range(blocks), key=lambda b: most(lambda t: b in t))
-        rest = [b for b in range(blocks) if b != end]
-        start = min(
-            itertools.combinations(rest, blocks * FIRST_PART // 8),
-            key=lambda c: most(lambda t: end not in t and not t <= set(c)),
-        )
-        self.pieces = [list(start), [b for b in rest if b not in start], [end]]
+        half = blocks // 2
         self.full = [list(range(blocks))]
-        events = []
-        for blocks_of in touched:
-            events.append(max(n for n, piece in enumerate(self.pieces) if blocks_of & set(piece)))
-
-        def rows_of(t, pieces, wanted):
-            rows = []
-            for m in range(width):
-                for n, u in enumerate(home[t ^ m]):
-                    if not wanted(u):
-                        continue
-                    one, two, kind = units[u].tolist()
-                    at = [
-                        (k, piece.index(b))
-                        for b in (one, two)
-                        for k, piece in enumerate(pieces)
-                        if b in piece
-                    ]
-                    rows.append([kind, one, two, *at[0], *at[1], m * units_dev + n, m, n])
+        self.pieces = [list(range(half)), list(range(half, blocks))]
+
+        def table_of(pieces, order):
+            rows = np.zeros((count, len(order), units_dev, COLUMNS), np.int32)
+            for t in range(count):
+                for n, m in enumerate(order):
+                    for k in range(units_dev):
+                        one, two, kind = units[(t ^ m) * units_dev + k].tolist()
+                        at = [
+                            (p, piece.index(b))
+                            for b in (one, two)
+                            for p, piece in enumerate(pieces)
+                            if b in piece
+                        ]
+                        rows[t, n, k] = [kind, one, two, *at[0], *at[1]]
             return rows
 
-        def table_of(pieces, wanted):
-            tables = [rows_of(t, pieces, wanted) for t in range(count)]
-            steps = max(len(rows) for rows in tables)
-            for rows in tables:
-                while len(rows) < steps:
-                    rows.append([2] + (rows[-1][1:] if rows else [0] * (COLUMNS - 1)))
-                    rows[-1][OUT_ROW] = width * units_dev
-            return np.array(tables, np.int32)
-
-        first_table = table_of(self.full, lambda u: True)
-        tables = [
-            table_of(self.pieces, lambda u, n=n: events[u] == n) for n in range(len(self.pieces))
-        ]
-
         def targets(index):
-            rows = np.zeros((count, width, units_dev, 2), np.int32)
+            rows = np.zeros((count, len(self.order), units_dev, 2), np.int32)
             for t in range(count):
-                for m in range(width):
-                    for n in range(units_dev):
-                        rows[t, m, n] = n, (t % width ^ m) * share + index
+                for n, m in enumerate(self.order):
+                    for k in range(units_dev):
+                        rows[t, n, k] = k, (t % width ^ m) * share + index
             return rows
 
+        self.order = list(range(width // 2, width)) + list(range(width // 2 - 1, -1, -1))
         starts = np.array([[(t % width ^ m) * share for m in range(width)] for t in range(count)])
-        parts = [starts, first_table, *tables, *[targets(n) for n in range(share)]]
-        parts = [part.reshape(count, -1).astype(np.int32) for part in parts]
+        parts = [starts, table_of(self.full, self.order), table_of(self.pieces, self.order)]
+        parts += [targets(n) for n in range(share)]
+        parts = [part.reshape(count, -1) for part in parts]
         ends = np.cumsum([part.shape[1] for part in parts]).tolist()
-        self.table = np.concatenate(parts, 1)
-        self.first_steps = (ends[0], first_table.shape[1])
-        self.steps = [(ends[1 + n], table.shape[1]) for n, table in enumerate(tables)]
-        self.targets = ends[1 + len(tables) :]
-
-
-FIRST_PART = 4
+        self.table = np.concatenate(parts, 1).astype(np.int32)
+        self.steps = ends[:2]
+        self.targets = ends[2:]
+        self.steps_per_home = units_dev * COLUMNS
+        self.targets_per_home = units_dev * 2
 
 
 def packed_small(source_dirs, source_flux, visible_list):
@@ -601,13 +577,8 @@
     blocks = antennas // span
     tile_index = lax.axis_index("tile")
     units = unit_table(blocks)
-    own_rows = np.tile(np.arange(units_dev), units.shape[0] // units_dev)
-    none = np.zeros_like(own_rows)
-    table = np.stack(
-        [units[:, 2], units[:, 0], units[:, 1], none, units[:, 0], none, units[:, 1]]
-        + [own_rows, none, own_rows],
-        1,
-    )
+    none = np.zeros_like(units[:, 0])
+    table = np.stack([units[:, 2], units[:, 0], units[:, 1], none, units[:, 0], none, units[:, 1]], 1)
     table = table.astype(np.int32).reshape(-1, units_dev * COLUMNS)
     table = np.pad(table, ((0, 0), (1, 0)))
     table = lax.dynamic_index_in_dim(jnp.asarray(table), tile_index, 0, keepdims=False)
@@ -636,14 +607,7 @@
         number = factors.shape[0] * per_group
         factors = factors.transpose(1, 2, 0, 3, 4).reshape(2, blocks * number, span)
         residual, grad = unit_work(
-            slot,
-            (1, units_dev),
-            table,
-            [[((factors,), 0, number)]],
-            visibility[None],
-            keep,
-            columns,
-            [units_dev],
+            slot, 1, table, [[((factors,), 0, number)]], [visibility], keep, columns
         )
         residuals.append(residual)
         grads.append(grad)
@@ -651,8 +615,38 @@
     return jnp.stack(residuals, 1), summed
 
 
+OWN, OWN_NEAR, OWN_FAR, REST, REST_NEAR, REST_FAR = 0, 1, 3, 5, 6, 8
+BEAM, SIDE_BEAMS, LATER_BEAMS, VIS, LATER = 10, 12, 15, 19, 23
+PIECE_NEAR, PIECE_FAR = (24, 26), (28, 30)
+WORK, HOME, PUT, LATER_WORK, LATER_HOME, PUT_NEAR, PUT_LAST = 32, 35, 38, 40, 43, 46, 47
+SUM_PLANES, SUM_PLANE = 48, 51
 GATES = {
-    "own": (),
+    1: (0,),
+    5: (0, 1, 2, 11),
+    6: (0, 11, 13),
+    12: (11,),
+    15: (13,),
+    19: (3, 4, 18),
+    20: (4, 6),
+    21: (3, 5, 14, 17),
+    22: (13, 21),
+    23: (18,),
+    24: (6, 16),
+    25: (6, 7, 23),
+    26: (9,),
+    27: (8, 23),
+    30: (26,),
+    31: (26,),
+    34: (28,),
+    35: (28,),
+    36: (9,),
+    37: (26, 27),
+    40: (36, 37),
+    43: (30,),
+    45: (44,),
+    46: (38, 43),
+    48: (35,),
+    51: (31, 45),
 }
 
 
@@ -664,163 +658,137 @@
     group = width * per_group
     tile_index = lax.axis_index("tile")
     mine = tile_index % width
-    others = range(1, width)
     table = lax.dynamic_index_in_dim(jnp.asarray(routes.table), tile_index, 0, keepdims=False)
     done = {}
 
-    def gated(name, value):
-        earlier = [done[gate] for gate in GATES.get(name, ())]
+    def gated(step, value):
+        earlier = [done[gate] for gate in GATES.get(step, ())]
         return lax.optimization_barrier((value, *earlier))[0] if earlier else value
 
-    def send(name, value, pairs):
-        done[name] = lax.ppermute(gated(name, value), "tile", pairs)
-        return done[name]
-
-    def near(name, piece):
+    def send(step, value, pairs):
+        done[step] = lax.ppermute(gated(step, value), "tile", pairs)
+        return done[step]
+
+    def near(step, piece):
+        return [send(step, piece, routes.onward), send(step + 1, piece, routes.backward)]
+
+    def far(step, sides):
         return [
-            send(name + " onward", piece, routes.onward),
-            send(name + " backward", piece, routes.backward),
-        ]
-
-    def far(name, sides):
-        return [
-            send(name + " onward", sides[0][0], routes.onward),
-            send(name + " backward", sides[1][1], routes.backward),
+            send(step, sides[0][0], routes.onward),
+            send(step + 1, sides[1][1], routes.backward),
         ]
 
     def entries(piece, sides, halves, first, number):
         found = [(piece,), (sides[0],), (sides[1],), tuple(halves)]
         return [(arrays, n * group + first, number) for n, arrays in enumerate(found)]
 
-    def sent_home(name, results):
-        parts = [results[m * units_dev : (m + 1) * units_dev] for m in others]
-        return [send(f"{name} {m}", part, routes.partner[m]) for m, part in zip(others, parts)]
-
-    first_slot = (0, share, per_group)
-    (own,) = build_factors(
-        first_slot,
-        gated("own", table),
-        beam,
-        [],
-        antenna_uvw,
-        [small],
-        routes.full,
-        span,
-        BRIGHT_ROWS,
-        small.shape[1],
+    def build(step, index, own_beam, messages, smalls, pieces, bright_rows):
+        built = build_factors(
+            (index, share, per_group),
+            gated(step, table),
+            own_beam,
+            messages,
+            antenna_uvw,
+            smalls,
+            pieces,
+            span,
+            bright_rows,
+            small.shape[1],
+        )
+        done[step] = built[0]
+        return built
+
+    core, *side = range(1, width)
+    (message,) = messages_for(beam, 0, [core], small, gated(BEAM, table))
+    message = send(BEAM + 1, message, routes.partner[core])
+    (own,) = build(OWN, 0, beam, [message], [small, message], routes.full, BRIGHT_ROWS)
+    own_sides = near(OWN_NEAR, own)
+    messages = messages_for(beam, 0, side, small, gated(SIDE_BEAMS, table))
+    messages = [
+        send(SIDE_BEAMS + 1 + n, messages[n], routes.partner[m]) for n, m in enumerate(side)
+    ]
+    own_far = far(OWN_FAR, own_sides)
+    (rest,) = build(REST, 0, None, messages, messages, routes.full, BRIGHT_ROWS)
+    rest_sides = near(REST_NEAR, rest)
+
+    later = messages_for(beam, 1, [core, *side], None, gated(LATER_BEAMS, table))
+    later = [send(LATER_BEAMS + m, later[m - 1], routes.partner[m]) for m in (core, *side)]
+    vis = slices_for(
+        visibility, 1, share, [(m, 0) for m in (core, *side)], gated(VIS, table)
     )
-    done["own"] = own
-    own_sides = near("own near", own)
-    messages = messages_for(beam, 0, others, small, gated("beams", table))
-    messages = [send(f"beams {m}", messages[m - 1], routes.partner[m]) for m in others]
-    own_far = far("own far", own_sides)
-    (rest,) = build_factors(
-        first_slot,
-        gated("rest", table),
-        None,
-        messages,
-        antenna_uvw,
-        messages,
-        routes.full,
-        span,
-        BRIGHT_ROWS,
-        small.shape[1],
+    vis = [visibility] + [send(VIS + m, vis[m - 1], routes.partner[m]) for m in (core, *side)]
+    later_pieces = build(
+        LATER, 1, beam, later, [small, message, *messages], routes.pieces, 0
     )
-    done["rest"] = rest
-    rest_sides = near("rest near", rest)
-
-    later = messages_for(beam, 1, others, None, gated("later beams", table))
-    later = [send(f"later beams {m}", later[m - 1], routes.partner[m]) for m in others]
-    vis = slices_for(
-        visibility, 1, share, [(m, 0) for m in range(width)], gated("vis", table)
-    )
-    vis = [vis[0]] + [send(f"vis {m}", vis[m], routes.partner[m]) for m in others]
-    later_pieces = build_factors(
-        (1, share, per_group),
-        gated("later", table),
-        beam,
-        later,
-        antenna_uvw,
-        [small, *messages],
-        routes.pieces,
-        span,
-        0,
-        small.shape[1],
-    )
-    rest_far = far("rest far", rest_sides)
-    near_0 = near("piece 0 near", later_pieces[0])
-    near_1 = near("piece 1 near", later_pieces[1])
-    far_0 = far("piece 0 far", near_0)
-
-    vis = jnp.stack(vis, 0)
-    pieces = entries(own, own_sides, own_far, 0, per_group)
-    pieces += entries(rest, rest_sides, rest_far, per_group, group - per_group)
-    results, grad, columns = unit_work(
-        0,
-        routes.first_steps,
-        gated("work", table),
-        [pieces],
-        vis,
-        keep,
-        share,
-        [width * units_dev],
-    )
-    done["work"] = grad
-    grads = [grad]
-    home = sent_home("home", results)
-    far_1 = far("piece 1 far", near_1)
-    near_2 = near("piece 2 near", later_pieces[2])
-    far_2 = far("piece 2 far", near_2)
+    rest_far = far(REST_FAR, rest_sides)
+    near_0 = near(PIECE_NEAR[0], later_pieces[0])
+    near_1 = near(PIECE_NEAR[1], later_pieces[1])
+    far_0 = far(PIECE_FAR[0], near_0)
+
+    grads = []
+
+    def work(index, step, home_step, ready, bright):
+        arrived, total = [], None
+        for n, homes in enumerate([routes.order[:1], routes.order[1:2], routes.order[2:]]):
+            made = unit_work(
+                index,
+                routes.steps[index] + len(arrived) * routes.steps_per_home,
+                gated(step + n, table),
+                ready,
+                [vis[m] for m in homes],
+                keep,
+                bright,
+            )
+            results, grad = made[: len(homes)], made[len(homes)]
+            if isinstance(bright, int):
+                bright = made[-1]
+            done[step + n] = grad
+            total = grad if total is None else total + grad
+            arrived += [
+                send(home_step - 1 + m, part, routes.partner[m]) if m else part
+                for m, part in zip(homes, results)
+            ]
+        grads.append(total)
+        return arrived, bright
+
+    def put(step, homes, arrays, index, residual):
+        rows = [(n, k) for n in range(len(arrays)) for k in range(units_dev)]
+        offset = routes.targets[index] + homes * routes.targets_per_home
+        done[step] = put_residuals(
+            rows, arrays, offset, gated(step, table), visibility.shape, residual
+        )
+        return done[step]
+
+    number = group // 2
+    pieces = entries(own, own_sides, own_far, 0, number)
+    pieces += entries(rest, rest_sides, rest_far, number, number)
+    arrived, columns = work(0, WORK, HOME, [pieces], share)
+    far_1 = far(PIECE_FAR[1], near_1)
+    residual = put(PUT, 0, arrived, 0, None)
     ready = [
         entries(piece, sides, halves, 0, group)
-        for piece, sides, halves in zip(
-            later_pieces, (near_0, near_1, near_2), (far_0, far_1, far_2)
-        )
+        for piece, sides, halves in zip(later_pieces, (near_0, near_1), (far_0, far_1))
     ]
-    pairs = [(m, n) for m in range(width) for n in range(units_dev)]
-    residual = put_residuals(
-        pairs, [results, *home], routes.targets[0], gated("put", table), visibility.shape, None
-    )
-    done["put"] = residual
-
-    results = width * units_dev + 1
-    for n, steps in enumerate(routes.steps):
-        results, grad = unit_work(
-            1,
-            steps,
-            gated(f"work {n}", table),
-            ready[: n + 1],
-            vis,
-            keep,
-            columns,
-            [results],
-        )
-        done[f"work {n}"] = grad
-        grads.append(grad)
-    returned = sent_home("later home", results)
-
-    partial = jnp.concatenate([grads[0], sum(grads[2:], grads[1])], 0)
+    arrived, _ = work(1, LATER_WORK, LATER_HOME, ready, columns)
+
+    partial = jnp.concatenate(grads, 0)
     parts = [partial[:, n * group : (n + 1) * group] for n in range(4)]
-    plane_sum = (parts[0] + send("sum opposite", parts[3], routes.opposite)) + (
-        send("sum backward", parts[1], routes.backward)
-        + send("sum onward", parts[2], routes.onward)
+    plane_sum = (parts[0] + send(SUM_PLANES, parts[3], routes.opposite)) + (
+        send(SUM_PLANES + 1, parts[1], routes.backward)
+        + send(SUM_PLANES + 2, parts[2], routes.onward)
     )
     sums = [plane_sum[:, m * per_group : (m + 1) * per_group] for m in range(width)]
-    sums = [sums[0]] + [send(f"sum {m}", sums[m], routes.partner[m]) for m in others]
+    sums = [sums[0]] + [
+        send(SUM_PLANE - 1 + m, sums[m], routes.partner[m]) for m in (core, *side)
+    ]
     sums = jnp.stack(sums, 0)
     ids = jnp.arange(width, dtype=jnp.int32)
     here = jnp.bitwise_xor(ids[:, None], mine) == ids[None, :]
     summed = jnp.sum(jnp.where(here[:, :, None, None], sums[None], 0.0), axis=1)
     summed = summed.reshape(slots, per_group)
 
-    residual = put_residuals(
-        pairs,
-        [results, *returned],
-        routes.targets[1],
-        gated("later put", table),
-        visibility.shape,
-        residual,
-    )
+    residual = put(PUT_NEAR, 2, arrived[2:], 1, residual)
+    residual = put(PUT_LAST, 0, arrived[:2], 1, residual)
     return residual, summed
 
 

time: 274 us -> 215 us (0.78)
  waiting for transfers between devices: 162 us -> 51.5 us
  starting transfers between devices: 42.4 us -> 75.3 us
  local copies, waits for them, and re-layouts: 10.4 us -> 22.1 us
  Pallas kernels: 52.5 us -> 60.6 us
    ppermute x41 -> x37, waiting for transfers between devices: 162 us -> 51.5 us  [send(): done[step] = lax.ppermute(gated(step, value), 'tile', pairs)]
    ppermute x41 -> x37, starting transfers between devices: 42.4 us -> 75.3 us  [send(): done[step] = lax.ppermute(gated(step, value), 'tile', pairs)]
    unnamed x41 -> x93, local copies, waits for them, and re-layouts: 7.39 us -> 18.6 us
    pallas_call x4 -> x6, Pallas kernels: 27.6 us -> 32.3 us  [unit_work(): pl.pallas_call(functools.partial(unit_kernel, index, offset, kinds, brigh...]
    pallas_call x2 -> x3, Pallas kernels: 7.27 us -> 9.98 us  [put_residuals(): pl.pallas_call(functools.partial(put_kernel, sources), grid_spec=pltpu.Pr...]
    pallas_call x2 -> x3, Pallas kernels: 5.5 us -> 7.68 us  [messages_for(): pl.pallas_call(functools.partial(message_kernel, per_group), grid_spec=pl...]
  transfers between devices with their start and end apart: 41 -> 37, of which waited for: 12 -> 11; matrix products, arithmetic and copies ran while one was open for 2% -> 2% of each run, Pallas kernels for 15% -> 26%
where the time goes in v6:
time: 215 us; the launch traced here: 214 us
  starting transfers between devices  75.3 us (35%)
  Pallas kernels  60.6 us (28%)
  waiting for transfers between devices  51.5 us (24%)
  local copies, waits for them, and re-layouts  22.1 us (10%)
  other arithmetic  3.59 us (2%)
    ppermute x37, starting transfers between devices, send(): done[step] = lax.ppermute(gated(step, value), 'tile', pairs)  75.3 us
    ppermute x37, waiting for transfers between devices, send(): done[step] = lax.ppermute(gated(step, value), 'tile', pairs)  51.5 us
    pallas_call x6, Pallas kernels, unit_work(): pl.pallas_call(functools.partial(unit_kernel, index, offset, kinds, brigh...  32.3 us
    unnamed x93, local copies, waits for them, and re-layouts  18.6 us
    pallas_call x3, Pallas kernels, put_residuals(): pl.pallas_call(functools.partial(put_kernel, sources), grid_spec=pltpu.Pr...  9.98 us
    pallas_call x3, Pallas kernels, messages_for(): pl.pallas_call(functools.partial(message_kernel, per_group), grid_spec=pl...  7.68 us
    pallas_call x3, Pallas kernels, build_factors(): pl.pallas_call(functools.partial(build_kernel, sets, slot_ids, pieces, br...  6.63 us
  transfers between devices with their start and end apart: 37, of which 11 were waited for; matrix products, arithmetic and copies ran while one was open for 2% of the time, Pallas kernels for 26%

profile of v6, /device:TPU:0, one launch (start us, length us, event | category | flops | bytes accessed | tf_op | source)
XLA Modules:
  0.0 214.1 jit_solution(16047363242752363725)
XLA Ops:
  2.2 1.2 constant_dynamic-slice_fusion
  3.5 1.3 pad_maximum_fusion.refs_1_.refs_2_.refs_4_
  4.7 2.4 %messages_for.3 = bf16[80,2048]{1,0:T(8,128)(2,1)} custom-call(s32[148]{0:T(256)} %bitcast.24, bf16[8,2,32,2048]{3,2,1,0:T(8,128)(2,1)} %refs_0_.11, f32[4,256]{1,0:T(4,128)} %pad_maximum_fusion.refs_1_.refs_2_.refs_4_), custom_call_target="tpu_custom_call" | custom-call | flops 1 | bytes 1 | tf_op jit(solution)/shard_map/messages_for/pallas_call | solution.py:183
  7.6 1.1 copy.15.refs_3_.refs_2_.refs_8_
  10.4 1.6 build_factors.3.refs_0_
  12.0 3.0 %collective-permute-start.1 = (bf16[2,528,256]{2,1,0:T(8,128)(2,1)S(1)}, bf16[2,528,256]{2,1,0:T(8,128)(2,1)S(1)}, u32[]{:S(2)}, u32[]{:S(2)}) collective-permute-start(bf16[2,528,256]{2,1,0:T(8,128)(2,1)S(1)} %build_factors.3.refs_0_), channel_id=1, source_target_pairs={{0,4},{1,5},{2,6},{3,7},{4,12},{5,13},{6,14},{7,15},{8,0},{9,1},{1... | collective-permute-start | bytes 1622024 | tf_op jit(solution)/shard_map/ppermute | solution.py:669
  15.0 2.6 %messages_for.4 = (bf16[80,2048]{1,0:T(8,128)(2,1)}, bf16[80,2048]{1,0:T(8,128)(2,1)}) custom-call(s32[148]{0:T(256)} %bitcast.25, bf16[8,2,32,2048]{3,2,1,0:T(8,128)(2,1)} %refs_0_.11, bf16[8,2,32,2048]{3,2,1,0:T(8,128)(2,1)} %refs_0_.11, f32[4,256]{1,0:T(4,128)} %pad_maximum_fusion.refs_1_.refs_2_.refs_4_), custom_call_target="tpu_custom_call" | custom-call | flops 1 | bytes 1 | tf_op jit(solution)/shard_map/messages_for/pallas_call | solution.py:183
  17.6 1.5 collective-permute-start.5
  19.1 1.3 collective-permute-start.2
  20.5 7.9 %collective-permute-done.5.refs_0_.refs_6_ = bf16[80,2048]{1,0:T(8,128)(2,1)S(1)} collective-permute-done((bf16[80,2048]{1,0:T(8,128)(2,1)}, bf16[80,2048]{1,0:T(8,128)(2,1)S(1)}, u32[]{:S(2)}, u32[]{:S(2)}) %collective-permute-start.5) | collective-permute-done | bytes 327712 | tf_op jit(solution)/shard_map/ppermute | solution.py:669
  28.4 2.7 %messages_for.5 = (bf16[64,2048]{1,0:T(8,128)(2,1)}, bf16[64,2048]{1,0:T(8,128)(2,1)}, bf16[64,2048]{1,0:T(8,128)(2,1)}) custom-call(s32[148]{0:T(256)} %bitcast.26, bf16[8,2,32,2048]{3,2,1,0:T(8,128)(2,1)} %refs_0_.11, bf16[8,2,32,2048]{3,2,1,0:T(8,128)(2,1)} %refs_0_.11, bf16[8,2,32,2048]{3,2,1,0:T(8,128)(2,1)} %refs_0_.11), custom_call_target="tpu_custom_call" | custom-call | flops 1 | bytes 1 | tf_op jit(solution)/shard_map/messages_for/pallas_call | solution.py:183
  31.1 10.0 %collective-permute-start.3 = (bf16[528,256]{1,0:T(8,128)(2,1)S(1)}, bf16[528,256]{1,0:T(8,128)(2,1)S(1)}, u32[]{:S(2)}, u32[]{:S(2)}) collective-permute-start(bf16[528,256]{1,0:T(8,128)(2,1)S(1)} %slice_bitcast_fusion.3), channel_id=1, source_target_pairs={{0,4},{1,5},{2,6},{3,7},{4,12},{5,13},{6,14},{7,15},{8,0},{9,1},{1... | collective-permute-start | bytes 811016 | tf_op jit(solution)/shard_map/ppermute | solution.py:669
  41.2 1.5 collective-permute-start.4
  42.7 1.5 collective-permute-start.12
  44.3 1.6 build_factors.4.refs_5_
  46.6 1.9 collective-permute-start.7
  51.0 5.0 %collective-permute-done.4.refs_4_ = bf16[528,256]{1,0:T(8,128)(2,1)S(1)} collective-permute-done((bf16[528,256]{1,0:T(8,128)(2,1)S(1)}, bf16[528,256]{1,0:T(8,128)(2,1)S(1)}, u32[]{:S(2)}, u32[]{:S(2)}) %collective-permute-start.4) | collective-permute-done | bytes 270368 | tf_op jit(solution)/shard_map/ppermute | solution.py:669
  56.7 4.0 %slices_for.1 = (bf16[2,2,2,256,256]{4,3,2,1,0:T(8,128)(2,1)}, bf16[2,2,2,256,256]{4,3,2,1,0:T(8,128)(2,1)}, bf16[2,2,2,256,256]{4,3,2,1,0:T(8,128)(2,1)}) custom-call(s32[148]{0:T(256)} %bitcast.27, bf16[2,8,2,256,256]{4,3,2,1,0:T(8,128)(2,1)} %refs_11_.3, bf16[2,8,2,256,256]{4,3,2,1,0:T(8,128)(2,1)} %refs_11_.3, bf16[2,8,2,256,256]{4,3,2,1,0:T(8,128)(2,1)} %refs_11_.3), custom_call_target="tpu_custom_call" | custom-call | flops 1 | bytes 1 | tf_op jit(solution)/shard_map/slices_for/pallas_call | solution.py:213
  60.7 2.9 %collective-permute-start.13 = (bf16[2,2,2,256,256]{4,3,2,1,0:T(8,128)(2,1)}, bf16[2,2,2,256,256]{4,3,2,1,0:T(8,128)(2,1)S(1)}, u32[]{:S(2)}, u32[]{:S(2)}) collective-permute-start(bf16[2,2,2,256,256]{4,3,2,1,0:T(8,128)(2,1)} %get-tuple-element.64), channel_id=1, source_target_pairs={{0,2},{1,3},{2,0},{3,1},{4,6},{5,7},{6,4},{7,5},{8,10},{9,11},{10,... | collective-permute-start | bytes 3145736 | tf_op jit(solution)/shard_map/ppermute | solution.py:669
  63.6 1.7 collective-permute-done.16.refs_1_
  69.2 3.4 %build_factors.5 = (bf16[2,512,256]{2,1,0:T(8,128)(2,1)S(1)}, bf16[2,512,256]{2,1,0:T(8,128)(2,1)S(1)}) custom-call(s32[148]{0:T(256)S(1)} %bitcast.30, bf16[8,2,32,2048]{3,2,1,0:T(8,128)(2,1)S(1)} %copy-done.1, bf16[64,2048]{1,0:T(8,128)(2,1)S(1)} %collective-permute-done.16.refs_1_, bf16[64,2048]{1,0:T(8,128)(2,1)} %collective-permute-done.12.refs_2_, ...), custom_call_target="tpu_custom_call" | custom-call | flops 1 | bytes 1 | tf_op jit(solution)/shard_map/build_factors/pallas_call | solution.py:145
  72.7 5.0 %collective-permute-start.20 = (bf16[2,512,256]{2,1,0:T(8,128)(2,1)S(1)}, bf16[2,512,256]{2,1,0:T(8,128)(2,1)S(1)}, u32[]{:S(2)}, u32[]{:S(2)}) collective-permute-start(bf16[2,512,256]{2,1,0:T(8,128)(2,1)S(1)} %get-tuple-element.80.refs_0_), channel_id=1, source_target_pairs={{0,4},{1,5},{2,6},{3,7},{4,12},{5,13},{6,14},{7,15},{8,0},{9,1},{1... | collective-permute-start | bytes 1572872 | tf_op jit(solution)/shard_map/ppermute | solution.py:669
  78.7 1.3 collective-permute-start.10
  80.9 2.4 %collective-permute-start.9 = (bf16[528,256]{1,0:T(8,128)(2,1)S(1)}, bf16[528,256]{1,0:T(8,128)(2,1)S(1)}, u32[]{:S(2)}, u32[]{:S(2)}) collective-permute-start(bf16[528,256]{1,0:T(8,128)(2,1)S(1)} %slice_bitcast_fusion.1), channel_id=1, source_target_pairs={{0,4},{1,5},{2,6},{3,7},{4,12},{5,13},{6,14},{7,15},{8,0},{9,1},{1... | collective-permute-start | bytes 811016 | tf_op jit(solution)/shard_map/ppermute | solution.py:669
  83.3 3.6 %collective-permute-done.13.refs_10_ = bf16[2,2,2,256,256]{4,3,2,1,0:T(8,128)(2,1)S(1)} collective-permute-done((bf16[2,2,2,256,256]{4,3,2,1,0:T(8,128)(2,1)}, bf16[2,2,2,256,256]{4,3,2,1,0:T(8,128)(2,1)S(1)}, u32[]{:S(2)}, u32[]{:S(2)}) %collective-permute-start.13) | collective-permute-done | bytes 1048608 | tf_op jit(solution)/shard_map/ppermute | solution.py:669
  87.3 12.0 %collective-permute-done.10.refs_9_ = bf16[528,256]{1,0:T(8,128)(2,1)S(1)} collective-permute-done((bf16[528,256]{1,0:T(8,128)(2,1)S(1)}, bf16[528,256]{1,0:T(8,128)(2,1)S(1)}, u32[]{:S(2)}, u32[]{:S(2)}) %collective-permute-start.10) | collective-permute-done | bytes 270368 | tf_op jit(solution)/shard_map/ppermute | solution.py:669
  99.3 2.9 %collective-permute-done.9.refs_8_ = bf16[528,256]{1,0:T(8,128)(2,1)S(1)} collective-permute-done((bf16[528,256]{1,0:T(8,128)(2,1)S(1)}, bf16[528,256]{1,0:T(8,128)(2,1)S(1)}, u32[]{:S(2)}, u32[]{:S(2)}) %collective-permute-start.9) | collective-permute-done | bytes 270368 | tf_op jit(solution)/shard_map/ppermute | solution.py:669
  102.2 13.4 %collective-permute-start.17 = (bf16[2,512,256]{2,1,0:T(8,128)(2,1)S(1)}, bf16[2,512,256]{2,1,0:T(8,128)(2,1)S(1)}, u32[]{:S(2)}, u32[]{:S(2)}) collective-permute-start(bf16[2,512,256]{2,1,0:T(8,128)(2,1)S(1)} %get-tuple-element.76.refs_5_), channel_id=1, source_target_pairs={{0,4},{1,5},{2,6},{3,7},{4,12},{5,13},{6,14},{7,15},{8,0},{9,1},{1... | collective-permute-start | bytes 1572872 | tf_op jit(solution)/shard_map/ppermute | solution.py:669
  115.7 3.4 %collective-permute-start.22 = (bf16[512,256]{1,0:T(8,128)(2,1)S(1)}, bf16[512,256]{1,0:T(8,128)(2,1)S(1)}, u32[]{:S(2)}, u32[]{:S(2)}) collective-permute-start(bf16[512,256]{1,0:T(8,128)(2,1)S(1)} %slice_bitcast_fusion.7), channel_id=1, source_target_pairs={{0,4},{1,5},{2,6},{3,7},{4,12},{5,13},{6,14},{7,15},{8,0},{9,1},{1... | collective-permute-start | bytes 786440 | tf_op jit(solution)/shard_map/ppermute | solution.py:669
  119.2 4.5 %unit_work.6 = (bf16[2,2,256,256]{3,2,1,0:T(8,128)(2,1)S(1)}, f32[1,512]{1,0:T(1,128)S(1)}, f32[2,512,128]{2,1,0:T(8,128)S(1)}) custom-call(s32[148]{0:T(256)S(1)} %bitcast.31, bf16[2,528,256]{2,1,0:T(8,128)(2,1)S(1)} %build_factors.3.refs_0_, bf16[2,528,256]{2,1,0:T(8,128)(2,1)S(1)} %copy-done.3, bf16[2,528,256]{2,1,0:T(8,128)(2,1)S(1)} %copy-done.5, ...), custom_call_target="tpu_custom_call" | custom-call | flops 1 | bytes 1 | tf_op jit(solution)/shard_map/unit_work/pallas_call | solution.py:450
  124.7 4.3 %unit_work.7 = (bf16[2,2,256,256]{3,2,1,0:T(8,128)(2,1)S(1)}, f32[1,512]{1,0:T(1,128)S(1)}) custom-call(s32[148]{0:T(256)S(1)} %bitcast.32, bf16[2,528,256]{2,1,0:T(8,128)(2,1)S(1)} %build_factors.3.refs_0_, bf16[2,528,256]{2,1,0:T(8,128)(2,1)S(1)} %copy-done.3, bf16[2,528,256]{2,1,0:T(8,128)(2,1)S(1)} %copy-done.5, bf16[528,256]{1,0:T(8,128)(2,1)S(1)} %copy-done.15, ...), custom_call_target="tpu_custom_call" | custom-call | flops 1 | bytes 1 | tf_op jit(solution)/shard_map/unit_work/pallas_call | solution.py:450
  129.1 1.2 collective-permute-start.14
  130.3 12.3 %collective-permute-done.18.refs_7_ = bf16[2,512,256]{2,1,0:T(8,128)(2,1)S(1)} collective-permute-done((bf16[2,512,256]{2,1,0:T(8,128)(2,1)S(1)}, bf16[2,512,256]{2,1,0:T(8,128)(2,1)S(1)}, u32[]{:S(2)}, u32[]{:S(2)}) %collective-permute-start.18) | collective-permute-done | bytes 524320 | tf_op jit(solution)/shard_map/ppermute | solution.py:669
  143.2 1.7 collective-permute-done.22.refs_3_
  144.9 7.3 %collective-permute-start.24 = (bf16[512,256]{1,0:T(8,128)(2,1)S(1)}, bf16[512,256]{1,0:T(8,128)(2,1)S(1)}, u32[]{:S(2)}, u32[]{:S(2)}) collective-permute-start(bf16[512,256]{1,0:T(8,128)(2,1)S(1)} %slice_bitcast_fusion.5), channel_id=1, source_target_pairs={{0,4},{1,5},{2,6},{3,7},{4,12},{5,13},{6,14},{7,15},{8,0},{9,1},{1... | collective-permute-start | bytes 786440 | tf_op jit(solution)/shard_map/ppermute | solution.py:669
  153.3 7.5 %unit_work.10 = (bf16[2,2,256,256]{3,2,1,0:T(8,128)(2,1)}, bf16[2,2,256,256]{3,2,1,0:T(8,128)(2,1)S(1)}, f32[1,512]{1,0:T(1,128)S(1)}) custom-call(s32[148]{0:T(256)S(1)} %bitcast.33, bf16[2,528,256]{2,1,0:T(8,128)(2,1)S(1)} %build_factors.3.refs_0_, bf16[2,528,256]{2,1,0:T(8,128)(2,1)S(1)} %copy-done.3, bf16[2,528,256]{2,1,0:T(8,128)(2,1)S(1)} %copy-done.5, ...), custom_call_target="tpu_custom_call" | custom-call | flops 1 | bytes 1 | tf_op jit(solution)/shard_map/unit_work/pallas_call | solution.py:450
  163.3 4.7 %unit_work.8 = (bf16[2,2,256,256]{3,2,1,0:T(8,128)(2,1)}, f32[1,512]{1,0:T(1,128)S(1)}) custom-call(s32[148]{0:T(256)S(1)} %bitcast.34, bf16[2,512,256]{2,1,0:T(8,128)(2,1)S(1)} %get-tuple-element.80.refs_0_, bf16[2,512,256]{2,1,0:T(8,128)(2,1)S(1)} %collective-permute-done.20.refs_1_, bf16[2,512,256]{2,1,0:T(8,128)(2,1)S(1)} %collective-permute-done.21.refs_2_, ...), custom_call_target="tpu_custom_call" | custom-call | flops 1 | bytes 1 | tf_op jit(solution)/shard_map/unit_work/pallas_call | solution.py:450
  168.6 7.2 %unit_work.11 = (bf16[2,2,256,256]{3,2,1,0:T(8,128)(2,1)}, bf16[2,2,256,256]{3,2,1,0:T(8,128)(2,1)S(1)}, f32[1,512]{1,0:T(1,128)S(1)}) custom-call(s32[148]{0:T(256)S(1)} %bitcast.35, bf16[2,512,256]{2,1,0:T(8,128)(2,1)S(1)} %get-tuple-element.80.refs_0_, bf16[2,512,256]{2,1,0:T(8,128)(2,1)S(1)} %collective-permute-done.20.refs_1_, ...), custom_call_target="tpu_custom_call" | custom-call | flops 1 | bytes 1 | tf_op jit(solution)/shard_map/unit_work/pallas_call | solution.py:450
  177.2 1.0 copy-done.9
  182.2 4.0 %unit_work.9 = (bf16[2,2,256,256]{3,2,1,0:T(8,128)(2,1)S(1)}, f32[1,512]{1,0:T(1,128)S(1)}) custom-call(s32[148]{0:T(256)S(1)} %bitcast.36, bf16[2,512,256]{2,1,0:T(8,128)(2,1)S(1)} %copy-done.11, bf16[2,512,256]{2,1,0:T(8,128)(2,1)S(1)} %collective-permute-done.20.refs_1_, bf16[2,512,256]{2,1,0:T(8,128)(2,1)S(1)} %collective-permute-done.21.refs_2_, ...), custom_call_target="tpu_custom_call" | custom-call | flops 1 | bytes 1 | tf_op jit(solution)/shard_map/unit_work/pallas_call | solution.py:450
  186.3 2.8 %collective-permute-start.32 = (f32[2,128]{1,0:T(2,128)S(1)}, f32[2,128]{1,0:T(2,128)S(1)}, u32[]{:S(2)}, u32[]{:S(2)}) collective-permute-start(f32[2,128]{1,0:T(2,128)S(1)} %get-tuple-element.106), channel_id=1, source_target_pairs={{0,8},{1,9},{2,10},{3,11},{4,0},{5,1},{6,2},{7,3},{8,12},{9,13},{1... | collective-permute-start | bytes 3080 | tf_op jit(solution)/shard_map/ppermute | solution.py:669
  190.0 6.8 %collective-permute-start.31 = (f32[2,128]{1,0:T(2,128)S(1)}, f32[2,128]{1,0:T(2,128)S(1)}, u32[]{:S(2)}, u32[]{:S(2)}) collective-permute-start(f32[2,128]{1,0:T(2,128)S(1)} %get-tuple-element.102), channel_id=1, source_target_pairs={{0,12},{1,13},{2,14},{3,15},{4,8},{5,9},{6,10},{7,11},{8,4},{9,5},... | collective-permute-start | bytes 3080 | tf_op jit(solution)/shard_map/ppermute | solution.py:669
  197.1 4.7 %put_residuals.3.refs_2_ = bf16[2,8,2,256,256]{4,3,2,1,0:T(8,128)(2,1)} custom-call(s32[148]{0:T(256)S(1)} %bitcast.37, bf16[2,2,256,256]{3,2,1,0:T(8,128)(2,1)S(1)} %copy-done.29, bf16[2,2,256,256]{3,2,1,0:T(8,128)(2,1)S(1)} %copy-done.31, bf16[2,2,256,256]{3,2,1,0:T(8,128)(2,1)} %collective-permute-done.29.refs_2_, bf16[2,2,256,256]{3,2,1,0:T(8,128)(2,1)S(1)} %copy-done.33), custom_call_target="tpu_custom_call" | custom-call | flops 1 | bytes 1 | tf_op jit(solution)/shard_map/put_residuals/pallas_call | solution.py:490
  201.8 3.2 %put_residuals.4.refs_2_ = bf16[2,8,2,256,256]{4,3,2,1,0:T(8,128)(2,1)} custom-call(s32[148]{0:T(256)S(1)} %bitcast.38, bf16[2,2,256,256]{3,2,1,0:T(8,128)(2,1)} %collective-permute-done.30.refs_0_, bf16[2,2,256,256]{3,2,1,0:T(8,128)(2,1)S(1)} %get-tuple-element.95.refs_1_, ...), custom_call_target="tpu_custom_call", output_to_operand_aliasing={{}: (3, {})} | custom-call | flops 1 | bytes 1 | tf_op jit(solution)/shard_map/put_residuals/pallas_call | solution.py:490
  205.1 1.5 collective-permute-start.36
  206.6 1.5 collective-permute-start.35
  208.1 3.0 %collective-permute-done.27.refs_1_ = bf16[2,2,256,256]{3,2,1,0:T(8,128)(2,1)S(1)} collective-permute-done((bf16[2,2,256,256]{3,2,1,0:T(8,128)(2,1)S(1)}, bf16[2,2,256,256]{3,2,1,0:T(8,128)(2,1)S(1)}, u32[]{:S(2)}, u32[]{:S(2)}) %collective-permute-start.27) | collective-permute-done | bytes 524320 | tf_op jit(solution)/shard_map/ppermute | solution.py:669
  211.2 2.1 put_residuals.5
  (159 shorter events, 27.2 us)
Async XLA Ops:
  7.2 1.9 collective-permute-start
  12.0 19.1 %collective-permute-start.1 = (bf16[2,528,256]{2,1,0:T(8,128)(2,1)S(1)}, bf16[2,528,256]{2,1,0:T(8,128)(2,1)S(1)}, u32[]{:S(2)}, u32[]{:S(2)}) collective-permute-start(bf16[2,528,256]{2,1,0:T(8,128)(2,1)S(1)} %build_factors.3.refs_0_), channel_id=1, source_target_pairs={{0,4},{1,5},{2,6},{3,7},{4,12},{5,13},{6,14},{7,15},{8,0},{9,1},{1... | collective-permute-start | bytes 1622024 | tf_op jit(solution)/shard_map/ppermute | solution.py:669
  17.6 26.7 %copy-start.35 = (s32[1,148]{1,0:T(1,128)S(1)}, s32[1,148]{1,0:T(1,128)}, u32[]{:S(2)}) copy-start(s32[1,148]{1,0:T(1,128)} %constant_dynamic-slice_fusion) | copy-start | bytes 1780
  17.6 10.8 %collective-permute-start.5 = (bf16[80,2048]{1,0:T(8,128)(2,1)}, bf16[80,2048]{1,0:T(8,128)(2,1)S(1)}, u32[]{:S(2)}, u32[]{:S(2)}) collective-permute-start(bf16[80,2048]{1,0:T(8,128)(2,1)} %get-tuple-element.56), channel_id=1, source_target_pairs={{0,2},{1,3},{2,0},{3,1},{4,6},{5,7},{6,4},{7,5},{8,10},{9,11},{10,... | collective-permute-start | bytes 983048 | tf_op jit(solution)/shard_map/ppermute | solution.py:669
  19.1 22.1 %collective-permute-start.2 = (bf16[2,528,256]{2,1,0:T(8,128)(2,1)S(1)}, bf16[2,528,256]{2,1,0:T(8,128)(2,1)S(1)}, u32[]{:S(2)}, u32[]{:S(2)}) collective-permute-start(bf16[2,528,256]{2,1,0:T(8,128)(2,1)S(1)} %build_factors.3.refs_0_), channel_id=1, source_target_pairs={{0,8},{1,9},{2,10},{3,11},{4,0},{5,1},{6,2},{7,3},{8,12},{9,13},{1... | collective-permute-start | bytes 1622024 | tf_op jit(solution)/shard_map/ppermute | solution.py:669
  20.5 23.8 %collective-permute-start.6 = (bf16[80,2048]{1,0:T(8,128)(2,1)}, bf16[80,2048]{1,0:T(8,128)(2,1)S(1)}, u32[]{:S(2)}, u32[]{:S(2)}) collective-permute-start(bf16[80,2048]{1,0:T(8,128)(2,1)} %get-tuple-element.57), channel_id=1, source_target_pairs={{0,3},{1,2},{2,1},{3,0},{4,7},{5,6},{6,5},{7,4},{8,11},{9,10},{10,... | collective-permute-start | bytes 983048 | tf_op jit(solution)/shard_map/ppermute | solution.py:669
  31.1 17.5 %collective-permute-start.11 = (bf16[64,2048]{1,0:T(8,128)(2,1)}, bf16[64,2048]{1,0:T(8,128)(2,1)S(1)}, u32[]{:S(2)}, u32[]{:S(2)}) collective-permute-start(bf16[64,2048]{1,0:T(8,128)(2,1)} %get-tuple-element.60), channel_id=1, source_target_pairs={{0,3},{1,2},{2,1},{3,0},{4,7},{5,6},{6,5},{7,4},{8,11},{9,10},{10,... | collective-permute-start | bytes 786440 | tf_op jit(solution)/shard_map/ppermute | solution.py:669
  31.1 19.2 %collective-permute-start.3 = (bf16[528,256]{1,0:T(8,128)(2,1)S(1)}, bf16[528,256]{1,0:T(8,128)(2,1)S(1)}, u32[]{:S(2)}, u32[]{:S(2)}) collective-permute-start(bf16[528,256]{1,0:T(8,128)(2,1)S(1)} %slice_bitcast_fusion.3), channel_id=1, source_target_pairs={{0,4},{1,5},{2,6},{3,7},{4,12},{5,13},{6,14},{7,15},{8,0},{9,1},{1... | collective-permute-start | bytes 811016 | tf_op jit(solution)/shard_map/ppermute | solution.py:669
  41.2 14.8 %collective-permute-start.4 = (bf16[528,256]{1,0:T(8,128)(2,1)S(1)}, bf16[528,256]{1,0:T(8,128)(2,1)S(1)}, u32[]{:S(2)}, u32[]{:S(2)}) collective-permute-start(bf16[528,256]{1,0:T(8,128)(2,1)S(1)} %slice_bitcast_fusion.2), channel_id=1, source_target_pairs={{0,8},{1,9},{2,10},{3,11},{4,0},{5,1},{6,2},{7,3},{8,12},{9,13},{1... | collective-permute-start | bytes 811016 | tf_op jit(solution)/shard_map/ppermute | solution.py:669
  42.7 18.0 %collective-permute-start.12 = (bf16[64,2048]{1,0:T(8,128)(2,1)}, bf16[64,2048]{1,0:T(8,128)(2,1)}, u32[]{:S(2)}, u32[]{:S(2)}) collective-permute-start(bf16[64,2048]{1,0:T(8,128)(2,1)} %get-tuple-element.63), channel_id=1, source_target_pairs={{0,2},{1,3},{2,0},{3,1},{4,6},{5,7},{6,4},{7,5},{8,10},{9,11},{10,... | collective-permute-start | bytes 786440 | tf_op jit(solution)/shard_map/ppermute | solution.py:669
  46.6 26.0 %collective-permute-start.7 = (bf16[2,528,256]{2,1,0:T(8,128)(2,1)S(1)}, bf16[2,528,256]{2,1,0:T(8,128)(2,1)}, u32[]{:S(2)}, u32[]{:S(2)}) collective-permute-start(bf16[2,528,256]{2,1,0:T(8,128)(2,1)S(1)} %build_factors.4.refs_5_), channel_id=1, source_target_pairs={{0,4},{1,5},{2,6},{3,7},{4,12},{5,13},{6,14},{7,15},{8,0},{9,1},{1... | collective-permute-start | bytes 1622024 | tf_op jit(solution)/shard_map/ppermute | solution.py:669
  49.3 28.4 %collective-permute-start.8 = (bf16[2,528,256]{2,1,0:T(8,128)(2,1)S(1)}, bf16[2,528,256]{2,1,0:T(8,128)(2,1)}, u32[]{:S(2)}, u32[]{:S(2)}) collective-permute-start(bf16[2,528,256]{2,1,0:T(8,128)(2,1)S(1)} %build_factors.4.refs_5_), channel_id=1, source_target_pairs={{0,8},{1,9},{2,10},{3,11},{4,0},{5,1},{6,2},{7,3},{8,12},{9,13},{1... | collective-permute-start | bytes 1622024 | tf_op jit(solution)/shard_map/ppermute | solution.py:669
  56.7 58.9 %copy-start.44 = (s32[8,2048]{1,0:T(8,128)S(1)}, s32[8,2048]{1,0:T(8,128)}, u32[]{:S(2)}) copy-start(s32[8,2048]{1,0:T(8,128)} %param.14) | copy-start | bytes 196612
  60.7 58.5 %copy-start.3 = (bf16[2,528,256]{2,1,0:T(8,128)(2,1)S(1)}, bf16[2,528,256]{2,1,0:T(8,128)(2,1)}, u32[]{:S(2)}) copy-start(bf16[2,528,256]{2,1,0:T(8,128)(2,1)} %copy-done.2) | copy-start | bytes 1622020
  60.7 58.5 %copy-start.5 = (bf16[2,528,256]{2,1,0:T(8,128)(2,1)S(1)}, bf16[2,528,256]{2,1,0:T(8,128)(2,1)}, u32[]{:S(2)}) copy-start(bf16[2,528,256]{2,1,0:T(8,128)(2,1)} %copy-done.4) | copy-start | bytes 1622020
  60.7 58.5 %copy-start.15 = (bf16[528,256]{1,0:T(8,128)(2,1)S(1)}, bf16[528,256]{1,0:T(8,128)(2,1)}, u32[]{:S(2)}) copy-start(bf16[528,256]{1,0:T(8,128)(2,1)} %copy-done.14) | copy-start | bytes 811012
  60.7 58.5 %copy-start.17 = (bf16[528,256]{1,0:T(8,128)(2,1)S(1)}, bf16[528,256]{1,0:T(8,128)(2,1)}, u32[]{:S(2)}) copy-start(bf16[528,256]{1,0:T(8,128)(2,1)} %copy-done.16) | copy-start | bytes 811012
  60.7 26.3 %collective-permute-start.13 = (bf16[2,2,2,256,256]{4,3,2,1,0:T(8,128)(2,1)}, bf16[2,2,2,256,256]{4,3,2,1,0:T(8,128)(2,1)S(1)}, u32[]{:S(2)}, u32[]{:S(2)}) collective-permute-start(bf16[2,2,2,256,256]{4,3,2,1,0:T(8,128)(2,1)} %get-tuple-element.64), channel_id=1, source_target_pairs={{0,2},{1,3},{2,0},{3,1},{4,6},{5,7},{6,4},{7,5},{8,10},{9,11},{10,... | collective-permute-start | bytes 3145736 | tf_op jit(solution)/shard_map/ppermute | solution.py:669
  63.6 1.7 collective-permute-start.16
  69.2 30.1 %copy-start.45 = (bf16[2,2,2,256,256]{4,3,2,1,0:T(8,128)(2,1)S(1)}, bf16[2,2,2,256,256]{4,3,2,1,0:T(8,128)(2,1)}, u32[]{:S(2)}) copy-start(bf16[2,2,2,256,256]{4,3,2,1,0:T(8,128)(2,1)} %get-tuple-element.88) | copy-start | bytes 3145732
  72.6 95.9 %copy-start.10 = (bf16[2,512,256]{2,1,0:T(8,128)(2,1)}, bf16[2,512,256]{2,1,0:T(8,128)(2,1)S(1)}, u32[]{:S(2)}) copy-start(bf16[2,512,256]{2,1,0:T(8,128)(2,1)S(1)} %get-tuple-element.80.refs_0_) | copy-start | bytes 1572868
  72.6 95.9 %copy-start.12 = (bf16[2,512,256]{2,1,0:T(8,128)(2,1)}, bf16[2,512,256]{2,1,0:T(8,128)(2,1)S(1)}, u32[]{:S(2)}) copy-start(bf16[2,512,256]{2,1,0:T(8,128)(2,1)S(1)} %get-tuple-element.76.refs_5_) | copy-start | bytes 1572868
  72.7 43.0 %collective-permute-start.20 = (bf16[2,512,256]{2,1,0:T(8,128)(2,1)S(1)}, bf16[2,512,256]{2,1,0:T(8,128)(2,1)S(1)}, u32[]{:S(2)}, u32[]{:S(2)}) collective-permute-start(bf16[2,512,256]{2,1,0:T(8,128)(2,1)S(1)} %get-tuple-element.80.refs_0_), channel_id=1, source_target_pairs={{0,4},{1,5},{2,6},{3,7},{4,12},{5,13},{6,14},{7,15},{8,0},{9,1},{1... | collective-permute-start | bytes 1572872 | tf_op jit(solution)/shard_map/ppermute | solution.py:669
  78.7 20.6 %collective-permute-start.10 = (bf16[528,256]{1,0:T(8,128)(2,1)S(1)}, bf16[528,256]{1,0:T(8,128)(2,1)S(1)}, u32[]{:S(2)}, u32[]{:S(2)}) collective-permute-start(bf16[528,256]{1,0:T(8,128)(2,1)S(1)} %slice_bitcast_fusion), channel_id=1, source_target_pairs={{0,8},{1,9},{2,10},{3,11},{4,0},{5,1},{6,2},{7,3},{8,12},{9,13},{1... | collective-permute-start | bytes 811016 | tf_op jit(solution)/shard_map/ppermute | solution.py:669
  80.9 21.3 %collective-permute-start.9 = (bf16[528,256]{1,0:T(8,128)(2,1)S(1)}, bf16[528,256]{1,0:T(8,128)(2,1)S(1)}, u32[]{:S(2)}, u32[]{:S(2)}) collective-permute-start(bf16[528,256]{1,0:T(8,128)(2,1)S(1)} %slice_bitcast_fusion.1), channel_id=1, source_target_pairs={{0,4},{1,5},{2,6},{3,7},{4,12},{5,13},{6,14},{7,15},{8,0},{9,1},{1... | collective-permute-start | bytes 811016 | tf_op jit(solution)/shard_map/ppermute | solution.py:669
  87.0 32.2 %copy-start.42 = (bf16[2,2,2,256,256]{4,3,2,1,0:T(8,128)(2,1)}, bf16[2,2,2,256,256]{4,3,2,1,0:T(8,128)(2,1)S(1)}, u32[]{:S(2)}) copy-start(bf16[2,2,2,256,256]{4,3,2,1,0:T(8,128)(2,1)S(1)} %collective-permute-done.13.refs_10_) | copy-start | bytes 3145732
  87.0 36.8 %collective-permute-start.15 = (bf16[2,2,2,256,256]{4,3,2,1,0:T(8,128)(2,1)}, bf16[2,2,2,256,256]{4,3,2,1,0:T(8,128)(2,1)S(1)}, u32[]{:S(2)}, u32[]{:S(2)}) collective-permute-start(bf16[2,2,2,256,256]{4,3,2,1,0:T(8,128)(2,1)} %get-tuple-element.68), channel_id=1, source_target_pairs={{0,3},{1,2},{2,1},{3,0},{4,7},{5,6},{6,5},{7,4},{8,11},{9,10},{10,... | collective-permute-start | bytes 3145736 | tf_op jit(solution)/shard_map/ppermute | solution.py:669
  87.3 28.4 %collective-permute-start.21 = (bf16[2,512,256]{2,1,0:T(8,128)(2,1)S(1)}, bf16[2,512,256]{2,1,0:T(8,128)(2,1)S(1)}, u32[]{:S(2)}, u32[]{:S(2)}) collective-permute-start(bf16[2,512,256]{2,1,0:T(8,128)(2,1)S(1)} %get-tuple-element.80.refs_0_), channel_id=1, source_target_pairs={{0,8},{1,9},{2,10},{3,11},{4,0},{5,1},{6,2},{7,3},{8,12},{9,13},{1... | collective-permute-start | bytes 1572872 | tf_op jit(solution)/shard_map/ppermute | solution.py:669
  99.3 53.0 %collective-permute-start.28 = (bf16[2,2,2,256,256]{4,3,2,1,0:T(8,128)(2,1)S(1)}, bf16[2,2,2,256,256]{4,3,2,1,0:T(8,128)(2,1)S(1)}, u32[]{:S(2)}, u32[]{:S(2)}) collective-permute-start(bf16[2,2,2,256,256]{4,3,2,1,0:T(8,128)(2,1)S(1)} %copy-done.45), channel_id=1, source_target_pairs={{0,1},{1,0},{2,3},{3,2},{4,5},{5,4},{6,7},{7,6},{8,9},{9,8},{10,11... | collective-permute-start | bytes 3145736 | tf_op jit(solution)/shard_map/ppermute | solution.py:669
  102.2 26.8 %collective-permute-start.17 = (bf16[2,512,256]{2,1,0:T(8,128)(2,1)S(1)}, bf16[2,512,256]{2,1,0:T(8,128)(2,1)S(1)}, u32[]{:S(2)}, u32[]{:S(2)}) collective-permute-start(bf16[2,512,256]{2,1,0:T(8,128)(2,1)S(1)} %get-tuple-element.76.refs_5_), channel_id=1, source_target_pairs={{0,4},{1,5},{2,6},{3,7},{4,12},{5,13},{6,14},{7,15},{8,0},{9,1},{1... | collective-permute-start | bytes 1572872 | tf_op jit(solution)/shard_map/ppermute | solution.py:669
  115.6 27.0 %collective-permute-start.18 = (bf16[2,512,256]{2,1,0:T(8,128)(2,1)S(1)}, bf16[2,512,256]{2,1,0:T(8,128)(2,1)S(1)}, u32[]{:S(2)}, u32[]{:S(2)}) collective-permute-start(bf16[2,512,256]{2,1,0:T(8,128)(2,1)S(1)} %get-tuple-element.76.refs_5_), channel_id=1, source_target_pairs={{0,8},{1,9},{2,10},{3,11},{4,0},{5,1},{6,2},{7,3},{8,12},{9,13},{1... | collective-permute-start | bytes 1572872 | tf_op jit(solution)/shard_map/ppermute | solution.py:669
  115.7 29.2 %collective-permute-start.22 = (bf16[512,256]{1,0:T(8,128)(2,1)S(1)}, bf16[512,256]{1,0:T(8,128)(2,1)S(1)}, u32[]{:S(2)}, u32[]{:S(2)}) collective-permute-start(bf16[512,256]{1,0:T(8,128)(2,1)S(1)} %slice_bitcast_fusion.7), channel_id=1, source_target_pairs={{0,4},{1,5},{2,6},{3,7},{4,12},{5,13},{6,14},{7,15},{8,0},{9,1},{1... | collective-permute-start | bytes 786440 | tf_op jit(solution)/shard_map/ppermute | solution.py:669
  123.8 38.7 %collective-permute-start.23 = (bf16[512,256]{1,0:T(8,128)(2,1)S(1)}, bf16[512,256]{1,0:T(8,128)(2,1)S(1)}, u32[]{:S(2)}, u32[]{:S(2)}) collective-permute-start(bf16[512,256]{1,0:T(8,128)(2,1)S(1)} %slice_bitcast_fusion.6), channel_id=1, source_target_pairs={{0,8},{1,9},{2,10},{3,11},{4,0},{5,1},{6,2},{7,3},{8,12},{9,13},{1... | collective-permute-start | bytes 786440 | tf_op jit(solution)/shard_map/ppermute | solution.py:669
  129.1 39.5 %copy-start.6 = (bf16[2,512,256]{2,1,0:T(8,128)(2,1)}, bf16[2,512,256]{2,1,0:T(8,128)(2,1)S(1)}, u32[]{:S(2)}) copy-start(bf16[2,512,256]{2,1,0:T(8,128)(2,1)S(1)} %collective-permute-done.17.refs_6_) | copy-start | bytes 1572868
  129.1 32.5 %collective-permute-start.14 = (bf16[2,2,256,256]{3,2,1,0:T(8,128)(2,1)S(1)}, bf16[2,2,256,256]{3,2,1,0:T(8,128)(2,1)S(1)}, u32[]{:S(2)}, u32[]{:S(2)}) collective-permute-start(bf16[2,2,256,256]{3,2,1,0:T(8,128)(2,1)S(1)} %get-tuple-element.66), channel_id=1, source_target_pairs={{0,2},{1,3},{2,0},{3,1},{4,6},{5,7},{6,4},{7,5},{8,10},{9,11},{10,... | collective-permute-start | bytes 1572872 | tf_op jit(solution)/shard_map/ppermute | solution.py:669
  142.6 19.8 %collective-permute-start.19 = (bf16[2,2,256,256]{3,2,1,0:T(8,128)(2,1)S(1)}, bf16[2,2,256,256]{3,2,1,0:T(8,128)(2,1)S(1)}, u32[]{:S(2)}, u32[]{:S(2)}) collective-permute-start(bf16[2,2,256,256]{3,2,1,0:T(8,128)(2,1)S(1)} %get-tuple-element.77), channel_id=1, source_target_pairs={{0,3},{1,2},{2,1},{3,0},{4,7},{5,6},{6,5},{7,4},{8,11},{9,10},{10,... | collective-permute-start | bytes 1572872 | tf_op jit(solution)/shard_map/ppermute | solution.py:669
  144.9 17.5 %collective-permute-start.24 = (bf16[512,256]{1,0:T(8,128)(2,1)S(1)}, bf16[512,256]{1,0:T(8,128)(2,1)S(1)}, u32[]{:S(2)}, u32[]{:S(2)}) collective-permute-start(bf16[512,256]{1,0:T(8,128)(2,1)S(1)} %slice_bitcast_fusion.5), channel_id=1, source_target_pairs={{0,4},{1,5},{2,6},{3,7},{4,12},{5,13},{6,14},{7,15},{8,0},{9,1},{1... | collective-permute-start | bytes 786440 | tf_op jit(solution)/shard_map/ppermute | solution.py:669
  152.3 11.0 %collective-permute-start.25 = (bf16[512,256]{1,0:T(8,128)(2,1)S(1)}, bf16[512,256]{1,0:T(8,128)(2,1)S(1)}, u32[]{:S(2)}, u32[]{:S(2)}) collective-permute-start(bf16[512,256]{1,0:T(8,128)(2,1)S(1)} %slice_bitcast_fusion.4), channel_id=1, source_target_pairs={{0,8},{1,9},{2,10},{3,11},{4,0},{5,1},{6,2},{7,3},{8,12},{9,13},{1... | collective-permute-start | bytes 786440 | tf_op jit(solution)/shard_map/ppermute | solution.py:669
  162.4 27.6 %collective-permute-start.29 = (bf16[2,2,256,256]{3,2,1,0:T(8,128)(2,1)}, bf16[2,2,256,256]{3,2,1,0:T(8,128)(2,1)}, u32[]{:S(2)}, u32[]{:S(2)}) collective-permute-start(bf16[2,2,256,256]{3,2,1,0:T(8,128)(2,1)} %get-tuple-element.90), channel_id=1, source_target_pairs={{0,1},{1,0},{2,3},{3,2},{4,5},{5,4},{6,7},{7,6},{8,9},{9,8},{10,11... | collective-permute-start | bytes 1572872 | tf_op jit(solution)/shard_map/ppermute | solution.py:669
  167.9 28.9 %collective-permute-start.26 = (bf16[2,2,256,256]{3,2,1,0:T(8,128)(2,1)}, bf16[2,2,256,256]{3,2,1,0:T(8,128)(2,1)S(1)}, u32[]{:S(2)}, u32[]{:S(2)}) collective-permute-start(bf16[2,2,256,256]{3,2,1,0:T(8,128)(2,1)} %get-tuple-element.83), channel_id=1, source_target_pairs={{0,2},{1,3},{2,0},{3,1},{4,6},{5,7},{6,4},{7,5},{8,10},{9,11},{10,... | collective-permute-start | bytes 1572872 | tf_op jit(solution)/shard_map/ppermute | solution.py:669
  175.8 26.0 %collective-permute-start.30 = (bf16[2,2,256,256]{3,2,1,0:T(8,128)(2,1)}, bf16[2,2,256,256]{3,2,1,0:T(8,128)(2,1)}, u32[]{:S(2)}, u32[]{:S(2)}) collective-permute-start(bf16[2,2,256,256]{3,2,1,0:T(8,128)(2,1)} %get-tuple-element.93), channel_id=1, source_target_pairs={{0,1},{1,0},{2,3},{3,2},{4,5},{5,4},{6,7},{7,6},{8,9},{9,8},{10,11... | collective-permute-start | bytes 1572872 | tf_op jit(solution)/shard_map/ppermute | solution.py:669
  186.3 18.7 %collective-permute-start.32 = (f32[2,128]{1,0:T(2,128)S(1)}, f32[2,128]{1,0:T(2,128)S(1)}, u32[]{:S(2)}, u32[]{:S(2)}) collective-permute-start(f32[2,128]{1,0:T(2,128)S(1)} %get-tuple-element.106), channel_id=1, source_target_pairs={{0,8},{1,9},{2,10},{3,11},{4,0},{5,1},{6,2},{7,3},{8,12},{9,13},{1... | collective-permute-start | bytes 3080 | tf_op jit(solution)/shard_map/ppermute | solution.py:669
  189.0 16.0 %collective-permute-start.33 = (f32[2,128]{1,0:T(2,128)S(1)}, f32[2,128]{1,0:T(2,128)S(1)}, u32[]{:S(2)}, u32[]{:S(2)}) collective-permute-start(f32[2,128]{1,0:T(2,128)S(1)} %get-tuple-element.105), channel_id=1, source_target_pairs={{0,4},{1,5},{2,6},{3,7},{4,12},{5,13},{6,14},{7,15},{8,0},{9,1},{1... | collective-permute-start | bytes 3080 | tf_op jit(solution)/shard_map/ppermute | solution.py:669
  190.0 15.0 %collective-permute-start.31 = (f32[2,128]{1,0:T(2,128)S(1)}, f32[2,128]{1,0:T(2,128)S(1)}, u32[]{:S(2)}, u32[]{:S(2)}) collective-permute-start(f32[2,128]{1,0:T(2,128)S(1)} %get-tuple-element.102), channel_id=1, source_target_pairs={{0,12},{1,13},{2,14},{3,15},{4,8},{5,9},{6,10},{7,11},{8,4},{9,5},... | collective-permute-start | bytes 3080 | tf_op jit(solution)/shard_map/ppermute | solution.py:669
  196.8 14.2 %collective-permute-start.27 = (bf16[2,2,256,256]{3,2,1,0:T(8,128)(2,1)S(1)}, bf16[2,2,256,256]{3,2,1,0:T(8,128)(2,1)S(1)}, u32[]{:S(2)}, u32[]{:S(2)}) collective-permute-start(bf16[2,2,256,256]{3,2,1,0:T(8,128)(2,1)S(1)} %get-tuple-element.85), channel_id=1, source_target_pairs={{0,3},{1,2},{2,1},{3,0},{4,7},{5,6},{6,5},{7,4},{8,11},{9,10},{10,... | collective-permute-start | bytes 1572872 | tf_op jit(solution)/shard_map/ppermute | solution.py:669
  205.1 8.3 %collective-permute-start.36 = (f32[2,32]{1,0:T(2,128)S(1)}, f32[2,32]{1,0:T(2,128)S(1)}, u32[]{:S(2)}, u32[]{:S(2)}) collective-permute-start(f32[2,32]{1,0:T(2,128)S(1)} %get-tuple-element.108), channel_id=1, source_target_pairs={{0,3},{1,2},{2,1},{3,0},{4,7},{5,6},{6,5},{7,4},{8,11},{9,10},{10,... | collective-permute-start | bytes 776 | tf_op jit(solution)/shard_map/ppermute | solution.py:669
  206.6 6.8 %collective-permute-start.35 = (f32[2,32]{1,0:T(2,128)S(1)}, f32[2,32]{1,0:T(2,128)S(1)}, u32[]{:S(2)}, u32[]{:S(2)}) collective-permute-start(f32[2,32]{1,0:T(2,128)S(1)} %get-tuple-element.109), channel_id=1, source_target_pairs={{0,2},{1,3},{2,0},{3,1},{4,6},{5,7},{6,4},{7,5},{8,10},{9,11},{10,... | collective-permute-start | bytes 776 | tf_op jit(solution)/shard_map/ppermute | solution.py:669
  211.0 2.3 %collective-permute-start.34 = (f32[2,32]{1,0:T(2,128)S(1)}, f32[2,32]{1,0:T(2,128)S(1)}, u32[]{:S(2)}, u32[]{:S(2)}) collective-permute-start(f32[2,32]{1,0:T(2,128)S(1)} %get-tuple-element.103), channel_id=1, source_target_pairs={{0,1},{1,0},{2,3},{3,2},{4,5},{5,4},{6,7},{7,6},{8,9},{9,8},{10,11... | collective-permute-start | bytes 776 | tf_op jit(solution)/shard_map/ppermute | solution.py:669
  (35 other events, 245.0 us)

commit v7 on v6

--- a/solution.py
+++ b/solution.py
@@ -42,6 +42,7 @@
 
 
 def build_kernel(sets, slot_ids, pieces, bright_rows, width, tab_ref, *refs):
+    refs, scratch_ref = refs[:-1], refs[-1]
     uvw_ref, outs = refs[-1 - len(pieces)], refs[-len(pieces) :]
     per_group = sets[0][0]
     span = outs[0].shape[2]
@@ -54,11 +55,10 @@
             beam = [beam_ref.at[0, 0], beam_ref.at[0, 1]]
         else:
             beam = [beam_ref.at[pl.ds(n * per_group, per_group)] for n in (0, 1)]
-        small_ref = refs[small_at]
-        if small_ref.dtype == jnp.float32:
-            small = small_ref[...]
+        if refs[small_at].dtype == jnp.float32:
+            small = small_rows(scratch_ref, *refs[small_at : small_at + 3])
         else:
-            small = unsplit(small_ref, 2 * per_group, width)
+            small = unsplit(refs[small_at], 2 * per_group, width)
         lanes = lax.broadcasted_iota(jnp.int32, (per_group, width), 1)
         rows = lax.broadcasted_iota(jnp.int32, (per_group, width), 0)
 
@@ -66,7 +66,9 @@
             return jnp.sum(jnp.where(chosen, small[row : row + 1, :], 0.0), axis=1, keepdims=True)
 
         def chosen_at(index):
-            listed = pick(lanes == (tab_ref[0] + index) * per_group + rows, 3)
+            here = lax.broadcasted_iota(jnp.int32, small.shape, 0) == LIST_ROW + tab_ref[0] + index
+            line = jnp.sum(jnp.where(here, small, 0.0), axis=0, keepdims=True)
+            listed = jnp.sum(jnp.where(lanes == rows, line, 0.0), axis=1, keepdims=True)
             return listed.astype(jnp.int32) == lanes
 
         group = part * per_group
@@ -108,8 +110,22 @@
             outs[0][part, pl.ds(len(pieces[0]) * count, bright_rows)] = block
 
 
+def small_rows(rows_ref, dirs_ref, flux_ref, list_ref):
+    rows_ref[...] = jnp.zeros_like(rows_ref)
+    rows_ref[0:2, 0 : dirs_ref.shape[1]] = dirs_ref[...]
+    rows_ref[2:3, 0 : flux_ref.shape[1]] = flux_ref[...]
+    slots, count = list_ref.shape
+    rows_ref[LIST_ROW : LIST_ROW + slots, 0:count] = list_ref[...].astype(jnp.float32)
+    return rows_ref[...]
+
+
+LIST_ROW = 8
+SMALL_ROWS = 16
+
+
 def unsplit(message_ref, start, width):
-    terms = [message_ref[pl.ds(start, 16), pl.ds(n * width, width)].astype(jnp.float32) for n in range(3)]
+    rows = pl.ds(start, SMALL_ROWS)
+    terms = [message_ref[rows, pl.ds(n * width, width)].astype(jnp.float32) for n in range(3)]
     return (terms[0] + terms[1]) + terms[2]
 
 
@@ -134,7 +150,7 @@
     for n, small in enumerate(smalls):
         at = next((k for k, known in enumerate(operands) if known is small), len(operands))
         if at == len(operands):
-            operands.append(small)
+            operands += small if isinstance(small, tuple) else [small]
         sets.append((per_group, n, at))
     in_specs += [whole] * (len(operands) - len(in_specs))
     in_specs.append(pl.BlockSpec((1, 3, antennas), lambda n, tab: (tab[0] + index, 0, 0)))
@@ -149,6 +165,7 @@
             grid=(1,),
             in_specs=in_specs,
             out_specs=[whole] * len(pieces),
+            scratch_shapes=[pltpu.VMEM((SMALL_ROWS, small_width), jnp.float32)],
         ),
         out_shape=[jax.ShapeDtypeStruct(shape, jnp.bfloat16) for shape in shapes],
         compiler_params=pltpu.CompilerParams(vmem_limit_bytes=40 * 1024 * 1024),
@@ -160,28 +177,39 @@
 LITTLE = pl.CostEstimate(flops=1, bytes_accessed=1, transcendentals=0)
 
 
-def message_kernel(per_group, tab_ref, *refs):
-    outs = [ref for ref in refs if ref.dtype == jnp.bfloat16 and len(ref.shape) == 2]
-    small_ref = refs[len(outs)] if len(refs) > 2 * len(outs) else None
-    for beam_ref, out_ref in zip(refs, outs):
+def message_kernel(count, with_small, tab_ref, *refs):
+    beams, refs = refs[:count], refs[count:]
+    if with_small:
+        smalls, outs, scratch_ref = refs[:3], refs[3:-1], refs[-1]
+        terms = []
+        rest = small_rows(scratch_ref, *smalls)
+        width = rest.shape[1]
+        for _ in range(3):
+            terms.append(rest.astype(jnp.bfloat16))
+            rest = rest - terms[-1].astype(jnp.float32)
+    else:
+        outs = refs
+    for beam_ref, out_ref in zip(beams, outs):
+        per_group = beam_ref.shape[2]
         for part in (0, 1):
             out_ref[pl.ds(part * per_group, per_group)] = beam_ref[0, part]
-        if small_ref is not None:
-            count, width = small_ref.shape
-            rest = jnp.concatenate([small_ref[...], jnp.zeros((16 - count, width), jnp.float32)], 0)
-            out_ref[pl.ds(2 * per_group, 16)] = jnp.zeros((16, out_ref.shape[1]), jnp.bfloat16)
-            for n in range(3):
-                term = rest.astype(jnp.bfloat16)
-                out_ref[pl.ds(2 * per_group, 16), pl.ds(n * width, width)] = term
-                rest = rest - term.astype(jnp.float32)
+        if with_small:
+            rows = pl.ds(2 * per_group, SMALL_ROWS)
+            out_ref[rows] = jnp.zeros((SMALL_ROWS, out_ref.shape[1]), jnp.bfloat16)
+            for n, term in enumerate(terms):
+                out_ref[rows, pl.ds(n * width, width)] = term
 
 
 def messages_for(beam, index, others, small, table):
     _, _, per_group, antennas = beam.shape
-    rows = 2 * per_group + (0 if small is None else 16)
+    smalls = small or ()
+    rows = 2 * per_group + (SMALL_ROWS if smalls else 0)
     whole = pl.BlockSpec(memory_space=pltpu.VMEM)
+    scratch = []
+    if smalls:
+        scratch.append(pltpu.VMEM((SMALL_ROWS, smalls[0].shape[1]), jnp.float32))
     return pl.pallas_call(
-        functools.partial(message_kernel, per_group),
+        functools.partial(message_kernel, len(others), bool(smalls)),
         grid_spec=pltpu.PrefetchScalarGridSpec(
             num_scalar_prefetch=1,
             grid=(1,),
@@ -191,13 +219,14 @@
                 )
                 for m in others
             ]
-            + ([] if small is None else [whole]),
+            + [whole for _ in smalls],
             out_specs=[whole for _ in others],
+            scratch_shapes=scratch,
         ),
         out_shape=[jax.ShapeDtypeStruct((rows, antennas), jnp.bfloat16) for _ in others],
         cost_estimate=LITTLE,
         name="messages_for",
-    )(table, *[beam] * len(others), *([] if small is None else [small]))
+    )(table, *[beam] * len(others), *smalls)
 
 
 def slice_kernel(count, tab_ref, *refs):
@@ -563,14 +592,6 @@
         self.targets_per_home = units_dev * 2
 
 
-def packed_small(source_dirs, source_flux, visible_list):
-    listed = visible_list.astype(jnp.float32).reshape(1, -1)
-    rows = [source_dirs, source_flux.astype(jnp.float32)[None], listed]
-    width = max(row.shape[1] for row in rows)
-    rows = [jnp.pad(row, ((0, 0), (0, width - row.shape[1]))) for row in rows]
-    return jnp.concatenate(rows, 0)
-
-
 def plain_program(visibility, beam, antenna_uvw, small, keep):
     units_dev, slots, _, span, _ = visibility.shape
     _, _, per_group, antennas = beam.shape
@@ -595,7 +616,7 @@
             [list(range(blocks))],
             span,
             0 if slot else BRIGHT_ROWS,
-            small.shape[1],
+            small[0].shape[1],
         )
         everyone = lax.all_gather(owned, "tile", axis=0)
         rows = blocks * per_group
@@ -622,31 +643,35 @@
 SUM_PLANES, SUM_PLANE = 48, 51
 GATES = {
     1: (0,),
-    5: (0, 1, 2, 11),
-    6: (0, 11, 13),
-    12: (11,),
-    15: (13,),
-    19: (3, 4, 18),
-    20: (4, 6),
-    21: (3, 5, 14, 17),
-    22: (13, 21),
-    23: (18,),
-    24: (6, 16),
-    25: (6, 7, 23),
+    3: (0, 1),
+    5: (0, 2, 13),
+    6: (1, 2, 11),
+    7: (1, 2),
+    14: (13,),
+    16: (2,),
+    17: (1,),
+    19: (18,),
+    20: (3, 4, 6, 7, 17),
+    21: (3, 4, 5, 13, 14, 16, 17),
+    23: (4, 17),
+    24: (6, 9, 17),
+    25: (6, 9, 17, 23),
     26: (9,),
-    27: (8, 23),
-    30: (26,),
-    31: (26,),
-    34: (28,),
-    35: (28,),
-    36: (9,),
-    37: (26, 27),
-    40: (36, 37),
-    43: (30,),
-    45: (44,),
-    46: (38, 43),
+    27: (8,),
+    28: (22,),
+    31: (25, 27),
+    33: (23, 32),
+    34: (33,),
+    35: (8, 9, 24, 25),
+    40: (28, 34, 36, 37),
+    41: (40,),
+    42: (29, 41),
+    43: (41,),
+    45: (28, 32),
     48: (35,),
-    51: (31, 45),
+    49: (44,),
+    51: (34,),
+    52: (38,),
 }
 
 
@@ -693,7 +718,7 @@
             pieces,
             span,
             bright_rows,
-            small.shape[1],
+            small[0].shape[1],
         )
         done[step] = built[0]
         return built
@@ -797,7 +822,7 @@
 ):
     span = visibility.shape[4]
     antennas = station_beam.shape[3]
-    small = packed_small(source_dirs, source_flux, visible_list)
+    small = (source_dirs, source_flux.astype(jnp.float32)[None], visible_list)
     keep = 1.0 - antenna_flags.astype(jnp.float32)
     arguments = (visibility, station_beam, antenna_uvw, small, keep)
     if lax.axis_size("tile") == 16:

time: 215 us -> 202 us (0.940)
  starting transfers between devices: 75.3 us -> 51.3 us
  waiting for transfers between devices: 51.5 us -> 64.7 us
    ppermute x37, starting transfers between devices: 75.3 us -> 51.3 us  [send(): done[step] = lax.ppermute(gated(step, value), 'tile', pairs)]
    ppermute x37, waiting for transfers between devices: 51.5 us -> 64.7 us  [send(): done[step] = lax.ppermute(gated(step, value), 'tile', pairs)]
    unnamed x93 -> x97, local copies, waits for them, and re-layouts: 18.6 us -> 15.5 us
  transfers between devices with their start and end apart: 37 -> 37, of which waited for: 11 -> 12; matrix products, arithmetic and copies ran while one was open for 2% -> 3% of each run, Pallas kernels for 26% -> 28%
where the time goes in v7:
time: 202 us; the launch traced here: 201 us
  waiting for transfers between devices  64.7 us (32%)
  Pallas kernels  60.7 us (30%)
  starting transfers between devices  51.3 us (25%)
  local copies, waits for them, and re-layouts  21.2 us (10%)
  other arithmetic  2.15 us (1%)
    ppermute x37, waiting for transfers between devices, send(): done[step] = lax.ppermute(gated(step, value), 'tile', pairs)  64.7 us
    ppermute x37, starting transfers between devices, send(): done[step] = lax.ppermute(gated(step, value), 'tile', pairs)  51.3 us
    pallas_call x6, Pallas kernels, unit_work(): pl.pallas_call(functools.partial(unit_kernel, index, offset, kinds, brigh...  33.3 us
    unnamed x97, local copies, waits for them, and re-layouts  15.5 us
    pallas_call x3, Pallas kernels, put_residuals(): pl.pallas_call(functools.partial(put_kernel, sources), grid_spec=pltpu.Pr...  9.1 us
    pallas_call x3, Pallas kernels, messages_for(): pl.pallas_call(functools.partial(message_kernel, len(others), bool(smalls...  7.71 us
    pallas_call x3, Pallas kernels, build_factors(): pl.pallas_call(functools.partial(build_kernel, sets, slot_ids, pieces, br...  6.7 us
  transfers between devices with their start and end apart: 37, of which 12 were waited for; matrix products, arithmetic and copies ran while one was open for 3% of the time, Pallas kernels for 28%

profile of v7, /device:TPU:0, one launch (start us, length us, event | category | flops | bytes accessed | tf_op | source)
XLA Modules:
  0.0 201.2 jit_solution(13865268783025286234)
XLA Ops:
  0.6 1.3 broadcast_in_dim.34
  2.0 1.3 constant_dynamic-slice_fusion
  3.2 2.4 %messages_for.3 = bf16[80,2048]{1,0:T(8,128)(2,1)} custom-call(s32[148]{0:T(256)} %bitcast.24, bf16[8,2,32,2048]{3,2,1,0:T(8,128)(2,1)} %refs_0_.10, f32[2,256]{1,0:T(2,128)} %refs_4_.5, f32[1,256]{1,0:T(1,128)} %bitcast.40, s32[8,32]{1,0:T(8,128)} %refs_6_.1), custom_call_target="tpu_custom_call" | custom-call | flops 1 | bytes 1 | tf_op jit(solution)/shard_map/messages_for/pallas_call | solution.py:211
  6.1 1.1 copy.15.refs_5_.refs_10_.refs_2_
  10.2 1.6 build_factors.3.refs_0_
  11.9 4.0 %collective-permute-start.1 = (bf16[2,528,256]{2,1,0:T(8,128)(2,1)S(1)}, bf16[2,528,256]{2,1,0:T(8,128)(2,1)S(1)}, u32[]{:S(2)}, u32[]{:S(2)}) collective-permute-start(bf16[2,528,256]{2,1,0:T(8,128)(2,1)S(1)} %build_factors.3.refs_0_), channel_id=1, source_target_pairs={{0,8},{1,9},{2,10},{3,11},{4,0},{5,1},{6,2},{7,3},{8,12},{9,13},{1... | collective-permute-start | bytes 1622024 | tf_op jit(solution)/shard_map/ppermute | solution.py:694
  15.9 2.6 %messages_for.5 = (bf16[80,2048]{1,0:T(8,128)(2,1)}, bf16[80,2048]{1,0:T(8,128)(2,1)}) custom-call(s32[148]{0:T(256)} %bitcast.25, bf16[8,2,32,2048]{3,2,1,0:T(8,128)(2,1)} %refs_0_.10, bf16[8,2,32,2048]{3,2,1,0:T(8,128)(2,1)} %refs_0_.10, f32[2,256]{1,0:T(2,128)} %refs_4_.5, f32[1,256]{1,0:T(1,128)} %bitcast.41, s32[8,32]{1,0:T(8,128)} %refs_6_.1), custom_call_target="tpu_custom_call" | custom-call | flops 1 | bytes 1 | tf_op jit(solution)/shard_map/messages_for/pallas_call | solution.py:211
  18.4 1.5 collective-permute-start.7
  20.0 2.7 %messages_for.4 = (bf16[64,2048]{1,0:T(8,128)(2,1)}, bf16[64,2048]{1,0:T(8,128)(2,1)}, bf16[64,2048]{1,0:T(8,128)(2,1)}) custom-call(s32[148]{0:T(256)} %bitcast.26, bf16[8,2,32,2048]{3,2,1,0:T(8,128)(2,1)} %refs_0_.10, bf16[8,2,32,2048]{3,2,1,0:T(8,128)(2,1)} %refs_0_.10, bf16[8,2,32,2048]{3,2,1,0:T(8,128)(2,1)} %refs_0_.10), custom_call_target="tpu_custom_call" | custom-call | flops 1 | bytes 1 | tf_op jit(solution)/shard_map/messages_for/pallas_call | solution.py:211
  22.7 6.5 %collective-permute-done.7.refs_8_.refs_0_ = bf16[80,2048]{1,0:T(8,128)(2,1)S(1)} collective-permute-done((bf16[80,2048]{1,0:T(8,128)(2,1)}, bf16[80,2048]{1,0:T(8,128)(2,1)S(1)}, u32[]{:S(2)}, u32[]{:S(2)}) %collective-permute-start.7) | collective-permute-done | bytes 327712 | tf_op jit(solution)/shard_map/ppermute | solution.py:694
  30.1 2.6 %collective-permute-start.2 = (bf16[528,256]{1,0:T(8,128)(2,1)}, bf16[528,256]{1,0:T(8,128)(2,1)}, u32[]{:S(2)}, u32[]{:S(2)}) collective-permute-start(bf16[528,256]{1,0:T(8,128)(2,1)} %slice_bitcast_fusion.3), channel_id=1, source_target_pairs={{0,8},{1,9},{2,10},{3,11},{4,0},{5,1},{6,2},{7,3},{8,12},{9,13},{1... | collective-permute-start | bytes 811016 | tf_op jit(solution)/shard_map/ppermute | solution.py:694
  32.7 9.2 %collective-permute-done.3.refs_1_ = bf16[2,528,256]{2,1,0:T(8,128)(2,1)S(1)} collective-permute-done((bf16[2,528,256]{2,1,0:T(8,128)(2,1)S(1)}, bf16[2,528,256]{2,1,0:T(8,128)(2,1)S(1)}, u32[]{:S(2)}, u32[]{:S(2)}) %collective-permute-start.3) | collective-permute-done | bytes 540704 | tf_op jit(solution)/shard_map/ppermute | solution.py:694
  43.4 1.5 collective-permute-start.4
  44.9 1.6 build_factors.5.refs_5_
  48.0 2.2 %collective-permute-start.10 = (bf16[2,528,256]{2,1,0:T(8,128)(2,1)S(1)}, bf16[2,528,256]{2,1,0:T(8,128)(2,1)}, u32[]{:S(2)}, u32[]{:S(2)}) collective-permute-start(bf16[2,528,256]{2,1,0:T(8,128)(2,1)S(1)} %build_factors.5.refs_5_), channel_id=1, source_target_pairs={{0,8},{1,9},{2,10},{3,11},{4,0},{5,1},{6,2},{7,3},{8,12},{9,13},{1... | collective-permute-start | bytes 1622024 | tf_op jit(solution)/shard_map/ppermute | solution.py:694
  51.8 2.8 %collective-permute-start.9 = (bf16[2,528,256]{2,1,0:T(8,128)(2,1)S(1)}, bf16[2,528,256]{2,1,0:T(8,128)(2,1)}, u32[]{:S(2)}, u32[]{:S(2)}) collective-permute-start(bf16[2,528,256]{2,1,0:T(8,128)(2,1)S(1)} %build_factors.5.refs_5_), channel_id=1, source_target_pairs={{0,4},{1,5},{2,6},{3,7},{4,12},{5,13},{6,14},{7,15},{8,0},{9,1},{1... | collective-permute-start | bytes 1622024 | tf_op jit(solution)/shard_map/ppermute | solution.py:694
  54.5 4.0 %slices_for.1 = (bf16[2,2,2,256,256]{4,3,2,1,0:T(8,128)(2,1)}, bf16[2,2,2,256,256]{4,3,2,1,0:T(8,128)(2,1)}, bf16[2,2,2,256,256]{4,3,2,1,0:T(8,128)(2,1)}) custom-call(s32[148]{0:T(256)} %bitcast.27, bf16[2,8,2,256,256]{4,3,2,1,0:T(8,128)(2,1)} %refs_11_.3, bf16[2,8,2,256,256]{4,3,2,1,0:T(8,128)(2,1)} %refs_11_.3, bf16[2,8,2,256,256]{4,3,2,1,0:T(8,128)(2,1)} %refs_11_.3), custom_call_target="tpu_custom_call" | custom-call | flops 1 | bytes 1 | tf_op jit(solution)/shard_map/slices_for/pallas_call | solution.py:242
  58.5 1.6 collective-permute-start.17
  60.1 4.4 %collective-permute-done.10.refs_7_ = bf16[2,528,256]{2,1,0:T(8,128)(2,1)} collective-permute-done((bf16[2,528,256]{2,1,0:T(8,128)(2,1)S(1)}, bf16[2,528,256]{2,1,0:T(8,128)(2,1)}, u32[]{:S(2)}, u32[]{:S(2)}) %collective-permute-start.10) | collective-permute-done | bytes 540704 | tf_op jit(solution)/shard_map/ppermute | solution.py:694
  64.6 1.0 slice_bitcast_fusion.2
  65.5 1.9 collective-permute-start.11
  67.4 10.1 %collective-permute-done.9.refs_6_ = bf16[2,528,256]{2,1,0:T(8,128)(2,1)} collective-permute-done((bf16[2,528,256]{2,1,0:T(8,128)(2,1)S(1)}, bf16[2,528,256]{2,1,0:T(8,128)(2,1)}, u32[]{:S(2)}, u32[]{:S(2)}) %collective-permute-start.9) | collective-permute-done | bytes 540704 | tf_op jit(solution)/shard_map/ppermute | solution.py:694
  77.5 1.0 slice_bitcast_fusion
  83.5 3.5 %build_factors.4 = (bf16[2,512,256]{2,1,0:T(8,128)(2,1)S(1)}, bf16[2,512,256]{2,1,0:T(8,128)(2,1)S(1)}) custom-call(s32[148]{0:T(256)S(1)} %bitcast.30, bf16[8,2,32,2048]{3,2,1,0:T(8,128)(2,1)S(1)} %copy-done.1, bf16[64,2048]{1,0:T(8,128)(2,1)} %collective-permute-done.5.refs_1_, bf16[64,2048]{1,0:T(8,128)(2,1)S(1)} %copy-done.36, ...), custom_call_target="tpu_custom_call" | custom-call | flops 1 | bytes 1 | tf_op jit(solution)/shard_map/build_factors/pallas_call | solution.py:161
  87.0 7.2 %collective-permute-start.12 = (bf16[2,512,256]{2,1,0:T(8,128)(2,1)S(1)}, bf16[2,512,256]{2,1,0:T(8,128)(2,1)S(1)}, u32[]{:S(2)}, u32[]{:S(2)}) collective-permute-start(bf16[2,512,256]{2,1,0:T(8,128)(2,1)S(1)} %get-tuple-element.89.refs_0_), channel_id=1, source_target_pairs={{0,4},{1,5},{2,6},{3,7},{4,12},{5,13},{6,14},{7,15},{8,0},{9,1},{1... | collective-permute-start | bytes 1572872 | tf_op jit(solution)/shard_map/ppermute | solution.py:694
  95.2 5.4 %unit_work.6 = (bf16[2,2,256,256]{3,2,1,0:T(8,128)(2,1)}, f32[1,512]{1,0:T(1,128)S(1)}, f32[2,512,128]{2,1,0:T(8,128)S(1)}) custom-call(s32[148]{0:T(256)S(1)} %bitcast.31, bf16[2,528,256]{2,1,0:T(8,128)(2,1)S(1)} %build_factors.3.refs_0_, bf16[2,528,256]{2,1,0:T(8,128)(2,1)S(1)} %copy-done.6, bf16[2,528,256]{2,1,0:T(8,128)(2,1)S(1)} %copy-done.3, ...), custom_call_target="tpu_custom_call" | custom-call | flops 1 | bytes 1 | tf_op jit(solution)/shard_map/unit_work/pallas_call | solution.py:479
  100.6 3.4 %collective-permute-done.13.refs_10_ = bf16[2,2,2,256,256]{4,3,2,1,0:T(8,128)(2,1)S(1)} collective-permute-done((bf16[2,2,2,256,256]{4,3,2,1,0:T(8,128)(2,1)}, bf16[2,2,2,256,256]{4,3,2,1,0:T(8,128)(2,1)S(1)}, u32[]{:S(2)}, u32[]{:S(2)}) %collective-permute-start.13) | collective-permute-done | bytes 1048608 | tf_op jit(solution)/shard_map/ppermute | solution.py:694
  105.0 5.2 %unit_work.7 = (bf16[2,2,256,256]{3,2,1,0:T(8,128)(2,1)}, f32[1,512]{1,0:T(1,128)S(1)}) custom-call(s32[148]{0:T(256)S(1)} %bitcast.32, bf16[2,528,256]{2,1,0:T(8,128)(2,1)S(1)} %build_factors.3.refs_0_, bf16[2,528,256]{2,1,0:T(8,128)(2,1)S(1)} %copy-done.6, bf16[2,528,256]{2,1,0:T(8,128)(2,1)S(1)} %copy-done.3, ...), custom_call_target="tpu_custom_call" | custom-call | flops 1 | bytes 1 | tf_op jit(solution)/shard_map/unit_work/pallas_call | solution.py:479
  110.3 2.2 %collective-permute-start.20 = (bf16[2,2,256,256]{3,2,1,0:T(8,128)(2,1)}, bf16[2,2,256,256]{3,2,1,0:T(8,128)(2,1)}, u32[]{:S(2)}, u32[]{:S(2)}) collective-permute-start(bf16[2,2,256,256]{3,2,1,0:T(8,128)(2,1)} %get-tuple-element.87), channel_id=1, source_target_pairs={{0,3},{1,2},{2,1},{3,0},{4,7},{5,6},{6,5},{7,4},{8,11},{9,10},{10,... | collective-permute-start | bytes 1572872 | tf_op jit(solution)/shard_map/ppermute | solution.py:694
  113.3 15.7 %collective-permute-done.24.refs_7_ = bf16[2,512,256]{2,1,0:T(8,128)(2,1)S(1)} collective-permute-done((bf16[2,512,256]{2,1,0:T(8,128)(2,1)S(1)}, bf16[2,512,256]{2,1,0:T(8,128)(2,1)S(1)}, u32[]{:S(2)}, u32[]{:S(2)}) %collective-permute-start.24) | collective-permute-done | bytes 524320 | tf_op jit(solution)/shard_map/ppermute | solution.py:694
  129.0 1.1 collective-permute-start.19
  131.4 8.8 %collective-permute-done.23.refs_6_ = bf16[2,512,256]{2,1,0:T(8,128)(2,1)S(1)} collective-permute-done((bf16[2,512,256]{2,1,0:T(8,128)(2,1)S(1)}, bf16[2,512,256]{2,1,0:T(8,128)(2,1)S(1)}, u32[]{:S(2)}, u32[]{:S(2)}) %collective-permute-start.23) | collective-permute-done | bytes 524320 | tf_op jit(solution)/shard_map/ppermute | solution.py:694
  142.2 2.9 %collective-permute-start.22 = (bf16[512,256]{1,0:T(8,128)(2,1)S(1)}, bf16[512,256]{1,0:T(8,128)(2,1)}, u32[]{:S(2)}, u32[]{:S(2)}) collective-permute-start(bf16[512,256]{1,0:T(8,128)(2,1)S(1)} %slice_bitcast_fusion.6), channel_id=1, source_target_pairs={{0,8},{1,9},{2,10},{3,11},{4,0},{5,1},{6,2},{7,3},{8,12},{9,13},{1... | collective-permute-start | bytes 786440 | tf_op jit(solution)/shard_map/ppermute | solution.py:694
  145.8 2.5 %collective-permute-start.25 = (bf16[512,256]{1,0:T(8,128)(2,1)}, bf16[512,256]{1,0:T(8,128)(2,1)}, u32[]{:S(2)}, u32[]{:S(2)}) collective-permute-start(bf16[512,256]{1,0:T(8,128)(2,1)} %slice_bitcast_fusion.5), channel_id=1, source_target_pairs={{0,4},{1,5},{2,6},{3,7},{4,12},{5,13},{6,14},{7,15},{8,0},{9,1},{1... | collective-permute-start | bytes 786440 | tf_op jit(solution)/shard_map/ppermute | solution.py:694
  150.3 7.3 %unit_work.8 = (bf16[2,2,256,256]{3,2,1,0:T(8,128)(2,1)S(1)}, bf16[2,2,256,256]{3,2,1,0:T(8,128)(2,1)S(1)}, f32[1,512]{1,0:T(1,128)S(1)}) custom-call(s32[148]{0:T(256)S(1)} %bitcast.33, bf16[2,528,256]{2,1,0:T(8,128)(2,1)S(1)} %build_factors.3.refs_0_, bf16[2,528,256]{2,1,0:T(8,128)(2,1)S(1)} %copy-done.7, bf16[2,528,256]{2,1,0:T(8,128)(2,1)S(1)} %copy-done.4, ...), custom_call_target="tpu_custom_call" | custom-call | flops 1 | bytes 1 | tf_op jit(solution)/shard_map/unit_work/pallas_call | solution.py:479
  158.0 4.2 %collective-permute-done.25.refs_8_ = bf16[512,256]{1,0:T(8,128)(2,1)} collective-permute-done((bf16[512,256]{1,0:T(8,128)(2,1)}, bf16[512,256]{1,0:T(8,128)(2,1)}, u32[]{:S(2)}, u32[]{:S(2)}) %collective-permute-start.25) | collective-permute-done | bytes 262176 | tf_op jit(solution)/shard_map/ppermute | solution.py:694
  162.2 4.3 %unit_work.9 = (bf16[2,2,256,256]{3,2,1,0:T(8,128)(2,1)S(1)}, f32[1,512]{1,0:T(1,128)S(1)}) custom-call(s32[148]{0:T(256)S(1)} %bitcast.34, bf16[2,512,256]{2,1,0:T(8,128)(2,1)S(1)} %copy-done.17, bf16[2,512,256]{2,1,0:T(8,128)(2,1)S(1)} %copy-done.9, bf16[2,512,256]{2,1,0:T(8,128)(2,1)S(1)} %copy-done.11, ...), custom_call_target="tpu_custom_call" | custom-call | flops 1 | bytes 1 | tf_op jit(solution)/shard_map/unit_work/pallas_call | solution.py:479
  166.4 1.2 collective-permute-start.27
  167.6 4.3 %unit_work.10 = (bf16[2,2,256,256]{3,2,1,0:T(8,128)(2,1)S(1)}, f32[1,512]{1,0:T(1,128)S(1)}) custom-call(s32[148]{0:T(256)S(1)} %bitcast.35, bf16[2,512,256]{2,1,0:T(8,128)(2,1)S(1)} %copy-done.17, bf16[2,512,256]{2,1,0:T(8,128)(2,1)S(1)} %copy-done.9, bf16[2,512,256]{2,1,0:T(8,128)(2,1)S(1)} %copy-done.11, ...), custom_call_target="tpu_custom_call" | custom-call | flops 1 | bytes 1 | tf_op jit(solution)/shard_map/unit_work/pallas_call | solution.py:479
  171.9 6.8 %unit_work.11 = (bf16[2,2,256,256]{3,2,1,0:T(8,128)(2,1)S(1)}, bf16[2,2,256,256]{3,2,1,0:T(8,128)(2,1)S(1)}, f32[1,512]{1,0:T(1,128)S(1)}) custom-call(s32[148]{0:T(256)S(1)} %bitcast.36, bf16[2,512,256]{2,1,0:T(8,128)(2,1)S(1)} %copy-done.17, bf16[2,512,256]{2,1,0:T(8,128)(2,1)S(1)} %copy-done.9, bf16[2,512,256]{2,1,0:T(8,128)(2,1)S(1)} %copy-done.11, ...), custom_call_target="tpu_custom_call" | custom-call | flops 1 | bytes 1 | tf_op jit(solution)/shard_map/unit_work/pallas_call | solution.py:479
  178.7 2.1 %collective-permute-start.33 = (f32[2,128]{1,0:T(2,128)S(1)}, f32[2,128]{1,0:T(2,128)S(1)}, u32[]{:S(2)}, u32[]{:S(2)}) collective-permute-start(f32[2,128]{1,0:T(2,128)S(1)} %get-tuple-element.113), channel_id=1, source_target_pairs={{0,4},{1,5},{2,6},{3,7},{4,12},{5,13},{6,14},{7,15},{8,0},{9,1},{1... | collective-permute-start | bytes 3080 | tf_op jit(solution)/shard_map/ppermute | solution.py:694
  180.8 1.1 collective-permute-start.28
  181.9 5.5 %collective-permute-start.31 = (f32[2,128]{1,0:T(2,128)S(1)}, f32[2,128]{1,0:T(2,128)S(1)}, u32[]{:S(2)}, u32[]{:S(2)}) collective-permute-start(f32[2,128]{1,0:T(2,128)S(1)} %get-tuple-element.108), channel_id=1, source_target_pairs={{0,12},{1,13},{2,14},{3,15},{4,8},{5,9},{6,10},{7,11},{8,4},{9,5},... | collective-permute-start | bytes 3080 | tf_op jit(solution)/shard_map/ppermute | solution.py:694
  187.4 1.9 collective-permute-start.32
  189.4 4.8 %put_residuals.3.refs_2_ = bf16[2,8,2,256,256]{4,3,2,1,0:T(8,128)(2,1)} custom-call(s32[148]{0:T(256)S(1)} %bitcast.37, bf16[2,2,256,256]{3,2,1,0:T(8,128)(2,1)} %collective-permute-done.19.refs_0_, bf16[2,2,256,256]{3,2,1,0:T(8,128)(2,1)} %collective-permute-done.20.refs_1_, bf16[2,2,256,256]{3,2,1,0:T(8,128)(2,1)S(1)} %collective-permute-done.30.refs_2_, ...), custom_call_target="tpu_custom_call" | custom-call | flops 1 | bytes 1 | tf_op jit(solution)/shard_map/put_residuals/pallas_call | solution.py:519
  194.4 1.8 collective-permute-start.36
  196.2 2.1 %put_residuals.4.refs_2_ = bf16[2,8,2,256,256]{4,3,2,1,0:T(8,128)(2,1)} custom-call(s32[148]{0:T(256)S(1)} %bitcast.38, bf16[2,2,256,256]{3,2,1,0:T(8,128)(2,1)S(1)} %collective-permute-done.29.refs_0_, bf16[2,2,256,256]{3,2,1,0:T(8,128)(2,1)S(1)} %get-tuple-element.103.refs_1_, ...), custom_call_target="tpu_custom_call", output_to_operand_aliasing={{}: (3, {})} | custom-call | flops 1 | bytes 1 | tf_op jit(solution)/shard_map/put_residuals/pallas_call | solution.py:519
  198.4 2.1 %put_residuals.5 = bf16[2,8,2,256,256]{4,3,2,1,0:T(8,128)(2,1)} custom-call(s32[148]{0:T(256)S(1)} %bitcast.39, bf16[2,2,256,256]{3,2,1,0:T(8,128)(2,1)S(1)} %collective-permute-done.27.refs_0_, bf16[2,2,256,256]{3,2,1,0:T(8,128)(2,1)S(1)} %collective-permute-done.28.refs_1_, ...), custom_call_target="tpu_custom_call", output_to_operand_aliasing={{}: (3, {})} | custom-call | flops 1 | bytes 1 | tf_op jit(solution)/shard_map/put_residuals/pallas_call | solution.py:519
  (161 shorter events, 23.8 us)
Async XLA Ops:
  5.6 1.9 collective-permute-start
  11.9 17.4 %collective-permute-start.1 = (bf16[2,528,256]{2,1,0:T(8,128)(2,1)S(1)}, bf16[2,528,256]{2,1,0:T(8,128)(2,1)S(1)}, u32[]{:S(2)}, u32[]{:S(2)}) collective-permute-start(bf16[2,528,256]{2,1,0:T(8,128)(2,1)S(1)} %build_factors.3.refs_0_), channel_id=1, source_target_pairs={{0,8},{1,9},{2,10},{3,11},{4,0},{5,1},{6,2},{7,3},{8,12},{9,13},{1... | collective-permute-start | bytes 1622024 | tf_op jit(solution)/shard_map/ppermute | solution.py:694
  18.4 26.5 %copy-start.31 = (s32[1,148]{1,0:T(1,128)S(1)}, s32[1,148]{1,0:T(1,128)}, u32[]{:S(2)}) copy-start(s32[1,148]{1,0:T(1,128)} %constant_dynamic-slice_fusion) | copy-start | bytes 1780
  18.4 10.8 %collective-permute-start.7 = (bf16[80,2048]{1,0:T(8,128)(2,1)}, bf16[80,2048]{1,0:T(8,128)(2,1)S(1)}, u32[]{:S(2)}, u32[]{:S(2)}) collective-permute-start(bf16[80,2048]{1,0:T(8,128)(2,1)} %get-tuple-element.64), channel_id=1, source_target_pairs={{0,2},{1,3},{2,0},{3,1},{4,6},{5,7},{6,4},{7,5},{8,10},{9,11},{10,... | collective-permute-start | bytes 983048 | tf_op jit(solution)/shard_map/ppermute | solution.py:694
  20.0 22.0 %collective-permute-start.3 = (bf16[2,528,256]{2,1,0:T(8,128)(2,1)S(1)}, bf16[2,528,256]{2,1,0:T(8,128)(2,1)S(1)}, u32[]{:S(2)}, u32[]{:S(2)}) collective-permute-start(bf16[2,528,256]{2,1,0:T(8,128)(2,1)S(1)} %build_factors.3.refs_0_), channel_id=1, source_target_pairs={{0,4},{1,5},{2,6},{3,7},{4,12},{5,13},{6,14},{7,15},{8,0},{9,1},{1... | collective-permute-start | bytes 1622024 | tf_op jit(solution)/shard_map/ppermute | solution.py:694
  22.7 24.6 %collective-permute-start.6 = (bf16[64,2048]{1,0:T(8,128)(2,1)}, bf16[64,2048]{1,0:T(8,128)(2,1)S(1)}, u32[]{:S(2)}, u32[]{:S(2)}) collective-permute-start(bf16[64,2048]{1,0:T(8,128)(2,1)} %get-tuple-element.63), channel_id=1, source_target_pairs={{0,3},{1,2},{2,1},{3,0},{4,7},{5,6},{6,5},{7,4},{8,11},{9,10},{10,... | collective-permute-start | bytes 786440 | tf_op jit(solution)/shard_map/ppermute | solution.py:694
  29.3 15.7 %collective-permute-start.8 = (bf16[80,2048]{1,0:T(8,128)(2,1)S(1)}, bf16[80,2048]{1,0:T(8,128)(2,1)S(1)}, u32[]{:S(2)}, u32[]{:S(2)}) collective-permute-start(bf16[80,2048]{1,0:T(8,128)(2,1)S(1)} %copy-done.47), channel_id=1, source_target_pairs={{0,3},{1,2},{2,1},{3,0},{4,7},{5,6},{6,5},{7,4},{8,11},{9,10},{10,... | collective-permute-start | bytes 983048 | tf_op jit(solution)/shard_map/ppermute | solution.py:694
  30.1 28.4 %collective-permute-start.2 = (bf16[528,256]{1,0:T(8,128)(2,1)}, bf16[528,256]{1,0:T(8,128)(2,1)}, u32[]{:S(2)}, u32[]{:S(2)}) collective-permute-start(bf16[528,256]{1,0:T(8,128)(2,1)} %slice_bitcast_fusion.3), channel_id=1, source_target_pairs={{0,8},{1,9},{2,10},{3,11},{4,0},{5,1},{6,2},{7,3},{8,12},{9,13},{1... | collective-permute-start | bytes 811016 | tf_op jit(solution)/shard_map/ppermute | solution.py:694
  42.7 15.8 %collective-permute-start.15 = (bf16[528,256]{1,0:T(8,128)(2,1)}, bf16[528,256]{1,0:T(8,128)(2,1)}, u32[]{:S(2)}, u32[]{:S(2)}) collective-permute-start(bf16[528,256]{1,0:T(8,128)(2,1)} %slice_bitcast_fusion.1), channel_id=1, source_target_pairs={{0,4},{1,5},{2,6},{3,7},{4,12},{5,13},{6,14},{7,15},{8,0},{9,1},{1... | collective-permute-start | bytes 811016 | tf_op jit(solution)/shard_map/ppermute | solution.py:694
  43.4 7.7 %collective-permute-start.4 = (bf16[64,2048]{1,0:T(8,128)(2,1)}, bf16[64,2048]{1,0:T(8,128)(2,1)S(1)}, u32[]{:S(2)}, u32[]{:S(2)}) collective-permute-start(bf16[64,2048]{1,0:T(8,128)(2,1)} %get-tuple-element.59), channel_id=1, source_target_pairs={{0,2},{1,3},{2,0},{3,1},{4,6},{5,7},{6,4},{7,5},{8,10},{9,11},{10,... | collective-permute-start | bytes 786440 | tf_op jit(solution)/shard_map/ppermute | solution.py:694
  44.9 13.6 %collective-permute-start.5 = (bf16[64,2048]{1,0:T(8,128)(2,1)}, bf16[64,2048]{1,0:T(8,128)(2,1)}, u32[]{:S(2)}, u32[]{:S(2)}) collective-permute-start(bf16[64,2048]{1,0:T(8,128)(2,1)} %get-tuple-element.62), channel_id=1, source_target_pairs={{0,1},{1,0},{2,3},{3,2},{4,5},{5,4},{6,7},{7,6},{8,9},{9,8},{10,11... | collective-permute-start | bytes 786440 | tf_op jit(solution)/shard_map/ppermute | solution.py:694
  47.3 31.3 %copy-start.1 = (bf16[8,2,32,2048]{3,2,1,0:T(8,128)(2,1)S(1)}, bf16[8,2,32,2048]{3,2,1,0:T(8,128)(2,1)}, u32[]{:S(2)}) copy-start(bf16[8,2,32,2048]{3,2,1,0:T(8,128)(2,1)} %refs_0_.10) | copy-start | bytes 6291460
  47.3 31.3 %copy-start.32 = (s32[1,148]{1,0:T(1,128)S(1)}, s32[1,148]{1,0:T(1,128)}, u32[]{:S(2)}) copy-start(s32[1,148]{1,0:T(1,128)} %constant_dynamic-slice_fusion) | copy-start | bytes 1780
  47.3 31.3 %copy-start.38 = (s32[8,32]{1,0:T(8,128)S(1)}, s32[8,32]{1,0:T(8,128)}, u32[]{:S(2)}) copy-start(s32[8,32]{1,0:T(8,128)} %refs_6_.1) | copy-start | bytes 3076
  47.3 31.3 %copy-start.40 = (f32[2,256]{1,0:T(2,128)S(1)}, f32[2,256]{1,0:T(2,128)}, u32[]{:S(2)}) copy-start(f32[2,256]{1,0:T(2,128)} %refs_4_.5) | copy-start | bytes 6148
  47.3 31.3 %copy-start.42 = (f32[256]{0:T(256)S(1)}, f32[256]{0:T(256)}, u32[]{:S(2)}) copy-start(f32[256]{0:T(256)} %broadcast_in_dim.34) | copy-start | bytes 3076
  48.0 16.5 %collective-permute-start.10 = (bf16[2,528,256]{2,1,0:T(8,128)(2,1)S(1)}, bf16[2,528,256]{2,1,0:T(8,128)(2,1)}, u32[]{:S(2)}, u32[]{:S(2)}) collective-permute-start(bf16[2,528,256]{2,1,0:T(8,128)(2,1)S(1)} %build_factors.5.refs_5_), channel_id=1, source_target_pairs={{0,8},{1,9},{2,10},{3,11},{4,0},{5,1},{6,2},{7,3},{8,12},{9,13},{1... | collective-permute-start | bytes 1622024 | tf_op jit(solution)/shard_map/ppermute | solution.py:694
  51.8 25.8 %collective-permute-start.9 = (bf16[2,528,256]{2,1,0:T(8,128)(2,1)S(1)}, bf16[2,528,256]{2,1,0:T(8,128)(2,1)}, u32[]{:S(2)}, u32[]{:S(2)}) collective-permute-start(bf16[2,528,256]{2,1,0:T(8,128)(2,1)S(1)} %build_factors.5.refs_5_), channel_id=1, source_target_pairs={{0,4},{1,5},{2,6},{3,7},{4,12},{5,13},{6,14},{7,15},{8,0},{9,1},{1... | collective-permute-start | bytes 1622024 | tf_op jit(solution)/shard_map/ppermute | solution.py:694
  54.5 40.6 %copy-start.46 = (s32[8,2048]{1,0:T(8,128)S(1)}, s32[8,2048]{1,0:T(8,128)}, u32[]{:S(2)}) copy-start(s32[8,2048]{1,0:T(8,128)} %param.14) | copy-start | bytes 196612
  58.5 36.7 %copy-start.3 = (bf16[2,528,256]{2,1,0:T(8,128)(2,1)S(1)}, bf16[2,528,256]{2,1,0:T(8,128)(2,1)}, u32[]{:S(2)}) copy-start(bf16[2,528,256]{2,1,0:T(8,128)(2,1)} %copy-done.2) | copy-start | bytes 1622020
  58.5 36.7 %copy-start.6 = (bf16[2,528,256]{2,1,0:T(8,128)(2,1)S(1)}, bf16[2,528,256]{2,1,0:T(8,128)(2,1)}, u32[]{:S(2)}) copy-start(bf16[2,528,256]{2,1,0:T(8,128)(2,1)} %copy-done.5) | copy-start | bytes 1622020
  58.5 35.7 %collective-permute-start.17 = (bf16[2,2,2,256,256]{4,3,2,1,0:T(8,128)(2,1)}, bf16[2,2,2,256,256]{4,3,2,1,0:T(8,128)(2,1)S(1)}, u32[]{:S(2)}, u32[]{:S(2)}) collective-permute-start(bf16[2,2,2,256,256]{4,3,2,1,0:T(8,128)(2,1)} %get-tuple-element.77), channel_id=1, source_target_pairs={{0,2},{1,3},{2,0},{3,1},{4,6},{5,7},{6,4},{7,5},{8,10},{9,11},{10,... | collective-permute-start | bytes 3145736 | tf_op jit(solution)/shard_map/ppermute | solution.py:694
  60.1 43.9 %collective-permute-start.13 = (bf16[2,2,2,256,256]{4,3,2,1,0:T(8,128)(2,1)}, bf16[2,2,2,256,256]{4,3,2,1,0:T(8,128)(2,1)S(1)}, u32[]{:S(2)}, u32[]{:S(2)}) collective-permute-start(bf16[2,2,2,256,256]{4,3,2,1,0:T(8,128)(2,1)} %get-tuple-element.73), channel_id=1, source_target_pairs={{0,3},{1,2},{2,1},{3,0},{4,7},{5,6},{6,5},{7,4},{8,11},{9,10},{10,... | collective-permute-start | bytes 3145736 | tf_op jit(solution)/shard_map/ppermute | solution.py:694
  65.5 21.4 %collective-permute-start.11 = (bf16[528,256]{1,0:T(8,128)(2,1)S(1)}, bf16[528,256]{1,0:T(8,128)(2,1)S(1)}, u32[]{:S(2)}, u32[]{:S(2)}) collective-permute-start(bf16[528,256]{1,0:T(8,128)(2,1)S(1)} %slice_bitcast_fusion.2), channel_id=1, source_target_pairs={{0,8},{1,9},{2,10},{3,11},{4,0},{5,1},{6,2},{7,3},{8,12},{9,13},{1... | collective-permute-start | bytes 811016 | tf_op jit(solution)/shard_map/ppermute | solution.py:694
  78.5 15.6 %collective-permute-start.16 = (bf16[528,256]{1,0:T(8,128)(2,1)S(1)}, bf16[528,256]{1,0:T(8,128)(2,1)S(1)}, u32[]{:S(2)}, u32[]{:S(2)}) collective-permute-start(bf16[528,256]{1,0:T(8,128)(2,1)S(1)} %slice_bitcast_fusion), channel_id=1, source_target_pairs={{0,4},{1,5},{2,6},{3,7},{4,12},{5,13},{6,14},{7,15},{8,0},{9,1},{1... | collective-permute-start | bytes 811016 | tf_op jit(solution)/shard_map/ppermute | solution.py:694
  87.0 23.3 %collective-permute-start.12 = (bf16[2,512,256]{2,1,0:T(8,128)(2,1)S(1)}, bf16[2,512,256]{2,1,0:T(8,128)(2,1)S(1)}, u32[]{:S(2)}, u32[]{:S(2)}) collective-permute-start(bf16[2,512,256]{2,1,0:T(8,128)(2,1)S(1)} %get-tuple-element.89.refs_0_), channel_id=1, source_target_pairs={{0,4},{1,5},{2,6},{3,7},{4,12},{5,13},{6,14},{7,15},{8,0},{9,1},{1... | collective-permute-start | bytes 1572872 | tf_op jit(solution)/shard_map/ppermute | solution.py:694
  94.1 48.1 %collective-permute-start.18 = (bf16[2,2,2,256,256]{4,3,2,1,0:T(8,128)(2,1)}, bf16[2,2,2,256,256]{4,3,2,1,0:T(8,128)(2,1)S(1)}, u32[]{:S(2)}, u32[]{:S(2)}) collective-permute-start(bf16[2,2,2,256,256]{4,3,2,1,0:T(8,128)(2,1)} %get-tuple-element.84), channel_id=1, source_target_pairs={{0,1},{1,0},{2,3},{3,2},{4,5},{5,4},{6,7},{7,6},{8,9},{9,8},{10,11... | collective-permute-start | bytes 3145736 | tf_op jit(solution)/shard_map/ppermute | solution.py:694
  94.1 36.0 %collective-permute-start.21 = (bf16[2,512,256]{2,1,0:T(8,128)(2,1)S(1)}, bf16[2,512,256]{2,1,0:T(8,128)(2,1)S(1)}, u32[]{:S(2)}, u32[]{:S(2)}) collective-permute-start(bf16[2,512,256]{2,1,0:T(8,128)(2,1)S(1)} %get-tuple-element.89.refs_0_), channel_id=1, source_target_pairs={{0,8},{1,9},{2,10},{3,11},{4,0},{5,1},{6,2},{7,3},{8,12},{9,13},{1... | collective-permute-start | bytes 1572872 | tf_op jit(solution)/shard_map/ppermute | solution.py:694
  94.2 34.7 %collective-permute-start.24 = (bf16[2,512,256]{2,1,0:T(8,128)(2,1)S(1)}, bf16[2,512,256]{2,1,0:T(8,128)(2,1)S(1)}, u32[]{:S(2)}, u32[]{:S(2)}) collective-permute-start(bf16[2,512,256]{2,1,0:T(8,128)(2,1)S(1)} %get-tuple-element.92.refs_5_), channel_id=1, source_target_pairs={{0,8},{1,9},{2,10},{3,11},{4,0},{5,1},{6,2},{7,3},{8,12},{9,13},{1... | collective-permute-start | bytes 1572872 | tf_op jit(solution)/shard_map/ppermute | solution.py:694
  100.6 47.7 %copy-start.4 = (bf16[2,528,256]{2,1,0:T(8,128)(2,1)S(1)}, bf16[2,528,256]{2,1,0:T(8,128)(2,1)}, u32[]{:S(2)}) copy-start(bf16[2,528,256]{2,1,0:T(8,128)(2,1)} %copy-done.2) | copy-start | bytes 1622020
  100.6 47.7 %copy-start.7 = (bf16[2,528,256]{2,1,0:T(8,128)(2,1)S(1)}, bf16[2,528,256]{2,1,0:T(8,128)(2,1)}, u32[]{:S(2)}) copy-start(bf16[2,528,256]{2,1,0:T(8,128)(2,1)} %copy-done.5) | copy-start | bytes 1622020
  104.0 36.2 %collective-permute-start.23 = (bf16[2,512,256]{2,1,0:T(8,128)(2,1)S(1)}, bf16[2,512,256]{2,1,0:T(8,128)(2,1)S(1)}, u32[]{:S(2)}, u32[]{:S(2)}) collective-permute-start(bf16[2,512,256]{2,1,0:T(8,128)(2,1)S(1)} %get-tuple-element.92.refs_5_), channel_id=1, source_target_pairs={{0,4},{1,5},{2,6},{3,7},{4,12},{5,13},{6,14},{7,15},{8,0},{9,1},{1... | collective-permute-start | bytes 1572872 | tf_op jit(solution)/shard_map/ppermute | solution.py:694
  110.3 47.3 %collective-permute-start.20 = (bf16[2,2,256,256]{3,2,1,0:T(8,128)(2,1)}, bf16[2,2,256,256]{3,2,1,0:T(8,128)(2,1)}, u32[]{:S(2)}, u32[]{:S(2)}) collective-permute-start(bf16[2,2,256,256]{3,2,1,0:T(8,128)(2,1)} %get-tuple-element.87), channel_id=1, source_target_pairs={{0,3},{1,2},{2,1},{3,0},{4,7},{5,6},{6,5},{7,4},{8,11},{9,10},{10,... | collective-permute-start | bytes 1572872 | tf_op jit(solution)/shard_map/ppermute | solution.py:694
  129.0 28.7 %collective-permute-start.19 = (bf16[2,2,256,256]{3,2,1,0:T(8,128)(2,1)}, bf16[2,2,256,256]{3,2,1,0:T(8,128)(2,1)}, u32[]{:S(2)}, u32[]{:S(2)}) collective-permute-start(bf16[2,2,256,256]{3,2,1,0:T(8,128)(2,1)} %get-tuple-element.86), channel_id=1, source_target_pairs={{0,2},{1,3},{2,0},{3,1},{4,6},{5,7},{6,4},{7,5},{8,10},{9,11},{10,... | collective-permute-start | bytes 1572872 | tf_op jit(solution)/shard_map/ppermute | solution.py:694
  130.1 15.7 %collective-permute-start.14 = (bf16[512,256]{1,0:T(8,128)(2,1)S(1)}, bf16[512,256]{1,0:T(8,128)(2,1)S(1)}, u32[]{:S(2)}, u32[]{:S(2)}) collective-permute-start(bf16[512,256]{1,0:T(8,128)(2,1)S(1)} %slice_bitcast_fusion.7), channel_id=1, source_target_pairs={{0,4},{1,5},{2,6},{3,7},{4,12},{5,13},{6,14},{7,15},{8,0},{9,1},{1... | collective-permute-start | bytes 786440 | tf_op jit(solution)/shard_map/ppermute | solution.py:694
  140.2 17.5 %collective-permute-start.26 = (bf16[512,256]{1,0:T(8,128)(2,1)S(1)}, bf16[512,256]{1,0:T(8,128)(2,1)}, u32[]{:S(2)}, u32[]{:S(2)}) collective-permute-start(bf16[512,256]{1,0:T(8,128)(2,1)S(1)} %slice_bitcast_fusion.4), channel_id=1, source_target_pairs={{0,8},{1,9},{2,10},{3,11},{4,0},{5,1},{6,2},{7,3},{8,12},{9,13},{1... | collective-permute-start | bytes 786440 | tf_op jit(solution)/shard_map/ppermute | solution.py:694
  142.2 15.8 %collective-permute-start.22 = (bf16[512,256]{1,0:T(8,128)(2,1)S(1)}, bf16[512,256]{1,0:T(8,128)(2,1)}, u32[]{:S(2)}, u32[]{:S(2)}) collective-permute-start(bf16[512,256]{1,0:T(8,128)(2,1)S(1)} %slice_bitcast_fusion.6), channel_id=1, source_target_pairs={{0,8},{1,9},{2,10},{3,11},{4,0},{5,1},{6,2},{7,3},{8,12},{9,13},{1... | collective-permute-start | bytes 786440 | tf_op jit(solution)/shard_map/ppermute | solution.py:694
  145.8 16.3 %collective-permute-start.25 = (bf16[512,256]{1,0:T(8,128)(2,1)}, bf16[512,256]{1,0:T(8,128)(2,1)}, u32[]{:S(2)}, u32[]{:S(2)}) collective-permute-start(bf16[512,256]{1,0:T(8,128)(2,1)} %slice_bitcast_fusion.5), channel_id=1, source_target_pairs={{0,4},{1,5},{2,6},{3,7},{4,12},{5,13},{6,14},{7,15},{8,0},{9,1},{1... | collective-permute-start | bytes 786440 | tf_op jit(solution)/shard_map/ppermute | solution.py:694
  157.6 24.3 %collective-permute-start.30 = (bf16[2,2,256,256]{3,2,1,0:T(8,128)(2,1)S(1)}, bf16[2,2,256,256]{3,2,1,0:T(8,128)(2,1)S(1)}, u32[]{:S(2)}, u32[]{:S(2)}) collective-permute-start(bf16[2,2,256,256]{3,2,1,0:T(8,128)(2,1)S(1)} %get-tuple-element.105), channel_id=1, source_target_pairs={{0,1},{1,0},{2,3},{3,2},{4,5},{5,4},{6,7},{7,6},{8,9},{9,8},{10,11... | collective-permute-start | bytes 1572872 | tf_op jit(solution)/shard_map/ppermute | solution.py:694
  166.4 20.9 %collective-permute-start.27 = (bf16[2,2,256,256]{3,2,1,0:T(8,128)(2,1)S(1)}, bf16[2,2,256,256]{3,2,1,0:T(8,128)(2,1)S(1)}, u32[]{:S(2)}, u32[]{:S(2)}) collective-permute-start(bf16[2,2,256,256]{3,2,1,0:T(8,128)(2,1)S(1)} %get-tuple-element.94), channel_id=1, source_target_pairs={{0,2},{1,3},{2,0},{3,1},{4,6},{5,7},{6,4},{7,5},{8,10},{9,11},{10,... | collective-permute-start | bytes 1572872 | tf_op jit(solution)/shard_map/ppermute | solution.py:694
  178.7 15.5 %collective-permute-start.33 = (f32[2,128]{1,0:T(2,128)S(1)}, f32[2,128]{1,0:T(2,128)S(1)}, u32[]{:S(2)}, u32[]{:S(2)}) collective-permute-start(f32[2,128]{1,0:T(2,128)S(1)} %get-tuple-element.113), channel_id=1, source_target_pairs={{0,4},{1,5},{2,6},{3,7},{4,12},{5,13},{6,14},{7,15},{8,0},{9,1},{1... | collective-permute-start | bytes 3080 | tf_op jit(solution)/shard_map/ppermute | solution.py:694
  180.8 15.4 %collective-permute-start.29 = (bf16[2,2,256,256]{3,2,1,0:T(8,128)(2,1)S(1)}, bf16[2,2,256,256]{3,2,1,0:T(8,128)(2,1)S(1)}, u32[]{:S(2)}, u32[]{:S(2)}) collective-permute-start(bf16[2,2,256,256]{3,2,1,0:T(8,128)(2,1)S(1)} %get-tuple-element.102), channel_id=1, source_target_pairs={{0,1},{1,0},{2,3},{3,2},{4,5},{5,4},{6,7},{7,6},{8,9},{9,8},{10,11... | collective-permute-start | bytes 1572872 | tf_op jit(solution)/shard_map/ppermute | solution.py:694
  180.8 17.5 %collective-permute-start.28 = (bf16[2,2,256,256]{3,2,1,0:T(8,128)(2,1)S(1)}, bf16[2,2,256,256]{3,2,1,0:T(8,128)(2,1)S(1)}, u32[]{:S(2)}, u32[]{:S(2)}) collective-permute-start(bf16[2,2,256,256]{3,2,1,0:T(8,128)(2,1)S(1)} %get-tuple-element.98), channel_id=1, source_target_pairs={{0,3},{1,2},{2,1},{3,0},{4,7},{5,6},{6,5},{7,4},{8,11},{9,10},{10,... | collective-permute-start | bytes 1572872 | tf_op jit(solution)/shard_map/ppermute | solution.py:694
  181.9 12.4 %collective-permute-start.31 = (f32[2,128]{1,0:T(2,128)S(1)}, f32[2,128]{1,0:T(2,128)S(1)}, u32[]{:S(2)}, u32[]{:S(2)}) collective-permute-start(f32[2,128]{1,0:T(2,128)S(1)} %get-tuple-element.108), channel_id=1, source_target_pairs={{0,12},{1,13},{2,14},{3,15},{4,8},{5,9},{6,10},{7,11},{8,4},{9,5},... | collective-permute-start | bytes 3080 | tf_op jit(solution)/shard_map/ppermute | solution.py:694
  187.4 6.8 %collective-permute-start.32 = (f32[2,128]{1,0:T(2,128)S(1)}, f32[2,128]{1,0:T(2,128)S(1)}, u32[]{:S(2)}, u32[]{:S(2)}) collective-permute-start(f32[2,128]{1,0:T(2,128)S(1)} %get-tuple-element.109), channel_id=1, source_target_pairs={{0,8},{1,9},{2,10},{3,11},{4,0},{5,1},{6,2},{7,3},{8,12},{9,13},{1... | collective-permute-start | bytes 3080 | tf_op jit(solution)/shard_map/ppermute | solution.py:694
  194.3 6.2 %collective-permute-start.34 = (f32[2,32]{1,0:T(2,128)S(1)}, f32[2,32]{1,0:T(2,128)S(1)}, u32[]{:S(2)}, u32[]{:S(2)}) collective-permute-start(f32[2,32]{1,0:T(2,128)S(1)} %get-tuple-element.110), channel_id=1, source_target_pairs={{0,1},{1,0},{2,3},{3,2},{4,5},{5,4},{6,7},{7,6},{8,9},{9,8},{10,11... | collective-permute-start | bytes 776 | tf_op jit(solution)/shard_map/ppermute | solution.py:694
  194.4 6.1 %collective-permute-start.35 = (f32[2,32]{1,0:T(2,128)S(1)}, f32[2,32]{1,0:T(2,128)S(1)}, u32[]{:S(2)}, u32[]{:S(2)}) collective-permute-start(f32[2,32]{1,0:T(2,128)S(1)} %get-tuple-element.111), channel_id=1, source_target_pairs={{0,2},{1,3},{2,0},{3,1},{4,6},{5,7},{6,4},{7,5},{8,10},{9,11},{10,... | collective-permute-start | bytes 776 | tf_op jit(solution)/shard_map/ppermute | solution.py:694
  194.4 6.1 %collective-permute-start.36 = (f32[2,32]{1,0:T(2,128)S(1)}, f32[2,32]{1,0:T(2,128)S(1)}, u32[]{:S(2)}, u32[]{:S(2)}) collective-permute-start(f32[2,32]{1,0:T(2,128)S(1)} %get-tuple-element.116), channel_id=1, source_target_pairs={{0,3},{1,2},{2,1},{3,0},{4,7},{5,6},{6,5},{7,4},{8,11},{9,10},{10,... | collective-permute-start | bytes 776 | tf_op jit(solution)/shard_map/ppermute | solution.py:694
  (37 other events, 232.8 us)

commit v8 on v7

--- a/solution.py
+++ b/solution.py
@@ -323,11 +323,8 @@
         return lax.dot_general(a, b, (((1,), (0,)), ((), ())), preferred_element_type=jnp.float32)
 
     def scaled_of(re, im):
-        column = jnp.concatenate([columns_ref[index]] * (span // 128), 1)
-        return (
-            (re.astype(jnp.float32) * column).astype(jnp.bfloat16),
-            (im.astype(jnp.float32) * column).astype(jnp.bfloat16),
-        )
+        column = jnp.concatenate([columns_ref[index].astype(jnp.bfloat16)] * (span // 128), 1)
+        return re * column, im * column
 
     def outer(a, b):
         row_ids = lax.broadcasted_iota(jnp.int32, a.shape, 0)
@@ -642,36 +639,40 @@
 WORK, HOME, PUT, LATER_WORK, LATER_HOME, PUT_NEAR, PUT_LAST = 32, 35, 38, 40, 43, 46, 47
 SUM_PLANES, SUM_PLANE = 48, 51
 GATES = {
-    1: (0,),
-    3: (0, 1),
+    1: (0, 11),
+    2: (0, 11),
+    3: (0,),
+    4: (0, 13),
     5: (0, 2, 13),
-    6: (1, 2, 11),
+    6: (13,),
     7: (1, 2),
     14: (13,),
-    16: (2,),
-    17: (1,),
-    19: (18,),
-    20: (3, 4, 6, 7, 17),
-    21: (3, 4, 5, 13, 14, 16, 17),
-    23: (4, 17),
-    24: (6, 9, 17),
-    25: (6, 9, 17, 23),
-    26: (9,),
+    16: (0, 2),
+    17: (0, 1),
+    18: (0,),
+    19: (3, 4, 18),
+    20: (3, 4, 6, 17),
+    21: (3, 4, 13, 14, 16, 17),
+    24: (6, 7, 16, 17, 21),
+    25: (7, 9, 17, 21, 23),
     27: (8,),
-    28: (22,),
-    31: (25, 27),
-    33: (23, 32),
-    34: (33,),
-    35: (8, 9, 24, 25),
-    40: (28, 34, 36, 37),
-    41: (40,),
-    42: (29, 41),
-    43: (41,),
-    45: (28, 32),
+    28: (22, 25),
+    29: (25,),
+    31: (27, 28, 37),
+    33: (32,),
+    35: (8, 9, 24, 25, 36),
+    37: (24,),
+    38: (25,),
+    40: (24, 33, 36, 37),
+    41: (28, 31, 40),
+    44: (28, 30),
+    45: (28, 32, 35),
+    46: (40,),
     48: (35,),
     49: (44,),
-    51: (34,),
-    52: (38,),
+    51: (33,),
+    52: (38, 40, 44),
+    53: (49,),
 }
 
 
@@ -754,7 +755,7 @@
 
     def work(index, step, home_step, ready, bright):
         arrived, total = [], None
-        for n, homes in enumerate([routes.order[:1], routes.order[1:2], routes.order[2:]]):
+        for n, homes in enumerate([routes.order[:1], routes.order[1:]]):
             made = unit_work(
                 index,
                 routes.steps[index] + len(arrived) * routes.steps_per_home,

time: 202 us -> 205 us (1.015)
  starting transfers between devices: 51.3 us -> 69.3 us
  waiting for transfers between devices: 64.7 us -> 57.4 us
  Pallas kernels: 60.7 us -> 55.9 us
  local copies, waits for them, and re-layouts: 21.2 us -> 18.2 us
    ppermute x37, starting transfers between devices: 51.3 us -> 69.3 us  [send(): done[step] = lax.ppermute(gated(step, value), 'tile', pairs)]
    ppermute x37, waiting for transfers between devices: 64.7 us -> 57.4 us  [send(): done[step] = lax.ppermute(gated(step, value), 'tile', pairs)]
    pallas_call x6 -> x4, Pallas kernels: 33.3 us -> 28.5 us  [unit_work(): pl.pallas_call(functools.partial(unit_kernel, index, offset, kinds, brigh...]
    unnamed x97 -> x95, local copies, waits for them, and re-layouts: 15.5 us -> 14.8 us
  transfers between devices with their start and end apart: 37 -> 37, of which waited for: 12 -> 11; matrix products, arithmetic and copies ran while one was open for 3% -> 2% of each run, Pallas kernels for 28% -> 25%
where the time goes in v8:
time: 205 us; the launch traced here: 204 us
  starting transfers between devices  69.3 us (34%)
  waiting for transfers between devices  57.4 us (28%)
  Pallas kernels  55.9 us (27%)
  local copies, waits for them, and re-layouts  18.2 us (9%)
  other arithmetic  2.19 us (1%)
    ppermute x37, starting transfers between devices, send(): done[step] = lax.ppermute(gated(step, value), 'tile', pairs)  69.3 us
    ppermute x37, waiting for transfers between devices, send(): done[step] = lax.ppermute(gated(step, value), 'tile', pairs)  57.4 us
    pallas_call x4, Pallas kernels, unit_work(): pl.pallas_call(functools.partial(unit_kernel, index, offset, kinds, brigh...  28.5 us
    unnamed x95, local copies, waits for them, and re-layouts  14.8 us
    pallas_call x3, Pallas kernels, put_residuals(): pl.pallas_call(functools.partial(put_kernel, sources), grid_spec=pltpu.Pr...  8.94 us
    pallas_call x3, Pallas kernels, messages_for(): pl.pallas_call(functools.partial(message_kernel, len(others), bool(smalls...  7.71 us
    pallas_call x3, Pallas kernels, build_factors(): pl.pallas_call(functools.partial(build_kernel, sets, slot_ids, pieces, br...  6.76 us
  transfers between devices with their start and end apart: 37, of which 11 were waited for; matrix products, arithmetic and copies ran while one was open for 2% of the time, Pallas kernels for 25%

profile of v8, /device:TPU:0, one launch (start us, length us, event | category | flops | bytes accessed | tf_op | source)
XLA Modules:
  0.0 204.1 jit_solution(12541913755234903302)
XLA Ops:
  0.6 1.4 broadcast_in_dim.34
  2.0 1.3 constant_dynamic-slice_fusion
  3.3 2.4 %messages_for.4 = bf16[80,2048]{1,0:T(8,128)(2,1)} custom-call(s32[148]{0:T(256)} %bitcast.24, bf16[8,2,32,2048]{3,2,1,0:T(8,128)(2,1)} %refs_0_.10, f32[2,256]{1,0:T(2,128)} %refs_4_.5, f32[1,256]{1,0:T(1,128)} %bitcast.38, s32[8,32]{1,0:T(8,128)} %refs_6_.1), custom_call_target="tpu_custom_call" | custom-call | flops 1 | bytes 1 | tf_op jit(solution)/shard_map/messages_for/pallas_call | solution.py:211
  6.1 1.1 copy.15.refs_5_.refs_10_.refs_2_
  10.3 1.6 build_factors.3.refs_0_
  12.7 2.9 %collective-permute-start.3 = (bf16[2,528,256]{2,1,0:T(8,128)(2,1)S(1)}, bf16[2,528,256]{2,1,0:T(8,128)(2,1)S(1)}, u32[]{:S(2)}, u32[]{:S(2)}) collective-permute-start(bf16[2,528,256]{2,1,0:T(8,128)(2,1)S(1)} %build_factors.3.refs_0_), channel_id=1, source_target_pairs={{0,4},{1,5},{2,6},{3,7},{4,12},{5,13},{6,14},{7,15},{8,0},{9,1},{1... | collective-permute-start | bytes 1622024 | tf_op jit(solution)/shard_map/ppermute | solution.py:695
  15.6 2.6 %messages_for.5 = (bf16[80,2048]{1,0:T(8,128)(2,1)}, bf16[80,2048]{1,0:T(8,128)(2,1)}) custom-call(s32[148]{0:T(256)} %bitcast.25, bf16[8,2,32,2048]{3,2,1,0:T(8,128)(2,1)} %refs_0_.10, bf16[8,2,32,2048]{3,2,1,0:T(8,128)(2,1)} %refs_0_.10, f32[2,256]{1,0:T(2,128)} %refs_4_.5, f32[1,256]{1,0:T(1,128)} %bitcast.39, s32[8,32]{1,0:T(8,128)} %refs_6_.1), custom_call_target="tpu_custom_call" | custom-call | flops 1 | bytes 1 | tf_op jit(solution)/shard_map/messages_for/pallas_call | solution.py:211
  18.2 1.5 collective-permute-start.6
  19.7 1.3 collective-permute-start.1
  21.1 2.7 %messages_for.3 = (bf16[64,2048]{1,0:T(8,128)(2,1)}, bf16[64,2048]{1,0:T(8,128)(2,1)}, bf16[64,2048]{1,0:T(8,128)(2,1)}) custom-call(s32[148]{0:T(256)} %bitcast.26, bf16[8,2,32,2048]{3,2,1,0:T(8,128)(2,1)} %refs_0_.10, bf16[8,2,32,2048]{3,2,1,0:T(8,128)(2,1)} %refs_0_.10, bf16[8,2,32,2048]{3,2,1,0:T(8,128)(2,1)} %refs_0_.10), custom_call_target="tpu_custom_call" | custom-call | flops 1 | bytes 1 | tf_op jit(solution)/shard_map/messages_for/pallas_call | solution.py:211
  23.8 4.9 %collective-permute-done.6.refs_8_.refs_0_ = bf16[80,2048]{1,0:T(8,128)(2,1)S(1)} collective-permute-done((bf16[80,2048]{1,0:T(8,128)(2,1)}, bf16[80,2048]{1,0:T(8,128)(2,1)S(1)}, u32[]{:S(2)}, u32[]{:S(2)}) %collective-permute-start.6) | collective-permute-done | bytes 327712 | tf_op jit(solution)/shard_map/ppermute | solution.py:695
  29.3 12.4 %collective-permute-start.10 = (bf16[528,256]{1,0:T(8,128)(2,1)S(1)}, bf16[528,256]{1,0:T(8,128)(2,1)S(1)}, u32[]{:S(2)}, u32[]{:S(2)}) collective-permute-start(bf16[528,256]{1,0:T(8,128)(2,1)S(1)} %slice_bitcast_fusion.3), channel_id=1, source_target_pairs={{0,4},{1,5},{2,6},{3,7},{4,12},{5,13},{6,14},{7,15},{8,0},{9,1},{1... | collective-permute-start | bytes 811016 | tf_op jit(solution)/shard_map/ppermute | solution.py:695
  41.8 1.5 collective-permute-start.11
  43.4 1.6 build_factors.5.refs_5_
  45.0 2.0 collective-permute-start.8
  47.8 1.5 collective-permute-start.4
  50.0 3.3 %collective-permute-start.9 = (bf16[2,528,256]{2,1,0:T(8,128)(2,1)S(1)}, bf16[2,528,256]{2,1,0:T(8,128)(2,1)}, u32[]{:S(2)}, u32[]{:S(2)}) collective-permute-start(bf16[2,528,256]{2,1,0:T(8,128)(2,1)S(1)} %build_factors.5.refs_5_), channel_id=1, source_target_pairs={{0,8},{1,9},{2,10},{3,11},{4,0},{5,1},{6,2},{7,3},{8,12},{9,13},{1... | collective-permute-start | bytes 1622024 | tf_op jit(solution)/shard_map/ppermute | solution.py:695
  53.3 4.6 %collective-permute-done.11.refs_4_ = bf16[528,256]{1,0:T(8,128)(2,1)S(1)} collective-permute-done((bf16[528,256]{1,0:T(8,128)(2,1)S(1)}, bf16[528,256]{1,0:T(8,128)(2,1)S(1)}, u32[]{:S(2)}, u32[]{:S(2)}) %collective-permute-start.11) | collective-permute-done | bytes 270368 | tf_op jit(solution)/shard_map/ppermute | solution.py:695
  58.6 4.0 %slices_for.1 = (bf16[2,2,2,256,256]{4,3,2,1,0:T(8,128)(2,1)}, bf16[2,2,2,256,256]{4,3,2,1,0:T(8,128)(2,1)}, bf16[2,2,2,256,256]{4,3,2,1,0:T(8,128)(2,1)}) custom-call(s32[148]{0:T(256)} %bitcast.27, bf16[2,8,2,256,256]{4,3,2,1,0:T(8,128)(2,1)} %refs_12_.3, bf16[2,8,2,256,256]{4,3,2,1,0:T(8,128)(2,1)} %refs_12_.3, bf16[2,8,2,256,256]{4,3,2,1,0:T(8,128)(2,1)} %refs_12_.3), custom_call_target="tpu_custom_call" | custom-call | flops 1 | bytes 1 | tf_op jit(solution)/shard_map/slices_for/pallas_call | solution.py:242
  62.6 1.6 collective-permute-start.12
  64.2 2.0 collective-permute-done.8.refs_6_
  67.1 12.2 %collective-permute-start.14 = (bf16[528,256]{1,0:T(8,128)(2,1)S(1)}, bf16[528,256]{1,0:T(8,128)(2,1)S(1)}, u32[]{:S(2)}, u32[]{:S(2)}) collective-permute-start(bf16[528,256]{1,0:T(8,128)(2,1)S(1)} %slice_bitcast_fusion.1), channel_id=1, source_target_pairs={{0,4},{1,5},{2,6},{3,7},{4,12},{5,13},{6,14},{7,15},{8,0},{9,1},{1... | collective-permute-start | bytes 811016 | tf_op jit(solution)/shard_map/ppermute | solution.py:695
  83.2 3.5 %build_factors.4 = (bf16[2,512,256]{2,1,0:T(8,128)(2,1)S(1)}, bf16[2,512,256]{2,1,0:T(8,128)(2,1)S(1)}) custom-call(s32[148]{0:T(256)S(1)} %bitcast.30, bf16[8,2,32,2048]{3,2,1,0:T(8,128)(2,1)S(1)} %copy-done.1, bf16[64,2048]{1,0:T(8,128)(2,1)} %collective-permute-done.2.refs_1_, bf16[64,2048]{1,0:T(8,128)(2,1)} %collective-permute-done.4.refs_2_, ...), custom_call_target="tpu_custom_call" | custom-call | flops 1 | bytes 1 | tf_op jit(solution)/shard_map/build_factors/pallas_call | solution.py:161
  86.8 3.6 %collective-permute-start.23 = (bf16[2,512,256]{2,1,0:T(8,128)(2,1)S(1)}, bf16[2,512,256]{2,1,0:T(8,128)(2,1)S(1)}, u32[]{:S(2)}, u32[]{:S(2)}) collective-permute-start(bf16[2,512,256]{2,1,0:T(8,128)(2,1)S(1)} %get-tuple-element.93.refs_5_), channel_id=1, source_target_pairs={{0,4},{1,5},{2,6},{3,7},{4,12},{5,13},{6,14},{7,15},{8,0},{9,1},{1... | collective-permute-start | bytes 1572872 | tf_op jit(solution)/shard_map/ppermute | solution.py:695
  90.4 1.6 collective-permute-start.17
  93.2 15.4 %collective-permute-done.15.refs_9_ = bf16[528,256]{1,0:T(8,128)(2,1)S(1)} collective-permute-done((bf16[528,256]{1,0:T(8,128)(2,1)S(1)}, bf16[528,256]{1,0:T(8,128)(2,1)S(1)}, u32[]{:S(2)}, u32[]{:S(2)}) %collective-permute-start.15) | collective-permute-done | bytes 270368 | tf_op jit(solution)/shard_map/ppermute | solution.py:695
  109.1 2.9 %collective-permute-start.20 = (bf16[2,512,256]{2,1,0:T(8,128)(2,1)S(1)}, bf16[2,512,256]{2,1,0:T(8,128)(2,1)S(1)}, u32[]{:S(2)}, u32[]{:S(2)}) collective-permute-start(bf16[2,512,256]{2,1,0:T(8,128)(2,1)S(1)} %get-tuple-element.89.refs_0_), channel_id=1, source_target_pairs={{0,8},{1,9},{2,10},{3,11},{4,0},{5,1},{6,2},{7,3},{8,12},{9,13},{1... | collective-permute-start | bytes 1572872 | tf_op jit(solution)/shard_map/ppermute | solution.py:695
  112.0 4.5 %unit_work.4 = (bf16[2,2,256,256]{3,2,1,0:T(8,128)(2,1)S(1)}, f32[1,512]{1,0:T(1,128)S(1)}, f32[2,512,128]{2,1,0:T(8,128)S(1)}) custom-call(s32[148]{0:T(256)S(1)} %bitcast.31, bf16[2,528,256]{2,1,0:T(8,128)(2,1)S(1)} %build_factors.3.refs_0_, bf16[2,528,256]{2,1,0:T(8,128)(2,1)S(1)} %copy-done.4, bf16[2,528,256]{2,1,0:T(8,128)(2,1)S(1)} %copy-done.6, ...), custom_call_target="tpu_custom_call" | custom-call | flops 1 | bytes 1 | tf_op jit(solution)/shard_map/unit_work/pallas_call | solution.py:476
  116.9 1.6 collective-permute-start.18
  118.5 10.1 %unit_work.5 = (bf16[2,2,256,256]{3,2,1,0:T(8,128)(2,1)S(1)}, bf16[2,2,256,256]{3,2,1,0:T(8,128)(2,1)}, bf16[2,2,256,256]{3,2,1,0:T(8,128)(2,1)S(1)}, f32[1,512]{1,0:T(1,128)S(1)}) custom-call(s32[148]{0:T(256)S(1)} %bitcast.32, bf16[2,528,256]{2,1,0:T(8,128)(2,1)S(1)} %build_factors.3.refs_0_, bf16[2,528,256]{2,1,0:T(8,128)(2,1)S(1)} %copy-done.4, ...), custom_call_target="tpu_custom_call" | custom-call | flops 1 | bytes 1 | tf_op jit(solution)/shard_map/unit_work/pallas_call | solution.py:476
  128.5 2.6 %collective-permute-done.13.refs_1_ = bf16[2,512,256]{2,1,0:T(8,128)(2,1)S(1)} collective-permute-done((bf16[2,512,256]{2,1,0:T(8,128)(2,1)S(1)}, bf16[2,512,256]{2,1,0:T(8,128)(2,1)S(1)}, u32[]{:S(2)}, u32[]{:S(2)}) %collective-permute-start.13) | collective-permute-done | bytes 524320 | tf_op jit(solution)/shard_map/ppermute | solution.py:695
  132.1 10.3 %collective-permute-done.20.refs_2_ = bf16[2,512,256]{2,1,0:T(8,128)(2,1)S(1)} collective-permute-done((bf16[2,512,256]{2,1,0:T(8,128)(2,1)S(1)}, bf16[2,512,256]{2,1,0:T(8,128)(2,1)S(1)}, u32[]{:S(2)}, u32[]{:S(2)}) %collective-permute-start.20) | collective-permute-done | bytes 524320 | tf_op jit(solution)/shard_map/ppermute | solution.py:695
  142.9 2.9 %collective-permute-start.22 = (bf16[512,256]{1,0:T(8,128)(2,1)S(1)}, bf16[512,256]{1,0:T(8,128)(2,1)S(1)}, u32[]{:S(2)}, u32[]{:S(2)}) collective-permute-start(bf16[512,256]{1,0:T(8,128)(2,1)S(1)} %slice_bitcast_fusion.6), channel_id=1, source_target_pairs={{0,8},{1,9},{2,10},{3,11},{4,0},{5,1},{6,2},{7,3},{8,12},{9,13},{1... | collective-permute-start | bytes 786440 | tf_op jit(solution)/shard_map/ppermute | solution.py:695
  145.9 8.6 %collective-permute-done.21.refs_3_ = bf16[512,256]{1,0:T(8,128)(2,1)S(1)} collective-permute-done((bf16[512,256]{1,0:T(8,128)(2,1)S(1)}, bf16[512,256]{1,0:T(8,128)(2,1)S(1)}, u32[]{:S(2)}, u32[]{:S(2)}) %collective-permute-start.21) | collective-permute-done | bytes 262176 | tf_op jit(solution)/shard_map/ppermute | solution.py:695
  155.0 4.2 %collective-permute-done.22.refs_4_ = bf16[512,256]{1,0:T(8,128)(2,1)S(1)} collective-permute-done((bf16[512,256]{1,0:T(8,128)(2,1)S(1)}, bf16[512,256]{1,0:T(8,128)(2,1)S(1)}, u32[]{:S(2)}, u32[]{:S(2)}) %collective-permute-start.22) | collective-permute-done | bytes 262176 | tf_op jit(solution)/shard_map/ppermute | solution.py:695
  159.2 3.8 %collective-permute-done.26.refs_9_ = bf16[512,256]{1,0:T(8,128)(2,1)S(1)} collective-permute-done((bf16[512,256]{1,0:T(8,128)(2,1)S(1)}, bf16[512,256]{1,0:T(8,128)(2,1)S(1)}, u32[]{:S(2)}, u32[]{:S(2)}) %collective-permute-start.26) | collective-permute-done | bytes 262176 | tf_op jit(solution)/shard_map/ppermute | solution.py:695
  163.1 4.7 %unit_work.6 = (bf16[2,2,256,256]{3,2,1,0:T(8,128)(2,1)}, f32[1,512]{1,0:T(1,128)S(1)}) custom-call(s32[148]{0:T(256)S(1)} %bitcast.33, bf16[2,512,256]{2,1,0:T(8,128)(2,1)S(1)} %get-tuple-element.89.refs_0_, bf16[2,512,256]{2,1,0:T(8,128)(2,1)S(1)} %collective-permute-done.13.refs_1_, bf16[2,512,256]{2,1,0:T(8,128)(2,1)S(1)} %collective-permute-done.20.refs_2_, ...), custom_call_target="tpu_custom_call" | custom-call | flops 1 | bytes 1 | tf_op jit(solution)/shard_map/unit_work/pallas_call | solution.py:476
  167.8 1.6 collective-permute-start.27
  170.4 1.0 copy-done.10
  171.5 1.0 copy-done.12
  173.6 9.2 %unit_work.7 = (bf16[2,2,256,256]{3,2,1,0:T(8,128)(2,1)S(1)}, bf16[2,2,256,256]{3,2,1,0:T(8,128)(2,1)S(1)}, bf16[2,2,256,256]{3,2,1,0:T(8,128)(2,1)S(1)}, f32[1,512]{1,0:T(1,128)S(1)}) custom-call(s32[148]{0:T(256)S(1)} %bitcast.34, bf16[2,512,256]{2,1,0:T(8,128)(2,1)S(1)} %copy-done.12, bf16[2,512,256]{2,1,0:T(8,128)(2,1)S(1)} %copy-done.8, ...), custom_call_target="tpu_custom_call" | custom-call | flops 1 | bytes 1 | tf_op jit(solution)/shard_map/unit_work/pallas_call | solution.py:476
  182.9 1.8 collective-permute-start.33
  184.8 5.2 %collective-permute-start.31 = (f32[2,128]{1,0:T(2,128)S(1)}, f32[2,128]{1,0:T(2,128)S(1)}, u32[]{:S(2)}, u32[]{:S(2)}) collective-permute-start(f32[2,128]{1,0:T(2,128)S(1)} %get-tuple-element.109), channel_id=1, source_target_pairs={{0,12},{1,13},{2,14},{3,15},{4,8},{5,9},{6,10},{7,11},{8,4},{9,5},... | collective-permute-start | bytes 3080 | tf_op jit(solution)/shard_map/ppermute | solution.py:695
  190.7 1.7 collective-permute-start.32
  192.4 4.7 %put_residuals.3.refs_2_ = bf16[2,8,2,256,256]{4,3,2,1,0:T(8,128)(2,1)} custom-call(s32[148]{0:T(256)S(1)} %bitcast.35, bf16[2,2,256,256]{3,2,1,0:T(8,128)(2,1)S(1)} %copy-done.26, bf16[2,2,256,256]{3,2,1,0:T(8,128)(2,1)S(1)} %copy-done.30, bf16[2,2,256,256]{3,2,1,0:T(8,128)(2,1)} %collective-permute-done.28.refs_2_, bf16[2,2,256,256]{3,2,1,0:T(8,128)(2,1)S(1)} %copy-done.28), custom_call_target="tpu_custom_call" | custom-call | flops 1 | bytes 1 | tf_op jit(solution)/shard_map/put_residuals/pallas_call | solution.py:516
  197.5 1.1 collective-permute-start.35
  199.1 2.1 %put_residuals.4.refs_2_ = bf16[2,8,2,256,256]{4,3,2,1,0:T(8,128)(2,1)} custom-call(s32[148]{0:T(256)S(1)} %bitcast.36, bf16[2,2,256,256]{3,2,1,0:T(8,128)(2,1)S(1)} %collective-permute-done.30.refs_0_, bf16[2,2,256,256]{3,2,1,0:T(8,128)(2,1)S(1)} %get-tuple-element.105.refs_1_, ...), custom_call_target="tpu_custom_call", output_to_operand_aliasing={{}: (3, {})} | custom-call | flops 1 | bytes 1 | tf_op jit(solution)/shard_map/put_residuals/pallas_call | solution.py:516
  201.2 2.1 %put_residuals.5 = bf16[2,8,2,256,256]{4,3,2,1,0:T(8,128)(2,1)} custom-call(s32[148]{0:T(256)S(1)} %bitcast.37, bf16[2,2,256,256]{3,2,1,0:T(8,128)(2,1)S(1)} %collective-permute-done.27.refs_0_, bf16[2,2,256,256]{3,2,1,0:T(8,128)(2,1)S(1)} %collective-permute-done.29.refs_1_, ...), custom_call_target="tpu_custom_call", output_to_operand_aliasing={{}: (3, {})} | custom-call | flops 1 | bytes 1 | tf_op jit(solution)/shard_map/put_residuals/pallas_call | solution.py:516
  (157 shorter events, 20.5 us)
Async XLA Ops:
  5.7 1.9 collective-permute-start
  12.7 16.6 %collective-permute-start.3 = (bf16[2,528,256]{2,1,0:T(8,128)(2,1)S(1)}, bf16[2,528,256]{2,1,0:T(8,128)(2,1)S(1)}, u32[]{:S(2)}, u32[]{:S(2)}) collective-permute-start(bf16[2,528,256]{2,1,0:T(8,128)(2,1)S(1)} %build_factors.3.refs_0_), channel_id=1, source_target_pairs={{0,4},{1,5},{2,6},{3,7},{4,12},{5,13},{6,14},{7,15},{8,0},{9,1},{1... | collective-permute-start | bytes 1622024 | tf_op jit(solution)/shard_map/ppermute | solution.py:695
  18.2 10.5 %collective-permute-start.6 = (bf16[80,2048]{1,0:T(8,128)(2,1)}, bf16[80,2048]{1,0:T(8,128)(2,1)S(1)}, u32[]{:S(2)}, u32[]{:S(2)}) collective-permute-start(bf16[80,2048]{1,0:T(8,128)(2,1)} %get-tuple-element.65), channel_id=1, source_target_pairs={{0,2},{1,3},{2,0},{3,1},{4,6},{5,7},{6,4},{7,5},{8,10},{9,11},{10,... | collective-permute-start | bytes 983048 | tf_op jit(solution)/shard_map/ppermute | solution.py:695
  19.7 22.1 %collective-permute-start.1 = (bf16[2,528,256]{2,1,0:T(8,128)(2,1)S(1)}, bf16[2,528,256]{2,1,0:T(8,128)(2,1)S(1)}, u32[]{:S(2)}, u32[]{:S(2)}) collective-permute-start(bf16[2,528,256]{2,1,0:T(8,128)(2,1)S(1)} %build_factors.3.refs_0_), channel_id=1, source_target_pairs={{0,8},{1,9},{2,10},{3,11},{4,0},{5,1},{6,2},{7,3},{8,12},{9,13},{1... | collective-permute-start | bytes 1622024 | tf_op jit(solution)/shard_map/ppermute | solution.py:695
  23.8 23.2 %collective-permute-start.5 = (bf16[64,2048]{1,0:T(8,128)(2,1)}, bf16[64,2048]{1,0:T(8,128)(2,1)S(1)}, u32[]{:S(2)}, u32[]{:S(2)}) collective-permute-start(bf16[64,2048]{1,0:T(8,128)(2,1)} %get-tuple-element.64), channel_id=1, source_target_pairs={{0,3},{1,2},{2,1},{3,0},{4,7},{5,6},{6,5},{7,4},{8,11},{9,10},{10,... | collective-permute-start | bytes 786440 | tf_op jit(solution)/shard_map/ppermute | solution.py:695
  28.7 14.6 %collective-permute-start.7 = (bf16[80,2048]{1,0:T(8,128)(2,1)S(1)}, bf16[80,2048]{1,0:T(8,128)(2,1)S(1)}, u32[]{:S(2)}, u32[]{:S(2)}) collective-permute-start(bf16[80,2048]{1,0:T(8,128)(2,1)S(1)} %copy-done.46), channel_id=1, source_target_pairs={{0,3},{1,2},{2,1},{3,0},{4,7},{5,6},{6,5},{7,4},{8,11},{9,10},{10,... | collective-permute-start | bytes 983048 | tf_op jit(solution)/shard_map/ppermute | solution.py:695
  29.3 19.9 %collective-permute-start.10 = (bf16[528,256]{1,0:T(8,128)(2,1)S(1)}, bf16[528,256]{1,0:T(8,128)(2,1)S(1)}, u32[]{:S(2)}, u32[]{:S(2)}) collective-permute-start(bf16[528,256]{1,0:T(8,128)(2,1)S(1)} %slice_bitcast_fusion.3), channel_id=1, source_target_pairs={{0,4},{1,5},{2,6},{3,7},{4,12},{5,13},{6,14},{7,15},{8,0},{9,1},{1... | collective-permute-start | bytes 811016 | tf_op jit(solution)/shard_map/ppermute | solution.py:695
  41.8 16.1 %collective-permute-start.11 = (bf16[528,256]{1,0:T(8,128)(2,1)S(1)}, bf16[528,256]{1,0:T(8,128)(2,1)S(1)}, u32[]{:S(2)}, u32[]{:S(2)}) collective-permute-start(bf16[528,256]{1,0:T(8,128)(2,1)S(1)} %slice_bitcast_fusion.2), channel_id=1, source_target_pairs={{0,8},{1,9},{2,10},{3,11},{4,0},{5,1},{6,2},{7,3},{8,12},{9,13},{1... | collective-permute-start | bytes 811016 | tf_op jit(solution)/shard_map/ppermute | solution.py:695
  45.0 21.1 %collective-permute-start.8 = (bf16[2,528,256]{2,1,0:T(8,128)(2,1)S(1)}, bf16[2,528,256]{2,1,0:T(8,128)(2,1)}, u32[]{:S(2)}, u32[]{:S(2)}) collective-permute-start(bf16[2,528,256]{2,1,0:T(8,128)(2,1)S(1)} %build_factors.5.refs_5_), channel_id=1, source_target_pairs={{0,4},{1,5},{2,6},{3,7},{4,12},{5,13},{6,14},{7,15},{8,0},{9,1},{1... | collective-permute-start | bytes 1622024 | tf_op jit(solution)/shard_map/ppermute | solution.py:695
  46.9 15.6 %collective-permute-start.2 = (bf16[64,2048]{1,0:T(8,128)(2,1)}, bf16[64,2048]{1,0:T(8,128)(2,1)}, u32[]{:S(2)}, u32[]{:S(2)}) collective-permute-start(bf16[64,2048]{1,0:T(8,128)(2,1)} %get-tuple-element.60), channel_id=1, source_target_pairs={{0,1},{1,0},{2,3},{3,2},{4,5},{5,4},{6,7},{7,6},{8,9},{9,8},{10,11... | collective-permute-start | bytes 786440 | tf_op jit(solution)/shard_map/ppermute | solution.py:695
  47.0 32.4 %copy-start.1 = (bf16[8,2,32,2048]{3,2,1,0:T(8,128)(2,1)S(1)}, bf16[8,2,32,2048]{3,2,1,0:T(8,128)(2,1)}, u32[]{:S(2)}) copy-start(bf16[8,2,32,2048]{3,2,1,0:T(8,128)(2,1)} %refs_0_.10) | copy-start | bytes 6291460
  47.0 32.4 %copy-start.35 = (s32[1,148]{1,0:T(1,128)S(1)}, s32[1,148]{1,0:T(1,128)}, u32[]{:S(2)}) copy-start(s32[1,148]{1,0:T(1,128)} %constant_dynamic-slice_fusion) | copy-start | bytes 1780
  47.0 32.4 %copy-start.37 = (s32[8,32]{1,0:T(8,128)S(1)}, s32[8,32]{1,0:T(8,128)}, u32[]{:S(2)}) copy-start(s32[8,32]{1,0:T(8,128)} %refs_6_.1) | copy-start | bytes 3076
  47.8 14.8 %collective-permute-start.4 = (bf16[64,2048]{1,0:T(8,128)(2,1)}, bf16[64,2048]{1,0:T(8,128)(2,1)}, u32[]{:S(2)}, u32[]{:S(2)}) collective-permute-start(bf16[64,2048]{1,0:T(8,128)(2,1)} %get-tuple-element.62), channel_id=1, source_target_pairs={{0,2},{1,3},{2,0},{3,1},{4,6},{5,7},{6,4},{7,5},{8,10},{9,11},{10,... | collective-permute-start | bytes 786440 | tf_op jit(solution)/shard_map/ppermute | solution.py:695
  50.0 40.4 %collective-permute-start.9 = (bf16[2,528,256]{2,1,0:T(8,128)(2,1)S(1)}, bf16[2,528,256]{2,1,0:T(8,128)(2,1)}, u32[]{:S(2)}, u32[]{:S(2)}) collective-permute-start(bf16[2,528,256]{2,1,0:T(8,128)(2,1)S(1)} %build_factors.5.refs_5_), channel_id=1, source_target_pairs={{0,8},{1,9},{2,10},{3,11},{4,0},{5,1},{6,2},{7,3},{8,12},{9,13},{1... | collective-permute-start | bytes 1622024 | tf_op jit(solution)/shard_map/ppermute | solution.py:695
  58.6 53.4 %copy-start.45 = (s32[8,2048]{1,0:T(8,128)S(1)}, s32[8,2048]{1,0:T(8,128)}, u32[]{:S(2)}) copy-start(s32[8,2048]{1,0:T(8,128)} %param.14) | copy-start | bytes 196612
  62.6 49.5 %copy-start.4 = (bf16[2,528,256]{2,1,0:T(8,128)(2,1)S(1)}, bf16[2,528,256]{2,1,0:T(8,128)(2,1)}, u32[]{:S(2)}) copy-start(bf16[2,528,256]{2,1,0:T(8,128)(2,1)} %copy-done.3) | copy-start | bytes 1622020
  62.6 49.5 %copy-start.6 = (bf16[2,528,256]{2,1,0:T(8,128)(2,1)S(1)}, bf16[2,528,256]{2,1,0:T(8,128)(2,1)}, u32[]{:S(2)}) copy-start(bf16[2,528,256]{2,1,0:T(8,128)(2,1)} %copy-done.5) | copy-start | bytes 1622020
  62.6 30.5 %collective-permute-start.12 = (bf16[2,2,2,256,256]{4,3,2,1,0:T(8,128)(2,1)}, bf16[2,2,2,256,256]{4,3,2,1,0:T(8,128)(2,1)S(1)}, u32[]{:S(2)}, u32[]{:S(2)}) collective-permute-start(bf16[2,2,2,256,256]{4,3,2,1,0:T(8,128)(2,1)} %get-tuple-element.76), channel_id=1, source_target_pairs={{0,2},{1,3},{2,0},{3,1},{4,6},{5,7},{6,4},{7,5},{8,10},{9,11},{10,... | collective-permute-start | bytes 3145736 | tf_op jit(solution)/shard_map/ppermute | solution.py:695
  67.1 25.9 %collective-permute-start.14 = (bf16[528,256]{1,0:T(8,128)(2,1)S(1)}, bf16[528,256]{1,0:T(8,128)(2,1)S(1)}, u32[]{:S(2)}, u32[]{:S(2)}) collective-permute-start(bf16[528,256]{1,0:T(8,128)(2,1)S(1)} %slice_bitcast_fusion.1), channel_id=1, source_target_pairs={{0,4},{1,5},{2,6},{3,7},{4,12},{5,13},{6,14},{7,15},{8,0},{9,1},{1... | collective-permute-start | bytes 811016 | tf_op jit(solution)/shard_map/ppermute | solution.py:695
  86.8 76.3 %copy-start.11 = (bf16[2,512,256]{2,1,0:T(8,128)(2,1)}, bf16[2,512,256]{2,1,0:T(8,128)(2,1)S(1)}, u32[]{:S(2)}) copy-start(bf16[2,512,256]{2,1,0:T(8,128)(2,1)S(1)} %get-tuple-element.89.refs_0_) | copy-start | bytes 1572868
  86.8 76.3 %copy-start.13 = (bf16[2,512,256]{2,1,0:T(8,128)(2,1)}, bf16[2,512,256]{2,1,0:T(8,128)(2,1)S(1)}, u32[]{:S(2)}) copy-start(bf16[2,512,256]{2,1,0:T(8,128)(2,1)S(1)} %get-tuple-element.93.refs_5_) | copy-start | bytes 1572868
  86.8 22.3 %collective-permute-start.23 = (bf16[2,512,256]{2,1,0:T(8,128)(2,1)S(1)}, bf16[2,512,256]{2,1,0:T(8,128)(2,1)S(1)}, u32[]{:S(2)}, u32[]{:S(2)}) collective-permute-start(bf16[2,512,256]{2,1,0:T(8,128)(2,1)S(1)} %get-tuple-element.93.refs_5_), channel_id=1, source_target_pairs={{0,4},{1,5},{2,6},{3,7},{4,12},{5,13},{6,14},{7,15},{8,0},{9,1},{1... | collective-permute-start | bytes 1572872 | tf_op jit(solution)/shard_map/ppermute | solution.py:695
  90.4 26.2 %collective-permute-start.16 = (bf16[2,2,2,256,256]{4,3,2,1,0:T(8,128)(2,1)}, bf16[2,2,2,256,256]{4,3,2,1,0:T(8,128)(2,1)S(1)}, u32[]{:S(2)}, u32[]{:S(2)}) collective-permute-start(bf16[2,2,2,256,256]{4,3,2,1,0:T(8,128)(2,1)} %get-tuple-element.80), channel_id=1, source_target_pairs={{0,3},{1,2},{2,1},{3,0},{4,7},{5,6},{6,5},{7,4},{8,11},{9,10},{10,... | collective-permute-start | bytes 3145736 | tf_op jit(solution)/shard_map/ppermute | solution.py:695
  90.4 26.4 %collective-permute-start.17 = (bf16[2,2,2,256,256]{4,3,2,1,0:T(8,128)(2,1)}, bf16[2,2,2,256,256]{4,3,2,1,0:T(8,128)(2,1)S(1)}, u32[]{:S(2)}, u32[]{:S(2)}) collective-permute-start(bf16[2,2,2,256,256]{4,3,2,1,0:T(8,128)(2,1)} %get-tuple-element.82), channel_id=1, source_target_pairs={{0,1},{1,0},{2,3},{3,2},{4,5},{5,4},{6,7},{7,6},{8,9},{9,8},{10,11... | collective-permute-start | bytes 3145736 | tf_op jit(solution)/shard_map/ppermute | solution.py:695
  93.0 15.6 %collective-permute-start.15 = (bf16[528,256]{1,0:T(8,128)(2,1)S(1)}, bf16[528,256]{1,0:T(8,128)(2,1)S(1)}, u32[]{:S(2)}, u32[]{:S(2)}) collective-permute-start(bf16[528,256]{1,0:T(8,128)(2,1)S(1)} %slice_bitcast_fusion), channel_id=1, source_target_pairs={{0,8},{1,9},{2,10},{3,11},{4,0},{5,1},{6,2},{7,3},{8,12},{9,13},{1... | collective-permute-start | bytes 811016 | tf_op jit(solution)/shard_map/ppermute | solution.py:695
  93.1 49.8 %collective-permute-start.24 = (bf16[2,512,256]{2,1,0:T(8,128)(2,1)S(1)}, bf16[2,512,256]{2,1,0:T(8,128)(2,1)S(1)}, u32[]{:S(2)}, u32[]{:S(2)}) collective-permute-start(bf16[2,512,256]{2,1,0:T(8,128)(2,1)S(1)} %get-tuple-element.93.refs_5_), channel_id=1, source_target_pairs={{0,8},{1,9},{2,10},{3,11},{4,0},{5,1},{6,2},{7,3},{8,12},{9,13},{1... | collective-permute-start | bytes 1572872 | tf_op jit(solution)/shard_map/ppermute | solution.py:695
  108.6 22.6 %collective-permute-start.13 = (bf16[2,512,256]{2,1,0:T(8,128)(2,1)S(1)}, bf16[2,512,256]{2,1,0:T(8,128)(2,1)S(1)}, u32[]{:S(2)}, u32[]{:S(2)}) collective-permute-start(bf16[2,512,256]{2,1,0:T(8,128)(2,1)S(1)} %get-tuple-element.89.refs_0_), channel_id=1, source_target_pairs={{0,4},{1,5},{2,6},{3,7},{4,12},{5,13},{6,14},{7,15},{8,0},{9,1},{1... | collective-permute-start | bytes 1572872 | tf_op jit(solution)/shard_map/ppermute | solution.py:695
  109.1 33.3 %collective-permute-start.20 = (bf16[2,512,256]{2,1,0:T(8,128)(2,1)S(1)}, bf16[2,512,256]{2,1,0:T(8,128)(2,1)S(1)}, u32[]{:S(2)}, u32[]{:S(2)}) collective-permute-start(bf16[2,512,256]{2,1,0:T(8,128)(2,1)S(1)} %get-tuple-element.89.refs_0_), channel_id=1, source_target_pairs={{0,8},{1,9},{2,10},{3,11},{4,0},{5,1},{6,2},{7,3},{8,12},{9,13},{1... | collective-permute-start | bytes 1572872 | tf_op jit(solution)/shard_map/ppermute | solution.py:695
  116.6 46.5 %copy-start.2 = (f32[2,512,128]{2,1,0:T(8,128)}, f32[2,512,128]{2,1,0:T(8,128)S(1)}, u32[]{:S(2)}) copy-start(f32[2,512,128]{2,1,0:T(8,128)S(1)} %get-tuple-element.83.refs_15_.refs_13_) | copy-start | bytes 1572868
  116.6 38.4 %collective-permute-start.25 = (bf16[512,256]{1,0:T(8,128)(2,1)S(1)}, bf16[512,256]{1,0:T(8,128)(2,1)S(1)}, u32[]{:S(2)}, u32[]{:S(2)}) collective-permute-start(bf16[512,256]{1,0:T(8,128)(2,1)S(1)} %slice_bitcast_fusion.5), channel_id=1, source_target_pairs={{0,4},{1,5},{2,6},{3,7},{4,12},{5,13},{6,14},{7,15},{8,0},{9,1},{1... | collective-permute-start | bytes 786440 | tf_op jit(solution)/shard_map/ppermute | solution.py:695
  116.9 38.1 %collective-permute-start.18 = (bf16[2,2,256,256]{3,2,1,0:T(8,128)(2,1)S(1)}, bf16[2,2,256,256]{3,2,1,0:T(8,128)(2,1)S(1)}, u32[]{:S(2)}, u32[]{:S(2)}) collective-permute-start(bf16[2,2,256,256]{3,2,1,0:T(8,128)(2,1)S(1)} %get-tuple-element.85), channel_id=1, source_target_pairs={{0,2},{1,3},{2,0},{3,1},{4,6},{5,7},{6,4},{7,5},{8,10},{9,11},{10,... | collective-permute-start | bytes 1572872 | tf_op jit(solution)/shard_map/ppermute | solution.py:695
  128.5 39.2 %copy-start.27 = (bf16[2,2,256,256]{3,2,1,0:T(8,128)(2,1)}, bf16[2,2,256,256]{3,2,1,0:T(8,128)(2,1)S(1)}, u32[]{:S(2)}) copy-start(bf16[2,2,256,256]{3,2,1,0:T(8,128)(2,1)S(1)} %get-tuple-element.107.refs_3_) | copy-start | bytes 1572868
  131.1 36.6 %copy-start.7 = (bf16[2,512,256]{2,1,0:T(8,128)(2,1)}, bf16[2,512,256]{2,1,0:T(8,128)(2,1)S(1)}, u32[]{:S(2)}) copy-start(bf16[2,512,256]{2,1,0:T(8,128)(2,1)S(1)} %collective-permute-done.13.refs_1_) | copy-start | bytes 1572868
  131.1 23.3 %collective-permute-start.19 = (bf16[2,2,256,256]{3,2,1,0:T(8,128)(2,1)S(1)}, bf16[2,2,256,256]{3,2,1,0:T(8,128)(2,1)S(1)}, u32[]{:S(2)}, u32[]{:S(2)}) collective-permute-start(bf16[2,2,256,256]{3,2,1,0:T(8,128)(2,1)S(1)} %get-tuple-element.87), channel_id=1, source_target_pairs={{0,3},{1,2},{2,1},{3,0},{4,7},{5,6},{6,5},{7,4},{8,11},{9,10},{10,... | collective-permute-start | bytes 1572872 | tf_op jit(solution)/shard_map/ppermute | solution.py:695
  142.4 12.1 %collective-permute-start.21 = (bf16[512,256]{1,0:T(8,128)(2,1)S(1)}, bf16[512,256]{1,0:T(8,128)(2,1)S(1)}, u32[]{:S(2)}, u32[]{:S(2)}) collective-permute-start(bf16[512,256]{1,0:T(8,128)(2,1)S(1)} %slice_bitcast_fusion.7), channel_id=1, source_target_pairs={{0,4},{1,5},{2,6},{3,7},{4,12},{5,13},{6,14},{7,15},{8,0},{9,1},{1... | collective-permute-start | bytes 786440 | tf_op jit(solution)/shard_map/ppermute | solution.py:695
  142.9 16.3 %collective-permute-start.22 = (bf16[512,256]{1,0:T(8,128)(2,1)S(1)}, bf16[512,256]{1,0:T(8,128)(2,1)S(1)}, u32[]{:S(2)}, u32[]{:S(2)}) collective-permute-start(bf16[512,256]{1,0:T(8,128)(2,1)S(1)} %slice_bitcast_fusion.6), channel_id=1, source_target_pairs={{0,8},{1,9},{2,10},{3,11},{4,0},{5,1},{6,2},{7,3},{8,12},{9,13},{1... | collective-permute-start | bytes 786440 | tf_op jit(solution)/shard_map/ppermute | solution.py:695
  154.4 8.6 %collective-permute-start.26 = (bf16[512,256]{1,0:T(8,128)(2,1)S(1)}, bf16[512,256]{1,0:T(8,128)(2,1)S(1)}, u32[]{:S(2)}, u32[]{:S(2)}) collective-permute-start(bf16[512,256]{1,0:T(8,128)(2,1)S(1)} %slice_bitcast_fusion.4), channel_id=1, source_target_pairs={{0,8},{1,9},{2,10},{3,11},{4,0},{5,1},{6,2},{7,3},{8,12},{9,13},{1... | collective-permute-start | bytes 786440 | tf_op jit(solution)/shard_map/ppermute | solution.py:695
  155.0 27.8 %collective-permute-start.28 = (bf16[2,2,256,256]{3,2,1,0:T(8,128)(2,1)}, bf16[2,2,256,256]{3,2,1,0:T(8,128)(2,1)}, u32[]{:S(2)}, u32[]{:S(2)}) collective-permute-start(bf16[2,2,256,256]{3,2,1,0:T(8,128)(2,1)} %get-tuple-element.101), channel_id=1, source_target_pairs={{0,1},{1,0},{2,3},{3,2},{4,5},{5,4},{6,7},{7,6},{8,9},{9,8},{10,11... | collective-permute-start | bytes 1572872 | tf_op jit(solution)/shard_map/ppermute | solution.py:695
  167.8 22.9 %collective-permute-start.27 = (bf16[2,2,256,256]{3,2,1,0:T(8,128)(2,1)}, bf16[2,2,256,256]{3,2,1,0:T(8,128)(2,1)S(1)}, u32[]{:S(2)}, u32[]{:S(2)}) collective-permute-start(bf16[2,2,256,256]{3,2,1,0:T(8,128)(2,1)} %get-tuple-element.96), channel_id=1, source_target_pairs={{0,2},{1,3},{2,0},{3,1},{4,6},{5,7},{6,4},{7,5},{8,10},{9,11},{10,... | collective-permute-start | bytes 1572872 | tf_op jit(solution)/shard_map/ppermute | solution.py:695
  182.8 18.4 %collective-permute-start.29 = (bf16[2,2,256,256]{3,2,1,0:T(8,128)(2,1)S(1)}, bf16[2,2,256,256]{3,2,1,0:T(8,128)(2,1)S(1)}, u32[]{:S(2)}, u32[]{:S(2)}) collective-permute-start(bf16[2,2,256,256]{3,2,1,0:T(8,128)(2,1)S(1)} %get-tuple-element.102), channel_id=1, source_target_pairs={{0,3},{1,2},{2,1},{3,0},{4,7},{5,6},{6,5},{7,4},{8,11},{9,10},{10,... | collective-permute-start | bytes 1572872 | tf_op jit(solution)/shard_map/ppermute | solution.py:695
  182.9 14.2 %collective-permute-start.33 = (f32[2,128]{1,0:T(2,128)S(1)}, f32[2,128]{1,0:T(2,128)S(1)}, u32[]{:S(2)}, u32[]{:S(2)}) collective-permute-start(f32[2,128]{1,0:T(2,128)S(1)} %get-tuple-element.115), channel_id=1, source_target_pairs={{0,4},{1,5},{2,6},{3,7},{4,12},{5,13},{6,14},{7,15},{8,0},{9,1},{1... | collective-permute-start | bytes 3080 | tf_op jit(solution)/shard_map/ppermute | solution.py:695
  184.8 12.4 %collective-permute-start.31 = (f32[2,128]{1,0:T(2,128)S(1)}, f32[2,128]{1,0:T(2,128)S(1)}, u32[]{:S(2)}, u32[]{:S(2)}) collective-permute-start(f32[2,128]{1,0:T(2,128)S(1)} %get-tuple-element.109), channel_id=1, source_target_pairs={{0,12},{1,13},{2,14},{3,15},{4,8},{5,9},{6,10},{7,11},{8,4},{9,5},... | collective-permute-start | bytes 3080 | tf_op jit(solution)/shard_map/ppermute | solution.py:695
  190.0 9.1 %collective-permute-start.30 = (bf16[2,2,256,256]{3,2,1,0:T(8,128)(2,1)S(1)}, bf16[2,2,256,256]{3,2,1,0:T(8,128)(2,1)S(1)}, u32[]{:S(2)}, u32[]{:S(2)}) collective-permute-start(bf16[2,2,256,256]{3,2,1,0:T(8,128)(2,1)S(1)} %get-tuple-element.104), channel_id=1, source_target_pairs={{0,1},{1,0},{2,3},{3,2},{4,5},{5,4},{6,7},{7,6},{8,9},{9,8},{10,11... | collective-permute-start | bytes 1572872 | tf_op jit(solution)/shard_map/ppermute | solution.py:695
  190.7 6.4 %collective-permute-start.32 = (f32[2,128]{1,0:T(2,128)S(1)}, f32[2,128]{1,0:T(2,128)S(1)}, u32[]{:S(2)}, u32[]{:S(2)}) collective-permute-start(f32[2,128]{1,0:T(2,128)S(1)} %get-tuple-element.110), channel_id=1, source_target_pairs={{0,8},{1,9},{2,10},{3,11},{4,0},{5,1},{6,2},{7,3},{8,12},{9,13},{1... | collective-permute-start | bytes 3080 | tf_op jit(solution)/shard_map/ppermute | solution.py:695
  197.2 6.1 %collective-permute-start.36 = (f32[2,32]{1,0:T(2,128)S(1)}, f32[2,32]{1,0:T(2,128)S(1)}, u32[]{:S(2)}, u32[]{:S(2)}) collective-permute-start(f32[2,32]{1,0:T(2,128)S(1)} %get-tuple-element.113), channel_id=1, source_target_pairs={{0,3},{1,2},{2,1},{3,0},{4,7},{5,6},{6,5},{7,4},{8,11},{9,10},{10,... | collective-permute-start | bytes 776 | tf_op jit(solution)/shard_map/ppermute | solution.py:695
  197.5 5.8 %collective-permute-start.35 = (f32[2,32]{1,0:T(2,128)S(1)}, f32[2,32]{1,0:T(2,128)S(1)}, u32[]{:S(2)}, u32[]{:S(2)}) collective-permute-start(f32[2,32]{1,0:T(2,128)S(1)} %get-tuple-element.112), channel_id=1, source_target_pairs={{0,2},{1,3},{2,0},{3,1},{4,6},{5,7},{6,4},{7,5},{8,10},{9,11},{10,... | collective-permute-start | bytes 776 | tf_op jit(solution)/shard_map/ppermute | solution.py:695
  198.7 4.7 %collective-permute-start.34 = (f32[2,32]{1,0:T(2,128)S(1)}, f32[2,32]{1,0:T(2,128)S(1)}, u32[]{:S(2)}, u32[]{:S(2)}) collective-permute-start(f32[2,32]{1,0:T(2,128)S(1)} %get-tuple-element.111), channel_id=1, source_target_pairs={{0,1},{1,0},{2,3},{3,2},{4,5},{5,4},{6,7},{7,6},{8,9},{9,8},{10,11... | collective-permute-start | bytes 776 | tf_op jit(solution)/shard_map/ppermute | solution.py:695
  (36 other events, 352.4 us)

commit v9 on v7

--- a/solution.py
+++ b/solution.py
@@ -132,6 +132,10 @@
 BRIGHT_ROWS = 16
 
 
+def full(array):
+    return pl.BlockSpec(array.shape, lambda *_: (0,) * array.ndim)
+
+
 def build_factors(
     slot_ids, table, beam, messages, antenna_uvw, smalls, pieces, span, bright_rows, small_width
 ):
@@ -152,7 +156,7 @@
         if at == len(operands):
             operands += small if isinstance(small, tuple) else [small]
         sets.append((per_group, n, at))
-    in_specs += [whole] * (len(operands) - len(in_specs))
+    in_specs += [full(array) for array in operands[len(in_specs) :]]
     in_specs.append(pl.BlockSpec((1, 3, antennas), lambda n, tab: (tab[0] + index, 0, 0)))
     count = beams * per_group
     shapes = [
@@ -219,7 +223,7 @@
                 )
                 for m in others
             ]
-            + [whole for _ in smalls],
+            + [full(array) for array in smalls],
             out_specs=[whole for _ in others],
             scratch_shapes=scratch,
         ),
@@ -323,11 +327,8 @@
         return lax.dot_general(a, b, (((1,), (0,)), ((), ())), preferred_element_type=jnp.float32)
 
     def scaled_of(re, im):
-        column = jnp.concatenate([columns_ref[index]] * (span // 128), 1)
-        return (
-            (re.astype(jnp.float32) * column).astype(jnp.bfloat16),
-            (im.astype(jnp.float32) * column).astype(jnp.bfloat16),
-        )
+        column = jnp.concatenate([columns_ref[index].astype(jnp.bfloat16)] * (span // 128), 1)
+        return re * column, im * column
 
     def outer(a, b):
         row_ids = lax.broadcasted_iota(jnp.int32, a.shape, 0)
@@ -432,7 +433,6 @@
     slots = keep.shape[0]
     sources = sum(number for _, _, number in pieces[0])
     count = units_dev * len(vis)
-    whole = pl.BlockSpec(memory_space=pltpu.VMEM)
     arrays = [array for piece in pieces for entry, _, _ in piece for array in entry]
 
     def at(tab, step, column):
@@ -441,7 +441,7 @@
     def unit(step, home):
         return jnp.clip(step - home * units_dev, 0, units_dev - 1)
 
-    in_specs = [whole] * len(arrays)
+    in_specs = [full(array) for array in arrays]
     for home, array in enumerate(vis):
         if array.shape[1] == slots:
             slot = lambda tab: tab[0] + index
@@ -463,7 +463,7 @@
         first = pieces[0][0]
         bright_at = (first[0][0].shape[1] - BRIGHT_ROWS) // first[2]
     else:
-        in_specs.append(whole)
+        in_specs.append(full(bright))
         operands.append(bright)
     out_specs = [
         pl.BlockSpec((1, 2, span, span), lambda u, tab, home=home: (unit(u, home), 0, 0, 0))
@@ -508,9 +508,8 @@
 
 def put_residuals(sources, arrays, offset, table, shape, residual):
     span = shape[-1]
-    whole = pl.BlockSpec(memory_space=pltpu.VMEM)
     operands = [table, *arrays]
-    in_specs = [whole] * len(arrays)
+    in_specs = [full(array) for array in arrays]
     aliases = {}
     if residual is not None:
         aliases = {len(operands): 0}
@@ -642,36 +641,38 @@
 WORK, HOME, PUT, LATER_WORK, LATER_HOME, PUT_NEAR, PUT_LAST = 32, 35, 38, 40, 43, 46, 47
 SUM_PLANES, SUM_PLANE = 48, 51
 GATES = {
-    1: (0,),
     3: (0, 1),
-    5: (0, 2, 13),
-    6: (1, 2, 11),
+    5: (0, 2),
+    6: (1, 11),
     7: (1, 2),
-    14: (13,),
-    16: (2,),
+    14: (11, 13),
     17: (1,),
-    19: (18,),
-    20: (3, 4, 6, 7, 17),
+    19: (2, 18),
+    20: (3, 4, 7, 16, 17),
     21: (3, 4, 5, 13, 14, 16, 17),
-    23: (4, 17),
-    24: (6, 9, 17),
-    25: (6, 9, 17, 23),
+    23: (17, 4),
+    24: (9, 17),
+    25: (9, 23, 6, 17),
     26: (9,),
     27: (8,),
     28: (22,),
-    31: (25, 27),
-    33: (23, 32),
-    34: (33,),
-    35: (8, 9, 24, 25),
-    40: (28, 34, 36, 37),
+    31: (25, 26, 27, 37),
+    33: (32, 25, 23),
+    35: (8, 9, 22, 24, 25, 26, 28, 29),
+    40: (33, 36, 37, 28, 29, 30, 31),
+    49: (44,),
+    53: (35,),
+    46: (30, 31),
+    37: (32, 9),
+    38: (25,),
+    30: (26,),
+    43: (32,),
+    44: (26, 27, 30, 31),
+    36: (8, 9),
+    4: (0,),
+    16: (0,),
+    13: (0,),
     41: (40,),
-    42: (29, 41),
-    43: (41,),
-    45: (28, 32),
-    48: (35,),
-    49: (44,),
-    51: (34,),
-    52: (38,),
 }
 
 
@@ -754,7 +755,7 @@
 
     def work(index, step, home_step, ready, bright):
         arrived, total = [], None
-        for n, homes in enumerate([routes.order[:1], routes.order[1:2], routes.order[2:]]):
+        for n, homes in enumerate([routes.order[:1], routes.order[1:]]):
             made = unit_work(
                 index,
                 routes.steps[index] + len(arrived) * routes.steps_per_home,

time: 202 us -> 206 us (1.020)
  starting transfers between devices: 51.3 us -> 66.2 us
  Pallas kernels: 60.7 us -> 55.9 us
  waiting for transfers between devices: 64.7 us -> 60.6 us
  local copies, waits for them, and re-layouts: 21.2 us -> 19 us
    ppermute x37, starting transfers between devices: 51.3 us -> 66.2 us  [send(): done[step] = lax.ppermute(gated(step, value), 'tile', pairs)]
    pallas_call x6 -> x4, Pallas kernels: 33.3 us -> 28.5 us  [unit_work(): pl.pallas_call(functools.partial(unit_kernel, index, offset, kinds, brigh...]
    ppermute x37, waiting for transfers between devices: 64.7 us -> 60.6 us  [send(): done[step] = lax.ppermute(gated(step, value), 'tile', pairs)]
    unnamed x97 -> x87, local copies, waits for them, and re-layouts: 15.5 us -> 15 us
  transfers between devices with their start and end apart: 37 -> 37, of which waited for: 12 -> 13; matrix products, arithmetic and copies ran while one was open for 3% -> 2% of each run, Pallas kernels for 28% -> 23%
where the time goes in v9:
time: 206 us; the launch traced here: 205 us
  starting transfers between devices  66.2 us (32%)
  waiting for transfers between devices  60.6 us (29%)
  Pallas kernels  55.9 us (27%)
  local copies, waits for them, and re-layouts  19 us (9%)
  other arithmetic  2.2 us (1%)
    ppermute x37, starting transfers between devices, send(): done[step] = lax.ppermute(gated(step, value), 'tile', pairs)  66.2 us
    ppermute x37, waiting for transfers between devices, send(): done[step] = lax.ppermute(gated(step, value), 'tile', pairs)  60.6 us
    pallas_call x4, Pallas kernels, unit_work(): pl.pallas_call(functools.partial(unit_kernel, index, offset, kinds, brigh...  28.5 us
    unnamed x87, local copies, waits for them, and re-layouts  15 us
    pallas_call x3, Pallas kernels, put_residuals(): pl.pallas_call(functools.partial(put_kernel, sources), grid_spec=pltpu.Pr...  8.94 us
    pallas_call x3, Pallas kernels, messages_for(): pl.pallas_call(functools.partial(message_kernel, len(others), bool(smalls...  7.7 us
    pallas_call x3, Pallas kernels, build_factors(): pl.pallas_call(functools.partial(build_kernel, sets, slot_ids, pieces, br...  6.75 us
  transfers between devices with their start and end apart: 37, of which 13 were waited for; matrix products, arithmetic and copies ran while one was open for 2% of the time, Pallas kernels for 23%

profile of v9, /device:TPU:0, one launch (start us, length us, event | category | flops | bytes accessed | tf_op | source)
XLA Modules:
  0.0 204.9 jit_solution(4719003528776039522)
XLA Ops:
  0.6 1.4 broadcast_in_dim.34
  2.0 1.3 constant_dynamic-slice_fusion
  3.3 2.4 %messages_for.3 = bf16[80,2048]{1,0:T(8,128)(2,1)} custom-call(s32[148]{0:T(256)} %bitcast.24, bf16[8,2,32,2048]{3,2,1,0:T(8,128)(2,1)} %refs_0_.11, f32[2,256]{1,0:T(2,128)} %refs_4_.5, f32[1,256]{1,0:T(1,128)} %bitcast.38, s32[8,32]{1,0:T(8,128)} %refs_6_.1), custom_call_target="tpu_custom_call" | custom-call | flops 1 | bytes 1 | tf_op jit(solution)/shard_map/messages_for/pallas_call | solution.py:215
  6.1 1.1 copy.15.refs_5_.refs_2_.refs_10_
  10.3 1.6 build_factors.3.refs_0_
  12.7 2.9 %collective-permute-start.1 = (bf16[2,528,256]{2,1,0:T(8,128)(2,1)S(1)}, bf16[2,528,256]{2,1,0:T(8,128)(2,1)S(1)}, u32[]{:S(2)}, u32[]{:S(2)}) collective-permute-start(bf16[2,528,256]{2,1,0:T(8,128)(2,1)S(1)} %build_factors.3.refs_0_), channel_id=1, source_target_pairs={{0,4},{1,5},{2,6},{3,7},{4,12},{5,13},{6,14},{7,15},{8,0},{9,1},{1... | collective-permute-start | bytes 1622024 | tf_op jit(solution)/shard_map/ppermute | solution.py:695
  15.6 2.6 %messages_for.4 = (bf16[80,2048]{1,0:T(8,128)(2,1)}, bf16[80,2048]{1,0:T(8,128)(2,1)}) custom-call(s32[148]{0:T(256)} %bitcast.25, bf16[8,2,32,2048]{3,2,1,0:T(8,128)(2,1)} %refs_0_.11, bf16[8,2,32,2048]{3,2,1,0:T(8,128)(2,1)} %refs_0_.11, f32[2,256]{1,0:T(2,128)} %refs_4_.5, f32[1,256]{1,0:T(1,128)} %bitcast.39, s32[8,32]{1,0:T(8,128)} %refs_6_.1), custom_call_target="tpu_custom_call" | custom-call | flops 1 | bytes 1 | tf_op jit(solution)/shard_map/messages_for/pallas_call | solution.py:215
  18.2 1.5 collective-permute-start.5
  19.7 1.3 collective-permute-start.2
  21.1 2.7 %messages_for.5 = (bf16[64,2048]{1,0:T(8,128)(2,1)}, bf16[64,2048]{1,0:T(8,128)(2,1)}, bf16[64,2048]{1,0:T(8,128)(2,1)}) custom-call(s32[148]{0:T(256)} %bitcast.26, bf16[8,2,32,2048]{3,2,1,0:T(8,128)(2,1)} %refs_0_.11, bf16[8,2,32,2048]{3,2,1,0:T(8,128)(2,1)} %refs_0_.11, bf16[8,2,32,2048]{3,2,1,0:T(8,128)(2,1)} %refs_0_.11), custom_call_target="tpu_custom_call" | custom-call | flops 1 | bytes 1 | tf_op jit(solution)/shard_map/messages_for/pallas_call | solution.py:215
  23.8 4.9 %collective-permute-done.5.refs_0_.refs_8_ = bf16[80,2048]{1,0:T(8,128)(2,1)S(1)} collective-permute-done((bf16[80,2048]{1,0:T(8,128)(2,1)}, bf16[80,2048]{1,0:T(8,128)(2,1)S(1)}, u32[]{:S(2)}, u32[]{:S(2)}) %collective-permute-start.5) | collective-permute-done | bytes 327712 | tf_op jit(solution)/shard_map/ppermute | solution.py:695
  30.1 12.4 %collective-permute-start.3 = (bf16[528,256]{1,0:T(8,128)(2,1)}, bf16[528,256]{1,0:T(8,128)(2,1)}, u32[]{:S(2)}, u32[]{:S(2)}) collective-permute-start(bf16[528,256]{1,0:T(8,128)(2,1)} %slice_bitcast_fusion.3), channel_id=1, source_target_pairs={{0,4},{1,5},{2,6},{3,7},{4,12},{5,13},{6,14},{7,15},{8,0},{9,1},{1... | collective-permute-start | bytes 811016 | tf_op jit(solution)/shard_map/ppermute | solution.py:695
  44.1 1.6 collective-permute-start.13
  45.7 1.6 build_factors.4.refs_5_
  48.8 2.5 %collective-permute-start.8 = (bf16[2,528,256]{2,1,0:T(8,128)(2,1)S(1)}, bf16[2,528,256]{2,1,0:T(8,128)(2,1)}, u32[]{:S(2)}, u32[]{:S(2)}) collective-permute-start(bf16[2,528,256]{2,1,0:T(8,128)(2,1)S(1)} %build_factors.4.refs_5_), channel_id=1, source_target_pairs={{0,8},{1,9},{2,10},{3,11},{4,0},{5,1},{6,2},{7,3},{8,12},{9,13},{1... | collective-permute-start | bytes 1622024 | tf_op jit(solution)/shard_map/ppermute | solution.py:695
  51.3 4.0 %slices_for.1 = (bf16[2,2,2,256,256]{4,3,2,1,0:T(8,128)(2,1)}, bf16[2,2,2,256,256]{4,3,2,1,0:T(8,128)(2,1)}, bf16[2,2,2,256,256]{4,3,2,1,0:T(8,128)(2,1)}) custom-call(s32[148]{0:T(256)} %bitcast.27, bf16[2,8,2,256,256]{4,3,2,1,0:T(8,128)(2,1)} %refs_12_.3, bf16[2,8,2,256,256]{4,3,2,1,0:T(8,128)(2,1)} %refs_12_.3, bf16[2,8,2,256,256]{4,3,2,1,0:T(8,128)(2,1)} %refs_12_.3), custom_call_target="tpu_custom_call" | custom-call | flops 1 | bytes 1 | tf_op jit(solution)/shard_map/slices_for/pallas_call | solution.py:246
  56.8 8.6 %collective-permute-done.8.refs_7_ = bf16[2,528,256]{2,1,0:T(8,128)(2,1)} collective-permute-done((bf16[2,528,256]{2,1,0:T(8,128)(2,1)S(1)}, bf16[2,528,256]{2,1,0:T(8,128)(2,1)}, u32[]{:S(2)}, u32[]{:S(2)}) %collective-permute-start.8) | collective-permute-done | bytes 540704 | tf_op jit(solution)/shard_map/ppermute | solution.py:695
  66.3 12.4 %collective-permute-start.10 = (bf16[528,256]{1,0:T(8,128)(2,1)S(1)}, bf16[528,256]{1,0:T(8,128)(2,1)S(1)}, u32[]{:S(2)}, u32[]{:S(2)}) collective-permute-start(bf16[528,256]{1,0:T(8,128)(2,1)S(1)} %slice_bitcast_fusion), channel_id=1, source_target_pairs={{0,8},{1,9},{2,10},{3,11},{4,0},{5,1},{6,2},{7,3},{8,12},{9,13},{1... | collective-permute-start | bytes 811016 | tf_op jit(solution)/shard_map/ppermute | solution.py:695
  78.7 3.2 %collective-permute-done.7.refs_6_ = bf16[2,528,256]{2,1,0:T(8,128)(2,1)S(1)} collective-permute-done((bf16[2,528,256]{2,1,0:T(8,128)(2,1)S(1)}, bf16[2,528,256]{2,1,0:T(8,128)(2,1)S(1)}, u32[]{:S(2)}, u32[]{:S(2)}) %collective-permute-start.7) | collective-permute-done | bytes 540704 | tf_op jit(solution)/shard_map/ppermute | solution.py:695
  81.9 3.2 %collective-permute-start.9 = (bf16[528,256]{1,0:T(8,128)(2,1)S(1)}, bf16[528,256]{1,0:T(8,128)(2,1)S(1)}, u32[]{:S(2)}, u32[]{:S(2)}) collective-permute-start(bf16[528,256]{1,0:T(8,128)(2,1)S(1)} %slice_bitcast_fusion.1), channel_id=1, source_target_pairs={{0,4},{1,5},{2,6},{3,7},{4,12},{5,13},{6,14},{7,15},{8,0},{9,1},{1... | collective-permute-start | bytes 811016 | tf_op jit(solution)/shard_map/ppermute | solution.py:695
  89.0 3.5 %build_factors.5 = (bf16[2,512,256]{2,1,0:T(8,128)(2,1)S(1)}, bf16[2,512,256]{2,1,0:T(8,128)(2,1)S(1)}) custom-call(s32[148]{0:T(256)S(1)} %bitcast.30, bf16[8,2,32,2048]{3,2,1,0:T(8,128)(2,1)S(1)} %copy-done.1, bf16[64,2048]{1,0:T(8,128)(2,1)} %collective-permute-done.12.refs_1_, bf16[64,2048]{1,0:T(8,128)(2,1)} %collective-permute-done.13.refs_2_, ...), custom_call_target="tpu_custom_call" | custom-call | flops 1 | bytes 1 | tf_op jit(solution)/shard_map/build_factors/pallas_call | solution.py:165
  92.6 3.7 %collective-permute-start.20 = (bf16[2,512,256]{2,1,0:T(8,128)(2,1)S(1)}, bf16[2,512,256]{2,1,0:T(8,128)(2,1)S(1)}, u32[]{:S(2)}, u32[]{:S(2)}) collective-permute-start(bf16[2,512,256]{2,1,0:T(8,128)(2,1)S(1)} %get-tuple-element.88.refs_0_), channel_id=1, source_target_pairs={{0,4},{1,5},{2,6},{3,7},{4,12},{5,13},{6,14},{7,15},{8,0},{9,1},{1... | collective-permute-start | bytes 1572872 | tf_op jit(solution)/shard_map/ppermute | solution.py:695
  96.3 2.0 collective-permute-start.23
  98.3 4.5 %unit_work.4 = (bf16[2,2,256,256]{3,2,1,0:T(8,128)(2,1)S(1)}, f32[1,512]{1,0:T(1,128)S(1)}, f32[2,512,128]{2,1,0:T(8,128)S(1)}) custom-call(s32[148]{0:T(256)S(1)} %bitcast.31, bf16[2,528,256]{2,1,0:T(8,128)(2,1)S(1)} %build_factors.3.refs_0_, bf16[2,528,256]{2,1,0:T(8,128)(2,1)S(1)} %copy-done.4, bf16[2,528,256]{2,1,0:T(8,128)(2,1)S(1)} %copy-done.6, ...), custom_call_target="tpu_custom_call" | custom-call | flops 1 | bytes 1 | tf_op jit(solution)/shard_map/unit_work/pallas_call | solution.py:479
  102.9 16.6 %collective-permute-done.20.refs_1_ = bf16[2,512,256]{2,1,0:T(8,128)(2,1)S(1)} collective-permute-done((bf16[2,512,256]{2,1,0:T(8,128)(2,1)S(1)}, bf16[2,512,256]{2,1,0:T(8,128)(2,1)S(1)}, u32[]{:S(2)}, u32[]{:S(2)}) %collective-permute-start.20) | collective-permute-done | bytes 524320 | tf_op jit(solution)/shard_map/ppermute | solution.py:695
  119.9 1.4 collective-permute-start.18
  121.3 2.0 collective-permute-start.21
  124.3 10.1 %unit_work.5 = (bf16[2,2,256,256]{3,2,1,0:T(8,128)(2,1)S(1)}, bf16[2,2,256,256]{3,2,1,0:T(8,128)(2,1)}, bf16[2,2,256,256]{3,2,1,0:T(8,128)(2,1)S(1)}, f32[1,512]{1,0:T(1,128)S(1)}) custom-call(s32[148]{0:T(256)S(1)} %bitcast.32, bf16[2,528,256]{2,1,0:T(8,128)(2,1)S(1)} %build_factors.3.refs_0_, bf16[2,528,256]{2,1,0:T(8,128)(2,1)S(1)} %copy-done.4, ...), custom_call_target="tpu_custom_call" | custom-call | flops 1 | bytes 1 | tf_op jit(solution)/shard_map/unit_work/pallas_call | solution.py:479
  134.4 4.1 %collective-permute-done.23.refs_6_ = bf16[2,512,256]{2,1,0:T(8,128)(2,1)S(1)} collective-permute-done((bf16[2,512,256]{2,1,0:T(8,128)(2,1)S(1)}, bf16[2,512,256]{2,1,0:T(8,128)(2,1)S(1)}, u32[]{:S(2)}, u32[]{:S(2)}) %collective-permute-start.23) | collective-permute-done | bytes 524320 | tf_op jit(solution)/shard_map/ppermute | solution.py:695
  138.5 3.8 %collective-permute-done.25.refs_7_ = bf16[2,512,256]{2,1,0:T(8,128)(2,1)S(1)} collective-permute-done((bf16[2,512,256]{2,1,0:T(8,128)(2,1)S(1)}, bf16[2,512,256]{2,1,0:T(8,128)(2,1)S(1)}, u32[]{:S(2)}, u32[]{:S(2)}) %collective-permute-start.25) | collective-permute-done | bytes 524320 | tf_op jit(solution)/shard_map/ppermute | solution.py:695
  142.3 1.8 collective-permute-start.24
  144.1 3.3 %collective-permute-done.19.refs_1_ = bf16[2,2,256,256]{3,2,1,0:T(8,128)(2,1)S(1)} collective-permute-done((bf16[2,2,256,256]{3,2,1,0:T(8,128)(2,1)S(1)}, bf16[2,2,256,256]{3,2,1,0:T(8,128)(2,1)S(1)}, u32[]{:S(2)}, u32[]{:S(2)}) %collective-permute-start.19) | collective-permute-done | bytes 524320 | tf_op jit(solution)/shard_map/ppermute | solution.py:695
  147.4 2.0 collective-permute-start.26
  149.4 2.3 %collective-permute-done.22.refs_4_ = bf16[512,256]{1,0:T(8,128)(2,1)S(1)} collective-permute-done((bf16[512,256]{1,0:T(8,128)(2,1)S(1)}, bf16[512,256]{1,0:T(8,128)(2,1)S(1)}, u32[]{:S(2)}, u32[]{:S(2)}) %collective-permute-start.22) | collective-permute-done | bytes 262176 | tf_op jit(solution)/shard_map/ppermute | solution.py:695
  151.8 6.7 %collective-permute-done.24.refs_8_ = bf16[512,256]{1,0:T(8,128)(2,1)S(1)} collective-permute-done((bf16[512,256]{1,0:T(8,128)(2,1)S(1)}, bf16[512,256]{1,0:T(8,128)(2,1)S(1)}, u32[]{:S(2)}, u32[]{:S(2)}) %collective-permute-start.24) | collective-permute-done | bytes 262176 | tf_op jit(solution)/shard_map/ppermute | solution.py:695
  158.5 5.6 %collective-permute-done.26.refs_9_ = bf16[512,256]{1,0:T(8,128)(2,1)S(1)} collective-permute-done((bf16[512,256]{1,0:T(8,128)(2,1)S(1)}, bf16[512,256]{1,0:T(8,128)(2,1)S(1)}, u32[]{:S(2)}, u32[]{:S(2)}) %collective-permute-start.26) | collective-permute-done | bytes 262176 | tf_op jit(solution)/shard_map/ppermute | solution.py:695
  164.1 4.7 %unit_work.6 = (bf16[2,2,256,256]{3,2,1,0:T(8,128)(2,1)}, f32[1,512]{1,0:T(1,128)S(1)}) custom-call(s32[148]{0:T(256)S(1)} %bitcast.33, bf16[2,512,256]{2,1,0:T(8,128)(2,1)S(1)} %get-tuple-element.88.refs_0_, bf16[2,512,256]{2,1,0:T(8,128)(2,1)S(1)} %collective-permute-done.20.refs_1_, bf16[2,512,256]{2,1,0:T(8,128)(2,1)S(1)} %collective-permute-done.15.refs_2_, ...), custom_call_target="tpu_custom_call" | custom-call | flops 1 | bytes 1 | tf_op jit(solution)/shard_map/unit_work/pallas_call | solution.py:479
  170.9 1.0 copy-done.10
  171.9 1.0 copy-done.12
  174.0 9.2 %unit_work.7 = (bf16[2,2,256,256]{3,2,1,0:T(8,128)(2,1)S(1)}, bf16[2,2,256,256]{3,2,1,0:T(8,128)(2,1)S(1)}, bf16[2,2,256,256]{3,2,1,0:T(8,128)(2,1)S(1)}, f32[1,512]{1,0:T(1,128)S(1)}) custom-call(s32[148]{0:T(256)S(1)} %bitcast.34, bf16[2,512,256]{2,1,0:T(8,128)(2,1)S(1)} %copy-done.12, bf16[2,512,256]{2,1,0:T(8,128)(2,1)S(1)} %collective-permute-done.20.refs_1_, ...), custom_call_target="tpu_custom_call" | custom-call | flops 1 | bytes 1 | tf_op jit(solution)/shard_map/unit_work/pallas_call | solution.py:479
  183.2 1.3 collective-permute-start.28
  184.6 1.9 collective-permute-start.33
  186.5 4.7 %collective-permute-start.31 = (f32[2,128]{1,0:T(2,128)S(1)}, f32[2,128]{1,0:T(2,128)S(1)}, u32[]{:S(2)}, u32[]{:S(2)}) collective-permute-start(f32[2,128]{1,0:T(2,128)S(1)} %get-tuple-element.112), channel_id=1, source_target_pairs={{0,12},{1,13},{2,14},{3,15},{4,8},{5,9},{6,10},{7,11},{8,4},{9,5},... | collective-permute-start | bytes 3080 | tf_op jit(solution)/shard_map/ppermute | solution.py:695
  191.2 1.9 collective-permute-start.32
  193.2 4.7 %put_residuals.3.refs_2_ = bf16[2,8,2,256,256]{4,3,2,1,0:T(8,128)(2,1)} custom-call(s32[148]{0:T(256)S(1)} %bitcast.35, bf16[2,2,256,256]{3,2,1,0:T(8,128)(2,1)S(1)} %copy-done.22, bf16[2,2,256,256]{3,2,1,0:T(8,128)(2,1)S(1)} %copy-done.26, bf16[2,2,256,256]{3,2,1,0:T(8,128)(2,1)} %collective-permute-done.30.refs_2_, bf16[2,2,256,256]{3,2,1,0:T(8,128)(2,1)S(1)} %copy-done.24), custom_call_target="tpu_custom_call" | custom-call | flops 1 | bytes 1 | tf_op jit(solution)/shard_map/put_residuals/pallas_call | solution.py:518
  198.0 1.2 collective-permute-start.35
  199.9 2.1 %put_residuals.4.refs_2_ = bf16[2,8,2,256,256]{4,3,2,1,0:T(8,128)(2,1)} custom-call(s32[148]{0:T(256)S(1)} %bitcast.36, bf16[2,2,256,256]{3,2,1,0:T(8,128)(2,1)S(1)} %collective-permute-done.29.refs_0_, bf16[2,2,256,256]{3,2,1,0:T(8,128)(2,1)S(1)} %get-tuple-element.104.refs_1_, ...), custom_call_target="tpu_custom_call", output_to_operand_aliasing={{}: (3, {})} | custom-call | flops 1 | bytes 1 | tf_op jit(solution)/shard_map/put_residuals/pallas_call | solution.py:518
  202.0 2.1 %put_residuals.5 = bf16[2,8,2,256,256]{4,3,2,1,0:T(8,128)(2,1)} custom-call(s32[148]{0:T(256)S(1)} %bitcast.37, bf16[2,2,256,256]{3,2,1,0:T(8,128)(2,1)S(1)} %collective-permute-done.27.refs_0_, bf16[2,2,256,256]{3,2,1,0:T(8,128)(2,1)S(1)} %collective-permute-done.28.refs_1_, ...), custom_call_target="tpu_custom_call", output_to_operand_aliasing={{}: (3, {})} | custom-call | flops 1 | bytes 1 | tf_op jit(solution)/shard_map/put_residuals/pallas_call | solution.py:518
  (149 shorter events, 21.2 us)
Async XLA Ops:
  5.7 1.9 collective-permute-start
  12.7 16.6 %collective-permute-start.1 = (bf16[2,528,256]{2,1,0:T(8,128)(2,1)S(1)}, bf16[2,528,256]{2,1,0:T(8,128)(2,1)S(1)}, u32[]{:S(2)}, u32[]{:S(2)}) collective-permute-start(bf16[2,528,256]{2,1,0:T(8,128)(2,1)S(1)} %build_factors.3.refs_0_), channel_id=1, source_target_pairs={{0,4},{1,5},{2,6},{3,7},{4,12},{5,13},{6,14},{7,15},{8,0},{9,1},{1... | collective-permute-start | bytes 1622024 | tf_op jit(solution)/shard_map/ppermute | solution.py:695
  18.2 10.5 %collective-permute-start.5 = (bf16[80,2048]{1,0:T(8,128)(2,1)}, bf16[80,2048]{1,0:T(8,128)(2,1)S(1)}, u32[]{:S(2)}, u32[]{:S(2)}) collective-permute-start(bf16[80,2048]{1,0:T(8,128)(2,1)} %get-tuple-element.61), channel_id=1, source_target_pairs={{0,2},{1,3},{2,0},{3,1},{4,6},{5,7},{6,4},{7,5},{8,10},{9,11},{10,... | collective-permute-start | bytes 983048 | tf_op jit(solution)/shard_map/ppermute | solution.py:695
  19.7 22.7 %collective-permute-start.2 = (bf16[2,528,256]{2,1,0:T(8,128)(2,1)S(1)}, bf16[2,528,256]{2,1,0:T(8,128)(2,1)S(1)}, u32[]{:S(2)}, u32[]{:S(2)}) collective-permute-start(bf16[2,528,256]{2,1,0:T(8,128)(2,1)S(1)} %build_factors.3.refs_0_), channel_id=1, source_target_pairs={{0,8},{1,9},{2,10},{3,11},{4,0},{5,1},{6,2},{7,3},{8,12},{9,13},{1... | collective-permute-start | bytes 1622024 | tf_op jit(solution)/shard_map/ppermute | solution.py:695
  23.8 24.3 %collective-permute-start.11 = (bf16[64,2048]{1,0:T(8,128)(2,1)}, bf16[64,2048]{1,0:T(8,128)(2,1)S(1)}, u32[]{:S(2)}, u32[]{:S(2)}) collective-permute-start(bf16[64,2048]{1,0:T(8,128)(2,1)} %get-tuple-element.66), channel_id=1, source_target_pairs={{0,3},{1,2},{2,1},{3,0},{4,7},{5,6},{6,5},{7,4},{8,11},{9,10},{10,... | collective-permute-start | bytes 786440 | tf_op jit(solution)/shard_map/ppermute | solution.py:695
  28.7 15.3 %collective-permute-start.6 = (bf16[80,2048]{1,0:T(8,128)(2,1)S(1)}, bf16[80,2048]{1,0:T(8,128)(2,1)S(1)}, u32[]{:S(2)}, u32[]{:S(2)}) collective-permute-start(bf16[80,2048]{1,0:T(8,128)(2,1)S(1)} %copy-done.42), channel_id=1, source_target_pairs={{0,3},{1,2},{2,1},{3,0},{4,7},{5,6},{6,5},{7,4},{8,11},{9,10},{10,... | collective-permute-start | bytes 983048 | tf_op jit(solution)/shard_map/ppermute | solution.py:695
  30.1 25.3 %collective-permute-start.3 = (bf16[528,256]{1,0:T(8,128)(2,1)}, bf16[528,256]{1,0:T(8,128)(2,1)}, u32[]{:S(2)}, u32[]{:S(2)}) collective-permute-start(bf16[528,256]{1,0:T(8,128)(2,1)} %slice_bitcast_fusion.3), channel_id=1, source_target_pairs={{0,4},{1,5},{2,6},{3,7},{4,12},{5,13},{6,14},{7,15},{8,0},{9,1},{1... | collective-permute-start | bytes 811016 | tf_op jit(solution)/shard_map/ppermute | solution.py:695
  43.3 12.1 %collective-permute-start.4 = (bf16[528,256]{1,0:T(8,128)(2,1)}, bf16[528,256]{1,0:T(8,128)(2,1)}, u32[]{:S(2)}, u32[]{:S(2)}) collective-permute-start(bf16[528,256]{1,0:T(8,128)(2,1)} %slice_bitcast_fusion.2), channel_id=1, source_target_pairs={{0,8},{1,9},{2,10},{3,11},{4,0},{5,1},{6,2},{7,3},{8,12},{9,13},{1... | collective-permute-start | bytes 811016 | tf_op jit(solution)/shard_map/ppermute | solution.py:695
  44.1 11.3 %collective-permute-start.12 = (bf16[64,2048]{1,0:T(8,128)(2,1)}, bf16[64,2048]{1,0:T(8,128)(2,1)}, u32[]{:S(2)}, u32[]{:S(2)}) collective-permute-start(bf16[64,2048]{1,0:T(8,128)(2,1)} %get-tuple-element.70), channel_id=1, source_target_pairs={{0,1},{1,0},{2,3},{3,2},{4,5},{5,4},{6,7},{7,6},{8,9},{9,8},{10,11... | collective-permute-start | bytes 786440 | tf_op jit(solution)/shard_map/ppermute | solution.py:695
  44.1 11.3 %collective-permute-start.13 = (bf16[64,2048]{1,0:T(8,128)(2,1)}, bf16[64,2048]{1,0:T(8,128)(2,1)}, u32[]{:S(2)}, u32[]{:S(2)}) collective-permute-start(bf16[64,2048]{1,0:T(8,128)(2,1)} %get-tuple-element.72), channel_id=1, source_target_pairs={{0,2},{1,3},{2,0},{3,1},{4,6},{5,7},{6,4},{7,5},{8,10},{9,11},{10,... | collective-permute-start | bytes 786440 | tf_op jit(solution)/shard_map/ppermute | solution.py:695
  48.0 37.1 %copy-start.1 = (bf16[8,2,32,2048]{3,2,1,0:T(8,128)(2,1)S(1)}, bf16[8,2,32,2048]{3,2,1,0:T(8,128)(2,1)}, u32[]{:S(2)}) copy-start(bf16[8,2,32,2048]{3,2,1,0:T(8,128)(2,1)} %refs_0_.11) | copy-start | bytes 6291460
  48.0 37.1 %copy-start.31 = (s32[1,148]{1,0:T(1,128)S(1)}, s32[1,148]{1,0:T(1,128)}, u32[]{:S(2)}) copy-start(s32[1,148]{1,0:T(1,128)} %constant_dynamic-slice_fusion) | copy-start | bytes 1780
  48.0 37.1 %copy-start.33 = (s32[8,32]{1,0:T(8,128)S(1)}, s32[8,32]{1,0:T(8,128)}, u32[]{:S(2)}) copy-start(s32[8,32]{1,0:T(8,128)} %refs_6_.1) | copy-start | bytes 3076
  48.0 37.1 %copy-start.35 = (f32[2,256]{1,0:T(2,128)S(1)}, f32[2,256]{1,0:T(2,128)}, u32[]{:S(2)}) copy-start(f32[2,256]{1,0:T(2,128)} %refs_4_.5) | copy-start | bytes 6148
  48.0 37.1 %copy-start.37 = (f32[256]{0:T(256)S(1)}, f32[256]{0:T(256)}, u32[]{:S(2)}) copy-start(f32[256]{0:T(256)} %broadcast_in_dim.34) | copy-start | bytes 3076
  48.8 16.6 %collective-permute-start.8 = (bf16[2,528,256]{2,1,0:T(8,128)(2,1)S(1)}, bf16[2,528,256]{2,1,0:T(8,128)(2,1)}, u32[]{:S(2)}, u32[]{:S(2)}) collective-permute-start(bf16[2,528,256]{2,1,0:T(8,128)(2,1)S(1)} %build_factors.4.refs_5_), channel_id=1, source_target_pairs={{0,8},{1,9},{2,10},{3,11},{4,0},{5,1},{6,2},{7,3},{8,12},{9,13},{1... | collective-permute-start | bytes 1622024 | tf_op jit(solution)/shard_map/ppermute | solution.py:695
  51.3 46.9 %copy-start.41 = (s32[8,2048]{1,0:T(8,128)S(1)}, s32[8,2048]{1,0:T(8,128)}, u32[]{:S(2)}) copy-start(s32[8,2048]{1,0:T(8,128)} %param.14) | copy-start | bytes 196612
  55.3 43.0 %copy-start.4 = (bf16[2,528,256]{2,1,0:T(8,128)(2,1)S(1)}, bf16[2,528,256]{2,1,0:T(8,128)(2,1)}, u32[]{:S(2)}) copy-start(bf16[2,528,256]{2,1,0:T(8,128)(2,1)} %copy-done.3) | copy-start | bytes 1622020
  55.3 43.0 %copy-start.6 = (bf16[2,528,256]{2,1,0:T(8,128)(2,1)S(1)}, bf16[2,528,256]{2,1,0:T(8,128)(2,1)}, u32[]{:S(2)}) copy-start(bf16[2,528,256]{2,1,0:T(8,128)(2,1)} %copy-done.5) | copy-start | bytes 1622020
  55.3 26.5 %collective-permute-start.7 = (bf16[2,528,256]{2,1,0:T(8,128)(2,1)S(1)}, bf16[2,528,256]{2,1,0:T(8,128)(2,1)S(1)}, u32[]{:S(2)}, u32[]{:S(2)}) collective-permute-start(bf16[2,528,256]{2,1,0:T(8,128)(2,1)S(1)} %build_factors.4.refs_5_), channel_id=1, source_target_pairs={{0,4},{1,5},{2,6},{3,7},{4,12},{5,13},{6,14},{7,15},{8,0},{9,1},{1... | collective-permute-start | bytes 1622024 | tf_op jit(solution)/shard_map/ppermute | solution.py:695
  55.4 40.8 %collective-permute-start.14 = (bf16[2,2,2,256,256]{4,3,2,1,0:T(8,128)(2,1)}, bf16[2,2,2,256,256]{4,3,2,1,0:T(8,128)(2,1)S(1)}, u32[]{:S(2)}, u32[]{:S(2)}) collective-permute-start(bf16[2,2,2,256,256]{4,3,2,1,0:T(8,128)(2,1)} %get-tuple-element.73), channel_id=1, source_target_pairs={{0,2},{1,3},{2,0},{3,1},{4,6},{5,7},{6,4},{7,5},{8,10},{9,11},{10,... | collective-permute-start | bytes 3145736 | tf_op jit(solution)/shard_map/ppermute | solution.py:695
  56.0 65.3 %collective-permute-start.16 = (bf16[2,2,2,256,256]{4,3,2,1,0:T(8,128)(2,1)}, bf16[2,2,2,256,256]{4,3,2,1,0:T(8,128)(2,1)S(1)}, u32[]{:S(2)}, u32[]{:S(2)}) collective-permute-start(bf16[2,2,2,256,256]{4,3,2,1,0:T(8,128)(2,1)} %get-tuple-element.79), channel_id=1, source_target_pairs={{0,3},{1,2},{2,1},{3,0},{4,7},{5,6},{6,5},{7,4},{8,11},{9,10},{10,... | collective-permute-start | bytes 3145736 | tf_op jit(solution)/shard_map/ppermute | solution.py:695
  66.3 26.3 %collective-permute-start.10 = (bf16[528,256]{1,0:T(8,128)(2,1)S(1)}, bf16[528,256]{1,0:T(8,128)(2,1)S(1)}, u32[]{:S(2)}, u32[]{:S(2)}) collective-permute-start(bf16[528,256]{1,0:T(8,128)(2,1)S(1)} %slice_bitcast_fusion), channel_id=1, source_target_pairs={{0,8},{1,9},{2,10},{3,11},{4,0},{5,1},{6,2},{7,3},{8,12},{9,13},{1... | collective-permute-start | bytes 811016 | tf_op jit(solution)/shard_map/ppermute | solution.py:695
  78.7 44.6 %collective-permute-start.17 = (bf16[2,2,2,256,256]{4,3,2,1,0:T(8,128)(2,1)}, bf16[2,2,2,256,256]{4,3,2,1,0:T(8,128)(2,1)S(1)}, u32[]{:S(2)}, u32[]{:S(2)}) collective-permute-start(bf16[2,2,2,256,256]{4,3,2,1,0:T(8,128)(2,1)} %get-tuple-element.81), channel_id=1, source_target_pairs={{0,1},{1,0},{2,3},{3,2},{4,5},{5,4},{6,7},{7,6},{8,9},{9,8},{10,11... | collective-permute-start | bytes 3145736 | tf_op jit(solution)/shard_map/ppermute | solution.py:695
  81.9 14.4 %collective-permute-start.9 = (bf16[528,256]{1,0:T(8,128)(2,1)S(1)}, bf16[528,256]{1,0:T(8,128)(2,1)S(1)}, u32[]{:S(2)}, u32[]{:S(2)}) collective-permute-start(bf16[528,256]{1,0:T(8,128)(2,1)S(1)} %slice_bitcast_fusion.1), channel_id=1, source_target_pairs={{0,4},{1,5},{2,6},{3,7},{4,12},{5,13},{6,14},{7,15},{8,0},{9,1},{1... | collective-permute-start | bytes 811016 | tf_op jit(solution)/shard_map/ppermute | solution.py:695
  92.6 71.6 %copy-start.11 = (bf16[2,512,256]{2,1,0:T(8,128)(2,1)}, bf16[2,512,256]{2,1,0:T(8,128)(2,1)S(1)}, u32[]{:S(2)}) copy-start(bf16[2,512,256]{2,1,0:T(8,128)(2,1)S(1)} %get-tuple-element.88.refs_0_) | copy-start | bytes 1572868
  92.6 71.6 %copy-start.13 = (bf16[2,512,256]{2,1,0:T(8,128)(2,1)}, bf16[2,512,256]{2,1,0:T(8,128)(2,1)S(1)}, u32[]{:S(2)}) copy-start(bf16[2,512,256]{2,1,0:T(8,128)(2,1)S(1)} %get-tuple-element.93.refs_5_) | copy-start | bytes 1572868
  92.6 26.8 %collective-permute-start.20 = (bf16[2,512,256]{2,1,0:T(8,128)(2,1)S(1)}, bf16[2,512,256]{2,1,0:T(8,128)(2,1)S(1)}, u32[]{:S(2)}, u32[]{:S(2)}) collective-permute-start(bf16[2,512,256]{2,1,0:T(8,128)(2,1)S(1)} %get-tuple-element.88.refs_0_), channel_id=1, source_target_pairs={{0,4},{1,5},{2,6},{3,7},{4,12},{5,13},{6,14},{7,15},{8,0},{9,1},{1... | collective-permute-start | bytes 1572872 | tf_op jit(solution)/shard_map/ppermute | solution.py:695
  96.3 23.7 %collective-permute-start.15 = (bf16[2,512,256]{2,1,0:T(8,128)(2,1)S(1)}, bf16[2,512,256]{2,1,0:T(8,128)(2,1)S(1)}, u32[]{:S(2)}, u32[]{:S(2)}) collective-permute-start(bf16[2,512,256]{2,1,0:T(8,128)(2,1)S(1)} %get-tuple-element.88.refs_0_), channel_id=1, source_target_pairs={{0,8},{1,9},{2,10},{3,11},{4,0},{5,1},{6,2},{7,3},{8,12},{9,13},{1... | collective-permute-start | bytes 1572872 | tf_op jit(solution)/shard_map/ppermute | solution.py:695
  96.3 42.2 %collective-permute-start.23 = (bf16[2,512,256]{2,1,0:T(8,128)(2,1)S(1)}, bf16[2,512,256]{2,1,0:T(8,128)(2,1)S(1)}, u32[]{:S(2)}, u32[]{:S(2)}) collective-permute-start(bf16[2,512,256]{2,1,0:T(8,128)(2,1)S(1)} %get-tuple-element.93.refs_5_), channel_id=1, source_target_pairs={{0,4},{1,5},{2,6},{3,7},{4,12},{5,13},{6,14},{7,15},{8,0},{9,1},{1... | collective-permute-start | bytes 1572872 | tf_op jit(solution)/shard_map/ppermute | solution.py:695
  102.8 61.3 %copy-start.2 = (f32[2,512,128]{2,1,0:T(8,128)}, f32[2,512,128]{2,1,0:T(8,128)S(1)}, u32[]{:S(2)}) copy-start(f32[2,512,128]{2,1,0:T(8,128)S(1)} %get-tuple-element.82.refs_15_.refs_13_) | copy-start | bytes 1572868
  119.4 22.9 %collective-permute-start.25 = (bf16[2,512,256]{2,1,0:T(8,128)(2,1)S(1)}, bf16[2,512,256]{2,1,0:T(8,128)(2,1)S(1)}, u32[]{:S(2)}, u32[]{:S(2)}) collective-permute-start(bf16[2,512,256]{2,1,0:T(8,128)(2,1)S(1)} %get-tuple-element.93.refs_5_), channel_id=1, source_target_pairs={{0,8},{1,9},{2,10},{3,11},{4,0},{5,1},{6,2},{7,3},{8,12},{9,13},{1... | collective-permute-start | bytes 1572872 | tf_op jit(solution)/shard_map/ppermute | solution.py:695
  119.9 38.6 %collective-permute-start.18 = (bf16[2,2,256,256]{3,2,1,0:T(8,128)(2,1)S(1)}, bf16[2,2,256,256]{3,2,1,0:T(8,128)(2,1)S(1)}, u32[]{:S(2)}, u32[]{:S(2)}) collective-permute-start(bf16[2,2,256,256]{3,2,1,0:T(8,128)(2,1)S(1)} %get-tuple-element.85), channel_id=1, source_target_pairs={{0,2},{1,3},{2,0},{3,1},{4,6},{5,7},{6,4},{7,5},{8,10},{9,11},{10,... | collective-permute-start | bytes 1572872 | tf_op jit(solution)/shard_map/ppermute | solution.py:695
  121.3 28.1 %collective-permute-start.21 = (bf16[512,256]{1,0:T(8,128)(2,1)S(1)}, bf16[512,256]{1,0:T(8,128)(2,1)S(1)}, u32[]{:S(2)}, u32[]{:S(2)}) collective-permute-start(bf16[512,256]{1,0:T(8,128)(2,1)S(1)} %slice_bitcast_fusion.7), channel_id=1, source_target_pairs={{0,4},{1,5},{2,6},{3,7},{4,12},{5,13},{6,14},{7,15},{8,0},{9,1},{1... | collective-permute-start | bytes 786440 | tf_op jit(solution)/shard_map/ppermute | solution.py:695
  134.4 13.0 %collective-permute-start.19 = (bf16[2,2,256,256]{3,2,1,0:T(8,128)(2,1)S(1)}, bf16[2,2,256,256]{3,2,1,0:T(8,128)(2,1)S(1)}, u32[]{:S(2)}, u32[]{:S(2)}) collective-permute-start(bf16[2,2,256,256]{3,2,1,0:T(8,128)(2,1)S(1)} %get-tuple-element.87), channel_id=1, source_target_pairs={{0,3},{1,2},{2,1},{3,0},{4,7},{5,6},{6,5},{7,4},{8,11},{9,10},{10,... | collective-permute-start | bytes 1572872 | tf_op jit(solution)/shard_map/ppermute | solution.py:695
  138.5 13.3 %collective-permute-start.22 = (bf16[512,256]{1,0:T(8,128)(2,1)S(1)}, bf16[512,256]{1,0:T(8,128)(2,1)S(1)}, u32[]{:S(2)}, u32[]{:S(2)}) collective-permute-start(bf16[512,256]{1,0:T(8,128)(2,1)S(1)} %slice_bitcast_fusion.6), channel_id=1, source_target_pairs={{0,8},{1,9},{2,10},{3,11},{4,0},{5,1},{6,2},{7,3},{8,12},{9,13},{1... | collective-permute-start | bytes 786440 | tf_op jit(solution)/shard_map/ppermute | solution.py:695
  142.3 16.1 %collective-permute-start.24 = (bf16[512,256]{1,0:T(8,128)(2,1)S(1)}, bf16[512,256]{1,0:T(8,128)(2,1)S(1)}, u32[]{:S(2)}, u32[]{:S(2)}) collective-permute-start(bf16[512,256]{1,0:T(8,128)(2,1)S(1)} %slice_bitcast_fusion.5), channel_id=1, source_target_pairs={{0,4},{1,5},{2,6},{3,7},{4,12},{5,13},{6,14},{7,15},{8,0},{9,1},{1... | collective-permute-start | bytes 786440 | tf_op jit(solution)/shard_map/ppermute | solution.py:695
  147.4 16.7 %collective-permute-start.26 = (bf16[512,256]{1,0:T(8,128)(2,1)S(1)}, bf16[512,256]{1,0:T(8,128)(2,1)S(1)}, u32[]{:S(2)}, u32[]{:S(2)}) collective-permute-start(bf16[512,256]{1,0:T(8,128)(2,1)S(1)} %slice_bitcast_fusion.4), channel_id=1, source_target_pairs={{0,8},{1,9},{2,10},{3,11},{4,0},{5,1},{6,2},{7,3},{8,12},{9,13},{1... | collective-permute-start | bytes 786440 | tf_op jit(solution)/shard_map/ppermute | solution.py:695
  168.8 17.7 %collective-permute-start.27 = (bf16[2,2,256,256]{3,2,1,0:T(8,128)(2,1)}, bf16[2,2,256,256]{3,2,1,0:T(8,128)(2,1)S(1)}, u32[]{:S(2)}, u32[]{:S(2)}) collective-permute-start(bf16[2,2,256,256]{3,2,1,0:T(8,128)(2,1)} %get-tuple-element.97), channel_id=1, source_target_pairs={{0,2},{1,3},{2,0},{3,1},{4,6},{5,7},{6,4},{7,5},{8,10},{9,11},{10,... | collective-permute-start | bytes 1572872 | tf_op jit(solution)/shard_map/ppermute | solution.py:695
  169.7 21.5 %collective-permute-start.30 = (bf16[2,2,256,256]{3,2,1,0:T(8,128)(2,1)}, bf16[2,2,256,256]{3,2,1,0:T(8,128)(2,1)}, u32[]{:S(2)}, u32[]{:S(2)}) collective-permute-start(bf16[2,2,256,256]{3,2,1,0:T(8,128)(2,1)} %get-tuple-element.107), channel_id=1, source_target_pairs={{0,1},{1,0},{2,3},{3,2},{4,5},{5,4},{6,7},{7,6},{8,9},{9,8},{10,11... | collective-permute-start | bytes 1572872 | tf_op jit(solution)/shard_map/ppermute | solution.py:695
  183.2 18.8 %collective-permute-start.28 = (bf16[2,2,256,256]{3,2,1,0:T(8,128)(2,1)S(1)}, bf16[2,2,256,256]{3,2,1,0:T(8,128)(2,1)S(1)}, u32[]{:S(2)}, u32[]{:S(2)}) collective-permute-start(bf16[2,2,256,256]{3,2,1,0:T(8,128)(2,1)S(1)} %get-tuple-element.100), channel_id=1, source_target_pairs={{0,3},{1,2},{2,1},{3,0},{4,7},{5,6},{6,5},{7,4},{8,11},{9,10},{10,... | collective-permute-start | bytes 1572872 | tf_op jit(solution)/shard_map/ppermute | solution.py:695
  184.5 15.4 %collective-permute-start.29 = (bf16[2,2,256,256]{3,2,1,0:T(8,128)(2,1)S(1)}, bf16[2,2,256,256]{3,2,1,0:T(8,128)(2,1)S(1)}, u32[]{:S(2)}, u32[]{:S(2)}) collective-permute-start(bf16[2,2,256,256]{3,2,1,0:T(8,128)(2,1)S(1)} %get-tuple-element.103), channel_id=1, source_target_pairs={{0,1},{1,0},{2,3},{3,2},{4,5},{5,4},{6,7},{7,6},{8,9},{9,8},{10,11... | collective-permute-start | bytes 1572872 | tf_op jit(solution)/shard_map/ppermute | solution.py:695
  184.6 13.3 %collective-permute-start.33 = (f32[2,128]{1,0:T(2,128)S(1)}, f32[2,128]{1,0:T(2,128)S(1)}, u32[]{:S(2)}, u32[]{:S(2)}) collective-permute-start(f32[2,128]{1,0:T(2,128)S(1)} %get-tuple-element.113), channel_id=1, source_target_pairs={{0,4},{1,5},{2,6},{3,7},{4,12},{5,13},{6,14},{7,15},{8,0},{9,1},{1... | collective-permute-start | bytes 3080 | tf_op jit(solution)/shard_map/ppermute | solution.py:695
  186.5 11.4 %collective-permute-start.31 = (f32[2,128]{1,0:T(2,128)S(1)}, f32[2,128]{1,0:T(2,128)S(1)}, u32[]{:S(2)}, u32[]{:S(2)}) collective-permute-start(f32[2,128]{1,0:T(2,128)S(1)} %get-tuple-element.112), channel_id=1, source_target_pairs={{0,12},{1,13},{2,14},{3,15},{4,8},{5,9},{6,10},{7,11},{8,4},{9,5},... | collective-permute-start | bytes 3080 | tf_op jit(solution)/shard_map/ppermute | solution.py:695
  191.2 6.7 %collective-permute-start.32 = (f32[2,128]{1,0:T(2,128)S(1)}, f32[2,128]{1,0:T(2,128)S(1)}, u32[]{:S(2)}, u32[]{:S(2)}) collective-permute-start(f32[2,128]{1,0:T(2,128)S(1)} %get-tuple-element.110), channel_id=1, source_target_pairs={{0,8},{1,9},{2,10},{3,11},{4,0},{5,1},{6,2},{7,3},{8,12},{9,13},{1... | collective-permute-start | bytes 3080 | tf_op jit(solution)/shard_map/ppermute | solution.py:695
  198.0 6.1 %collective-permute-start.36 = (f32[2,32]{1,0:T(2,128)S(1)}, f32[2,32]{1,0:T(2,128)S(1)}, u32[]{:S(2)}, u32[]{:S(2)}) collective-permute-start(f32[2,32]{1,0:T(2,128)S(1)} %get-tuple-element.111), channel_id=1, source_target_pairs={{0,3},{1,2},{2,1},{3,0},{4,7},{5,6},{6,5},{7,4},{8,11},{9,10},{10,... | collective-permute-start | bytes 776 | tf_op jit(solution)/shard_map/ppermute | solution.py:695
  198.0 6.1 %collective-permute-start.35 = (f32[2,32]{1,0:T(2,128)S(1)}, f32[2,32]{1,0:T(2,128)S(1)}, u32[]{:S(2)}, u32[]{:S(2)}) collective-permute-start(f32[2,32]{1,0:T(2,128)S(1)} %get-tuple-element.117), channel_id=1, source_target_pairs={{0,2},{1,3},{2,0},{3,1},{4,6},{5,7},{6,4},{7,5},{8,10},{9,11},{10,... | collective-permute-start | bytes 776 | tf_op jit(solution)/shard_map/ppermute | solution.py:695
  199.3 4.9 %collective-permute-start.34 = (f32[2,32]{1,0:T(2,128)S(1)}, f32[2,32]{1,0:T(2,128)S(1)}, u32[]{:S(2)}, u32[]{:S(2)}) collective-permute-start(f32[2,32]{1,0:T(2,128)S(1)} %get-tuple-element.118), channel_id=1, source_target_pairs={{0,1},{1,0},{2,3},{3,2},{4,5},{5,4},{6,7},{7,6},{8,9},{9,8},{10,11... | collective-permute-start | bytes 776 | tf_op jit(solution)/shard_map/ppermute | solution.py:695
  (32 other events, 267.5 us)

commit v10 on v7

--- a/solution.py
+++ b/solution.py
@@ -168,7 +168,7 @@
             scratch_shapes=[pltpu.VMEM((SMALL_ROWS, small_width), jnp.float32)],
         ),
         out_shape=[jax.ShapeDtypeStruct(shape, jnp.bfloat16) for shape in shapes],
-        compiler_params=pltpu.CompilerParams(vmem_limit_bytes=40 * 1024 * 1024),
+        compiler_params=pltpu.CompilerParams(vmem_limit_bytes=16 * 1024 * 1024),
         cost_estimate=LITTLE,
         name="build_factors",
     )(table, *operands, antenna_uvw)
@@ -323,11 +323,8 @@
         return lax.dot_general(a, b, (((1,), (0,)), ((), ())), preferred_element_type=jnp.float32)
 
     def scaled_of(re, im):
-        column = jnp.concatenate([columns_ref[index]] * (span // 128), 1)
-        return (
-            (re.astype(jnp.float32) * column).astype(jnp.bfloat16),
-            (im.astype(jnp.float32) * column).astype(jnp.bfloat16),
-        )
+        column = jnp.concatenate([columns_ref[index].astype(jnp.bfloat16)] * (span // 128), 1)
+        return re * column, im * column
 
     def outer(a, b):
         row_ids = lax.broadcasted_iota(jnp.int32, a.shape, 0)
@@ -491,7 +488,7 @@
             ],
         ),
         out_shape=out_shapes,
-        compiler_params=pltpu.CompilerParams(vmem_limit_bytes=48 * 1024 * 1024),
+        compiler_params=pltpu.CompilerParams(vmem_limit_bytes=16 * 1024 * 1024),
         cost_estimate=LITTLE,
         name="unit_work",
     )(*operands)
@@ -529,7 +526,7 @@
         ),
         out_shape=jax.ShapeDtypeStruct(shape, jnp.bfloat16),
         input_output_aliases=aliases,
-        compiler_params=pltpu.CompilerParams(vmem_limit_bytes=32 * 1024 * 1024),
+        compiler_params=pltpu.CompilerParams(vmem_limit_bytes=16 * 1024 * 1024),
         cost_estimate=LITTLE,
         name="put_residuals",
     )(*operands)

time: 202 us -> 202 us (level)
  local copies, waits for them, and re-layouts: 21.2 us -> 25.2 us
  waiting for transfers between devices: 64.7 us -> 61.5 us
    unnamed x97 -> x109, local copies, waits for them, and re-layouts: 15.5 us -> 19.6 us
    ppermute x37, waiting for transfers between devices: 64.7 us -> 61.5 us  [send(): done[step] = lax.ppermute(gated(step, value), 'tile', pairs)]
  transfers between devices with their start and end apart: 37 -> 37, of which waited for: 12 -> 10; matrix products, arithmetic and copies ran while one was open for 3% -> 3% of each run, Pallas kernels for 28% -> 28%
where the time goes in v10:
time: 202 us; the launch traced here: 201 us
  waiting for transfers between devices  61.5 us (30%)
  Pallas kernels  59.8 us (30%)
  starting transfers between devices  50.7 us (25%)
  local copies, waits for them, and re-layouts  25.2 us (12%)
  other arithmetic  2.16 us (1%)
    ppermute x37, waiting for transfers between devices, send(): done[step] = lax.ppermute(gated(step, value), 'tile', pairs)  61.5 us
    ppermute x37, starting transfers between devices, send(): done[step] = lax.ppermute(gated(step, value), 'tile', pairs)  50.7 us
    pallas_call x6, Pallas kernels, unit_work(): pl.pallas_call(functools.partial(unit_kernel, index, offset, kinds, brigh...  32.4 us
    unnamed x109, local copies, waits for them, and re-layouts  19.6 us
    pallas_call x3, Pallas kernels, put_residuals(): pl.pallas_call(functools.partial(put_kernel, sources), grid_spec=pltpu.Pr...  9.1 us
    pallas_call x3, Pallas kernels, messages_for(): pl.pallas_call(functools.partial(message_kernel, len(others), bool(smalls...  7.69 us
    pallas_call x3, Pallas kernels, build_factors(): pl.pallas_call(functools.partial(build_kernel, sets, slot_ids, pieces, br...  6.7 us
  transfers between devices with their start and end apart: 37, of which 10 were waited for; matrix products, arithmetic and copies ran while one was open for 3% of the time, Pallas kernels for 28%

profile of v10, /device:TPU:0, one launch (start us, length us, event | category | flops | bytes accessed | tf_op | source)
XLA Modules:
  0.0 200.7 jit_solution(12273685182907837313)
XLA Ops:
  0.6 1.3 broadcast_in_dim.34
  2.0 1.3 constant_dynamic-slice_fusion
  3.3 2.4 %messages_for.3 = bf16[80,2048]{1,0:T(8,128)(2,1)} custom-call(s32[148]{0:T(256)} %bitcast.24, bf16[8,2,32,2048]{3,2,1,0:T(8,128)(2,1)} %refs_0_.10, f32[2,256]{1,0:T(2,128)} %refs_4_.5, f32[1,256]{1,0:T(1,128)} %bitcast.40, s32[8,32]{1,0:T(8,128)} %refs_6_.1), custom_call_target="tpu_custom_call" | custom-call | flops 1 | bytes 1 | tf_op jit(solution)/shard_map/messages_for/pallas_call | solution.py:211
  6.1 1.1 copy.15.refs_5_.refs_10_.refs_2_
  10.3 1.6 build_factors.3.refs_0_
  11.9 4.0 %collective-permute-start.1 = (bf16[2,528,256]{2,1,0:T(8,128)(2,1)S(1)}, bf16[2,528,256]{2,1,0:T(8,128)(2,1)S(1)}, u32[]{:S(2)}, u32[]{:S(2)}) collective-permute-start(bf16[2,528,256]{2,1,0:T(8,128)(2,1)S(1)} %build_factors.3.refs_0_), channel_id=1, source_target_pairs={{0,8},{1,9},{2,10},{3,11},{4,0},{5,1},{6,2},{7,3},{8,12},{9,13},{1... | collective-permute-start | bytes 1622024 | tf_op jit(solution)/shard_map/ppermute | solution.py:691
  15.9 2.6 %messages_for.5 = (bf16[80,2048]{1,0:T(8,128)(2,1)}, bf16[80,2048]{1,0:T(8,128)(2,1)}) custom-call(s32[148]{0:T(256)} %bitcast.25, bf16[8,2,32,2048]{3,2,1,0:T(8,128)(2,1)} %refs_0_.10, bf16[8,2,32,2048]{3,2,1,0:T(8,128)(2,1)} %refs_0_.10, f32[2,256]{1,0:T(2,128)} %refs_4_.5, f32[1,256]{1,0:T(1,128)} %bitcast.41, s32[8,32]{1,0:T(8,128)} %refs_6_.1), custom_call_target="tpu_custom_call" | custom-call | flops 1 | bytes 1 | tf_op jit(solution)/shard_map/messages_for/pallas_call | solution.py:211
  18.5 1.5 collective-permute-start.7
  20.0 2.7 %messages_for.4 = (bf16[64,2048]{1,0:T(8,128)(2,1)}, bf16[64,2048]{1,0:T(8,128)(2,1)}, bf16[64,2048]{1,0:T(8,128)(2,1)}) custom-call(s32[148]{0:T(256)} %bitcast.26, bf16[8,2,32,2048]{3,2,1,0:T(8,128)(2,1)} %refs_0_.10, bf16[8,2,32,2048]{3,2,1,0:T(8,128)(2,1)} %refs_0_.10, bf16[8,2,32,2048]{3,2,1,0:T(8,128)(2,1)} %refs_0_.10), custom_call_target="tpu_custom_call" | custom-call | flops 1 | bytes 1 | tf_op jit(solution)/shard_map/messages_for/pallas_call | solution.py:211
  22.7 6.6 %collective-permute-done.7.refs_8_.refs_0_ = bf16[80,2048]{1,0:T(8,128)(2,1)S(1)} collective-permute-done((bf16[80,2048]{1,0:T(8,128)(2,1)}, bf16[80,2048]{1,0:T(8,128)(2,1)S(1)}, u32[]{:S(2)}, u32[]{:S(2)}) %collective-permute-start.7) | collective-permute-done | bytes 327712 | tf_op jit(solution)/shard_map/ppermute | solution.py:691
  30.1 2.7 %collective-permute-start.2 = (bf16[528,256]{1,0:T(8,128)(2,1)}, bf16[528,256]{1,0:T(8,128)(2,1)}, u32[]{:S(2)}, u32[]{:S(2)}) collective-permute-start(bf16[528,256]{1,0:T(8,128)(2,1)} %slice_bitcast_fusion.3), channel_id=1, source_target_pairs={{0,8},{1,9},{2,10},{3,11},{4,0},{5,1},{6,2},{7,3},{8,12},{9,13},{1... | collective-permute-start | bytes 811016 | tf_op jit(solution)/shard_map/ppermute | solution.py:691
  32.7 9.2 %collective-permute-done.3.refs_1_ = bf16[2,528,256]{2,1,0:T(8,128)(2,1)S(1)} collective-permute-done((bf16[2,528,256]{2,1,0:T(8,128)(2,1)S(1)}, bf16[2,528,256]{2,1,0:T(8,128)(2,1)S(1)}, u32[]{:S(2)}, u32[]{:S(2)}) %collective-permute-start.3) | collective-permute-done | bytes 540704 | tf_op jit(solution)/shard_map/ppermute | solution.py:691
  43.4 1.5 collective-permute-start.4
  45.0 1.6 build_factors.5.refs_5_
  48.1 2.2 %collective-permute-start.10 = (bf16[2,528,256]{2,1,0:T(8,128)(2,1)S(1)}, bf16[2,528,256]{2,1,0:T(8,128)(2,1)}, u32[]{:S(2)}, u32[]{:S(2)}) collective-permute-start(bf16[2,528,256]{2,1,0:T(8,128)(2,1)S(1)} %build_factors.5.refs_5_), channel_id=1, source_target_pairs={{0,8},{1,9},{2,10},{3,11},{4,0},{5,1},{6,2},{7,3},{8,12},{9,13},{1... | collective-permute-start | bytes 1622024 | tf_op jit(solution)/shard_map/ppermute | solution.py:691
  51.9 2.8 %collective-permute-start.9 = (bf16[2,528,256]{2,1,0:T(8,128)(2,1)S(1)}, bf16[2,528,256]{2,1,0:T(8,128)(2,1)}, u32[]{:S(2)}, u32[]{:S(2)}) collective-permute-start(bf16[2,528,256]{2,1,0:T(8,128)(2,1)S(1)} %build_factors.5.refs_5_), channel_id=1, source_target_pairs={{0,4},{1,5},{2,6},{3,7},{4,12},{5,13},{6,14},{7,15},{8,0},{9,1},{1... | collective-permute-start | bytes 1622024 | tf_op jit(solution)/shard_map/ppermute | solution.py:691
  54.6 4.0 %slices_for.1 = (bf16[2,2,2,256,256]{4,3,2,1,0:T(8,128)(2,1)}, bf16[2,2,2,256,256]{4,3,2,1,0:T(8,128)(2,1)}, bf16[2,2,2,256,256]{4,3,2,1,0:T(8,128)(2,1)}) custom-call(s32[148]{0:T(256)} %bitcast.27, bf16[2,8,2,256,256]{4,3,2,1,0:T(8,128)(2,1)} %refs_11_.3, bf16[2,8,2,256,256]{4,3,2,1,0:T(8,128)(2,1)} %refs_11_.3, bf16[2,8,2,256,256]{4,3,2,1,0:T(8,128)(2,1)} %refs_11_.3), custom_call_target="tpu_custom_call" | custom-call | flops 1 | bytes 1 | tf_op jit(solution)/shard_map/slices_for/pallas_call | solution.py:242
  58.6 1.6 collective-permute-start.17
  60.2 4.4 %collective-permute-done.10.refs_7_ = bf16[2,528,256]{2,1,0:T(8,128)(2,1)} collective-permute-done((bf16[2,528,256]{2,1,0:T(8,128)(2,1)S(1)}, bf16[2,528,256]{2,1,0:T(8,128)(2,1)}, u32[]{:S(2)}, u32[]{:S(2)}) %collective-permute-start.10) | collective-permute-done | bytes 540704 | tf_op jit(solution)/shard_map/ppermute | solution.py:691
  65.6 1.9 collective-permute-start.11
  67.5 10.1 %collective-permute-done.9.refs_6_ = bf16[2,528,256]{2,1,0:T(8,128)(2,1)} collective-permute-done((bf16[2,528,256]{2,1,0:T(8,128)(2,1)S(1)}, bf16[2,528,256]{2,1,0:T(8,128)(2,1)}, u32[]{:S(2)}, u32[]{:S(2)}) %collective-permute-start.9) | collective-permute-done | bytes 540704 | tf_op jit(solution)/shard_map/ppermute | solution.py:691
  83.5 3.5 %build_factors.4 = (bf16[2,512,256]{2,1,0:T(8,128)(2,1)S(1)}, bf16[2,512,256]{2,1,0:T(8,128)(2,1)S(1)}) custom-call(s32[148]{0:T(256)S(1)} %bitcast.30, bf16[8,2,32,2048]{3,2,1,0:T(8,128)(2,1)S(1)} %copy-done.1, bf16[64,2048]{1,0:T(8,128)(2,1)} %collective-permute-done.5.refs_1_, bf16[64,2048]{1,0:T(8,128)(2,1)S(1)} %copy-done.45, ...), custom_call_target="tpu_custom_call" | custom-call | flops 1 | bytes 1 | tf_op jit(solution)/shard_map/build_factors/pallas_call | solution.py:161
  87.0 7.1 %collective-permute-start.12 = (bf16[2,512,256]{2,1,0:T(8,128)(2,1)S(1)}, bf16[2,512,256]{2,1,0:T(8,128)(2,1)S(1)}, u32[]{:S(2)}, u32[]{:S(2)}) collective-permute-start(bf16[2,512,256]{2,1,0:T(8,128)(2,1)S(1)} %get-tuple-element.89.refs_0_), channel_id=1, source_target_pairs={{0,4},{1,5},{2,6},{3,7},{4,12},{5,13},{6,14},{7,15},{8,0},{9,1},{1... | collective-permute-start | bytes 1572872 | tf_op jit(solution)/shard_map/ppermute | solution.py:691
  95.2 5.4 %unit_work.6 = (bf16[2,2,256,256]{3,2,1,0:T(8,128)(2,1)}, f32[1,512]{1,0:T(1,128)S(1)}, f32[2,512,128]{2,1,0:T(8,128)S(1)}) custom-call(s32[148]{0:T(256)S(1)} %bitcast.31, bf16[2,528,256]{2,1,0:T(8,128)(2,1)S(1)} %build_factors.3.refs_0_, bf16[2,528,256]{2,1,0:T(8,128)(2,1)S(1)} %copy-done.8, bf16[2,528,256]{2,1,0:T(8,128)(2,1)S(1)} %copy-done.5, ...), custom_call_target="tpu_custom_call" | custom-call | flops 1 | bytes 1 | tf_op jit(solution)/shard_map/unit_work/pallas_call | solution.py:476
  100.6 3.5 %collective-permute-done.13.refs_10_ = bf16[2,2,2,256,256]{4,3,2,1,0:T(8,128)(2,1)S(1)} collective-permute-done((bf16[2,2,2,256,256]{4,3,2,1,0:T(8,128)(2,1)}, bf16[2,2,2,256,256]{4,3,2,1,0:T(8,128)(2,1)S(1)}, u32[]{:S(2)}, u32[]{:S(2)}) %collective-permute-start.13) | collective-permute-done | bytes 1048608 | tf_op jit(solution)/shard_map/ppermute | solution.py:691
  104.7 5.1 %unit_work.7 = (bf16[2,2,256,256]{3,2,1,0:T(8,128)(2,1)}, f32[1,512]{1,0:T(1,128)S(1)}) custom-call(s32[148]{0:T(256)S(1)} %bitcast.32, bf16[2,528,256]{2,1,0:T(8,128)(2,1)S(1)} %build_factors.3.refs_0_, bf16[2,528,256]{2,1,0:T(8,128)(2,1)S(1)} %copy-done.8, bf16[2,528,256]{2,1,0:T(8,128)(2,1)S(1)} %copy-done.5, ...), custom_call_target="tpu_custom_call" | custom-call | flops 1 | bytes 1 | tf_op jit(solution)/shard_map/unit_work/pallas_call | solution.py:476
  109.9 1.9 collective-permute-start.20
  112.7 16.4 %collective-permute-done.24.refs_7_ = bf16[2,512,256]{2,1,0:T(8,128)(2,1)S(1)} collective-permute-done((bf16[2,512,256]{2,1,0:T(8,128)(2,1)S(1)}, bf16[2,512,256]{2,1,0:T(8,128)(2,1)S(1)}, u32[]{:S(2)}, u32[]{:S(2)}) %collective-permute-start.24) | collective-permute-done | bytes 524320 | tf_op jit(solution)/shard_map/ppermute | solution.py:691
  129.0 1.1 collective-permute-start.19
  131.5 8.8 %collective-permute-done.23.refs_6_ = bf16[2,512,256]{2,1,0:T(8,128)(2,1)S(1)} collective-permute-done((bf16[2,512,256]{2,1,0:T(8,128)(2,1)S(1)}, bf16[2,512,256]{2,1,0:T(8,128)(2,1)S(1)}, u32[]{:S(2)}, u32[]{:S(2)}) %collective-permute-start.23) | collective-permute-done | bytes 524320 | tf_op jit(solution)/shard_map/ppermute | solution.py:691
  143.2 2.8 %collective-permute-start.22 = (bf16[512,256]{1,0:T(8,128)(2,1)S(1)}, bf16[512,256]{1,0:T(8,128)(2,1)}, u32[]{:S(2)}, u32[]{:S(2)}) collective-permute-start(bf16[512,256]{1,0:T(8,128)(2,1)S(1)} %slice_bitcast_fusion.6), channel_id=1, source_target_pairs={{0,8},{1,9},{2,10},{3,11},{4,0},{5,1},{6,2},{7,3},{8,12},{9,13},{1... | collective-permute-start | bytes 786440 | tf_op jit(solution)/shard_map/ppermute | solution.py:691
  146.0 2.3 %collective-permute-start.25 = (bf16[512,256]{1,0:T(8,128)(2,1)}, bf16[512,256]{1,0:T(8,128)(2,1)}, u32[]{:S(2)}, u32[]{:S(2)}) collective-permute-start(bf16[512,256]{1,0:T(8,128)(2,1)} %slice_bitcast_fusion.5), channel_id=1, source_target_pairs={{0,4},{1,5},{2,6},{3,7},{4,12},{5,13},{6,14},{7,15},{8,0},{9,1},{1... | collective-permute-start | bytes 786440 | tf_op jit(solution)/shard_map/ppermute | solution.py:691
  148.4 2.2 %copy-done.2 = bf16[2,8,2,256,256]{4,3,2,1,0:T(8,128)(2,1)S(1)} copy-done((bf16[2,8,2,256,256]{4,3,2,1,0:T(8,128)(2,1)S(1)}, bf16[2,8,2,256,256]{4,3,2,1,0:T(8,128)(2,1)}, u32[]{:S(2)}) %copy-start.2) | copy-done | bytes 4194328
  150.6 1.2 copy-done.27
  153.7 7.0 %unit_work.8 = (bf16[2,2,256,256]{3,2,1,0:T(8,128)(2,1)S(1)}, bf16[2,2,256,256]{3,2,1,0:T(8,128)(2,1)S(1)}, f32[1,512]{1,0:T(1,128)S(1)}) custom-call(s32[148]{0:T(256)S(1)} %bitcast.33, bf16[2,528,256]{2,1,0:T(8,128)(2,1)S(1)} %build_factors.3.refs_0_, bf16[2,528,256]{2,1,0:T(8,128)(2,1)S(1)} %copy-done.9, bf16[2,528,256]{2,1,0:T(8,128)(2,1)S(1)} %copy-done.6, ...), custom_call_target="tpu_custom_call" | custom-call | flops 1 | bytes 1 | tf_op jit(solution)/shard_map/unit_work/pallas_call | solution.py:476
  160.9 1.3 collective-permute-done.25.refs_8_
  162.2 4.2 %unit_work.9 = (bf16[2,2,256,256]{3,2,1,0:T(8,128)(2,1)S(1)}, f32[1,512]{1,0:T(1,128)S(1)}) custom-call(s32[148]{0:T(256)S(1)} %bitcast.34, bf16[2,512,256]{2,1,0:T(8,128)(2,1)S(1)} %copy-done.19, bf16[2,512,256]{2,1,0:T(8,128)(2,1)S(1)} %copy-done.11, bf16[2,512,256]{2,1,0:T(8,128)(2,1)S(1)} %copy-done.13, ...), custom_call_target="tpu_custom_call" | custom-call | flops 1 | bytes 1 | tf_op jit(solution)/shard_map/unit_work/pallas_call | solution.py:476
  166.4 1.2 collective-permute-start.27
  167.6 4.2 %unit_work.10 = (bf16[2,2,256,256]{3,2,1,0:T(8,128)(2,1)S(1)}, f32[1,512]{1,0:T(1,128)S(1)}) custom-call(s32[148]{0:T(256)S(1)} %bitcast.35, bf16[2,512,256]{2,1,0:T(8,128)(2,1)S(1)} %copy-done.19, bf16[2,512,256]{2,1,0:T(8,128)(2,1)S(1)} %copy-done.11, bf16[2,512,256]{2,1,0:T(8,128)(2,1)S(1)} %copy-done.13, ...), custom_call_target="tpu_custom_call" | custom-call | flops 1 | bytes 1 | tf_op jit(solution)/shard_map/unit_work/pallas_call | solution.py:476
  171.8 6.5 %unit_work.11 = (bf16[2,2,256,256]{3,2,1,0:T(8,128)(2,1)S(1)}, bf16[2,2,256,256]{3,2,1,0:T(8,128)(2,1)S(1)}, f32[1,512]{1,0:T(1,128)S(1)}) custom-call(s32[148]{0:T(256)S(1)} %bitcast.36, bf16[2,512,256]{2,1,0:T(8,128)(2,1)S(1)} %copy-done.19, bf16[2,512,256]{2,1,0:T(8,128)(2,1)S(1)} %copy-done.11, bf16[2,512,256]{2,1,0:T(8,128)(2,1)S(1)} %copy-done.13, ...), custom_call_target="tpu_custom_call" | custom-call | flops 1 | bytes 1 | tf_op jit(solution)/shard_map/unit_work/pallas_call | solution.py:476
  178.4 2.1 %collective-permute-start.33 = (f32[2,128]{1,0:T(2,128)S(1)}, f32[2,128]{1,0:T(2,128)S(1)}, u32[]{:S(2)}, u32[]{:S(2)}) collective-permute-start(f32[2,128]{1,0:T(2,128)S(1)} %get-tuple-element.113), channel_id=1, source_target_pairs={{0,4},{1,5},{2,6},{3,7},{4,12},{5,13},{6,14},{7,15},{8,0},{9,1},{1... | collective-permute-start | bytes 3080 | tf_op jit(solution)/shard_map/ppermute | solution.py:691
  180.5 1.0 collective-permute-start.28
  181.5 5.4 %collective-permute-start.31 = (f32[2,128]{1,0:T(2,128)S(1)}, f32[2,128]{1,0:T(2,128)S(1)}, u32[]{:S(2)}, u32[]{:S(2)}) collective-permute-start(f32[2,128]{1,0:T(2,128)S(1)} %get-tuple-element.108), channel_id=1, source_target_pairs={{0,12},{1,13},{2,14},{3,15},{4,8},{5,9},{6,10},{7,11},{8,4},{9,5},... | collective-permute-start | bytes 3080 | tf_op jit(solution)/shard_map/ppermute | solution.py:691
  186.9 1.9 collective-permute-start.32
  188.9 4.8 %put_residuals.3.refs_2_ = bf16[2,8,2,256,256]{4,3,2,1,0:T(8,128)(2,1)} custom-call(s32[148]{0:T(256)S(1)} %bitcast.37, bf16[2,2,256,256]{3,2,1,0:T(8,128)(2,1)} %collective-permute-done.19.refs_0_, bf16[2,2,256,256]{3,2,1,0:T(8,128)(2,1)} %collective-permute-done.20.refs_1_, bf16[2,2,256,256]{3,2,1,0:T(8,128)(2,1)S(1)} %collective-permute-done.30.refs_2_, ...), custom_call_target="tpu_custom_call" | custom-call | flops 1 | bytes 1 | tf_op jit(solution)/shard_map/put_residuals/pallas_call | solution.py:516
  193.9 1.8 collective-permute-start.36
  195.7 2.1 %put_residuals.4.refs_2_ = bf16[2,8,2,256,256]{4,3,2,1,0:T(8,128)(2,1)} custom-call(s32[148]{0:T(256)S(1)} %bitcast.38, bf16[2,2,256,256]{3,2,1,0:T(8,128)(2,1)S(1)} %collective-permute-done.29.refs_0_, bf16[2,2,256,256]{3,2,1,0:T(8,128)(2,1)S(1)} %get-tuple-element.103.refs_1_, ...), custom_call_target="tpu_custom_call", output_to_operand_aliasing={{}: (3, {})} | custom-call | flops 1 | bytes 1 | tf_op jit(solution)/shard_map/put_residuals/pallas_call | solution.py:516
  197.8 2.1 %put_residuals.5 = bf16[2,8,2,256,256]{4,3,2,1,0:T(8,128)(2,1)} custom-call(s32[148]{0:T(256)S(1)} %bitcast.39, bf16[2,2,256,256]{3,2,1,0:T(8,128)(2,1)S(1)} %collective-permute-done.27.refs_0_, bf16[2,2,256,256]{3,2,1,0:T(8,128)(2,1)S(1)} %collective-permute-done.28.refs_1_, ...), custom_call_target="tpu_custom_call", output_to_operand_aliasing={{}: (3, {})} | custom-call | flops 1 | bytes 1 | tf_op jit(solution)/shard_map/put_residuals/pallas_call | solution.py:516
  (173 shorter events, 25.3 us)
Async XLA Ops:
  5.7 1.9 collective-permute-start
  11.9 17.4 %collective-permute-start.1 = (bf16[2,528,256]{2,1,0:T(8,128)(2,1)S(1)}, bf16[2,528,256]{2,1,0:T(8,128)(2,1)S(1)}, u32[]{:S(2)}, u32[]{:S(2)}) collective-permute-start(bf16[2,528,256]{2,1,0:T(8,128)(2,1)S(1)} %build_factors.3.refs_0_), channel_id=1, source_target_pairs={{0,8},{1,9},{2,10},{3,11},{4,0},{5,1},{6,2},{7,3},{8,12},{9,13},{1... | collective-permute-start | bytes 1622024 | tf_op jit(solution)/shard_map/ppermute | solution.py:691
  18.5 10.8 %collective-permute-start.7 = (bf16[80,2048]{1,0:T(8,128)(2,1)}, bf16[80,2048]{1,0:T(8,128)(2,1)S(1)}, u32[]{:S(2)}, u32[]{:S(2)}) collective-permute-start(bf16[80,2048]{1,0:T(8,128)(2,1)} %get-tuple-element.64), channel_id=1, source_target_pairs={{0,2},{1,3},{2,0},{3,1},{4,6},{5,7},{6,4},{7,5},{8,10},{9,11},{10,... | collective-permute-start | bytes 983048 | tf_op jit(solution)/shard_map/ppermute | solution.py:691
  20.0 22.0 %collective-permute-start.3 = (bf16[2,528,256]{2,1,0:T(8,128)(2,1)S(1)}, bf16[2,528,256]{2,1,0:T(8,128)(2,1)S(1)}, u32[]{:S(2)}, u32[]{:S(2)}) collective-permute-start(bf16[2,528,256]{2,1,0:T(8,128)(2,1)S(1)} %build_factors.3.refs_0_), channel_id=1, source_target_pairs={{0,4},{1,5},{2,6},{3,7},{4,12},{5,13},{6,14},{7,15},{8,0},{9,1},{1... | collective-permute-start | bytes 1622024 | tf_op jit(solution)/shard_map/ppermute | solution.py:691
  22.7 24.7 %collective-permute-start.6 = (bf16[64,2048]{1,0:T(8,128)(2,1)}, bf16[64,2048]{1,0:T(8,128)(2,1)S(1)}, u32[]{:S(2)}, u32[]{:S(2)}) collective-permute-start(bf16[64,2048]{1,0:T(8,128)(2,1)} %get-tuple-element.63), channel_id=1, source_target_pairs={{0,3},{1,2},{2,1},{3,0},{4,7},{5,6},{6,5},{7,4},{8,11},{9,10},{10,... | collective-permute-start | bytes 786440 | tf_op jit(solution)/shard_map/ppermute | solution.py:691
  29.3 15.7 %collective-permute-start.8 = (bf16[80,2048]{1,0:T(8,128)(2,1)S(1)}, bf16[80,2048]{1,0:T(8,128)(2,1)S(1)}, u32[]{:S(2)}, u32[]{:S(2)}) collective-permute-start(bf16[80,2048]{1,0:T(8,128)(2,1)S(1)} %copy-done.53), channel_id=1, source_target_pairs={{0,3},{1,2},{2,1},{3,0},{4,7},{5,6},{6,5},{7,4},{8,11},{9,10},{10,... | collective-permute-start | bytes 983048 | tf_op jit(solution)/shard_map/ppermute | solution.py:691
  30.1 28.5 %collective-permute-start.2 = (bf16[528,256]{1,0:T(8,128)(2,1)}, bf16[528,256]{1,0:T(8,128)(2,1)}, u32[]{:S(2)}, u32[]{:S(2)}) collective-permute-start(bf16[528,256]{1,0:T(8,128)(2,1)} %slice_bitcast_fusion.3), channel_id=1, source_target_pairs={{0,8},{1,9},{2,10},{3,11},{4,0},{5,1},{6,2},{7,3},{8,12},{9,13},{1... | collective-permute-start | bytes 811016 | tf_op jit(solution)/shard_map/ppermute | solution.py:691
  42.8 15.8 %collective-permute-start.15 = (bf16[528,256]{1,0:T(8,128)(2,1)}, bf16[528,256]{1,0:T(8,128)(2,1)}, u32[]{:S(2)}, u32[]{:S(2)}) collective-permute-start(bf16[528,256]{1,0:T(8,128)(2,1)} %slice_bitcast_fusion.1), channel_id=1, source_target_pairs={{0,4},{1,5},{2,6},{3,7},{4,12},{5,13},{6,14},{7,15},{8,0},{9,1},{1... | collective-permute-start | bytes 811016 | tf_op jit(solution)/shard_map/ppermute | solution.py:691
  43.4 7.7 %collective-permute-start.4 = (bf16[64,2048]{1,0:T(8,128)(2,1)}, bf16[64,2048]{1,0:T(8,128)(2,1)S(1)}, u32[]{:S(2)}, u32[]{:S(2)}) collective-permute-start(bf16[64,2048]{1,0:T(8,128)(2,1)} %get-tuple-element.59), channel_id=1, source_target_pairs={{0,2},{1,3},{2,0},{3,1},{4,6},{5,7},{6,4},{7,5},{8,10},{9,11},{10,... | collective-permute-start | bytes 786440 | tf_op jit(solution)/shard_map/ppermute | solution.py:691
  45.0 13.6 %collective-permute-start.5 = (bf16[64,2048]{1,0:T(8,128)(2,1)}, bf16[64,2048]{1,0:T(8,128)(2,1)}, u32[]{:S(2)}, u32[]{:S(2)}) collective-permute-start(bf16[64,2048]{1,0:T(8,128)(2,1)} %get-tuple-element.62), channel_id=1, source_target_pairs={{0,1},{1,0},{2,3},{3,2},{4,5},{5,4},{6,7},{7,6},{8,9},{9,8},{10,11... | collective-permute-start | bytes 786440 | tf_op jit(solution)/shard_map/ppermute | solution.py:691
  47.4 31.3 %copy-start.1 = (bf16[8,2,32,2048]{3,2,1,0:T(8,128)(2,1)S(1)}, bf16[8,2,32,2048]{3,2,1,0:T(8,128)(2,1)}, u32[]{:S(2)}) copy-start(bf16[8,2,32,2048]{3,2,1,0:T(8,128)(2,1)} %refs_0_.10) | copy-start | bytes 6291460
  47.4 31.3 %copy-start.41 = (s32[1,148]{1,0:T(1,128)S(1)}, s32[1,148]{1,0:T(1,128)}, u32[]{:S(2)}) copy-start(s32[1,148]{1,0:T(1,128)} %constant_dynamic-slice_fusion) | copy-start | bytes 1780
  47.4 31.3 %copy-start.47 = (s32[8,32]{1,0:T(8,128)S(1)}, s32[8,32]{1,0:T(8,128)}, u32[]{:S(2)}) copy-start(s32[8,32]{1,0:T(8,128)} %refs_6_.1) | copy-start | bytes 3076
  47.4 31.3 %copy-start.49 = (f32[2,256]{1,0:T(2,128)S(1)}, f32[2,256]{1,0:T(2,128)}, u32[]{:S(2)}) copy-start(f32[2,256]{1,0:T(2,128)} %refs_4_.5) | copy-start | bytes 6148
  47.4 31.3 %copy-start.51 = (f32[256]{0:T(256)S(1)}, f32[256]{0:T(256)}, u32[]{:S(2)}) copy-start(f32[256]{0:T(256)} %broadcast_in_dim.34) | copy-start | bytes 3076
  48.1 16.5 %collective-permute-start.10 = (bf16[2,528,256]{2,1,0:T(8,128)(2,1)S(1)}, bf16[2,528,256]{2,1,0:T(8,128)(2,1)}, u32[]{:S(2)}, u32[]{:S(2)}) collective-permute-start(bf16[2,528,256]{2,1,0:T(8,128)(2,1)S(1)} %build_factors.5.refs_5_), channel_id=1, source_target_pairs={{0,8},{1,9},{2,10},{3,11},{4,0},{5,1},{6,2},{7,3},{8,12},{9,13},{1... | collective-permute-start | bytes 1622024 | tf_op jit(solution)/shard_map/ppermute | solution.py:691
  51.9 25.8 %collective-permute-start.9 = (bf16[2,528,256]{2,1,0:T(8,128)(2,1)S(1)}, bf16[2,528,256]{2,1,0:T(8,128)(2,1)}, u32[]{:S(2)}, u32[]{:S(2)}) collective-permute-start(bf16[2,528,256]{2,1,0:T(8,128)(2,1)S(1)} %build_factors.5.refs_5_), channel_id=1, source_target_pairs={{0,4},{1,5},{2,6},{3,7},{4,12},{5,13},{6,14},{7,15},{8,0},{9,1},{1... | collective-permute-start | bytes 1622024 | tf_op jit(solution)/shard_map/ppermute | solution.py:691
  54.6 40.5 %copy-start.52 = (s32[8,2048]{1,0:T(8,128)S(1)}, s32[8,2048]{1,0:T(8,128)}, u32[]{:S(2)}) copy-start(s32[8,2048]{1,0:T(8,128)} %param.14) | copy-start | bytes 196612
  58.6 36.6 %copy-start.5 = (bf16[2,528,256]{2,1,0:T(8,128)(2,1)S(1)}, bf16[2,528,256]{2,1,0:T(8,128)(2,1)}, u32[]{:S(2)}) copy-start(bf16[2,528,256]{2,1,0:T(8,128)(2,1)} %copy-done.4) | copy-start | bytes 1622020
  58.6 36.6 %copy-start.8 = (bf16[2,528,256]{2,1,0:T(8,128)(2,1)S(1)}, bf16[2,528,256]{2,1,0:T(8,128)(2,1)}, u32[]{:S(2)}) copy-start(bf16[2,528,256]{2,1,0:T(8,128)(2,1)} %copy-done.7) | copy-start | bytes 1622020
  58.6 35.6 %collective-permute-start.17 = (bf16[2,2,2,256,256]{4,3,2,1,0:T(8,128)(2,1)}, bf16[2,2,2,256,256]{4,3,2,1,0:T(8,128)(2,1)S(1)}, u32[]{:S(2)}, u32[]{:S(2)}) collective-permute-start(bf16[2,2,2,256,256]{4,3,2,1,0:T(8,128)(2,1)} %get-tuple-element.77), channel_id=1, source_target_pairs={{0,2},{1,3},{2,0},{3,1},{4,6},{5,7},{6,4},{7,5},{8,10},{9,11},{10,... | collective-permute-start | bytes 3145736 | tf_op jit(solution)/shard_map/ppermute | solution.py:691
  60.2 43.9 %collective-permute-start.13 = (bf16[2,2,2,256,256]{4,3,2,1,0:T(8,128)(2,1)}, bf16[2,2,2,256,256]{4,3,2,1,0:T(8,128)(2,1)S(1)}, u32[]{:S(2)}, u32[]{:S(2)}) collective-permute-start(bf16[2,2,2,256,256]{4,3,2,1,0:T(8,128)(2,1)} %get-tuple-element.73), channel_id=1, source_target_pairs={{0,3},{1,2},{2,1},{3,0},{4,7},{5,6},{6,5},{7,4},{8,11},{9,10},{10,... | collective-permute-start | bytes 3145736 | tf_op jit(solution)/shard_map/ppermute | solution.py:691
  65.6 21.4 %collective-permute-start.11 = (bf16[528,256]{1,0:T(8,128)(2,1)S(1)}, bf16[528,256]{1,0:T(8,128)(2,1)S(1)}, u32[]{:S(2)}, u32[]{:S(2)}) collective-permute-start(bf16[528,256]{1,0:T(8,128)(2,1)S(1)} %slice_bitcast_fusion.2), channel_id=1, source_target_pairs={{0,8},{1,9},{2,10},{3,11},{4,0},{5,1},{6,2},{7,3},{8,12},{9,13},{1... | collective-permute-start | bytes 811016 | tf_op jit(solution)/shard_map/ppermute | solution.py:691
  78.6 15.6 %collective-permute-start.16 = (bf16[528,256]{1,0:T(8,128)(2,1)S(1)}, bf16[528,256]{1,0:T(8,128)(2,1)S(1)}, u32[]{:S(2)}, u32[]{:S(2)}) collective-permute-start(bf16[528,256]{1,0:T(8,128)(2,1)S(1)} %slice_bitcast_fusion), channel_id=1, source_target_pairs={{0,4},{1,5},{2,6},{3,7},{4,12},{5,13},{6,14},{7,15},{8,0},{9,1},{1... | collective-permute-start | bytes 811016 | tf_op jit(solution)/shard_map/ppermute | solution.py:691
  87.0 22.8 %collective-permute-start.12 = (bf16[2,512,256]{2,1,0:T(8,128)(2,1)S(1)}, bf16[2,512,256]{2,1,0:T(8,128)(2,1)S(1)}, u32[]{:S(2)}, u32[]{:S(2)}) collective-permute-start(bf16[2,512,256]{2,1,0:T(8,128)(2,1)S(1)} %get-tuple-element.89.refs_0_), channel_id=1, source_target_pairs={{0,4},{1,5},{2,6},{3,7},{4,12},{5,13},{6,14},{7,15},{8,0},{9,1},{1... | collective-permute-start | bytes 1572872 | tf_op jit(solution)/shard_map/ppermute | solution.py:691
  94.2 48.1 %collective-permute-start.18 = (bf16[2,2,2,256,256]{4,3,2,1,0:T(8,128)(2,1)}, bf16[2,2,2,256,256]{4,3,2,1,0:T(8,128)(2,1)S(1)}, u32[]{:S(2)}, u32[]{:S(2)}) collective-permute-start(bf16[2,2,2,256,256]{4,3,2,1,0:T(8,128)(2,1)} %get-tuple-element.84), channel_id=1, source_target_pairs={{0,1},{1,0},{2,3},{3,2},{4,5},{5,4},{6,7},{7,6},{8,9},{9,8},{10,11... | collective-permute-start | bytes 3145736 | tf_op jit(solution)/shard_map/ppermute | solution.py:691
  94.2 36.0 %collective-permute-start.21 = (bf16[2,512,256]{2,1,0:T(8,128)(2,1)S(1)}, bf16[2,512,256]{2,1,0:T(8,128)(2,1)S(1)}, u32[]{:S(2)}, u32[]{:S(2)}) collective-permute-start(bf16[2,512,256]{2,1,0:T(8,128)(2,1)S(1)} %get-tuple-element.89.refs_0_), channel_id=1, source_target_pairs={{0,8},{1,9},{2,10},{3,11},{4,0},{5,1},{6,2},{7,3},{8,12},{9,13},{1... | collective-permute-start | bytes 1572872 | tf_op jit(solution)/shard_map/ppermute | solution.py:691
  94.3 34.7 %collective-permute-start.24 = (bf16[2,512,256]{2,1,0:T(8,128)(2,1)S(1)}, bf16[2,512,256]{2,1,0:T(8,128)(2,1)S(1)}, u32[]{:S(2)}, u32[]{:S(2)}) collective-permute-start(bf16[2,512,256]{2,1,0:T(8,128)(2,1)S(1)} %get-tuple-element.92.refs_5_), channel_id=1, source_target_pairs={{0,8},{1,9},{2,10},{3,11},{4,0},{5,1},{6,2},{7,3},{8,12},{9,13},{1... | collective-permute-start | bytes 1572872 | tf_op jit(solution)/shard_map/ppermute | solution.py:691
  100.6 47.8 %copy-start.6 = (bf16[2,528,256]{2,1,0:T(8,128)(2,1)S(1)}, bf16[2,528,256]{2,1,0:T(8,128)(2,1)}, u32[]{:S(2)}) copy-start(bf16[2,528,256]{2,1,0:T(8,128)(2,1)} %copy-done.4) | copy-start | bytes 1622020
  100.6 47.8 %copy-start.9 = (bf16[2,528,256]{2,1,0:T(8,128)(2,1)S(1)}, bf16[2,528,256]{2,1,0:T(8,128)(2,1)}, u32[]{:S(2)}) copy-start(bf16[2,528,256]{2,1,0:T(8,128)(2,1)} %copy-done.7) | copy-start | bytes 1622020
  104.1 37.3 %copy-start.22 = (bf16[2,2,2,256,256]{4,3,2,1,0:T(8,128)(2,1)}, bf16[2,2,2,256,256]{4,3,2,1,0:T(8,128)(2,1)S(1)}, u32[]{:S(2)}) copy-start(bf16[2,2,2,256,256]{4,3,2,1,0:T(8,128)(2,1)S(1)} %collective-permute-done.13.refs_10_) | copy-start | bytes 3145732
  104.1 36.1 %collective-permute-start.23 = (bf16[2,512,256]{2,1,0:T(8,128)(2,1)S(1)}, bf16[2,512,256]{2,1,0:T(8,128)(2,1)S(1)}, u32[]{:S(2)}, u32[]{:S(2)}) collective-permute-start(bf16[2,512,256]{2,1,0:T(8,128)(2,1)S(1)} %get-tuple-element.92.refs_5_), channel_id=1, source_target_pairs={{0,4},{1,5},{2,6},{3,7},{4,12},{5,13},{6,14},{7,15},{8,0},{9,1},{1... | collective-permute-start | bytes 1572872 | tf_op jit(solution)/shard_map/ppermute | solution.py:691
  109.9 50.9 %collective-permute-start.20 = (bf16[2,2,256,256]{3,2,1,0:T(8,128)(2,1)}, bf16[2,2,256,256]{3,2,1,0:T(8,128)(2,1)}, u32[]{:S(2)}, u32[]{:S(2)}) collective-permute-start(bf16[2,2,256,256]{3,2,1,0:T(8,128)(2,1)} %get-tuple-element.87), channel_id=1, source_target_pairs={{0,3},{1,2},{2,1},{3,0},{4,7},{5,6},{6,5},{7,4},{8,11},{9,10},{10,... | collective-permute-start | bytes 1572872 | tf_op jit(solution)/shard_map/ppermute | solution.py:691
  129.0 31.8 %collective-permute-start.19 = (bf16[2,2,256,256]{3,2,1,0:T(8,128)(2,1)}, bf16[2,2,256,256]{3,2,1,0:T(8,128)(2,1)}, u32[]{:S(2)}, u32[]{:S(2)}) collective-permute-start(bf16[2,2,256,256]{3,2,1,0:T(8,128)(2,1)} %get-tuple-element.86), channel_id=1, source_target_pairs={{0,2},{1,3},{2,0},{3,1},{4,6},{5,7},{6,4},{7,5},{8,10},{9,11},{10,... | collective-permute-start | bytes 1572872 | tf_op jit(solution)/shard_map/ppermute | solution.py:691
  130.2 15.8 %collective-permute-start.14 = (bf16[512,256]{1,0:T(8,128)(2,1)S(1)}, bf16[512,256]{1,0:T(8,128)(2,1)S(1)}, u32[]{:S(2)}, u32[]{:S(2)}) collective-permute-start(bf16[512,256]{1,0:T(8,128)(2,1)S(1)} %slice_bitcast_fusion.7), channel_id=1, source_target_pairs={{0,4},{1,5},{2,6},{3,7},{4,12},{5,13},{6,14},{7,15},{8,0},{9,1},{1... | collective-permute-start | bytes 786440 | tf_op jit(solution)/shard_map/ppermute | solution.py:691
  140.2 20.6 %collective-permute-start.26 = (bf16[512,256]{1,0:T(8,128)(2,1)S(1)}, bf16[512,256]{1,0:T(8,128)(2,1)}, u32[]{:S(2)}, u32[]{:S(2)}) collective-permute-start(bf16[512,256]{1,0:T(8,128)(2,1)S(1)} %slice_bitcast_fusion.4), channel_id=1, source_target_pairs={{0,8},{1,9},{2,10},{3,11},{4,0},{5,1},{6,2},{7,3},{8,12},{9,13},{1... | collective-permute-start | bytes 786440 | tf_op jit(solution)/shard_map/ppermute | solution.py:691
  143.2 17.7 %collective-permute-start.22 = (bf16[512,256]{1,0:T(8,128)(2,1)S(1)}, bf16[512,256]{1,0:T(8,128)(2,1)}, u32[]{:S(2)}, u32[]{:S(2)}) collective-permute-start(bf16[512,256]{1,0:T(8,128)(2,1)S(1)} %slice_bitcast_fusion.6), channel_id=1, source_target_pairs={{0,8},{1,9},{2,10},{3,11},{4,0},{5,1},{6,2},{7,3},{8,12},{9,13},{1... | collective-permute-start | bytes 786440 | tf_op jit(solution)/shard_map/ppermute | solution.py:691
  146.0 16.2 %collective-permute-start.25 = (bf16[512,256]{1,0:T(8,128)(2,1)}, bf16[512,256]{1,0:T(8,128)(2,1)}, u32[]{:S(2)}, u32[]{:S(2)}) collective-permute-start(bf16[512,256]{1,0:T(8,128)(2,1)} %slice_bitcast_fusion.5), channel_id=1, source_target_pairs={{0,4},{1,5},{2,6},{3,7},{4,12},{5,13},{6,14},{7,15},{8,0},{9,1},{1... | collective-permute-start | bytes 786440 | tf_op jit(solution)/shard_map/ppermute | solution.py:691
  160.8 20.7 %collective-permute-start.30 = (bf16[2,2,256,256]{3,2,1,0:T(8,128)(2,1)S(1)}, bf16[2,2,256,256]{3,2,1,0:T(8,128)(2,1)S(1)}, u32[]{:S(2)}, u32[]{:S(2)}) collective-permute-start(bf16[2,2,256,256]{3,2,1,0:T(8,128)(2,1)S(1)} %get-tuple-element.105), channel_id=1, source_target_pairs={{0,1},{1,0},{2,3},{3,2},{4,5},{5,4},{6,7},{7,6},{8,9},{9,8},{10,11... | collective-permute-start | bytes 1572872 | tf_op jit(solution)/shard_map/ppermute | solution.py:691
  166.4 20.5 %collective-permute-start.27 = (bf16[2,2,256,256]{3,2,1,0:T(8,128)(2,1)S(1)}, bf16[2,2,256,256]{3,2,1,0:T(8,128)(2,1)S(1)}, u32[]{:S(2)}, u32[]{:S(2)}) collective-permute-start(bf16[2,2,256,256]{3,2,1,0:T(8,128)(2,1)S(1)} %get-tuple-element.94), channel_id=1, source_target_pairs={{0,2},{1,3},{2,0},{3,1},{4,6},{5,7},{6,4},{7,5},{8,10},{9,11},{10,... | collective-permute-start | bytes 1572872 | tf_op jit(solution)/shard_map/ppermute | solution.py:691
  178.4 15.3 %collective-permute-start.33 = (f32[2,128]{1,0:T(2,128)S(1)}, f32[2,128]{1,0:T(2,128)S(1)}, u32[]{:S(2)}, u32[]{:S(2)}) collective-permute-start(f32[2,128]{1,0:T(2,128)S(1)} %get-tuple-element.113), channel_id=1, source_target_pairs={{0,4},{1,5},{2,6},{3,7},{4,12},{5,13},{6,14},{7,15},{8,0},{9,1},{1... | collective-permute-start | bytes 3080 | tf_op jit(solution)/shard_map/ppermute | solution.py:691
  180.5 15.2 %collective-permute-start.29 = (bf16[2,2,256,256]{3,2,1,0:T(8,128)(2,1)S(1)}, bf16[2,2,256,256]{3,2,1,0:T(8,128)(2,1)S(1)}, u32[]{:S(2)}, u32[]{:S(2)}) collective-permute-start(bf16[2,2,256,256]{3,2,1,0:T(8,128)(2,1)S(1)} %get-tuple-element.102), channel_id=1, source_target_pairs={{0,1},{1,0},{2,3},{3,2},{4,5},{5,4},{6,7},{7,6},{8,9},{9,8},{10,11... | collective-permute-start | bytes 1572872 | tf_op jit(solution)/shard_map/ppermute | solution.py:691
  180.5 17.4 %collective-permute-start.28 = (bf16[2,2,256,256]{3,2,1,0:T(8,128)(2,1)S(1)}, bf16[2,2,256,256]{3,2,1,0:T(8,128)(2,1)S(1)}, u32[]{:S(2)}, u32[]{:S(2)}) collective-permute-start(bf16[2,2,256,256]{3,2,1,0:T(8,128)(2,1)S(1)} %get-tuple-element.98), channel_id=1, source_target_pairs={{0,3},{1,2},{2,1},{3,0},{4,7},{5,6},{6,5},{7,4},{8,11},{9,10},{10,... | collective-permute-start | bytes 1572872 | tf_op jit(solution)/shard_map/ppermute | solution.py:691
  181.5 12.2 %collective-permute-start.31 = (f32[2,128]{1,0:T(2,128)S(1)}, f32[2,128]{1,0:T(2,128)S(1)}, u32[]{:S(2)}, u32[]{:S(2)}) collective-permute-start(f32[2,128]{1,0:T(2,128)S(1)} %get-tuple-element.108), channel_id=1, source_target_pairs={{0,12},{1,13},{2,14},{3,15},{4,8},{5,9},{6,10},{7,11},{8,4},{9,5},... | collective-permute-start | bytes 3080 | tf_op jit(solution)/shard_map/ppermute | solution.py:691
  186.9 6.8 %collective-permute-start.32 = (f32[2,128]{1,0:T(2,128)S(1)}, f32[2,128]{1,0:T(2,128)S(1)}, u32[]{:S(2)}, u32[]{:S(2)}) collective-permute-start(f32[2,128]{1,0:T(2,128)S(1)} %get-tuple-element.109), channel_id=1, source_target_pairs={{0,8},{1,9},{2,10},{3,11},{4,0},{5,1},{6,2},{7,3},{8,12},{9,13},{1... | collective-permute-start | bytes 3080 | tf_op jit(solution)/shard_map/ppermute | solution.py:691
  193.8 6.2 %collective-permute-start.34 = (f32[2,32]{1,0:T(2,128)S(1)}, f32[2,32]{1,0:T(2,128)S(1)}, u32[]{:S(2)}, u32[]{:S(2)}) collective-permute-start(f32[2,32]{1,0:T(2,128)S(1)} %get-tuple-element.110), channel_id=1, source_target_pairs={{0,1},{1,0},{2,3},{3,2},{4,5},{5,4},{6,7},{7,6},{8,9},{9,8},{10,11... | collective-permute-start | bytes 776 | tf_op jit(solution)/shard_map/ppermute | solution.py:691
  193.8 6.1 %collective-permute-start.35 = (f32[2,32]{1,0:T(2,128)S(1)}, f32[2,32]{1,0:T(2,128)S(1)}, u32[]{:S(2)}, u32[]{:S(2)}) collective-permute-start(f32[2,32]{1,0:T(2,128)S(1)} %get-tuple-element.111), channel_id=1, source_target_pairs={{0,2},{1,3},{2,0},{3,1},{4,6},{5,7},{6,4},{7,5},{8,10},{9,11},{10,... | collective-permute-start | bytes 776 | tf_op jit(solution)/shard_map/ppermute | solution.py:691
  193.9 6.1 %collective-permute-start.36 = (f32[2,32]{1,0:T(2,128)S(1)}, f32[2,32]{1,0:T(2,128)S(1)}, u32[]{:S(2)}, u32[]{:S(2)}) collective-permute-start(f32[2,32]{1,0:T(2,128)S(1)} %get-tuple-element.116), channel_id=1, source_target_pairs={{0,3},{1,2},{2,1},{3,0},{4,7},{5,6},{6,5},{7,4},{8,11},{9,10},{10,... | collective-permute-start | bytes 776 | tf_op jit(solution)/shard_map/ppermute | solution.py:691
  (43 other events, 277.9 us)

commit v11 on v9

--- a/solution.py
+++ b/solution.py
@@ -133,7 +133,7 @@
 
 
 def full(array):
-    return pl.BlockSpec(array.shape, lambda *_: (0,) * array.ndim)
+    return pl.BlockSpec(array.shape, lambda *_: (0,) * len(array.shape))
 
 
 def build_factors(
@@ -142,7 +142,6 @@
     slots, _, antennas = antenna_uvw.shape
     per_group = slot_ids[2]
     index = slot_ids[0]
-    whole = pl.BlockSpec(memory_space=pltpu.VMEM)
     operands, in_specs, sets = [], [], []
     if beam is not None:
         operands.append(beam)
@@ -159,8 +158,11 @@
     in_specs += [full(array) for array in operands[len(in_specs) :]]
     in_specs.append(pl.BlockSpec((1, 3, antennas), lambda n, tab: (tab[0] + index, 0, 0)))
     count = beams * per_group
-    shapes = [
-        (2, len(piece) * count + (0 if n else bright_rows), span) for n, piece in enumerate(pieces)
+    made = [
+        jax.ShapeDtypeStruct(
+            (2, len(piece) * count + (0 if n else bright_rows), span), jnp.bfloat16
+        )
+        for n, piece in enumerate(pieces)
     ]
     return pl.pallas_call(
         functools.partial(build_kernel, sets, slot_ids, pieces, bright_rows, small_width),
@@ -168,11 +170,11 @@
             num_scalar_prefetch=1,
             grid=(1,),
             in_specs=in_specs,
-            out_specs=[whole] * len(pieces),
+            out_specs=[full(array) for array in made],
             scratch_shapes=[pltpu.VMEM((SMALL_ROWS, small_width), jnp.float32)],
         ),
-        out_shape=[jax.ShapeDtypeStruct(shape, jnp.bfloat16) for shape in shapes],
-        compiler_params=pltpu.CompilerParams(vmem_limit_bytes=40 * 1024 * 1024),
+        out_shape=made,
+        compiler_params=pltpu.CompilerParams(vmem_limit_bytes=61 * 1024 * 1024),
         cost_estimate=LITTLE,
         name="build_factors",
     )(table, *operands, antenna_uvw)
@@ -208,7 +210,7 @@
     _, _, per_group, antennas = beam.shape
     smalls = small or ()
     rows = 2 * per_group + (SMALL_ROWS if smalls else 0)
-    whole = pl.BlockSpec(memory_space=pltpu.VMEM)
+    made = [jax.ShapeDtypeStruct((rows, antennas), jnp.bfloat16) for _ in others]
     scratch = []
     if smalls:
         scratch.append(pltpu.VMEM((SMALL_ROWS, smalls[0].shape[1]), jnp.float32))
@@ -224,10 +226,11 @@
                 for m in others
             ]
             + [full(array) for array in smalls],
-            out_specs=[whole for _ in others],
+            out_specs=[full(array) for array in made],
             scratch_shapes=scratch,
         ),
-        out_shape=[jax.ShapeDtypeStruct((rows, antennas), jnp.bfloat16) for _ in others],
+        out_shape=made,
+        compiler_params=pltpu.CompilerParams(vmem_limit_bytes=61 * 1024 * 1024),
         cost_estimate=LITTLE,
         name="messages_for",
     )(table, *[beam] * len(others), *smalls)
@@ -264,6 +267,7 @@
             ],
         ),
         out_shape=[jax.ShapeDtypeStruct(shape, array.dtype) for _ in starts],
+        compiler_params=pltpu.CompilerParams(vmem_limit_bytes=61 * 1024 * 1024),
         cost_estimate=LITTLE,
         name="slices_for",
     )(table, *[array] * len(starts))
@@ -491,7 +495,7 @@
             ],
         ),
         out_shape=out_shapes,
-        compiler_params=pltpu.CompilerParams(vmem_limit_bytes=48 * 1024 * 1024),
+        compiler_params=pltpu.CompilerParams(vmem_limit_bytes=61 * 1024 * 1024),
         cost_estimate=LITTLE,
         name="unit_work",
     )(*operands)
@@ -528,7 +532,7 @@
         ),
         out_shape=jax.ShapeDtypeStruct(shape, jnp.bfloat16),
         input_output_aliases=aliases,
-        compiler_params=pltpu.CompilerParams(vmem_limit_bytes=32 * 1024 * 1024),
+        compiler_params=pltpu.CompilerParams(vmem_limit_bytes=61 * 1024 * 1024),
         cost_estimate=LITTLE,
         name="put_residuals",
     )(*operands)
@@ -641,38 +645,40 @@
 WORK, HOME, PUT, LATER_WORK, LATER_HOME, PUT_NEAR, PUT_LAST = 32, 35, 38, 40, 43, 46, 47
 SUM_PLANES, SUM_PLANE = 48, 51
 GATES = {
-    3: (0, 1),
+    3: (0,),
     5: (0, 2),
-    6: (1, 11),
+    6: (1,),
     7: (1, 2),
-    14: (11, 13),
-    17: (1,),
+    14: (13,),
     19: (2, 18),
-    20: (3, 4, 7, 16, 17),
+    20: (17, 14, 7),
     21: (3, 4, 5, 13, 14, 16, 17),
-    23: (17, 4),
-    24: (9, 17),
-    25: (9, 23, 6, 17),
-    26: (9,),
+    23: (4,),
+    24: (16, 9, 17),
+    25: (6, 9, 16, 17, 18, 23),
+    26: (16, 9),
     27: (8,),
-    28: (22,),
-    31: (25, 26, 27, 37),
+    28: (9, 22),
+    31: (8, 25, 27, 37),
     33: (32, 25, 23),
-    35: (8, 9, 22, 24, 25, 26, 28, 29),
-    40: (33, 36, 37, 28, 29, 30, 31),
-    49: (44,),
-    53: (35,),
-    46: (30, 31),
-    37: (32, 9),
-    38: (25,),
-    30: (26,),
+    35: (33, 8, 22, 23, 24, 25, 26, 28, 29),
+    40: (32, 33, 36, 37, 27, 28, 29, 30, 31),
+    49: (40, 36, 44),
+    38: (24, 25),
+    30: (8, 26),
     43: (32,),
-    44: (26, 27, 30, 31),
-    36: (8, 9),
+    44: (26, 30, 31),
+    36: (8, 9, 32),
     4: (0,),
-    16: (0,),
     13: (0,),
-    41: (40,),
+    41: (40, 33),
+    48: (35,),
+    51: (49, 31),
+    9: (17,),
+    50: (35, 30, 31),
+    45: (40, 36),
+    52: (48,),
+    29: (9, 28),
 }
 
 

time: 206 us -> 212 us (1.029)
  Pallas kernels: 55.9 us -> 73.1 us
  starting transfers between devices: 66.2 us -> 56.8 us
  local copies, waits for them, and re-layouts: 19 us -> 15.4 us
    ppermute x37, starting transfers between devices: 66.2 us -> 56.8 us  [send(): done[step] = lax.ppermute(gated(step, value), 'tile', pairs)]
    pallas_call x4, Pallas kernels: 28.5 us -> 37.1 us  [unit_work(): pl.pallas_call(functools.partial(unit_kernel, index, offset, kinds, brigh...]
    unnamed x87 -> x55, local copies, waits for them, and re-layouts: 15 us -> 7.4 us
    pallas_call x3, Pallas kernels: 6.75 us -> 12.3 us  [build_factors(): pl.pallas_call(functools.partial(build_kernel, sets, slot_ids, pieces, br...]
    pallas_call x3, Pallas kernels: 8.94 us -> 12.2 us  [put_residuals(): pl.pallas_call(functools.partial(put_kernel, sources), grid_spec=pltpu.Pr...]
    squeeze x4, local copies, waits for them, and re-layouts: 0.81 us -> 3.21 us  [far(): sides[0][0]]
  transfers between devices with their start and end apart: 37 -> 37, of which waited for: 13 -> 10; matrix products, arithmetic and copies ran while one was open for 2% -> 5% of each run, Pallas kernels for 23% -> 32%
where the time goes in v11:
time: 212 us; the launch traced here: 211 us
  Pallas kernels  73.1 us (34%)
  waiting for transfers between devices  61.1 us (29%)
  starting transfers between devices  56.8 us (27%)
  local copies, waits for them, and re-layouts  15.4 us (7%)
  other arithmetic  3.33 us (2%)
    ppermute x37, waiting for transfers between devices, send(): done[step] = lax.ppermute(gated(step, value), 'tile', pairs)  61.1 us
    ppermute x37, starting transfers between devices, send(): done[step] = lax.ppermute(gated(step, value), 'tile', pairs)  56.8 us
    pallas_call x4, Pallas kernels, unit_work(): pl.pallas_call(functools.partial(unit_kernel, index, offset, kinds, brigh...  37.1 us
    pallas_call x3, Pallas kernels, build_factors(): pl.pallas_call(functools.partial(build_kernel, sets, slot_ids, pieces, br...  12.3 us
    pallas_call x3, Pallas kernels, put_residuals(): pl.pallas_call(functools.partial(put_kernel, sources), grid_spec=pltpu.Pr...  12.2 us
    pallas_call x3, Pallas kernels, messages_for(): pl.pallas_call(functools.partial(message_kernel, len(others), bool(smalls...  7.71 us
    unnamed x55, local copies, waits for them, and re-layouts  7.4 us
  transfers between devices with their start and end apart: 37, of which 10 were waited for; matrix products, arithmetic and copies ran while one was open for 5% of the time, Pallas kernels for 32%

profile of v11, /device:TPU:0, one launch (start us, length us, event | category | flops | bytes accessed | tf_op | source)
XLA Modules:
  0.0 210.7 jit_solution(1126386788865877646)
XLA Ops:
  0.6 1.2 broadcast_in_dim.34
  1.9 1.3 constant_dynamic-slice_fusion
  3.1 2.4 %messages_for.3 = bf16[80,2048]{1,0:T(8,128)(2,1)} custom-call(s32[148]{0:T(256)} %bitcast.24, bf16[8,2,32,2048]{3,2,1,0:T(8,128)(2,1)} %refs_0_.11, f32[2,256]{1,0:T(2,128)} %refs_4_.5, f32[1,256]{1,0:T(1,128)} %bitcast.38, s32[8,32]{1,0:T(8,128)} %refs_6_.1), custom_call_target="tpu_custom_call" | custom-call | flops 1 | bytes 1 | tf_op jit(solution)/shard_map/messages_for/pallas_call | solution.py:217
  6.0 1.8 copy.15.refs_5_.refs_2_.refs_10_
  8.5 3.7 %build_factors.3.refs_0_ = bf16[2,528,256]{2,1,0:T(8,128)(2,1)} custom-call(s32[148]{0:T(256)} %bitcast.25, bf16[8,2,32,2048]{3,2,1,0:T(8,128)(2,1)} %refs_0_.11, bf16[80,2048]{1,0:T(8,128)(2,1)} %copy-done.9, f32[2,256]{1,0:T(2,128)} %refs_4_.5, f32[1,256]{1,0:T(1,128)} %bitcast.39, s32[8,32]{1,0:T(8,128)} %refs_6_.1, ...), custom_call_target="tpu_custom_call" | custom-call | flops 1 | bytes 1 | tf_op jit(solution)/shard_map/build_factors/pallas_call | solution.py:167
  12.2 2.6 %collective-permute-start.1 = (bf16[2,528,256]{2,1,0:T(8,128)(2,1)}, bf16[2,528,256]{2,1,0:T(8,128)(2,1)S(1)}, u32[]{:S(2)}, u32[]{:S(2)}) collective-permute-start(bf16[2,528,256]{2,1,0:T(8,128)(2,1)} %build_factors.3.refs_0_), channel_id=1, source_target_pairs={{0,4},{1,5},{2,6},{3,7},{4,12},{5,13},{6,14},{7,15},{8,0},{9,1},{1... | collective-permute-start | bytes 1622024 | tf_op jit(solution)/shard_map/ppermute | solution.py:701
  14.8 2.6 %messages_for.4 = (bf16[80,2048]{1,0:T(8,128)(2,1)}, bf16[80,2048]{1,0:T(8,128)(2,1)}) custom-call(s32[148]{0:T(256)} %bitcast.26, bf16[8,2,32,2048]{3,2,1,0:T(8,128)(2,1)} %refs_0_.11, bf16[8,2,32,2048]{3,2,1,0:T(8,128)(2,1)} %refs_0_.11, f32[2,256]{1,0:T(2,128)} %refs_4_.5, f32[1,256]{1,0:T(1,128)} %bitcast.40, s32[8,32]{1,0:T(8,128)} %refs_6_.1), custom_call_target="tpu_custom_call" | custom-call | flops 1 | bytes 1 | tf_op jit(solution)/shard_map/messages_for/pallas_call | solution.py:217
  17.4 1.5 collective-permute-start.5
  19.0 1.3 collective-permute-start.2
  20.3 2.7 %messages_for.5 = (bf16[64,2048]{1,0:T(8,128)(2,1)}, bf16[64,2048]{1,0:T(8,128)(2,1)}, bf16[64,2048]{1,0:T(8,128)(2,1)}) custom-call(s32[148]{0:T(256)} %bitcast.27, bf16[8,2,32,2048]{3,2,1,0:T(8,128)(2,1)} %refs_0_.11, bf16[8,2,32,2048]{3,2,1,0:T(8,128)(2,1)} %refs_0_.11, bf16[8,2,32,2048]{3,2,1,0:T(8,128)(2,1)} %refs_0_.11), custom_call_target="tpu_custom_call" | custom-call | flops 1 | bytes 1 | tf_op jit(solution)/shard_map/messages_for/pallas_call | solution.py:217
  23.0 5.2 %collective-permute-done.5.refs_0_.refs_8_ = bf16[80,2048]{1,0:T(8,128)(2,1)S(1)} collective-permute-done((bf16[80,2048]{1,0:T(8,128)(2,1)}, bf16[80,2048]{1,0:T(8,128)(2,1)S(1)}, u32[]{:S(2)}, u32[]{:S(2)}) %collective-permute-start.5) | collective-permute-done | bytes 327712 | tf_op jit(solution)/shard_map/ppermute | solution.py:701
  29.9 12.4 %collective-permute-start.3 = (bf16[528,256]{1,0:T(8,128)(2,1)}, bf16[528,256]{1,0:T(8,128)(2,1)}, u32[]{:S(2)}, u32[]{:S(2)}) collective-permute-start(bf16[528,256]{1,0:T(8,128)(2,1)} %slice_bitcast_fusion.3), channel_id=1, source_target_pairs={{0,4},{1,5},{2,6},{3,7},{4,12},{5,13},{6,14},{7,15},{8,0},{9,1},{1... | collective-permute-start | bytes 811016 | tf_op jit(solution)/shard_map/ppermute | solution.py:701
  43.0 1.5 collective-permute-start.10
  45.3 3.6 %build_factors.4.refs_5_ = bf16[2,528,256]{2,1,0:T(8,128)(2,1)} custom-call(s32[148]{0:T(256)} %bitcast.28, bf16[80,2048]{1,0:T(8,128)(2,1)} %copy-done.10, bf16[80,2048]{1,0:T(8,128)(2,1)} %copy-done.11, f32[8,3,2048]{2,1,0:T(4,128)} %copy.15.refs_5_.refs_2_.refs_10_), custom_call_target="tpu_custom_call" | custom-call | flops 1 | bytes 1 | tf_op jit(solution)/shard_map/build_factors/pallas_call | solution.py:167
  48.9 3.3 %collective-permute-start.8 = (bf16[2,528,256]{2,1,0:T(8,128)(2,1)}, bf16[2,528,256]{2,1,0:T(8,128)(2,1)S(1)}, u32[]{:S(2)}, u32[]{:S(2)}) collective-permute-start(bf16[2,528,256]{2,1,0:T(8,128)(2,1)} %build_factors.4.refs_5_), channel_id=1, source_target_pairs={{0,8},{1,9},{2,10},{3,11},{4,0},{5,1},{6,2},{7,3},{8,12},{9,13},{1... | collective-permute-start | bytes 1622024 | tf_op jit(solution)/shard_map/ppermute | solution.py:701
  52.2 3.8 %slices_for.1 = (bf16[2,2,2,256,256]{4,3,2,1,0:T(8,128)(2,1)}, bf16[2,2,2,256,256]{4,3,2,1,0:T(8,128)(2,1)}, bf16[2,2,2,256,256]{4,3,2,1,0:T(8,128)(2,1)}) custom-call(s32[148]{0:T(256)} %bitcast.29, bf16[2,8,2,256,256]{4,3,2,1,0:T(8,128)(2,1)} %refs_12_.3, bf16[2,8,2,256,256]{4,3,2,1,0:T(8,128)(2,1)} %refs_12_.3, bf16[2,8,2,256,256]{4,3,2,1,0:T(8,128)(2,1)} %refs_12_.3), custom_call_target="tpu_custom_call" | custom-call | flops 1 | bytes 1 | tf_op jit(solution)/shard_map/slices_for/pallas_call | solution.py:249
  57.2 9.6 %collective-permute-done.8.refs_7_ = bf16[2,528,256]{2,1,0:T(8,128)(2,1)S(1)} collective-permute-done((bf16[2,528,256]{2,1,0:T(8,128)(2,1)}, bf16[2,528,256]{2,1,0:T(8,128)(2,1)S(1)}, u32[]{:S(2)}, u32[]{:S(2)}) %collective-permute-start.8) | collective-permute-done | bytes 540704 | tf_op jit(solution)/shard_map/ppermute | solution.py:701
  67.6 3.3 %collective-permute-start.11 = (bf16[528,256]{1,0:T(8,128)(2,1)}, bf16[528,256]{1,0:T(8,128)(2,1)S(1)}, u32[]{:S(2)}, u32[]{:S(2)}) collective-permute-start(bf16[528,256]{1,0:T(8,128)(2,1)} %slice_bitcast_fusion), channel_id=1, source_target_pairs={{0,8},{1,9},{2,10},{3,11},{4,0},{5,1},{6,2},{7,3},{8,12},{9,13},{1... | collective-permute-start | bytes 811016 | tf_op jit(solution)/shard_map/ppermute | solution.py:701
  70.9 10.7 %collective-permute-done.7.refs_6_ = bf16[2,528,256]{2,1,0:T(8,128)(2,1)S(1)} collective-permute-done((bf16[2,528,256]{2,1,0:T(8,128)(2,1)S(1)}, bf16[2,528,256]{2,1,0:T(8,128)(2,1)S(1)}, u32[]{:S(2)}, u32[]{:S(2)}) %collective-permute-start.7) | collective-permute-done | bytes 540704 | tf_op jit(solution)/shard_map/ppermute | solution.py:701
  83.0 4.6 %collective-permute-start.9 = (bf16[528,256]{1,0:T(8,128)(2,1)}, bf16[528,256]{1,0:T(8,128)(2,1)}, u32[]{:S(2)}, u32[]{:S(2)}) collective-permute-start(bf16[528,256]{1,0:T(8,128)(2,1)} %slice_bitcast_fusion.1), channel_id=1, source_target_pairs={{0,4},{1,5},{2,6},{3,7},{4,12},{5,13},{6,14},{7,15},{8,0},{9,1},{1... | collective-permute-start | bytes 811016 | tf_op jit(solution)/shard_map/ppermute | solution.py:701
  87.6 5.0 %build_factors.5 = (bf16[2,512,256]{2,1,0:T(8,128)(2,1)}, bf16[2,512,256]{2,1,0:T(8,128)(2,1)}) custom-call(s32[148]{0:T(256)} %bitcast.30, bf16[8,2,32,2048]{3,2,1,0:T(8,128)(2,1)} %refs_0_.11, bf16[64,2048]{1,0:T(8,128)(2,1)} %collective-permute-done.13.refs_1_, bf16[64,2048]{1,0:T(8,128)(2,1)} %collective-permute-done.10.refs_2_, ...), custom_call_target="tpu_custom_call" | custom-call | flops 1 | bytes 1 | tf_op jit(solution)/shard_map/build_factors/pallas_call | solution.py:167
  92.7 3.4 %collective-permute-start.21 = (bf16[2,512,256]{2,1,0:T(8,128)(2,1)}, bf16[2,512,256]{2,1,0:T(8,128)(2,1)S(1)}, u32[]{:S(2)}, u32[]{:S(2)}) collective-permute-start(bf16[2,512,256]{2,1,0:T(8,128)(2,1)} %get-tuple-element.90.refs_0_), channel_id=1, source_target_pairs={{0,4},{1,5},{2,6},{3,7},{4,12},{5,13},{6,14},{7,15},{8,0},{9,1},{1... | collective-permute-start | bytes 1572872 | tf_op jit(solution)/shard_map/ppermute | solution.py:701
  96.1 1.4 collective-permute-start.15
  98.8 6.6 %unit_work.4 = (bf16[2,2,256,256]{3,2,1,0:T(8,128)(2,1)}, f32[1,512]{1,0:T(1,128)}, f32[2,512,128]{2,1,0:T(8,128)}) custom-call(s32[148]{0:T(256)} %bitcast.31, bf16[2,528,256]{2,1,0:T(8,128)(2,1)} %build_factors.3.refs_0_, bf16[2,528,256]{2,1,0:T(8,128)(2,1)} %copy-done.4, bf16[2,528,256]{2,1,0:T(8,128)(2,1)} %copy-done.5, ...), custom_call_target="tpu_custom_call" | custom-call | flops 1 | bytes 1 | tf_op jit(solution)/shard_map/unit_work/pallas_call | solution.py:483
  105.3 14.7 %collective-permute-done.21.refs_1_ = bf16[2,512,256]{2,1,0:T(8,128)(2,1)S(1)} collective-permute-done((bf16[2,512,256]{2,1,0:T(8,128)(2,1)}, bf16[2,512,256]{2,1,0:T(8,128)(2,1)S(1)}, u32[]{:S(2)}, u32[]{:S(2)}) %collective-permute-start.21) | collective-permute-done | bytes 524320 | tf_op jit(solution)/shard_map/ppermute | solution.py:701
  120.8 1.5 collective-permute-start.18
  122.4 2.0 collective-permute-start.22
  124.3 1.0 copy-done.3
  125.3 12.0 %unit_work.5 = (bf16[2,2,256,256]{3,2,1,0:T(8,128)(2,1)}, bf16[2,2,256,256]{3,2,1,0:T(8,128)(2,1)}, bf16[2,2,256,256]{3,2,1,0:T(8,128)(2,1)}, f32[1,512]{1,0:T(1,128)}) custom-call(s32[148]{0:T(256)} %bitcast.32, bf16[2,528,256]{2,1,0:T(8,128)(2,1)} %build_factors.3.refs_0_, bf16[2,528,256]{2,1,0:T(8,128)(2,1)} %copy-done.4, bf16[2,528,256]{2,1,0:T(8,128)(2,1)} %copy-done.5, ...), custom_call_target="tpu_custom_call" | custom-call | flops 1 | bytes 1 | tf_op jit(solution)/shard_map/unit_work/pallas_call | solution.py:483
  137.4 5.1 %collective-permute-done.24.refs_6_ = bf16[2,512,256]{2,1,0:T(8,128)(2,1)} collective-permute-done((bf16[2,512,256]{2,1,0:T(8,128)(2,1)}, bf16[2,512,256]{2,1,0:T(8,128)(2,1)}, u32[]{:S(2)}, u32[]{:S(2)}) %collective-permute-start.24) | collective-permute-done | bytes 524320 | tf_op jit(solution)/shard_map/ppermute | solution.py:701
  142.6 1.0 slice_bitcast_fusion.5
  143.6 1.0 slice_bitcast_fusion.6
  144.6 3.6 %collective-permute-done.22.refs_3_ = bf16[512,256]{1,0:T(8,128)(2,1)S(1)} collective-permute-done((bf16[512,256]{1,0:T(8,128)(2,1)}, bf16[512,256]{1,0:T(8,128)(2,1)S(1)}, u32[]{:S(2)}, u32[]{:S(2)}) %collective-permute-start.22) | collective-permute-done | bytes 262176 | tf_op jit(solution)/shard_map/ppermute | solution.py:701
  148.6 1.0 slice_bitcast_fusion.4
  149.5 1.4 collective-permute-done.19.refs_1_
  150.9 1.6 collective-permute-start.26
  152.6 6.8 %collective-permute-done.23.refs_4_ = bf16[512,256]{1,0:T(8,128)(2,1)S(1)} collective-permute-done((bf16[512,256]{1,0:T(8,128)(2,1)S(1)}, bf16[512,256]{1,0:T(8,128)(2,1)S(1)}, u32[]{:S(2)}, u32[]{:S(2)}) %collective-permute-start.23) | collective-permute-done | bytes 262176 | tf_op jit(solution)/shard_map/ppermute | solution.py:701
  159.3 3.1 %collective-permute-done.26.refs_9_ = bf16[512,256]{1,0:T(8,128)(2,1)S(1)} collective-permute-done((bf16[512,256]{1,0:T(8,128)(2,1)S(1)}, bf16[512,256]{1,0:T(8,128)(2,1)S(1)}, u32[]{:S(2)}, u32[]{:S(2)}) %collective-permute-start.26) | collective-permute-done | bytes 262176 | tf_op jit(solution)/shard_map/ppermute | solution.py:701
  163.2 6.3 %unit_work.6 = (bf16[2,2,256,256]{3,2,1,0:T(8,128)(2,1)}, f32[1,512]{1,0:T(1,128)}) custom-call(s32[148]{0:T(256)} %bitcast.33, bf16[2,512,256]{2,1,0:T(8,128)(2,1)} %get-tuple-element.90.refs_0_, bf16[2,512,256]{2,1,0:T(8,128)(2,1)} %copy-done.8, bf16[2,512,256]{2,1,0:T(8,128)(2,1)} %collective-permute-done.15.refs_2_, bf16[512,256]{1,0:T(8,128)(2,1)} %copy-done.13, ...), custom_call_target="tpu_custom_call" | custom-call | flops 1 | bytes 1 | tf_op jit(solution)/shard_map/unit_work/pallas_call | solution.py:483
  169.5 1.6 collective-permute-start.27
  171.1 12.1 %unit_work.7 = (bf16[2,2,256,256]{3,2,1,0:T(8,128)(2,1)}, bf16[2,2,256,256]{3,2,1,0:T(8,128)(2,1)}, bf16[2,2,256,256]{3,2,1,0:T(8,128)(2,1)}, f32[1,512]{1,0:T(1,128)}) custom-call(s32[148]{0:T(256)} %bitcast.34, bf16[2,512,256]{2,1,0:T(8,128)(2,1)} %get-tuple-element.90.refs_0_, bf16[2,512,256]{2,1,0:T(8,128)(2,1)} %copy-done.8, ...), custom_call_target="tpu_custom_call" | custom-call | flops 1 | bytes 1 | tf_op jit(solution)/shard_map/unit_work/pallas_call | solution.py:483
  184.6 1.8 collective-permute-start.33
  186.4 5.7 %collective-permute-start.31 = (f32[2,128]{1,0:T(2,128)S(1)}, f32[2,128]{1,0:T(2,128)S(1)}, u32[]{:S(2)}, u32[]{:S(2)}) collective-permute-start(f32[2,128]{1,0:T(2,128)S(1)} %get-tuple-element.111), channel_id=1, source_target_pairs={{0,12},{1,13},{2,14},{3,15},{4,8},{5,9},{6,10},{7,11},{8,4},{9,5},... | collective-permute-start | bytes 3080 | tf_op jit(solution)/shard_map/ppermute | solution.py:701
  192.1 1.9 collective-permute-start.32
  194.2 5.3 %put_residuals.3.refs_2_ = bf16[2,8,2,256,256]{4,3,2,1,0:T(8,128)(2,1)} custom-call(s32[148]{0:T(256)} %bitcast.35, bf16[2,2,256,256]{3,2,1,0:T(8,128)(2,1)} %collective-permute-done.18.refs_0_, bf16[2,2,256,256]{3,2,1,0:T(8,128)(2,1)} %copy-done.20, bf16[2,2,256,256]{3,2,1,0:T(8,128)(2,1)} %copy-done.21, bf16[2,2,256,256]{3,2,1,0:T(8,128)(2,1)} %get-tuple-element.109.refs_3_), custom_call_target="tpu_custom_call" | custom-call | flops 1 | bytes 1 | tf_op jit(solution)/shard_map/put_residuals/pallas_call | solution.py:522
  200.4 1.1 collective-permute-start.34
  202.2 3.5 %put_residuals.4.refs_2_ = bf16[2,8,2,256,256]{4,3,2,1,0:T(8,128)(2,1)} custom-call(s32[148]{0:T(256)} %bitcast.36, bf16[2,2,256,256]{3,2,1,0:T(8,128)(2,1)} %copy-done.19, bf16[2,2,256,256]{3,2,1,0:T(8,128)(2,1)} %get-tuple-element.105.refs_1_, bf16[2,8,2,256,256]{4,3,2,1,0:T(8,128)(2,1)} %put_residuals.3.refs_2_), custom_call_target="tpu_custom_call", output_to_operand_aliasing={{}: (3, {})} | custom-call | flops 1 | bytes 1 | tf_op jit(solution)/shard_map/put_residuals/pallas_call | solution.py:522
  206.5 3.5 %put_residuals.5 = bf16[2,8,2,256,256]{4,3,2,1,0:T(8,128)(2,1)} custom-call(s32[148]{0:T(256)} %bitcast.37, bf16[2,2,256,256]{3,2,1,0:T(8,128)(2,1)} %copy-done.17, bf16[2,2,256,256]{3,2,1,0:T(8,128)(2,1)} %copy-done.18, bf16[2,8,2,256,256]{4,3,2,1,0:T(8,128)(2,1)} %put_residuals.4.refs_2_), custom_call_target="tpu_custom_call", output_to_operand_aliasing={{}: (3, {})} | custom-call | flops 1 | bytes 1 | tf_op jit(solution)/shard_map/put_residuals/pallas_call | solution.py:522
  (117 shorter events, 15.8 us)
Async XLA Ops:
  5.5 2.2 %collective-permute-start = (bf16[80,2048]{1,0:T(8,128)(2,1)}, bf16[80,2048]{1,0:T(8,128)(2,1)S(1)}, u32[]{:S(2)}, u32[]{:S(2)}) collective-permute-start(bf16[80,2048]{1,0:T(8,128)(2,1)} %messages_for.3), channel_id=1, source_target_pairs={{0,1},{1,0},{2,3},{3,2},{4,5},{5,4},{6,7},{7,6},{8,9},{9,8},{10,11... | collective-permute-start | bytes 983048 | tf_op jit(solution)/shard_map/ppermute | solution.py:701
  12.2 16.9 %collective-permute-start.1 = (bf16[2,528,256]{2,1,0:T(8,128)(2,1)}, bf16[2,528,256]{2,1,0:T(8,128)(2,1)S(1)}, u32[]{:S(2)}, u32[]{:S(2)}) collective-permute-start(bf16[2,528,256]{2,1,0:T(8,128)(2,1)} %build_factors.3.refs_0_), channel_id=1, source_target_pairs={{0,4},{1,5},{2,6},{3,7},{4,12},{5,13},{6,14},{7,15},{8,0},{9,1},{1... | collective-permute-start | bytes 1622024 | tf_op jit(solution)/shard_map/ppermute | solution.py:701
  17.4 10.8 %collective-permute-start.5 = (bf16[80,2048]{1,0:T(8,128)(2,1)}, bf16[80,2048]{1,0:T(8,128)(2,1)S(1)}, u32[]{:S(2)}, u32[]{:S(2)}) collective-permute-start(bf16[80,2048]{1,0:T(8,128)(2,1)} %get-tuple-element.63), channel_id=1, source_target_pairs={{0,2},{1,3},{2,0},{3,1},{4,6},{5,7},{6,4},{7,5},{8,10},{9,11},{10,... | collective-permute-start | bytes 983048 | tf_op jit(solution)/shard_map/ppermute | solution.py:701
  19.0 23.3 %collective-permute-start.2 = (bf16[2,528,256]{2,1,0:T(8,128)(2,1)S(1)}, bf16[2,528,256]{2,1,0:T(8,128)(2,1)S(1)}, u32[]{:S(2)}, u32[]{:S(2)}) collective-permute-start(bf16[2,528,256]{2,1,0:T(8,128)(2,1)S(1)} %copy-done), channel_id=1, source_target_pairs={{0,8},{1,9},{2,10},{3,11},{4,0},{5,1},{6,2},{7,3},{8,12},{9,13},{1... | collective-permute-start | bytes 1622024 | tf_op jit(solution)/shard_map/ppermute | solution.py:701
  23.0 25.9 %collective-permute-start.12 = (bf16[64,2048]{1,0:T(8,128)(2,1)}, bf16[64,2048]{1,0:T(8,128)(2,1)}, u32[]{:S(2)}, u32[]{:S(2)}) collective-permute-start(bf16[64,2048]{1,0:T(8,128)(2,1)} %get-tuple-element.70), channel_id=1, source_target_pairs={{0,3},{1,2},{2,1},{3,0},{4,7},{5,6},{6,5},{7,4},{8,11},{9,10},{10,... | collective-permute-start | bytes 786440 | tf_op jit(solution)/shard_map/ppermute | solution.py:701
  28.2 16.4 %copy-start.10 = (bf16[80,2048]{1,0:T(8,128)(2,1)}, bf16[80,2048]{1,0:T(8,128)(2,1)S(1)}, u32[]{:S(2)}) copy-start(bf16[80,2048]{1,0:T(8,128)(2,1)S(1)} %collective-permute-done.5.refs_0_.refs_8_) | copy-start | bytes 983044
  28.2 16.3 %collective-permute-start.6 = (bf16[80,2048]{1,0:T(8,128)(2,1)S(1)}, bf16[80,2048]{1,0:T(8,128)(2,1)S(1)}, u32[]{:S(2)}, u32[]{:S(2)}) collective-permute-start(bf16[80,2048]{1,0:T(8,128)(2,1)S(1)} %copy-done.26), channel_id=1, source_target_pairs={{0,3},{1,2},{2,1},{3,0},{4,7},{5,6},{6,5},{7,4},{8,11},{9,10},{10,... | collective-permute-start | bytes 983048 | tf_op jit(solution)/shard_map/ppermute | solution.py:701
  29.1 26.9 %copy-start.4 = (bf16[2,528,256]{2,1,0:T(8,128)(2,1)}, bf16[2,528,256]{2,1,0:T(8,128)(2,1)S(1)}, u32[]{:S(2)}) copy-start(bf16[2,528,256]{2,1,0:T(8,128)(2,1)S(1)} %collective-permute-done.1.refs_1_) | copy-start | bytes 1622020
  29.9 26.4 %collective-permute-start.3 = (bf16[528,256]{1,0:T(8,128)(2,1)}, bf16[528,256]{1,0:T(8,128)(2,1)}, u32[]{:S(2)}, u32[]{:S(2)}) collective-permute-start(bf16[528,256]{1,0:T(8,128)(2,1)} %slice_bitcast_fusion.3), channel_id=1, source_target_pairs={{0,4},{1,5},{2,6},{3,7},{4,12},{5,13},{6,14},{7,15},{8,0},{9,1},{1... | collective-permute-start | bytes 811016 | tf_op jit(solution)/shard_map/ppermute | solution.py:701
  42.3 13.8 %copy-start.5 = (bf16[2,528,256]{2,1,0:T(8,128)(2,1)}, bf16[2,528,256]{2,1,0:T(8,128)(2,1)S(1)}, u32[]{:S(2)}) copy-start(bf16[2,528,256]{2,1,0:T(8,128)(2,1)S(1)} %collective-permute-done.2.refs_2_) | copy-start | bytes 1622020
  43.0 13.3 %collective-permute-start.4 = (bf16[528,256]{1,0:T(8,128)(2,1)}, bf16[528,256]{1,0:T(8,128)(2,1)}, u32[]{:S(2)}, u32[]{:S(2)}) collective-permute-start(bf16[528,256]{1,0:T(8,128)(2,1)} %slice_bitcast_fusion.2), channel_id=1, source_target_pairs={{0,8},{1,9},{2,10},{3,11},{4,0},{5,1},{6,2},{7,3},{8,12},{9,13},{1... | collective-permute-start | bytes 811016 | tf_op jit(solution)/shard_map/ppermute | solution.py:701
  43.0 13.0 %collective-permute-start.10 = (bf16[64,2048]{1,0:T(8,128)(2,1)}, bf16[64,2048]{1,0:T(8,128)(2,1)}, u32[]{:S(2)}, u32[]{:S(2)}) collective-permute-start(bf16[64,2048]{1,0:T(8,128)(2,1)} %get-tuple-element.68), channel_id=1, source_target_pairs={{0,2},{1,3},{2,0},{3,1},{4,6},{5,7},{6,4},{7,5},{8,10},{9,11},{10,... | collective-permute-start | bytes 786440 | tf_op jit(solution)/shard_map/ppermute | solution.py:701
  44.6 11.7 %collective-permute-start.13 = (bf16[64,2048]{1,0:T(8,128)(2,1)}, bf16[64,2048]{1,0:T(8,128)(2,1)}, u32[]{:S(2)}, u32[]{:S(2)}) collective-permute-start(bf16[64,2048]{1,0:T(8,128)(2,1)} %get-tuple-element.73), channel_id=1, source_target_pairs={{0,1},{1,0},{2,3},{3,2},{4,5},{5,4},{6,7},{7,6},{8,9},{9,8},{10,11... | collective-permute-start | bytes 786440 | tf_op jit(solution)/shard_map/ppermute | solution.py:701
  48.9 17.9 %collective-permute-start.8 = (bf16[2,528,256]{2,1,0:T(8,128)(2,1)}, bf16[2,528,256]{2,1,0:T(8,128)(2,1)S(1)}, u32[]{:S(2)}, u32[]{:S(2)}) collective-permute-start(bf16[2,528,256]{2,1,0:T(8,128)(2,1)} %build_factors.4.refs_5_), channel_id=1, source_target_pairs={{0,8},{1,9},{2,10},{3,11},{4,0},{5,1},{6,2},{7,3},{8,12},{9,13},{1... | collective-permute-start | bytes 1622024 | tf_op jit(solution)/shard_map/ppermute | solution.py:701
  56.1 42.1 %copy-start.22 = (s32[8,2048]{1,0:T(8,128)S(1)}, s32[8,2048]{1,0:T(8,128)}, u32[]{:S(2)}) copy-start(s32[8,2048]{1,0:T(8,128)} %param.14) | copy-start | bytes 196612
  56.1 25.4 %collective-permute-start.7 = (bf16[2,528,256]{2,1,0:T(8,128)(2,1)S(1)}, bf16[2,528,256]{2,1,0:T(8,128)(2,1)S(1)}, u32[]{:S(2)}, u32[]{:S(2)}) collective-permute-start(bf16[2,528,256]{2,1,0:T(8,128)(2,1)S(1)} %copy-done.1), channel_id=1, source_target_pairs={{0,4},{1,5},{2,6},{3,7},{4,12},{5,13},{6,14},{7,15},{8,0},{9,1},{1... | collective-permute-start | bytes 1622024 | tf_op jit(solution)/shard_map/ppermute | solution.py:701
  56.3 41.1 %collective-permute-start.14 = (bf16[2,2,2,256,256]{4,3,2,1,0:T(8,128)(2,1)}, bf16[2,2,2,256,256]{4,3,2,1,0:T(8,128)(2,1)}, u32[]{:S(2)}, u32[]{:S(2)}) collective-permute-start(bf16[2,2,2,256,256]{4,3,2,1,0:T(8,128)(2,1)} %get-tuple-element.74), channel_id=1, source_target_pairs={{0,2},{1,3},{2,0},{3,1},{4,6},{5,7},{6,4},{7,5},{8,10},{9,11},{10,... | collective-permute-start | bytes 3145736 | tf_op jit(solution)/shard_map/ppermute | solution.py:701
  56.9 65.5 %collective-permute-start.16 = (bf16[2,2,2,256,256]{4,3,2,1,0:T(8,128)(2,1)}, bf16[2,2,2,256,256]{4,3,2,1,0:T(8,128)(2,1)S(1)}, u32[]{:S(2)}, u32[]{:S(2)}) collective-permute-start(bf16[2,2,2,256,256]{4,3,2,1,0:T(8,128)(2,1)} %get-tuple-element.80), channel_id=1, source_target_pairs={{0,3},{1,2},{2,1},{3,0},{4,7},{5,6},{6,5},{7,4},{8,11},{9,10},{10,... | collective-permute-start | bytes 3145736 | tf_op jit(solution)/shard_map/ppermute | solution.py:701
  67.6 25.1 %collective-permute-start.11 = (bf16[528,256]{1,0:T(8,128)(2,1)}, bf16[528,256]{1,0:T(8,128)(2,1)S(1)}, u32[]{:S(2)}, u32[]{:S(2)}) collective-permute-start(bf16[528,256]{1,0:T(8,128)(2,1)} %slice_bitcast_fusion), channel_id=1, source_target_pairs={{0,8},{1,9},{2,10},{3,11},{4,0},{5,1},{6,2},{7,3},{8,12},{9,13},{1... | collective-permute-start | bytes 811016 | tf_op jit(solution)/shard_map/ppermute | solution.py:701
  70.9 53.5 %collective-permute-start.17 = (bf16[2,2,2,256,256]{4,3,2,1,0:T(8,128)(2,1)}, bf16[2,2,2,256,256]{4,3,2,1,0:T(8,128)(2,1)S(1)}, u32[]{:S(2)}, u32[]{:S(2)}) collective-permute-start(bf16[2,2,2,256,256]{4,3,2,1,0:T(8,128)(2,1)} %get-tuple-element.82), channel_id=1, source_target_pairs={{0,1},{1,0},{2,3},{3,2},{4,5},{5,4},{6,7},{7,6},{8,9},{9,8},{10,11... | collective-permute-start | bytes 3145736 | tf_op jit(solution)/shard_map/ppermute | solution.py:701
  83.0 13.0 %collective-permute-start.9 = (bf16[528,256]{1,0:T(8,128)(2,1)}, bf16[528,256]{1,0:T(8,128)(2,1)}, u32[]{:S(2)}, u32[]{:S(2)}) collective-permute-start(bf16[528,256]{1,0:T(8,128)(2,1)} %slice_bitcast_fusion.1), channel_id=1, source_target_pairs={{0,4},{1,5},{2,6},{3,7},{4,12},{5,13},{6,14},{7,15},{8,0},{9,1},{1... | collective-permute-start | bytes 811016 | tf_op jit(solution)/shard_map/ppermute | solution.py:701
  92.7 27.4 %collective-permute-start.21 = (bf16[2,512,256]{2,1,0:T(8,128)(2,1)}, bf16[2,512,256]{2,1,0:T(8,128)(2,1)S(1)}, u32[]{:S(2)}, u32[]{:S(2)}) collective-permute-start(bf16[2,512,256]{2,1,0:T(8,128)(2,1)} %get-tuple-element.90.refs_0_), channel_id=1, source_target_pairs={{0,4},{1,5},{2,6},{3,7},{4,12},{5,13},{6,14},{7,15},{8,0},{9,1},{1... | collective-permute-start | bytes 1572872 | tf_op jit(solution)/shard_map/ppermute | solution.py:701
  96.1 24.7 %collective-permute-start.15 = (bf16[2,512,256]{2,1,0:T(8,128)(2,1)}, bf16[2,512,256]{2,1,0:T(8,128)(2,1)}, u32[]{:S(2)}, u32[]{:S(2)}) collective-permute-start(bf16[2,512,256]{2,1,0:T(8,128)(2,1)} %get-tuple-element.90.refs_0_), channel_id=1, source_target_pairs={{0,8},{1,9},{2,10},{3,11},{4,0},{5,1},{6,2},{7,3},{8,12},{9,13},{1... | collective-permute-start | bytes 1572872 | tf_op jit(solution)/shard_map/ppermute | solution.py:701
  97.4 45.1 %collective-permute-start.24 = (bf16[2,512,256]{2,1,0:T(8,128)(2,1)}, bf16[2,512,256]{2,1,0:T(8,128)(2,1)}, u32[]{:S(2)}, u32[]{:S(2)}) collective-permute-start(bf16[2,512,256]{2,1,0:T(8,128)(2,1)} %get-tuple-element.93.refs_5_), channel_id=1, source_target_pairs={{0,4},{1,5},{2,6},{3,7},{4,12},{5,13},{6,14},{7,15},{8,0},{9,1},{1... | collective-permute-start | bytes 1572872 | tf_op jit(solution)/shard_map/ppermute | solution.py:701
  120.1 17.3 %copy-start.8 = (bf16[2,512,256]{2,1,0:T(8,128)(2,1)}, bf16[2,512,256]{2,1,0:T(8,128)(2,1)S(1)}, u32[]{:S(2)}) copy-start(bf16[2,512,256]{2,1,0:T(8,128)(2,1)S(1)} %collective-permute-done.21.refs_1_) | copy-start | bytes 1572868
  120.1 28.5 %collective-permute-start.20 = (bf16[2,512,256]{2,1,0:T(8,128)(2,1)}, bf16[2,512,256]{2,1,0:T(8,128)(2,1)}, u32[]{:S(2)}, u32[]{:S(2)}) collective-permute-start(bf16[2,512,256]{2,1,0:T(8,128)(2,1)} %get-tuple-element.93.refs_5_), channel_id=1, source_target_pairs={{0,8},{1,9},{2,10},{3,11},{4,0},{5,1},{6,2},{7,3},{8,12},{9,13},{1... | collective-permute-start | bytes 1572872 | tf_op jit(solution)/shard_map/ppermute | solution.py:701
  120.8 38.5 %collective-permute-start.18 = (bf16[2,2,256,256]{3,2,1,0:T(8,128)(2,1)}, bf16[2,2,256,256]{3,2,1,0:T(8,128)(2,1)}, u32[]{:S(2)}, u32[]{:S(2)}) collective-permute-start(bf16[2,2,256,256]{3,2,1,0:T(8,128)(2,1)} %get-tuple-element.86), channel_id=1, source_target_pairs={{0,2},{1,3},{2,0},{3,1},{4,6},{5,7},{6,4},{7,5},{8,10},{9,11},{10,... | collective-permute-start | bytes 1572872 | tf_op jit(solution)/shard_map/ppermute | solution.py:701
  122.4 25.8 %collective-permute-start.22 = (bf16[512,256]{1,0:T(8,128)(2,1)}, bf16[512,256]{1,0:T(8,128)(2,1)S(1)}, u32[]{:S(2)}, u32[]{:S(2)}) collective-permute-start(bf16[512,256]{1,0:T(8,128)(2,1)} %slice_bitcast_fusion.7), channel_id=1, source_target_pairs={{0,4},{1,5},{2,6},{3,7},{4,12},{5,13},{6,14},{7,15},{8,0},{9,1},{1... | collective-permute-start | bytes 786440 | tf_op jit(solution)/shard_map/ppermute | solution.py:701
  137.3 33.8 %copy-start.23 = (f32[1,512]{1,0:T(1,128)S(1)}, f32[1,512]{1,0:T(1,128)}, u32[]{:S(2)}) copy-start(f32[1,512]{1,0:T(1,128)} %get-tuple-element.75) | copy-start | bytes 6148
  137.4 33.8 %copy-start.24 = (f32[1,512]{1,0:T(1,128)S(1)}, f32[1,512]{1,0:T(1,128)}, u32[]{:S(2)}) copy-start(f32[1,512]{1,0:T(1,128)} %get-tuple-element.84) | copy-start | bytes 6148
  137.4 13.5 %collective-permute-start.19 = (bf16[2,2,256,256]{3,2,1,0:T(8,128)(2,1)}, bf16[2,2,256,256]{3,2,1,0:T(8,128)(2,1)S(1)}, u32[]{:S(2)}, u32[]{:S(2)}) collective-permute-start(bf16[2,2,256,256]{3,2,1,0:T(8,128)(2,1)} %get-tuple-element.87), channel_id=1, source_target_pairs={{0,3},{1,2},{2,1},{3,0},{4,7},{5,6},{6,5},{7,4},{8,11},{9,10},{10,... | collective-permute-start | bytes 1572872 | tf_op jit(solution)/shard_map/ppermute | solution.py:701
  143.5 15.8 %collective-permute-start.25 = (bf16[512,256]{1,0:T(8,128)(2,1)S(1)}, bf16[512,256]{1,0:T(8,128)(2,1)S(1)}, u32[]{:S(2)}, u32[]{:S(2)}) collective-permute-start(bf16[512,256]{1,0:T(8,128)(2,1)S(1)} %slice_bitcast_fusion.5), channel_id=1, source_target_pairs={{0,4},{1,5},{2,6},{3,7},{4,12},{5,13},{6,14},{7,15},{8,0},{9,1},{1... | collective-permute-start | bytes 786440 | tf_op jit(solution)/shard_map/ppermute | solution.py:701
  148.2 14.2 %copy-start.13 = (bf16[512,256]{1,0:T(8,128)(2,1)}, bf16[512,256]{1,0:T(8,128)(2,1)S(1)}, u32[]{:S(2)}) copy-start(bf16[512,256]{1,0:T(8,128)(2,1)S(1)} %collective-permute-done.22.refs_3_) | copy-start | bytes 786436
  148.2 11.1 %collective-permute-start.23 = (bf16[512,256]{1,0:T(8,128)(2,1)S(1)}, bf16[512,256]{1,0:T(8,128)(2,1)S(1)}, u32[]{:S(2)}, u32[]{:S(2)}) collective-permute-start(bf16[512,256]{1,0:T(8,128)(2,1)S(1)} %slice_bitcast_fusion.6), channel_id=1, source_target_pairs={{0,8},{1,9},{2,10},{3,11},{4,0},{5,1},{6,2},{7,3},{8,12},{9,13},{1... | collective-permute-start | bytes 786440 | tf_op jit(solution)/shard_map/ppermute | solution.py:701
  150.9 43.3 %copy-start.20 = (bf16[2,2,256,256]{3,2,1,0:T(8,128)(2,1)}, bf16[2,2,256,256]{3,2,1,0:T(8,128)(2,1)S(1)}, u32[]{:S(2)}) copy-start(bf16[2,2,256,256]{3,2,1,0:T(8,128)(2,1)S(1)} %collective-permute-done.19.refs_1_) | copy-start | bytes 1572868
  150.9 11.5 %collective-permute-start.26 = (bf16[512,256]{1,0:T(8,128)(2,1)S(1)}, bf16[512,256]{1,0:T(8,128)(2,1)S(1)}, u32[]{:S(2)}, u32[]{:S(2)}) collective-permute-start(bf16[512,256]{1,0:T(8,128)(2,1)S(1)} %slice_bitcast_fusion.4), channel_id=1, source_target_pairs={{0,8},{1,9},{2,10},{3,11},{4,0},{5,1},{6,2},{7,3},{8,12},{9,13},{1... | collective-permute-start | bytes 786440 | tf_op jit(solution)/shard_map/ppermute | solution.py:701
  159.3 25.3 %collective-permute-start.30 = (bf16[2,2,256,256]{3,2,1,0:T(8,128)(2,1)}, bf16[2,2,256,256]{3,2,1,0:T(8,128)(2,1)S(1)}, u32[]{:S(2)}, u32[]{:S(2)}) collective-permute-start(bf16[2,2,256,256]{3,2,1,0:T(8,128)(2,1)} %get-tuple-element.108), channel_id=1, source_target_pairs={{0,1},{1,0},{2,3},{3,2},{4,5},{5,4},{6,7},{7,6},{8,9},{9,8},{10,11... | collective-permute-start | bytes 1572872 | tf_op jit(solution)/shard_map/ppermute | solution.py:701
  169.5 22.6 %collective-permute-start.27 = (bf16[2,2,256,256]{3,2,1,0:T(8,128)(2,1)}, bf16[2,2,256,256]{3,2,1,0:T(8,128)(2,1)S(1)}, u32[]{:S(2)}, u32[]{:S(2)}) collective-permute-start(bf16[2,2,256,256]{3,2,1,0:T(8,128)(2,1)} %get-tuple-element.98), channel_id=1, source_target_pairs={{0,2},{1,3},{2,0},{3,1},{4,6},{5,7},{6,4},{7,5},{8,10},{9,11},{10,... | collective-permute-start | bytes 1572872 | tf_op jit(solution)/shard_map/ppermute | solution.py:701
  171.1 12.8 %copy-start.25 = (f32[1,512]{1,0:T(1,128)S(1)}, f32[1,512]{1,0:T(1,128)}, u32[]{:S(2)}) copy-start(f32[1,512]{1,0:T(1,128)} %get-tuple-element.99) | copy-start | bytes 6148
  183.3 22.5 %collective-permute-start.28 = (bf16[2,2,256,256]{3,2,1,0:T(8,128)(2,1)}, bf16[2,2,256,256]{3,2,1,0:T(8,128)(2,1)S(1)}, u32[]{:S(2)}, u32[]{:S(2)}) collective-permute-start(bf16[2,2,256,256]{3,2,1,0:T(8,128)(2,1)} %get-tuple-element.102), channel_id=1, source_target_pairs={{0,3},{1,2},{2,1},{3,0},{4,7},{5,6},{6,5},{7,4},{8,11},{9,10},{10,... | collective-permute-start | bytes 1572872 | tf_op jit(solution)/shard_map/ppermute | solution.py:701
  183.3 18.1 %collective-permute-start.29 = (bf16[2,2,256,256]{3,2,1,0:T(8,128)(2,1)}, bf16[2,2,256,256]{3,2,1,0:T(8,128)(2,1)S(1)}, u32[]{:S(2)}, u32[]{:S(2)}) collective-permute-start(bf16[2,2,256,256]{3,2,1,0:T(8,128)(2,1)} %get-tuple-element.104), channel_id=1, source_target_pairs={{0,1},{1,0},{2,3},{3,2},{4,5},{5,4},{6,7},{7,6},{8,9},{9,8},{10,11... | collective-permute-start | bytes 1572872 | tf_op jit(solution)/shard_map/ppermute | solution.py:701
  184.6 14.8 %collective-permute-start.33 = (f32[2,128]{1,0:T(2,128)S(1)}, f32[2,128]{1,0:T(2,128)S(1)}, u32[]{:S(2)}, u32[]{:S(2)}) collective-permute-start(f32[2,128]{1,0:T(2,128)S(1)} %get-tuple-element.113), channel_id=1, source_target_pairs={{0,4},{1,5},{2,6},{3,7},{4,12},{5,13},{6,14},{7,15},{8,0},{9,1},{1... | collective-permute-start | bytes 3080 | tf_op jit(solution)/shard_map/ppermute | solution.py:701
  186.4 13.0 %collective-permute-start.31 = (f32[2,128]{1,0:T(2,128)S(1)}, f32[2,128]{1,0:T(2,128)S(1)}, u32[]{:S(2)}, u32[]{:S(2)}) collective-permute-start(f32[2,128]{1,0:T(2,128)S(1)} %get-tuple-element.111), channel_id=1, source_target_pairs={{0,12},{1,13},{2,14},{3,15},{4,8},{5,9},{6,10},{7,11},{8,4},{9,5},... | collective-permute-start | bytes 3080 | tf_op jit(solution)/shard_map/ppermute | solution.py:701
  192.1 13.6 %copy-start.17 = (bf16[2,2,256,256]{3,2,1,0:T(8,128)(2,1)}, bf16[2,2,256,256]{3,2,1,0:T(8,128)(2,1)S(1)}, u32[]{:S(2)}) copy-start(bf16[2,2,256,256]{3,2,1,0:T(8,128)(2,1)S(1)} %collective-permute-done.27.refs_0_) | copy-start | bytes 1572868
  192.1 7.3 %collective-permute-start.32 = (f32[2,128]{1,0:T(2,128)S(1)}, f32[2,128]{1,0:T(2,128)S(1)}, u32[]{:S(2)}, u32[]{:S(2)}) collective-permute-start(f32[2,128]{1,0:T(2,128)S(1)} %get-tuple-element.112), channel_id=1, source_target_pairs={{0,8},{1,9},{2,10},{3,11},{4,0},{5,1},{6,2},{7,3},{8,12},{9,13},{1... | collective-permute-start | bytes 3080 | tf_op jit(solution)/shard_map/ppermute | solution.py:701
  199.6 10.4 %collective-permute-start.36 = (f32[2,32]{1,0:T(2,128)S(1)}, f32[2,32]{1,0:T(2,128)S(1)}, u32[]{:S(2)}, u32[]{:S(2)}) collective-permute-start(f32[2,32]{1,0:T(2,128)S(1)} %get-tuple-element.120), channel_id=1, source_target_pairs={{0,3},{1,2},{2,1},{3,0},{4,7},{5,6},{6,5},{7,4},{8,11},{9,10},{10,... | collective-permute-start | bytes 776 | tf_op jit(solution)/shard_map/ppermute | solution.py:701
  199.6 10.4 %collective-permute-start.35 = (f32[2,32]{1,0:T(2,128)S(1)}, f32[2,32]{1,0:T(2,128)S(1)}, u32[]{:S(2)}, u32[]{:S(2)}) collective-permute-start(f32[2,32]{1,0:T(2,128)S(1)} %get-tuple-element.115), channel_id=1, source_target_pairs={{0,2},{1,3},{2,0},{3,1},{4,6},{5,7},{6,4},{7,5},{8,10},{9,11},{10,... | collective-permute-start | bytes 776 | tf_op jit(solution)/shard_map/ppermute | solution.py:701
  200.4 9.6 %collective-permute-start.34 = (f32[2,32]{1,0:T(2,128)S(1)}, f32[2,32]{1,0:T(2,128)S(1)}, u32[]{:S(2)}, u32[]{:S(2)}) collective-permute-start(f32[2,32]{1,0:T(2,128)S(1)} %get-tuple-element.114), channel_id=1, source_target_pairs={{0,1},{1,0},{2,3},{3,2},{4,5},{5,4},{6,7},{7,6},{8,9},{9,8},{10,11... | collective-permute-start | bytes 776 | tf_op jit(solution)/shard_map/ppermute | solution.py:701
  (16 other events, 58.2 us)

commit v12 on v10

--- a/solution.py
+++ b/solution.py
@@ -657,7 +657,7 @@
     27: (8,),
     28: (22,),
     31: (25, 27),
-    33: (23, 32),
+    33: (23, 32, 20),
     34: (33,),
     35: (8, 9, 24, 25),
     40: (28, 34, 36, 37),
@@ -669,6 +669,9 @@
     49: (44,),
     51: (34,),
     52: (38,),
+    8: (23,),
+    9: (23,),
+    47: (51, 52, 53),
 }
 
 

time: 202 us -> 207 us (1.025)
  starting transfers between devices: 50.7 us -> 67.7 us
  waiting for transfers between devices: 61.5 us -> 51.7 us
    ppermute x37, starting transfers between devices: 50.7 us -> 67.7 us  [send(): done[step] = lax.ppermute(gated(step, value), 'tile', pairs)]
    ppermute x37, waiting for transfers between devices: 61.5 us -> 51.7 us  [send(): done[step] = lax.ppermute(gated(step, value), 'tile', pairs)]
    unnamed x109, local copies, waits for them, and re-layouts: 19.6 us -> 16.6 us
  transfers between devices with their start and end apart: 37 -> 37, of which waited for: 10 -> 11; matrix products, arithmetic and copies ran while one was open for 3% -> 4% of each run, Pallas kernels for 28% -> 26%
where the time goes in v12:
time: 207 us
  starting transfers between devices  67.7 us (33%)
  Pallas kernels  59.9 us (29%)
  waiting for transfers between devices  51.7 us (25%)
  local copies, waits for them, and re-layouts  23.8 us (11%)
  other arithmetic  2.16 us (1%)
    ppermute x37, starting transfers between devices, send(): done[step] = lax.ppermute(gated(step, value), 'tile', pairs)  67.7 us
    ppermute x37, waiting for transfers between devices, send(): done[step] = lax.ppermute(gated(step, value), 'tile', pairs)  51.7 us
    pallas_call x6, Pallas kernels, unit_work(): pl.pallas_call(functools.partial(unit_kernel, index, offset, kinds, brigh...  32.4 us
    unnamed x109, local copies, waits for them, and re-layouts  16.6 us
    pallas_call x3, Pallas kernels, put_residuals(): pl.pallas_call(functools.partial(put_kernel, sources), grid_spec=pltpu.Pr...  9.1 us
    pallas_call x3, Pallas kernels, messages_for(): pl.pallas_call(functools.partial(message_kernel, len(others), bool(smalls...  7.69 us
    pallas_call x3, Pallas kernels, build_factors(): pl.pallas_call(functools.partial(build_kernel, sets, slot_ids, pieces, br...  6.78 us
  transfers between devices with their start and end apart: 37, of which 11 were waited for; matrix products, arithmetic and copies ran while one was open for 4% of the time, Pallas kernels for 26%

profile of v12, /device:TPU:0, one launch (start us, length us, event | category | flops | bytes accessed | tf_op | source)
XLA Modules:
  0.0 206.5 jit_solution(11253731530332934128)
XLA Ops:
  0.6 1.3 broadcast_in_dim.34
  2.0 1.3 constant_dynamic-slice_fusion
  3.3 2.4 %messages_for.3 = bf16[80,2048]{1,0:T(8,128)(2,1)} custom-call(s32[148]{0:T(256)} %bitcast.24, bf16[8,2,32,2048]{3,2,1,0:T(8,128)(2,1)} %refs_0_.10, f32[2,256]{1,0:T(2,128)} %refs_4_.5, f32[1,256]{1,0:T(1,128)} %bitcast.40, s32[8,32]{1,0:T(8,128)} %refs_6_.1), custom_call_target="tpu_custom_call" | custom-call | flops 1 | bytes 1 | tf_op jit(solution)/shard_map/messages_for/pallas_call | solution.py:211
  10.3 1.6 build_factors.3.refs_0_
  11.9 4.0 %collective-permute-start.2 = (bf16[2,528,256]{2,1,0:T(8,128)(2,1)S(1)}, bf16[2,528,256]{2,1,0:T(8,128)(2,1)S(1)}, u32[]{:S(2)}, u32[]{:S(2)}) collective-permute-start(bf16[2,528,256]{2,1,0:T(8,128)(2,1)S(1)} %build_factors.3.refs_0_), channel_id=1, source_target_pairs={{0,8},{1,9},{2,10},{3,11},{4,0},{5,1},{6,2},{7,3},{8,12},{9,13},{1... | collective-permute-start | bytes 1622024 | tf_op jit(solution)/shard_map/ppermute | solution.py:694
  15.9 2.6 %messages_for.4 = (bf16[80,2048]{1,0:T(8,128)(2,1)}, bf16[80,2048]{1,0:T(8,128)(2,1)}) custom-call(s32[148]{0:T(256)} %bitcast.25, bf16[8,2,32,2048]{3,2,1,0:T(8,128)(2,1)} %refs_0_.10, bf16[8,2,32,2048]{3,2,1,0:T(8,128)(2,1)} %refs_0_.10, f32[2,256]{1,0:T(2,128)} %refs_4_.5, f32[1,256]{1,0:T(1,128)} %bitcast.41, s32[8,32]{1,0:T(8,128)} %refs_6_.1), custom_call_target="tpu_custom_call" | custom-call | flops 1 | bytes 1 | tf_op jit(solution)/shard_map/messages_for/pallas_call | solution.py:211
  18.5 1.5 collective-permute-start.5
  20.0 2.7 %messages_for.5 = (bf16[64,2048]{1,0:T(8,128)(2,1)}, bf16[64,2048]{1,0:T(8,128)(2,1)}, bf16[64,2048]{1,0:T(8,128)(2,1)}) custom-call(s32[148]{0:T(256)} %bitcast.26, bf16[8,2,32,2048]{3,2,1,0:T(8,128)(2,1)} %refs_0_.10, bf16[8,2,32,2048]{3,2,1,0:T(8,128)(2,1)} %refs_0_.10, bf16[8,2,32,2048]{3,2,1,0:T(8,128)(2,1)} %refs_0_.10), custom_call_target="tpu_custom_call" | custom-call | flops 1 | bytes 1 | tf_op jit(solution)/shard_map/messages_for/pallas_call | solution.py:211
  22.7 6.6 %collective-permute-done.5.refs_0_.refs_8_ = bf16[80,2048]{1,0:T(8,128)(2,1)S(1)} collective-permute-done((bf16[80,2048]{1,0:T(8,128)(2,1)}, bf16[80,2048]{1,0:T(8,128)(2,1)S(1)}, u32[]{:S(2)}, u32[]{:S(2)}) %collective-permute-start.5) | collective-permute-done | bytes 327712 | tf_op jit(solution)/shard_map/ppermute | solution.py:694
  30.1 2.7 %collective-permute-start.4 = (bf16[528,256]{1,0:T(8,128)(2,1)}, bf16[528,256]{1,0:T(8,128)(2,1)}, u32[]{:S(2)}, u32[]{:S(2)}) collective-permute-start(bf16[528,256]{1,0:T(8,128)(2,1)} %slice_bitcast_fusion.2), channel_id=1, source_target_pairs={{0,8},{1,9},{2,10},{3,11},{4,0},{5,1},{6,2},{7,3},{8,12},{9,13},{1... | collective-permute-start | bytes 811016 | tf_op jit(solution)/shard_map/ppermute | solution.py:694
  32.7 9.2 %collective-permute-done.1.refs_1_ = bf16[2,528,256]{2,1,0:T(8,128)(2,1)S(1)} collective-permute-done((bf16[2,528,256]{2,1,0:T(8,128)(2,1)S(1)}, bf16[2,528,256]{2,1,0:T(8,128)(2,1)S(1)}, u32[]{:S(2)}, u32[]{:S(2)}) %collective-permute-start.1) | collective-permute-done | bytes 540704 | tf_op jit(solution)/shard_map/ppermute | solution.py:694
  43.4 1.5 collective-permute-start.9
  45.0 1.6 build_factors.4.refs_5_
  48.1 2.2 %collective-permute-start.8 = (bf16[2,528,256]{2,1,0:T(8,128)(2,1)S(1)}, bf16[2,528,256]{2,1,0:T(8,128)(2,1)}, u32[]{:S(2)}, u32[]{:S(2)}) collective-permute-start(bf16[2,528,256]{2,1,0:T(8,128)(2,1)S(1)} %build_factors.4.refs_5_), channel_id=1, source_target_pairs={{0,8},{1,9},{2,10},{3,11},{4,0},{5,1},{6,2},{7,3},{8,12},{9,13},{1... | collective-permute-start | bytes 1622024 | tf_op jit(solution)/shard_map/ppermute | solution.py:694
  51.9 2.8 %collective-permute-start.7 = (bf16[2,528,256]{2,1,0:T(8,128)(2,1)S(1)}, bf16[2,528,256]{2,1,0:T(8,128)(2,1)}, u32[]{:S(2)}, u32[]{:S(2)}) collective-permute-start(bf16[2,528,256]{2,1,0:T(8,128)(2,1)S(1)} %build_factors.4.refs_5_), channel_id=1, source_target_pairs={{0,4},{1,5},{2,6},{3,7},{4,12},{5,13},{6,14},{7,15},{8,0},{9,1},{1... | collective-permute-start | bytes 1622024 | tf_op jit(solution)/shard_map/ppermute | solution.py:694
  54.6 4.0 %slices_for.1 = (bf16[2,2,2,256,256]{4,3,2,1,0:T(8,128)(2,1)}, bf16[2,2,2,256,256]{4,3,2,1,0:T(8,128)(2,1)}, bf16[2,2,2,256,256]{4,3,2,1,0:T(8,128)(2,1)}) custom-call(s32[148]{0:T(256)} %bitcast.27, bf16[2,8,2,256,256]{4,3,2,1,0:T(8,128)(2,1)} %refs_11_.3, bf16[2,8,2,256,256]{4,3,2,1,0:T(8,128)(2,1)} %refs_11_.3, bf16[2,8,2,256,256]{4,3,2,1,0:T(8,128)(2,1)} %refs_11_.3), custom_call_target="tpu_custom_call" | custom-call | flops 1 | bytes 1 | tf_op jit(solution)/shard_map/slices_for/pallas_call | solution.py:242
  58.6 1.6 collective-permute-start.14
  65.0 3.5 %build_factors.5 = (bf16[2,512,256]{2,1,0:T(8,128)(2,1)S(1)}, bf16[2,512,256]{2,1,0:T(8,128)(2,1)S(1)}) custom-call(s32[148]{0:T(256)S(1)} %bitcast.30, bf16[8,2,32,2048]{3,2,1,0:T(8,128)(2,1)S(1)} %copy-done.1, bf16[64,2048]{1,0:T(8,128)(2,1)} %collective-permute-done.10.refs_1_, bf16[64,2048]{1,0:T(8,128)(2,1)S(1)} %copy-done.43, ...), custom_call_target="tpu_custom_call" | custom-call | flops 1 | bytes 1 | tf_op jit(solution)/shard_map/build_factors/pallas_call | solution.py:161
  68.6 1.2 slice_bitcast_fusion
  70.0 7.6 %collective-permute-done.7.refs_6_ = bf16[2,528,256]{2,1,0:T(8,128)(2,1)} collective-permute-done((bf16[2,528,256]{2,1,0:T(8,128)(2,1)S(1)}, bf16[2,528,256]{2,1,0:T(8,128)(2,1)}, u32[]{:S(2)}, u32[]{:S(2)}) %collective-permute-start.7) | collective-permute-done | bytes 540704 | tf_op jit(solution)/shard_map/ppermute | solution.py:694
  78.8 1.5 collective-permute-start.15
  80.2 2.7 %collective-permute-done.13.refs_9_ = bf16[528,256]{1,0:T(8,128)(2,1)S(1)} collective-permute-done((bf16[528,256]{1,0:T(8,128)(2,1)S(1)}, bf16[528,256]{1,0:T(8,128)(2,1)S(1)}, u32[]{:S(2)}, u32[]{:S(2)}) %collective-permute-start.13) | collective-permute-done | bytes 270368 | tf_op jit(solution)/shard_map/ppermute | solution.py:694
  83.8 5.0 %collective-permute-done.12.refs_8_ = bf16[528,256]{1,0:T(8,128)(2,1)S(1)} collective-permute-done((bf16[528,256]{1,0:T(8,128)(2,1)S(1)}, bf16[528,256]{1,0:T(8,128)(2,1)S(1)}, u32[]{:S(2)}, u32[]{:S(2)}) %collective-permute-start.12) | collective-permute-done | bytes 270368 | tf_op jit(solution)/shard_map/ppermute | solution.py:694
  88.8 14.2 %collective-permute-start.17 = (bf16[2,512,256]{2,1,0:T(8,128)(2,1)S(1)}, bf16[2,512,256]{2,1,0:T(8,128)(2,1)S(1)}, u32[]{:S(2)}, u32[]{:S(2)}) collective-permute-start(bf16[2,512,256]{2,1,0:T(8,128)(2,1)S(1)} %get-tuple-element.89.refs_0_), channel_id=1, source_target_pairs={{0,4},{1,5},{2,6},{3,7},{4,12},{5,13},{6,14},{7,15},{8,0},{9,1},{1... | collective-permute-start | bytes 1572872 | tf_op jit(solution)/shard_map/ppermute | solution.py:694
  103.0 3.4 %collective-permute-start.23 = (bf16[2,512,256]{2,1,0:T(8,128)(2,1)S(1)}, bf16[2,512,256]{2,1,0:T(8,128)(2,1)S(1)}, u32[]{:S(2)}, u32[]{:S(2)}) collective-permute-start(bf16[2,512,256]{2,1,0:T(8,128)(2,1)S(1)} %get-tuple-element.97.refs_5_), channel_id=1, source_target_pairs={{0,4},{1,5},{2,6},{3,7},{4,12},{5,13},{6,14},{7,15},{8,0},{9,1},{1... | collective-permute-start | bytes 1572872 | tf_op jit(solution)/shard_map/ppermute | solution.py:694
  106.4 5.3 %unit_work.6 = (bf16[2,2,256,256]{3,2,1,0:T(8,128)(2,1)}, f32[1,512]{1,0:T(1,128)S(1)}, f32[2,512,128]{2,1,0:T(8,128)S(1)}) custom-call(s32[148]{0:T(256)S(1)} %bitcast.31, bf16[2,528,256]{2,1,0:T(8,128)(2,1)S(1)} %build_factors.3.refs_0_, bf16[2,528,256]{2,1,0:T(8,128)(2,1)S(1)} %copy-done.8, bf16[2,528,256]{2,1,0:T(8,128)(2,1)S(1)} %copy-done.5, ...), custom_call_target="tpu_custom_call" | custom-call | flops 1 | bytes 1 | tf_op jit(solution)/shard_map/unit_work/pallas_call | solution.py:476
  112.6 2.8 %collective-permute-done.17.refs_1_ = bf16[2,512,256]{2,1,0:T(8,128)(2,1)S(1)} collective-permute-done((bf16[2,512,256]{2,1,0:T(8,128)(2,1)S(1)}, bf16[2,512,256]{2,1,0:T(8,128)(2,1)S(1)}, u32[]{:S(2)}, u32[]{:S(2)}) %collective-permute-start.17) | collective-permute-done | bytes 524320 | tf_op jit(solution)/shard_map/ppermute | solution.py:694
  115.4 1.1 collective-permute-start.19
  116.6 3.9 %collective-permute-start.22 = (bf16[512,256]{1,0:T(8,128)(2,1)}, bf16[512,256]{1,0:T(8,128)(2,1)}, u32[]{:S(2)}, u32[]{:S(2)}) collective-permute-start(bf16[512,256]{1,0:T(8,128)(2,1)} %slice_bitcast_fusion.6), channel_id=1, source_target_pairs={{0,8},{1,9},{2,10},{3,11},{4,0},{5,1},{6,2},{7,3},{8,12},{9,13},{1... | collective-permute-start | bytes 786440 | tf_op jit(solution)/shard_map/ppermute | solution.py:694
  120.5 5.1 %unit_work.7 = (bf16[2,2,256,256]{3,2,1,0:T(8,128)(2,1)}, f32[1,512]{1,0:T(1,128)S(1)}) custom-call(s32[148]{0:T(256)S(1)} %bitcast.32, bf16[2,528,256]{2,1,0:T(8,128)(2,1)S(1)} %build_factors.3.refs_0_, bf16[2,528,256]{2,1,0:T(8,128)(2,1)S(1)} %copy-done.8, bf16[2,528,256]{2,1,0:T(8,128)(2,1)S(1)} %copy-done.5, ...), custom_call_target="tpu_custom_call" | custom-call | flops 1 | bytes 1 | tf_op jit(solution)/shard_map/unit_work/pallas_call | solution.py:476
  128.2 11.7 %collective-permute-done.24.refs_7_ = bf16[2,512,256]{2,1,0:T(8,128)(2,1)S(1)} collective-permute-done((bf16[2,512,256]{2,1,0:T(8,128)(2,1)S(1)}, bf16[2,512,256]{2,1,0:T(8,128)(2,1)S(1)}, u32[]{:S(2)}, u32[]{:S(2)}) %collective-permute-start.24) | collective-permute-done | bytes 524320 | tf_op jit(solution)/shard_map/ppermute | solution.py:694
  139.8 8.6 %collective-permute-start.25 = (bf16[512,256]{1,0:T(8,128)(2,1)}, bf16[512,256]{1,0:T(8,128)(2,1)}, u32[]{:S(2)}, u32[]{:S(2)}) collective-permute-start(bf16[512,256]{1,0:T(8,128)(2,1)} %slice_bitcast_fusion.5), channel_id=1, source_target_pairs={{0,4},{1,5},{2,6},{3,7},{4,12},{5,13},{6,14},{7,15},{8,0},{9,1},{1... | collective-permute-start | bytes 786440 | tf_op jit(solution)/shard_map/ppermute | solution.py:694
  150.7 1.5 collective-permute-start.26
  152.2 2.2 %copy-done.2 = bf16[2,8,2,256,256]{4,3,2,1,0:T(8,128)(2,1)S(1)} copy-done((bf16[2,8,2,256,256]{4,3,2,1,0:T(8,128)(2,1)S(1)}, bf16[2,8,2,256,256]{4,3,2,1,0:T(8,128)(2,1)}, u32[]{:S(2)}) %copy-start.2) | copy-done | bytes 4194328
  154.4 1.2 copy-done.27
  155.7 7.1 %unit_work.8 = (bf16[2,2,256,256]{3,2,1,0:T(8,128)(2,1)S(1)}, bf16[2,2,256,256]{3,2,1,0:T(8,128)(2,1)S(1)}, f32[1,512]{1,0:T(1,128)S(1)}) custom-call(s32[148]{0:T(256)S(1)} %bitcast.33, bf16[2,528,256]{2,1,0:T(8,128)(2,1)S(1)} %build_factors.3.refs_0_, bf16[2,528,256]{2,1,0:T(8,128)(2,1)S(1)} %copy-done.9, bf16[2,528,256]{2,1,0:T(8,128)(2,1)S(1)} %copy-done.6, ...), custom_call_target="tpu_custom_call" | custom-call | flops 1 | bytes 1 | tf_op jit(solution)/shard_map/unit_work/pallas_call | solution.py:476
  163.0 4.2 %unit_work.9 = (bf16[2,2,256,256]{3,2,1,0:T(8,128)(2,1)S(1)}, f32[1,512]{1,0:T(1,128)S(1)}) custom-call(s32[148]{0:T(256)S(1)} %bitcast.34, bf16[2,512,256]{2,1,0:T(8,128)(2,1)S(1)} %copy-done.19, bf16[2,512,256]{2,1,0:T(8,128)(2,1)S(1)} %copy-done.13, bf16[2,512,256]{2,1,0:T(8,128)(2,1)S(1)} %copy-done.11, bf16[512,256]{1,0:T(8,128)(2,1)S(1)} %copy-done.30, ...), custom_call_target="tpu_custom_call" | custom-call | flops 1 | bytes 1 | tf_op jit(solution)/shard_map/unit_work/pallas_call | solution.py:476
  167.2 1.2 collective-permute-start.29
  168.4 4.2 %unit_work.10 = (bf16[2,2,256,256]{3,2,1,0:T(8,128)(2,1)S(1)}, f32[1,512]{1,0:T(1,128)S(1)}) custom-call(s32[148]{0:T(256)S(1)} %bitcast.35, bf16[2,512,256]{2,1,0:T(8,128)(2,1)S(1)} %copy-done.19, bf16[2,512,256]{2,1,0:T(8,128)(2,1)S(1)} %copy-done.13, bf16[2,512,256]{2,1,0:T(8,128)(2,1)S(1)} %copy-done.11, bf16[512,256]{1,0:T(8,128)(2,1)S(1)} %copy-done.30, ...), custom_call_target="tpu_custom_call" | custom-call | flops 1 | bytes 1 | tf_op jit(solution)/shard_map/unit_work/pallas_call | solution.py:476
  172.6 6.5 %unit_work.11 = (bf16[2,2,256,256]{3,2,1,0:T(8,128)(2,1)S(1)}, bf16[2,2,256,256]{3,2,1,0:T(8,128)(2,1)S(1)}, f32[1,512]{1,0:T(1,128)S(1)}) custom-call(s32[148]{0:T(256)S(1)} %bitcast.36, bf16[2,512,256]{2,1,0:T(8,128)(2,1)S(1)} %copy-done.19, bf16[2,512,256]{2,1,0:T(8,128)(2,1)S(1)} %copy-done.13, bf16[2,512,256]{2,1,0:T(8,128)(2,1)S(1)} %copy-done.11, ...), custom_call_target="tpu_custom_call" | custom-call | flops 1 | bytes 1 | tf_op jit(solution)/shard_map/unit_work/pallas_call | solution.py:476
  179.1 2.6 %collective-permute-start.31 = (f32[2,128]{1,0:T(2,128)S(1)}, f32[2,128]{1,0:T(2,128)S(1)}, u32[]{:S(2)}, u32[]{:S(2)}) collective-permute-start(f32[2,128]{1,0:T(2,128)S(1)} %get-tuple-element.119), channel_id=1, source_target_pairs={{0,4},{1,5},{2,6},{3,7},{4,12},{5,13},{6,14},{7,15},{8,0},{9,1},{1... | collective-permute-start | bytes 3080 | tf_op jit(solution)/shard_map/ppermute | solution.py:694
  181.7 5.7 %collective-permute-start.28 = (f32[2,128]{1,0:T(2,128)S(1)}, f32[2,128]{1,0:T(2,128)S(1)}, u32[]{:S(2)}, u32[]{:S(2)}) collective-permute-start(f32[2,128]{1,0:T(2,128)S(1)} %get-tuple-element.106), channel_id=1, source_target_pairs={{0,12},{1,13},{2,14},{3,15},{4,8},{5,9},{6,10},{7,11},{8,4},{9,5},... | collective-permute-start | bytes 3080 | tf_op jit(solution)/shard_map/ppermute | solution.py:694
  187.4 1.9 collective-permute-start.30
  189.4 1.4 collective-permute-start.35
  190.8 4.8 %put_residuals.3.refs_2_ = bf16[2,8,2,256,256]{4,3,2,1,0:T(8,128)(2,1)} custom-call(s32[148]{0:T(256)S(1)} %bitcast.37, bf16[2,2,256,256]{3,2,1,0:T(8,128)(2,1)} %collective-permute-done.19.refs_0_, bf16[2,2,256,256]{3,2,1,0:T(8,128)(2,1)} %collective-permute-done.20.refs_1_, bf16[2,2,256,256]{3,2,1,0:T(8,128)(2,1)S(1)} %collective-permute-done.27.refs_2_, ...), custom_call_target="tpu_custom_call" | custom-call | flops 1 | bytes 1 | tf_op jit(solution)/shard_map/put_residuals/pallas_call | solution.py:516
  197.6 2.1 %put_residuals.4.refs_2_ = bf16[2,8,2,256,256]{4,3,2,1,0:T(8,128)(2,1)} custom-call(s32[148]{0:T(256)S(1)} %bitcast.38, bf16[2,2,256,256]{3,2,1,0:T(8,128)(2,1)S(1)} %collective-permute-done.36.refs_0_, bf16[2,2,256,256]{3,2,1,0:T(8,128)(2,1)S(1)} %get-tuple-element.117.refs_1_, ...), custom_call_target="tpu_custom_call", output_to_operand_aliasing={{}: (3, {})} | custom-call | flops 1 | bytes 1 | tf_op jit(solution)/shard_map/put_residuals/pallas_call | solution.py:516
  199.7 3.9 %collective-permute-done.33 = f32[2,32]{1,0:T(2,128)S(1)} collective-permute-done((f32[2,32]{1,0:T(2,128)S(1)}, f32[2,32]{1,0:T(2,128)S(1)}, u32[]{:S(2)}, u32[]{:S(2)}) %collective-permute-start.33) | collective-permute-done | bytes 288 | tf_op jit(solution)/shard_map/ppermute | solution.py:694
  204.4 2.1 %put_residuals.5 = bf16[2,8,2,256,256]{4,3,2,1,0:T(8,128)(2,1)} custom-call(s32[148]{0:T(256)S(1)} %bitcast.39, bf16[2,2,256,256]{3,2,1,0:T(8,128)(2,1)S(1)} %collective-permute-done.29.refs_0_, bf16[2,2,256,256]{3,2,1,0:T(8,128)(2,1)S(1)} %collective-permute-done.35.refs_1_, ...), custom_call_target="tpu_custom_call", output_to_operand_aliasing={{}: (3, {})} | custom-call | flops 1 | bytes 1 | tf_op jit(solution)/shard_map/put_residuals/pallas_call | solution.py:516
  (173 shorter events, 25.4 us)
Async XLA Ops:
  5.7 1.9 collective-permute-start
  11.9 17.4 %collective-permute-start.2 = (bf16[2,528,256]{2,1,0:T(8,128)(2,1)S(1)}, bf16[2,528,256]{2,1,0:T(8,128)(2,1)S(1)}, u32[]{:S(2)}, u32[]{:S(2)}) collective-permute-start(bf16[2,528,256]{2,1,0:T(8,128)(2,1)S(1)} %build_factors.3.refs_0_), channel_id=1, source_target_pairs={{0,8},{1,9},{2,10},{3,11},{4,0},{5,1},{6,2},{7,3},{8,12},{9,13},{1... | collective-permute-start | bytes 1622024 | tf_op jit(solution)/shard_map/ppermute | solution.py:694
  18.5 26.5 %copy-start.38 = (s32[1,148]{1,0:T(1,128)S(1)}, s32[1,148]{1,0:T(1,128)}, u32[]{:S(2)}) copy-start(s32[1,148]{1,0:T(1,128)} %constant_dynamic-slice_fusion) | copy-start | bytes 1780
  18.5 10.8 %collective-permute-start.5 = (bf16[80,2048]{1,0:T(8,128)(2,1)}, bf16[80,2048]{1,0:T(8,128)(2,1)S(1)}, u32[]{:S(2)}, u32[]{:S(2)}) collective-permute-start(bf16[80,2048]{1,0:T(8,128)(2,1)} %get-tuple-element.62), channel_id=1, source_target_pairs={{0,2},{1,3},{2,0},{3,1},{4,6},{5,7},{6,4},{7,5},{8,10},{9,11},{10,... | collective-permute-start | bytes 983048 | tf_op jit(solution)/shard_map/ppermute | solution.py:694
  20.0 22.0 %collective-permute-start.1 = (bf16[2,528,256]{2,1,0:T(8,128)(2,1)S(1)}, bf16[2,528,256]{2,1,0:T(8,128)(2,1)S(1)}, u32[]{:S(2)}, u32[]{:S(2)}) collective-permute-start(bf16[2,528,256]{2,1,0:T(8,128)(2,1)S(1)} %build_factors.3.refs_0_), channel_id=1, source_target_pairs={{0,4},{1,5},{2,6},{3,7},{4,12},{5,13},{6,14},{7,15},{8,0},{9,1},{1... | collective-permute-start | bytes 1622024 | tf_op jit(solution)/shard_map/ppermute | solution.py:694
  22.7 24.7 %collective-permute-start.11 = (bf16[64,2048]{1,0:T(8,128)(2,1)}, bf16[64,2048]{1,0:T(8,128)(2,1)S(1)}, u32[]{:S(2)}, u32[]{:S(2)}) collective-permute-start(bf16[64,2048]{1,0:T(8,128)(2,1)} %get-tuple-element.73), channel_id=1, source_target_pairs={{0,3},{1,2},{2,1},{3,0},{4,7},{5,6},{6,5},{7,4},{8,11},{9,10},{10,... | collective-permute-start | bytes 786440 | tf_op jit(solution)/shard_map/ppermute | solution.py:694
  29.3 15.7 %collective-permute-start.6 = (bf16[80,2048]{1,0:T(8,128)(2,1)S(1)}, bf16[80,2048]{1,0:T(8,128)(2,1)S(1)}, u32[]{:S(2)}, u32[]{:S(2)}) collective-permute-start(bf16[80,2048]{1,0:T(8,128)(2,1)S(1)} %copy-done.53), channel_id=1, source_target_pairs={{0,3},{1,2},{2,1},{3,0},{4,7},{5,6},{6,5},{7,4},{8,11},{9,10},{10,... | collective-permute-start | bytes 983048 | tf_op jit(solution)/shard_map/ppermute | solution.py:694
  30.1 28.5 %collective-permute-start.4 = (bf16[528,256]{1,0:T(8,128)(2,1)}, bf16[528,256]{1,0:T(8,128)(2,1)}, u32[]{:S(2)}, u32[]{:S(2)}) collective-permute-start(bf16[528,256]{1,0:T(8,128)(2,1)} %slice_bitcast_fusion.2), channel_id=1, source_target_pairs={{0,8},{1,9},{2,10},{3,11},{4,0},{5,1},{6,2},{7,3},{8,12},{9,13},{1... | collective-permute-start | bytes 811016 | tf_op jit(solution)/shard_map/ppermute | solution.py:694
  42.8 15.8 %collective-permute-start.3 = (bf16[528,256]{1,0:T(8,128)(2,1)}, bf16[528,256]{1,0:T(8,128)(2,1)}, u32[]{:S(2)}, u32[]{:S(2)}) collective-permute-start(bf16[528,256]{1,0:T(8,128)(2,1)} %slice_bitcast_fusion.3), channel_id=1, source_target_pairs={{0,4},{1,5},{2,6},{3,7},{4,12},{5,13},{6,14},{7,15},{8,0},{9,1},{1... | collective-permute-start | bytes 811016 | tf_op jit(solution)/shard_map/ppermute | solution.py:694
  43.4 7.7 %collective-permute-start.9 = (bf16[64,2048]{1,0:T(8,128)(2,1)}, bf16[64,2048]{1,0:T(8,128)(2,1)S(1)}, u32[]{:S(2)}, u32[]{:S(2)}) collective-permute-start(bf16[64,2048]{1,0:T(8,128)(2,1)} %get-tuple-element.69), channel_id=1, source_target_pairs={{0,2},{1,3},{2,0},{3,1},{4,6},{5,7},{6,4},{7,5},{8,10},{9,11},{10,... | collective-permute-start | bytes 786440 | tf_op jit(solution)/shard_map/ppermute | solution.py:694
  45.0 13.6 %collective-permute-start.10 = (bf16[64,2048]{1,0:T(8,128)(2,1)}, bf16[64,2048]{1,0:T(8,128)(2,1)}, u32[]{:S(2)}, u32[]{:S(2)}) collective-permute-start(bf16[64,2048]{1,0:T(8,128)(2,1)} %get-tuple-element.72), channel_id=1, source_target_pairs={{0,1},{1,0},{2,3},{3,2},{4,5},{5,4},{6,7},{7,6},{8,9},{9,8},{10,11... | collective-permute-start | bytes 786440 | tf_op jit(solution)/shard_map/ppermute | solution.py:694
  48.1 20.5 %collective-permute-start.8 = (bf16[2,528,256]{2,1,0:T(8,128)(2,1)S(1)}, bf16[2,528,256]{2,1,0:T(8,128)(2,1)}, u32[]{:S(2)}, u32[]{:S(2)}) collective-permute-start(bf16[2,528,256]{2,1,0:T(8,128)(2,1)S(1)} %build_factors.4.refs_5_), channel_id=1, source_target_pairs={{0,8},{1,9},{2,10},{3,11},{4,0},{5,1},{6,2},{7,3},{8,12},{9,13},{1... | collective-permute-start | bytes 1622024 | tf_op jit(solution)/shard_map/ppermute | solution.py:694
  51.9 25.8 %collective-permute-start.7 = (bf16[2,528,256]{2,1,0:T(8,128)(2,1)S(1)}, bf16[2,528,256]{2,1,0:T(8,128)(2,1)}, u32[]{:S(2)}, u32[]{:S(2)}) collective-permute-start(bf16[2,528,256]{2,1,0:T(8,128)(2,1)S(1)} %build_factors.4.refs_5_), channel_id=1, source_target_pairs={{0,4},{1,5},{2,6},{3,7},{4,12},{5,13},{6,14},{7,15},{8,0},{9,1},{1... | collective-permute-start | bytes 1622024 | tf_op jit(solution)/shard_map/ppermute | solution.py:694
  54.6 51.8 %copy-start.50 = (s32[8,2048]{1,0:T(8,128)S(1)}, s32[8,2048]{1,0:T(8,128)}, u32[]{:S(2)}) copy-start(s32[8,2048]{1,0:T(8,128)} %param.14) | copy-start | bytes 196612
  58.6 47.8 %copy-start.5 = (bf16[2,528,256]{2,1,0:T(8,128)(2,1)S(1)}, bf16[2,528,256]{2,1,0:T(8,128)(2,1)}, u32[]{:S(2)}) copy-start(bf16[2,528,256]{2,1,0:T(8,128)(2,1)} %copy-done.4) | copy-start | bytes 1622020
  58.6 47.8 %copy-start.8 = (bf16[2,528,256]{2,1,0:T(8,128)(2,1)S(1)}, bf16[2,528,256]{2,1,0:T(8,128)(2,1)}, u32[]{:S(2)}) copy-start(bf16[2,528,256]{2,1,0:T(8,128)(2,1)} %copy-done.7) | copy-start | bytes 1622020
  58.6 44.4 %collective-permute-start.14 = (bf16[2,2,2,256,256]{4,3,2,1,0:T(8,128)(2,1)}, bf16[2,2,2,256,256]{4,3,2,1,0:T(8,128)(2,1)S(1)}, u32[]{:S(2)}, u32[]{:S(2)}) collective-permute-start(bf16[2,2,2,256,256]{4,3,2,1,0:T(8,128)(2,1)} %get-tuple-element.79), channel_id=1, source_target_pairs={{0,2},{1,3},{2,0},{3,1},{4,6},{5,7},{6,4},{7,5},{8,10},{9,11},{10,... | collective-permute-start | bytes 3145736 | tf_op jit(solution)/shard_map/ppermute | solution.py:694
  68.6 46.8 %copy-start.18 = (bf16[2,512,256]{2,1,0:T(8,128)(2,1)}, bf16[2,512,256]{2,1,0:T(8,128)(2,1)S(1)}, u32[]{:S(2)}) copy-start(bf16[2,512,256]{2,1,0:T(8,128)(2,1)S(1)} %get-tuple-element.89.refs_0_) | copy-start | bytes 1572868
  68.6 57.0 %copy-start.20 = (bf16[2,512,256]{2,1,0:T(8,128)(2,1)}, bf16[2,512,256]{2,1,0:T(8,128)(2,1)S(1)}, u32[]{:S(2)}) copy-start(bf16[2,512,256]{2,1,0:T(8,128)(2,1)S(1)} %get-tuple-element.97.refs_5_) | copy-start | bytes 1572868
  69.8 13.1 %collective-permute-start.13 = (bf16[528,256]{1,0:T(8,128)(2,1)S(1)}, bf16[528,256]{1,0:T(8,128)(2,1)S(1)}, u32[]{:S(2)}, u32[]{:S(2)}) collective-permute-start(bf16[528,256]{1,0:T(8,128)(2,1)S(1)} %slice_bitcast_fusion), channel_id=1, source_target_pairs={{0,8},{1,9},{2,10},{3,11},{4,0},{5,1},{6,2},{7,3},{8,12},{9,13},{1... | collective-permute-start | bytes 811016 | tf_op jit(solution)/shard_map/ppermute | solution.py:694
  78.6 10.2 %collective-permute-start.12 = (bf16[528,256]{1,0:T(8,128)(2,1)S(1)}, bf16[528,256]{1,0:T(8,128)(2,1)S(1)}, u32[]{:S(2)}, u32[]{:S(2)}) collective-permute-start(bf16[528,256]{1,0:T(8,128)(2,1)S(1)} %slice_bitcast_fusion.1), channel_id=1, source_target_pairs={{0,4},{1,5},{2,6},{3,7},{4,12},{5,13},{6,14},{7,15},{8,0},{9,1},{1... | collective-permute-start | bytes 811016 | tf_op jit(solution)/shard_map/ppermute | solution.py:694
  78.7 37.9 %collective-permute-start.16 = (bf16[2,2,2,256,256]{4,3,2,1,0:T(8,128)(2,1)S(1)}, bf16[2,2,2,256,256]{4,3,2,1,0:T(8,128)(2,1)S(1)}, u32[]{:S(2)}, u32[]{:S(2)}) collective-permute-start(bf16[2,2,2,256,256]{4,3,2,1,0:T(8,128)(2,1)S(1)} %copy-done.52), channel_id=1, source_target_pairs={{0,3},{1,2},{2,1},{3,0},{4,7},{5,6},{6,5},{7,4},{8,11},{9,10},{10,... | collective-permute-start | bytes 3145736 | tf_op jit(solution)/shard_map/ppermute | solution.py:694
  78.8 41.7 %collective-permute-start.15 = (bf16[2,2,2,256,256]{4,3,2,1,0:T(8,128)(2,1)S(1)}, bf16[2,2,2,256,256]{4,3,2,1,0:T(8,128)(2,1)S(1)}, u32[]{:S(2)}, u32[]{:S(2)}) collective-permute-start(bf16[2,2,2,256,256]{4,3,2,1,0:T(8,128)(2,1)S(1)} %copy-done.51), channel_id=1, source_target_pairs={{0,1},{1,0},{2,3},{3,2},{4,5},{5,4},{6,7},{7,6},{8,9},{9,8},{10,11... | collective-permute-start | bytes 3145736 | tf_op jit(solution)/shard_map/ppermute | solution.py:694
  82.9 28.8 %collective-permute-start.21 = (bf16[2,512,256]{2,1,0:T(8,128)(2,1)S(1)}, bf16[2,512,256]{2,1,0:T(8,128)(2,1)S(1)}, u32[]{:S(2)}, u32[]{:S(2)}) collective-permute-start(bf16[2,512,256]{2,1,0:T(8,128)(2,1)S(1)} %get-tuple-element.89.refs_0_), channel_id=1, source_target_pairs={{0,8},{1,9},{2,10},{3,11},{4,0},{5,1},{6,2},{7,3},{8,12},{9,13},{1... | collective-permute-start | bytes 1572872 | tf_op jit(solution)/shard_map/ppermute | solution.py:694
  88.8 26.6 %collective-permute-start.17 = (bf16[2,512,256]{2,1,0:T(8,128)(2,1)S(1)}, bf16[2,512,256]{2,1,0:T(8,128)(2,1)S(1)}, u32[]{:S(2)}, u32[]{:S(2)}) collective-permute-start(bf16[2,512,256]{2,1,0:T(8,128)(2,1)S(1)} %get-tuple-element.89.refs_0_), channel_id=1, source_target_pairs={{0,4},{1,5},{2,6},{3,7},{4,12},{5,13},{6,14},{7,15},{8,0},{9,1},{1... | collective-permute-start | bytes 1572872 | tf_op jit(solution)/shard_map/ppermute | solution.py:694
  103.0 22.6 %copy-start.24 = (bf16[2,2,2,256,256]{4,3,2,1,0:T(8,128)(2,1)}, bf16[2,2,2,256,256]{4,3,2,1,0:T(8,128)(2,1)S(1)}, u32[]{:S(2)}) copy-start(bf16[2,2,2,256,256]{4,3,2,1,0:T(8,128)(2,1)S(1)} %collective-permute-done.14.refs_10_) | copy-start | bytes 3145732
  103.0 23.6 %collective-permute-start.23 = (bf16[2,512,256]{2,1,0:T(8,128)(2,1)S(1)}, bf16[2,512,256]{2,1,0:T(8,128)(2,1)S(1)}, u32[]{:S(2)}, u32[]{:S(2)}) collective-permute-start(bf16[2,512,256]{2,1,0:T(8,128)(2,1)S(1)} %get-tuple-element.97.refs_5_), channel_id=1, source_target_pairs={{0,4},{1,5},{2,6},{3,7},{4,12},{5,13},{6,14},{7,15},{8,0},{9,1},{1... | collective-permute-start | bytes 1572872 | tf_op jit(solution)/shard_map/ppermute | solution.py:694
  111.8 40.4 %copy-start.6 = (bf16[2,528,256]{2,1,0:T(8,128)(2,1)S(1)}, bf16[2,528,256]{2,1,0:T(8,128)(2,1)}, u32[]{:S(2)}) copy-start(bf16[2,528,256]{2,1,0:T(8,128)(2,1)} %copy-done.4) | copy-start | bytes 1622020
  111.8 40.4 %copy-start.9 = (bf16[2,528,256]{2,1,0:T(8,128)(2,1)S(1)}, bf16[2,528,256]{2,1,0:T(8,128)(2,1)}, u32[]{:S(2)}) copy-start(bf16[2,528,256]{2,1,0:T(8,128)(2,1)} %copy-done.7) | copy-start | bytes 1622020
  111.8 28.0 %collective-permute-start.24 = (bf16[2,512,256]{2,1,0:T(8,128)(2,1)S(1)}, bf16[2,512,256]{2,1,0:T(8,128)(2,1)S(1)}, u32[]{:S(2)}, u32[]{:S(2)}) collective-permute-start(bf16[2,512,256]{2,1,0:T(8,128)(2,1)S(1)} %get-tuple-element.97.refs_5_), channel_id=1, source_target_pairs={{0,8},{1,9},{2,10},{3,11},{4,0},{5,1},{6,2},{7,3},{8,12},{9,13},{1... | collective-permute-start | bytes 1572872 | tf_op jit(solution)/shard_map/ppermute | solution.py:694
  115.4 47.4 %collective-permute-start.19 = (bf16[2,2,256,256]{3,2,1,0:T(8,128)(2,1)}, bf16[2,2,256,256]{3,2,1,0:T(8,128)(2,1)}, u32[]{:S(2)}, u32[]{:S(2)}) collective-permute-start(bf16[2,2,256,256]{3,2,1,0:T(8,128)(2,1)} %get-tuple-element.91), channel_id=1, source_target_pairs={{0,2},{1,3},{2,0},{3,1},{4,6},{5,7},{6,4},{7,5},{8,10},{9,11},{10,... | collective-permute-start | bytes 1572872 | tf_op jit(solution)/shard_map/ppermute | solution.py:694
  116.6 32.6 %copy-start.22 = (bf16[2,2,2,256,256]{4,3,2,1,0:T(8,128)(2,1)}, bf16[2,2,2,256,256]{4,3,2,1,0:T(8,128)(2,1)S(1)}, u32[]{:S(2)}) copy-start(bf16[2,2,2,256,256]{4,3,2,1,0:T(8,128)(2,1)S(1)} %collective-permute-done.16.refs_10_) | copy-start | bytes 3145732
  116.6 46.3 %collective-permute-start.22 = (bf16[512,256]{1,0:T(8,128)(2,1)}, bf16[512,256]{1,0:T(8,128)(2,1)}, u32[]{:S(2)}, u32[]{:S(2)}) collective-permute-start(bf16[512,256]{1,0:T(8,128)(2,1)} %slice_bitcast_fusion.6), channel_id=1, source_target_pairs={{0,8},{1,9},{2,10},{3,11},{4,0},{5,1},{6,2},{7,3},{8,12},{9,13},{1... | collective-permute-start | bytes 786440 | tf_op jit(solution)/shard_map/ppermute | solution.py:694
  120.4 29.5 %copy-start.26 = (bf16[2,2,2,256,256]{4,3,2,1,0:T(8,128)(2,1)}, bf16[2,2,2,256,256]{4,3,2,1,0:T(8,128)(2,1)S(1)}, u32[]{:S(2)}) copy-start(bf16[2,2,2,256,256]{4,3,2,1,0:T(8,128)(2,1)S(1)} %collective-permute-done.15.refs_10_) | copy-start | bytes 3145732
  120.4 29.5 %collective-permute-start.18 = (bf16[512,256]{1,0:T(8,128)(2,1)S(1)}, bf16[512,256]{1,0:T(8,128)(2,1)S(1)}, u32[]{:S(2)}, u32[]{:S(2)}) collective-permute-start(bf16[512,256]{1,0:T(8,128)(2,1)S(1)} %slice_bitcast_fusion.7), channel_id=1, source_target_pairs={{0,4},{1,5},{2,6},{3,7},{4,12},{5,13},{6,14},{7,15},{8,0},{9,1},{1... | collective-permute-start | bytes 786440 | tf_op jit(solution)/shard_map/ppermute | solution.py:694
  126.6 36.2 %collective-permute-start.20 = (bf16[2,2,256,256]{3,2,1,0:T(8,128)(2,1)}, bf16[2,2,256,256]{3,2,1,0:T(8,128)(2,1)}, u32[]{:S(2)}, u32[]{:S(2)}) collective-permute-start(bf16[2,2,256,256]{3,2,1,0:T(8,128)(2,1)} %get-tuple-element.92), channel_id=1, source_target_pairs={{0,3},{1,2},{2,1},{3,0},{4,7},{5,6},{6,5},{7,4},{8,11},{9,10},{10,... | collective-permute-start | bytes 1572872 | tf_op jit(solution)/shard_map/ppermute | solution.py:694
  139.8 23.1 %collective-permute-start.25 = (bf16[512,256]{1,0:T(8,128)(2,1)}, bf16[512,256]{1,0:T(8,128)(2,1)}, u32[]{:S(2)}, u32[]{:S(2)}) collective-permute-start(bf16[512,256]{1,0:T(8,128)(2,1)} %slice_bitcast_fusion.5), channel_id=1, source_target_pairs={{0,4},{1,5},{2,6},{3,7},{4,12},{5,13},{6,14},{7,15},{8,0},{9,1},{1... | collective-permute-start | bytes 786440 | tf_op jit(solution)/shard_map/ppermute | solution.py:694
  150.7 12.2 %collective-permute-start.26 = (bf16[512,256]{1,0:T(8,128)(2,1)}, bf16[512,256]{1,0:T(8,128)(2,1)}, u32[]{:S(2)}, u32[]{:S(2)}) collective-permute-start(bf16[512,256]{1,0:T(8,128)(2,1)} %slice_bitcast_fusion.4), channel_id=1, source_target_pairs={{0,8},{1,9},{2,10},{3,11},{4,0},{5,1},{6,2},{7,3},{8,12},{9,13},{1... | collective-permute-start | bytes 786440 | tf_op jit(solution)/shard_map/ppermute | solution.py:694
  162.8 18.9 %collective-permute-start.27 = (bf16[2,2,256,256]{3,2,1,0:T(8,128)(2,1)S(1)}, bf16[2,2,256,256]{3,2,1,0:T(8,128)(2,1)S(1)}, u32[]{:S(2)}, u32[]{:S(2)}) collective-permute-start(bf16[2,2,256,256]{3,2,1,0:T(8,128)(2,1)S(1)} %get-tuple-element.105), channel_id=1, source_target_pairs={{0,1},{1,0},{2,3},{3,2},{4,5},{5,4},{6,7},{7,6},{8,9},{9,8},{10,11... | collective-permute-start | bytes 1572872 | tf_op jit(solution)/shard_map/ppermute | solution.py:694
  167.2 20.2 %collective-permute-start.29 = (bf16[2,2,256,256]{3,2,1,0:T(8,128)(2,1)S(1)}, bf16[2,2,256,256]{3,2,1,0:T(8,128)(2,1)S(1)}, u32[]{:S(2)}, u32[]{:S(2)}) collective-permute-start(bf16[2,2,256,256]{3,2,1,0:T(8,128)(2,1)S(1)} %get-tuple-element.107), channel_id=1, source_target_pairs={{0,2},{1,3},{2,0},{3,1},{4,6},{5,7},{6,4},{7,5},{8,10},{9,11},{10,... | collective-permute-start | bytes 1572872 | tf_op jit(solution)/shard_map/ppermute | solution.py:694
  179.1 16.5 %collective-permute-start.31 = (f32[2,128]{1,0:T(2,128)S(1)}, f32[2,128]{1,0:T(2,128)S(1)}, u32[]{:S(2)}, u32[]{:S(2)}) collective-permute-start(f32[2,128]{1,0:T(2,128)S(1)} %get-tuple-element.119), channel_id=1, source_target_pairs={{0,4},{1,5},{2,6},{3,7},{4,12},{5,13},{6,14},{7,15},{8,0},{9,1},{1... | collective-permute-start | bytes 3080 | tf_op jit(solution)/shard_map/ppermute | solution.py:694
  181.7 13.9 %collective-permute-start.28 = (f32[2,128]{1,0:T(2,128)S(1)}, f32[2,128]{1,0:T(2,128)S(1)}, u32[]{:S(2)}, u32[]{:S(2)}) collective-permute-start(f32[2,128]{1,0:T(2,128)S(1)} %get-tuple-element.106), channel_id=1, source_target_pairs={{0,12},{1,13},{2,14},{3,15},{4,8},{5,9},{6,10},{7,11},{8,4},{9,5},... | collective-permute-start | bytes 3080 | tf_op jit(solution)/shard_map/ppermute | solution.py:694
  187.4 10.2 %collective-permute-start.36 = (bf16[2,2,256,256]{3,2,1,0:T(8,128)(2,1)S(1)}, bf16[2,2,256,256]{3,2,1,0:T(8,128)(2,1)S(1)}, u32[]{:S(2)}, u32[]{:S(2)}) collective-permute-start(bf16[2,2,256,256]{3,2,1,0:T(8,128)(2,1)S(1)} %get-tuple-element.116), channel_id=1, source_target_pairs={{0,1},{1,0},{2,3},{3,2},{4,5},{5,4},{6,7},{7,6},{8,9},{9,8},{10,11... | collective-permute-start | bytes 1572872 | tf_op jit(solution)/shard_map/ppermute | solution.py:694
  187.4 8.2 %collective-permute-start.30 = (f32[2,128]{1,0:T(2,128)S(1)}, f32[2,128]{1,0:T(2,128)S(1)}, u32[]{:S(2)}, u32[]{:S(2)}) collective-permute-start(f32[2,128]{1,0:T(2,128)S(1)} %get-tuple-element.108), channel_id=1, source_target_pairs={{0,8},{1,9},{2,10},{3,11},{4,0},{5,1},{6,2},{7,3},{8,12},{9,13},{1... | collective-permute-start | bytes 3080 | tf_op jit(solution)/shard_map/ppermute | solution.py:694
  189.4 15.0 %collective-permute-start.35 = (bf16[2,2,256,256]{3,2,1,0:T(8,128)(2,1)S(1)}, bf16[2,2,256,256]{3,2,1,0:T(8,128)(2,1)S(1)}, u32[]{:S(2)}, u32[]{:S(2)}) collective-permute-start(bf16[2,2,256,256]{3,2,1,0:T(8,128)(2,1)S(1)} %get-tuple-element.114), channel_id=1, source_target_pairs={{0,3},{1,2},{2,1},{3,0},{4,7},{5,6},{6,5},{7,4},{8,11},{9,10},{10,... | collective-permute-start | bytes 1572872 | tf_op jit(solution)/shard_map/ppermute | solution.py:694
  195.7 4.0 %collective-permute-start.32 = (f32[2,32]{1,0:T(2,128)S(1)}, f32[2,32]{1,0:T(2,128)S(1)}, u32[]{:S(2)}, u32[]{:S(2)}) collective-permute-start(f32[2,32]{1,0:T(2,128)S(1)} %get-tuple-element.109), channel_id=1, source_target_pairs={{0,1},{1,0},{2,3},{3,2},{4,5},{5,4},{6,7},{7,6},{8,9},{9,8},{10,11... | collective-permute-start | bytes 776 | tf_op jit(solution)/shard_map/ppermute | solution.py:694
  196.0 7.7 %collective-permute-start.33 = (f32[2,32]{1,0:T(2,128)S(1)}, f32[2,32]{1,0:T(2,128)S(1)}, u32[]{:S(2)}, u32[]{:S(2)}) collective-permute-start(f32[2,32]{1,0:T(2,128)S(1)} %get-tuple-element.111), channel_id=1, source_target_pairs={{0,2},{1,3},{2,0},{3,1},{4,6},{5,7},{6,4},{7,5},{8,10},{9,11},{10,... | collective-permute-start | bytes 776 | tf_op jit(solution)/shard_map/ppermute | solution.py:694
  196.5 7.2 %collective-permute-start.34 = (f32[2,32]{1,0:T(2,128)S(1)}, f32[2,32]{1,0:T(2,128)S(1)}, u32[]{:S(2)}, u32[]{:S(2)}) collective-permute-start(f32[2,32]{1,0:T(2,128)S(1)} %get-tuple-element.122), channel_id=1, source_target_pairs={{0,3},{1,2},{2,1},{3,0},{4,7},{5,6},{6,5},{7,4},{8,11},{9,10},{10,... | collective-permute-start | bytes 776 | tf_op jit(solution)/shard_map/ppermute | solution.py:694
  (43 other events, 260.8 us)

commit v13 on v10

--- a/solution.py
+++ b/solution.py
@@ -661,9 +661,7 @@
     34: (33,),
     35: (8, 9, 24, 25),
     40: (28, 34, 36, 37),
-    41: (40,),
-    42: (29, 41),
-    43: (41,),
+    41: (29, 40),
     45: (28, 32),
     48: (35,),
     49: (44,),
@@ -749,9 +747,9 @@
 
     grads = []
 
-    def work(index, step, home_step, ready, bright):
+    def work(index, step, home_step, ready, bright, calls):
         arrived, total = [], None
-        for n, homes in enumerate([routes.order[:1], routes.order[1:2], routes.order[2:]]):
+        for n, homes in enumerate(calls):
             made = unit_work(
                 index,
                 routes.steps[index] + len(arrived) * routes.steps_per_home,
@@ -784,14 +782,17 @@
     number = group // 2
     pieces = entries(own, own_sides, own_far, 0, number)
     pieces += entries(rest, rest_sides, rest_far, number, number)
-    arrived, columns = work(0, WORK, HOME, [pieces], share)
+    order = routes.order
+    arrived, columns = work(
+        0, WORK, HOME, [pieces], share, [order[:1], order[1:2], order[2:]]
+    )
     far_1 = far(PIECE_FAR[1], near_1)
     residual = put(PUT, 0, arrived, 0, None)
     ready = [
         entries(piece, sides, halves, 0, group)
         for piece, sides, halves in zip(later_pieces, (near_0, near_1), (far_0, far_1))
     ]
-    arrived, _ = work(1, LATER_WORK, LATER_HOME, ready, columns)
+    arrived, _ = work(1, LATER_WORK, LATER_HOME, ready, columns, [order[:1], order[1:]])
 
     partial = jnp.concatenate(grads, 0)
     parts = [partial[:, n * group : (n + 1) * group] for n in range(4)]

time: 202 us -> 211 us (1.045)
  waiting for transfers between devices: 61.5 us -> 70.2 us
  local copies, waits for them, and re-layouts: 25.2 us -> 28.7 us
  Pallas kernels: 59.8 us -> 56.4 us
    ppermute x37, waiting for transfers between devices: 61.5 us -> 70.2 us  [send(): done[step] = lax.ppermute(gated(step, value), 'tile', pairs)]
    pallas_call x6 -> x5, Pallas kernels: 32.4 us -> 28.1 us  [unit_work(): pl.pallas_call(functools.partial(unit_kernel, index, offset, kinds, brigh...]
    unnamed x109 -> x115, local copies, waits for them, and re-layouts: 19.6 us -> 23.8 us
  transfers between devices with their start and end apart: 37 -> 37, of which waited for: 10 -> 12; matrix products, arithmetic and copies ran while one was open for 3% -> 2% of each run, Pallas kernels for 28% -> 25%
where the time goes in v13:
time: 211 us; the launch traced here: 210 us
  waiting for transfers between devices  70.2 us (33%)
  Pallas kernels  56.4 us (27%)
  starting transfers between devices  50.8 us (24%)
  local copies, waits for them, and re-layouts  28.7 us (14%)
  other arithmetic  2.2 us (1%)
    ppermute x37, waiting for transfers between devices, send(): done[step] = lax.ppermute(gated(step, value), 'tile', pairs)  70.2 us
    ppermute x37, starting transfers between devices, send(): done[step] = lax.ppermute(gated(step, value), 'tile', pairs)  50.8 us
    pallas_call x5, Pallas kernels, unit_work(): pl.pallas_call(functools.partial(unit_kernel, index, offset, kinds, brigh...  28.1 us
    unnamed x115, local copies, waits for them, and re-layouts  23.8 us
    pallas_call x3, Pallas kernels, put_residuals(): pl.pallas_call(functools.partial(put_kernel, sources), grid_spec=pltpu.Pr...  9.98 us
    pallas_call x3, Pallas kernels, messages_for(): pl.pallas_call(functools.partial(message_kernel, len(others), bool(smalls...  7.72 us
    pallas_call x3, Pallas kernels, build_factors(): pl.pallas_call(functools.partial(build_kernel, sets, slot_ids, pieces, br...  6.7 us
  transfers between devices with their start and end apart: 37, of which 12 were waited for; matrix products, arithmetic and copies ran while one was open for 2% of the time, Pallas kernels for 25%

profile of v13, /device:TPU:0, one launch (start us, length us, event | category | flops | bytes accessed | tf_op | source)
XLA Modules:
  0.0 209.6 jit_solution(5319588987880297164)
XLA Ops:
  0.6 1.4 broadcast_in_dim.34
  2.0 1.3 constant_dynamic-slice_fusion
  3.3 2.4 %messages_for.3 = bf16[80,2048]{1,0:T(8,128)(2,1)} custom-call(s32[148]{0:T(256)} %bitcast.24, bf16[8,2,32,2048]{3,2,1,0:T(8,128)(2,1)} %refs_0_.10, f32[2,256]{1,0:T(2,128)} %refs_4_.5, f32[1,256]{1,0:T(1,128)} %bitcast.39, s32[8,32]{1,0:T(8,128)} %refs_6_.1), custom_call_target="tpu_custom_call" | custom-call | flops 1 | bytes 1 | tf_op jit(solution)/shard_map/messages_for/pallas_call | solution.py:211
  6.1 1.1 copy.15.refs_5_.refs_10_.refs_2_
  10.3 1.6 build_factors.3.refs_0_
  12.0 4.0 %collective-permute-start.1 = (bf16[2,528,256]{2,1,0:T(8,128)(2,1)S(1)}, bf16[2,528,256]{2,1,0:T(8,128)(2,1)S(1)}, u32[]{:S(2)}, u32[]{:S(2)}) collective-permute-start(bf16[2,528,256]{2,1,0:T(8,128)(2,1)S(1)} %build_factors.3.refs_0_), channel_id=1, source_target_pairs={{0,8},{1,9},{2,10},{3,11},{4,0},{5,1},{6,2},{7,3},{8,12},{9,13},{1... | collective-permute-start | bytes 1622024 | tf_op jit(solution)/shard_map/ppermute | solution.py:689
  16.0 2.6 %messages_for.5 = (bf16[80,2048]{1,0:T(8,128)(2,1)}, bf16[80,2048]{1,0:T(8,128)(2,1)}) custom-call(s32[148]{0:T(256)} %bitcast.25, bf16[8,2,32,2048]{3,2,1,0:T(8,128)(2,1)} %refs_0_.10, bf16[8,2,32,2048]{3,2,1,0:T(8,128)(2,1)} %refs_0_.10, f32[2,256]{1,0:T(2,128)} %refs_4_.5, f32[1,256]{1,0:T(1,128)} %bitcast.40, s32[8,32]{1,0:T(8,128)} %refs_6_.1), custom_call_target="tpu_custom_call" | custom-call | flops 1 | bytes 1 | tf_op jit(solution)/shard_map/messages_for/pallas_call | solution.py:211
  18.6 1.5 collective-permute-start.7
  20.1 2.7 %messages_for.4 = (bf16[64,2048]{1,0:T(8,128)(2,1)}, bf16[64,2048]{1,0:T(8,128)(2,1)}, bf16[64,2048]{1,0:T(8,128)(2,1)}) custom-call(s32[148]{0:T(256)} %bitcast.26, bf16[8,2,32,2048]{3,2,1,0:T(8,128)(2,1)} %refs_0_.10, bf16[8,2,32,2048]{3,2,1,0:T(8,128)(2,1)} %refs_0_.10, bf16[8,2,32,2048]{3,2,1,0:T(8,128)(2,1)} %refs_0_.10), custom_call_target="tpu_custom_call" | custom-call | flops 1 | bytes 1 | tf_op jit(solution)/shard_map/messages_for/pallas_call | solution.py:211
  22.8 6.6 %collective-permute-done.7.refs_8_.refs_0_ = bf16[80,2048]{1,0:T(8,128)(2,1)S(1)} collective-permute-done((bf16[80,2048]{1,0:T(8,128)(2,1)}, bf16[80,2048]{1,0:T(8,128)(2,1)S(1)}, u32[]{:S(2)}, u32[]{:S(2)}) %collective-permute-start.7) | collective-permute-done | bytes 327712 | tf_op jit(solution)/shard_map/ppermute | solution.py:689
  30.2 2.6 %collective-permute-start.2 = (bf16[528,256]{1,0:T(8,128)(2,1)}, bf16[528,256]{1,0:T(8,128)(2,1)}, u32[]{:S(2)}, u32[]{:S(2)}) collective-permute-start(bf16[528,256]{1,0:T(8,128)(2,1)} %slice_bitcast_fusion.3), channel_id=1, source_target_pairs={{0,8},{1,9},{2,10},{3,11},{4,0},{5,1},{6,2},{7,3},{8,12},{9,13},{1... | collective-permute-start | bytes 811016 | tf_op jit(solution)/shard_map/ppermute | solution.py:689
  32.8 9.2 %collective-permute-done.3.refs_1_ = bf16[2,528,256]{2,1,0:T(8,128)(2,1)S(1)} collective-permute-done((bf16[2,528,256]{2,1,0:T(8,128)(2,1)S(1)}, bf16[2,528,256]{2,1,0:T(8,128)(2,1)S(1)}, u32[]{:S(2)}, u32[]{:S(2)}) %collective-permute-start.3) | collective-permute-done | bytes 540704 | tf_op jit(solution)/shard_map/ppermute | solution.py:689
  43.5 1.5 collective-permute-start.4
  45.0 1.6 build_factors.5.refs_5_
  48.1 2.2 %collective-permute-start.10 = (bf16[2,528,256]{2,1,0:T(8,128)(2,1)S(1)}, bf16[2,528,256]{2,1,0:T(8,128)(2,1)}, u32[]{:S(2)}, u32[]{:S(2)}) collective-permute-start(bf16[2,528,256]{2,1,0:T(8,128)(2,1)S(1)} %build_factors.5.refs_5_), channel_id=1, source_target_pairs={{0,8},{1,9},{2,10},{3,11},{4,0},{5,1},{6,2},{7,3},{8,12},{9,13},{1... | collective-permute-start | bytes 1622024 | tf_op jit(solution)/shard_map/ppermute | solution.py:689
  51.9 2.8 %collective-permute-start.9 = (bf16[2,528,256]{2,1,0:T(8,128)(2,1)S(1)}, bf16[2,528,256]{2,1,0:T(8,128)(2,1)}, u32[]{:S(2)}, u32[]{:S(2)}) collective-permute-start(bf16[2,528,256]{2,1,0:T(8,128)(2,1)S(1)} %build_factors.5.refs_5_), channel_id=1, source_target_pairs={{0,4},{1,5},{2,6},{3,7},{4,12},{5,13},{6,14},{7,15},{8,0},{9,1},{1... | collective-permute-start | bytes 1622024 | tf_op jit(solution)/shard_map/ppermute | solution.py:689
  54.7 4.0 %slices_for.1 = (bf16[2,2,2,256,256]{4,3,2,1,0:T(8,128)(2,1)}, bf16[2,2,2,256,256]{4,3,2,1,0:T(8,128)(2,1)}, bf16[2,2,2,256,256]{4,3,2,1,0:T(8,128)(2,1)}) custom-call(s32[148]{0:T(256)} %bitcast.27, bf16[2,8,2,256,256]{4,3,2,1,0:T(8,128)(2,1)} %refs_12_.1, bf16[2,8,2,256,256]{4,3,2,1,0:T(8,128)(2,1)} %refs_12_.1, bf16[2,8,2,256,256]{4,3,2,1,0:T(8,128)(2,1)} %refs_12_.1), custom_call_target="tpu_custom_call" | custom-call | flops 1 | bytes 1 | tf_op jit(solution)/shard_map/slices_for/pallas_call | solution.py:242
  58.7 1.6 collective-permute-start.17
  60.3 4.4 %collective-permute-done.10.refs_7_ = bf16[2,528,256]{2,1,0:T(8,128)(2,1)} collective-permute-done((bf16[2,528,256]{2,1,0:T(8,128)(2,1)S(1)}, bf16[2,528,256]{2,1,0:T(8,128)(2,1)}, u32[]{:S(2)}, u32[]{:S(2)}) %collective-permute-start.10) | collective-permute-done | bytes 540704 | tf_op jit(solution)/shard_map/ppermute | solution.py:689
  65.6 1.9 collective-permute-start.11
  67.5 10.1 %collective-permute-done.9.refs_6_ = bf16[2,528,256]{2,1,0:T(8,128)(2,1)} collective-permute-done((bf16[2,528,256]{2,1,0:T(8,128)(2,1)S(1)}, bf16[2,528,256]{2,1,0:T(8,128)(2,1)}, u32[]{:S(2)}, u32[]{:S(2)}) %collective-permute-start.9) | collective-permute-done | bytes 540704 | tf_op jit(solution)/shard_map/ppermute | solution.py:689
  83.6 3.5 %build_factors.4 = (bf16[2,512,256]{2,1,0:T(8,128)(2,1)S(1)}, bf16[2,512,256]{2,1,0:T(8,128)(2,1)S(1)}) custom-call(s32[148]{0:T(256)S(1)} %bitcast.30, bf16[8,2,32,2048]{3,2,1,0:T(8,128)(2,1)S(1)} %copy-done.1, bf16[64,2048]{1,0:T(8,128)(2,1)} %collective-permute-done.5.refs_1_, bf16[64,2048]{1,0:T(8,128)(2,1)S(1)} %copy-done.45, ...), custom_call_target="tpu_custom_call" | custom-call | flops 1 | bytes 1 | tf_op jit(solution)/shard_map/build_factors/pallas_call | solution.py:161
  87.1 7.1 %collective-permute-start.12 = (bf16[2,512,256]{2,1,0:T(8,128)(2,1)S(1)}, bf16[2,512,256]{2,1,0:T(8,128)(2,1)S(1)}, u32[]{:S(2)}, u32[]{:S(2)}) collective-permute-start(bf16[2,512,256]{2,1,0:T(8,128)(2,1)S(1)} %get-tuple-element.86.refs_0_), channel_id=1, source_target_pairs={{0,4},{1,5},{2,6},{3,7},{4,12},{5,13},{6,14},{7,15},{8,0},{9,1},{1... | collective-permute-start | bytes 1572872 | tf_op jit(solution)/shard_map/ppermute | solution.py:689
  95.3 4.6 %unit_work.5 = (bf16[2,2,256,256]{3,2,1,0:T(8,128)(2,1)S(1)}, f32[1,512]{1,0:T(1,128)S(1)}, f32[2,512,128]{2,1,0:T(8,128)S(1)}) custom-call(s32[148]{0:T(256)S(1)} %bitcast.31, bf16[2,528,256]{2,1,0:T(8,128)(2,1)S(1)} %build_factors.3.refs_0_, bf16[2,528,256]{2,1,0:T(8,128)(2,1)S(1)} %copy-done.7, bf16[2,528,256]{2,1,0:T(8,128)(2,1)S(1)} %copy-done.5, ...), custom_call_target="tpu_custom_call" | custom-call | flops 1 | bytes 1 | tf_op jit(solution)/shard_map/unit_work/pallas_call | solution.py:476
  99.9 4.3 %collective-permute-done.13.refs_10_ = bf16[2,2,2,256,256]{4,3,2,1,0:T(8,128)(2,1)S(1)} collective-permute-done((bf16[2,2,2,256,256]{4,3,2,1,0:T(8,128)(2,1)}, bf16[2,2,2,256,256]{4,3,2,1,0:T(8,128)(2,1)S(1)}, u32[]{:S(2)}, u32[]{:S(2)}) %collective-permute-start.13) | collective-permute-done | bytes 1048608 | tf_op jit(solution)/shard_map/ppermute | solution.py:689
  104.8 4.4 %unit_work.6 = (bf16[2,2,256,256]{3,2,1,0:T(8,128)(2,1)S(1)}, f32[1,512]{1,0:T(1,128)S(1)}) custom-call(s32[148]{0:T(256)S(1)} %bitcast.32, bf16[2,528,256]{2,1,0:T(8,128)(2,1)S(1)} %build_factors.3.refs_0_, bf16[2,528,256]{2,1,0:T(8,128)(2,1)S(1)} %copy-done.7, bf16[2,528,256]{2,1,0:T(8,128)(2,1)S(1)} %copy-done.5, ...), custom_call_target="tpu_custom_call" | custom-call | flops 1 | bytes 1 | tf_op jit(solution)/shard_map/unit_work/pallas_call | solution.py:476
  109.2 1.9 collective-permute-start.20
  111.1 17.9 %collective-permute-done.24.refs_7_ = bf16[2,512,256]{2,1,0:T(8,128)(2,1)S(1)} collective-permute-done((bf16[2,512,256]{2,1,0:T(8,128)(2,1)S(1)}, bf16[2,512,256]{2,1,0:T(8,128)(2,1)S(1)}, u32[]{:S(2)}, u32[]{:S(2)}) %collective-permute-start.24) | collective-permute-done | bytes 524320 | tf_op jit(solution)/shard_map/ppermute | solution.py:689
  129.1 1.1 collective-permute-start.19
  130.7 9.6 %collective-permute-done.23.refs_6_ = bf16[2,512,256]{2,1,0:T(8,128)(2,1)S(1)} collective-permute-done((bf16[2,512,256]{2,1,0:T(8,128)(2,1)S(1)}, bf16[2,512,256]{2,1,0:T(8,128)(2,1)S(1)}, u32[]{:S(2)}, u32[]{:S(2)}) %collective-permute-start.23) | collective-permute-done | bytes 524320 | tf_op jit(solution)/shard_map/ppermute | solution.py:689
  140.8 2.9 %collective-permute-start.22 = (bf16[512,256]{1,0:T(8,128)(2,1)S(1)}, bf16[512,256]{1,0:T(8,128)(2,1)S(1)}, u32[]{:S(2)}, u32[]{:S(2)}) collective-permute-start(bf16[512,256]{1,0:T(8,128)(2,1)S(1)} %slice_bitcast_fusion.6), channel_id=1, source_target_pairs={{0,8},{1,9},{2,10},{3,11},{4,0},{5,1},{6,2},{7,3},{8,12},{9,13},{1... | collective-permute-start | bytes 786440 | tf_op jit(solution)/shard_map/ppermute | solution.py:689
  143.6 2.3 %collective-permute-done.14.refs_3_ = bf16[512,256]{1,0:T(8,128)(2,1)S(1)} collective-permute-done((bf16[512,256]{1,0:T(8,128)(2,1)S(1)}, bf16[512,256]{1,0:T(8,128)(2,1)S(1)}, u32[]{:S(2)}, u32[]{:S(2)}) %collective-permute-start.14) | collective-permute-done | bytes 262176 | tf_op jit(solution)/shard_map/ppermute | solution.py:689
  145.9 2.5 %collective-permute-start.25 = (bf16[512,256]{1,0:T(8,128)(2,1)S(1)}, bf16[512,256]{1,0:T(8,128)(2,1)S(1)}, u32[]{:S(2)}, u32[]{:S(2)}) collective-permute-start(bf16[512,256]{1,0:T(8,128)(2,1)S(1)} %slice_bitcast_fusion.5), channel_id=1, source_target_pairs={{0,4},{1,5},{2,6},{3,7},{4,12},{5,13},{6,14},{7,15},{8,0},{9,1},{1... | collective-permute-start | bytes 786440 | tf_op jit(solution)/shard_map/ppermute | solution.py:689
  148.4 7.5 %unit_work.7 = (bf16[2,2,256,256]{3,2,1,0:T(8,128)(2,1)}, bf16[2,2,256,256]{3,2,1,0:T(8,128)(2,1)S(1)}, f32[1,512]{1,0:T(1,128)S(1)}) custom-call(s32[148]{0:T(256)S(1)} %bitcast.33, bf16[2,528,256]{2,1,0:T(8,128)(2,1)S(1)} %build_factors.3.refs_0_, bf16[2,528,256]{2,1,0:T(8,128)(2,1)S(1)} %copy-done.7, bf16[2,528,256]{2,1,0:T(8,128)(2,1)S(1)} %copy-done.5, ...), custom_call_target="tpu_custom_call" | custom-call | flops 1 | bytes 1 | tf_op jit(solution)/shard_map/unit_work/pallas_call | solution.py:476
  157.9 4.2 %collective-permute-done.25.refs_8_ = bf16[512,256]{1,0:T(8,128)(2,1)S(1)} collective-permute-done((bf16[512,256]{1,0:T(8,128)(2,1)S(1)}, bf16[512,256]{1,0:T(8,128)(2,1)S(1)}, u32[]{:S(2)}, u32[]{:S(2)}) %collective-permute-start.25) | collective-permute-done | bytes 262176 | tf_op jit(solution)/shard_map/ppermute | solution.py:689
  162.2 3.8 %unit_work.8 = (bf16[2,2,256,256]{3,2,1,0:T(8,128)(2,1)}, f32[1,512]{1,0:T(1,128)S(1)}) custom-call(s32[148]{0:T(256)S(1)} %bitcast.34, bf16[2,512,256]{2,1,0:T(8,128)(2,1)S(1)} %get-tuple-element.86.refs_0_, bf16[2,512,256]{2,1,0:T(8,128)(2,1)S(1)} %collective-permute-done.12.refs_1_, bf16[2,512,256]{2,1,0:T(8,128)(2,1)S(1)} %collective-permute-done.21.refs_2_, ...), custom_call_target="tpu_custom_call" | custom-call | flops 1 | bytes 1 | tf_op jit(solution)/shard_map/unit_work/pallas_call | solution.py:476
  166.0 1.2 collective-permute-start.27
  167.2 2.2 %copy-done.3 = bf16[2,8,2,256,256]{4,3,2,1,0:T(8,128)(2,1)S(1)} copy-done((bf16[2,8,2,256,256]{4,3,2,1,0:T(8,128)(2,1)S(1)}, bf16[2,8,2,256,256]{4,3,2,1,0:T(8,128)(2,1)}, u32[]{:S(2)}) %copy-start.3) | copy-done | bytes 4194328
  169.4 1.0 copy-done.13
  171.5 1.0 copy-done.17
  178.5 7.8 %unit_work.9 = (bf16[2,2,256,256]{3,2,1,0:T(8,128)(2,1)S(1)}, bf16[2,2,256,256]{3,2,1,0:T(8,128)(2,1)S(1)}, bf16[2,2,256,256]{3,2,1,0:T(8,128)(2,1)S(1)}, f32[1,512]{1,0:T(1,128)S(1)}) custom-call(s32[148]{0:T(256)S(1)} %bitcast.35, bf16[2,512,256]{2,1,0:T(8,128)(2,1)S(1)} %copy-done.21, bf16[2,512,256]{2,1,0:T(8,128)(2,1)S(1)} %copy-done.13, ...), custom_call_target="tpu_custom_call" | custom-call | flops 1 | bytes 1 | tf_op jit(solution)/shard_map/unit_work/pallas_call | solution.py:476
  186.3 2.1 collective-permute-start.33
  189.5 5.4 %collective-permute-start.31 = (f32[2,128]{1,0:T(2,128)S(1)}, f32[2,128]{1,0:T(2,128)S(1)}, u32[]{:S(2)}, u32[]{:S(2)}) collective-permute-start(f32[2,128]{1,0:T(2,128)S(1)} %get-tuple-element.102), channel_id=1, source_target_pairs={{0,12},{1,13},{2,14},{3,15},{4,8},{5,9},{6,10},{7,11},{8,4},{9,5},... | collective-permute-start | bytes 3080 | tf_op jit(solution)/shard_map/ppermute | solution.py:689
  194.8 1.9 collective-permute-start.32
  196.9 4.7 %put_residuals.3.refs_2_ = bf16[2,8,2,256,256]{4,3,2,1,0:T(8,128)(2,1)} custom-call(s32[148]{0:T(256)S(1)} %bitcast.36, bf16[2,2,256,256]{3,2,1,0:T(8,128)(2,1)S(1)} %copy-done.39, bf16[2,2,256,256]{3,2,1,0:T(8,128)(2,1)S(1)} %copy-done.37, bf16[2,2,256,256]{3,2,1,0:T(8,128)(2,1)} %collective-permute-done.30.refs_2_, bf16[2,2,256,256]{3,2,1,0:T(8,128)(2,1)S(1)} %copy-done.41), custom_call_target="tpu_custom_call" | custom-call | flops 1 | bytes 1 | tf_op jit(solution)/shard_map/put_residuals/pallas_call | solution.py:516
  201.7 1.8 collective-permute-start.36
  203.5 2.1 %put_residuals.4.refs_2_ = bf16[2,8,2,256,256]{4,3,2,1,0:T(8,128)(2,1)} custom-call(s32[148]{0:T(256)S(1)} %bitcast.37, bf16[2,2,256,256]{3,2,1,0:T(8,128)(2,1)S(1)} %collective-permute-done.29.refs_0_, bf16[2,2,256,256]{3,2,1,0:T(8,128)(2,1)S(1)} %get-tuple-element.97.refs_1_, ...), custom_call_target="tpu_custom_call", output_to_operand_aliasing={{}: (3, {})} | custom-call | flops 1 | bytes 1 | tf_op jit(solution)/shard_map/put_residuals/pallas_call | solution.py:516
  205.7 3.2 %put_residuals.5 = bf16[2,8,2,256,256]{4,3,2,1,0:T(8,128)(2,1)} custom-call(s32[148]{0:T(256)S(1)} %bitcast.38, bf16[2,2,256,256]{3,2,1,0:T(8,128)(2,1)} %collective-permute-done.27.refs_0_, bf16[2,2,256,256]{3,2,1,0:T(8,128)(2,1)S(1)} %collective-permute-done.28.refs_1_, ...), custom_call_target="tpu_custom_call", output_to_operand_aliasing={{}: (3, {})} | custom-call | flops 1 | bytes 1 | tf_op jit(solution)/shard_map/put_residuals/pallas_call | solution.py:516
  (178 shorter events, 29.3 us)
Async XLA Ops:
  5.7 1.9 collective-permute-start
  12.0 17.4 %collective-permute-start.1 = (bf16[2,528,256]{2,1,0:T(8,128)(2,1)S(1)}, bf16[2,528,256]{2,1,0:T(8,128)(2,1)S(1)}, u32[]{:S(2)}, u32[]{:S(2)}) collective-permute-start(bf16[2,528,256]{2,1,0:T(8,128)(2,1)S(1)} %build_factors.3.refs_0_), channel_id=1, source_target_pairs={{0,8},{1,9},{2,10},{3,11},{4,0},{5,1},{6,2},{7,3},{8,12},{9,13},{1... | collective-permute-start | bytes 1622024 | tf_op jit(solution)/shard_map/ppermute | solution.py:689
  18.6 10.8 %collective-permute-start.7 = (bf16[80,2048]{1,0:T(8,128)(2,1)}, bf16[80,2048]{1,0:T(8,128)(2,1)S(1)}, u32[]{:S(2)}, u32[]{:S(2)}) collective-permute-start(bf16[80,2048]{1,0:T(8,128)(2,1)} %get-tuple-element.61), channel_id=1, source_target_pairs={{0,2},{1,3},{2,0},{3,1},{4,6},{5,7},{6,4},{7,5},{8,10},{9,11},{10,... | collective-permute-start | bytes 983048 | tf_op jit(solution)/shard_map/ppermute | solution.py:689
  20.1 22.0 %collective-permute-start.3 = (bf16[2,528,256]{2,1,0:T(8,128)(2,1)S(1)}, bf16[2,528,256]{2,1,0:T(8,128)(2,1)S(1)}, u32[]{:S(2)}, u32[]{:S(2)}) collective-permute-start(bf16[2,528,256]{2,1,0:T(8,128)(2,1)S(1)} %build_factors.3.refs_0_), channel_id=1, source_target_pairs={{0,4},{1,5},{2,6},{3,7},{4,12},{5,13},{6,14},{7,15},{8,0},{9,1},{1... | collective-permute-start | bytes 1622024 | tf_op jit(solution)/shard_map/ppermute | solution.py:689
  22.8 24.6 %collective-permute-start.6 = (bf16[64,2048]{1,0:T(8,128)(2,1)}, bf16[64,2048]{1,0:T(8,128)(2,1)S(1)}, u32[]{:S(2)}, u32[]{:S(2)}) collective-permute-start(bf16[64,2048]{1,0:T(8,128)(2,1)} %get-tuple-element.60), channel_id=1, source_target_pairs={{0,3},{1,2},{2,1},{3,0},{4,7},{5,6},{6,5},{7,4},{8,11},{9,10},{10,... | collective-permute-start | bytes 786440 | tf_op jit(solution)/shard_map/ppermute | solution.py:689
  29.4 15.6 %collective-permute-start.8 = (bf16[80,2048]{1,0:T(8,128)(2,1)S(1)}, bf16[80,2048]{1,0:T(8,128)(2,1)S(1)}, u32[]{:S(2)}, u32[]{:S(2)}) collective-permute-start(bf16[80,2048]{1,0:T(8,128)(2,1)S(1)} %copy-done.56), channel_id=1, source_target_pairs={{0,3},{1,2},{2,1},{3,0},{4,7},{5,6},{6,5},{7,4},{8,11},{9,10},{10,... | collective-permute-start | bytes 983048 | tf_op jit(solution)/shard_map/ppermute | solution.py:689
  30.2 28.5 %collective-permute-start.2 = (bf16[528,256]{1,0:T(8,128)(2,1)}, bf16[528,256]{1,0:T(8,128)(2,1)}, u32[]{:S(2)}, u32[]{:S(2)}) collective-permute-start(bf16[528,256]{1,0:T(8,128)(2,1)} %slice_bitcast_fusion.3), channel_id=1, source_target_pairs={{0,8},{1,9},{2,10},{3,11},{4,0},{5,1},{6,2},{7,3},{8,12},{9,13},{1... | collective-permute-start | bytes 811016 | tf_op jit(solution)/shard_map/ppermute | solution.py:689
  42.8 15.9 %collective-permute-start.15 = (bf16[528,256]{1,0:T(8,128)(2,1)}, bf16[528,256]{1,0:T(8,128)(2,1)}, u32[]{:S(2)}, u32[]{:S(2)}) collective-permute-start(bf16[528,256]{1,0:T(8,128)(2,1)} %slice_bitcast_fusion.1), channel_id=1, source_target_pairs={{0,4},{1,5},{2,6},{3,7},{4,12},{5,13},{6,14},{7,15},{8,0},{9,1},{1... | collective-permute-start | bytes 811016 | tf_op jit(solution)/shard_map/ppermute | solution.py:689
  43.5 7.7 %collective-permute-start.4 = (bf16[64,2048]{1,0:T(8,128)(2,1)}, bf16[64,2048]{1,0:T(8,128)(2,1)S(1)}, u32[]{:S(2)}, u32[]{:S(2)}) collective-permute-start(bf16[64,2048]{1,0:T(8,128)(2,1)} %get-tuple-element.56), channel_id=1, source_target_pairs={{0,2},{1,3},{2,0},{3,1},{4,6},{5,7},{6,4},{7,5},{8,10},{9,11},{10,... | collective-permute-start | bytes 786440 | tf_op jit(solution)/shard_map/ppermute | solution.py:689
  45.0 13.6 %collective-permute-start.5 = (bf16[64,2048]{1,0:T(8,128)(2,1)}, bf16[64,2048]{1,0:T(8,128)(2,1)}, u32[]{:S(2)}, u32[]{:S(2)}) collective-permute-start(bf16[64,2048]{1,0:T(8,128)(2,1)} %get-tuple-element.59), channel_id=1, source_target_pairs={{0,1},{1,0},{2,3},{3,2},{4,5},{5,4},{6,7},{7,6},{8,9},{9,8},{10,11... | collective-permute-start | bytes 786440 | tf_op jit(solution)/shard_map/ppermute | solution.py:689
  47.4 31.3 %copy-start.54 = (f32[256]{0:T(256)S(1)}, f32[256]{0:T(256)}, u32[]{:S(2)}) copy-start(f32[256]{0:T(256)} %broadcast_in_dim.34) | copy-start | bytes 3076
  48.1 16.5 %collective-permute-start.10 = (bf16[2,528,256]{2,1,0:T(8,128)(2,1)S(1)}, bf16[2,528,256]{2,1,0:T(8,128)(2,1)}, u32[]{:S(2)}, u32[]{:S(2)}) collective-permute-start(bf16[2,528,256]{2,1,0:T(8,128)(2,1)S(1)} %build_factors.5.refs_5_), channel_id=1, source_target_pairs={{0,8},{1,9},{2,10},{3,11},{4,0},{5,1},{6,2},{7,3},{8,12},{9,13},{1... | collective-permute-start | bytes 1622024 | tf_op jit(solution)/shard_map/ppermute | solution.py:689
  51.9 25.7 %collective-permute-start.9 = (bf16[2,528,256]{2,1,0:T(8,128)(2,1)S(1)}, bf16[2,528,256]{2,1,0:T(8,128)(2,1)}, u32[]{:S(2)}, u32[]{:S(2)}) collective-permute-start(bf16[2,528,256]{2,1,0:T(8,128)(2,1)S(1)} %build_factors.5.refs_5_), channel_id=1, source_target_pairs={{0,4},{1,5},{2,6},{3,7},{4,12},{5,13},{6,14},{7,15},{8,0},{9,1},{1... | collective-permute-start | bytes 1622024 | tf_op jit(solution)/shard_map/ppermute | solution.py:689
  54.7 40.6 %copy-start.55 = (s32[8,2048]{1,0:T(8,128)S(1)}, s32[8,2048]{1,0:T(8,128)}, u32[]{:S(2)}) copy-start(s32[8,2048]{1,0:T(8,128)} %param.14) | copy-start | bytes 196612
  58.6 36.6 %copy-start.5 = (bf16[2,528,256]{2,1,0:T(8,128)(2,1)S(1)}, bf16[2,528,256]{2,1,0:T(8,128)(2,1)}, u32[]{:S(2)}) copy-start(bf16[2,528,256]{2,1,0:T(8,128)(2,1)} %copy-done.4) | copy-start | bytes 1622020
  58.7 36.6 %copy-start.7 = (bf16[2,528,256]{2,1,0:T(8,128)(2,1)S(1)}, bf16[2,528,256]{2,1,0:T(8,128)(2,1)}, u32[]{:S(2)}) copy-start(bf16[2,528,256]{2,1,0:T(8,128)(2,1)} %copy-done.6) | copy-start | bytes 1622020
  58.7 35.6 %collective-permute-start.17 = (bf16[2,2,2,256,256]{4,3,2,1,0:T(8,128)(2,1)}, bf16[2,2,2,256,256]{4,3,2,1,0:T(8,128)(2,1)S(1)}, u32[]{:S(2)}, u32[]{:S(2)}) collective-permute-start(bf16[2,2,2,256,256]{4,3,2,1,0:T(8,128)(2,1)} %get-tuple-element.74), channel_id=1, source_target_pairs={{0,2},{1,3},{2,0},{3,1},{4,6},{5,7},{6,4},{7,5},{8,10},{9,11},{10,... | collective-permute-start | bytes 3145736 | tf_op jit(solution)/shard_map/ppermute | solution.py:689
  60.3 43.9 %collective-permute-start.13 = (bf16[2,2,2,256,256]{4,3,2,1,0:T(8,128)(2,1)}, bf16[2,2,2,256,256]{4,3,2,1,0:T(8,128)(2,1)S(1)}, u32[]{:S(2)}, u32[]{:S(2)}) collective-permute-start(bf16[2,2,2,256,256]{4,3,2,1,0:T(8,128)(2,1)} %get-tuple-element.70), channel_id=1, source_target_pairs={{0,3},{1,2},{2,1},{3,0},{4,7},{5,6},{6,5},{7,4},{8,11},{9,10},{10,... | collective-permute-start | bytes 3145736 | tf_op jit(solution)/shard_map/ppermute | solution.py:689
  65.6 21.4 %collective-permute-start.11 = (bf16[528,256]{1,0:T(8,128)(2,1)S(1)}, bf16[528,256]{1,0:T(8,128)(2,1)S(1)}, u32[]{:S(2)}, u32[]{:S(2)}) collective-permute-start(bf16[528,256]{1,0:T(8,128)(2,1)S(1)} %slice_bitcast_fusion.2), channel_id=1, source_target_pairs={{0,8},{1,9},{2,10},{3,11},{4,0},{5,1},{6,2},{7,3},{8,12},{9,13},{1... | collective-permute-start | bytes 811016 | tf_op jit(solution)/shard_map/ppermute | solution.py:689
  78.6 15.6 %collective-permute-start.16 = (bf16[528,256]{1,0:T(8,128)(2,1)S(1)}, bf16[528,256]{1,0:T(8,128)(2,1)S(1)}, u32[]{:S(2)}, u32[]{:S(2)}) collective-permute-start(bf16[528,256]{1,0:T(8,128)(2,1)S(1)} %slice_bitcast_fusion), channel_id=1, source_target_pairs={{0,4},{1,5},{2,6},{3,7},{4,12},{5,13},{6,14},{7,15},{8,0},{9,1},{1... | collective-permute-start | bytes 811016 | tf_op jit(solution)/shard_map/ppermute | solution.py:689
  87.0 75.1 %copy-start.20 = (bf16[2,512,256]{2,1,0:T(8,128)(2,1)}, bf16[2,512,256]{2,1,0:T(8,128)(2,1)S(1)}, u32[]{:S(2)}) copy-start(bf16[2,512,256]{2,1,0:T(8,128)(2,1)S(1)} %get-tuple-element.86.refs_0_) | copy-start | bytes 1572868
  87.1 75.1 %copy-start.22 = (bf16[2,512,256]{2,1,0:T(8,128)(2,1)}, bf16[2,512,256]{2,1,0:T(8,128)(2,1)S(1)}, u32[]{:S(2)}) copy-start(bf16[2,512,256]{2,1,0:T(8,128)(2,1)S(1)} %get-tuple-element.89.refs_5_) | copy-start | bytes 1572868
  87.1 22.1 %collective-permute-start.12 = (bf16[2,512,256]{2,1,0:T(8,128)(2,1)S(1)}, bf16[2,512,256]{2,1,0:T(8,128)(2,1)S(1)}, u32[]{:S(2)}, u32[]{:S(2)}) collective-permute-start(bf16[2,512,256]{2,1,0:T(8,128)(2,1)S(1)} %get-tuple-element.86.refs_0_), channel_id=1, source_target_pairs={{0,4},{1,5},{2,6},{3,7},{4,12},{5,13},{6,14},{7,15},{8,0},{9,1},{1... | collective-permute-start | bytes 1572872 | tf_op jit(solution)/shard_map/ppermute | solution.py:689
  94.2 46.5 %collective-permute-start.18 = (bf16[2,2,2,256,256]{4,3,2,1,0:T(8,128)(2,1)}, bf16[2,2,2,256,256]{4,3,2,1,0:T(8,128)(2,1)S(1)}, u32[]{:S(2)}, u32[]{:S(2)}) collective-permute-start(bf16[2,2,2,256,256]{4,3,2,1,0:T(8,128)(2,1)} %get-tuple-element.81), channel_id=1, source_target_pairs={{0,1},{1,0},{2,3},{3,2},{4,5},{5,4},{6,7},{7,6},{8,9},{9,8},{10,11... | collective-permute-start | bytes 3145736 | tf_op jit(solution)/shard_map/ppermute | solution.py:689
  94.2 36.0 %collective-permute-start.21 = (bf16[2,512,256]{2,1,0:T(8,128)(2,1)S(1)}, bf16[2,512,256]{2,1,0:T(8,128)(2,1)S(1)}, u32[]{:S(2)}, u32[]{:S(2)}) collective-permute-start(bf16[2,512,256]{2,1,0:T(8,128)(2,1)S(1)} %get-tuple-element.86.refs_0_), channel_id=1, source_target_pairs={{0,8},{1,9},{2,10},{3,11},{4,0},{5,1},{6,2},{7,3},{8,12},{9,13},{1... | collective-permute-start | bytes 1572872 | tf_op jit(solution)/shard_map/ppermute | solution.py:689
  94.2 34.8 %collective-permute-start.24 = (bf16[2,512,256]{2,1,0:T(8,128)(2,1)S(1)}, bf16[2,512,256]{2,1,0:T(8,128)(2,1)S(1)}, u32[]{:S(2)}, u32[]{:S(2)}) collective-permute-start(bf16[2,512,256]{2,1,0:T(8,128)(2,1)S(1)} %get-tuple-element.89.refs_5_), channel_id=1, source_target_pairs={{0,8},{1,9},{2,10},{3,11},{4,0},{5,1},{6,2},{7,3},{8,12},{9,13},{1... | collective-permute-start | bytes 1572872 | tf_op jit(solution)/shard_map/ppermute | solution.py:689
  99.9 48.5 %copy-start.2 = (bf16[2,8,2,256,256]{4,3,2,1,0:T(8,128)(2,1)S(1)}, bf16[2,8,2,256,256]{4,3,2,1,0:T(8,128)(2,1)}, u32[]{:S(2)}) copy-start(bf16[2,8,2,256,256]{4,3,2,1,0:T(8,128)(2,1)} %refs_12_.1) | copy-start | bytes 12582916
  104.2 51.7 %copy-start.8 = (bf16[2,2,2,256,256]{4,3,2,1,0:T(8,128)(2,1)}, bf16[2,2,2,256,256]{4,3,2,1,0:T(8,128)(2,1)S(1)}, u32[]{:S(2)}) copy-start(bf16[2,2,2,256,256]{4,3,2,1,0:T(8,128)(2,1)S(1)} %collective-permute-done.13.refs_10_) | copy-start | bytes 3145732
  104.2 36.1 %collective-permute-start.23 = (bf16[2,512,256]{2,1,0:T(8,128)(2,1)S(1)}, bf16[2,512,256]{2,1,0:T(8,128)(2,1)S(1)}, u32[]{:S(2)}, u32[]{:S(2)}) collective-permute-start(bf16[2,512,256]{2,1,0:T(8,128)(2,1)S(1)} %get-tuple-element.89.refs_5_), channel_id=1, source_target_pairs={{0,4},{1,5},{2,6},{3,7},{4,12},{5,13},{6,14},{7,15},{8,0},{9,1},{1... | collective-permute-start | bytes 1572872 | tf_op jit(solution)/shard_map/ppermute | solution.py:689
  109.2 52.9 %copy-start.12 = (bf16[2,512,256]{2,1,0:T(8,128)(2,1)}, bf16[2,512,256]{2,1,0:T(8,128)(2,1)S(1)}, u32[]{:S(2)}) copy-start(bf16[2,512,256]{2,1,0:T(8,128)(2,1)S(1)} %collective-permute-done.12.refs_1_) | copy-start | bytes 1572868
  109.2 47.5 %collective-permute-start.20 = (bf16[2,2,256,256]{3,2,1,0:T(8,128)(2,1)S(1)}, bf16[2,2,256,256]{3,2,1,0:T(8,128)(2,1)S(1)}, u32[]{:S(2)}, u32[]{:S(2)}) collective-permute-start(bf16[2,2,256,256]{3,2,1,0:T(8,128)(2,1)S(1)} %get-tuple-element.84), channel_id=1, source_target_pairs={{0,3},{1,2},{2,1},{3,0},{4,7},{5,6},{6,5},{7,4},{8,11},{9,10},{10,... | collective-permute-start | bytes 1572872 | tf_op jit(solution)/shard_map/ppermute | solution.py:689
  129.1 33.1 %copy-start.16 = (bf16[2,512,256]{2,1,0:T(8,128)(2,1)}, bf16[2,512,256]{2,1,0:T(8,128)(2,1)S(1)}, u32[]{:S(2)}) copy-start(bf16[2,512,256]{2,1,0:T(8,128)(2,1)S(1)} %collective-permute-done.24.refs_7_) | copy-start | bytes 1572868
  129.1 28.4 %collective-permute-start.19 = (bf16[2,2,256,256]{3,2,1,0:T(8,128)(2,1)S(1)}, bf16[2,2,256,256]{3,2,1,0:T(8,128)(2,1)S(1)}, u32[]{:S(2)}, u32[]{:S(2)}) collective-permute-start(bf16[2,2,256,256]{3,2,1,0:T(8,128)(2,1)S(1)} %get-tuple-element.83), channel_id=1, source_target_pairs={{0,2},{1,3},{2,0},{3,1},{4,6},{5,7},{6,4},{7,5},{8,10},{9,11},{10,... | collective-permute-start | bytes 1572872 | tf_op jit(solution)/shard_map/ppermute | solution.py:689
  130.2 31.9 %copy-start.14 = (bf16[2,512,256]{2,1,0:T(8,128)(2,1)}, bf16[2,512,256]{2,1,0:T(8,128)(2,1)S(1)}, u32[]{:S(2)}) copy-start(bf16[2,512,256]{2,1,0:T(8,128)(2,1)S(1)} %collective-permute-done.21.refs_2_) | copy-start | bytes 1572868
  130.2 15.7 %collective-permute-start.14 = (bf16[512,256]{1,0:T(8,128)(2,1)S(1)}, bf16[512,256]{1,0:T(8,128)(2,1)S(1)}, u32[]{:S(2)}, u32[]{:S(2)}) collective-permute-start(bf16[512,256]{1,0:T(8,128)(2,1)S(1)} %slice_bitcast_fusion.7), channel_id=1, source_target_pairs={{0,4},{1,5},{2,6},{3,7},{4,12},{5,13},{6,14},{7,15},{8,0},{9,1},{1... | collective-permute-start | bytes 786440 | tf_op jit(solution)/shard_map/ppermute | solution.py:689
  140.3 17.2 %collective-permute-start.26 = (bf16[512,256]{1,0:T(8,128)(2,1)S(1)}, bf16[512,256]{1,0:T(8,128)(2,1)S(1)}, u32[]{:S(2)}, u32[]{:S(2)}) collective-permute-start(bf16[512,256]{1,0:T(8,128)(2,1)S(1)} %slice_bitcast_fusion.4), channel_id=1, source_target_pairs={{0,8},{1,9},{2,10},{3,11},{4,0},{5,1},{6,2},{7,3},{8,12},{9,13},{1... | collective-permute-start | bytes 786440 | tf_op jit(solution)/shard_map/ppermute | solution.py:689
  140.8 17.2 %collective-permute-start.22 = (bf16[512,256]{1,0:T(8,128)(2,1)S(1)}, bf16[512,256]{1,0:T(8,128)(2,1)S(1)}, u32[]{:S(2)}, u32[]{:S(2)}) collective-permute-start(bf16[512,256]{1,0:T(8,128)(2,1)S(1)} %slice_bitcast_fusion.6), channel_id=1, source_target_pairs={{0,8},{1,9},{2,10},{3,11},{4,0},{5,1},{6,2},{7,3},{8,12},{9,13},{1... | collective-permute-start | bytes 786440 | tf_op jit(solution)/shard_map/ppermute | solution.py:689
  145.9 16.2 %collective-permute-start.25 = (bf16[512,256]{1,0:T(8,128)(2,1)S(1)}, bf16[512,256]{1,0:T(8,128)(2,1)S(1)}, u32[]{:S(2)}, u32[]{:S(2)}) collective-permute-start(bf16[512,256]{1,0:T(8,128)(2,1)S(1)} %slice_bitcast_fusion.5), channel_id=1, source_target_pairs={{0,4},{1,5},{2,6},{3,7},{4,12},{5,13},{6,14},{7,15},{8,0},{9,1},{1... | collective-permute-start | bytes 786440 | tf_op jit(solution)/shard_map/ppermute | solution.py:689
  157.5 32.0 %collective-permute-start.30 = (bf16[2,2,256,256]{3,2,1,0:T(8,128)(2,1)}, bf16[2,2,256,256]{3,2,1,0:T(8,128)(2,1)}, u32[]{:S(2)}, u32[]{:S(2)}) collective-permute-start(bf16[2,2,256,256]{3,2,1,0:T(8,128)(2,1)} %get-tuple-element.99), channel_id=1, source_target_pairs={{0,1},{1,0},{2,3},{3,2},{4,5},{5,4},{6,7},{7,6},{8,9},{9,8},{10,11... | collective-permute-start | bytes 1572872 | tf_op jit(solution)/shard_map/ppermute | solution.py:689
  166.0 28.9 %collective-permute-start.27 = (bf16[2,2,256,256]{3,2,1,0:T(8,128)(2,1)}, bf16[2,2,256,256]{3,2,1,0:T(8,128)(2,1)}, u32[]{:S(2)}, u32[]{:S(2)}) collective-permute-start(bf16[2,2,256,256]{3,2,1,0:T(8,128)(2,1)} %get-tuple-element.91), channel_id=1, source_target_pairs={{0,2},{1,3},{2,0},{3,1},{4,6},{5,7},{6,4},{7,5},{8,10},{9,11},{10,... | collective-permute-start | bytes 1572872 | tf_op jit(solution)/shard_map/ppermute | solution.py:689
  186.3 15.2 %collective-permute-start.33 = (f32[2,128]{1,0:T(2,128)S(1)}, f32[2,128]{1,0:T(2,128)S(1)}, u32[]{:S(2)}, u32[]{:S(2)}) collective-permute-start(f32[2,128]{1,0:T(2,128)S(1)} %get-tuple-element.107), channel_id=1, source_target_pairs={{0,4},{1,5},{2,6},{3,7},{4,12},{5,13},{6,14},{7,15},{8,0},{9,1},{1... | collective-permute-start | bytes 3080 | tf_op jit(solution)/shard_map/ppermute | solution.py:689
  188.4 15.1 %collective-permute-start.29 = (bf16[2,2,256,256]{3,2,1,0:T(8,128)(2,1)S(1)}, bf16[2,2,256,256]{3,2,1,0:T(8,128)(2,1)S(1)}, u32[]{:S(2)}, u32[]{:S(2)}) collective-permute-start(bf16[2,2,256,256]{3,2,1,0:T(8,128)(2,1)S(1)} %get-tuple-element.96), channel_id=1, source_target_pairs={{0,1},{1,0},{2,3},{3,2},{4,5},{5,4},{6,7},{7,6},{8,9},{9,8},{10,11... | collective-permute-start | bytes 1572872 | tf_op jit(solution)/shard_map/ppermute | solution.py:689
  188.4 17.2 %collective-permute-start.28 = (bf16[2,2,256,256]{3,2,1,0:T(8,128)(2,1)S(1)}, bf16[2,2,256,256]{3,2,1,0:T(8,128)(2,1)S(1)}, u32[]{:S(2)}, u32[]{:S(2)}) collective-permute-start(bf16[2,2,256,256]{3,2,1,0:T(8,128)(2,1)S(1)} %get-tuple-element.95), channel_id=1, source_target_pairs={{0,3},{1,2},{2,1},{3,0},{4,7},{5,6},{6,5},{7,4},{8,11},{9,10},{10,... | collective-permute-start | bytes 1572872 | tf_op jit(solution)/shard_map/ppermute | solution.py:689
  189.5 12.1 %collective-permute-start.31 = (f32[2,128]{1,0:T(2,128)S(1)}, f32[2,128]{1,0:T(2,128)S(1)}, u32[]{:S(2)}, u32[]{:S(2)}) collective-permute-start(f32[2,128]{1,0:T(2,128)S(1)} %get-tuple-element.102), channel_id=1, source_target_pairs={{0,12},{1,13},{2,14},{3,15},{4,8},{5,9},{6,10},{7,11},{8,4},{9,5},... | collective-permute-start | bytes 3080 | tf_op jit(solution)/shard_map/ppermute | solution.py:689
  194.8 6.7 %collective-permute-start.32 = (f32[2,128]{1,0:T(2,128)S(1)}, f32[2,128]{1,0:T(2,128)S(1)}, u32[]{:S(2)}, u32[]{:S(2)}) collective-permute-start(f32[2,128]{1,0:T(2,128)S(1)} %get-tuple-element.103), channel_id=1, source_target_pairs={{0,8},{1,9},{2,10},{3,11},{4,0},{5,1},{6,2},{7,3},{8,12},{9,13},{1... | collective-permute-start | bytes 3080 | tf_op jit(solution)/shard_map/ppermute | solution.py:689
  201.6 7.2 %collective-permute-start.34 = (f32[2,32]{1,0:T(2,128)S(1)}, f32[2,32]{1,0:T(2,128)S(1)}, u32[]{:S(2)}, u32[]{:S(2)}) collective-permute-start(f32[2,32]{1,0:T(2,128)S(1)} %get-tuple-element.104), channel_id=1, source_target_pairs={{0,1},{1,0},{2,3},{3,2},{4,5},{5,4},{6,7},{7,6},{8,9},{9,8},{10,11... | collective-permute-start | bytes 776 | tf_op jit(solution)/shard_map/ppermute | solution.py:689
  201.7 7.2 %collective-permute-start.35 = (f32[2,32]{1,0:T(2,128)S(1)}, f32[2,32]{1,0:T(2,128)S(1)}, u32[]{:S(2)}, u32[]{:S(2)}) collective-permute-start(f32[2,32]{1,0:T(2,128)S(1)} %get-tuple-element.105), channel_id=1, source_target_pairs={{0,2},{1,3},{2,0},{3,1},{4,6},{5,7},{6,4},{7,5},{8,10},{9,11},{10,... | collective-permute-start | bytes 776 | tf_op jit(solution)/shard_map/ppermute | solution.py:689
  201.7 7.1 %collective-permute-start.36 = (f32[2,32]{1,0:T(2,128)S(1)}, f32[2,32]{1,0:T(2,128)S(1)}, u32[]{:S(2)}, u32[]{:S(2)}) collective-permute-start(f32[2,32]{1,0:T(2,128)S(1)} %get-tuple-element.110), channel_id=1, source_target_pairs={{0,3},{1,2},{2,1},{3,0},{4,7},{5,6},{6,5},{7,4},{8,11},{9,10},{10,... | collective-permute-start | bytes 776 | tf_op jit(solution)/shard_map/ppermute | solution.py:689
  (46 other events, 370.4 us)

commit v14 on v10

--- a/solution.py
+++ b/solution.py
@@ -494,17 +494,17 @@
     )(*operands)
 
 
-def put_kernel(sources, tab_ref, *refs):
+def put_kernel(count, tab_ref, *refs):
     out_ref = refs[-1]
-    for step, (which, row) in enumerate(sources):
+    for step in range(count):
 
         @pl.when(pl.program_id(0) == step)
-        def _(which=which, row=row):
-            out_ref[0, 0] = refs[which][...] if row is None else refs[which][row]
-
-
-def put_residuals(sources, arrays, offset, table, shape, residual):
-    span = shape[-1]
+        def _(step=step):
+            out_ref[:, 0] = refs[step][...]
+
+
+def put_residuals(arrays, offset, stride, table, shape, residual):
+    units_dev, span = shape[0], shape[-1]
     whole = pl.BlockSpec(memory_space=pltpu.VMEM)
     operands = [table, *arrays]
     in_specs = [whole] * len(arrays)
@@ -514,14 +514,14 @@
         operands.append(residual)
         in_specs.append(pl.BlockSpec(memory_space=pl.ANY))
     return pl.pallas_call(
-        functools.partial(put_kernel, sources),
+        functools.partial(put_kernel, len(arrays)),
         grid_spec=pltpu.PrefetchScalarGridSpec(
             num_scalar_prefetch=1,
-            grid=(len(sources),),
+            grid=(len(arrays),),
             in_specs=in_specs,
             out_specs=pl.BlockSpec(
-                (1, 1, 2, span, span),
-                lambda n, tab: (tab[offset + 2 * n], tab[offset + 2 * n + 1], 0, 0, 0),
+                (units_dev, 1, 2, span, span),
+                lambda n, tab: (0, tab[offset + stride * n], 0, 0, 0),
             ),
         ),
         out_shape=jax.ShapeDtypeStruct(shape, jnp.bfloat16),
@@ -569,11 +569,10 @@
             return rows
 
         def targets(index):
-            rows = np.zeros((count, len(self.order), units_dev, 2), np.int32)
+            rows = np.zeros((count, len(self.order)), np.int32)
             for t in range(count):
                 for n, m in enumerate(self.order):
-                    for k in range(units_dev):
-                        rows[t, n, k] = k, (t % width ^ m) * share + index
+                    rows[t, n] = (t % width ^ m) * share + index
             return rows
 
         self.order = list(range(width // 2, width)) + list(range(width // 2 - 1, -1, -1))
@@ -586,7 +585,7 @@
         self.steps = ends[:2]
         self.targets = ends[2:]
         self.steps_per_home = units_dev * COLUMNS
-        self.targets_per_home = units_dev * 2
+        self.targets_per_home = 1
 
 
 def plain_program(visibility, beam, antenna_uvw, small, keep):
@@ -774,10 +773,10 @@
         return arrived, bright
 
     def put(step, homes, arrays, index, residual):
-        rows = [(n, k) for n in range(len(arrays)) for k in range(units_dev)]
-        offset = routes.targets[index] + homes * routes.targets_per_home
+        stride = routes.targets_per_home
+        offset = routes.targets[index] + homes * stride
         done[step] = put_residuals(
-            rows, arrays, offset, gated(step, table), visibility.shape, residual
+            arrays, offset, stride, gated(step, table), visibility.shape, residual
         )
         return done[step]
 

time: 202 us -> 200 us (0.990)
  Pallas kernels: 59.8 us -> 57.2 us
    pallas_call x3, Pallas kernels: 9.1 us -> 6.77 us  [put_residuals(): pl.pallas_call(functools.partial(put_kernel, len(arrays)), grid_spec=pltp...]
  transfers between devices with their start and end apart: 37 -> 37, of which waited for: 10 -> 10; matrix products, arithmetic and copies ran while one was open for 3% -> 3% of each run, Pallas kernels for 28% -> 27%
where the time goes in v14:
time: 200 us; the launch traced here: 198 us
  waiting for transfers between devices  60.8 us (30%)
  Pallas kernels  57.2 us (29%)
  starting transfers between devices  50.7 us (25%)
  local copies, waits for them, and re-layouts  25.9 us (13%)
  other arithmetic  2.18 us (1%)
    ppermute x37, waiting for transfers between devices, send(): done[step] = lax.ppermute(gated(step, value), 'tile', pairs)  60.8 us
    ppermute x37, starting transfers between devices, send(): done[step] = lax.ppermute(gated(step, value), 'tile', pairs)  50.7 us
    pallas_call x6, Pallas kernels, unit_work(): pl.pallas_call(functools.partial(unit_kernel, index, offset, kinds, brigh...  32.2 us
    unnamed x109, local copies, waits for them, and re-layouts  19.6 us
    pallas_call x3, Pallas kernels, messages_for(): pl.pallas_call(functools.partial(message_kernel, len(others), bool(smalls...  7.63 us
    pallas_call x3, Pallas kernels, put_residuals(): pl.pallas_call(functools.partial(put_kernel, len(arrays)), grid_spec=pltp...  6.77 us
    pallas_call x3, Pallas kernels, build_factors(): pl.pallas_call(functools.partial(build_kernel, sets, slot_ids, pieces, br...  6.67 us
  transfers between devices with their start and end apart: 37, of which 10 were waited for; matrix products, arithmetic and copies ran while one was open for 3% of the time, Pallas kernels for 27%

profile of v14, /device:TPU:0, one launch (start us, length us, event | category | flops | bytes accessed | tf_op | source)
XLA Modules:
  0.0 198.0 jit_solution(13459797559053312191)
XLA Ops:
  0.6 1.4 broadcast_in_dim.34
  2.0 1.2 dynamic-slice_bitcast_fusion.tab_ref
  3.2 2.4 %messages_for.3 = bf16[80,2048]{1,0:T(8,128)(2,1)} custom-call(s32[124]{0:T(128)} %dynamic-slice_bitcast_fusion.tab_ref, bf16[8,2,32,2048]{3,2,1,0:T(8,128)(2,1)} %refs_0_.10, f32[2,256]{1,0:T(2,128)} %refs_4_.5, f32[1,256]{1,0:T(1,128)} %bitcast.25, s32[8,32]{1,0:T(8,128)} %refs_6_.1), custom_call_target="tpu_custom_call" | custom-call | flops 1 | bytes 1 | tf_op jit(solution)/shard_map/messages_for/pallas_call | solution.py:211
  6.1 1.1 copy.15.refs_5_.refs_10_.refs_2_
  10.2 1.6 build_factors.3.refs_0_
  11.8 4.0 %collective-permute-start.1 = (bf16[2,528,256]{2,1,0:T(8,128)(2,1)S(1)}, bf16[2,528,256]{2,1,0:T(8,128)(2,1)S(1)}, u32[]{:S(2)}, u32[]{:S(2)}) collective-permute-start(bf16[2,528,256]{2,1,0:T(8,128)(2,1)S(1)} %build_factors.3.refs_0_), channel_id=1, source_target_pairs={{0,8},{1,9},{2,10},{3,11},{4,0},{5,1},{6,2},{7,3},{8,12},{9,13},{1... | collective-permute-start | bytes 1622024 | tf_op jit(solution)/shard_map/ppermute | solution.py:690
  15.8 2.6 %messages_for.5 = (bf16[80,2048]{1,0:T(8,128)(2,1)}, bf16[80,2048]{1,0:T(8,128)(2,1)}) custom-call(s32[124]{0:T(128)} %dynamic-slice_bitcast_fusion.tab_ref, bf16[8,2,32,2048]{3,2,1,0:T(8,128)(2,1)} %refs_0_.10, bf16[8,2,32,2048]{3,2,1,0:T(8,128)(2,1)} %refs_0_.10, f32[2,256]{1,0:T(2,128)} %refs_4_.5, f32[1,256]{1,0:T(1,128)} %bitcast.26, s32[8,32]{1,0:T(8,128)} %refs_6_.1), custom_call_target="tpu_custom_call" | custom-call | flops 1 | bytes 1 | tf_op jit(solution)/shard_map/messages_for/pallas_call | solution.py:211
  18.4 1.5 collective-permute-start.7
  19.9 2.7 %messages_for.4 = (bf16[64,2048]{1,0:T(8,128)(2,1)}, bf16[64,2048]{1,0:T(8,128)(2,1)}, bf16[64,2048]{1,0:T(8,128)(2,1)}) custom-call(s32[124]{0:T(128)} %dynamic-slice_bitcast_fusion.tab_ref, bf16[8,2,32,2048]{3,2,1,0:T(8,128)(2,1)} %refs_0_.10, bf16[8,2,32,2048]{3,2,1,0:T(8,128)(2,1)} %refs_0_.10, bf16[8,2,32,2048]{3,2,1,0:T(8,128)(2,1)} %refs_0_.10), custom_call_target="tpu_custom_call" | custom-call | flops 1 | bytes 1 | tf_op jit(solution)/shard_map/messages_for/pallas_call | solution.py:211
  22.6 6.6 %collective-permute-done.7.refs_8_.refs_0_ = bf16[80,2048]{1,0:T(8,128)(2,1)S(1)} collective-permute-done((bf16[80,2048]{1,0:T(8,128)(2,1)}, bf16[80,2048]{1,0:T(8,128)(2,1)S(1)}, u32[]{:S(2)}, u32[]{:S(2)}) %collective-permute-start.7) | collective-permute-done | bytes 327712 | tf_op jit(solution)/shard_map/ppermute | solution.py:690
  30.0 2.7 %collective-permute-start.2 = (bf16[528,256]{1,0:T(8,128)(2,1)}, bf16[528,256]{1,0:T(8,128)(2,1)}, u32[]{:S(2)}, u32[]{:S(2)}) collective-permute-start(bf16[528,256]{1,0:T(8,128)(2,1)} %slice_bitcast_fusion.3), channel_id=1, source_target_pairs={{0,8},{1,9},{2,10},{3,11},{4,0},{5,1},{6,2},{7,3},{8,12},{9,13},{1... | collective-permute-start | bytes 811016 | tf_op jit(solution)/shard_map/ppermute | solution.py:690
  32.7 9.2 %collective-permute-done.3.refs_1_ = bf16[2,528,256]{2,1,0:T(8,128)(2,1)S(1)} collective-permute-done((bf16[2,528,256]{2,1,0:T(8,128)(2,1)S(1)}, bf16[2,528,256]{2,1,0:T(8,128)(2,1)S(1)}, u32[]{:S(2)}, u32[]{:S(2)}) %collective-permute-start.3) | collective-permute-done | bytes 540704 | tf_op jit(solution)/shard_map/ppermute | solution.py:690
  43.4 1.5 collective-permute-start.4
  44.9 1.6 build_factors.5.refs_5_
  48.0 2.2 %collective-permute-start.10 = (bf16[2,528,256]{2,1,0:T(8,128)(2,1)S(1)}, bf16[2,528,256]{2,1,0:T(8,128)(2,1)}, u32[]{:S(2)}, u32[]{:S(2)}) collective-permute-start(bf16[2,528,256]{2,1,0:T(8,128)(2,1)S(1)} %build_factors.5.refs_5_), channel_id=1, source_target_pairs={{0,8},{1,9},{2,10},{3,11},{4,0},{5,1},{6,2},{7,3},{8,12},{9,13},{1... | collective-permute-start | bytes 1622024 | tf_op jit(solution)/shard_map/ppermute | solution.py:690
  51.8 2.8 %collective-permute-start.9 = (bf16[2,528,256]{2,1,0:T(8,128)(2,1)S(1)}, bf16[2,528,256]{2,1,0:T(8,128)(2,1)}, u32[]{:S(2)}, u32[]{:S(2)}) collective-permute-start(bf16[2,528,256]{2,1,0:T(8,128)(2,1)S(1)} %build_factors.5.refs_5_), channel_id=1, source_target_pairs={{0,4},{1,5},{2,6},{3,7},{4,12},{5,13},{6,14},{7,15},{8,0},{9,1},{1... | collective-permute-start | bytes 1622024 | tf_op jit(solution)/shard_map/ppermute | solution.py:690
  54.6 3.9 %slices_for.1 = (bf16[2,2,2,256,256]{4,3,2,1,0:T(8,128)(2,1)}, bf16[2,2,2,256,256]{4,3,2,1,0:T(8,128)(2,1)}, bf16[2,2,2,256,256]{4,3,2,1,0:T(8,128)(2,1)}) custom-call(s32[124]{0:T(128)} %dynamic-slice_bitcast_fusion.tab_ref, bf16[2,8,2,256,256]{4,3,2,1,0:T(8,128)(2,1)} %refs_11_.3, bf16[2,8,2,256,256]{4,3,2,1,0:T(8,128)(2,1)} %refs_11_.3, ...), custom_call_target="tpu_custom_call" | custom-call | flops 1 | bytes 1 | tf_op jit(solution)/shard_map/slices_for/pallas_call | solution.py:242
  58.5 1.6 collective-permute-start.17
  60.1 4.4 %collective-permute-done.10.refs_7_ = bf16[2,528,256]{2,1,0:T(8,128)(2,1)} collective-permute-done((bf16[2,528,256]{2,1,0:T(8,128)(2,1)S(1)}, bf16[2,528,256]{2,1,0:T(8,128)(2,1)}, u32[]{:S(2)}, u32[]{:S(2)}) %collective-permute-start.10) | collective-permute-done | bytes 540704 | tf_op jit(solution)/shard_map/ppermute | solution.py:690
  65.5 1.9 collective-permute-start.11
  67.4 10.1 %collective-permute-done.9.refs_6_ = bf16[2,528,256]{2,1,0:T(8,128)(2,1)} collective-permute-done((bf16[2,528,256]{2,1,0:T(8,128)(2,1)S(1)}, bf16[2,528,256]{2,1,0:T(8,128)(2,1)}, u32[]{:S(2)}, u32[]{:S(2)}) %collective-permute-start.9) | collective-permute-done | bytes 540704 | tf_op jit(solution)/shard_map/ppermute | solution.py:690
  83.5 3.5 %build_factors.4 = (bf16[2,512,256]{2,1,0:T(8,128)(2,1)S(1)}, bf16[2,512,256]{2,1,0:T(8,128)(2,1)S(1)}) custom-call(s32[124]{0:T(128)S(1)} %copy-done.45, bf16[8,2,32,2048]{3,2,1,0:T(8,128)(2,1)S(1)} %copy-done.1, bf16[64,2048]{1,0:T(8,128)(2,1)} %collective-permute-done.5.refs_1_, bf16[64,2048]{1,0:T(8,128)(2,1)S(1)} %copy-done.42, ...), custom_call_target="tpu_custom_call" | custom-call | flops 1 | bytes 1 | tf_op jit(solution)/shard_map/build_factors/pallas_call | solution.py:161
  87.0 7.1 %collective-permute-start.12 = (bf16[2,512,256]{2,1,0:T(8,128)(2,1)S(1)}, bf16[2,512,256]{2,1,0:T(8,128)(2,1)S(1)}, u32[]{:S(2)}, u32[]{:S(2)}) collective-permute-start(bf16[2,512,256]{2,1,0:T(8,128)(2,1)S(1)} %get-tuple-element.89.refs_0_), channel_id=1, source_target_pairs={{0,4},{1,5},{2,6},{3,7},{4,12},{5,13},{6,14},{7,15},{8,0},{9,1},{1... | collective-permute-start | bytes 1572872 | tf_op jit(solution)/shard_map/ppermute | solution.py:690
  95.1 5.4 %unit_work.6 = (bf16[2,2,256,256]{3,2,1,0:T(8,128)(2,1)}, f32[1,512]{1,0:T(1,128)S(1)}, f32[2,512,128]{2,1,0:T(8,128)S(1)}) custom-call(s32[124]{0:T(128)S(1)} %copy-done.45, bf16[2,528,256]{2,1,0:T(8,128)(2,1)S(1)} %build_factors.3.refs_0_, bf16[2,528,256]{2,1,0:T(8,128)(2,1)S(1)} %copy-done.8, bf16[2,528,256]{2,1,0:T(8,128)(2,1)S(1)} %copy-done.5, ...), custom_call_target="tpu_custom_call" | custom-call | flops 1 | bytes 1 | tf_op jit(solution)/shard_map/unit_work/pallas_call | solution.py:476
  100.5 3.5 %collective-permute-done.13.refs_10_ = bf16[2,2,2,256,256]{4,3,2,1,0:T(8,128)(2,1)S(1)} collective-permute-done((bf16[2,2,2,256,256]{4,3,2,1,0:T(8,128)(2,1)}, bf16[2,2,2,256,256]{4,3,2,1,0:T(8,128)(2,1)S(1)}, u32[]{:S(2)}, u32[]{:S(2)}) %collective-permute-start.13) | collective-permute-done | bytes 1048608 | tf_op jit(solution)/shard_map/ppermute | solution.py:690
  104.6 5.1 %unit_work.7 = (bf16[2,2,256,256]{3,2,1,0:T(8,128)(2,1)}, f32[1,512]{1,0:T(1,128)S(1)}) custom-call(s32[124]{0:T(128)S(1)} %copy-done.45, bf16[2,528,256]{2,1,0:T(8,128)(2,1)S(1)} %build_factors.3.refs_0_, bf16[2,528,256]{2,1,0:T(8,128)(2,1)S(1)} %copy-done.8, bf16[2,528,256]{2,1,0:T(8,128)(2,1)S(1)} %copy-done.5, ...), custom_call_target="tpu_custom_call" | custom-call | flops 1 | bytes 1 | tf_op jit(solution)/shard_map/unit_work/pallas_call | solution.py:476
  109.8 1.9 collective-permute-start.20
  112.6 16.4 %collective-permute-done.24.refs_7_ = bf16[2,512,256]{2,1,0:T(8,128)(2,1)S(1)} collective-permute-done((bf16[2,512,256]{2,1,0:T(8,128)(2,1)S(1)}, bf16[2,512,256]{2,1,0:T(8,128)(2,1)S(1)}, u32[]{:S(2)}, u32[]{:S(2)}) %collective-permute-start.24) | collective-permute-done | bytes 524320 | tf_op jit(solution)/shard_map/ppermute | solution.py:690
  128.9 1.1 collective-permute-start.19
  132.1 8.1 %collective-permute-done.23.refs_6_ = bf16[2,512,256]{2,1,0:T(8,128)(2,1)S(1)} collective-permute-done((bf16[2,512,256]{2,1,0:T(8,128)(2,1)S(1)}, bf16[2,512,256]{2,1,0:T(8,128)(2,1)S(1)}, u32[]{:S(2)}, u32[]{:S(2)}) %collective-permute-start.23) | collective-permute-done | bytes 524320 | tf_op jit(solution)/shard_map/ppermute | solution.py:690
  143.1 2.8 %collective-permute-start.22 = (bf16[512,256]{1,0:T(8,128)(2,1)}, bf16[512,256]{1,0:T(8,128)(2,1)}, u32[]{:S(2)}, u32[]{:S(2)}) collective-permute-start(bf16[512,256]{1,0:T(8,128)(2,1)} %slice_bitcast_fusion.6), channel_id=1, source_target_pairs={{0,8},{1,9},{2,10},{3,11},{4,0},{5,1},{6,2},{7,3},{8,12},{9,13},{1... | collective-permute-start | bytes 786440 | tf_op jit(solution)/shard_map/ppermute | solution.py:690
  145.9 2.3 %collective-permute-start.25 = (bf16[512,256]{1,0:T(8,128)(2,1)}, bf16[512,256]{1,0:T(8,128)(2,1)}, u32[]{:S(2)}, u32[]{:S(2)}) collective-permute-start(bf16[512,256]{1,0:T(8,128)(2,1)} %slice_bitcast_fusion.5), channel_id=1, source_target_pairs={{0,4},{1,5},{2,6},{3,7},{4,12},{5,13},{6,14},{7,15},{8,0},{9,1},{1... | collective-permute-start | bytes 786440 | tf_op jit(solution)/shard_map/ppermute | solution.py:690
  148.3 2.2 %copy-done.2 = bf16[2,8,2,256,256]{4,3,2,1,0:T(8,128)(2,1)S(1)} copy-done((bf16[2,8,2,256,256]{4,3,2,1,0:T(8,128)(2,1)S(1)}, bf16[2,8,2,256,256]{4,3,2,1,0:T(8,128)(2,1)}, u32[]{:S(2)}) %copy-start.2) | copy-done | bytes 4194328
  150.5 1.2 copy-done.23
  153.7 7.0 %unit_work.8 = (bf16[2,2,256,256]{3,2,1,0:T(8,128)(2,1)S(1)}, bf16[2,2,256,256]{3,2,1,0:T(8,128)(2,1)S(1)}, f32[1,512]{1,0:T(1,128)S(1)}) custom-call(s32[124]{0:T(128)S(1)} %copy-done.45, bf16[2,528,256]{2,1,0:T(8,128)(2,1)S(1)} %build_factors.3.refs_0_, bf16[2,528,256]{2,1,0:T(8,128)(2,1)S(1)} %copy-done.9, bf16[2,528,256]{2,1,0:T(8,128)(2,1)S(1)} %copy-done.6, ...), custom_call_target="tpu_custom_call" | custom-call | flops 1 | bytes 1 | tf_op jit(solution)/shard_map/unit_work/pallas_call | solution.py:476
  160.8 1.3 collective-permute-done.25.refs_8_
  162.2 4.1 %unit_work.9 = (bf16[2,2,256,256]{3,2,1,0:T(8,128)(2,1)S(1)}, f32[1,512]{1,0:T(1,128)S(1)}) custom-call(s32[124]{0:T(128)S(1)} %copy-done.45, bf16[2,512,256]{2,1,0:T(8,128)(2,1)S(1)} %copy-done.19, bf16[2,512,256]{2,1,0:T(8,128)(2,1)S(1)} %copy-done.11, bf16[2,512,256]{2,1,0:T(8,128)(2,1)S(1)} %copy-done.13, ...), custom_call_target="tpu_custom_call" | custom-call | flops 1 | bytes 1 | tf_op jit(solution)/shard_map/unit_work/pallas_call | solution.py:476
  166.3 1.2 collective-permute-start.27
  167.5 4.1 %unit_work.10 = (bf16[2,2,256,256]{3,2,1,0:T(8,128)(2,1)S(1)}, f32[1,512]{1,0:T(1,128)S(1)}) custom-call(s32[124]{0:T(128)S(1)} %copy-done.45, bf16[2,512,256]{2,1,0:T(8,128)(2,1)S(1)} %copy-done.19, bf16[2,512,256]{2,1,0:T(8,128)(2,1)S(1)} %copy-done.11, bf16[2,512,256]{2,1,0:T(8,128)(2,1)S(1)} %copy-done.13, ...), custom_call_target="tpu_custom_call" | custom-call | flops 1 | bytes 1 | tf_op jit(solution)/shard_map/unit_work/pallas_call | solution.py:476
  171.6 6.5 %unit_work.11 = (bf16[2,2,256,256]{3,2,1,0:T(8,128)(2,1)S(1)}, bf16[2,2,256,256]{3,2,1,0:T(8,128)(2,1)S(1)}, f32[1,512]{1,0:T(1,128)S(1)}) custom-call(s32[124]{0:T(128)S(1)} %copy-done.45, bf16[2,512,256]{2,1,0:T(8,128)(2,1)S(1)} %copy-done.19, bf16[2,512,256]{2,1,0:T(8,128)(2,1)S(1)} %copy-done.11, bf16[2,512,256]{2,1,0:T(8,128)(2,1)S(1)} %copy-done.13, ...), custom_call_target="tpu_custom_call" | custom-call | flops 1 | bytes 1 | tf_op jit(solution)/shard_map/unit_work/pallas_call | solution.py:476
  178.1 2.1 %collective-permute-start.33 = (f32[2,128]{1,0:T(2,128)S(1)}, f32[2,128]{1,0:T(2,128)S(1)}, u32[]{:S(2)}, u32[]{:S(2)}) collective-permute-start(f32[2,128]{1,0:T(2,128)S(1)} %get-tuple-element.113), channel_id=1, source_target_pairs={{0,4},{1,5},{2,6},{3,7},{4,12},{5,13},{6,14},{7,15},{8,0},{9,1},{1... | collective-permute-start | bytes 3080 | tf_op jit(solution)/shard_map/ppermute | solution.py:690
  180.2 1.0 collective-permute-start.28
  181.2 5.4 %collective-permute-start.31 = (f32[2,128]{1,0:T(2,128)S(1)}, f32[2,128]{1,0:T(2,128)S(1)}, u32[]{:S(2)}, u32[]{:S(2)}) collective-permute-start(f32[2,128]{1,0:T(2,128)S(1)} %get-tuple-element.108), channel_id=1, source_target_pairs={{0,12},{1,13},{2,14},{3,15},{4,8},{5,9},{6,10},{7,11},{8,4},{9,5},... | collective-permute-start | bytes 3080 | tf_op jit(solution)/shard_map/ppermute | solution.py:690
  186.5 1.9 collective-permute-start.32
  188.5 3.6 %put_residuals.3.refs_2_ = bf16[2,8,2,256,256]{4,3,2,1,0:T(8,128)(2,1)} custom-call(s32[124]{0:T(128)S(1)} %copy-done.45, bf16[2,2,256,256]{3,2,1,0:T(8,128)(2,1)} %collective-permute-done.19.refs_0_, bf16[2,2,256,256]{3,2,1,0:T(8,128)(2,1)} %collective-permute-done.20.refs_1_, bf16[2,2,256,256]{3,2,1,0:T(8,128)(2,1)S(1)} %collective-permute-done.30.refs_2_, ...), custom_call_target="tpu_custom_call" | custom-call | flops 1 | bytes 1 | tf_op jit(solution)/shard_map/put_residuals/pallas_call | solution.py:516
  192.4 1.8 collective-permute-start.36
  194.1 1.6 put_residuals.4.refs_2_
  195.7 1.6 put_residuals.5
  (173 shorter events, 26.1 us)
Async XLA Ops:
  5.6 1.9 collective-permute-start
  11.8 17.4 %collective-permute-start.1 = (bf16[2,528,256]{2,1,0:T(8,128)(2,1)S(1)}, bf16[2,528,256]{2,1,0:T(8,128)(2,1)S(1)}, u32[]{:S(2)}, u32[]{:S(2)}) collective-permute-start(bf16[2,528,256]{2,1,0:T(8,128)(2,1)S(1)} %build_factors.3.refs_0_), channel_id=1, source_target_pairs={{0,8},{1,9},{2,10},{3,11},{4,0},{5,1},{6,2},{7,3},{8,12},{9,13},{1... | collective-permute-start | bytes 1622024 | tf_op jit(solution)/shard_map/ppermute | solution.py:690
  18.4 10.8 %collective-permute-start.7 = (bf16[80,2048]{1,0:T(8,128)(2,1)}, bf16[80,2048]{1,0:T(8,128)(2,1)S(1)}, u32[]{:S(2)}, u32[]{:S(2)}) collective-permute-start(bf16[80,2048]{1,0:T(8,128)(2,1)} %get-tuple-element.64), channel_id=1, source_target_pairs={{0,2},{1,3},{2,0},{3,1},{4,6},{5,7},{6,4},{7,5},{8,10},{9,11},{10,... | collective-permute-start | bytes 983048 | tf_op jit(solution)/shard_map/ppermute | solution.py:690
  19.9 22.0 %collective-permute-start.3 = (bf16[2,528,256]{2,1,0:T(8,128)(2,1)S(1)}, bf16[2,528,256]{2,1,0:T(8,128)(2,1)S(1)}, u32[]{:S(2)}, u32[]{:S(2)}) collective-permute-start(bf16[2,528,256]{2,1,0:T(8,128)(2,1)S(1)} %build_factors.3.refs_0_), channel_id=1, source_target_pairs={{0,4},{1,5},{2,6},{3,7},{4,12},{5,13},{6,14},{7,15},{8,0},{9,1},{1... | collective-permute-start | bytes 1622024 | tf_op jit(solution)/shard_map/ppermute | solution.py:690
  22.6 24.7 %collective-permute-start.6 = (bf16[64,2048]{1,0:T(8,128)(2,1)}, bf16[64,2048]{1,0:T(8,128)(2,1)S(1)}, u32[]{:S(2)}, u32[]{:S(2)}) collective-permute-start(bf16[64,2048]{1,0:T(8,128)(2,1)} %get-tuple-element.63), channel_id=1, source_target_pairs={{0,3},{1,2},{2,1},{3,0},{4,7},{5,6},{6,5},{7,4},{8,11},{9,10},{10,... | collective-permute-start | bytes 786440 | tf_op jit(solution)/shard_map/ppermute | solution.py:690
  29.2 15.7 %collective-permute-start.8 = (bf16[80,2048]{1,0:T(8,128)(2,1)S(1)}, bf16[80,2048]{1,0:T(8,128)(2,1)S(1)}, u32[]{:S(2)}, u32[]{:S(2)}) collective-permute-start(bf16[80,2048]{1,0:T(8,128)(2,1)S(1)} %copy-done.53), channel_id=1, source_target_pairs={{0,3},{1,2},{2,1},{3,0},{4,7},{5,6},{6,5},{7,4},{8,11},{9,10},{10,... | collective-permute-start | bytes 983048 | tf_op jit(solution)/shard_map/ppermute | solution.py:690
  30.0 28.5 %collective-permute-start.2 = (bf16[528,256]{1,0:T(8,128)(2,1)}, bf16[528,256]{1,0:T(8,128)(2,1)}, u32[]{:S(2)}, u32[]{:S(2)}) collective-permute-start(bf16[528,256]{1,0:T(8,128)(2,1)} %slice_bitcast_fusion.3), channel_id=1, source_target_pairs={{0,8},{1,9},{2,10},{3,11},{4,0},{5,1},{6,2},{7,3},{8,12},{9,13},{1... | collective-permute-start | bytes 811016 | tf_op jit(solution)/shard_map/ppermute | solution.py:690
  42.7 15.8 %collective-permute-start.15 = (bf16[528,256]{1,0:T(8,128)(2,1)}, bf16[528,256]{1,0:T(8,128)(2,1)}, u32[]{:S(2)}, u32[]{:S(2)}) collective-permute-start(bf16[528,256]{1,0:T(8,128)(2,1)} %slice_bitcast_fusion.1), channel_id=1, source_target_pairs={{0,4},{1,5},{2,6},{3,7},{4,12},{5,13},{6,14},{7,15},{8,0},{9,1},{1... | collective-permute-start | bytes 811016 | tf_op jit(solution)/shard_map/ppermute | solution.py:690
  43.4 7.7 %collective-permute-start.4 = (bf16[64,2048]{1,0:T(8,128)(2,1)}, bf16[64,2048]{1,0:T(8,128)(2,1)S(1)}, u32[]{:S(2)}, u32[]{:S(2)}) collective-permute-start(bf16[64,2048]{1,0:T(8,128)(2,1)} %get-tuple-element.59), channel_id=1, source_target_pairs={{0,2},{1,3},{2,0},{3,1},{4,6},{5,7},{6,4},{7,5},{8,10},{9,11},{10,... | collective-permute-start | bytes 786440 | tf_op jit(solution)/shard_map/ppermute | solution.py:690
  44.9 13.6 %collective-permute-start.5 = (bf16[64,2048]{1,0:T(8,128)(2,1)}, bf16[64,2048]{1,0:T(8,128)(2,1)}, u32[]{:S(2)}, u32[]{:S(2)}) collective-permute-start(bf16[64,2048]{1,0:T(8,128)(2,1)} %get-tuple-element.62), channel_id=1, source_target_pairs={{0,1},{1,0},{2,3},{3,2},{4,5},{5,4},{6,7},{7,6},{8,9},{9,8},{10,11... | collective-permute-start | bytes 786440 | tf_op jit(solution)/shard_map/ppermute | solution.py:690
  47.3 31.3 %copy-start.1 = (bf16[8,2,32,2048]{3,2,1,0:T(8,128)(2,1)S(1)}, bf16[8,2,32,2048]{3,2,1,0:T(8,128)(2,1)}, u32[]{:S(2)}) copy-start(bf16[8,2,32,2048]{3,2,1,0:T(8,128)(2,1)} %refs_0_.10) | copy-start | bytes 6291460
  47.3 31.3 %copy-start.45 = (s32[124]{0:T(128)S(1)}, s32[124]{0:T(128)}, u32[]{:S(2)}) copy-start(s32[124]{0:T(128)} %dynamic-slice_bitcast_fusion.tab_ref) | copy-start | bytes 1492
  47.3 31.3 %copy-start.47 = (s32[8,32]{1,0:T(8,128)S(1)}, s32[8,32]{1,0:T(8,128)}, u32[]{:S(2)}) copy-start(s32[8,32]{1,0:T(8,128)} %refs_6_.1) | copy-start | bytes 3076
  47.3 31.3 %copy-start.49 = (f32[2,256]{1,0:T(2,128)S(1)}, f32[2,256]{1,0:T(2,128)}, u32[]{:S(2)}) copy-start(f32[2,256]{1,0:T(2,128)} %refs_4_.5) | copy-start | bytes 6148
  47.3 31.3 %copy-start.51 = (f32[256]{0:T(256)S(1)}, f32[256]{0:T(256)}, u32[]{:S(2)}) copy-start(f32[256]{0:T(256)} %broadcast_in_dim.34) | copy-start | bytes 3076
  48.0 16.5 %collective-permute-start.10 = (bf16[2,528,256]{2,1,0:T(8,128)(2,1)S(1)}, bf16[2,528,256]{2,1,0:T(8,128)(2,1)}, u32[]{:S(2)}, u32[]{:S(2)}) collective-permute-start(bf16[2,528,256]{2,1,0:T(8,128)(2,1)S(1)} %build_factors.5.refs_5_), channel_id=1, source_target_pairs={{0,8},{1,9},{2,10},{3,11},{4,0},{5,1},{6,2},{7,3},{8,12},{9,13},{1... | collective-permute-start | bytes 1622024 | tf_op jit(solution)/shard_map/ppermute | solution.py:690
  51.8 25.8 %collective-permute-start.9 = (bf16[2,528,256]{2,1,0:T(8,128)(2,1)S(1)}, bf16[2,528,256]{2,1,0:T(8,128)(2,1)}, u32[]{:S(2)}, u32[]{:S(2)}) collective-permute-start(bf16[2,528,256]{2,1,0:T(8,128)(2,1)S(1)} %build_factors.5.refs_5_), channel_id=1, source_target_pairs={{0,4},{1,5},{2,6},{3,7},{4,12},{5,13},{6,14},{7,15},{8,0},{9,1},{1... | collective-permute-start | bytes 1622024 | tf_op jit(solution)/shard_map/ppermute | solution.py:690
  54.6 40.6 %copy-start.52 = (s32[8,2048]{1,0:T(8,128)S(1)}, s32[8,2048]{1,0:T(8,128)}, u32[]{:S(2)}) copy-start(s32[8,2048]{1,0:T(8,128)} %param.14) | copy-start | bytes 196612
  58.5 36.6 %copy-start.5 = (bf16[2,528,256]{2,1,0:T(8,128)(2,1)S(1)}, bf16[2,528,256]{2,1,0:T(8,128)(2,1)}, u32[]{:S(2)}) copy-start(bf16[2,528,256]{2,1,0:T(8,128)(2,1)} %copy-done.4) | copy-start | bytes 1622020
  58.5 36.6 %copy-start.8 = (bf16[2,528,256]{2,1,0:T(8,128)(2,1)S(1)}, bf16[2,528,256]{2,1,0:T(8,128)(2,1)}, u32[]{:S(2)}) copy-start(bf16[2,528,256]{2,1,0:T(8,128)(2,1)} %copy-done.7) | copy-start | bytes 1622020
  58.5 35.7 %collective-permute-start.17 = (bf16[2,2,2,256,256]{4,3,2,1,0:T(8,128)(2,1)}, bf16[2,2,2,256,256]{4,3,2,1,0:T(8,128)(2,1)S(1)}, u32[]{:S(2)}, u32[]{:S(2)}) collective-permute-start(bf16[2,2,2,256,256]{4,3,2,1,0:T(8,128)(2,1)} %get-tuple-element.77), channel_id=1, source_target_pairs={{0,2},{1,3},{2,0},{3,1},{4,6},{5,7},{6,4},{7,5},{8,10},{9,11},{10,... | collective-permute-start | bytes 3145736 | tf_op jit(solution)/shard_map/ppermute | solution.py:690
  60.1 43.9 %collective-permute-start.13 = (bf16[2,2,2,256,256]{4,3,2,1,0:T(8,128)(2,1)}, bf16[2,2,2,256,256]{4,3,2,1,0:T(8,128)(2,1)S(1)}, u32[]{:S(2)}, u32[]{:S(2)}) collective-permute-start(bf16[2,2,2,256,256]{4,3,2,1,0:T(8,128)(2,1)} %get-tuple-element.73), channel_id=1, source_target_pairs={{0,3},{1,2},{2,1},{3,0},{4,7},{5,6},{6,5},{7,4},{8,11},{9,10},{10,... | collective-permute-start | bytes 3145736 | tf_op jit(solution)/shard_map/ppermute | solution.py:690
  65.5 21.4 %collective-permute-start.11 = (bf16[528,256]{1,0:T(8,128)(2,1)S(1)}, bf16[528,256]{1,0:T(8,128)(2,1)S(1)}, u32[]{:S(2)}, u32[]{:S(2)}) collective-permute-start(bf16[528,256]{1,0:T(8,128)(2,1)S(1)} %slice_bitcast_fusion.2), channel_id=1, source_target_pairs={{0,8},{1,9},{2,10},{3,11},{4,0},{5,1},{6,2},{7,3},{8,12},{9,13},{1... | collective-permute-start | bytes 811016 | tf_op jit(solution)/shard_map/ppermute | solution.py:690
  78.5 15.6 %collective-permute-start.16 = (bf16[528,256]{1,0:T(8,128)(2,1)S(1)}, bf16[528,256]{1,0:T(8,128)(2,1)S(1)}, u32[]{:S(2)}, u32[]{:S(2)}) collective-permute-start(bf16[528,256]{1,0:T(8,128)(2,1)S(1)} %slice_bitcast_fusion), channel_id=1, source_target_pairs={{0,4},{1,5},{2,6},{3,7},{4,12},{5,13},{6,14},{7,15},{8,0},{9,1},{1... | collective-permute-start | bytes 811016 | tf_op jit(solution)/shard_map/ppermute | solution.py:690
  87.0 22.8 %collective-permute-start.12 = (bf16[2,512,256]{2,1,0:T(8,128)(2,1)S(1)}, bf16[2,512,256]{2,1,0:T(8,128)(2,1)S(1)}, u32[]{:S(2)}, u32[]{:S(2)}) collective-permute-start(bf16[2,512,256]{2,1,0:T(8,128)(2,1)S(1)} %get-tuple-element.89.refs_0_), channel_id=1, source_target_pairs={{0,4},{1,5},{2,6},{3,7},{4,12},{5,13},{6,14},{7,15},{8,0},{9,1},{1... | collective-permute-start | bytes 1572872 | tf_op jit(solution)/shard_map/ppermute | solution.py:690
  94.1 48.1 %collective-permute-start.18 = (bf16[2,2,2,256,256]{4,3,2,1,0:T(8,128)(2,1)}, bf16[2,2,2,256,256]{4,3,2,1,0:T(8,128)(2,1)S(1)}, u32[]{:S(2)}, u32[]{:S(2)}) collective-permute-start(bf16[2,2,2,256,256]{4,3,2,1,0:T(8,128)(2,1)} %get-tuple-element.84), channel_id=1, source_target_pairs={{0,1},{1,0},{2,3},{3,2},{4,5},{5,4},{6,7},{7,6},{8,9},{9,8},{10,11... | collective-permute-start | bytes 3145736 | tf_op jit(solution)/shard_map/ppermute | solution.py:690
  94.1 36.0 %collective-permute-start.21 = (bf16[2,512,256]{2,1,0:T(8,128)(2,1)S(1)}, bf16[2,512,256]{2,1,0:T(8,128)(2,1)S(1)}, u32[]{:S(2)}, u32[]{:S(2)}) collective-permute-start(bf16[2,512,256]{2,1,0:T(8,128)(2,1)S(1)} %get-tuple-element.89.refs_0_), channel_id=1, source_target_pairs={{0,8},{1,9},{2,10},{3,11},{4,0},{5,1},{6,2},{7,3},{8,12},{9,13},{1... | collective-permute-start | bytes 1572872 | tf_op jit(solution)/shard_map/ppermute | solution.py:690
  94.2 34.7 %collective-permute-start.24 = (bf16[2,512,256]{2,1,0:T(8,128)(2,1)S(1)}, bf16[2,512,256]{2,1,0:T(8,128)(2,1)S(1)}, u32[]{:S(2)}, u32[]{:S(2)}) collective-permute-start(bf16[2,512,256]{2,1,0:T(8,128)(2,1)S(1)} %get-tuple-element.92.refs_5_), channel_id=1, source_target_pairs={{0,8},{1,9},{2,10},{3,11},{4,0},{5,1},{6,2},{7,3},{8,12},{9,13},{1... | collective-permute-start | bytes 1572872 | tf_op jit(solution)/shard_map/ppermute | solution.py:690
  100.5 47.8 %copy-start.6 = (bf16[2,528,256]{2,1,0:T(8,128)(2,1)S(1)}, bf16[2,528,256]{2,1,0:T(8,128)(2,1)}, u32[]{:S(2)}) copy-start(bf16[2,528,256]{2,1,0:T(8,128)(2,1)} %copy-done.4) | copy-start | bytes 1622020
  100.5 47.8 %copy-start.9 = (bf16[2,528,256]{2,1,0:T(8,128)(2,1)S(1)}, bf16[2,528,256]{2,1,0:T(8,128)(2,1)}, u32[]{:S(2)}) copy-start(bf16[2,528,256]{2,1,0:T(8,128)(2,1)} %copy-done.7) | copy-start | bytes 1622020
  104.0 38.1 %copy-start.25 = (bf16[2,2,2,256,256]{4,3,2,1,0:T(8,128)(2,1)}, bf16[2,2,2,256,256]{4,3,2,1,0:T(8,128)(2,1)S(1)}, u32[]{:S(2)}) copy-start(bf16[2,2,2,256,256]{4,3,2,1,0:T(8,128)(2,1)S(1)} %collective-permute-done.13.refs_10_) | copy-start | bytes 3145732
  104.0 36.1 %collective-permute-start.23 = (bf16[2,512,256]{2,1,0:T(8,128)(2,1)S(1)}, bf16[2,512,256]{2,1,0:T(8,128)(2,1)S(1)}, u32[]{:S(2)}, u32[]{:S(2)}) collective-permute-start(bf16[2,512,256]{2,1,0:T(8,128)(2,1)S(1)} %get-tuple-element.92.refs_5_), channel_id=1, source_target_pairs={{0,4},{1,5},{2,6},{3,7},{4,12},{5,13},{6,14},{7,15},{8,0},{9,1},{1... | collective-permute-start | bytes 1572872 | tf_op jit(solution)/shard_map/ppermute | solution.py:690
  109.8 50.9 %collective-permute-start.20 = (bf16[2,2,256,256]{3,2,1,0:T(8,128)(2,1)}, bf16[2,2,256,256]{3,2,1,0:T(8,128)(2,1)}, u32[]{:S(2)}, u32[]{:S(2)}) collective-permute-start(bf16[2,2,256,256]{3,2,1,0:T(8,128)(2,1)} %get-tuple-element.87), channel_id=1, source_target_pairs={{0,3},{1,2},{2,1},{3,0},{4,7},{5,6},{6,5},{7,4},{8,11},{9,10},{10,... | collective-permute-start | bytes 1572872 | tf_op jit(solution)/shard_map/ppermute | solution.py:690
  128.9 31.9 %collective-permute-start.19 = (bf16[2,2,256,256]{3,2,1,0:T(8,128)(2,1)}, bf16[2,2,256,256]{3,2,1,0:T(8,128)(2,1)}, u32[]{:S(2)}, u32[]{:S(2)}) collective-permute-start(bf16[2,2,256,256]{3,2,1,0:T(8,128)(2,1)} %get-tuple-element.86), channel_id=1, source_target_pairs={{0,2},{1,3},{2,0},{3,1},{4,6},{5,7},{6,4},{7,5},{8,10},{9,11},{10,... | collective-permute-start | bytes 1572872 | tf_op jit(solution)/shard_map/ppermute | solution.py:690
  130.1 15.8 %collective-permute-start.14 = (bf16[512,256]{1,0:T(8,128)(2,1)S(1)}, bf16[512,256]{1,0:T(8,128)(2,1)S(1)}, u32[]{:S(2)}, u32[]{:S(2)}) collective-permute-start(bf16[512,256]{1,0:T(8,128)(2,1)S(1)} %slice_bitcast_fusion.7), channel_id=1, source_target_pairs={{0,4},{1,5},{2,6},{3,7},{4,12},{5,13},{6,14},{7,15},{8,0},{9,1},{1... | collective-permute-start | bytes 786440 | tf_op jit(solution)/shard_map/ppermute | solution.py:690
  140.2 20.6 %collective-permute-start.26 = (bf16[512,256]{1,0:T(8,128)(2,1)S(1)}, bf16[512,256]{1,0:T(8,128)(2,1)S(1)}, u32[]{:S(2)}, u32[]{:S(2)}) collective-permute-start(bf16[512,256]{1,0:T(8,128)(2,1)S(1)} %slice_bitcast_fusion.4), channel_id=1, source_target_pairs={{0,8},{1,9},{2,10},{3,11},{4,0},{5,1},{6,2},{7,3},{8,12},{9,13},{1... | collective-permute-start | bytes 786440 | tf_op jit(solution)/shard_map/ppermute | solution.py:690
  143.1 17.7 %collective-permute-start.22 = (bf16[512,256]{1,0:T(8,128)(2,1)}, bf16[512,256]{1,0:T(8,128)(2,1)}, u32[]{:S(2)}, u32[]{:S(2)}) collective-permute-start(bf16[512,256]{1,0:T(8,128)(2,1)} %slice_bitcast_fusion.6), channel_id=1, source_target_pairs={{0,8},{1,9},{2,10},{3,11},{4,0},{5,1},{6,2},{7,3},{8,12},{9,13},{1... | collective-permute-start | bytes 786440 | tf_op jit(solution)/shard_map/ppermute | solution.py:690
  145.9 16.2 %collective-permute-start.25 = (bf16[512,256]{1,0:T(8,128)(2,1)}, bf16[512,256]{1,0:T(8,128)(2,1)}, u32[]{:S(2)}, u32[]{:S(2)}) collective-permute-start(bf16[512,256]{1,0:T(8,128)(2,1)} %slice_bitcast_fusion.5), channel_id=1, source_target_pairs={{0,4},{1,5},{2,6},{3,7},{4,12},{5,13},{6,14},{7,15},{8,0},{9,1},{1... | collective-permute-start | bytes 786440 | tf_op jit(solution)/shard_map/ppermute | solution.py:690
  160.7 20.5 %collective-permute-start.30 = (bf16[2,2,256,256]{3,2,1,0:T(8,128)(2,1)S(1)}, bf16[2,2,256,256]{3,2,1,0:T(8,128)(2,1)S(1)}, u32[]{:S(2)}, u32[]{:S(2)}) collective-permute-start(bf16[2,2,256,256]{3,2,1,0:T(8,128)(2,1)S(1)} %get-tuple-element.105), channel_id=1, source_target_pairs={{0,1},{1,0},{2,3},{3,2},{4,5},{5,4},{6,7},{7,6},{8,9},{9,8},{10,11... | collective-permute-start | bytes 1572872 | tf_op jit(solution)/shard_map/ppermute | solution.py:690
  166.3 20.3 %collective-permute-start.27 = (bf16[2,2,256,256]{3,2,1,0:T(8,128)(2,1)S(1)}, bf16[2,2,256,256]{3,2,1,0:T(8,128)(2,1)S(1)}, u32[]{:S(2)}, u32[]{:S(2)}) collective-permute-start(bf16[2,2,256,256]{3,2,1,0:T(8,128)(2,1)S(1)} %get-tuple-element.94), channel_id=1, source_target_pairs={{0,2},{1,3},{2,0},{3,1},{4,6},{5,7},{6,4},{7,5},{8,10},{9,11},{10,... | collective-permute-start | bytes 1572872 | tf_op jit(solution)/shard_map/ppermute | solution.py:690
  178.1 14.1 %collective-permute-start.33 = (f32[2,128]{1,0:T(2,128)S(1)}, f32[2,128]{1,0:T(2,128)S(1)}, u32[]{:S(2)}, u32[]{:S(2)}) collective-permute-start(f32[2,128]{1,0:T(2,128)S(1)} %get-tuple-element.113), channel_id=1, source_target_pairs={{0,4},{1,5},{2,6},{3,7},{4,12},{5,13},{6,14},{7,15},{8,0},{9,1},{1... | collective-permute-start | bytes 3080 | tf_op jit(solution)/shard_map/ppermute | solution.py:690
  180.1 14.0 %collective-permute-start.29 = (bf16[2,2,256,256]{3,2,1,0:T(8,128)(2,1)S(1)}, bf16[2,2,256,256]{3,2,1,0:T(8,128)(2,1)S(1)}, u32[]{:S(2)}, u32[]{:S(2)}) collective-permute-start(bf16[2,2,256,256]{3,2,1,0:T(8,128)(2,1)S(1)} %get-tuple-element.102), channel_id=1, source_target_pairs={{0,1},{1,0},{2,3},{3,2},{4,5},{5,4},{6,7},{7,6},{8,9},{9,8},{10,11... | collective-permute-start | bytes 1572872 | tf_op jit(solution)/shard_map/ppermute | solution.py:690
  180.2 15.6 %collective-permute-start.28 = (bf16[2,2,256,256]{3,2,1,0:T(8,128)(2,1)S(1)}, bf16[2,2,256,256]{3,2,1,0:T(8,128)(2,1)S(1)}, u32[]{:S(2)}, u32[]{:S(2)}) collective-permute-start(bf16[2,2,256,256]{3,2,1,0:T(8,128)(2,1)S(1)} %get-tuple-element.98), channel_id=1, source_target_pairs={{0,3},{1,2},{2,1},{3,0},{4,7},{5,6},{6,5},{7,4},{8,11},{9,10},{10,... | collective-permute-start | bytes 1572872 | tf_op jit(solution)/shard_map/ppermute | solution.py:690
  181.2 11.0 %collective-permute-start.31 = (f32[2,128]{1,0:T(2,128)S(1)}, f32[2,128]{1,0:T(2,128)S(1)}, u32[]{:S(2)}, u32[]{:S(2)}) collective-permute-start(f32[2,128]{1,0:T(2,128)S(1)} %get-tuple-element.108), channel_id=1, source_target_pairs={{0,12},{1,13},{2,14},{3,15},{4,8},{5,9},{6,10},{7,11},{8,4},{9,5},... | collective-permute-start | bytes 3080 | tf_op jit(solution)/shard_map/ppermute | solution.py:690
  186.5 5.6 %collective-permute-start.32 = (f32[2,128]{1,0:T(2,128)S(1)}, f32[2,128]{1,0:T(2,128)S(1)}, u32[]{:S(2)}, u32[]{:S(2)}) collective-permute-start(f32[2,128]{1,0:T(2,128)S(1)} %get-tuple-element.109), channel_id=1, source_target_pairs={{0,8},{1,9},{2,10},{3,11},{4,0},{5,1},{6,2},{7,3},{8,12},{9,13},{1... | collective-permute-start | bytes 3080 | tf_op jit(solution)/shard_map/ppermute | solution.py:690
  192.3 5.0 %collective-permute-start.34 = (f32[2,32]{1,0:T(2,128)S(1)}, f32[2,32]{1,0:T(2,128)S(1)}, u32[]{:S(2)}, u32[]{:S(2)}) collective-permute-start(f32[2,32]{1,0:T(2,128)S(1)} %get-tuple-element.110), channel_id=1, source_target_pairs={{0,1},{1,0},{2,3},{3,2},{4,5},{5,4},{6,7},{7,6},{8,9},{9,8},{10,11... | collective-permute-start | bytes 776 | tf_op jit(solution)/shard_map/ppermute | solution.py:690
  192.3 5.0 %collective-permute-start.35 = (f32[2,32]{1,0:T(2,128)S(1)}, f32[2,32]{1,0:T(2,128)S(1)}, u32[]{:S(2)}, u32[]{:S(2)}) collective-permute-start(f32[2,32]{1,0:T(2,128)S(1)} %get-tuple-element.111), channel_id=1, source_target_pairs={{0,2},{1,3},{2,0},{3,1},{4,6},{5,7},{6,4},{7,5},{8,10},{9,11},{10,... | collective-permute-start | bytes 776 | tf_op jit(solution)/shard_map/ppermute | solution.py:690
  192.4 5.0 %collective-permute-start.36 = (f32[2,32]{1,0:T(2,128)S(1)}, f32[2,32]{1,0:T(2,128)S(1)}, u32[]{:S(2)}, u32[]{:S(2)}) collective-permute-start(f32[2,32]{1,0:T(2,128)S(1)} %get-tuple-element.116), channel_id=1, source_target_pairs={{0,3},{1,2},{2,1},{3,0},{4,7},{5,6},{6,5},{7,4},{8,11},{9,10},{10,... | collective-permute-start | bytes 776 | tf_op jit(solution)/shard_map/ppermute | solution.py:690
  (43 other events, 278.2 us)

commit v15 on v14

--- a/solution.py
+++ b/solution.py
@@ -785,12 +785,14 @@
     pieces += entries(rest, rest_sides, rest_far, number, number)
     arrived, columns = work(0, WORK, HOME, [pieces], share)
     far_1 = far(PIECE_FAR[1], near_1)
-    residual = put(PUT, 0, arrived, 0, None)
+    first_arrived = arrived
     ready = [
         entries(piece, sides, halves, 0, group)
         for piece, sides, halves in zip(later_pieces, (near_0, near_1), (far_0, far_1))
     ]
     arrived, _ = work(1, LATER_WORK, LATER_HOME, ready, columns)
+
+    residual = put(PUT, 0, [*first_arrived, arrived[0]], 0, None)
 
     partial = jnp.concatenate(grads, 0)
     parts = [partial[:, n * group : (n + 1) * group] for n in range(4)]
@@ -809,7 +811,7 @@
     summed = summed.reshape(slots, per_group)
 
     residual = put(PUT_NEAR, 2, arrived[2:], 1, residual)
-    residual = put(PUT_LAST, 0, arrived[:2], 1, residual)
+    residual = put(PUT_LAST, 1, arrived[1:2], 1, residual)
     return residual, summed
 
 

time: 200 us -> 200 us (level)
  no operation moved by 1% of the time
where the time goes in v15:
time: 200 us; the launch traced here: 198 us
  waiting for transfers between devices  60.8 us (30%)
  Pallas kernels  57.6 us (29%)
  starting transfers between devices  50.7 us (25%)
  local copies, waits for them, and re-layouts  25.9 us (13%)
  other arithmetic  2.18 us (1%)
    ppermute x37, waiting for transfers between devices, send(): done[step] = lax.ppermute(gated(step, value), 'tile', pairs)  60.8 us
    ppermute x37, starting transfers between devices, send(): done[step] = lax.ppermute(gated(step, value), 'tile', pairs)  50.7 us
    pallas_call x6, Pallas kernels, unit_work(): pl.pallas_call(functools.partial(unit_kernel, index, offset, kinds, brigh...  32.2 us
    unnamed x109, local copies, waits for them, and re-layouts  19.6 us
    pallas_call x3, Pallas kernels, messages_for(): pl.pallas_call(functools.partial(message_kernel, len(others), bool(smalls...  7.63 us
    pallas_call x3, Pallas kernels, put_residuals(): pl.pallas_call(functools.partial(put_kernel, len(arrays)), grid_spec=pltp...  7.23 us
    pallas_call x3, Pallas kernels, build_factors(): pl.pallas_call(functools.partial(build_kernel, sets, slot_ids, pieces, br...  6.67 us
  transfers between devices with their start and end apart: 37, of which 10 were waited for; matrix products, arithmetic and copies ran while one was open for 3% of the time, Pallas kernels for 27%

profile of v15, /device:TPU:0, one launch (start us, length us, event | category | flops | bytes accessed | tf_op | source)
XLA Modules:
  0.0 198.5 jit_solution(7175820855059218952)
XLA Ops:
  0.6 1.4 broadcast_in_dim.34
  2.0 1.2 dynamic-slice_bitcast_fusion.tab_ref
  3.2 2.4 %messages_for.3 = bf16[80,2048]{1,0:T(8,128)(2,1)} custom-call(s32[124]{0:T(128)} %dynamic-slice_bitcast_fusion.tab_ref, bf16[8,2,32,2048]{3,2,1,0:T(8,128)(2,1)} %refs_0_.10, f32[2,256]{1,0:T(2,128)} %refs_4_.5, f32[1,256]{1,0:T(1,128)} %bitcast.25, s32[8,32]{1,0:T(8,128)} %refs_6_.1), custom_call_target="tpu_custom_call" | custom-call | flops 1 | bytes 1 | tf_op jit(solution)/shard_map/messages_for/pallas_call | solution.py:211
  6.1 1.1 copy.15.refs_5_.refs_10_.refs_2_
  10.2 1.6 build_factors.3.refs_0_
  11.8 4.0 %collective-permute-start.1 = (bf16[2,528,256]{2,1,0:T(8,128)(2,1)S(1)}, bf16[2,528,256]{2,1,0:T(8,128)(2,1)S(1)}, u32[]{:S(2)}, u32[]{:S(2)}) collective-permute-start(bf16[2,528,256]{2,1,0:T(8,128)(2,1)S(1)} %build_factors.3.refs_0_), channel_id=1, source_target_pairs={{0,8},{1,9},{2,10},{3,11},{4,0},{5,1},{6,2},{7,3},{8,12},{9,13},{1... | collective-permute-start | bytes 1622024 | tf_op jit(solution)/shard_map/ppermute | solution.py:690
  15.8 2.6 %messages_for.5 = (bf16[80,2048]{1,0:T(8,128)(2,1)}, bf16[80,2048]{1,0:T(8,128)(2,1)}) custom-call(s32[124]{0:T(128)} %dynamic-slice_bitcast_fusion.tab_ref, bf16[8,2,32,2048]{3,2,1,0:T(8,128)(2,1)} %refs_0_.10, bf16[8,2,32,2048]{3,2,1,0:T(8,128)(2,1)} %refs_0_.10, f32[2,256]{1,0:T(2,128)} %refs_4_.5, f32[1,256]{1,0:T(1,128)} %bitcast.26, s32[8,32]{1,0:T(8,128)} %refs_6_.1), custom_call_target="tpu_custom_call" | custom-call | flops 1 | bytes 1 | tf_op jit(solution)/shard_map/messages_for/pallas_call | solution.py:211
  18.4 1.5 collective-permute-start.7
  19.9 2.7 %messages_for.4 = (bf16[64,2048]{1,0:T(8,128)(2,1)}, bf16[64,2048]{1,0:T(8,128)(2,1)}, bf16[64,2048]{1,0:T(8,128)(2,1)}) custom-call(s32[124]{0:T(128)} %dynamic-slice_bitcast_fusion.tab_ref, bf16[8,2,32,2048]{3,2,1,0:T(8,128)(2,1)} %refs_0_.10, bf16[8,2,32,2048]{3,2,1,0:T(8,128)(2,1)} %refs_0_.10, bf16[8,2,32,2048]{3,2,1,0:T(8,128)(2,1)} %refs_0_.10), custom_call_target="tpu_custom_call" | custom-call | flops 1 | bytes 1 | tf_op jit(solution)/shard_map/messages_for/pallas_call | solution.py:211
  22.6 6.6 %collective-permute-done.7.refs_8_.refs_0_ = bf16[80,2048]{1,0:T(8,128)(2,1)S(1)} collective-permute-done((bf16[80,2048]{1,0:T(8,128)(2,1)}, bf16[80,2048]{1,0:T(8,128)(2,1)S(1)}, u32[]{:S(2)}, u32[]{:S(2)}) %collective-permute-start.7) | collective-permute-done | bytes 327712 | tf_op jit(solution)/shard_map/ppermute | solution.py:690
  30.0 2.7 %collective-permute-start.2 = (bf16[528,256]{1,0:T(8,128)(2,1)}, bf16[528,256]{1,0:T(8,128)(2,1)}, u32[]{:S(2)}, u32[]{:S(2)}) collective-permute-start(bf16[528,256]{1,0:T(8,128)(2,1)} %slice_bitcast_fusion.3), channel_id=1, source_target_pairs={{0,8},{1,9},{2,10},{3,11},{4,0},{5,1},{6,2},{7,3},{8,12},{9,13},{1... | collective-permute-start | bytes 811016 | tf_op jit(solution)/shard_map/ppermute | solution.py:690
  32.7 9.2 %collective-permute-done.3.refs_1_ = bf16[2,528,256]{2,1,0:T(8,128)(2,1)S(1)} collective-permute-done((bf16[2,528,256]{2,1,0:T(8,128)(2,1)S(1)}, bf16[2,528,256]{2,1,0:T(8,128)(2,1)S(1)}, u32[]{:S(2)}, u32[]{:S(2)}) %collective-permute-start.3) | collective-permute-done | bytes 540704 | tf_op jit(solution)/shard_map/ppermute | solution.py:690
  43.4 1.5 collective-permute-start.4
  44.9 1.6 build_factors.5.refs_5_
  48.0 2.2 %collective-permute-start.10 = (bf16[2,528,256]{2,1,0:T(8,128)(2,1)S(1)}, bf16[2,528,256]{2,1,0:T(8,128)(2,1)}, u32[]{:S(2)}, u32[]{:S(2)}) collective-permute-start(bf16[2,528,256]{2,1,0:T(8,128)(2,1)S(1)} %build_factors.5.refs_5_), channel_id=1, source_target_pairs={{0,8},{1,9},{2,10},{3,11},{4,0},{5,1},{6,2},{7,3},{8,12},{9,13},{1... | collective-permute-start | bytes 1622024 | tf_op jit(solution)/shard_map/ppermute | solution.py:690
  51.8 2.8 %collective-permute-start.9 = (bf16[2,528,256]{2,1,0:T(8,128)(2,1)S(1)}, bf16[2,528,256]{2,1,0:T(8,128)(2,1)}, u32[]{:S(2)}, u32[]{:S(2)}) collective-permute-start(bf16[2,528,256]{2,1,0:T(8,128)(2,1)S(1)} %build_factors.5.refs_5_), channel_id=1, source_target_pairs={{0,4},{1,5},{2,6},{3,7},{4,12},{5,13},{6,14},{7,15},{8,0},{9,1},{1... | collective-permute-start | bytes 1622024 | tf_op jit(solution)/shard_map/ppermute | solution.py:690
  54.6 3.9 %slices_for.1 = (bf16[2,2,2,256,256]{4,3,2,1,0:T(8,128)(2,1)}, bf16[2,2,2,256,256]{4,3,2,1,0:T(8,128)(2,1)}, bf16[2,2,2,256,256]{4,3,2,1,0:T(8,128)(2,1)}) custom-call(s32[124]{0:T(128)} %dynamic-slice_bitcast_fusion.tab_ref, bf16[2,8,2,256,256]{4,3,2,1,0:T(8,128)(2,1)} %refs_11_.3, bf16[2,8,2,256,256]{4,3,2,1,0:T(8,128)(2,1)} %refs_11_.3, ...), custom_call_target="tpu_custom_call" | custom-call | flops 1 | bytes 1 | tf_op jit(solution)/shard_map/slices_for/pallas_call | solution.py:242
  58.5 1.6 collective-permute-start.17
  60.1 4.4 %collective-permute-done.10.refs_7_ = bf16[2,528,256]{2,1,0:T(8,128)(2,1)} collective-permute-done((bf16[2,528,256]{2,1,0:T(8,128)(2,1)S(1)}, bf16[2,528,256]{2,1,0:T(8,128)(2,1)}, u32[]{:S(2)}, u32[]{:S(2)}) %collective-permute-start.10) | collective-permute-done | bytes 540704 | tf_op jit(solution)/shard_map/ppermute | solution.py:690
  65.5 1.9 collective-permute-start.11
  67.4 10.1 %collective-permute-done.9.refs_6_ = bf16[2,528,256]{2,1,0:T(8,128)(2,1)} collective-permute-done((bf16[2,528,256]{2,1,0:T(8,128)(2,1)S(1)}, bf16[2,528,256]{2,1,0:T(8,128)(2,1)}, u32[]{:S(2)}, u32[]{:S(2)}) %collective-permute-start.9) | collective-permute-done | bytes 540704 | tf_op jit(solution)/shard_map/ppermute | solution.py:690
  83.5 3.5 %build_factors.4 = (bf16[2,512,256]{2,1,0:T(8,128)(2,1)S(1)}, bf16[2,512,256]{2,1,0:T(8,128)(2,1)S(1)}) custom-call(s32[124]{0:T(128)S(1)} %copy-done.45, bf16[8,2,32,2048]{3,2,1,0:T(8,128)(2,1)S(1)} %copy-done.1, bf16[64,2048]{1,0:T(8,128)(2,1)} %collective-permute-done.5.refs_1_, bf16[64,2048]{1,0:T(8,128)(2,1)S(1)} %copy-done.42, ...), custom_call_target="tpu_custom_call" | custom-call | flops 1 | bytes 1 | tf_op jit(solution)/shard_map/build_factors/pallas_call | solution.py:161
  87.0 7.1 %collective-permute-start.12 = (bf16[2,512,256]{2,1,0:T(8,128)(2,1)S(1)}, bf16[2,512,256]{2,1,0:T(8,128)(2,1)S(1)}, u32[]{:S(2)}, u32[]{:S(2)}) collective-permute-start(bf16[2,512,256]{2,1,0:T(8,128)(2,1)S(1)} %get-tuple-element.89.refs_0_), channel_id=1, source_target_pairs={{0,4},{1,5},{2,6},{3,7},{4,12},{5,13},{6,14},{7,15},{8,0},{9,1},{1... | collective-permute-start | bytes 1572872 | tf_op jit(solution)/shard_map/ppermute | solution.py:690
  95.1 5.4 %unit_work.6 = (bf16[2,2,256,256]{3,2,1,0:T(8,128)(2,1)}, f32[1,512]{1,0:T(1,128)S(1)}, f32[2,512,128]{2,1,0:T(8,128)S(1)}) custom-call(s32[124]{0:T(128)S(1)} %copy-done.45, bf16[2,528,256]{2,1,0:T(8,128)(2,1)S(1)} %build_factors.3.refs_0_, bf16[2,528,256]{2,1,0:T(8,128)(2,1)S(1)} %copy-done.8, bf16[2,528,256]{2,1,0:T(8,128)(2,1)S(1)} %copy-done.5, ...), custom_call_target="tpu_custom_call" | custom-call | flops 1 | bytes 1 | tf_op jit(solution)/shard_map/unit_work/pallas_call | solution.py:476
  100.5 3.5 %collective-permute-done.13.refs_10_ = bf16[2,2,2,256,256]{4,3,2,1,0:T(8,128)(2,1)S(1)} collective-permute-done((bf16[2,2,2,256,256]{4,3,2,1,0:T(8,128)(2,1)}, bf16[2,2,2,256,256]{4,3,2,1,0:T(8,128)(2,1)S(1)}, u32[]{:S(2)}, u32[]{:S(2)}) %collective-permute-start.13) | collective-permute-done | bytes 1048608 | tf_op jit(solution)/shard_map/ppermute | solution.py:690
  104.6 5.1 %unit_work.7 = (bf16[2,2,256,256]{3,2,1,0:T(8,128)(2,1)}, f32[1,512]{1,0:T(1,128)S(1)}) custom-call(s32[124]{0:T(128)S(1)} %copy-done.45, bf16[2,528,256]{2,1,0:T(8,128)(2,1)S(1)} %build_factors.3.refs_0_, bf16[2,528,256]{2,1,0:T(8,128)(2,1)S(1)} %copy-done.8, bf16[2,528,256]{2,1,0:T(8,128)(2,1)S(1)} %copy-done.5, ...), custom_call_target="tpu_custom_call" | custom-call | flops 1 | bytes 1 | tf_op jit(solution)/shard_map/unit_work/pallas_call | solution.py:476
  109.8 1.9 collective-permute-start.20
  112.6 16.4 %collective-permute-done.24.refs_7_ = bf16[2,512,256]{2,1,0:T(8,128)(2,1)S(1)} collective-permute-done((bf16[2,512,256]{2,1,0:T(8,128)(2,1)S(1)}, bf16[2,512,256]{2,1,0:T(8,128)(2,1)S(1)}, u32[]{:S(2)}, u32[]{:S(2)}) %collective-permute-start.24) | collective-permute-done | bytes 524320 | tf_op jit(solution)/shard_map/ppermute | solution.py:690
  128.9 1.1 collective-permute-start.19
  132.1 8.1 %collective-permute-done.23.refs_6_ = bf16[2,512,256]{2,1,0:T(8,128)(2,1)S(1)} collective-permute-done((bf16[2,512,256]{2,1,0:T(8,128)(2,1)S(1)}, bf16[2,512,256]{2,1,0:T(8,128)(2,1)S(1)}, u32[]{:S(2)}, u32[]{:S(2)}) %collective-permute-start.23) | collective-permute-done | bytes 524320 | tf_op jit(solution)/shard_map/ppermute | solution.py:690
  143.1 2.8 %collective-permute-start.22 = (bf16[512,256]{1,0:T(8,128)(2,1)}, bf16[512,256]{1,0:T(8,128)(2,1)}, u32[]{:S(2)}, u32[]{:S(2)}) collective-permute-start(bf16[512,256]{1,0:T(8,128)(2,1)} %slice_bitcast_fusion.6), channel_id=1, source_target_pairs={{0,8},{1,9},{2,10},{3,11},{4,0},{5,1},{6,2},{7,3},{8,12},{9,13},{1... | collective-permute-start | bytes 786440 | tf_op jit(solution)/shard_map/ppermute | solution.py:690
  145.9 2.3 %collective-permute-start.25 = (bf16[512,256]{1,0:T(8,128)(2,1)}, bf16[512,256]{1,0:T(8,128)(2,1)}, u32[]{:S(2)}, u32[]{:S(2)}) collective-permute-start(bf16[512,256]{1,0:T(8,128)(2,1)} %slice_bitcast_fusion.5), channel_id=1, source_target_pairs={{0,4},{1,5},{2,6},{3,7},{4,12},{5,13},{6,14},{7,15},{8,0},{9,1},{1... | collective-permute-start | bytes 786440 | tf_op jit(solution)/shard_map/ppermute | solution.py:690
  148.3 2.2 %copy-done.2 = bf16[2,8,2,256,256]{4,3,2,1,0:T(8,128)(2,1)S(1)} copy-done((bf16[2,8,2,256,256]{4,3,2,1,0:T(8,128)(2,1)S(1)}, bf16[2,8,2,256,256]{4,3,2,1,0:T(8,128)(2,1)}, u32[]{:S(2)}) %copy-start.2) | copy-done | bytes 4194328
  150.5 1.2 copy-done.23
  153.7 7.0 %unit_work.8 = (bf16[2,2,256,256]{3,2,1,0:T(8,128)(2,1)S(1)}, bf16[2,2,256,256]{3,2,1,0:T(8,128)(2,1)S(1)}, f32[1,512]{1,0:T(1,128)S(1)}) custom-call(s32[124]{0:T(128)S(1)} %copy-done.45, bf16[2,528,256]{2,1,0:T(8,128)(2,1)S(1)} %build_factors.3.refs_0_, bf16[2,528,256]{2,1,0:T(8,128)(2,1)S(1)} %copy-done.9, bf16[2,528,256]{2,1,0:T(8,128)(2,1)S(1)} %copy-done.6, ...), custom_call_target="tpu_custom_call" | custom-call | flops 1 | bytes 1 | tf_op jit(solution)/shard_map/unit_work/pallas_call | solution.py:476
  160.8 1.3 collective-permute-done.25.refs_8_
  162.2 4.1 %unit_work.9 = (bf16[2,2,256,256]{3,2,1,0:T(8,128)(2,1)S(1)}, f32[1,512]{1,0:T(1,128)S(1)}) custom-call(s32[124]{0:T(128)S(1)} %copy-done.45, bf16[2,512,256]{2,1,0:T(8,128)(2,1)S(1)} %copy-done.19, bf16[2,512,256]{2,1,0:T(8,128)(2,1)S(1)} %copy-done.11, bf16[2,512,256]{2,1,0:T(8,128)(2,1)S(1)} %copy-done.13, ...), custom_call_target="tpu_custom_call" | custom-call | flops 1 | bytes 1 | tf_op jit(solution)/shard_map/unit_work/pallas_call | solution.py:476
  166.3 1.2 collective-permute-start.30
  167.5 4.1 %unit_work.10 = (bf16[2,2,256,256]{3,2,1,0:T(8,128)(2,1)S(1)}, f32[1,512]{1,0:T(1,128)S(1)}) custom-call(s32[124]{0:T(128)S(1)} %copy-done.45, bf16[2,512,256]{2,1,0:T(8,128)(2,1)S(1)} %copy-done.19, bf16[2,512,256]{2,1,0:T(8,128)(2,1)S(1)} %copy-done.11, bf16[2,512,256]{2,1,0:T(8,128)(2,1)S(1)} %copy-done.13, ...), custom_call_target="tpu_custom_call" | custom-call | flops 1 | bytes 1 | tf_op jit(solution)/shard_map/unit_work/pallas_call | solution.py:476
  171.6 6.5 %unit_work.11 = (bf16[2,2,256,256]{3,2,1,0:T(8,128)(2,1)S(1)}, bf16[2,2,256,256]{3,2,1,0:T(8,128)(2,1)S(1)}, f32[1,512]{1,0:T(1,128)S(1)}) custom-call(s32[124]{0:T(128)S(1)} %copy-done.45, bf16[2,512,256]{2,1,0:T(8,128)(2,1)S(1)} %copy-done.19, bf16[2,512,256]{2,1,0:T(8,128)(2,1)S(1)} %copy-done.11, bf16[2,512,256]{2,1,0:T(8,128)(2,1)S(1)} %copy-done.13, ...), custom_call_target="tpu_custom_call" | custom-call | flops 1 | bytes 1 | tf_op jit(solution)/shard_map/unit_work/pallas_call | solution.py:476
  178.1 2.1 %collective-permute-start.33 = (f32[2,128]{1,0:T(2,128)S(1)}, f32[2,128]{1,0:T(2,128)S(1)}, u32[]{:S(2)}, u32[]{:S(2)}) collective-permute-start(f32[2,128]{1,0:T(2,128)S(1)} %get-tuple-element.113), channel_id=1, source_target_pairs={{0,4},{1,5},{2,6},{3,7},{4,12},{5,13},{6,14},{7,15},{8,0},{9,1},{1... | collective-permute-start | bytes 3080 | tf_op jit(solution)/shard_map/ppermute | solution.py:690
  180.2 1.0 collective-permute-start.27
  181.2 5.4 %collective-permute-start.31 = (f32[2,128]{1,0:T(2,128)S(1)}, f32[2,128]{1,0:T(2,128)S(1)}, u32[]{:S(2)}, u32[]{:S(2)}) collective-permute-start(f32[2,128]{1,0:T(2,128)S(1)} %get-tuple-element.108), channel_id=1, source_target_pairs={{0,12},{1,13},{2,14},{3,15},{4,8},{5,9},{6,10},{7,11},{8,4},{9,5},... | collective-permute-start | bytes 3080 | tf_op jit(solution)/shard_map/ppermute | solution.py:690
  186.5 1.9 collective-permute-start.32
  188.5 4.3 %put_residuals.3.refs_2_ = bf16[2,8,2,256,256]{4,3,2,1,0:T(8,128)(2,1)} custom-call(s32[124]{0:T(128)S(1)} %copy-done.45, bf16[2,2,256,256]{3,2,1,0:T(8,128)(2,1)} %collective-permute-done.19.refs_0_, bf16[2,2,256,256]{3,2,1,0:T(8,128)(2,1)} %collective-permute-done.20.refs_1_, bf16[2,2,256,256]{3,2,1,0:T(8,128)(2,1)S(1)} %collective-permute-done.29.refs_2_, ...), custom_call_target="tpu_custom_call" | custom-call | flops 1 | bytes 1 | tf_op jit(solution)/shard_map/put_residuals/pallas_call | solution.py:516
  193.0 1.8 collective-permute-start.36
  194.8 1.6 put_residuals.4.refs_1_
  196.4 1.4 put_residuals.5
  (173 shorter events, 26.1 us)
Async XLA Ops:
  5.6 1.9 collective-permute-start
  11.8 17.4 %collective-permute-start.1 = (bf16[2,528,256]{2,1,0:T(8,128)(2,1)S(1)}, bf16[2,528,256]{2,1,0:T(8,128)(2,1)S(1)}, u32[]{:S(2)}, u32[]{:S(2)}) collective-permute-start(bf16[2,528,256]{2,1,0:T(8,128)(2,1)S(1)} %build_factors.3.refs_0_), channel_id=1, source_target_pairs={{0,8},{1,9},{2,10},{3,11},{4,0},{5,1},{6,2},{7,3},{8,12},{9,13},{1... | collective-permute-start | bytes 1622024 | tf_op jit(solution)/shard_map/ppermute | solution.py:690
  18.4 10.8 %collective-permute-start.7 = (bf16[80,2048]{1,0:T(8,128)(2,1)}, bf16[80,2048]{1,0:T(8,128)(2,1)S(1)}, u32[]{:S(2)}, u32[]{:S(2)}) collective-permute-start(bf16[80,2048]{1,0:T(8,128)(2,1)} %get-tuple-element.64), channel_id=1, source_target_pairs={{0,2},{1,3},{2,0},{3,1},{4,6},{5,7},{6,4},{7,5},{8,10},{9,11},{10,... | collective-permute-start | bytes 983048 | tf_op jit(solution)/shard_map/ppermute | solution.py:690
  19.9 22.0 %collective-permute-start.3 = (bf16[2,528,256]{2,1,0:T(8,128)(2,1)S(1)}, bf16[2,528,256]{2,1,0:T(8,128)(2,1)S(1)}, u32[]{:S(2)}, u32[]{:S(2)}) collective-permute-start(bf16[2,528,256]{2,1,0:T(8,128)(2,1)S(1)} %build_factors.3.refs_0_), channel_id=1, source_target_pairs={{0,4},{1,5},{2,6},{3,7},{4,12},{5,13},{6,14},{7,15},{8,0},{9,1},{1... | collective-permute-start | bytes 1622024 | tf_op jit(solution)/shard_map/ppermute | solution.py:690
  22.6 24.7 %collective-permute-start.6 = (bf16[64,2048]{1,0:T(8,128)(2,1)}, bf16[64,2048]{1,0:T(8,128)(2,1)S(1)}, u32[]{:S(2)}, u32[]{:S(2)}) collective-permute-start(bf16[64,2048]{1,0:T(8,128)(2,1)} %get-tuple-element.63), channel_id=1, source_target_pairs={{0,3},{1,2},{2,1},{3,0},{4,7},{5,6},{6,5},{7,4},{8,11},{9,10},{10,... | collective-permute-start | bytes 786440 | tf_op jit(solution)/shard_map/ppermute | solution.py:690
  29.2 15.7 %collective-permute-start.8 = (bf16[80,2048]{1,0:T(8,128)(2,1)S(1)}, bf16[80,2048]{1,0:T(8,128)(2,1)S(1)}, u32[]{:S(2)}, u32[]{:S(2)}) collective-permute-start(bf16[80,2048]{1,0:T(8,128)(2,1)S(1)} %copy-done.53), channel_id=1, source_target_pairs={{0,3},{1,2},{2,1},{3,0},{4,7},{5,6},{6,5},{7,4},{8,11},{9,10},{10,... | collective-permute-start | bytes 983048 | tf_op jit(solution)/shard_map/ppermute | solution.py:690
  30.0 28.5 %collective-permute-start.2 = (bf16[528,256]{1,0:T(8,128)(2,1)}, bf16[528,256]{1,0:T(8,128)(2,1)}, u32[]{:S(2)}, u32[]{:S(2)}) collective-permute-start(bf16[528,256]{1,0:T(8,128)(2,1)} %slice_bitcast_fusion.3), channel_id=1, source_target_pairs={{0,8},{1,9},{2,10},{3,11},{4,0},{5,1},{6,2},{7,3},{8,12},{9,13},{1... | collective-permute-start | bytes 811016 | tf_op jit(solution)/shard_map/ppermute | solution.py:690
  42.7 15.8 %collective-permute-start.15 = (bf16[528,256]{1,0:T(8,128)(2,1)}, bf16[528,256]{1,0:T(8,128)(2,1)}, u32[]{:S(2)}, u32[]{:S(2)}) collective-permute-start(bf16[528,256]{1,0:T(8,128)(2,1)} %slice_bitcast_fusion.1), channel_id=1, source_target_pairs={{0,4},{1,5},{2,6},{3,7},{4,12},{5,13},{6,14},{7,15},{8,0},{9,1},{1... | collective-permute-start | bytes 811016 | tf_op jit(solution)/shard_map/ppermute | solution.py:690
  43.4 7.7 %collective-permute-start.4 = (bf16[64,2048]{1,0:T(8,128)(2,1)}, bf16[64,2048]{1,0:T(8,128)(2,1)S(1)}, u32[]{:S(2)}, u32[]{:S(2)}) collective-permute-start(bf16[64,2048]{1,0:T(8,128)(2,1)} %get-tuple-element.59), channel_id=1, source_target_pairs={{0,2},{1,3},{2,0},{3,1},{4,6},{5,7},{6,4},{7,5},{8,10},{9,11},{10,... | collective-permute-start | bytes 786440 | tf_op jit(solution)/shard_map/ppermute | solution.py:690
  44.9 13.6 %collective-permute-start.5 = (bf16[64,2048]{1,0:T(8,128)(2,1)}, bf16[64,2048]{1,0:T(8,128)(2,1)}, u32[]{:S(2)}, u32[]{:S(2)}) collective-permute-start(bf16[64,2048]{1,0:T(8,128)(2,1)} %get-tuple-element.62), channel_id=1, source_target_pairs={{0,1},{1,0},{2,3},{3,2},{4,5},{5,4},{6,7},{7,6},{8,9},{9,8},{10,11... | collective-permute-start | bytes 786440 | tf_op jit(solution)/shard_map/ppermute | solution.py:690
  47.3 31.3 %copy-start.1 = (bf16[8,2,32,2048]{3,2,1,0:T(8,128)(2,1)S(1)}, bf16[8,2,32,2048]{3,2,1,0:T(8,128)(2,1)}, u32[]{:S(2)}) copy-start(bf16[8,2,32,2048]{3,2,1,0:T(8,128)(2,1)} %refs_0_.10) | copy-start | bytes 6291460
  47.3 31.3 %copy-start.45 = (s32[124]{0:T(128)S(1)}, s32[124]{0:T(128)}, u32[]{:S(2)}) copy-start(s32[124]{0:T(128)} %dynamic-slice_bitcast_fusion.tab_ref) | copy-start | bytes 1492
  47.3 31.3 %copy-start.47 = (s32[8,32]{1,0:T(8,128)S(1)}, s32[8,32]{1,0:T(8,128)}, u32[]{:S(2)}) copy-start(s32[8,32]{1,0:T(8,128)} %refs_6_.1) | copy-start | bytes 3076
  47.3 31.3 %copy-start.49 = (f32[2,256]{1,0:T(2,128)S(1)}, f32[2,256]{1,0:T(2,128)}, u32[]{:S(2)}) copy-start(f32[2,256]{1,0:T(2,128)} %refs_4_.5) | copy-start | bytes 6148
  47.3 31.3 %copy-start.51 = (f32[256]{0:T(256)S(1)}, f32[256]{0:T(256)}, u32[]{:S(2)}) copy-start(f32[256]{0:T(256)} %broadcast_in_dim.34) | copy-start | bytes 3076
  48.0 16.5 %collective-permute-start.10 = (bf16[2,528,256]{2,1,0:T(8,128)(2,1)S(1)}, bf16[2,528,256]{2,1,0:T(8,128)(2,1)}, u32[]{:S(2)}, u32[]{:S(2)}) collective-permute-start(bf16[2,528,256]{2,1,0:T(8,128)(2,1)S(1)} %build_factors.5.refs_5_), channel_id=1, source_target_pairs={{0,8},{1,9},{2,10},{3,11},{4,0},{5,1},{6,2},{7,3},{8,12},{9,13},{1... | collective-permute-start | bytes 1622024 | tf_op jit(solution)/shard_map/ppermute | solution.py:690
  51.8 25.8 %collective-permute-start.9 = (bf16[2,528,256]{2,1,0:T(8,128)(2,1)S(1)}, bf16[2,528,256]{2,1,0:T(8,128)(2,1)}, u32[]{:S(2)}, u32[]{:S(2)}) collective-permute-start(bf16[2,528,256]{2,1,0:T(8,128)(2,1)S(1)} %build_factors.5.refs_5_), channel_id=1, source_target_pairs={{0,4},{1,5},{2,6},{3,7},{4,12},{5,13},{6,14},{7,15},{8,0},{9,1},{1... | collective-permute-start | bytes 1622024 | tf_op jit(solution)/shard_map/ppermute | solution.py:690
  54.6 40.6 %copy-start.52 = (s32[8,2048]{1,0:T(8,128)S(1)}, s32[8,2048]{1,0:T(8,128)}, u32[]{:S(2)}) copy-start(s32[8,2048]{1,0:T(8,128)} %param.14) | copy-start | bytes 196612
  58.5 36.6 %copy-start.5 = (bf16[2,528,256]{2,1,0:T(8,128)(2,1)S(1)}, bf16[2,528,256]{2,1,0:T(8,128)(2,1)}, u32[]{:S(2)}) copy-start(bf16[2,528,256]{2,1,0:T(8,128)(2,1)} %copy-done.4) | copy-start | bytes 1622020
  58.5 36.6 %copy-start.8 = (bf16[2,528,256]{2,1,0:T(8,128)(2,1)S(1)}, bf16[2,528,256]{2,1,0:T(8,128)(2,1)}, u32[]{:S(2)}) copy-start(bf16[2,528,256]{2,1,0:T(8,128)(2,1)} %copy-done.7) | copy-start | bytes 1622020
  58.5 35.7 %collective-permute-start.17 = (bf16[2,2,2,256,256]{4,3,2,1,0:T(8,128)(2,1)}, bf16[2,2,2,256,256]{4,3,2,1,0:T(8,128)(2,1)S(1)}, u32[]{:S(2)}, u32[]{:S(2)}) collective-permute-start(bf16[2,2,2,256,256]{4,3,2,1,0:T(8,128)(2,1)} %get-tuple-element.77), channel_id=1, source_target_pairs={{0,2},{1,3},{2,0},{3,1},{4,6},{5,7},{6,4},{7,5},{8,10},{9,11},{10,... | collective-permute-start | bytes 3145736 | tf_op jit(solution)/shard_map/ppermute | solution.py:690
  60.1 43.9 %collective-permute-start.13 = (bf16[2,2,2,256,256]{4,3,2,1,0:T(8,128)(2,1)}, bf16[2,2,2,256,256]{4,3,2,1,0:T(8,128)(2,1)S(1)}, u32[]{:S(2)}, u32[]{:S(2)}) collective-permute-start(bf16[2,2,2,256,256]{4,3,2,1,0:T(8,128)(2,1)} %get-tuple-element.73), channel_id=1, source_target_pairs={{0,3},{1,2},{2,1},{3,0},{4,7},{5,6},{6,5},{7,4},{8,11},{9,10},{10,... | collective-permute-start | bytes 3145736 | tf_op jit(solution)/shard_map/ppermute | solution.py:690
  65.5 21.4 %collective-permute-start.11 = (bf16[528,256]{1,0:T(8,128)(2,1)S(1)}, bf16[528,256]{1,0:T(8,128)(2,1)S(1)}, u32[]{:S(2)}, u32[]{:S(2)}) collective-permute-start(bf16[528,256]{1,0:T(8,128)(2,1)S(1)} %slice_bitcast_fusion.2), channel_id=1, source_target_pairs={{0,8},{1,9},{2,10},{3,11},{4,0},{5,1},{6,2},{7,3},{8,12},{9,13},{1... | collective-permute-start | bytes 811016 | tf_op jit(solution)/shard_map/ppermute | solution.py:690
  78.5 15.6 %collective-permute-start.16 = (bf16[528,256]{1,0:T(8,128)(2,1)S(1)}, bf16[528,256]{1,0:T(8,128)(2,1)S(1)}, u32[]{:S(2)}, u32[]{:S(2)}) collective-permute-start(bf16[528,256]{1,0:T(8,128)(2,1)S(1)} %slice_bitcast_fusion), channel_id=1, source_target_pairs={{0,4},{1,5},{2,6},{3,7},{4,12},{5,13},{6,14},{7,15},{8,0},{9,1},{1... | collective-permute-start | bytes 811016 | tf_op jit(solution)/shard_map/ppermute | solution.py:690
  87.0 22.8 %collective-permute-start.12 = (bf16[2,512,256]{2,1,0:T(8,128)(2,1)S(1)}, bf16[2,512,256]{2,1,0:T(8,128)(2,1)S(1)}, u32[]{:S(2)}, u32[]{:S(2)}) collective-permute-start(bf16[2,512,256]{2,1,0:T(8,128)(2,1)S(1)} %get-tuple-element.89.refs_0_), channel_id=1, source_target_pairs={{0,4},{1,5},{2,6},{3,7},{4,12},{5,13},{6,14},{7,15},{8,0},{9,1},{1... | collective-permute-start | bytes 1572872 | tf_op jit(solution)/shard_map/ppermute | solution.py:690
  94.1 48.1 %collective-permute-start.18 = (bf16[2,2,2,256,256]{4,3,2,1,0:T(8,128)(2,1)}, bf16[2,2,2,256,256]{4,3,2,1,0:T(8,128)(2,1)S(1)}, u32[]{:S(2)}, u32[]{:S(2)}) collective-permute-start(bf16[2,2,2,256,256]{4,3,2,1,0:T(8,128)(2,1)} %get-tuple-element.84), channel_id=1, source_target_pairs={{0,1},{1,0},{2,3},{3,2},{4,5},{5,4},{6,7},{7,6},{8,9},{9,8},{10,11... | collective-permute-start | bytes 3145736 | tf_op jit(solution)/shard_map/ppermute | solution.py:690
  94.1 36.0 %collective-permute-start.21 = (bf16[2,512,256]{2,1,0:T(8,128)(2,1)S(1)}, bf16[2,512,256]{2,1,0:T(8,128)(2,1)S(1)}, u32[]{:S(2)}, u32[]{:S(2)}) collective-permute-start(bf16[2,512,256]{2,1,0:T(8,128)(2,1)S(1)} %get-tuple-element.89.refs_0_), channel_id=1, source_target_pairs={{0,8},{1,9},{2,10},{3,11},{4,0},{5,1},{6,2},{7,3},{8,12},{9,13},{1... | collective-permute-start | bytes 1572872 | tf_op jit(solution)/shard_map/ppermute | solution.py:690
  94.2 34.7 %collective-permute-start.24 = (bf16[2,512,256]{2,1,0:T(8,128)(2,1)S(1)}, bf16[2,512,256]{2,1,0:T(8,128)(2,1)S(1)}, u32[]{:S(2)}, u32[]{:S(2)}) collective-permute-start(bf16[2,512,256]{2,1,0:T(8,128)(2,1)S(1)} %get-tuple-element.92.refs_5_), channel_id=1, source_target_pairs={{0,8},{1,9},{2,10},{3,11},{4,0},{5,1},{6,2},{7,3},{8,12},{9,13},{1... | collective-permute-start | bytes 1572872 | tf_op jit(solution)/shard_map/ppermute | solution.py:690
  100.5 47.8 %copy-start.6 = (bf16[2,528,256]{2,1,0:T(8,128)(2,1)S(1)}, bf16[2,528,256]{2,1,0:T(8,128)(2,1)}, u32[]{:S(2)}) copy-start(bf16[2,528,256]{2,1,0:T(8,128)(2,1)} %copy-done.4) | copy-start | bytes 1622020
  100.5 47.8 %copy-start.9 = (bf16[2,528,256]{2,1,0:T(8,128)(2,1)S(1)}, bf16[2,528,256]{2,1,0:T(8,128)(2,1)}, u32[]{:S(2)}) copy-start(bf16[2,528,256]{2,1,0:T(8,128)(2,1)} %copy-done.7) | copy-start | bytes 1622020
  104.0 38.1 %copy-start.25 = (bf16[2,2,2,256,256]{4,3,2,1,0:T(8,128)(2,1)}, bf16[2,2,2,256,256]{4,3,2,1,0:T(8,128)(2,1)S(1)}, u32[]{:S(2)}) copy-start(bf16[2,2,2,256,256]{4,3,2,1,0:T(8,128)(2,1)S(1)} %collective-permute-done.13.refs_10_) | copy-start | bytes 3145732
  104.0 36.1 %collective-permute-start.23 = (bf16[2,512,256]{2,1,0:T(8,128)(2,1)S(1)}, bf16[2,512,256]{2,1,0:T(8,128)(2,1)S(1)}, u32[]{:S(2)}, u32[]{:S(2)}) collective-permute-start(bf16[2,512,256]{2,1,0:T(8,128)(2,1)S(1)} %get-tuple-element.92.refs_5_), channel_id=1, source_target_pairs={{0,4},{1,5},{2,6},{3,7},{4,12},{5,13},{6,14},{7,15},{8,0},{9,1},{1... | collective-permute-start | bytes 1572872 | tf_op jit(solution)/shard_map/ppermute | solution.py:690
  109.8 50.9 %collective-permute-start.20 = (bf16[2,2,256,256]{3,2,1,0:T(8,128)(2,1)}, bf16[2,2,256,256]{3,2,1,0:T(8,128)(2,1)}, u32[]{:S(2)}, u32[]{:S(2)}) collective-permute-start(bf16[2,2,256,256]{3,2,1,0:T(8,128)(2,1)} %get-tuple-element.87), channel_id=1, source_target_pairs={{0,3},{1,2},{2,1},{3,0},{4,7},{5,6},{6,5},{7,4},{8,11},{9,10},{10,... | collective-permute-start | bytes 1572872 | tf_op jit(solution)/shard_map/ppermute | solution.py:690
  128.9 31.9 %collective-permute-start.19 = (bf16[2,2,256,256]{3,2,1,0:T(8,128)(2,1)}, bf16[2,2,256,256]{3,2,1,0:T(8,128)(2,1)}, u32[]{:S(2)}, u32[]{:S(2)}) collective-permute-start(bf16[2,2,256,256]{3,2,1,0:T(8,128)(2,1)} %get-tuple-element.86), channel_id=1, source_target_pairs={{0,2},{1,3},{2,0},{3,1},{4,6},{5,7},{6,4},{7,5},{8,10},{9,11},{10,... | collective-permute-start | bytes 1572872 | tf_op jit(solution)/shard_map/ppermute | solution.py:690
  130.1 15.8 %collective-permute-start.14 = (bf16[512,256]{1,0:T(8,128)(2,1)S(1)}, bf16[512,256]{1,0:T(8,128)(2,1)S(1)}, u32[]{:S(2)}, u32[]{:S(2)}) collective-permute-start(bf16[512,256]{1,0:T(8,128)(2,1)S(1)} %slice_bitcast_fusion.7), channel_id=1, source_target_pairs={{0,4},{1,5},{2,6},{3,7},{4,12},{5,13},{6,14},{7,15},{8,0},{9,1},{1... | collective-permute-start | bytes 786440 | tf_op jit(solution)/shard_map/ppermute | solution.py:690
  140.2 20.6 %collective-permute-start.26 = (bf16[512,256]{1,0:T(8,128)(2,1)S(1)}, bf16[512,256]{1,0:T(8,128)(2,1)S(1)}, u32[]{:S(2)}, u32[]{:S(2)}) collective-permute-start(bf16[512,256]{1,0:T(8,128)(2,1)S(1)} %slice_bitcast_fusion.4), channel_id=1, source_target_pairs={{0,8},{1,9},{2,10},{3,11},{4,0},{5,1},{6,2},{7,3},{8,12},{9,13},{1... | collective-permute-start | bytes 786440 | tf_op jit(solution)/shard_map/ppermute | solution.py:690
  143.1 17.7 %collective-permute-start.22 = (bf16[512,256]{1,0:T(8,128)(2,1)}, bf16[512,256]{1,0:T(8,128)(2,1)}, u32[]{:S(2)}, u32[]{:S(2)}) collective-permute-start(bf16[512,256]{1,0:T(8,128)(2,1)} %slice_bitcast_fusion.6), channel_id=1, source_target_pairs={{0,8},{1,9},{2,10},{3,11},{4,0},{5,1},{6,2},{7,3},{8,12},{9,13},{1... | collective-permute-start | bytes 786440 | tf_op jit(solution)/shard_map/ppermute | solution.py:690
  145.9 16.2 %collective-permute-start.25 = (bf16[512,256]{1,0:T(8,128)(2,1)}, bf16[512,256]{1,0:T(8,128)(2,1)}, u32[]{:S(2)}, u32[]{:S(2)}) collective-permute-start(bf16[512,256]{1,0:T(8,128)(2,1)} %slice_bitcast_fusion.5), channel_id=1, source_target_pairs={{0,4},{1,5},{2,6},{3,7},{4,12},{5,13},{6,14},{7,15},{8,0},{9,1},{1... | collective-permute-start | bytes 786440 | tf_op jit(solution)/shard_map/ppermute | solution.py:690
  160.7 20.5 %collective-permute-start.29 = (bf16[2,2,256,256]{3,2,1,0:T(8,128)(2,1)S(1)}, bf16[2,2,256,256]{3,2,1,0:T(8,128)(2,1)S(1)}, u32[]{:S(2)}, u32[]{:S(2)}) collective-permute-start(bf16[2,2,256,256]{3,2,1,0:T(8,128)(2,1)S(1)} %get-tuple-element.104), channel_id=1, source_target_pairs={{0,1},{1,0},{2,3},{3,2},{4,5},{5,4},{6,7},{7,6},{8,9},{9,8},{10,11... | collective-permute-start | bytes 1572872 | tf_op jit(solution)/shard_map/ppermute | solution.py:690
  166.3 20.3 %collective-permute-start.30 = (bf16[2,2,256,256]{3,2,1,0:T(8,128)(2,1)S(1)}, bf16[2,2,256,256]{3,2,1,0:T(8,128)(2,1)S(1)}, u32[]{:S(2)}, u32[]{:S(2)}) collective-permute-start(bf16[2,2,256,256]{3,2,1,0:T(8,128)(2,1)S(1)} %get-tuple-element.106), channel_id=1, source_target_pairs={{0,2},{1,3},{2,0},{3,1},{4,6},{5,7},{6,4},{7,5},{8,10},{9,11},{10,... | collective-permute-start | bytes 1572872 | tf_op jit(solution)/shard_map/ppermute | solution.py:690
  178.1 14.8 %collective-permute-start.33 = (f32[2,128]{1,0:T(2,128)S(1)}, f32[2,128]{1,0:T(2,128)S(1)}, u32[]{:S(2)}, u32[]{:S(2)}) collective-permute-start(f32[2,128]{1,0:T(2,128)S(1)} %get-tuple-element.113), channel_id=1, source_target_pairs={{0,4},{1,5},{2,6},{3,7},{4,12},{5,13},{6,14},{7,15},{8,0},{9,1},{1... | collective-permute-start | bytes 3080 | tf_op jit(solution)/shard_map/ppermute | solution.py:690
  180.1 14.7 %collective-permute-start.28 = (bf16[2,2,256,256]{3,2,1,0:T(8,128)(2,1)S(1)}, bf16[2,2,256,256]{3,2,1,0:T(8,128)(2,1)S(1)}, u32[]{:S(2)}, u32[]{:S(2)}) collective-permute-start(bf16[2,2,256,256]{3,2,1,0:T(8,128)(2,1)S(1)} %get-tuple-element.101), channel_id=1, source_target_pairs={{0,1},{1,0},{2,3},{3,2},{4,5},{5,4},{6,7},{7,6},{8,9},{9,8},{10,11... | collective-permute-start | bytes 1572872 | tf_op jit(solution)/shard_map/ppermute | solution.py:690
  180.2 16.2 %collective-permute-start.27 = (bf16[2,2,256,256]{3,2,1,0:T(8,128)(2,1)S(1)}, bf16[2,2,256,256]{3,2,1,0:T(8,128)(2,1)S(1)}, u32[]{:S(2)}, u32[]{:S(2)}) collective-permute-start(bf16[2,2,256,256]{3,2,1,0:T(8,128)(2,1)S(1)} %get-tuple-element.97), channel_id=1, source_target_pairs={{0,3},{1,2},{2,1},{3,0},{4,7},{5,6},{6,5},{7,4},{8,11},{9,10},{10,... | collective-permute-start | bytes 1572872 | tf_op jit(solution)/shard_map/ppermute | solution.py:690
  181.2 11.6 %collective-permute-start.31 = (f32[2,128]{1,0:T(2,128)S(1)}, f32[2,128]{1,0:T(2,128)S(1)}, u32[]{:S(2)}, u32[]{:S(2)}) collective-permute-start(f32[2,128]{1,0:T(2,128)S(1)} %get-tuple-element.108), channel_id=1, source_target_pairs={{0,12},{1,13},{2,14},{3,15},{4,8},{5,9},{6,10},{7,11},{8,4},{9,5},... | collective-permute-start | bytes 3080 | tf_op jit(solution)/shard_map/ppermute | solution.py:690
  186.5 6.3 %collective-permute-start.32 = (f32[2,128]{1,0:T(2,128)S(1)}, f32[2,128]{1,0:T(2,128)S(1)}, u32[]{:S(2)}, u32[]{:S(2)}) collective-permute-start(f32[2,128]{1,0:T(2,128)S(1)} %get-tuple-element.109), channel_id=1, source_target_pairs={{0,8},{1,9},{2,10},{3,11},{4,0},{5,1},{6,2},{7,3},{8,12},{9,13},{1... | collective-permute-start | bytes 3080 | tf_op jit(solution)/shard_map/ppermute | solution.py:690
  192.9 4.8 %collective-permute-start.34 = (f32[2,32]{1,0:T(2,128)S(1)}, f32[2,32]{1,0:T(2,128)S(1)}, u32[]{:S(2)}, u32[]{:S(2)}) collective-permute-start(f32[2,32]{1,0:T(2,128)S(1)} %get-tuple-element.110), channel_id=1, source_target_pairs={{0,1},{1,0},{2,3},{3,2},{4,5},{5,4},{6,7},{7,6},{8,9},{9,8},{10,11... | collective-permute-start | bytes 776 | tf_op jit(solution)/shard_map/ppermute | solution.py:690
  192.9 4.8 %collective-permute-start.35 = (f32[2,32]{1,0:T(2,128)S(1)}, f32[2,32]{1,0:T(2,128)S(1)}, u32[]{:S(2)}, u32[]{:S(2)}) collective-permute-start(f32[2,32]{1,0:T(2,128)S(1)} %get-tuple-element.111), channel_id=1, source_target_pairs={{0,2},{1,3},{2,0},{3,1},{4,6},{5,7},{6,4},{7,5},{8,10},{9,11},{10,... | collective-permute-start | bytes 776 | tf_op jit(solution)/shard_map/ppermute | solution.py:690
  193.0 4.7 %collective-permute-start.36 = (f32[2,32]{1,0:T(2,128)S(1)}, f32[2,32]{1,0:T(2,128)S(1)}, u32[]{:S(2)}, u32[]{:S(2)}) collective-permute-start(f32[2,32]{1,0:T(2,128)S(1)} %get-tuple-element.116), channel_id=1, source_target_pairs={{0,3},{1,2},{2,1},{3,0},{4,7},{5,6},{6,5},{7,4},{8,11},{9,10},{10,... | collective-permute-start | bytes 776 | tf_op jit(solution)/shard_map/ppermute | solution.py:690
  (43 other events, 278.2 us)
